TPU v7x, 32 devices: a whole 2x2x4 slice. The times are simulated.
32 devices in a mesh: row: 2 (over x), seq: 16 (over z, y, core).
Axes of the slice: x: 2, y: 2, z: 4, core: 2. Of those that a mesh axis runs over, the one named last changes fastest.
Arguments:
- inputs: bfloat16 [2, 16384, 768], P('row', 'seq'), may hold values from -4 to 4
- doc_lengths: int32 [2, 4], P('row'), may hold values from 64 to 15916, as said below
- w_qkv: bfloat16 [768, 2304], replicated, may hold values from -0.21875 to 0.21875
- bias_q: float32 [768], replicated, may hold values from -2.5 to 2.5
- bias_v: float32 [768], replicated, may hold values from -2.5 to 2.5
- conv_taps: float32 [12, 33], replicated, may hold values from -2.5 to 2.5
- w_out: bfloat16 [768, 768], replicated, may hold values from -0.21875 to 0.21875
- bias_out: float32 [768], replicated, may hold values from -1.5 to 1.5
- norm1_gain: float32 [768], replicated, may hold values from 0.25 to 1.75
- norm1_bias: float32 [768], replicated, may hold values from -1.5 to 1.5
- w_up: bfloat16 [768, 3072], replicated, may hold values from -0.21875 to 0.21875
- bias_up: float32 [3072], replicated, may hold values from -2.5 to 2.5
- w_down: bfloat16 [3072, 768], replicated, may hold values from -0.109375 to 0.109375
- bias_down: float32 [768], replicated, may hold values from -1.5 to 1.5
- norm2_gain: float32 [768], replicated, may hold values from 0.25 to 1.75
- norm2_bias: float32 [768], replicated, may hold values from -1.5 to 1.5
- cotangent: bfloat16 [2, 16384, 768], P('row', 'seq'), may hold values from -6 to 6
Outputs:
- result: float32 [2, 16384, 768], P('row', 'seq')
- grad_input: float32 [2, 16384, 768], P('row', 'seq')
- grad_w_qkv: float32 [768, 2304], replicated
- grad_bias_q: float32 [768], replicated
- grad_bias_v: float32 [768], replicated
- grad_conv_taps: float32 [12, 33], replicated
- grad_w_out: float32 [768, 768], replicated
- grad_bias_out: float32 [768], replicated
- grad_norm1_gain: float32 [768], replicated
- grad_norm1_bias: float32 [768], replicated
- grad_w_up: float32 [768, 3072], replicated
- grad_bias_up: float32 [3072], replicated
- grad_w_down: float32 [3072, 768], replicated
- grad_bias_down: float32 [768], replicated
- grad_norm2_gain: float32 [768], replicated
- grad_norm2_bias: float32 [768], replicated
Inputs may be any that keep to these rules, and one draw needn't show every extreme that they name: `doc_lengths`: each row holds 4 documents laid end to end in the order of its tokens; their lengths sum to 16384. In every row one document has exactly the least length and one exactly the largest.
All inputs are finite; a program needn't handle non-finite values.
Results may differ from a plain program's by a relative error of at most 0.039.
Values may be sent and summed in bfloat16 or wider, within the bound.
No kernel may reach another device: no remote copies, remote signals or barrier semaphores. Data moves between devices by JAX's collectives and lax.ppermute only.
A program may use at most 576 MiB of HBM per device.

v0:
```python
import math

import jax
import jax.numpy as jnp
from jax import lax
from jax.sharding import PartitionSpec as P

LAND = 64
NS_ITERS = 6


PRECISE = lax.Precision.HIGHEST
NEGATIVE = -1e30


def extended(cells, sides, width):
    for axis, dim in sides:
        count = lax.axis_size(axis)
        ends = count - 1
        head = lax.slice_in_dim(cells, 0, width, axis=dim)
        tail = lax.slice_in_dim(cells, cells.shape[dim] - width, cells.shape[dim], axis=dim)
        cells = jnp.concatenate(
            [
                lax.ppermute(tail, axis, [(i, (i + 1) % count) for i in range(ends)]),
                cells,
                lax.ppermute(head, axis, [((i + 1) % count, i) for i in range(ends)]),
            ],
            axis=dim,
        )
    return cells


def locate(places, lengths):
    doc_ends = jnp.cumsum(lengths)
    doc_starts = doc_ends - lengths
    inside = (
        (places[:, None] >= doc_starts[None, :]) & (places[:, None] < doc_ends[None, :])
    ).astype(jnp.int32)
    doc_number = jnp.arange(lengths.shape[0], dtype=jnp.int32)
    doc_index = jnp.sum(inside * doc_number[None, :], axis=1)
    doc_start = jnp.sum(inside * doc_starts[None, :], axis=1)
    doc_length = jnp.maximum(jnp.sum(inside * lengths[None, :], axis=1), 1)
    segment = (places - doc_start) * LAND // doc_length
    inside_row = jnp.sum(inside, axis=1) > 0
    return (doc_index, doc_index * LAND + segment, inside_row)


def gelu_tanh(upper):
    return (
        0.5
        * upper
        * (1.0 + jnp.tanh(0.7978845608028654 * (upper + 0.044715 * upper * upper * upper)))
    )


def gelu_slope(upper):
    tangent = jnp.tanh(0.7978845608028654 * (upper + 0.044715 * upper * upper * upper))
    inner_slope = 0.7978845608028654 * (1.0 + 3.0 * 0.044715 * upper * upper)
    return 0.5 * (1.0 + tangent) + 0.5 * upper * (1.0 - tangent * tangent) * inner_slope


def normalize(residual):
    row_mean = jnp.mean(residual, axis=-1, keepdims=True)
    centered = residual - row_mean
    row_var = jnp.mean(centered * centered, axis=-1, keepdims=True)
    inverse_dev = lax.rsqrt(row_var + 1e-05)
    return (centered * inverse_dev, inverse_dev)


def norm_back(grad_normed, normed, inverse_dev):
    return inverse_dev * (
        grad_normed
        - jnp.mean(grad_normed, axis=-1, keepdims=True)
        - normed * jnp.mean(grad_normed * normed, axis=-1, keepdims=True)
    )


def pinv_kernel(mark_q, mark_k, head_count):
    mark_count, model_width = mark_q.shape
    head_size = model_width // head_count
    docs_here = mark_count // LAND
    score_scale = 1.0 / math.sqrt(head_size)
    queries = mark_q.reshape(docs_here, LAND, head_count, head_size)
    key_rows = mark_k.reshape(docs_here, LAND, head_count, head_size)
    scores = jnp.einsum("aihe,ajhe->ahij", queries, key_rows, precision=PRECISE) * score_scale
    row_max = jnp.max(scores, axis=-1, keepdims=True)
    weights = jnp.exp(scores - row_max)
    kernel = weights / jnp.sum(weights, axis=-1, keepdims=True)
    column_max = jnp.max(jnp.sum(kernel, axis=2), axis=-1)
    inverse = jnp.swapaxes(kernel, -1, -2) / column_max[..., None, None]
    identity = jnp.eye(LAND, dtype=jnp.float32)
    for sweep in range(NS_ITERS):
        product = jnp.matmul(kernel, inverse, precision=PRECISE)
        bracket = 7.0 * identity - product
        bracket = 15.0 * identity - jnp.matmul(product, bracket, precision=PRECISE)
        bracket = 13.0 * identity - jnp.matmul(product, bracket, precision=PRECISE)
        inverse = 0.25 * jnp.matmul(inverse, bracket, precision=PRECISE)
    return inverse


def landmark_mix(inverse, numer, total):
    head_count, mark_count, head_size = numer.shape
    docs_here = mark_count // LAND
    averaged = (numer / total[..., None]).reshape(head_count, docs_here, LAND, head_size)
    mixed_marks = jnp.einsum("ahij,haje->aihe", inverse, averaged, precision=PRECISE)
    return mixed_marks.reshape(mark_count, head_count * head_size)


def small_part(mark_q, mark_k, numer, total):
    return landmark_mix(pinv_kernel(mark_q, mark_k, numer.shape[0]), numer, total)


def combine(earlier, later):
    max_first, total_first, numer_first = earlier
    max_second, total_second, numer_second = later
    joint = jnp.maximum(max_first, max_second)
    scale_first = jnp.exp(max_first - joint)
    scale_second = jnp.exp(max_second - joint)
    return (
        joint,
        total_first * scale_first + total_second * scale_second,
        numer_first * scale_first[..., None] + numer_second * scale_second[..., None],
    )


def key_partial(mark_q, mark_doc, key_rows, values, key_doc, head_count, score_scale):
    mark_count, model_width = mark_q.shape
    tok_count = key_rows.shape[0]
    head_size = model_width // head_count
    scores = (
        jnp.einsum(
            "jhe,the->hjt",
            mark_q.reshape(mark_count, head_count, head_size),
            key_rows.reshape(tok_count, head_count, head_size),
            preferred_element_type=jnp.float32,
        )
        * score_scale
    )
    allowed = (mark_doc[:, None] == key_doc[None, :])[None]
    scores = jnp.where(allowed, scores, NEGATIVE)
    row_max = jnp.max(scores, axis=-1)
    weights = jnp.where(allowed, jnp.exp(scores - row_max[..., None]), 0.0)
    numer = jnp.einsum(
        "hjt,the->hje",
        weights.astype(jnp.bfloat16),
        values.reshape(tok_count, head_count, head_size),
        preferred_element_type=jnp.float32,
    )
    return (row_max, jnp.sum(weights, axis=-1), numer)


def fold_keys(state, pieces, mark_q, mark_doc, lengths, head_count, score_scale):
    key_rows, values = pieces
    row_total, model_width = key_rows.shape
    block_rows = math.gcd(row_total, 1024)
    block_count = row_total // block_rows
    key_blocks = key_rows.reshape(block_count, block_rows, model_width)
    value_blocks = values.reshape(block_count, block_rows, model_width)
    firsts = block_rows * jnp.arange(block_count, dtype=jnp.int32)

    def step_block(carried, operands):
        key_part, value_part, block_first = operands
        places = block_first + jnp.arange(block_rows, dtype=jnp.int32)
        key_doc, key_mark, key_inside = locate(places, lengths)
        partial_state = key_partial(
            mark_q, mark_doc, key_part, value_part, key_doc, head_count, score_scale
        )
        return (combine(carried, partial_state), None)

    state, unused = lax.scan(step_block, state, (key_blocks, value_blocks, firsts))
    return state


def per_device(
    inputs,
    doc_lengths,
    w_qkv,
    bias_q,
    bias_v,
    conv_taps,
    w_out,
    bias_out,
    norm1_gain,
    norm1_bias,
    w_up,
    bias_up,
    w_down,
    bias_down,
    norm2_gain,
    norm2_bias,
    cotangent,
):
    tokens = inputs[0]
    tok_count, model_width = tokens.shape
    head_count, tap_count = conv_taps.shape
    head_size = model_width // head_count
    radius = (tap_count - 1) // 2
    lengths = doc_lengths[0]
    mark_count = lengths.shape[0] * LAND
    score_scale = 1.0 / math.sqrt(head_size)
    seq_count = lax.axis_size("seq")
    row_first = lax.axis_index("seq") * tok_count
    places = row_first + jnp.arange(tok_count, dtype=jnp.int32)
    tok_doc, tok_mark, tok_inside = locate(places, lengths)
    mark_ids = jnp.arange(mark_count, dtype=jnp.int32)
    mark_doc = mark_ids // LAND
    within = mark_ids % LAND
    mark_len = jnp.repeat(lengths, LAND)
    counts = (
        ((within + 1) * mark_len + LAND - 1) // LAND - (within * mark_len + LAND - 1) // LAND
    ).astype(jnp.float32)
    contract_rows = (((0,), (0,)), ((), ()))
    contract_cols = (((1,), (1,)), ((), ()))
    projected = jnp.dot(tokens, w_qkv, preferred_element_type=jnp.float32)
    queries = (projected[:, :model_width] + bias_q).astype(jnp.bfloat16)
    key_rows = projected[:, model_width : 2 * model_width].astype(jnp.bfloat16)
    values = (projected[:, 2 * model_width :] + bias_v).astype(jnp.bfloat16)
    onehot = (tok_mark[:, None] == mark_ids[None, :]).astype(jnp.bfloat16)
    query_sums = lax.dot_general(onehot, queries, contract_rows, preferred_element_type=jnp.float32)
    key_sums = lax.dot_general(onehot, key_rows, contract_rows, preferred_element_type=jnp.float32)
    query_sums, key_sums = lax.psum((query_sums, key_sums), "seq")
    mark_q = (query_sums / counts[:, None]).astype(jnp.bfloat16)
    mark_k = (key_sums / counts[:, None]).astype(jnp.bfloat16)
    own_count = mark_count // seq_count
    own_first = lax.axis_index("seq") * own_count
    own_q = lax.dynamic_slice_in_dim(mark_q, own_first, own_count, 0)
    own_doc = lax.dynamic_slice_in_dim(mark_doc, own_first, own_count, 0)
    init_state = (
        jnp.full((head_count, own_count), NEGATIVE, jnp.float32),
        jnp.zeros((head_count, own_count), jnp.float32),
        jnp.zeros((head_count, own_count, head_size), jnp.float32),
    )
    own_state = fold_keys(
        init_state,
        (
            lax.all_gather(key_rows, "seq", axis=0, tiled=True),
            lax.all_gather(values, "seq", axis=0, tiled=True),
        ),
        own_q,
        own_doc,
        lengths,
        head_count,
        score_scale,
    )
    row_max, total, numer = (
        lax.all_gather(own_state[0], "seq", axis=1, tiled=True),
        lax.all_gather(own_state[1], "seq", axis=1, tiled=True),
        lax.all_gather(own_state[2], "seq", axis=1, tiled=True),
    )
    mixed_marks, small_pullback = jax.vjp(
        small_part, mark_q.astype(jnp.float32), mark_k.astype(jnp.float32), numer, total
    )
    heads_q = queries.reshape(tok_count, head_count, head_size)
    heads_mk = mark_k.reshape(mark_count, head_count, head_size)
    heads_mix = mixed_marks.reshape(mark_count, head_count, head_size)
    scores_one = (
        jnp.einsum("the,jhe->htj", heads_q, heads_mk, preferred_element_type=jnp.float32)
        * score_scale
    )
    allowed_one = (tok_doc[:, None] == mark_doc[None, :])[None]
    scores_one = jnp.where(allowed_one, scores_one, NEGATIVE)
    weights_one = jnp.where(
        allowed_one, jnp.exp(scores_one - jnp.max(scores_one, axis=-1, keepdims=True)), 0.0
    )
    probs_one = weights_one / jnp.sum(weights_one, axis=-1, keepdims=True)
    nystrom = jnp.einsum("htj,jhe->the", probs_one, heads_mix, precision=PRECISE).reshape(
        tok_count, model_width
    )
    value_ext = extended(values, (("seq", 0),), radius)
    ext_places = row_first - radius + jnp.arange(tok_count + 2 * radius, dtype=jnp.int32)
    ext_doc, ext_mark, ext_inside = locate(ext_places, lengths)
    tap_columns = jnp.repeat(conv_taps.T, head_size, axis=1)
    convolved = jnp.zeros((tok_count, model_width), jnp.float32)
    for offset in range(tap_count):
        keep_mask = (ext_doc[offset : offset + tok_count] == tok_doc) & ext_inside[
            offset : offset + tok_count
        ]
        convolved = convolved + jnp.where(
            keep_mask[:, None],
            value_ext[offset : offset + tok_count].astype(jnp.float32)
            * tap_columns[offset][None, :],
            0.0,
        )
    mixed = (nystrom + convolved).astype(jnp.bfloat16)
    attended = jnp.dot(mixed, w_out, preferred_element_type=jnp.float32) + bias_out
    norm_one, inverse_one = normalize(tokens.astype(jnp.float32) + attended)
    hidden_one = norm_one * norm1_gain + norm1_bias
    hidden_low = hidden_one.astype(jnp.bfloat16)
    upper = jnp.dot(hidden_low, w_up, preferred_element_type=jnp.float32) + bias_up
    active = gelu_tanh(upper).astype(jnp.bfloat16)
    lowered = jnp.dot(active, w_down, preferred_element_type=jnp.float32) + bias_down
    norm_two, inverse_two = normalize(hidden_one + lowered)
    result = norm_two * norm2_gain + norm2_bias
    upstream = cotangent[0].astype(jnp.float32)
    grad_gain_two = jnp.sum(upstream * norm_two, axis=0)
    grad_shift_two = jnp.sum(upstream, axis=0)
    grad_two = norm_back(upstream * norm2_gain, norm_two, inverse_two)
    grad_low_two = grad_two.astype(jnp.bfloat16)
    grad_bias_down = jnp.sum(grad_low_two.astype(jnp.float32), axis=0)
    grad_w_down = lax.dot_general(
        active, grad_low_two, contract_rows, preferred_element_type=jnp.float32
    )
    grad_active = lax.dot_general(
        grad_low_two, w_down, contract_cols, preferred_element_type=jnp.float32
    )
    grad_upper = (grad_active * gelu_slope(upper)).astype(jnp.bfloat16)
    grad_bias_up = jnp.sum(grad_upper.astype(jnp.float32), axis=0)
    grad_w_up = lax.dot_general(
        hidden_low, grad_upper, contract_rows, preferred_element_type=jnp.float32
    )
    grad_hidden = grad_two + lax.dot_general(
        grad_upper, w_up, contract_cols, preferred_element_type=jnp.float32
    )
    grad_gain_one = jnp.sum(grad_hidden * norm_one, axis=0)
    grad_shift_one = jnp.sum(grad_hidden, axis=0)
    grad_one = norm_back(grad_hidden * norm1_gain, norm_one, inverse_one)
    grad_low_one = grad_one.astype(jnp.bfloat16)
    grad_bias_out = jnp.sum(grad_low_one.astype(jnp.float32), axis=0)
    grad_w_out = lax.dot_general(
        mixed, grad_low_one, contract_rows, preferred_element_type=jnp.float32
    )
    grad_mixed = lax.dot_general(
        grad_low_one, w_out, contract_cols, preferred_element_type=jnp.float32
    ).astype(jnp.bfloat16)
    grad_mixed_wide = grad_mixed.astype(jnp.float32)
    grad_ext = extended(grad_mixed, (("seq", 0),), radius)
    tap_grads = []
    grad_values_conv = jnp.zeros((tok_count, model_width), jnp.float32)
    for offset in range(tap_count):
        keep_mask = (ext_doc[offset : offset + tok_count] == tok_doc) & ext_inside[
            offset : offset + tok_count
        ]
        tap_grads.append(
            jnp.sum(
                jnp.where(
                    keep_mask[:, None],
                    grad_mixed_wide * value_ext[offset : offset + tok_count].astype(jnp.float32),
                    0.0,
                ),
                axis=0,
            )
        )
        mirror = 2 * radius - offset
        keep_back = (ext_doc[mirror : mirror + tok_count] == tok_doc) & ext_inside[
            mirror : mirror + tok_count
        ]
        grad_values_conv = grad_values_conv + jnp.where(
            keep_back[:, None],
            grad_ext[mirror : mirror + tok_count].astype(jnp.float32)
            * tap_columns[offset][None, :],
            0.0,
        )
    grad_conv_taps = jnp.sum(
        jnp.stack(tap_grads, axis=1).reshape(head_count, head_size, tap_count), axis=1
    )
    heads_grad = grad_mixed_wide.reshape(tok_count, head_count, head_size)
    grad_probs = jnp.einsum("the,jhe->htj", heads_grad, heads_mix, precision=PRECISE)
    grad_mix_part = jnp.einsum("htj,the->jhe", probs_one, heads_grad, precision=PRECISE).reshape(
        mark_count, model_width
    )
    grad_scores_one = (
        probs_one * (grad_probs - jnp.sum(probs_one * grad_probs, axis=-1, keepdims=True))
    ).astype(jnp.bfloat16)
    grad_query_one = (
        jnp.einsum("htj,jhe->the", grad_scores_one, heads_mk, preferred_element_type=jnp.float32)
        * score_scale
    )
    grad_mk_part = (
        jnp.einsum("htj,the->jhe", grad_scores_one, heads_q, preferred_element_type=jnp.float32)
        * score_scale
    )
    grad_mix, grad_mk_one = lax.psum(
        (grad_mix_part, grad_mk_part.reshape(mark_count, model_width)), "seq"
    )
    grad_mq_small, grad_mk_small, grad_numer, grad_total = small_pullback(grad_mix)
    heads_mq = mark_q.reshape(mark_count, head_count, head_size)
    heads_k = key_rows.reshape(tok_count, head_count, head_size)
    heads_v = values.reshape(tok_count, head_count, head_size)
    scores_three = (
        jnp.einsum("jhe,the->hjt", heads_mq, heads_k, preferred_element_type=jnp.float32)
        * score_scale
    )
    allowed_three = (mark_doc[:, None] == tok_doc[None, :])[None]
    scores_three = jnp.where(allowed_three, scores_three, NEGATIVE)
    weights_three = jnp.where(allowed_three, jnp.exp(scores_three - row_max[..., None]), 0.0)
    grad_numer_low = grad_numer.astype(jnp.bfloat16)
    grad_weights = jnp.einsum(
        "hje,the->hjt", grad_numer_low, heads_v, preferred_element_type=jnp.float32
    )
    grad_values_three = jnp.einsum(
        "hjt,hje->the",
        weights_three.astype(jnp.bfloat16),
        grad_numer_low,
        preferred_element_type=jnp.float32,
    ).reshape(tok_count, model_width)
    grad_scores_three = (weights_three * (grad_weights + grad_total[..., None])).astype(
        jnp.bfloat16
    )
    grad_keys_three = (
        jnp.einsum("hjt,jhe->the", grad_scores_three, heads_mq, preferred_element_type=jnp.float32)
        * score_scale
    )
    grad_mq_part = (
        jnp.einsum("hjt,the->jhe", grad_scores_three, heads_k, preferred_element_type=jnp.float32)
        * score_scale
    )
    grad_mq_three = lax.psum(grad_mq_part.reshape(mark_count, model_width), "seq")
    grad_query_sums = (grad_mq_small + grad_mq_three) / counts[:, None]
    grad_key_sums = (grad_mk_small + grad_mk_one) / counts[:, None]
    onehot_wide = onehot.astype(jnp.float32)
    grad_queries = (
        grad_query_one.reshape(tok_count, model_width)
        + jnp.dot(onehot_wide, grad_query_sums, precision=PRECISE)
    ).astype(jnp.bfloat16)
    grad_keys = (
        grad_keys_three.reshape(tok_count, model_width)
        + jnp.dot(onehot_wide, grad_key_sums, precision=PRECISE)
    ).astype(jnp.bfloat16)
    grad_values = (grad_values_three + grad_values_conv).astype(jnp.bfloat16)
    grad_bias_q = jnp.sum(grad_queries.astype(jnp.float32), axis=0)
    grad_bias_v = jnp.sum(grad_values.astype(jnp.float32), axis=0)
    grad_projected = jnp.concatenate([grad_queries, grad_keys, grad_values], axis=1)
    grad_w_qkv = lax.dot_general(
        tokens, grad_projected, contract_rows, preferred_element_type=jnp.float32
    )
    grad_input = grad_one + lax.dot_general(
        grad_projected, w_qkv, contract_cols, preferred_element_type=jnp.float32
    )
    summed = lax.psum(
        (
            grad_w_qkv,
            grad_bias_q,
            grad_bias_v,
            grad_conv_taps,
            grad_w_out,
            grad_bias_out,
            grad_gain_one,
            grad_shift_one,
            grad_w_up,
            grad_bias_up,
            grad_w_down,
            grad_bias_down,
            grad_gain_two,
            grad_shift_two,
        ),
        ("row", "seq"),
    )
    return (
        result[None],
        grad_input[None],
        summed[0],
        summed[1],
        summed[2],
        summed[3],
        summed[4],
        summed[5],
        summed[6],
        summed[7],
        summed[8],
        summed[9],
        summed[10],
        summed[11],
        summed[12],
        summed[13],
    )


def solution(mesh):
    return jax.shard_map(
        per_device,
        mesh=mesh,
        in_specs=(
            P("row", "seq", None),
            P("row", None),
            P(),
            P(),
            P(),
            P(),
            P(),
            P(),
            P(),
            P(),
            P(),
            P(),
            P(),
            P(),
            P(),
            P(),
            P("row", "seq", None),
        ),
        out_specs=(
            P("row", "seq", None),
            P("row", "seq", None),
            P(),
            P(),
            P(),
            P(),
            P(),
            P(),
            P(),
            P(),
            P(),
            P(),
            P(),
            P(),
            P(),
            P(),
        ),
        check_vma=False,
    )
```

profile of v0, /device:TPU:0, one launch (start us, length us, event | category | flops | bytes accessed | tf_op | source)
XLA Modules:
  0.0 1839.5 jit_solution(12406957978483814013)
XLA Ops:
  10.0 5.2 fusion.280
  152.8 5.0 fusion.402
  214.3 6.3 fusion.439
  220.6 12.2 fusion.418
  232.8 18.2 all-gather.5.cloned.1.call-done
  251.0 130.8 %all-gather.3.cloned.1.call-done = bf16[16384,768]{1,0:T(8,128)(2,1)} async-done(((bf16[1024,768]{1,0:T(8,128)(2,1)}), bf16[16384,768]{1,0:T(8,128)(2,1)}) %all-gather.3.cloned.1.call-update) | async-done | bytes 25165840 | tf_op jit(solution)/shard_map/all_gather | solution.py:236
  381.8 346.7 %while.17 = (s32[]{:T(128)}, f32[12,16]{1,0:T(8,128)}, f32[12,16]{1,0:T(8,128)}, f32[12,16,64]{2,1,0:T(8,128)}, s32[16]{0:T(128)}, /*index=5*/s32[16]{0:T(128)},...) while((s32[]{:T(128)}, f32[12,16]{1,0:T(8,128)}, ...), condition=%wide.region_9.10_spmd.clone, body=%wide.region_5.9_spmd.clone.sunk | while | flops 52188288 | bytes 21501748 | solution.py:170
  385.3 3.8 constant_dynamic-slice_fusion.4
  407.0 3.8 constant_dynamic-slice_fusion.4
  428.6 3.8 constant_dynamic-slice_fusion.4
  450.3 3.8 constant_dynamic-slice_fusion.4
  472.0 3.8 constant_dynamic-slice_fusion.4
  493.6 3.8 constant_dynamic-slice_fusion.4
  515.3 3.8 constant_dynamic-slice_fusion.4
  536.9 3.8 constant_dynamic-slice_fusion.4
  558.6 3.8 constant_dynamic-slice_fusion.4
  580.3 3.8 constant_dynamic-slice_fusion.4
  601.9 3.8 constant_dynamic-slice_fusion.4
  623.6 3.8 constant_dynamic-slice_fusion.4
  645.2 3.8 constant_dynamic-slice_fusion.4
  666.9 3.8 constant_dynamic-slice_fusion.4
  688.6 3.8 constant_dynamic-slice_fusion.4
  710.2 3.8 constant_dynamic-slice_fusion.4
  729.3 22.1 %all_gather.18 = f32[12,256]{0,1:T(8,128)} all-gather(f32[12,16]{0,1:T(8,128)S(1)} %copy.333), channel_id=1, replica_groups=mesh['row'=2,'seq'=16] {'seq'}, dimensions={1}, use_global_device_ids=true | all-gather | bytes 13056 | tf_op jit(solution)/shard_map/all_gather | solution.py:247
  752.3 25.3 %all_gather.17 = f32[12,256,64]{2,1,0:T(8,128)S(1)} all-gather(f32[12,16,64]{2,1,0:T(8,128)} %get-tuple-element.139), channel_id=1, replica_groups=mesh['row'=2,'seq'=16] {'seq'}, dimensions={1}, use_global_device_ids=true | all-gather | bytes 835584 | tf_op jit(solution)/shard_map/all_gather | solution.py:248
  787.7 12.3 fusion.404
  803.6 61.6 %fusion.93 = bf16[1024,768]{1,0:T(8,128)(2,1)} fusion(f32[1024,768]{1,0:T(8,128)} %copy.350, bf16[1024,768]{1,0:T(8,128)(2,1)} %get-tuple-element.451, bf16[16,768]{1,0:T(8,128)(2,1)} %collective-permute-done.1, bf16[16,768]{1,0:T(8,128)(2,1)} %collective-permute-done, f32[768]{0:T(1024)} %broadcast_in_dim.986, f32[768]{0:T(1024)} %broadcast_in_dim.983, ...), kind=kLoop, calls=%fused_computation.246 | loop fusion | flops 180092928 | bytes 6475776 | tf_op jit(solution)/shard_map/convert_element_type | solution.py:284
  865.3 4.1 fusion.419
  870.2 11.2 fusion.400
  881.4 10.1 fusion.420
  898.3 17.2 convert_reduce_fusion
  915.5 9.6 multiply_reduce_fusion.1
  927.0 6.4 fusion.131
  936.0 11.9 convolution_bitcast_fusion.4
  947.9 11.7 multiply_reduce_fusion
  959.6 7.0 multiply_convert_fusion.1
  974.5 10.7 fusion.398
  985.2 11.0 fusion.403
  1007.6 22.4 %all_gather.19 = f32[12,256]{0,1:T(8,128)} all-gather(f32[12,16]{0,1:T(8,128)S(1)} %copy.382), channel_id=1, replica_groups=mesh['row'=2,'seq'=16] {'seq'}, dimensions={1}, use_global_device_ids=true | all-gather | bytes 13056 | tf_op jit(solution)/shard_map/all_gather | solution.py:246
  1032.4 4.0 collective-permute-start.3
  1036.4 5.2 fusion.386
  1041.6 55.7 %all-reduce.9.cloned.1.call-done = f32[4,12,64,64]{2,3,1,0:T(8,128)} async-done(((f32[4,12,64,64]{2,3,1,0:T(8,128)}), f32[4,12,64,64]{2,3,1,0:T(8,128)}) %all-reduce.9.cloned.1.call-update) | async-done | bytes 786448 | tf_op jit(solution)/shard_map/psum | solution.py:372
  1097.3 4.6 convolution_multiply_fusion.5
  1229.6 4.7 multiply_reduce_fusion.6
  1238.8 4.7 fusion.25
  1243.4 7.2 multiply_convert_fusion
  1268.0 60.7 %convert_reduce_fusion.4 = (f32[768]{0:T(1024)}, bf16[1024,768]{1,0:T(8,128)(2,1)}) fusion(f32[1024,768]{1,0:T(8,128)} %copy.401, f32[768]{0:T(1024)} %broadcast_in_dim.986, bf16[1024,768]{1,0:T(8,128)(2,1)} %get-tuple-element.513, bf16[16,768]{1,0:T(8,128)(2,1)} %collective-permute-done.3, pred[1024]{0:T(1024)(128)(4,1)} %get-tuple-element.461, ...), kind=kLoop, calls=%fused_computation.351 | loop fusion | flops 181665024 | bytes 6478848 | tf_op jit(solution)/shard_map/reduce_sum | solution.py:421
  1336.5 6.0 convolution_multiply_fusion.2
  1346.0 16.0 all-reduce.13.cloned.1.call-done
  1362.0 4.8 convert_reduce_fusion.5
  1369.9 7.0 convolution_bitcast_fusion
  1381.4 8.3 fusion.155
  1393.7 7.8 fusion.153
  1405.6 8.1 fusion.151
  1421.8 11.0 fusion.189
  1438.2 10.1 fusion.187
  1452.3 9.4 fusion.185
  1465.8 10.2 fusion.183
  1532.1 42.8 %all-reduce = (f32[768]{0:T(1024)}, f32[768]{0:T(1024)}, f32[12,33]{0,1:T(8,128)}, f32[768]{0:T(1024)}, f32[768]{0:T(1024)}, /*index=5*/f32[768]{0:T(1024)}, f32...) all-reduce(f32[768]{0:T(1024)} %get-tuple-element.511, ...), channel_id=1, replica_groups=mesh['row'=2,'seq'=16] {'row','seq'}, use_global_device_ids=true, to_apply=%region_39.40 | all-reduce | flops 9612 | bytes 76896 | tf_op jit(solution)/shard_map/psum | solution.py:429
  1576.3 8.9 add_bitcast_fusion
  1588.7 219.9 %all-reduce.11.cloned.1.call-done = (f32[768,2304]{0,1:T(8,128)}, f32[768,768]{1,0:T(8,128)}, f32[768,3072]{1,0:T(8,128)}, f32[3072,768]{1,0:T(8,128)}) async-done(((f32[768,2304]{0,1:T(8,128)}, f32[768,768]{1,0:T(8,128)}, f32[768,3072]{1,0:T(8,128)}, f32[3072,768]{1,0:T(8,128)}), (f32[768,2304]{0,1:T(8,128)}, f32[768,768]{1,0:T(8,128)}, f32[768,3072]{1,0:T(8,128)}, ...) | async-done | bytes 28311568 | tf_op jit(solution)/shard_map/psum | solution.py:429
  1808.6 8.0 copy.405
  1820.0 8.8 copy.529
  1828.7 3.7 copy.530
  (892 shorter events, 792.4 us)
Async XLA Ops:
  7.2 117.8 %all-reduce.15.cloned.1.call-start = ((), (), s32[]{:S(2)}) async-start(), calls=%async_computation.5 | async-start | bytes 3145728 | tf_op jit(solution)/shard_map/psum | solution.py:221
  10.0 5.3 copy-start.138
  15.3 5.1 copy-start.62
  16.3 4.2 copy-start.109
  23.3 227.7 %all-gather.5.cloned.1.call-start = ((), (), s32[]{:S(2)}) async-start(), calls=%async_computation.1 | async-start | bytes 26738688 | tf_op jit(solution)/shard_map/all_gather | solution.py:237
  24.0 357.7 %all-gather.3.cloned.1.call-start = ((), (), s32[]{:S(2)}) async-start(), calls=%async_computation | async-start | bytes 26738688 | tf_op jit(solution)/shard_map/all_gather | solution.py:236
  27.3 1070.0 %all-reduce.9.cloned.1.call-start = ((), (), s32[]{:S(2)}) async-start(), calls=%async_computation.2 | async-start | bytes 3145728 | tf_op jit(solution)/shard_map/psum | solution.py:372
  28.7 774.9 %collective-permute-start = (bf16[16,768]{1,0:T(8,128)(2,1)}, bf16[16,768]{1,0:T(8,128)(2,1)}, u32[]{:S(2)}, u32[]{:S(2)}) collective-permute-start(bf16[16,768]{1,0:T(8,128)(2,1)} %get-tuple-element.459), channel_id=1, source_target_pairs={{0,1},{1,2},{2,3},{3,4},{4,5},{5,6},{6,7},{7,8},{8,9},{9,10},{10,1... | collective-permute-start | bytes 73736 | tf_op jit(solution)/shard_map/ppermute | solution.py:24
  31.7 771.9 %collective-permute-start.1 = (bf16[16,768]{1,0:T(8,128)(2,1)}, bf16[16,768]{1,0:T(8,128)(2,1)}, u32[]{:S(2)}, u32[]{:S(2)}) collective-permute-start(bf16[16,768]{1,0:T(8,128)(2,1)} %get-tuple-element.460), channel_id=1, source_target_pairs={{1,0},{2,1},{3,2},{4,3},{5,4},{6,5},{7,6},{8,7},{9,8},{10,9},{11,1... | collective-permute-start | bytes 73736 | tf_op jit(solution)/shard_map/ppermute | solution.py:26
  40.8 4.0 copy-start.64
  114.4 5.8 copy-start.137
  120.3 9.0 copy-start.124
  147.5 14.0 copy-start.121
  152.8 5.0 copy-start.72
  152.8 5.1 copy-start.80
  163.7 8.0 copy-start.40
  174.7 7.7 copy-start.24
  185.5 7.5 copy-start.26
  194.9 7.8 copy-start.28
  204.5 6.8 copy-start.22
  752.3 25.8 %copy-start.102 = (f32[12,256]{1,0:T(8,128)}, f32[12,256]{1,0:T(8,128)S(1)}, u32[]{:S(2)}) copy-start(f32[12,256]{1,0:T(8,128)S(1)} %copy.334) | copy-start | bytes 36868
  865.3 16.1 slice-start.14
  869.3 55.8 %copy-start.16 = (f32[1024,768]{0,1:T(8,128)}, f32[1024,768]{0,1:T(8,128)S(1)}, u32[]{:S(2)}) copy-start(f32[1024,768]{0,1:T(8,128)S(1)} %get-tuple-element.501) | copy-start | bytes 9437188
  869.4 12.0 slice-start.15
  870.2 11.2 copy-start.141
  870.2 11.2 copy-start.143
  894.9 20.6 %slice-start.12 = ((s8[4718592]{0:T(1024)(128)(4,1)}), s8[4194304]{0:T(1024)(128)(4,1)S(1)}, s32[]{:S(2)}) async-start(s8[4718592]{0:T(1024)(128)(4,1)} %bitcast.324), calls=%async_computation.18 | async-start | bytes 8388608
  898.3 17.2 copy-start.81
  898.3 17.2 slice-start.13
  926.9 6.5 copy-start.78
  936.0 11.9 copy-start.84
  936.0 11.9 copy-start.90
  936.0 11.9 copy-start.107
  936.0 23.6 %slice-start.6 = ((s8[12582912]{0:T(1024)(128)(4,1)}), s8[4194304]{0:T(1024)(128)(4,1)S(1)}, s32[]{:S(2)}) async-start(s8[12582912]{0:T(1024)(128)(4,1)} %bitcast.311), calls=%async_computation.12 | async-start | bytes 8388608
  936.0 23.6 %slice-start.7 = ((s8[12582912]{0:T(1024)(128)(4,1)}), s8[4194304]{0:T(1024)(128)(4,1)S(1)}, s32[]{:S(2)}) async-start(s8[12582912]{0:T(1024)(128)(4,1)} %bitcast.311), calls=%async_computation.13 | async-start | bytes 8388608
  947.9 11.8 slice-start.8
  959.6 7.0 copy-start.74
  969.5 4.9 copy-start.17
  969.5 15.6 slice-start.3
  974.4 10.7 slice-start.4
  974.4 10.7 slice-start.5
  974.4 10.7 copy-start.82
  974.4 10.7 copy-start.142
  1001.6 360.4 %all-reduce.13.cloned.1.call-start = ((), (), s32[]{:S(2)}) async-start(), calls=%async_computation.4 | async-start | bytes 3145728 | tf_op jit(solution)/shard_map/psum | solution.py:372
  1031.1 236.3 %collective-permute-start.2 = (bf16[16,768]{1,0:T(8,128)(2,1)}, bf16[16,768]{1,0:T(8,128)(2,1)}, u32[]{:S(2)}, u32[]{:S(2)}) collective-permute-start(bf16[16,768]{1,0:T(8,128)(2,1)} %get-tuple-element.457), channel_id=1, source_target_pairs={{1,0},{2,1},{3,2},{4,3},{5,4},{6,5},{7,6},{8,7},{9,8},{10,9},{11,1... | collective-permute-start | bytes 73736 | tf_op jit(solution)/shard_map/ppermute | solution.py:26
  1032.4 235.0 %collective-permute-start.3 = (bf16[16,768]{1,0:T(8,128)(2,1)}, bf16[16,768]{1,0:T(8,128)(2,1)}, u32[]{:S(2)}, u32[]{:S(2)}) collective-permute-start(bf16[16,768]{1,0:T(8,128)(2,1)} %get-tuple-element.458), channel_id=1, source_target_pairs={{0,1},{1,2},{2,3},{3,4},{4,5},{5,6},{6,7},{7,8},{8,9},{9,10},{10,1... | collective-permute-start | bytes 73736 | tf_op jit(solution)/shard_map/ppermute | solution.py:24
  1097.3 4.6 copy-start.23
  1226.8 11.9 slice-start
  1226.8 11.9 slice-start.1
  1229.5 4.7 copy-start.37
  1229.6 4.7 copy-start.69
  1229.6 9.2 slice-start.2
  1238.7 4.7 copy-start.91
  1243.4 7.2 copy-start.34
  1267.3 541.3 %all-reduce.11.cloned.1.call-start = ((), (), s32[]{:S(2)}) async-start(), calls=%async_computation.3 | async-start | bytes 56623104 | tf_op jit(solution)/shard_map/psum | solution.py:429
  1342.4 19.6 %copy-start.110 = (s32[1024]{0:T(1024)S(1)}, s32[1024]{0:T(1024)}, u32[]{:S(2)}) copy-start(s32[1024]{0:T(1024)} %copy-done.109) | copy-start | bytes 12292
  1342.4 19.6 %copy-start.125 = (f32[256]{0:T(256)S(1)}, f32[256]{0:T(256)}, u32[]{:S(2)}) copy-start(f32[256]{0:T(256)} %copy-done.124) | copy-start | bytes 3076
  1362.0 4.9 copy-start.63
  1362.0 4.9 copy-start.77
  1362.0 4.9 copy-start.89
  1377.0 3.6 copy-start.134
  1816.6 12.1 slice-start.9
  1820.0 8.8 slice-start.10
  1820.0 8.8 slice-start.11
  (136 other events, 255.6 us)
Sparse Core Ops, SparseCore 0:
  23.4 98.3 all-reduce.14
  123.4 127.5 all-gather.4
  253.2 128.5 all-gather.2
  1001.8 95.4 all-reduce.8
  1267.4 94.5 all-reduce.12
  1377.1 431.4 all-reduce.10
where the time goes:
time: 1860 us; the launch traced here: 1840 us
  local copies, waits for them, and re-layouts  479 us (26%)
  matrix products  476 us (26%)
  waiting for transfers between devices  441 us (24%)
  other arithmetic  303 us (16%)
  blocking collectives  113 us (6%)
    psum x1, waiting for transfers between devices, per_device(): lax.psum((grad_w_qkv, grad_bias_q, grad_bias_v, grad_conv_taps, grad_w_ou...  220 us
    dynamic_slice x64, local copies, waits for them, and re-layouts, fold_keys(): lax.scan(step_block, state, (key_blocks, value_blocks, firsts))  161 us
    all_gather x1, waiting for transfers between devices, per_device(): lax.all_gather(key_rows, 'seq', axis=0, tiled=True)  131 us
    unnamed x357, local copies, waits for them, and re-layouts  92.2 us
    psum x2, waiting for transfers between devices, per_device(): lax.psum((grad_mix_part, grad_mk_part.reshape(mark_count, model_width)),...  71.7 us
    broadcast_in_dim x66, local copies, waits for them, and re-layouts, per_device(): tap_columns = jnp.repeat(conv_taps.T, head_size, axis=1)  67.5 us
    reduce_sum x7, other arithmetic, per_device(): jnp.sum(jnp.where(keep_mask[:, None], grad_mixed_wide * value_ext[offset:...  64.9 us
    convert_element_type x1, other arithmetic, per_device(): mixed = (nystrom + convolved).astype(jnp.bfloat16)  61.6 us
  transfers between devices with their start and end apart: 10, of which 5 were waited for; matrix products, arithmetic and copies ran while one was open for 53% of the time, Pallas kernels for 0%

commit v1 on v0

v1 whole, which is shorter than its diff:
```python
import math

import jax
import jax.numpy as jnp
from jax import lax
from jax.sharding import PartitionSpec as P

LAND = 64
NS_ITERS = 6
HIGH = lax.Precision.HIGHEST
NEGATIVE = -1e30
BF = jnp.bfloat16
F32 = jnp.float32

T_X = BF
T_NUM = BF
T_MIX = BF
T_GMIX = BF
T_GNUM = BF
T_Y = BF
T_W = BF
P_MIX = lax.Precision.DEFAULT


def swap(array, axis, bit):
    count = lax.axis_size(axis)
    return lax.ppermute(array, axis, [(i, i ^ bit) for i in range(count)])


def add_parts(parts):
    total = parts[0].astype(F32)
    for part in parts[1:]:
        total = total + part.astype(F32)
    return total


def scatter_blocks(blocks, join, kind):
    count = lax.axis_size("seq")
    me = lax.axis_index("seq")
    core, chip = me % 2, me // 2
    pairs = blocks.reshape((count // 2, 2) + blocks.shape[1:])
    mine = lax.dynamic_index_in_dim(pairs, core, 1, keepdims=False)
    other = lax.dynamic_index_in_dim(pairs, 1 - core, 1, keepdims=False)
    held = join([mine, swap(other.astype(kind), "seq", 1)]).astype(kind)
    parts = [lax.dynamic_index_in_dim(held, chip, 0, keepdims=False)]
    for step in range(1, count // 2):
        part = lax.dynamic_index_in_dim(held, chip ^ step, 0, keepdims=False)
        parts.append(swap(part, "seq", 2 * step))
    return join(parts)


def gather_blocks(block):
    count = lax.axis_size("seq")
    me = lax.axis_index("seq")
    core, chip = me % 2, me // 2
    held = jnp.zeros((count // 2,) + block.shape, block.dtype)
    held = lax.dynamic_update_index_in_dim(held, block, chip, 0)
    for step in range(1, count // 2):
        held = lax.dynamic_update_index_in_dim(
            held, swap(block, "seq", 2 * step), chip ^ step, 0
        )
    other = swap(held, "seq", 1)
    first = jnp.where(core == 0, held, other)
    second = jnp.where(core == 0, other, held)
    return jnp.stack([first, second], axis=1).reshape((count,) + block.shape)


def stages(first):
    seq_bits = [("seq", 1 << i) for i in range(1, lax.axis_size("seq").bit_length() - 1)]
    row_bits = [("row", 1 << i) for i in range(lax.axis_size("row").bit_length() - 1)]
    rest = row_bits + seq_bits if first == "row" else seq_bits[:1] + row_bits + seq_bits[1:]
    return [("seq", 1)] + rest


def all_sum(array, first):
    plan = stages(first)
    held = array
    for axis, bit in plan:
        half = held.shape[0] // 2
        side = (lax.axis_index(axis) // bit) % 2
        mine = lax.dynamic_slice_in_dim(held, side * half, half, 0)
        other = lax.dynamic_slice_in_dim(held, (1 - side) * half, half, 0)
        held = mine.astype(F32) + swap(other.astype(T_W), axis, bit).astype(F32)
        held = held.astype(T_W)
    for axis, bit in reversed(plan):
        half = held.shape[0]
        side = (lax.axis_index(axis) // bit) % 2
        other = swap(held, axis, bit)
        held = jnp.where(
            side == 0,
            jnp.concatenate([held, other], 0),
            jnp.concatenate([other, held], 0),
        )
    return held.astype(F32)


def small_sum(array):
    for axis, bit in stages("row"):
        array = array + swap(array, axis, bit)
    return array


def extended(cells, width):
    count = lax.axis_size("seq")
    head = cells[:width]
    tail = cells[-width:]
    return jnp.concatenate(
        [
            lax.ppermute(tail, "seq", [(i, i + 1) for i in range(count - 1)]),
            cells,
            lax.ppermute(head, "seq", [(i + 1, i) for i in range(count - 1)]),
        ],
        axis=0,
    )


def locate(places, lengths):
    doc_ends = jnp.cumsum(lengths)
    doc_starts = doc_ends - lengths
    inside = (
        (places[:, None] >= doc_starts[None, :]) & (places[:, None] < doc_ends[None, :])
    ).astype(jnp.int32)
    doc_number = jnp.arange(lengths.shape[0], dtype=jnp.int32)
    doc_index = jnp.sum(inside * doc_number[None, :], axis=1)
    doc_start = jnp.sum(inside * doc_starts[None, :], axis=1)
    doc_length = jnp.maximum(jnp.sum(inside * lengths[None, :], axis=1), 1)
    segment = (places - doc_start) * LAND // doc_length
    inside_row = jnp.sum(inside, axis=1) > 0
    return (doc_index, doc_index * LAND + segment, inside_row)


def gelu_both(upper):
    tangent = jnp.tanh(0.7978845608028654 * (upper + 0.044715 * upper * upper * upper))
    inner_slope = 0.7978845608028654 * (1.0 + 3.0 * 0.044715 * upper * upper)
    active = 0.5 * upper * (1.0 + tangent)
    slope = 0.5 * (1.0 + tangent) + 0.5 * upper * (1.0 - tangent * tangent) * inner_slope
    return active, slope


def normalize(residual):
    row_mean = jnp.mean(residual, axis=-1, keepdims=True)
    centered = residual - row_mean
    row_var = jnp.mean(centered * centered, axis=-1, keepdims=True)
    inverse_dev = lax.rsqrt(row_var + 1e-05)
    return (centered * inverse_dev, inverse_dev)


def norm_back(grad_normed, normed, inverse_dev):
    return inverse_dev * (
        grad_normed
        - jnp.mean(grad_normed, axis=-1, keepdims=True)
        - normed * jnp.mean(grad_normed * normed, axis=-1, keepdims=True)
    )


def pinv_kernel(queries, key_rows, score_scale):
    scores = jnp.einsum("pie,pje->pij", queries, key_rows, precision=HIGH) * score_scale
    row_max = jnp.max(scores, axis=-1, keepdims=True)
    weights = jnp.exp(scores - row_max)
    kernel = weights / jnp.sum(weights, axis=-1, keepdims=True)
    column_max = jnp.max(jnp.sum(kernel, axis=1), axis=-1)
    inverse = jnp.swapaxes(kernel, -1, -2) / column_max[:, None, None]
    identity = jnp.eye(LAND, dtype=F32)
    for sweep in range(NS_ITERS):
        product = jnp.matmul(kernel, inverse, precision=HIGH)
        bracket = 7.0 * identity - product
        bracket = 15.0 * identity - jnp.matmul(product, bracket, precision=HIGH)
        bracket = 13.0 * identity - jnp.matmul(product, bracket, precision=HIGH)
        inverse = 0.25 * jnp.matmul(inverse, bracket, precision=HIGH)
    return inverse


def small_part(mark_q, mark_k, numer, total, score_scale):
    inverse = pinv_kernel(mark_q, mark_k, score_scale)
    return jnp.einsum("pij,pje->pie", inverse, numer / total, precision=HIGH)


def join_stats(parts):
    parts = [part.astype(F32) for part in parts]
    top = parts[0][..., 65:66]
    for part in parts[1:]:
        top = jnp.maximum(top, part[..., 65:66])
    total = 0.0
    for part in parts:
        total = total + part[..., :65] * jnp.exp(part[..., 65:66] - top)
    rest = jnp.zeros(total.shape[:-1] + (62,), F32)
    return jnp.concatenate([total, top, rest], axis=-1)


def per_device(
    inputs, doc_lengths, w_qkv, bias_q, bias_v, conv_taps, w_out, bias_out, norm1_gain,
    norm1_bias, w_up, bias_up, w_down, bias_down, norm2_gain, norm2_bias, cotangent,
):
    tokens = inputs[0]
    tok_count, width = tokens.shape
    heads, tap_count = conv_taps.shape
    size = width // heads
    radius = (tap_count - 1) // 2
    lengths = doc_lengths[0]
    docs = lengths.shape[0]
    mark_count = docs * LAND
    scale = 1.0 / math.sqrt(size)
    seq_count = lax.axis_size("seq")
    me = lax.axis_index("seq")
    row_first = me * tok_count
    places = row_first + jnp.arange(tok_count, dtype=jnp.int32)
    tok_doc, tok_mark, tok_inside = locate(places, lengths)
    mark_ids = jnp.arange(mark_count, dtype=jnp.int32)
    mark_doc = mark_ids // LAND
    within = mark_ids % LAND
    mark_len = jnp.repeat(lengths, LAND)
    counts = (
        ((within + 1) * mark_len + LAND - 1) // LAND - (within * mark_len + LAND - 1) // LAND
    ).astype(F32)
    rows_in = (((0,), (0,)), ((), ()))
    cols_in = (((1,), (1,)), ((), ()))
    pair_count = docs * heads
    own_pairs = -(-pair_count // seq_count)
    padded = own_pairs * seq_count

    def to_pairs(array):
        array = array.reshape(docs, LAND, heads, -1).transpose(0, 2, 1, 3)
        array = array.reshape(pair_count, LAND, -1)
        return jnp.pad(array, ((0, padded - pair_count), (0, 0), (0, 0)))

    def from_pairs(array):
        array = array[:pair_count].reshape(docs, heads, LAND, -1)
        return array.transpose(0, 2, 1, 3).reshape(mark_count, -1)

    def own(array):
        return lax.dynamic_slice_in_dim(array, me * own_pairs, own_pairs, 0)

    onehot = (tok_mark[:, None] == mark_ids[None, :]).astype(BF)
    sums = lax.dot_general(onehot, tokens, rows_in, preferred_element_type=F32)
    means = (sums / counts[:, None]).reshape(seq_count, mark_count // seq_count, width)
    own_mean = scatter_blocks(means, add_parts, T_X).astype(T_X)
    mean_in = gather_blocks(own_mean).reshape(mark_count, width)
    mean_pre = HIGH if T_X == F32 else None
    mark_q = jnp.dot(
        mean_in, w_qkv[:, :width].astype(T_X), preferred_element_type=F32, precision=mean_pre
    )
    mark_q = (mark_q + bias_q).astype(BF)
    mark_k = jnp.dot(
        mean_in, w_qkv[:, width : 2 * width].astype(T_X), preferred_element_type=F32,
        precision=mean_pre,
    ).astype(BF)

    projected = jnp.dot(tokens, w_qkv, preferred_element_type=F32)
    queries = (projected[:, :width] + bias_q).astype(BF)
    key_rows = projected[:, width : 2 * width].astype(BF)
    values = (projected[:, 2 * width :] + bias_v).astype(BF)
    heads_q = queries.reshape(tok_count, heads, size)
    heads_k = key_rows.reshape(tok_count, heads, size)
    heads_v = values.reshape(tok_count, heads, size)
    heads_mq = mark_q.reshape(mark_count, heads, size)
    heads_mk = mark_k.reshape(mark_count, heads, size)

    allowed = (mark_doc[:, None] == tok_doc[None, :])[None]
    scores_three = (
        jnp.einsum("jhe,the->hjt", heads_mq, heads_k, preferred_element_type=F32) * scale
    )
    scores_three = jnp.where(allowed, scores_three, NEGATIVE)
    local_max = jnp.max(scores_three, axis=-1)
    weights = jnp.where(allowed, jnp.exp(scores_three - local_max[..., None]), 0.0)
    numer = jnp.einsum("hjt,the->hje", weights.astype(BF), heads_v, preferred_element_type=F32)
    total = jnp.sum(weights, axis=-1)
    stats = jnp.concatenate(
        [numer, total[..., None], local_max[..., None], jnp.zeros((heads, mark_count, 62), F32)],
        axis=-1,
    )
    if T_NUM == BF:
        stats = stats.at[..., :64].set(stats[..., :64].astype(BF).astype(F32))
    stats = stats.reshape(heads, docs, LAND, 128).transpose(1, 0, 2, 3)
    stats = stats.reshape(pair_count, LAND, 128)
    stats = jnp.pad(stats, ((0, padded - pair_count), (0, 0), (0, 0)))
    stats = scatter_blocks(stats.reshape(seq_count, own_pairs, LAND, 128), join_stats, F32)
    own_numer, own_total, own_max = stats[..., :64], stats[..., 64:65], stats[..., 65:66]
    own_total = jnp.maximum(own_total, 1e-30)
    own_q = own(to_pairs(mark_q)).astype(F32)
    own_k = own(to_pairs(mark_k)).astype(F32)
    own_mixed, small_pullback = jax.vjp(
        lambda a, b, c, d: small_part(a, b, c, d, scale), own_q, own_k, own_numer, own_total
    )
    own_mixed = own_mixed.astype(T_MIX).astype(F32)
    packed = jnp.concatenate([own_mixed, own_max, jnp.zeros((own_pairs, LAND, 63), F32)], -1)
    packed = gather_blocks(packed).reshape(padded, LAND, 128)[:pair_count]
    heads_mix = packed[..., :64].reshape(docs, heads, LAND, size).transpose(0, 2, 1, 3)
    heads_mix = heads_mix.reshape(mark_count, heads, size)
    row_max = packed[..., 64].reshape(docs, heads, LAND).transpose(1, 0, 2)
    row_max = row_max.reshape(heads, mark_count)

    scores_one = jnp.einsum("the,jhe->htj", heads_q, heads_mk, preferred_element_type=F32) * scale
    allowed_one = (tok_doc[:, None] == mark_doc[None, :])[None]
    scores_one = jnp.where(allowed_one, scores_one, NEGATIVE)
    weights_one = jnp.where(
        allowed_one, jnp.exp(scores_one - jnp.max(scores_one, axis=-1, keepdims=True)), 0.0
    )
    probs_one = weights_one / jnp.sum(weights_one, axis=-1, keepdims=True)
    nystrom = jnp.einsum(
        "htj,jhe->the", probs_one, heads_mix, precision=P_MIX, preferred_element_type=F32
    )

    value_ext = extended(values, radius)
    ext_places = row_first - radius + jnp.arange(tok_count + 2 * radius, dtype=jnp.int32)
    ext_doc, ext_mark, ext_inside = locate(ext_places, lengths)
    ext_doc = jnp.where(ext_inside, ext_doc, -1)
    block = 128
    reach = block + 2 * radius
    blocks = tok_count // block
    rows_at = jnp.arange(block)[:, None]
    cols_at = jnp.arange(reach)[None, :]
    offset_at = cols_at - rows_at
    in_band = (offset_at >= 0) & (offset_at < tap_count)
    taps_hi = conv_taps.astype(BF)
    taps_lo = (conv_taps - taps_hi.astype(F32)).astype(BF)

    def band(taps):
        return jnp.where(in_band[None], taps[:, jnp.clip(offset_at, 0, tap_count - 1)], 0)

    starts = jnp.arange(blocks) * block
    same = jnp.stack(
        [
            (tok_doc[b * block : (b + 1) * block, None] == ext_doc[None, b * block : b * block + reach])
            for b in range(blocks)
        ]
    )

    def windows(cells):
        return jnp.stack([cells[b * block : b * block + reach] for b in range(blocks)]).reshape(
            blocks, reach, heads, size
        )

    def convolve(bands, cells):
        return jnp.einsum("hbts,bshe->bthe", bands, cells, preferred_element_type=F32)

    value_win = windows(value_ext)
    masks = same[None]
    bands_hi = jnp.where(masks, band(taps_hi)[:, None], 0)
    bands_lo = jnp.where(masks, band(taps_lo)[:, None], 0)
    convolved = convolve(bands_hi, value_win) + convolve(bands_lo, value_win)
    mixed = (nystrom.reshape(tok_count, width) + convolved.reshape(tok_count, width)).astype(BF)

    attended = jnp.dot(mixed, w_out, preferred_element_type=F32) + bias_out
    norm_one, inverse_one = normalize(tokens.astype(F32) + attended)
    hidden_one = norm_one * norm1_gain + norm1_bias
    hidden_low = hidden_one.astype(BF)
    upper = jnp.dot(hidden_low, w_up, preferred_element_type=F32) + bias_up
    active, slope = gelu_both(upper)
    active = active.astype(BF)
    lowered = jnp.dot(active, w_down, preferred_element_type=F32) + bias_down
    norm_two, inverse_two = normalize(hidden_one + lowered)
    result = norm_two * norm2_gain + norm2_bias
    upstream = cotangent[0].astype(F32)
    grad_gain_two = jnp.sum(upstream * norm_two, axis=0)
    grad_shift_two = jnp.sum(upstream, axis=0)
    grad_two = norm_back(upstream * norm2_gain, norm_two, inverse_two)
    grad_low_two = grad_two.astype(BF)
    grad_bias_down = jnp.sum(grad_low_two.astype(F32), axis=0)
    grad_w_down = lax.dot_general(active, grad_low_two, rows_in, preferred_element_type=F32)
    grad_active = lax.dot_general(grad_low_two, w_down, cols_in, preferred_element_type=F32)
    grad_upper = (grad_active * slope).astype(BF)
    grad_bias_up = jnp.sum(grad_upper.astype(F32), axis=0)
    grad_w_up = lax.dot_general(hidden_low, grad_upper, rows_in, preferred_element_type=F32)
    grad_hidden = grad_two + lax.dot_general(
        grad_upper, w_up, cols_in, preferred_element_type=F32
    )
    grad_gain_one = jnp.sum(grad_hidden * norm_one, axis=0)
    grad_shift_one = jnp.sum(grad_hidden, axis=0)
    grad_one = norm_back(grad_hidden * norm1_gain, norm_one, inverse_one)
    grad_low_one = grad_one.astype(BF)
    grad_bias_out = jnp.sum(grad_low_one.astype(F32), axis=0)
    grad_w_out = lax.dot_general(mixed, grad_low_one, rows_in, preferred_element_type=F32)
    grad_mixed = lax.dot_general(
        grad_low_one, w_out, cols_in, preferred_element_type=F32
    ).astype(BF)

    heads_grad = grad_mixed.reshape(tok_count, heads, size)
    grad_mix_part = jnp.einsum(
        "htj,the->jhe", probs_one, heads_grad.astype(F32), precision=P_MIX,
        preferred_element_type=F32,
    ).reshape(mark_count, width)
    own_grad_mix = scatter_blocks(
        to_pairs(grad_mix_part).reshape(seq_count, own_pairs, LAND, size), add_parts, T_GMIX
    )
    grad_mq_small, grad_mk_small, grad_numer, grad_total = small_pullback(own_grad_mix)
    grad_numer = grad_numer.astype(T_GNUM).astype(F32)
    grads = jnp.concatenate([grad_numer, grad_total, jnp.zeros((own_pairs, LAND, 63), F32)], -1)
    grads = gather_blocks(grads).reshape(padded, LAND, 128)[:pair_count]
    grads = grads.reshape(docs, heads, LAND, 128).transpose(1, 0, 2, 3)
    grads = grads.reshape(heads, mark_count, 128)
    grad_numer_low, grad_total_all = grads[..., :64].astype(BF), grads[..., 64:65]

    grad_probs = jnp.einsum(
        "the,jhe->htj", heads_grad.astype(F32), heads_mix, precision=P_MIX,
        preferred_element_type=F32,
    )
    shared = jnp.sum(heads_grad.astype(F32) * nystrom, axis=-1).transpose(1, 0)[..., None]
    grad_scores_one = (probs_one * (grad_probs - shared)).astype(BF)
    grad_query_one = (
        jnp.einsum("htj,jhe->the", grad_scores_one, heads_mk, preferred_element_type=F32) * scale
    ).reshape(tok_count, width)
    grad_mk_part = (
        jnp.einsum("htj,the->jhe", grad_scores_one, heads_q, preferred_element_type=F32) * scale
    ).reshape(mark_count, width)

    grad_ext = extended(grad_mixed, radius)
    grad_win = windows(grad_ext)
    back_hi = jnp.where(masks, band(taps_hi[:, ::-1])[:, None], 0)
    back_lo = jnp.where(masks, band(taps_lo[:, ::-1])[:, None], 0)
    grad_values_conv = (convolve(back_hi, grad_win) + convolve(back_lo, grad_win)).reshape(
        tok_count, width
    )
    products = jnp.einsum(
        "bthe,bshe->hbts",
        grad_mixed.reshape(blocks, block, heads, size),
        value_win,
        preferred_element_type=F32,
    )
    products = jnp.sum(jnp.where(masks, products, 0.0), axis=1)
    grad_conv_taps = jnp.stack(
        [jnp.sum(jnp.where(offset_at == o, products, 0.0), axis=(1, 2)) for o in range(tap_count)],
        axis=1,
    )

    weights_three = jnp.where(allowed, jnp.exp(scores_three - row_max[..., None]), 0.0)
    grad_weights = jnp.einsum("hje,the->hjt", grad_numer_low, heads_v, preferred_element_type=F32)
    grad_values_three = jnp.einsum(
        "hjt,hje->the", weights_three.astype(BF), grad_numer_low, preferred_element_type=F32
    ).reshape(tok_count, width)
    grad_scores_three = (weights_three * (grad_weights + grad_total_all)).astype(BF)
    grad_keys_three = (
        jnp.einsum("hjt,jhe->the", grad_scores_three, heads_mq, preferred_element_type=F32) * scale
    ).reshape(tok_count, width)
    grad_mq_part = (
        jnp.einsum("hjt,the->jhe", grad_scores_three, heads_k, preferred_element_type=F32) * scale
    ).reshape(mark_count, width)

    def placed(array):
        empty = jnp.zeros((padded, LAND, size), F32)
        return from_pairs(lax.dynamic_update_slice_in_dim(empty, array, me * own_pairs, 0))

    grad_mq = grad_mq_part + placed(grad_mq_small)
    grad_mk = grad_mk_part + placed(grad_mk_small)
    grad_marks = jnp.concatenate([grad_mq, grad_mk], axis=1).astype(BF)
    mark_back = lax.dot_general(
        grad_marks, w_qkv[:, : 2 * width], cols_in, preferred_element_type=F32
    ) / counts[:, None]
    own_back = scatter_blocks(
        mark_back.reshape(seq_count, mark_count // seq_count, width), add_parts, T_Y
    ).astype(T_Y)
    mark_back = gather_blocks(own_back).reshape(mark_count, width)

    grad_queries = grad_query_one.astype(BF)
    grad_keys = grad_keys_three.astype(BF)
    grad_values = (grad_values_three + grad_values_conv).astype(BF)
    grad_bias_q = jnp.sum(grad_queries.astype(F32), axis=0) + jnp.sum(grad_mq, axis=0)
    grad_bias_v = jnp.sum(grad_values.astype(F32), axis=0)
    grad_projected = jnp.concatenate([grad_queries, grad_keys, grad_values], axis=1)
    grad_w_qkv = lax.dot_general(tokens, grad_projected, rows_in, preferred_element_type=F32)
    grad_w_marks = lax.dot_general(
        mean_in.astype(BF), grad_marks, rows_in, preferred_element_type=F32
    )
    grad_w_qkv = grad_w_qkv + jnp.pad(grad_w_marks, ((0, 0), (0, width)))
    grad_input = (
        grad_one
        + lax.dot_general(grad_projected, w_qkv, cols_in, preferred_element_type=F32)
        + jnp.dot(onehot, mark_back.astype(BF), preferred_element_type=F32)
    )

    small = [
        grad_bias_q, grad_bias_v, grad_conv_taps.reshape(-1), grad_bias_out, grad_gain_one,
        grad_shift_one, grad_bias_up, grad_bias_down, grad_gain_two, grad_shift_two,
    ]
    sizes = [part.shape[0] for part in small]
    flat = jnp.concatenate(small)
    lanes = -(-flat.shape[0] // 1024) * 8
    flat = jnp.pad(flat, (0, lanes * 128 - flat.shape[0])).reshape(lanes, 128)
    flat = small_sum(flat).reshape(-1)
    pieces = []
    at = 0
    for length in sizes:
        pieces.append(flat[at : at + length])
        at += length
    sum_w_down = all_sum(grad_w_down, "row")
    sum_w_up = all_sum(grad_w_up, "seq")
    sum_w_out = all_sum(grad_w_out, "seq")
    sum_w_qkv = all_sum(grad_w_qkv, "row")
    return (
        result[None], grad_input[None], sum_w_qkv, pieces[0], pieces[1],
        pieces[2].reshape(heads, tap_count), sum_w_out, pieces[3], pieces[4], pieces[5],
        sum_w_up, pieces[6], sum_w_down, pieces[7], pieces[8], pieces[9],
    )


def solution(mesh):
    whole, tokens = P(), P("row", "seq", None)
    return jax.shard_map(
        per_device,
        mesh=mesh,
        in_specs=(tokens, P("row", None)) + (whole,) * 14 + (tokens,),
        out_specs=(tokens, tokens) + (whole,) * 14,
        check_vma=False,
    )
```

time: 1860 us -> 1180 us (0.63)
  matrix products: 476 us -> 219 us
  waiting for transfers between devices: 441 us -> 186 us
  other arithmetic: 303 us -> 119 us
  starting transfers between devices: 9.78 us -> 143 us
  blocking collectives: 113 us -> 0 us
    gather x0 -> x8, local copies, waits for them, and re-layouts: none -> 313 us  [band(): taps[:, jnp.clip(offset_at, 0, tap_count - 1)]]
    psum x4 -> x0, waiting for transfers between devices: 292 us -> none  [the longest x1 220 us: per_device(): lax.psum((grad_w_qkv, grad_bias_q, grad_bias_v, grad_conv_taps, grad_w_ou...]
    dot_general x131 -> x107, matrix products: 442 us -> 191 us  [the longest x1 16.7 us: per_device(): lax.dot_general(grad_low_two, w_down, cols_in, preferred_element_type=F32)]
    ppermute x4 -> x113, waiting for transfers between devices: 0.01 us -> 186 us  [the longest x109 186 us: swap(): return lax.ppermute(array, axis, [(i, i ^ bit) for i in range(count)])]
    dynamic_slice x66 -> x16, local copies, waits for them, and re-layouts: 163 us -> 1.22 us  [all_sum(): other = lax.dynamic_slice_in_dim(held, (1 - side) * half, half, 0)]
    all_gather x2 -> x0, waiting for transfers between devices: 149 us -> none  [the longest x1 131 us: per_device(): lax.all_gather(key_rows, 'seq', axis=0, tiled=True)]
    reduce_sum x46 -> x8, other arithmetic: 164 us -> 16.4 us  [the longest x1 4.91 us: per_device(): total = jnp.sum(weights, axis=-1)]
    ppermute x4 -> x113, starting transfers between devices: 9.54 us -> 143 us  [the longest x109 135 us: swap(): return lax.ppermute(array, axis, [(i, i ^ bit) for i in range(count)])]
  transfers between devices with their start and end apart: 10 -> 113, of which waited for: 5 -> 39; matrix products, arithmetic and copies ran while one was open for 53% -> 54% of each run, Pallas kernels for 0% -> 0%
where the time goes in v1:
time: 1180 us; the launch traced here: 1170 us
  local copies, waits for them, and re-layouts  495 us (42%)
  matrix products  219 us (19%)
  waiting for transfers between devices  186 us (16%)
  starting transfers between devices  143 us (12%)
  other arithmetic  119 us (10%)
    gather x8, local copies, waits for them, and re-layouts, band(): taps[:, jnp.clip(offset_at, 0, tap_count - 1)]  313 us
    ppermute x109, waiting for transfers between devices, swap(): return lax.ppermute(array, axis, [(i, i ^ bit) for i in range(count)])  186 us
    ppermute x109, starting transfers between devices, swap(): return lax.ppermute(array, axis, [(i, i ^ bit) for i in range(count)])  135 us
    unnamed x419, local copies, waits for them, and re-layouts  48 us
  transfers between devices with their start and end apart: 113, of which 39 were waited for; matrix products, arithmetic and copies ran while one was open for 54% of the time, Pallas kernels for 0%

profile of v1, /device:TPU:0, one launch (start us, length us, event | category | flops | bytes accessed | tf_op | source)
XLA Modules:
  0.0 1168.3 jit_solution(8676774977476569316)
XLA Ops:
  7.8 3.8 fusion.63
  23.8 71.7 %gather_fusion = bf16[20480,12]{1,0:T(8,128)(2,1)} fusion(bf16[12,33]{0,1:T(8,128)(2,1)S(1)} %get-tuple-element.233, s32[20480]{0:T(1024)S(1)} %broadcast_clamp_fusion), kind=kCustom, calls=%fused_computation | custom fusion | bytes 1064960 | tf_op jit(solution)/shard_map/gather | solution.py:318
  95.5 72.4 %gather_fusion.1 = bf16[20480,12]{1,0:T(8,128)(2,1)} fusion(bf16[12,33]{0,1:T(8,128)(2,1)S(1)} %get-tuple-element.232, s32[20480]{0:T(1024)S(1)} %broadcast_clamp_fusion), kind=kCustom, calls=%fused_computation.1 | custom fusion | bytes 1064960 | tf_op jit(solution)/shard_map/gather | solution.py:318
  178.3 72.4 %gather_fusion.2 = bf16[20480,12]{1,0:T(8,128)(2,1)} fusion(bf16[12,33]{0,1:T(8,128)(2,1)S(1)} %rev.6, s32[20480]{0:T(1024)S(1)} %broadcast_clamp_fusion), kind=kCustom, calls=%fused_computation.2 | custom fusion | bytes 1064960 | tf_op jit(solution)/shard_map/gather | solution.py:318
  250.7 5.9 copy.1031
  256.6 72.3 %gather_fusion.3 = bf16[20480,12]{1,0:T(8,128)(2,1)} fusion(bf16[12,33]{0,1:T(8,128)(2,1)S(1)} %rev.7, s32[20480]{0:T(1024)S(1)} %broadcast_clamp_fusion), kind=kCustom, calls=%fused_computation.3 | custom fusion | bytes 1064960 | tf_op jit(solution)/shard_map/gather | solution.py:318
  328.9 6.0 copy.1033
  334.9 5.9 copy.1003
  340.9 5.9 copy.1006
  351.9 6.1 broadcast_select_fusion.1
  398.7 4.8 collective-permute-start.1
  411.3 3.6 collective-permute-start.6
  417.0 4.5 collective-permute-done.7
  423.9 4.4 fusion.29
  430.3 3.9 collective-permute-start.12
  434.2 3.8 collective-permute-start.14
  442.0 3.8 copy.1008
  450.8 3.7 fusion.13
  454.6 4.9 fusion.9
  524.3 3.5 collective-permute-start.22
  530.1 5.7 collective-permute-done.20
  543.5 4.1 collective-permute-start.25
  558.3 7.4 collective-permute-done.28
  567.7 12.3 %fusion.284 = (f32[12,1024]{1,0:T(8,128)}, f32[12,1024,256]{1,2,0:T(8,128)}) fusion(pred[1024,256]{0,1:T(8,128)(4,1)S(1)} %copy-done.111, bf16[1024,12,64]{0,2,1:T(8,128)(2,1)} %bitcast.644, bf16[256,12,64]{0,2,1:T(8,128)(2,1)S(1)} %bitcast.646), kind=kOutput, calls=%fused_computation.695 | convolution fusion | flops 418382080 | bytes 14860288 | tf_op jit(solution)/shard_map/sub | solution.py:296
  588.0 5.9 fusion.272
  598.9 8.6 fusion.270
  607.5 11.8 %fusion.286 = (f32[1024]{0:T(1024)S(1)}, f32[1024,768]{0,1:T(8,128)S(1)}) fusion(f32[768]{0:T(1024)S(1)} %copy-done.187, bf16[3072,768]{1,0:T(8,128)(2,1)} %param.31, f32[1024,3072]{1,0:T(8,128)} %fusion.270, f32[3072]{0:T(1024)S(1)} %copy-done.185, f32[768]{0:T(1024)S(1)} %copy-done.110, f32[768]{0:T(1024)S(1)} %copy-done.107, ...), kind=kOutput, calls=%fused_computation.697 | convolution fusion | flops 4868799488 | bytes 23626752 | tf_op jit(solution)/shard_map/dot_general | solution.py:350
  621.9 3.5 convert_reduce_fusion.2
  625.4 13.8 %fusion.273 = f32[3072,768]{1,0:T(8,128)} fusion(bf16[1024,768]{0,1:T(8,128)(2,1)S(1)} %get-tuple-element.212, f32[1024,3072]{1,0:T(8,128)} %fusion.270, f32[3072]{0:T(1024)S(1)} %copy-done.185), kind=kOutput, calls=%fused_computation.687 | convolution fusion | flops 4863295488 | bytes 23605248 | tf_op jit(solution)/shard_map/dot_general | solution.py:359
  639.2 16.7 %convert_reduce_fusion = (f32[3072]{0:T(1024)}, bf16[1024,3072]{1,0:T(8,128)(2,1)}) fusion(f32[1024,3072]{1,0:T(8,128)} %fusion.270, f32[3072]{0:T(1024)S(1)} %copy-done.185, bf16[1024,768]{0,1:T(8,128)(2,1)S(1)} %get-tuple-element.212, bf16[3072,768]{1,0:T(8,128)(2,1)} %param.31), kind=kOutput, calls=%fused_computation.15 | convolution fusion | flops 4901041152 | bytes 25190400 | tf_op jit(solution)/shard_map/dot_general | solution.py:360
  655.9 10.7 fusion.268
  666.6 7.2 multiply_reduce_fusion
  684.0 7.6 convolution_bitcast_fusion
  693.6 5.7 multiply_convert_fusion.1
  703.7 4.1 dynamic-slice_convert_fusion.1
  720.7 4.0 dynamic-slice_convert_fusion
  737.1 3.8 copy.1100
  780.0 3.9 copy.1035
  831.3 7.6 collective-permute-done.84
  857.5 10.5 convert_reduce_fusion.4
  868.0 8.0 multiply_convert_fusion
  890.2 5.5 fusion.56
  911.0 8.8 bitcast_add_fusion
  958.3 3.6 add_convert_fusion
  967.9 20.3 %collective-permute-done.104 = bf16[768,768]{1,0:T(8,128)(2,1)S(1)} collective-permute-done((bf16[768,768]{1,0:T(8,128)(2,1)S(1)}, bf16[768,768]{1,0:T(8,128)(2,1)S(1)}, u32[]{:S(2)}, u32[]{:S(2)}) %collective-permute-start.104) | collective-permute-done | bytes 1179680 | tf_op jit(solution)/shard_map/ppermute | solution.py:27
  994.1 13.9 %collective-permute-done.69 = bf16[192,2304]{1,0:T(8,128)(2,1)S(1)} collective-permute-done((bf16[192,2304]{1,0:T(8,128)(2,1)S(1)}, bf16[192,2304]{1,0:T(8,128)(2,1)S(1)}, u32[]{:S(2)}, u32[]{:S(2)}) %collective-permute-start.69) | collective-permute-done | bytes 884768 | tf_op jit(solution)/shard_map/ppermute | solution.py:27
  1010.5 7.3 collective-permute-done.95
  1020.2 6.9 collective-permute-done.106
  1027.3 4.1 collective-permute-done.96
  1031.5 4.0 collective-permute-done.71
  1035.7 10.9 collective-permute-done.72
  1049.6 4.5 collective-permute-done.97
  1057.2 5.3 collective-permute-done.108
  1064.7 4.0 collective-permute-done.74
  1078.3 6.7 collective-permute-done.75
  1087.8 9.2 collective-permute-done.110
  1102.2 7.9 collective-permute-done.76
  1111.8 10.9 collective-permute-done.111
  1129.6 4.3 collective-permute-done.91
  1136.6 4.4 add_bitcast_fusion
  1141.0 3.5 copy.1101
  1147.5 5.4 fusion.38
  1152.8 5.9 fusion.24
  1158.7 9.3 fusion.23
  (1037 shorter events, 470.1 us)
Async XLA Ops:
  7.4 389.7 %collective-permute-start = (bf16[8,16,768]{2,1,0:T(8,128)(2,1)}, bf16[8,16,768]{2,1,0:T(8,128)(2,1)}, u32[]{:S(2)}, u32[]{:S(2)}) collective-permute-start(bf16[8,16,768]{2,1,0:T(8,128)(2,1)} %fusion.108), channel_id=1, source_target_pairs={{0,1},{1,0},{2,3},{3,2},{4,5},{5,4},{6,7},{7,6},{8,9},{9,8},{10,11... | collective-permute-start | bytes 589832 | tf_op jit(solution)/shard_map/ppermute | solution.py:27
  17.1 356.8 %collective-permute-start.32 = (bf16[16,768]{1,0:T(8,128)(2,1)S(1)}, bf16[16,768]{1,0:T(8,128)(2,1)S(1)}, u32[]{:S(2)}, u32[]{:S(2)}) collective-permute-start(bf16[16,768]{1,0:T(8,128)(2,1)S(1)} %get-tuple-element.262), channel_id=1, source_target_pairs={{0,1},{1,2},{2,3},{3,4},{4,5},{5,6},{6,7},{7,8},{8,9},{9,10},{10,1... | collective-permute-start | bytes 73736 | tf_op jit(solution)/shard_map/ppermute | solution.py:109
  19.0 354.8 %collective-permute-start.33 = (bf16[16,768]{1,0:T(8,128)(2,1)S(1)}, bf16[16,768]{1,0:T(8,128)(2,1)S(1)}, u32[]{:S(2)}, u32[]{:S(2)}) collective-permute-start(bf16[16,768]{1,0:T(8,128)(2,1)S(1)} %get-tuple-element.261), channel_id=1, source_target_pairs={{1,0},{2,1},{3,2},{4,3},{5,4},{6,5},{7,6},{8,7},{9,8},{10,9},{11,1... | collective-permute-start | bytes 73736 | tf_op jit(solution)/shard_map/ppermute | solution.py:111
  398.7 12.7 %collective-permute-start.1 = (bf16[16,768]{1,0:T(8,128)(2,1)}, bf16[16,768]{1,0:T(8,128)(2,1)S(1)}, u32[]{:S(2)}, u32[]{:S(2)}) collective-permute-start(bf16[16,768]{1,0:T(8,128)(2,1)} %get-tuple-element.289), channel_id=1, source_target_pairs={{0,2},{1,3},{2,0},{3,1},{4,6},{5,7},{6,4},{7,5},{8,10},{9,11},{10,... | collective-permute-start | bytes 73736 | tf_op jit(solution)/shard_map/ppermute | solution.py:27
  403.5 11.4 collective-permute-start.2
  422.3 11.9 %collective-permute-start.8 = (bf16[16,768]{1,0:T(8,128)(2,1)S(1)}, bf16[16,768]{1,0:T(8,128)(2,1)S(1)}, u32[]{:S(2)}, u32[]{:S(2)}) collective-permute-start(bf16[16,768]{1,0:T(8,128)(2,1)S(1)} %get-tuple-element.231), channel_id=1, source_target_pairs={{0,2},{1,3},{2,0},{3,1},{4,6},{5,7},{6,4},{7,5},{8,10},{9,11},{10,... | collective-permute-start | bytes 73736 | tf_op jit(solution)/shard_map/ppermute | solution.py:27
  470.8 33.4 %collective-permute-start.16 = (f32[8,3,64,128]{3,2,1,0:T(8,128)}, f32[8,3,64,128]{3,2,1,0:T(8,128)}, u32[]{:S(2)}, u32[]{:S(2)}) collective-permute-start(f32[8,3,64,128]{3,2,1,0:T(8,128)} %get-tuple-element.251), channel_id=1, source_target_pairs={{0,1},{1,0},{2,3},{3,2},{4,5},{5,4},{6,7},{7,6},{8,9},{9,8},{10,11... | collective-permute-start | bytes 2359304 | tf_op jit(solution)/shard_map/ppermute | solution.py:27
  517.8 10.0 collective-permute-start.18
  518.4 11.7 %collective-permute-start.19 = (f32[3,64,128]{2,1,0:T(8,128)S(1)}, f32[3,64,128]{2,1,0:T(8,128)S(1)}, u32[]{:S(2)}, u32[]{:S(2)}) collective-permute-start(f32[3,64,128]{2,1,0:T(8,128)S(1)} %get-tuple-element.268), channel_id=1, source_target_pairs={{0,6},{1,7},{2,4},{3,5},{4,2},{5,3},{6,0},{7,1},{8,14},{9,15},{10,... | collective-permute-start | bytes 294920 | tf_op jit(solution)/shard_map/ppermute | solution.py:27
  521.2 14.6 %collective-permute-start.20 = (f32[3,64,128]{2,1,0:T(8,128)S(1)}, f32[3,64,128]{2,1,0:T(8,128)S(1)}, u32[]{:S(2)}, u32[]{:S(2)}) collective-permute-start(f32[3,64,128]{2,1,0:T(8,128)S(1)} %get-tuple-element.267), channel_id=1, source_target_pairs={{0,8},{1,9},{2,10},{3,11},{4,12},{5,13},{6,14},{7,15},{8,0},{9,1},... | collective-permute-start | bytes 294920 | tf_op jit(solution)/shard_map/ppermute | solution.py:27
  523.5 14.5 %collective-permute-start.21 = (f32[3,64,128]{2,1,0:T(8,128)S(1)}, f32[3,64,128]{2,1,0:T(8,128)S(1)}, u32[]{:S(2)}, u32[]{:S(2)}) collective-permute-start(f32[3,64,128]{2,1,0:T(8,128)S(1)} %get-tuple-element.266), channel_id=1, source_target_pairs={{0,10},{1,11},{2,8},{3,9},{4,14},{5,15},{6,12},{7,13},{8,2},{9,3},... | collective-permute-start | bytes 294920 | tf_op jit(solution)/shard_map/ppermute | solution.py:27
  524.3 13.7 %collective-permute-start.22 = (f32[3,64,128]{2,1,0:T(8,128)S(1)}, f32[3,64,128]{2,1,0:T(8,128)S(1)}, u32[]{:S(2)}, u32[]{:S(2)}) collective-permute-start(f32[3,64,128]{2,1,0:T(8,128)S(1)} %get-tuple-element.265), channel_id=1, source_target_pairs={{0,12},{1,13},{2,14},{3,15},{4,8},{5,9},{6,10},{7,11},{8,4},{9,5},... | collective-permute-start | bytes 294920 | tf_op jit(solution)/shard_map/ppermute | solution.py:27
  527.8 10.2 collective-permute-start.23
  541.6 10.3 collective-permute-start.24
  543.5 11.4 collective-permute-start.25
  551.0 14.8 %collective-permute-start.28 = (f32[3,64,128]{2,1,0:T(8,128)S(1)}, f32[3,64,128]{2,1,0:T(8,128)S(1)}, u32[]{:S(2)}, u32[]{:S(2)}) collective-permute-start(f32[3,64,128]{2,1,0:T(8,128)S(1)} %get-tuple-element.226), channel_id=1, source_target_pairs={{0,10},{1,11},{2,8},{3,9},{4,14},{5,15},{6,12},{7,13},{8,2},{9,3},... | collective-permute-start | bytes 294920 | tf_op jit(solution)/shard_map/ppermute | solution.py:27
  551.9 14.5 %collective-permute-start.29 = (f32[3,64,128]{2,1,0:T(8,128)S(1)}, f32[3,64,128]{2,1,0:T(8,128)S(1)}, u32[]{:S(2)}, u32[]{:S(2)}) collective-permute-start(f32[3,64,128]{2,1,0:T(8,128)S(1)} %get-tuple-element.226), channel_id=1, source_target_pairs={{0,12},{1,13},{2,14},{3,15},{4,8},{5,9},{6,10},{7,11},{8,4},{9,5},... | collective-permute-start | bytes 294920 | tf_op jit(solution)/shard_map/ppermute | solution.py:27
  554.9 12.1 %collective-permute-start.30 = (f32[3,64,128]{2,1,0:T(8,128)S(1)}, f32[3,64,128]{2,1,0:T(8,128)S(1)}, u32[]{:S(2)}, u32[]{:S(2)}) collective-permute-start(f32[3,64,128]{2,1,0:T(8,128)S(1)} %get-tuple-element.226), channel_id=1, source_target_pairs={{0,14},{1,15},{2,12},{3,13},{4,10},{5,11},{6,8},{7,9},{8,6},{9,7},... | collective-permute-start | bytes 294920 | tf_op jit(solution)/shard_map/ppermute | solution.py:27
  567.7 12.3 %collective-permute-start.31 = (f32[8,3,64,128]{3,2,1,0:T(8,128)}, f32[8,3,64,128]{3,2,1,0:T(8,128)}, u32[]{:S(2)}, u32[]{:S(2)}) collective-permute-start(f32[8,3,64,128]{3,2,1,0:T(8,128)} %bitcast_dynamic-update-slice_fusion.8), channel_id=1, source_target_pairs={{0,1},{1,0},{2,3},{3,2},{4,5},{5,4},{6,7},{7,6},{8,9},{9,8},{10,11... | collective-permute-start | bytes 2359304 | tf_op jit(solution)/shard_map/ppermute | solution.py:27
  716.2 24.7 %collective-permute-start.50 = (bf16[16,768]{1,0:T(8,128)(2,1)}, bf16[16,768]{1,0:T(8,128)(2,1)}, u32[]{:S(2)}, u32[]{:S(2)}) collective-permute-start(bf16[16,768]{1,0:T(8,128)(2,1)} %get-tuple-element.248), channel_id=1, source_target_pairs={{0,1},{1,2},{2,3},{3,4},{4,5},{5,6},{6,7},{7,8},{8,9},{9,10},{10,1... | collective-permute-start | bytes 73736 | tf_op jit(solution)/shard_map/ppermute | solution.py:109
  719.4 21.5 %collective-permute-start.51 = (bf16[16,768]{1,0:T(8,128)(2,1)}, bf16[16,768]{1,0:T(8,128)(2,1)}, u32[]{:S(2)}, u32[]{:S(2)}) collective-permute-start(bf16[16,768]{1,0:T(8,128)(2,1)} %get-tuple-element.247), channel_id=1, source_target_pairs={{1,0},{2,1},{3,2},{4,3},{5,4},{6,5},{7,6},{8,7},{9,8},{10,9},{11,1... | collective-permute-start | bytes 73736 | tf_op jit(solution)/shard_map/ppermute | solution.py:111
  735.2 26.1 %collective-permute-start.34 = (bf16[8,3,64,64]{3,2,1,0:T(8,128)(2,1)}, bf16[8,3,64,64]{3,2,1,0:T(8,128)(2,1)}, u32[]{:S(2)}, u32[]{:S(2)}) collective-permute-start(bf16[8,3,64,64]{3,2,1,0:T(8,128)(2,1)} %fusion.104), channel_id=1, source_target_pairs={{0,1},{1,0},{2,3},{3,2},{4,5},{5,4},{6,7},{7,6},{8,9},{9,8},{10,11... | collective-permute-start | bytes 589832 | tf_op jit(solution)/shard_map/ppermute | solution.py:27
  762.5 11.9 %collective-permute-start.35 = (bf16[3,64,64]{2,1,0:T(8,128)(2,1)S(1)}, bf16[3,64,64]{2,1,0:T(8,128)(2,1)S(1)}, u32[]{:S(2)}, u32[]{:S(2)}) collective-permute-start(bf16[3,64,64]{2,1,0:T(8,128)(2,1)S(1)} %get-tuple-element.273), channel_id=1, source_target_pairs={{0,2},{1,3},{2,0},{3,1},{4,6},{5,7},{6,4},{7,5},{8,10},{9,11},{10,... | collective-permute-start | bytes 73736 | tf_op jit(solution)/shard_map/ppermute | solution.py:27
  765.2 10.7 collective-permute-start.36
  769.6 14.3 %collective-permute-start.37 = (bf16[3,64,64]{2,1,0:T(8,128)(2,1)S(1)}, bf16[3,64,64]{2,1,0:T(8,128)(2,1)S(1)}, u32[]{:S(2)}, u32[]{:S(2)}) collective-permute-start(bf16[3,64,64]{2,1,0:T(8,128)(2,1)S(1)} %get-tuple-element.278), channel_id=1, source_target_pairs={{0,6},{1,7},{2,4},{3,5},{4,2},{5,3},{6,0},{7,1},{8,14},{9,15},{10,... | collective-permute-start | bytes 73736 | tf_op jit(solution)/shard_map/ppermute | solution.py:27
  771.1 13.0 %collective-permute-start.38 = (bf16[3,64,64]{2,1,0:T(8,128)(2,1)S(1)}, bf16[3,64,64]{2,1,0:T(8,128)(2,1)S(1)}, u32[]{:S(2)}, u32[]{:S(2)}) collective-permute-start(bf16[3,64,64]{2,1,0:T(8,128)(2,1)S(1)} %get-tuple-element.277), channel_id=1, source_target_pairs={{0,8},{1,9},{2,10},{3,11},{4,12},{5,13},{6,14},{7,15},{8,0},{9,1},... | collective-permute-start | bytes 73736 | tf_op jit(solution)/shard_map/ppermute | solution.py:27
  773.5 11.0 collective-permute-start.39
  774.4 10.2 collective-permute-start.40
  783.9 172.2 %collective-permute-start.103 = (bf16[1536,768]{1,0:T(8,128)(2,1)}, bf16[1536,768]{1,0:T(8,128)(2,1)}, u32[]{:S(2)}, u32[]{:S(2)}) collective-permute-start(bf16[1536,768]{1,0:T(8,128)(2,1)} %dynamic-slice_convert_fusion), channel_id=1, source_target_pairs={{0,1},{1,0},{2,3},{3,2},{4,5},{5,4},{6,7},{7,6},{8,9},{9,8},{10,11... | collective-permute-start | bytes 7077896 | tf_op jit(solution)/shard_map/ppermute | solution.py:27
  784.0 178.0 %collective-permute-start.93 = (bf16[384,3072]{1,0:T(8,128)(2,1)}, bf16[384,3072]{1,0:T(8,128)(2,1)}, u32[]{:S(2)}, u32[]{:S(2)}) collective-permute-start(bf16[384,3072]{1,0:T(8,128)(2,1)} %dynamic-slice_convert_fusion.1), channel_id=1, source_target_pairs={{0,1},{1,0},{2,3},{3,2},{4,5},{5,4},{6,7},{7,6},{8,9},{9,8},{10,11... | collective-permute-start | bytes 7077896 | tf_op jit(solution)/shard_map/ppermute | solution.py:27
  784.5 40.9 %collective-permute-start.83 = (bf16[384,768]{1,0:T(8,128)(2,1)}, bf16[384,768]{1,0:T(8,128)(2,1)}, u32[]{:S(2)}, u32[]{:S(2)}) collective-permute-start(bf16[384,768]{1,0:T(8,128)(2,1)} %dynamic-slice_convert_fusion.3), channel_id=1, source_target_pairs={{0,1},{1,0},{2,3},{3,2},{4,5},{5,4},{6,7},{7,6},{8,9},{9,8},{10,11... | collective-permute-start | bytes 1769480 | tf_op jit(solution)/shard_map/ppermute | solution.py:27
  801.6 12.6 %collective-permute-start.43 = (f32[3,64,128]{2,1,0:T(8,128)}, f32[3,64,128]{2,1,0:T(8,128)}, u32[]{:S(2)}, u32[]{:S(2)}) collective-permute-start(f32[3,64,128]{2,1,0:T(8,128)} %get-tuple-element.224), channel_id=1, source_target_pairs={{0,4},{1,5},{2,6},{3,7},{4,0},{5,1},{6,2},{7,3},{8,12},{9,13},{10,... | collective-permute-start | bytes 294920 | tf_op jit(solution)/shard_map/ppermute | solution.py:27
  816.5 12.3 %collective-permute-start.46 = (f32[3,64,128]{2,1,0:T(8,128)}, f32[3,64,128]{2,1,0:T(8,128)S(1)}, u32[]{:S(2)}, u32[]{:S(2)}) collective-permute-start(f32[3,64,128]{2,1,0:T(8,128)} %get-tuple-element.224), channel_id=1, source_target_pairs={{0,10},{1,11},{2,8},{3,9},{4,14},{5,15},{6,12},{7,13},{8,2},{9,3},... | collective-permute-start | bytes 294920 | tf_op jit(solution)/shard_map/ppermute | solution.py:27
  825.4 15.3 %collective-permute-start.48 = (f32[3,64,128]{2,1,0:T(8,128)}, f32[3,64,128]{2,1,0:T(8,128)S(1)}, u32[]{:S(2)}, u32[]{:S(2)}) collective-permute-start(f32[3,64,128]{2,1,0:T(8,128)} %get-tuple-element.224), channel_id=1, source_target_pairs={{0,14},{1,15},{2,12},{3,13},{4,10},{5,11},{6,8},{7,9},{8,6},{9,7},... | collective-permute-start | bytes 294920 | tf_op jit(solution)/shard_map/ppermute | solution.py:27
  828.8 10.2 collective-permute-start.84
  841.3 12.8 %collective-permute-start.49 = (f32[8,3,64,128]{3,2,1,0:T(8,128)}, f32[8,3,64,128]{3,2,1,0:T(8,128)}, u32[]{:S(2)}, u32[]{:S(2)}) collective-permute-start(f32[8,3,64,128]{3,2,1,0:T(8,128)} %bitcast_dynamic-update-slice_fusion), channel_id=1, source_target_pairs={{0,1},{1,0},{2,3},{3,2},{4,5},{5,4},{6,7},{7,6},{8,9},{9,8},{10,11... | collective-permute-start | bytes 2359304 | tf_op jit(solution)/shard_map/ppermute | solution.py:27
  852.4 44.9 %collective-permute-start.87 = (bf16[24,768]{1,0:T(8,128)(2,1)}, bf16[24,768]{1,0:T(8,128)(2,1)}, u32[]{:S(2)}, u32[]{:S(2)}) collective-permute-start(bf16[24,768]{1,0:T(8,128)(2,1)} %constant_dynamic-slice_fusion.7), channel_id=1, source_target_pairs={{0,8},{1,9},{2,10},{3,11},{4,12},{5,13},{6,14},{7,15},{8,0},{9,1},... | collective-permute-start | bytes 110600 | tf_op jit(solution)/shard_map/ppermute | solution.py:27
  882.2 13.4 %collective-permute-start.78 = (f32[80,128]{1,0:T(8,128)S(1)}, f32[80,128]{1,0:T(8,128)S(1)}, u32[]{:S(2)}, u32[]{:S(2)}) collective-permute-start(f32[80,128]{1,0:T(8,128)S(1)} %pad_bitcast_fusion), channel_id=1, source_target_pairs={{0,1},{1,0},{2,3},{3,2},{4,5},{5,4},{6,7},{7,6},{8,9},{9,8},{10,11... | collective-permute-start | bytes 122888 | tf_op jit(solution)/shard_map/ppermute | solution.py:27
  886.3 22.9 %collective-permute-start.52 = (bf16[8,16,768]{2,1,0:T(8,128)(2,1)S(1)}, bf16[8,16,768]{2,1,0:T(8,128)(2,1)S(1)}, u32[]{:S(2)}, u32[]{:S(2)}) collective-permute-start(bf16[8,16,768]{2,1,0:T(8,128)(2,1)S(1)} %fusion.109), channel_id=1, source_target_pairs={{0,1},{1,0},{2,3},{3,2},{4,5},{5,4},{6,7},{7,6},{8,9},{9,8},{10,11... | collective-permute-start | bytes 589832 | tf_op jit(solution)/shard_map/ppermute | solution.py:27
  905.5 14.3 %collective-permute-start.89 = (bf16[48,768]{1,0:T(8,128)(2,1)S(1)}, bf16[48,768]{1,0:T(8,128)(2,1)S(1)}, u32[]{:S(2)}, u32[]{:S(2)}) collective-permute-start(bf16[48,768]{1,0:T(8,128)(2,1)S(1)} %maximum_select_fusion.19), channel_id=1, source_target_pairs={{0,4},{1,5},{2,6},{3,7},{4,0},{5,1},{6,2},{7,3},{8,12},{9,13},{10,... | collective-permute-start | bytes 221192 | tf_op jit(solution)/shard_map/ppermute | solution.py:27
  907.9 12.5 %collective-permute-start.82 = (f32[80,128]{1,0:T(8,128)S(1)}, f32[80,128]{1,0:T(8,128)S(1)}, u32[]{:S(2)}, u32[]{:S(2)}) collective-permute-start(f32[80,128]{1,0:T(8,128)S(1)} %add.821), channel_id=1, source_target_pairs={{0,8},{1,9},{2,10},{3,11},{4,12},{5,13},{6,14},{7,15},{8,0},{9,1},... | collective-permute-start | bytes 122888 | tf_op jit(solution)/shard_map/ppermute | solution.py:27
  909.3 12.6 %collective-permute-start.53 = (bf16[16,768]{1,0:T(8,128)(2,1)S(1)}, bf16[16,768]{1,0:T(8,128)(2,1)S(1)}, u32[]{:S(2)}, u32[]{:S(2)}) collective-permute-start(bf16[16,768]{1,0:T(8,128)(2,1)S(1)} %get-tuple-element.282), channel_id=1, source_target_pairs={{0,2},{1,3},{2,0},{3,1},{4,6},{5,7},{6,4},{7,5},{8,10},{9,11},{10,... | collective-permute-start | bytes 73736 | tf_op jit(solution)/shard_map/ppermute | solution.py:27
  931.8 34.4 %collective-permute-start.68 = (bf16[384,2304]{1,0:T(8,128)(2,1)S(1)}, bf16[384,2304]{1,0:T(8,128)(2,1)S(1)}, u32[]{:S(2)}, u32[]{:S(2)}) collective-permute-start(bf16[384,2304]{1,0:T(8,128)(2,1)S(1)} %dynamic-slice_convert_fusion.2), channel_id=1, source_target_pairs={{0,1},{1,0},{2,3},{3,2},{4,5},{5,4},{6,7},{7,6},{8,9},{9,8},{10,11... | collective-permute-start | bytes 5308424 | tf_op jit(solution)/shard_map/ppermute | solution.py:27
  933.6 189.8 %collective-permute-start.90 = (bf16[96,768]{1,0:T(8,128)(2,1)S(1)}, bf16[96,768]{1,0:T(8,128)(2,1)S(1)}, u32[]{:S(2)}, u32[]{:S(2)}) collective-permute-start(bf16[96,768]{1,0:T(8,128)(2,1)S(1)} %maximum_select_fusion.18), channel_id=1, source_target_pairs={{0,16},{16,0},{1,17},{17,1},{2,18},{18,2},{3,19},{19,3},{4,20},{20... | collective-permute-start | bytes 442376 | tf_op jit(solution)/shard_map/ppermute | solution.py:27
  954.4 122.4 %collective-permute-start.64 = (bf16[16,768]{1,0:T(8,128)(2,1)S(1)}, bf16[16,768]{1,0:T(8,128)(2,1)S(1)}, u32[]{:S(2)}, u32[]{:S(2)}) collective-permute-start(bf16[16,768]{1,0:T(8,128)(2,1)S(1)} %get-tuple-element.216), channel_id=1, source_target_pairs={{0,10},{1,11},{2,8},{3,9},{4,14},{5,15},{6,12},{7,13},{8,2},{9,3},... | collective-permute-start | bytes 73736 | tf_op jit(solution)/shard_map/ppermute | solution.py:27
  956.1 143.7 %collective-permute-start.65 = (bf16[16,768]{1,0:T(8,128)(2,1)S(1)}, bf16[16,768]{1,0:T(8,128)(2,1)S(1)}, u32[]{:S(2)}, u32[]{:S(2)}) collective-permute-start(bf16[16,768]{1,0:T(8,128)(2,1)S(1)} %get-tuple-element.216), channel_id=1, source_target_pairs={{0,12},{1,13},{2,14},{3,15},{4,8},{5,9},{6,10},{7,11},{8,4},{9,5},... | collective-permute-start | bytes 73736 | tf_op jit(solution)/shard_map/ppermute | solution.py:27
  962.0 26.2 %collective-permute-start.104 = (bf16[768,768]{1,0:T(8,128)(2,1)S(1)}, bf16[768,768]{1,0:T(8,128)(2,1)S(1)}, u32[]{:S(2)}, u32[]{:S(2)}) collective-permute-start(bf16[768,768]{1,0:T(8,128)(2,1)S(1)} %constant_dynamic-slice_fusion.2), channel_id=1, source_target_pairs={{0,16},{16,0},{1,17},{17,1},{2,18},{18,2},{3,19},{19,3},{4,20},{20... | collective-permute-start | bytes 3538952 | tf_op jit(solution)/shard_map/ppermute | solution.py:27
  966.3 26.2 %collective-permute-start.94 = (bf16[192,3072]{1,0:T(8,128)(2,1)S(1)}, bf16[192,3072]{1,0:T(8,128)(2,1)S(1)}, u32[]{:S(2)}, u32[]{:S(2)}) collective-permute-start(bf16[192,3072]{1,0:T(8,128)(2,1)S(1)} %constant_dynamic-slice_fusion.6), channel_id=1, source_target_pairs={{0,2},{1,3},{2,0},{3,1},{4,6},{5,7},{6,4},{7,5},{8,10},{9,11},{10,... | collective-permute-start | bytes 3538952 | tf_op jit(solution)/shard_map/ppermute | solution.py:27
  988.2 19.7 %collective-permute-start.69 = (bf16[192,2304]{1,0:T(8,128)(2,1)S(1)}, bf16[192,2304]{1,0:T(8,128)(2,1)S(1)}, u32[]{:S(2)}, u32[]{:S(2)}) collective-permute-start(bf16[192,2304]{1,0:T(8,128)(2,1)S(1)} %constant_dynamic-slice_fusion.14), channel_id=1, source_target_pairs={{0,16},{16,0},{1,17},{17,1},{2,18},{18,2},{3,19},{19,3},{4,20},{20... | collective-permute-start | bytes 2654216 | tf_op jit(solution)/shard_map/ppermute | solution.py:27
  992.5 16.5 %collective-permute-start.105 = (bf16[384,768]{1,0:T(8,128)(2,1)S(1)}, bf16[384,768]{1,0:T(8,128)(2,1)S(1)}, u32[]{:S(2)}, u32[]{:S(2)}) collective-permute-start(bf16[384,768]{1,0:T(8,128)(2,1)S(1)} %constant_dynamic-slice_fusion.1), channel_id=1, source_target_pairs={{0,2},{1,3},{2,0},{3,1},{4,6},{5,7},{6,4},{7,5},{8,10},{9,11},{10,... | collective-permute-start | bytes 1769480 | tf_op jit(solution)/shard_map/ppermute | solution.py:27
  1018.8 12.6 %collective-permute-start.96 = (bf16[48,3072]{1,0:T(8,128)(2,1)S(1)}, bf16[48,3072]{1,0:T(8,128)(2,1)S(1)}, u32[]{:S(2)}, u32[]{:S(2)}) collective-permute-start(bf16[48,3072]{1,0:T(8,128)(2,1)S(1)} %constant_dynamic-slice_fusion.4), channel_id=1, source_target_pairs={{0,4},{1,5},{2,6},{3,7},{4,0},{5,1},{6,2},{7,3},{8,12},{9,13},{10,... | collective-permute-start | bytes 884744 | tf_op jit(solution)/shard_map/ppermute | solution.py:27
  1031.4 15.2 %collective-permute-start.107 = (bf16[96,768]{1,0:T(8,128)(2,1)S(1)}, bf16[96,768]{1,0:T(8,128)(2,1)S(1)}, u32[]{:S(2)}, u32[]{:S(2)}) collective-permute-start(bf16[96,768]{1,0:T(8,128)(2,1)S(1)} %constant_dynamic-slice_fusion.23), channel_id=1, source_target_pairs={{0,8},{1,9},{2,10},{3,11},{4,12},{5,13},{6,14},{7,15},{8,0},{9,1},... | collective-permute-start | bytes 442376 | tf_op jit(solution)/shard_map/ppermute | solution.py:27
  1035.6 11.0 collective-permute-start.72
  1071.9 13.1 %collective-permute-start.75 = (bf16[96,2304]{1,0:T(8,128)(2,1)S(1)}, bf16[96,2304]{1,0:T(8,128)(2,1)S(1)}, u32[]{:S(2)}, u32[]{:S(2)}) collective-permute-start(bf16[96,2304]{1,0:T(8,128)(2,1)S(1)} %maximum_select_fusion.13), channel_id=1, source_target_pairs={{0,2},{1,3},{2,0},{3,1},{4,6},{5,7},{6,4},{7,5},{8,10},{9,11},{10,... | collective-permute-start | bytes 1327112 | tf_op jit(solution)/shard_map/ppermute | solution.py:27
  1075.5 21.6 %collective-permute-start.110 = (bf16[384,768]{1,0:T(8,128)(2,1)S(1)}, bf16[384,768]{1,0:T(8,128)(2,1)S(1)}, u32[]{:S(2)}, u32[]{:S(2)}) collective-permute-start(bf16[384,768]{1,0:T(8,128)(2,1)S(1)} %maximum_select_fusion.12), channel_id=1, source_target_pairs={{0,2},{1,3},{2,0},{3,1},{4,6},{5,7},{6,4},{7,5},{8,10},{9,11},{10,... | collective-permute-start | bytes 1769480 | tf_op jit(solution)/shard_map/ppermute | solution.py:27
  1076.8 21.3 %collective-permute-start.100 = (bf16[96,3072]{1,0:T(8,128)(2,1)S(1)}, bf16[96,3072]{1,0:T(8,128)(2,1)S(1)}, u32[]{:S(2)}, u32[]{:S(2)}) collective-permute-start(bf16[96,3072]{1,0:T(8,128)(2,1)S(1)} %maximum_select_fusion.11), channel_id=1, source_target_pairs={{0,16},{16,0},{1,17},{17,1},{2,18},{18,2},{3,19},{19,3},{4,20},{20... | collective-permute-start | bytes 1769480 | tf_op jit(solution)/shard_map/ppermute | solution.py:27
  1085.0 16.6 %collective-permute-start.66 = (bf16[16,768]{1,0:T(8,128)(2,1)S(1)}, bf16[16,768]{1,0:T(8,128)(2,1)S(1)}, u32[]{:S(2)}, u32[]{:S(2)}) collective-permute-start(bf16[16,768]{1,0:T(8,128)(2,1)S(1)} %get-tuple-element.216), channel_id=1, source_target_pairs={{0,14},{1,15},{2,12},{3,13},{4,10},{5,11},{6,8},{7,9},{8,6},{9,7},... | collective-permute-start | bytes 73736 | tf_op jit(solution)/shard_map/ppermute | solution.py:27
  1097.0 13.0 %collective-permute-start.76 = (bf16[192,2304]{1,0:T(8,128)(2,1)S(1)}, bf16[192,2304]{1,0:T(8,128)(2,1)S(1)}, u32[]{:S(2)}, u32[]{:S(2)}) collective-permute-start(bf16[192,2304]{1,0:T(8,128)(2,1)S(1)} %maximum_select_fusion.9), channel_id=1, source_target_pairs={{0,16},{16,0},{1,17},{17,1},{2,18},{18,2},{3,19},{19,3},{4,20},{20... | collective-permute-start | bytes 2654216 | tf_op jit(solution)/shard_map/ppermute | solution.py:27
  1098.1 24.6 %collective-permute-start.111 = (bf16[768,768]{1,0:T(8,128)(2,1)S(1)}, bf16[768,768]{1,0:T(8,128)(2,1)S(1)}, u32[]{:S(2)}, u32[]{:S(2)}) collective-permute-start(bf16[768,768]{1,0:T(8,128)(2,1)S(1)} %maximum_select_fusion.8), channel_id=1, source_target_pairs={{0,16},{16,0},{1,17},{17,1},{2,18},{18,2},{3,19},{19,3},{4,20},{20... | collective-permute-start | bytes 3538952 | tf_op jit(solution)/shard_map/ppermute | solution.py:27
  1099.8 25.4 %collective-permute-start.101 = (bf16[192,3072]{1,0:T(8,128)(2,1)S(1)}, bf16[192,3072]{1,0:T(8,128)(2,1)S(1)}, u32[]{:S(2)}, u32[]{:S(2)}) collective-permute-start(bf16[192,3072]{1,0:T(8,128)(2,1)S(1)} %maximum_select_fusion.7), channel_id=1, source_target_pairs={{0,2},{1,3},{2,0},{3,1},{4,6},{5,7},{6,4},{7,5},{8,10},{9,11},{10,... | collective-permute-start | bytes 3538952 | tf_op jit(solution)/shard_map/ppermute | solution.py:27
  1102.2 33.2 %collective-permute-start.67 = (bf16[8,16,768]{2,1,0:T(8,128)(2,1)}, bf16[8,16,768]{2,1,0:T(8,128)(2,1)}, u32[]{:S(2)}, u32[]{:S(2)}) collective-permute-start(bf16[8,16,768]{2,1,0:T(8,128)(2,1)} %constant_dynamic-update-slice_fusion.16), channel_id=1, source_target_pairs={{0,1},{1,0},{2,3},{3,2},{4,5},{5,4},{6,7},{7,6},{8,9},{9,8},{10,11... | collective-permute-start | bytes 589832 | tf_op jit(solution)/shard_map/ppermute | solution.py:27
  1111.8 35.6 %collective-permute-start.77 = (bf16[384,2304]{1,0:T(8,128)(2,1)}, bf16[384,2304]{1,0:T(8,128)(2,1)}, u32[]{:S(2)}, u32[]{:S(2)}) collective-permute-start(bf16[384,2304]{1,0:T(8,128)(2,1)} %maximum_select_fusion.5), channel_id=1, source_target_pairs={{0,1},{1,0},{2,3},{3,2},{4,5},{5,4},{6,7},{7,6},{8,9},{9,8},{10,11... | collective-permute-start | bytes 5308424 | tf_op jit(solution)/shard_map/ppermute | solution.py:27
  1123.3 29.5 %collective-permute-start.112 = (bf16[1536,768]{1,0:T(8,128)(2,1)S(1)}, bf16[1536,768]{1,0:T(8,128)(2,1)}, u32[]{:S(2)}, u32[]{:S(2)}) collective-permute-start(bf16[1536,768]{1,0:T(8,128)(2,1)S(1)} %maximum_select_fusion.4), channel_id=1, source_target_pairs={{0,1},{1,0},{2,3},{3,2},{4,5},{5,4},{6,7},{7,6},{8,9},{9,8},{10,11... | collective-permute-start | bytes 7077896 | tf_op jit(solution)/shard_map/ppermute | solution.py:27
  1127.4 31.4 %collective-permute-start.102 = (bf16[384,3072]{1,0:T(8,128)(2,1)}, bf16[384,3072]{1,0:T(8,128)(2,1)}, u32[]{:S(2)}, u32[]{:S(2)}) collective-permute-start(bf16[384,3072]{1,0:T(8,128)(2,1)} %maximum_select_fusion.3), channel_id=1, source_target_pairs={{0,1},{1,0},{2,3},{3,2},{4,5},{5,4},{6,7},{7,6},{8,9},{9,8},{10,11... | collective-permute-start | bytes 7077896 | tf_op jit(solution)/shard_map/ppermute | solution.py:27
  (247 other events, 2930.8 us)

commit v2 on v1

v2 whole, which is shorter than its diff:
```python
import math

import jax
import jax.numpy as jnp
from jax import lax
from jax.experimental import pallas as pl
from jax.experimental.pallas import tpu as pltpu
from jax.sharding import PartitionSpec as P

LAND = 64
NS_ITERS = 6
HIGH = lax.Precision.HIGHEST
NEGATIVE = -1e30
BF = jnp.bfloat16
F32 = jnp.float32

T_W = BF
T_INV = BF
P_INV = lax.Precision.DEFAULT
BLOCK = 256
GROUP = 256
SUB = 128
TAPS = 33


def swap(array, axis, bit):
    count = lax.axis_size(axis)
    return lax.ppermute(array, axis, [(i, i ^ bit) for i in range(count)])


def add_parts(parts):
    total = parts[0].astype(F32)
    for part in parts[1:]:
        total = total + part.astype(F32)
    return total


def halves(array, bit):
    rows = array.shape[0] // 2
    side = (lax.axis_index("seq") // bit) % 2
    mine = lax.dynamic_slice_in_dim(array, side * rows, rows, 0)
    other = lax.dynamic_slice_in_dim(array, (1 - side) * rows, rows, 0)
    return mine, other


def seq_total(array, join):
    bits = [1 << i for i in range(lax.axis_size("seq").bit_length() - 1)]
    for bit in bits[:2]:
        mine, other = halves(array, bit)
        array = join(mine, swap(other, "seq", bit))
    for bit in bits[2:]:
        array = join(array, swap(array, "seq", bit))
    for bit in reversed(bits[:2]):
        other = swap(array, "seq", bit)
        side = (lax.axis_index("seq") // bit) % 2
        array = jnp.where(
            side == 0,
            jnp.concatenate([array, other], 0),
            jnp.concatenate([other, array], 0),
        )
    return array


def add_join(first, second):
    return (first.astype(F32) + second.astype(F32)).astype(BF)


def stages(first):
    seq_bits = [("seq", 1 << i) for i in range(1, lax.axis_size("seq").bit_length() - 1)]
    row_bits = [("row", 1 << i) for i in range(lax.axis_size("row").bit_length() - 1)]
    rest = row_bits + seq_bits if first == "row" else seq_bits[:1] + row_bits + seq_bits[1:]
    return [("seq", 1)] + rest


def all_sum(array, first):
    plan = stages(first)
    held = array
    for axis, bit in plan:
        half = held.shape[0] // 2
        side = (lax.axis_index(axis) // bit) % 2
        mine = lax.dynamic_slice_in_dim(held, side * half, half, 0)
        other = lax.dynamic_slice_in_dim(held, (1 - side) * half, half, 0)
        held = mine.astype(F32) + swap(other.astype(T_W), axis, bit).astype(F32)
        held = held.astype(T_W)
    for axis, bit in reversed(plan):
        half = held.shape[0]
        side = (lax.axis_index(axis) // bit) % 2
        other = swap(held, axis, bit)
        held = jnp.where(
            side == 0,
            jnp.concatenate([held, other], 0),
            jnp.concatenate([other, held], 0),
        )
    return held.astype(F32)


def small_sum(array):
    for axis, bit in stages("row"):
        array = array + swap(array, axis, bit)
    return array


def extended(cells, width, rows):
    count = lax.axis_size("seq")
    head = cells[:width]
    tail = cells[-width:]
    return jnp.concatenate(
        [
            lax.ppermute(tail, "seq", [(i, i + 1) for i in range(count - 1)]),
            cells,
            lax.ppermute(head, "seq", [(i + 1, i) for i in range(count - 1)]),
            jnp.zeros((rows - cells.shape[0] - 2 * width, cells.shape[1]), cells.dtype),
        ],
        axis=0,
    )


def dot_nn(a, b):
    return jnp.dot(a, b, preferred_element_type=F32)


def dot_nt(a, b):
    return lax.dot_general(a, b, (((1,), (1,)), ((), ())), preferred_element_type=F32)


def dot_tn(a, b):
    return lax.dot_general(a, b, (((0,), (0,)), ((), ())), preferred_element_type=F32)


def iota(shape, dim):
    return lax.broadcasted_iota(jnp.int32, shape, dim)


def spread(block):
    rows = block.shape[0]
    tall = jnp.concatenate([block] * 4, axis=0).astype(F32)
    shape = (4 * rows, GROUP)
    keep = iota(shape, 0) // rows == iota(shape, 1) // LAND
    return jnp.where(keep, tall, 0.0).astype(BF)


def gathered(square):
    rows = square.shape[0] // 4
    lane = iota((rows, GROUP), 1) // LAND
    out = square[:rows]
    for head in range(1, 4):
        out = jnp.where(lane == head, square[head * rows : (head + 1) * rows], out)
    return out


def by_head(columns, first, shape):
    lane = iota(shape, 1)
    out = jnp.zeros(shape, F32)
    for head, column in enumerate(columns):
        out = jnp.where((lane % 16 == first + head) & (lane < 48), column, out)
    return out


def split_three(cells):
    lane = iota(cells.shape, 1)
    high = cells.astype(BF).astype(F32)
    mid = (cells - high).astype(BF).astype(F32)
    low = cells - high - mid
    return jnp.where(lane < 16, high, jnp.where(lane < 32, mid, low)).astype(BF)


def merge_three(cells):
    cells = cells.astype(F32)
    return cells + pltpu.roll(cells, 112, 1) + pltpu.roll(cells, 96, 1)


def head_lanes(heads, width):
    return (iota((128, width), 0) == iota((128, width), 1) // LAND).astype(F32)


def doc_of(places, bounds, docs):
    out = (places >= bounds[2 * docs - 1]).astype(jnp.int32)
    for doc in range(docs):
        out = out + (places >= bounds[doc]).astype(jnp.int32)
    return out


def landmark_kernel(docs, scale, bounds, mq_ref, k_ref, v_ref, out_ref, max_s, sum_s, acc_s):
    tokens, width = k_ref.shape
    groups = width // GROUP
    heads = width // LAND
    out_ref[:, :width] = jnp.zeros((docs * LAND, width), BF)
    empty = jnp.full((docs * LAND, 128), NEGATIVE, F32)
    out_ref[:, width:] = jnp.where(iota(empty.shape, 1) < 48, split_three(empty).astype(F32), 0.0).astype(BF)
    for doc in range(docs):
        low = jnp.clip(bounds[doc], 0, tokens)
        high = jnp.clip(bounds[docs + doc], 0, tokens)
        rows = slice(doc * LAND, (doc + 1) * LAND)

        @pl.when(high > low)
        def _():
            max_s[...] = jnp.full(max_s.shape, NEGATIVE, F32)
            sum_s[...] = jnp.zeros(sum_s.shape, F32)
            acc_s[...] = jnp.zeros(acc_s.shape, F32)
            wide = [
                spread(mq_ref[rows, g * GROUP : (g + 1) * GROUP]) for g in range(groups)
            ]

            def step(block, carry):
                first = pl.multiple_of(block * BLOCK, BLOCK)
                at = pl.ds(first, BLOCK)
                place = iota((1, BLOCK), 1) + first
                valid = (place >= low) & (place < high)
                for g in range(groups):
                    cols = slice(g * GROUP, (g + 1) * GROUP)
                    scores = dot_nt(wide[g], k_ref[at, cols]) * scale
                    scores = jnp.where(valid, scores, NEGATIVE)
                    old = max_s[cols, :1]
                    top = jnp.maximum(old, jnp.max(scores, axis=1, keepdims=True))
                    weights = jnp.exp(scores - top)
                    shrink = jnp.exp(old - top)
                    sums = sum_s[cols, :1] * shrink + jnp.sum(weights, axis=1, keepdims=True)
                    acc_s[cols, :] = acc_s[cols, :] * shrink + dot_nn(
                        weights.astype(BF), v_ref[at, cols]
                    )
                    max_s[cols, :] = jnp.broadcast_to(top, (GROUP, 128))
                    sum_s[cols, :] = jnp.broadcast_to(sums, (GROUP, 128))
                return carry

            lax.fori_loop(low // BLOCK, (high + BLOCK - 1) // BLOCK, step, 0)
            columns = []
            for g in range(groups):
                cols = slice(g * GROUP, (g + 1) * GROUP)
                sums = sum_s[cols, :1]
                out_ref[rows, cols] = gathered(acc_s[cols, :] / sums).astype(BF)
                level = max_s[cols, :1] + jnp.log(sums)
                columns += [level[h * LAND : (h + 1) * LAND] for h in range(4)]
            out_ref[rows, width:] = split_three(by_head(columns, 0, (LAND, 128)))


def join_kernel(a_ref, b_ref, out_ref):
    width = a_ref.shape[1] - 128
    heads = width // LAND
    first, second = merge_three(a_ref[:, width:]), merge_three(b_ref[:, width:])
    lane = iota(first.shape, 1)
    first = jnp.where(lane < heads, first, 0.0)
    second = jnp.where(lane < heads, second, 0.0)
    top = jnp.maximum(first, second)
    exp_a, exp_b = jnp.exp(first - top), jnp.exp(second - top)
    both = exp_a + exp_b
    level = top + jnp.log(both)
    pick = head_lanes(heads, width)
    share_a = jnp.dot(exp_a / both, pick, precision=HIGH, preferred_element_type=F32)
    share_b = jnp.dot(exp_b / both, pick, precision=HIGH, preferred_element_type=F32)
    joined = a_ref[:, :width].astype(F32) * share_a + b_ref[:, :width].astype(F32) * share_b
    out_ref[:, :width] = joined.astype(BF)
    level = jnp.where(lane < heads, level, 0.0)
    level = level + pltpu.roll(level, 16, 1) + pltpu.roll(level, 32, 1)
    out_ref[:, width:] = split_three(level)


def join(first, second):
    return pl.pallas_call(
        join_kernel, out_shape=jax.ShapeDtypeStruct(first.shape, BF), name="join"
    )(first, second)


def mix_kernel(docs, inv_ref, stat_ref, mix_ref, level_ref):
    width = inv_ref.shape[1]
    for doc in range(docs):
        rows = slice(doc * LAND, (doc + 1) * LAND)
        for g in range(width // GROUP):
            cols = slice(g * GROUP, (g + 1) * GROUP)
            mix_ref[rows, cols] = dot_nn(
                inv_ref[rows, cols].astype(BF), spread(stat_ref[rows, cols])
            ).astype(BF)
    level_ref[...] = merge_three(stat_ref[:, width:])


def mix_back_kernel(docs, inv_ref, stat_ref, grad_ref, out_ref, dots_ref):
    width = inv_ref.shape[1]
    pick = (iota((width, 128), 1) == iota((width, 128), 0) // LAND).astype(BF)
    for doc in range(docs):
        rows = slice(doc * LAND, (doc + 1) * LAND)
        dots = jnp.zeros((LAND, 128), F32)
        for g in range(width // GROUP):
            cols = slice(g * GROUP, (g + 1) * GROUP)
            grad = gathered(dot_tn(inv_ref[rows, cols].astype(BF), grad_ref[rows, cols]))
            out_ref[rows, cols] = grad.astype(BF)
            product = grad * stat_ref[rows, cols].astype(F32)
            high = product.astype(BF)
            low = (product - high.astype(F32)).astype(BF)
            dots = dots + dot_nn(high, pick[cols]) + dot_nn(low, pick[cols])
        dots_ref[rows, :] = dots


def make_band(taps_ref, band_s):
    for head in range(taps_ref.shape[0]):
        row = jnp.broadcast_to(taps_ref[head : head + 1, :], (SUB, GROUP))
        band_s[head * SUB : (head + 1) * SUB, :] = pltpu.roll(row, 0, 1, stride=1, stride_axis=0).astype(BF)


def same_doc(first, bounds, docs, radius):
    rows = iota((SUB, GROUP), 0) + first
    cols = iota((SUB, GROUP), 1) + (first - radius)
    return doc_of(rows, bounds, docs) == doc_of(cols, bounds, docs)


def token_kernel(
    docs, scale, bounds, q_ref, v_ref, mk_ref, mix_ref, taps_ref, mixed_ref, probs_ref, band_s, sum_s
):
    width = q_ref.shape[1]
    groups = width // GROUP
    radius = (TAPS - 1) // 2
    first = pl.program_id(0) * BLOCK

    @pl.when(pl.program_id(0) == 0)
    def _():
        make_band(taps_ref, band_s)

    for sub in range(BLOCK // SUB):
        start = pl.multiple_of(first + sub * SUB, SUB)
        same = same_doc(start, bounds, docs, radius)
        same = jnp.where(jnp.concatenate([same] * 4, axis=0), 1.0, 0.0).astype(BF)
        for g in range(groups):
            cols = slice(g * GROUP, (g + 1) * GROUP)
            band = band_s[g * 4 * SUB : (g + 1) * 4 * SUB, :] * same
            res = dot_nn(band, v_ref[pl.ds(start, GROUP), cols])
            sum_s[sub * SUB : (sub + 1) * SUB, cols] = gathered(res)
    probs_ref[...] = jnp.zeros(probs_ref.shape, BF)
    for doc in range(docs):
        low, high = bounds[doc], bounds[docs + doc]
        rows = slice(doc * LAND, (doc + 1) * LAND)

        @pl.when((high > first) & (low < first + BLOCK))
        def _():
            place = iota((1, BLOCK), 1) + first
            valid = (place >= low) & (place < high)
            for g in range(groups):
                cols = slice(g * GROUP, (g + 1) * GROUP)
                scores = dot_nt(spread(mk_ref[rows, cols]), q_ref[:, cols]) * scale
                scores = scores.reshape(4, LAND, BLOCK)
                weights = jnp.exp(scores - jnp.max(scores, axis=1, keepdims=True))
                probs = weights / jnp.sum(weights, axis=1, keepdims=True)
                probs = jnp.where(valid, probs.reshape(GROUP, BLOCK), 0.0).astype(BF)
                probs_ref[cols, :] = probs_ref[cols, :] + probs
                sum_s[:, cols] = sum_s[:, cols] + dot_tn(probs, spread(mix_ref[rows, cols]))

    mixed_ref[...] = sum_s[...].astype(BF)


def token_back_kernel(
    docs, scale, bounds, q_ref, gm_ref, probs_ref, mk_ref, mix_ref, gq_ref, gmix_ref, gmk_ref, gq_s
):
    width = q_ref.shape[1]
    groups = width // GROUP
    first = pl.program_id(0) * BLOCK

    @pl.when(pl.program_id(0) == 0)
    def _():
        gmix_ref[...] = jnp.zeros(gmix_ref.shape, F32)
        gmk_ref[...] = jnp.zeros(gmk_ref.shape, F32)

    gq_s[...] = jnp.zeros(gq_s.shape, F32)
    for doc in range(docs):
        low, high = bounds[doc], bounds[docs + doc]
        rows = slice(doc * LAND, (doc + 1) * LAND)

        @pl.when((high > first) & (low < first + BLOCK))
        def _():
            place = iota((1, BLOCK), 1) + first
            valid = (place >= low) & (place < high)
            for g in range(groups):
                cols = slice(g * GROUP, (g + 1) * GROUP)
                probs = jnp.where(valid, probs_ref[cols, :].astype(F32), 0.0)
                gmix_ref[rows, cols] += gathered(dot_nn(probs.astype(BF), gm_ref[:, cols]))
                grad = dot_nt(spread(mix_ref[rows, cols]), gm_ref[:, cols])
                heavy = (probs * grad).reshape(4, LAND, BLOCK)
                shared = probs.reshape(4, LAND, BLOCK) * jnp.sum(heavy, axis=1, keepdims=True)
                grad = ((heavy - shared).reshape(GROUP, BLOCK) * scale).astype(BF)
                gmk_ref[rows, cols] += gathered(dot_nn(grad, q_ref[:, cols]))
                gq_s[:, cols] += dot_tn(grad, spread(mk_ref[rows, cols]))

    gq_ref[...] = gq_s[...].astype(BF)


def conv_back_kernel(docs, bounds, gm_ref, v_ref, taps_ref, out_ref, prod_ref, band_s):
    width = gm_ref.shape[1]
    groups = width // GROUP
    radius = (TAPS - 1) // 2
    first = pl.program_id(0) * BLOCK

    @pl.when(pl.program_id(0) == 0)
    def _():
        make_band(taps_ref, band_s)
        prod_ref[...] = jnp.zeros(prod_ref.shape, F32)

    for sub in range(BLOCK // SUB):
        start = pl.multiple_of(first + sub * SUB, SUB)
        same = same_doc(start, bounds, docs, radius)
        same = jnp.where(jnp.concatenate([same] * 4, axis=0), 1.0, 0.0)
        for g in range(groups):
            cols = slice(g * GROUP, (g + 1) * GROUP)
            tall = slice(g * 4 * SUB, (g + 1) * 4 * SUB)
            band = band_s[tall, :] * same.astype(BF)
            res = dot_nn(band, gm_ref[pl.ds(start, GROUP), cols])
            out_ref[sub * SUB : (sub + 1) * SUB, cols] = gathered(res)
            own = gm_ref[pl.ds(pl.multiple_of(start + radius, 16), SUB), cols]
            product = dot_nt(spread(own), v_ref[pl.ds(start, GROUP), cols])
            prod_ref[tall, :] += product * same


def landmark_back_kernel(
    docs, scale, bounds, k_ref, v_ref, conv_ref, mq_ref, grad_ref, level_ref, dots_ref,
    gk_ref, gv_ref, gmq_ref, gk_s, gv_s,
):
    width = k_ref.shape[1]
    groups = width // GROUP
    first = pl.program_id(0) * BLOCK

    @pl.when(pl.program_id(0) == 0)
    def _():
        gmq_ref[...] = jnp.zeros(gmq_ref.shape, F32)

    gk_s[...] = jnp.zeros(gk_s.shape, F32)
    gv_s[...] = conv_ref[...]
    for doc in range(docs):
        low, high = bounds[doc], bounds[docs + doc]
        rows = slice(doc * LAND, (doc + 1) * LAND)

        @pl.when((high > first) & (low < first + BLOCK))
        def _():
            place = iota((1, BLOCK), 1) + first
            valid = (place >= low) & (place < high)

            def column(ref, g):
                return jnp.concatenate(
                    [ref[rows, 4 * g + h : 4 * g + h + 1] for h in range(4)], axis=0
                )

            for g in range(groups):
                cols = slice(g * GROUP, (g + 1) * GROUP)
                wide_q, wide_g = spread(mq_ref[rows, cols]), spread(grad_ref[rows, cols])
                scores = dot_nt(wide_q, k_ref[:, cols]) * scale - column(level_ref, g)
                probs = jnp.exp(jnp.where(valid, scores, NEGATIVE))
                grad = dot_nt(wide_g, v_ref[:, cols]) - column(dots_ref, g)
                grad = (probs * grad * scale).astype(BF)
                gv_s[:, cols] += dot_tn(probs.astype(BF), wide_g)
                gk_s[:, cols] += dot_tn(grad, wide_q)
                gmq_ref[rows, cols] += gathered(dot_nn(grad, k_ref[:, cols]))

    gk_ref[...] = gk_s[...].astype(BF)
    gv_ref[...] = gv_s[...].astype(BF)


def gelu_both(upper):
    tangent = jnp.tanh(0.7978845608028654 * (upper + 0.044715 * upper * upper * upper))
    inner_slope = 0.7978845608028654 * (1.0 + 3.0 * 0.044715 * upper * upper)
    active = 0.5 * upper * (1.0 + tangent)
    slope = 0.5 * (1.0 + tangent) + 0.5 * upper * (1.0 - tangent * tangent) * inner_slope
    return active, slope


def normalize(residual):
    row_mean = jnp.mean(residual, axis=-1, keepdims=True)
    centered = residual - row_mean
    row_var = jnp.mean(centered * centered, axis=-1, keepdims=True)
    inverse_dev = lax.rsqrt(row_var + 1e-05)
    return (centered * inverse_dev, inverse_dev)


def norm_back(grad_normed, normed, inverse_dev):
    return inverse_dev * (
        grad_normed
        - jnp.mean(grad_normed, axis=-1, keepdims=True)
        - normed * jnp.mean(grad_normed * normed, axis=-1, keepdims=True)
    )


def pinv_kernel(queries, key_rows, score_scale):
    scores = jnp.einsum("pie,pje->pij", queries, key_rows, precision=HIGH) * score_scale
    row_max = jnp.max(scores, axis=-1, keepdims=True)
    weights = jnp.exp(scores - row_max)
    kernel = weights / jnp.sum(weights, axis=-1, keepdims=True)
    column_max = jnp.max(jnp.sum(kernel, axis=1), axis=-1)
    inverse = jnp.swapaxes(kernel, -1, -2) / column_max[:, None, None]
    identity = jnp.eye(LAND, dtype=F32)
    for sweep in range(NS_ITERS):
        product = jnp.matmul(kernel, inverse, precision=HIGH)
        bracket = 7.0 * identity - product
        bracket = 15.0 * identity - jnp.matmul(product, bracket, precision=HIGH)
        bracket = 13.0 * identity - jnp.matmul(product, bracket, precision=HIGH)
        inverse = 0.25 * jnp.matmul(inverse, bracket, precision=HIGH)
    return inverse


def per_device(
    inputs, doc_lengths, w_qkv, bias_q, bias_v, conv_taps, w_out, bias_out, norm1_gain,
    norm1_bias, w_up, bias_up, w_down, bias_down, norm2_gain, norm2_bias, cotangent,
):
    tokens = inputs[0]
    tok_count, width = tokens.shape
    heads, tap_count = conv_taps.shape
    size = width // heads
    radius = (tap_count - 1) // 2
    lengths = doc_lengths[0]
    docs = lengths.shape[0]
    mark_count = docs * LAND
    scale = 1.0 / math.sqrt(size)
    seq_count = lax.axis_size("seq")
    me = lax.axis_index("seq")
    row_first = me * tok_count
    ends = jnp.cumsum(lengths)
    starts = ends - lengths
    bounds = (jnp.concatenate([starts, ends]) - row_first).astype(jnp.int32)
    within = jnp.arange(LAND + 1, dtype=jnp.int32)
    edges = starts[:, None] + (within[None, :] * lengths[:, None] + LAND - 1) // LAND
    mark_low = edges[:, :-1].reshape(mark_count, 1)
    mark_high = edges[:, 1:].reshape(mark_count, 1)
    counts = (mark_high - mark_low).astype(F32)
    places = row_first + jnp.arange(tok_count, dtype=jnp.int32)[None, :]
    onehot = ((places >= mark_low) & (places < mark_high)).astype(BF)
    rows_in = (((0,), (0,)), ((), ()))
    cols_in = (((1,), (1,)), ((), ()))
    pair_count = docs * heads
    own_pairs = -(-pair_count // seq_count)
    padded = own_pairs * seq_count
    blocks = tok_count // BLOCK
    window_rows = tok_count + GROUP - SUB
    smem = pl.BlockSpec(memory_space=pltpu.SMEM)
    params = pltpu.CompilerParams(vmem_limit_bytes=40 * 1024 * 1024)
    tok_spec = pl.BlockSpec((BLOCK, width), lambda i: (i, 0))

    def part(col):
        return pl.BlockSpec((BLOCK, width), lambda i: (i, col))

    def fixed(*shape):
        return pl.BlockSpec(shape, lambda i: (0,) * len(shape))

    def shaped(shape, dtype):
        return jax.ShapeDtypeStruct(shape, dtype)

    means = jnp.dot(onehot, tokens, preferred_element_type=F32) / counts
    mean_in = seq_total(means.astype(BF), add_join)
    marks = jnp.dot(mean_in, w_qkv[:, : 2 * width], preferred_element_type=F32)
    mark_q = (marks[:, :width] + bias_q).astype(BF)
    mark_k = marks[:, width:].astype(BF)

    bias = jnp.concatenate([bias_q, jnp.zeros_like(bias_q), bias_v])
    qkv = (jnp.dot(tokens, w_qkv, preferred_element_type=F32) + bias).astype(BF)
    value_ext = extended(qkv[:, 2 * width :], radius, window_rows)

    def one_col(col):
        return pl.BlockSpec((tok_count, width), lambda i: (0, col))

    stats = pl.pallas_call(
        lambda *refs: landmark_kernel(docs, scale, *refs),
        grid=(1,),
        in_specs=[smem, fixed(mark_count, width), one_col(1), one_col(2)],
        out_specs=fixed(mark_count, width + 128),
        out_shape=shaped((mark_count, width + 128), BF),
        scratch_shapes=[
            pltpu.VMEM((width, 128), F32), pltpu.VMEM((width, 128), F32),
            pltpu.VMEM((width, GROUP), F32),
        ],
        compiler_params=params,
        name="landmark",
    )(bounds, mark_q, qkv, qkv)
    stats = seq_total(stats, join)

    def own(array):
        array = array.reshape(docs, LAND, heads, size).transpose(0, 2, 1, 3)
        array = array.reshape(pair_count, LAND, size)
        array = jnp.pad(array, ((0, padded - pair_count), (0, 0), (0, 0)))
        return lax.dynamic_slice_in_dim(array, me * own_pairs, own_pairs, 0)

    own_inverse, inverse_pullback = jax.vjp(
        lambda a, b: pinv_kernel(a, b, scale), own(mark_q).astype(F32), own(mark_k).astype(F32)
    )
    inverse = lax.all_gather(own_inverse.astype(T_INV), "seq", axis=0, tiled=True)[:pair_count]
    inverse = inverse.reshape(docs, heads, LAND, LAND).transpose(0, 2, 1, 3)
    inverse = inverse.reshape(mark_count, width)
    mix, level = pl.pallas_call(
        lambda *refs: mix_kernel(docs, *refs),
        out_shape=(shaped((mark_count, width), BF), shaped((mark_count, 128), F32)),
        name="mix",
    )(inverse, stats)

    taps = jnp.pad(conv_taps, ((0, 0), (0, GROUP - tap_count)))
    mark_spec = fixed(mark_count, width)
    mixed, probs = pl.pallas_call(
        lambda *refs: token_kernel(docs, scale, *refs),
        grid=(blocks,),
        in_specs=[
            smem, part(0), fixed(window_rows, width), mark_spec, mark_spec, fixed(heads, GROUP)
        ],
        out_specs=(tok_spec, pl.BlockSpec((width, BLOCK), lambda i: (0, i))),
        out_shape=(shaped((tok_count, width), BF), shaped((width, tok_count), BF)),
        scratch_shapes=[pltpu.VMEM((heads * SUB, GROUP), BF), pltpu.VMEM((BLOCK, width), F32)],
        compiler_params=params,
        name="token",
    )(bounds, qkv, value_ext, mark_k, mix, taps)

    attended = jnp.dot(mixed, w_out, preferred_element_type=F32) + bias_out
    norm_one, inverse_one = normalize(tokens.astype(F32) + attended)
    hidden_one = norm_one * norm1_gain + norm1_bias
    hidden_low = hidden_one.astype(BF)
    upper = jnp.dot(hidden_low, w_up, preferred_element_type=F32) + bias_up
    active, slope = gelu_both(upper)
    active = active.astype(BF)
    lowered = jnp.dot(active, w_down, preferred_element_type=F32) + bias_down
    norm_two, inverse_two = normalize(hidden_one + lowered)
    result = norm_two * norm2_gain + norm2_bias
    upstream = cotangent[0].astype(F32)
    grad_gain_two = jnp.sum(upstream * norm_two, axis=0)
    grad_shift_two = jnp.sum(upstream, axis=0)
    grad_two = norm_back(upstream * norm2_gain, norm_two, inverse_two)
    grad_low_two = grad_two.astype(BF)
    grad_bias_down = jnp.sum(grad_low_two.astype(F32), axis=0)
    grad_w_down = lax.dot_general(active, grad_low_two, rows_in, preferred_element_type=F32)
    grad_active = lax.dot_general(grad_low_two, w_down, cols_in, preferred_element_type=F32)
    grad_upper = (grad_active * slope).astype(BF)
    grad_bias_up = jnp.sum(grad_upper.astype(F32), axis=0)
    grad_w_up = lax.dot_general(hidden_low, grad_upper, rows_in, preferred_element_type=F32)
    grad_hidden = grad_two + lax.dot_general(
        grad_upper, w_up, cols_in, preferred_element_type=F32
    )
    grad_gain_one = jnp.sum(grad_hidden * norm_one, axis=0)
    grad_shift_one = jnp.sum(grad_hidden, axis=0)
    grad_one = norm_back(grad_hidden * norm1_gain, norm_one, inverse_one)
    grad_low_one = grad_one.astype(BF)
    grad_bias_out = jnp.sum(grad_low_one.astype(F32), axis=0)
    grad_w_out = lax.dot_general(mixed, grad_low_one, rows_in, preferred_element_type=F32)
    grad_mixed = lax.dot_general(
        grad_low_one, w_out, cols_in, preferred_element_type=F32
    ).astype(BF)

    grad_queries, grad_mix, grad_mk = pl.pallas_call(
        lambda *refs: token_back_kernel(docs, scale, *refs),
        grid=(blocks,),
        in_specs=[
            smem, part(0), tok_spec, pl.BlockSpec((width, BLOCK), lambda i: (0, i)), mark_spec,
            mark_spec,
        ],
        out_specs=(tok_spec, mark_spec, mark_spec),
        out_shape=(
            shaped((tok_count, width), BF), shaped((mark_count, width), F32),
            shaped((mark_count, width), F32),
        ),
        scratch_shapes=[pltpu.VMEM((BLOCK, width), F32)],
        compiler_params=params,
        name="token_back",
    )(bounds, qkv, grad_mixed, probs, mark_k, mix)
    grad_mix = seq_total(grad_mix.astype(BF), add_join)

    grad_ext = extended(grad_mixed, radius, window_rows)
    grad_conv, products = pl.pallas_call(
        lambda *refs: conv_back_kernel(docs, *refs),
        grid=(blocks,),
        in_specs=[
            smem, fixed(window_rows, width), fixed(window_rows, width), fixed(heads, GROUP)
        ],
        out_specs=(tok_spec, fixed(heads * SUB, GROUP)),
        out_shape=(shaped((tok_count, width), F32), shaped((heads * SUB, GROUP), F32)),
        scratch_shapes=[pltpu.VMEM((heads * SUB, GROUP), BF)],
        compiler_params=params,
        name="conv_back",
    )(bounds, grad_ext, value_ext, jnp.pad(conv_taps[:, ::-1], ((0, 0), (0, GROUP - tap_count))))
    reach = SUB + tap_count - 1
    products = products.reshape(heads, SUB, GROUP)[:, :, :reach].reshape(heads, SUB * reach)
    products = jnp.pad(products, ((0, 0), (0, SUB))).reshape(heads, SUB, reach + 1)
    grad_conv_taps = jnp.sum(products, axis=1)[:, :tap_count]

    grad_avg, dots = pl.pallas_call(
        lambda *refs: mix_back_kernel(docs, *refs),
        out_shape=(shaped((mark_count, width), BF), shaped((mark_count, 128), F32)),
        name="mix_back",
    )(inverse, stats, grad_mix)
    grad_inverse = jnp.einsum(
        "pie,pje->pij", own(grad_mix), own(stats[:, :width]), preferred_element_type=F32
    )
    grad_mq_small, grad_mk_small = inverse_pullback(grad_inverse)
    lane_spec = fixed(mark_count, 128)
    grad_keys, grad_values, grad_mq = pl.pallas_call(
        lambda *refs: landmark_back_kernel(docs, scale, *refs),
        grid=(blocks,),
        in_specs=[
            smem, part(1), part(2), tok_spec, mark_spec, mark_spec, lane_spec, lane_spec
        ],
        out_specs=(tok_spec, tok_spec, mark_spec),
        out_shape=(
            shaped((tok_count, width), BF), shaped((tok_count, width), BF),
            shaped((mark_count, width), F32),
        ),
        scratch_shapes=[pltpu.VMEM((BLOCK, width), F32), pltpu.VMEM((BLOCK, width), F32)],
        compiler_params=params,
        name="landmark_back",
    )(bounds, qkv, qkv, grad_conv, mark_q, grad_avg, level, dots)

    def placed(array):
        empty = jnp.zeros((padded, LAND, size), F32)
        array = lax.dynamic_update_slice_in_dim(empty, array, me * own_pairs, 0)[:pair_count]
        array = array.reshape(docs, heads, LAND, size).transpose(0, 2, 1, 3)
        return array.reshape(mark_count, width)

    grad_mq = grad_mq + placed(grad_mq_small)
    grad_mk = grad_mk + placed(grad_mk_small)
    grad_marks = jnp.concatenate([grad_mq, grad_mk], axis=1).astype(BF)
    mark_back = lax.dot_general(
        grad_marks, w_qkv[:, : 2 * width], cols_in, preferred_element_type=F32
    ) / counts
    mark_back = seq_total(mark_back.astype(BF), add_join)

    grad_bias_q = jnp.sum(grad_queries.astype(F32), axis=0) + jnp.sum(grad_mq, axis=0)
    grad_bias_v = jnp.sum(grad_values.astype(F32), axis=0)
    grad_projected = jnp.concatenate([grad_queries, grad_keys, grad_values], axis=1)
    grad_w_qkv = lax.dot_general(tokens, grad_projected, rows_in, preferred_element_type=F32)
    grad_w_marks = lax.dot_general(mean_in, grad_marks, rows_in, preferred_element_type=F32)
    grad_w_qkv = grad_w_qkv + jnp.pad(grad_w_marks, ((0, 0), (0, width)))
    grad_input = (
        grad_one
        + lax.dot_general(grad_projected, w_qkv, cols_in, preferred_element_type=F32)
        + lax.dot_general(onehot, mark_back, rows_in, preferred_element_type=F32)
    )

    small = [
        grad_bias_q, grad_bias_v, grad_conv_taps.reshape(-1), grad_bias_out, grad_gain_one,
        grad_shift_one, grad_bias_up, grad_bias_down, grad_gain_two, grad_shift_two,
    ]
    sizes = [piece.shape[0] for piece in small]
    flat = jnp.concatenate(small)
    lanes = -(-flat.shape[0] // 1024) * 8
    flat = jnp.pad(flat, (0, lanes * 128 - flat.shape[0])).reshape(lanes, 128)
    flat = small_sum(flat).reshape(-1)
    pieces = []
    at = 0
    for length in sizes:
        pieces.append(flat[at : at + length])
        at += length
    sum_w_down = all_sum(grad_w_down, "row")
    sum_w_up = all_sum(grad_w_up, "seq")
    sum_w_out = all_sum(grad_w_out, "seq")
    sum_w_qkv = all_sum(grad_w_qkv, "row")
    return (
        result[None], grad_input[None], sum_w_qkv, pieces[0], pieces[1],
        pieces[2].reshape(heads, tap_count), sum_w_out, pieces[3], pieces[4], pieces[5],
        sum_w_up, pieces[6], sum_w_down, pieces[7], pieces[8], pieces[9],
    )


def solution(mesh):
    whole, tokens = P(), P("row", "seq", None)
    return jax.shard_map(
        per_device,
        mesh=mesh,
        in_specs=(tokens, P("row", None)) + (whole,) * 14 + (tokens,),
        out_specs=(tokens, tokens) + (whole,) * 14,
        check_vma=False,
    )
```

time: 1180 us -> 653 us (0.55)
  local copies, waits for them, and re-layouts: 495 us -> 99.6 us
  matrix products: 219 us -> 127 us
  starting transfers between devices: 143 us -> 85.3 us
  other arithmetic: 119 us -> 67.6 us
  Pallas kernels: 0 us -> 51.3 us
  blocking collectives: 0 us -> 25.8 us
    gather x8 -> x0, local copies, waits for them, and re-layouts: 313 us -> none  [band(): taps[:, jnp.clip(offset_at, 0, tap_count - 1)]]
    dot_general x25 -> x6, matrix products: 80 us -> 14.1 us  [the longest x1 5.33 us: per_device(): lax.dot_general(onehot, mark_back, rows_in, preferred_element_type=F32)]
    ppermute x109 -> x69, starting transfers between devices: 135 us -> 78.6 us  [swap(): return lax.ppermute(array, axis, [(i, i ^ bit) for i in range(count)])]
    pallas_call x0 -> x11, Pallas kernels: none -> 51.3 us  [the longest x1 9.46 us: per_device(): pl.pallas_call(lambda *refs: landmark_kernel(docs, scale, *refs), grid=(1...]
    slice x28 -> x11, local copies, waits for them, and re-layouts: 34.5 us -> 2.55 us  [the longest x2 1.34 us: extended(): tail = cells[-width:]]
    all_gather x0 -> x1, blocking collectives: none -> 25.8 us  [per_device(): lax.all_gather(own_inverse.astype(T_INV), 'seq', axis=0, tiled=True)]
    dynamic_update_slice x28 -> x0, local copies, waits for them, and re-layouts: 15.1 us -> none  [gather_blocks(): lax.dynamic_update_index_in_dim(held, swap(block, 'seq', 2 * step), chip...]
    reshape x7 -> x12, local copies, waits for them, and re-layouts: 10.6 us -> 24.5 us  [the longest x4 9.75 us: placed(): return array.reshape(mark_count, width)]
  transfers between devices with their start and end apart: 113 -> 73, of which waited for: 39 -> 34; matrix products, arithmetic and copies ran while one was open for 54% -> 24% of each run, Pallas kernels for 0% -> 4%
where the time goes in v2:
time: 653 us; the launch traced here: 641 us
  waiting for transfers between devices  180 us (28%)
  matrix products  127 us (19%)
  local copies, waits for them, and re-layouts  99.6 us (15%)
  starting transfers between devices  85.3 us (13%)
  other arithmetic  67.6 us (10%)
  Pallas kernels  51.3 us (8%)
  blocking collectives  25.8 us (4%)
    ppermute x69, waiting for transfers between devices, swap(): return lax.ppermute(array, axis, [(i, i ^ bit) for i in range(count)])  180 us
    ppermute x69, starting transfers between devices, swap(): return lax.ppermute(array, axis, [(i, i ^ bit) for i in range(count)])  78.6 us
    unnamed x290, local copies, waits for them, and re-layouts  45.8 us
    all_gather x1, blocking collectives, per_device(): lax.all_gather(own_inverse.astype(T_INV), 'seq', axis=0, tiled=True)  25.8 us
    convert_element_type x4, other arithmetic, all_sum(): return held.astype(F32)  23.6 us
    dot_general x1, matrix products, per_device(): lax.dot_general(grad_low_two, w_down, cols_in, preferred_element_type=F32)  16.7 us
    dot_general x1, matrix products, per_device(): lax.dot_general(active, grad_low_two, rows_in, preferred_element_type=F32)  13.8 us
  transfers between devices with their start and end apart: 73, of which 34 were waited for; matrix products, arithmetic and copies ran while one was open for 24% of the time, Pallas kernels for 4%

profile of v2, /device:TPU:0, one launch (start us, length us, event | category | flops | bytes accessed | tf_op | source)
XLA Modules:
  0.0 640.9 jit_solution(6309144372462526209)
XLA Ops:
  7.7 4.1 add_convert_fusion.refs_2_.refs_3_.refs_1_
  19.5 2.7 copy.133
  23.4 4.9 collective-permute-start.3
  34.0 2.6 collective-permute-done.4
  36.6 3.9 collective-permute-start.5
  40.5 3.6 collective-permute-done.5
  45.0 3.9 collective-permute-done.6
  54.7 9.5 %landmark.1 = bf16[256,896]{1,0:T(8,128)(2,1)S(1)} custom-call(s32[8]{0:T(128)S(1)} %add_subtract_fusion.refs_0_, bf16[256,768]{1,0:T(8,128)(2,1)S(1)} %fusion.56.refs_1_.refs_4_, bf16[1024,2304]{1,0:T(8,128)(2,1)S(1)} %copy-done.3, bf16[1024,2304]{1,0:T(8,128)(2,1)S(1)} %copy-done.3), custom_call_target="tpu_custom_call" | custom-call | tf_op jit(solution)/shard_map/landmark/pallas_call | solution.py:551
  78.3 2.6 join.4
  82.8 4.8 collective-permute-done.9.b_ref
  91.1 4.4 collective-permute-done.10.b_ref
  98.3 7.8 %collective-permute-start.11 = (bf16[64,896]{1,0:T(8,128)(2,1)}, bf16[64,896]{1,0:T(8,128)(2,1)S(1)}, u32[]{:S(2)}, u32[]{:S(2)}) collective-permute-start(bf16[64,896]{1,0:T(8,128)(2,1)} %join.6.a_ref), channel_id=1, source_target_pairs={{0,8},{1,9},{2,10},{3,11},{4,12},{5,13},{6,14},{7,15},{8,0},{9,1},... | collective-permute-start | bytes 344072 | tf_op jit(solution)/shard_map/ppermute | solution.py:28
  106.3 4.4 collective-permute-done.11.b_ref
  114.2 4.3 collective-permute-done.12
  120.2 25.8 %all_gather.3 = bf16[48,64,64]{2,1,0:T(8,128)(2,1)} all-gather(bf16[3,64,64]{2,1,0:T(8,128)(2,1)S(1)} %fusion.49), channel_id=1, replica_groups=mesh['row'=2,'seq'=16] {'seq'}, dimensions={0}, use_global_device_ids=true | all-gather | bytes 417792 | tf_op jit(solution)/shard_map/all_gather | solution.py:575
  161.5 7.7 %token_.1 = (bf16[1024,768]{1,0:T(8,128)(2,1)S(1)}, bf16[768,1024]{1,0:T(8,128)(2,1)S(1)}) custom-call(s32[8]{0:T(128)S(1)} %add_subtract_fusion.refs_0_, bf16[1024,2304]{1,0:T(8,128)(2,1)S(1)} %copy-done.4, bf16[1152,768]{1,0:T(8,128)(2,1)S(1)} %copy-done.6, bf16[256,768]{1,0:T(8,128)(2,1)S(1)} %copy-done.11, bf16[256,768]{1,0:T(8,128)(2,1)S(1)} %copy-done.15, ...), custom_call_target="tpu_custom_call" | custom-call | tf_op jit(solution)/shard_map/token/pallas_call | solution.py:586
  171.8 8.6 %fusion.142 = f32[1024,3072]{1,0:T(8,128)} fusion(bf16[768,3072]{1,0:T(8,128)(2,1)S(1)} %bitcast.249, f32[1024,768]{0,1:T(8,128)S(1)} %get-tuple-element.134, f32[768]{0:T(1024)S(1)} %copy-done.92, f32[768]{0:T(1024)S(1)} %copy-done.91, f32[1024]{0:T(1024)S(1)} %add_rsqrt_fusion.1, f32[1024]{0:T(1024)S(1)} %broadcast_multiply_fusion.5), kind=kOutput, calls=%fused_computation.358 | convolution fusion | flops 4835770368 | bytes 20461568 | tf_op jit(solution)/shard_map/dot_general | solution.py:603
  180.4 11.8 %fusion.153 = (f32[1024]{0:T(1024)S(1)}, f32[1024,768]{0,1:T(8,128)S(1)}) fusion(f32[768]{0:T(1024)S(1)} %copy-done.127, bf16[3072,768]{1,0:T(8,128)(2,1)} %param.29, f32[1024,3072]{1,0:T(8,128)} %fusion.142, f32[3072]{0:T(1024)S(1)} %copy-done.125, f32[768]{0:T(1024)S(1)} %copy-done.92, f32[768]{0:T(1024)S(1)} %copy-done.91, ...), kind=kOutput, calls=%fused_computation.367 | convolution fusion | flops 4868799488 | bytes 23626752 | tf_op jit(solution)/shard_map/dot_general | solution.py:606
  195.0 2.9 convert_reduce_fusion.2
  197.9 13.8 %fusion.144 = f32[3072,768]{1,0:T(8,128)} fusion(bf16[1024,768]{0,1:T(8,128)(2,1)S(1)} %get-tuple-element.100, f32[1024,3072]{1,0:T(8,128)} %fusion.142, f32[3072]{0:T(1024)S(1)} %copy-done.125), kind=kOutput, calls=%fused_computation.359 | convolution fusion | flops 4863295488 | bytes 23605248 | tf_op jit(solution)/shard_map/dot_general | solution.py:615
  211.7 16.7 %convert_reduce_fusion = (f32[3072]{0:T(1024)}, bf16[1024,3072]{1,0:T(8,128)(2,1)}) fusion(f32[1024,3072]{1,0:T(8,128)} %fusion.142, f32[3072]{0:T(1024)S(1)} %copy-done.125, bf16[1024,768]{0,1:T(8,128)(2,1)S(1)} %get-tuple-element.100, bf16[3072,768]{1,0:T(8,128)(2,1)} %param.29), kind=kOutput, calls=%fused_computation.10 | convolution fusion | flops 4901041152 | bytes 25190400 | tf_op jit(solution)/shard_map/dot_general | solution.py:616
  228.4 10.7 %fusion.140 = f32[768,3072]{1,0:T(8,128)} fusion(bf16[1024,3072]{1,0:T(8,128)(2,1)} %get-tuple-element.143, f32[1024,768]{0,1:T(8,128)S(1)} %get-tuple-element.134, f32[768]{0:T(1024)S(1)} %copy-done.92, f32[768]{0:T(1024)S(1)} %copy-done.91, f32[1024]{0:T(1024)S(1)} %add_rsqrt_fusion.1, f32[1024]{0:T(1024)S(1)} %broadcast_multiply_fusion.5), kind=kOutput, calls=%fused_computation.357 | convolution fusion | flops 4835770368 | bytes 18888704 | tf_op jit(solution)/shard_map/dot_general | solution.py:619
  239.1 10.2 %multiply_reduce_fusion = (f32[768]{0:T(1024)}, f32[1024]{0:T(1024)S(1)}, f32[1024]{0:T(1024)S(1)}, f32[768]{0:T(1024)}, f32[1024,768]{0,1:T(8,128)S(1)}) fusion(f32[1024,768]{0,1:T(8,128)S(1)} %get-tuple-element.134, f32[1024]{0:T(1024)S(1)} %add_rsqrt_fusion.1, f32[1024]{0:T(1024)S(1)} %broadcast_multiply_fusion.5, f32[768]{0:T(1024)S(1)} %copy-done.91, ...), kind=kOutput, calls=%fused_computation.38 | convolution fusion | flops 4845989888 | bytes 22065152 | tf_op jit(solution)/shard_map/dot_general | solution.py:620
  253.6 4.6 dynamic-slice_convert_fusion
  258.5 4.1 dynamic-slice_convert_fusion.1
  262.9 6.0 token_back.1
  279.6 3.6 copy.165
  286.0 3.3 collective-permute-done.18
  289.3 4.3 collective-permute-start.19
  293.6 2.7 constant_dynamic-update-slice_fusion.2
  301.7 5.4 conv_back.1
  313.6 3.2 reshape.261
  321.0 2.9 collective-permute-start.44
  339.7 4.6 mix_back.1
  348.4 2.7 copy.196
  351.0 2.7 reshape.266
  357.9 6.8 %landmark_back.1 = (bf16[1024,768]{1,0:T(8,128)(2,1)S(1)}, bf16[1024,768]{1,0:T(8,128)(2,1)S(1)}, f32[256,768]{1,0:T(8,128)S(1)}) custom-call(s32[8]{0:T(128)S(1)} %add_subtract_fusion.refs_0_, bf16[1024,2304]{1,0:T(8,128)(2,1)S(1)} %copy-done.5, bf16[1024,2304]{1,0:T(8,128)(2,1)S(1)} %copy-done.5, f32[1024,768]{1,0:T(8,128)S(1)} %copy-done.14, ...), custom_call_target="tpu_custom_call" | custom-call | tf_op jit(solution)/shard_map/landmark_back/pallas_call | solution.py:679
  372.9 2.8 constant_dynamic-update-slice_fusion.1
  377.0 7.9 %fusion.154 = f32[1024,768]{0,1:T(8,128)} fusion(bf16[1024,2304]{1,0:T(8,128)(2,1)} %constant_dynamic-update-slice_fusion, bf16[768,2304]{1,0:T(8,128)(2,1)S(1)} %copy-done.124), kind=kOutput, calls=%fused_computation.368 | convolution fusion | flops 3623878656 | bytes 11403264 | tf_op jit(solution)/shard_map/dot_general | solution.py:717
  387.9 3.9 bitcast_add_fusion
  400.7 2.9 collective-permute-done.40
  404.2 3.4 collective-permute-done.41
  417.3 3.1 collective-permute-start.47
  435.3 34.5 %collective-permute-done.29 = bf16[192,2304]{1,0:T(8,128)(2,1)S(1)} collective-permute-done((bf16[192,2304]{1,0:T(8,128)(2,1)S(1)}, bf16[192,2304]{1,0:T(8,128)(2,1)S(1)}, u32[]{:S(2)}, u32[]{:S(2)}) %collective-permute-start.29) | collective-permute-done | bytes 884768 | tf_op jit(solution)/shard_map/ppermute | solution.py:28
  473.2 9.2 %collective-permute-done.30 = bf16[96,2304]{1,0:T(8,128)(2,1)S(1)} collective-permute-done((bf16[96,2304]{1,0:T(8,128)(2,1)S(1)}, bf16[96,2304]{1,0:T(8,128)(2,1)S(1)}, u32[]{:S(2)}, u32[]{:S(2)}) %collective-permute-start.30) | collective-permute-done | bytes 442400 | tf_op jit(solution)/shard_map/ppermute | solution.py:28
  485.3 7.0 %collective-permute-done.31 = bf16[48,2304]{1,0:T(8,128)(2,1)S(1)} collective-permute-done((bf16[48,2304]{1,0:T(8,128)(2,1)S(1)}, bf16[48,2304]{1,0:T(8,128)(2,1)S(1)}, u32[]{:S(2)}, u32[]{:S(2)}) %collective-permute-start.31) | collective-permute-done | bytes 221216 | tf_op jit(solution)/shard_map/ppermute | solution.py:28
  495.2 6.6 %collective-permute-done.32 = bf16[24,2304]{1,0:T(8,128)(2,1)S(1)} collective-permute-done((bf16[24,2304]{1,0:T(8,128)(2,1)S(1)}, bf16[24,2304]{1,0:T(8,128)(2,1)S(1)}, u32[]{:S(2)}, u32[]{:S(2)}) %collective-permute-start.32) | collective-permute-done | bytes 110624 | tf_op jit(solution)/shard_map/ppermute | solution.py:28
  508.8 9.8 %collective-permute-done.67 = bf16[96,768]{1,0:T(8,128)(2,1)S(1)} collective-permute-done((bf16[96,768]{1,0:T(8,128)(2,1)S(1)}, bf16[96,768]{1,0:T(8,128)(2,1)S(1)}, u32[]{:S(2)}, u32[]{:S(2)}) %collective-permute-start.67) | collective-permute-done | bytes 147488 | tf_op jit(solution)/shard_map/ppermute | solution.py:28
  523.0 3.4 collective-permute-done.68
  526.5 2.6 collective-permute-done.58
  529.3 2.7 collective-permute-done.34
  532.1 3.0 collective-permute-done.69
  535.4 3.3 collective-permute-done.59
  541.9 7.6 %collective-permute-done.70 = bf16[384,768]{1,0:T(8,128)(2,1)S(1)} collective-permute-done((bf16[384,768]{1,0:T(8,128)(2,1)S(1)}, bf16[384,768]{1,0:T(8,128)(2,1)S(1)}, u32[]{:S(2)}, u32[]{:S(2)}) %collective-permute-start.70) | collective-permute-done | bytes 589856 | tf_op jit(solution)/shard_map/ppermute | solution.py:28
  552.4 2.8 collective-permute-start.25
  558.7 15.4 %collective-permute-done.36 = bf16[192,2304]{1,0:T(8,128)(2,1)S(1)} collective-permute-done((bf16[192,2304]{1,0:T(8,128)(2,1)S(1)}, bf16[192,2304]{1,0:T(8,128)(2,1)S(1)}, u32[]{:S(2)}, u32[]{:S(2)}) %collective-permute-start.36) | collective-permute-done | bytes 884768 | tf_op jit(solution)/shard_map/ppermute | solution.py:28
  575.8 17.2 %collective-permute-done.71 = bf16[768,768]{1,0:T(8,128)(2,1)S(1)} collective-permute-done((bf16[768,768]{1,0:T(8,128)(2,1)S(1)}, bf16[768,768]{1,0:T(8,128)(2,1)S(1)}, u32[]{:S(2)}, u32[]{:S(2)}) %collective-permute-start.71) | collective-permute-done | bytes 1179680 | tf_op jit(solution)/shard_map/ppermute | solution.py:28
  600.6 4.8 collective-permute-done.51
  608.2 5.3 add_bitcast_fusion
  613.5 3.5 copy.166
  617.0 2.9 fusion.35
  619.9 5.6 fusion.15
  625.5 5.9 fusion.9
  631.3 9.3 %fusion.8 = f32[768,3072]{1,0:T(8,128)} fusion(bf16[384,3072]{1,0:T(8,128)(2,1)} %collective-permute-done.62, bf16[384,3072]{1,0:T(8,128)(2,1)} %maximum_select_fusion.3, pred[]{:T(512)S(6)} %eq.156), kind=kLoop, calls=%fused_computation.15 | loop fusion | flops 23592960 | bytes 14155777 | tf_op jit(solution)/shard_map/convert_element_type | solution.py:94
  (667 shorter events, 222.4 us)
Async XLA Ops:
  7.1 15.3 %collective-permute-start.2 = (bf16[128,768]{1,0:T(8,128)(2,1)S(1)}, bf16[128,768]{1,0:T(8,128)(2,1)}, u32[]{:S(2)}, u32[]{:S(2)}) collective-permute-start(bf16[128,768]{1,0:T(8,128)(2,1)S(1)} %constant_dynamic-slice_fusion.25), channel_id=1, source_target_pairs={{0,1},{1,0},{2,3},{3,2},{4,5},{5,4},{6,7},{7,6},{8,9},{9,8},{10,11... | collective-permute-start | bytes 589832 | tf_op jit(solution)/shard_map/ppermute | solution.py:28
  14.5 34.5 %collective-permute-start = (bf16[16,768]{1,0:T(8,128)(2,1)}, bf16[16,768]{1,0:T(8,128)(2,1)S(1)}, u32[]{:S(2)}, u32[]{:S(2)}) collective-permute-start(bf16[16,768]{1,0:T(8,128)(2,1)} %get-tuple-element.109), channel_id=1, source_target_pairs={{0,1},{1,2},{2,3},{3,4},{4,5},{5,6},{6,7},{7,8},{8,9},{9,10},{10,1... | collective-permute-start | bytes 73736 | tf_op jit(solution)/shard_map/ppermute | solution.py:109
  16.4 32.6 %collective-permute-start.1 = (bf16[16,768]{1,0:T(8,128)(2,1)S(1)}, bf16[16,768]{1,0:T(8,128)(2,1)S(1)}, u32[]{:S(2)}, u32[]{:S(2)}) collective-permute-start(bf16[16,768]{1,0:T(8,128)(2,1)S(1)} %get-tuple-element.110), channel_id=1, source_target_pairs={{1,0},{2,1},{3,2},{4,3},{5,4},{6,5},{7,6},{8,7},{9,8},{10,9},{11,1... | collective-permute-start | bytes 73736 | tf_op jit(solution)/shard_map/ppermute | solution.py:111
  23.4 8.0 %collective-permute-start.3 = (bf16[64,768]{1,0:T(8,128)(2,1)S(1)}, bf16[64,768]{1,0:T(8,128)(2,1)S(1)}, u32[]{:S(2)}, u32[]{:S(2)}) collective-permute-start(bf16[64,768]{1,0:T(8,128)(2,1)S(1)} %constant_dynamic-slice_fusion.24), channel_id=1, source_target_pairs={{0,2},{1,3},{2,0},{3,1},{4,6},{5,7},{6,4},{7,5},{8,10},{9,11},{10,... | collective-permute-start | bytes 294920 | tf_op jit(solution)/shard_map/ppermute | solution.py:28
  31.4 5.2 collective-permute-start.4
  36.6 7.5 %collective-permute-start.5 = (bf16[64,768]{1,0:T(8,128)(2,1)S(1)}, bf16[64,768]{1,0:T(8,128)(2,1)S(1)}, u32[]{:S(2)}, u32[]{:S(2)}) collective-permute-start(bf16[64,768]{1,0:T(8,128)(2,1)S(1)} %add_convert_fusion.31), channel_id=1, source_target_pairs={{0,8},{1,9},{2,10},{3,11},{4,12},{5,13},{6,14},{7,15},{8,0},{9,1},... | collective-permute-start | bytes 294920 | tf_op jit(solution)/shard_map/ppermute | solution.py:28
  65.0 13.3 %collective-permute-start.8 = (bf16[128,896]{1,0:T(8,128)(2,1)}, bf16[128,896]{1,0:T(8,128)(2,1)}, u32[]{:S(2)}, u32[]{:S(2)}) collective-permute-start(bf16[128,896]{1,0:T(8,128)(2,1)} %get-tuple-element.116), channel_id=1, source_target_pairs={{0,1},{1,0},{2,3},{3,2},{4,5},{5,4},{6,7},{7,6},{8,9},{9,8},{10,11... | collective-permute-start | bytes 688136 | tf_op jit(solution)/shard_map/ppermute | solution.py:28
  82.5 5.1 collective-permute-start.9
  90.4 5.0 collective-permute-start.10
  98.3 12.4 %collective-permute-start.11 = (bf16[64,896]{1,0:T(8,128)(2,1)}, bf16[64,896]{1,0:T(8,128)(2,1)S(1)}, u32[]{:S(2)}, u32[]{:S(2)}) collective-permute-start(bf16[64,896]{1,0:T(8,128)(2,1)} %join.6.a_ref), channel_id=1, source_target_pairs={{0,8},{1,9},{2,10},{3,11},{4,12},{5,13},{6,14},{7,15},{8,0},{9,1},... | collective-permute-start | bytes 344072 | tf_op jit(solution)/shard_map/ppermute | solution.py:28
  113.5 5.0 collective-permute-start.12
  120.2 32.4 %collective-permute-start.13 = (bf16[128,896]{1,0:T(8,128)(2,1)}, bf16[128,896]{1,0:T(8,128)(2,1)}, u32[]{:S(2)}, u32[]{:S(2)}) collective-permute-start(bf16[128,896]{1,0:T(8,128)(2,1)} %maximum_select_fusion.22), channel_id=1, source_target_pairs={{0,1},{1,0},{2,3},{3,2},{4,5},{5,4},{6,7},{7,6},{8,9},{9,8},{10,11... | collective-permute-start | bytes 688136 | tf_op jit(solution)/shard_map/ppermute | solution.py:28
  258.2 167.2 %collective-permute-start.63 = (bf16[1536,768]{1,0:T(8,128)(2,1)}, bf16[1536,768]{1,0:T(8,128)(2,1)}, u32[]{:S(2)}, u32[]{:S(2)}) collective-permute-start(bf16[1536,768]{1,0:T(8,128)(2,1)} %dynamic-slice_convert_fusion), channel_id=1, source_target_pairs={{0,1},{1,0},{2,3},{3,2},{4,5},{5,4},{6,7},{7,6},{8,9},{9,8},{10,11... | collective-permute-start | bytes 7077896 | tf_op jit(solution)/shard_map/ppermute | solution.py:28
  262.6 168.0 %collective-permute-start.53 = (bf16[384,3072]{1,0:T(8,128)(2,1)}, bf16[384,3072]{1,0:T(8,128)(2,1)}, u32[]{:S(2)}, u32[]{:S(2)}) collective-permute-start(bf16[384,3072]{1,0:T(8,128)(2,1)} %dynamic-slice_convert_fusion.1), channel_id=1, source_target_pairs={{0,1},{1,0},{2,3},{3,2},{4,5},{5,4},{6,7},{7,6},{8,9},{9,8},{10,11... | collective-permute-start | bytes 7077896 | tf_op jit(solution)/shard_map/ppermute | solution.py:28
  272.2 11.0 %collective-permute-start.17 = (bf16[64,768]{1,0:T(8,128)(2,1)}, bf16[64,768]{1,0:T(8,128)(2,1)}, u32[]{:S(2)}, u32[]{:S(2)}) collective-permute-start(bf16[64,768]{1,0:T(8,128)(2,1)} %constant_dynamic-slice_fusion.18), channel_id=1, source_target_pairs={{0,2},{1,3},{2,0},{3,1},{4,6},{5,7},{6,4},{7,5},{8,10},{9,11},{10,... | collective-permute-start | bytes 294920 | tf_op jit(solution)/shard_map/ppermute | solution.py:28
  273.1 45.5 %collective-permute-start.43 = (bf16[384,768]{1,0:T(8,128)(2,1)}, bf16[384,768]{1,0:T(8,128)(2,1)}, u32[]{:S(2)}, u32[]{:S(2)}) collective-permute-start(bf16[384,768]{1,0:T(8,128)(2,1)} %dynamic-slice_convert_fusion.3), channel_id=1, source_target_pairs={{0,1},{1,0},{2,3},{3,2},{4,5},{5,4},{6,7},{7,6},{8,9},{9,8},{10,11... | collective-permute-start | bytes 1769480 | tf_op jit(solution)/shard_map/ppermute | solution.py:28
  277.4 22.1 %collective-permute-start.14 = (bf16[16,768]{1,0:T(8,128)(2,1)}, bf16[16,768]{1,0:T(8,128)(2,1)S(1)}, u32[]{:S(2)}, u32[]{:S(2)}) collective-permute-start(bf16[16,768]{1,0:T(8,128)(2,1)} %get-tuple-element.114), channel_id=1, source_target_pairs={{0,1},{1,2},{2,3},{3,4},{4,5},{5,6},{6,7},{7,8},{8,9},{9,10},{10,1... | collective-permute-start | bytes 73736 | tf_op jit(solution)/shard_map/ppermute | solution.py:109
  284.2 5.1 collective-permute-start.18
  289.3 8.8 %collective-permute-start.19 = (bf16[64,768]{1,0:T(8,128)(2,1)S(1)}, bf16[64,768]{1,0:T(8,128)(2,1)S(1)}, u32[]{:S(2)}, u32[]{:S(2)}) collective-permute-start(bf16[64,768]{1,0:T(8,128)(2,1)S(1)} %add_convert_fusion.28), channel_id=1, source_target_pairs={{0,8},{1,9},{2,10},{3,11},{4,12},{5,13},{6,14},{7,15},{8,0},{9,1},... | collective-permute-start | bytes 294920 | tf_op jit(solution)/shard_map/ppermute | solution.py:28
  299.5 17.5 %collective-permute-start.20 = (bf16[64,768]{1,0:T(8,128)(2,1)S(1)}, bf16[64,768]{1,0:T(8,128)(2,1)S(1)}, u32[]{:S(2)}, u32[]{:S(2)}) collective-permute-start(bf16[64,768]{1,0:T(8,128)(2,1)S(1)} %add_convert_fusion.27), channel_id=1, source_target_pairs={{0,2},{1,3},{2,0},{3,1},{4,6},{5,7},{6,4},{7,5},{8,10},{9,11},{10,... | collective-permute-start | bytes 294920 | tf_op jit(solution)/shard_map/ppermute | solution.py:28
  317.0 6.9 %collective-permute-start.21 = (bf16[128,768]{1,0:T(8,128)(2,1)S(1)}, bf16[128,768]{1,0:T(8,128)(2,1)S(1)}, u32[]{:S(2)}, u32[]{:S(2)}) collective-permute-start(bf16[128,768]{1,0:T(8,128)(2,1)S(1)} %maximum_select_fusion.25), channel_id=1, source_target_pairs={{0,1},{1,0},{2,3},{3,2},{4,5},{5,4},{6,7},{7,6},{8,9},{9,8},{10,11... | collective-permute-start | bytes 589832 | tf_op jit(solution)/shard_map/ppermute | solution.py:28
  321.0 78.5 %collective-permute-start.44 = (bf16[192,768]{1,0:T(8,128)(2,1)}, bf16[192,768]{1,0:T(8,128)(2,1)}, u32[]{:S(2)}, u32[]{:S(2)}) collective-permute-start(bf16[192,768]{1,0:T(8,128)(2,1)} %constant_dynamic-slice_fusion.11), channel_id=1, source_target_pairs={{0,2},{1,3},{2,0},{3,1},{4,6},{5,7},{6,4},{7,5},{8,10},{9,11},{10,... | collective-permute-start | bytes 884744 | tf_op jit(solution)/shard_map/ppermute | solution.py:28
  367.3 26.6 %collective-permute-start.38 = (f32[80,128]{1,0:T(8,128)}, f32[80,128]{1,0:T(8,128)}, u32[]{:S(2)}, u32[]{:S(2)}) collective-permute-start(f32[80,128]{1,0:T(8,128)} %pad_bitcast_fusion), channel_id=1, source_target_pairs={{0,1},{1,0},{2,3},{3,2},{4,5},{5,4},{6,7},{7,6},{8,9},{9,8},{10,11... | collective-permute-start | bytes 122888 | tf_op jit(solution)/shard_map/ppermute | solution.py:28
  393.3 34.9 %collective-permute-start.28 = (bf16[384,2304]{1,0:T(8,128)(2,1)S(1)}, bf16[384,2304]{1,0:T(8,128)(2,1)S(1)}, u32[]{:S(2)}, u32[]{:S(2)}) collective-permute-start(bf16[384,2304]{1,0:T(8,128)(2,1)S(1)} %dynamic-slice_convert_fusion.2), channel_id=1, source_target_pairs={{0,1},{1,0},{2,3},{3,2},{4,5},{5,4},{6,7},{7,6},{8,9},{9,8},{10,11... | collective-permute-start | bytes 5308424 | tf_op jit(solution)/shard_map/ppermute | solution.py:28
  398.7 10.8 %collective-permute-start.22 = (bf16[128,768]{1,0:T(8,128)(2,1)S(1)}, bf16[128,768]{1,0:T(8,128)(2,1)S(1)}, u32[]{:S(2)}, u32[]{:S(2)}) collective-permute-start(bf16[128,768]{1,0:T(8,128)(2,1)S(1)} %constant_dynamic-slice_fusion.17), channel_id=1, source_target_pairs={{0,1},{1,0},{2,3},{3,2},{4,5},{5,4},{6,7},{7,6},{8,9},{9,8},{10,11... | collective-permute-start | bytes 589832 | tf_op jit(solution)/shard_map/ppermute | solution.py:28
  407.6 5.1 collective-permute-start.45
  414.5 5.8 collective-permute-start.23
  417.3 5.7 collective-permute-start.47
  420.4 131.1 %collective-permute-start.24 = (bf16[64,768]{1,0:T(8,128)(2,1)S(1)}, bf16[64,768]{1,0:T(8,128)(2,1)}, u32[]{:S(2)}, u32[]{:S(2)}) collective-permute-start(bf16[64,768]{1,0:T(8,128)(2,1)S(1)} %add_convert_fusion.26), channel_id=1, source_target_pairs={{0,4},{1,5},{2,6},{3,7},{4,0},{5,1},{6,2},{7,3},{8,12},{9,13},{10,... | collective-permute-start | bytes 294920 | tf_op jit(solution)/shard_map/ppermute | solution.py:28
  422.9 128.4 %collective-permute-start.48 = (bf16[24,768]{1,0:T(8,128)(2,1)S(1)}, bf16[24,768]{1,0:T(8,128)(2,1)S(1)}, u32[]{:S(2)}, u32[]{:S(2)}) collective-permute-start(bf16[24,768]{1,0:T(8,128)(2,1)S(1)} %add_convert_fusion.34), channel_id=1, source_target_pairs={{0,8},{1,9},{2,10},{3,11},{4,12},{5,13},{6,14},{7,15},{8,0},{9,1},... | collective-permute-start | bytes 110600 | tf_op jit(solution)/shard_map/ppermute | solution.py:28
  428.0 43.3 %collective-permute-start.64 = (bf16[768,768]{1,0:T(8,128)(2,1)S(1)}, bf16[768,768]{1,0:T(8,128)(2,1)S(1)}, u32[]{:S(2)}, u32[]{:S(2)}) collective-permute-start(bf16[768,768]{1,0:T(8,128)(2,1)S(1)} %constant_dynamic-slice_fusion.3), channel_id=1, source_target_pairs={{0,16},{16,0},{1,17},{17,1},{2,18},{18,2},{3,19},{19,3},{4,20},{20... | collective-permute-start | bytes 3538952 | tf_op jit(solution)/shard_map/ppermute | solution.py:28
  428.7 41.1 %collective-permute-start.29 = (bf16[192,2304]{1,0:T(8,128)(2,1)S(1)}, bf16[192,2304]{1,0:T(8,128)(2,1)S(1)}, u32[]{:S(2)}, u32[]{:S(2)}) collective-permute-start(bf16[192,2304]{1,0:T(8,128)(2,1)S(1)} %constant_dynamic-slice_fusion.15), channel_id=1, source_target_pairs={{0,16},{16,0},{1,17},{17,1},{2,18},{18,2},{3,19},{19,3},{4,20},{20... | collective-permute-start | bytes 2654216 | tf_op jit(solution)/shard_map/ppermute | solution.py:28
  433.3 39.3 %collective-permute-start.54 = (bf16[192,3072]{1,0:T(8,128)(2,1)S(1)}, bf16[192,3072]{1,0:T(8,128)(2,1)S(1)}, u32[]{:S(2)}, u32[]{:S(2)}) collective-permute-start(bf16[192,3072]{1,0:T(8,128)(2,1)S(1)} %constant_dynamic-slice_fusion.7), channel_id=1, source_target_pairs={{0,2},{1,3},{2,0},{3,1},{4,6},{5,7},{6,4},{7,5},{8,10},{9,11},{10,... | collective-permute-start | bytes 3538952 | tf_op jit(solution)/shard_map/ppermute | solution.py:28
  470.1 12.4 %collective-permute-start.30 = (bf16[96,2304]{1,0:T(8,128)(2,1)S(1)}, bf16[96,2304]{1,0:T(8,128)(2,1)S(1)}, u32[]{:S(2)}, u32[]{:S(2)}) collective-permute-start(bf16[96,2304]{1,0:T(8,128)(2,1)S(1)} %constant_dynamic-slice_fusion.14), channel_id=1, source_target_pairs={{0,2},{1,3},{2,0},{3,1},{4,6},{5,7},{6,4},{7,5},{8,10},{9,11},{10,... | collective-permute-start | bytes 1327112 | tf_op jit(solution)/shard_map/ppermute | solution.py:28
  471.7 20.7 %collective-permute-start.65 = (bf16[384,768]{1,0:T(8,128)(2,1)S(1)}, bf16[384,768]{1,0:T(8,128)(2,1)S(1)}, u32[]{:S(2)}, u32[]{:S(2)}) collective-permute-start(bf16[384,768]{1,0:T(8,128)(2,1)S(1)} %constant_dynamic-slice_fusion.2), channel_id=1, source_target_pairs={{0,2},{1,3},{2,0},{3,1},{4,6},{5,7},{6,4},{7,5},{8,10},{9,11},{10,... | collective-permute-start | bytes 1769480 | tf_op jit(solution)/shard_map/ppermute | solution.py:28
  482.6 9.6 %collective-permute-start.31 = (bf16[48,2304]{1,0:T(8,128)(2,1)S(1)}, bf16[48,2304]{1,0:T(8,128)(2,1)S(1)}, u32[]{:S(2)}, u32[]{:S(2)}) collective-permute-start(bf16[48,2304]{1,0:T(8,128)(2,1)S(1)} %constant_dynamic-slice_fusion.13), channel_id=1, source_target_pairs={{0,4},{1,5},{2,6},{3,7},{4,0},{5,1},{6,2},{7,3},{8,12},{9,13},{10,... | collective-permute-start | bytes 663560 | tf_op jit(solution)/shard_map/ppermute | solution.py:28
  484.1 10.8 %collective-permute-start.55 = (bf16[96,3072]{1,0:T(8,128)(2,1)S(1)}, bf16[96,3072]{1,0:T(8,128)(2,1)S(1)}, u32[]{:S(2)}, u32[]{:S(2)}) collective-permute-start(bf16[96,3072]{1,0:T(8,128)(2,1)S(1)} %constant_dynamic-slice_fusion.6), channel_id=1, source_target_pairs={{0,16},{16,0},{1,17},{17,1},{2,18},{18,2},{3,19},{19,3},{4,20},{20... | collective-permute-start | bytes 1769480 | tf_op jit(solution)/shard_map/ppermute | solution.py:28
  492.3 9.5 %collective-permute-start.32 = (bf16[24,2304]{1,0:T(8,128)(2,1)S(1)}, bf16[24,2304]{1,0:T(8,128)(2,1)S(1)}, u32[]{:S(2)}, u32[]{:S(2)}) collective-permute-start(bf16[24,2304]{1,0:T(8,128)(2,1)S(1)} %constant_dynamic-slice_fusion.12), channel_id=1, source_target_pairs={{0,8},{1,9},{2,10},{3,11},{4,12},{5,13},{6,14},{7,15},{8,0},{9,1},... | collective-permute-start | bytes 331784 | tf_op jit(solution)/shard_map/ppermute | solution.py:28
  492.6 10.9 %collective-permute-start.66 = (bf16[192,768]{1,0:T(8,128)(2,1)S(1)}, bf16[192,768]{1,0:T(8,128)(2,1)S(1)}, u32[]{:S(2)}, u32[]{:S(2)}) collective-permute-start(bf16[192,768]{1,0:T(8,128)(2,1)S(1)} %constant_dynamic-slice_fusion.1), channel_id=1, source_target_pairs={{0,4},{1,5},{2,6},{3,7},{4,0},{5,1},{6,2},{7,3},{8,12},{9,13},{10,... | collective-permute-start | bytes 884744 | tf_op jit(solution)/shard_map/ppermute | solution.py:28
  495.2 12.3 %collective-permute-start.56 = (bf16[48,3072]{1,0:T(8,128)(2,1)S(1)}, bf16[48,3072]{1,0:T(8,128)(2,1)S(1)}, u32[]{:S(2)}, u32[]{:S(2)}) collective-permute-start(bf16[48,3072]{1,0:T(8,128)(2,1)S(1)} %constant_dynamic-slice_fusion.5), channel_id=1, source_target_pairs={{0,4},{1,5},{2,6},{3,7},{4,0},{5,1},{6,2},{7,3},{8,12},{9,13},{10,... | collective-permute-start | bytes 884744 | tf_op jit(solution)/shard_map/ppermute | solution.py:28
  501.8 20.0 %collective-permute-start.33 = (bf16[24,2304]{1,0:T(8,128)(2,1)S(1)}, bf16[24,2304]{1,0:T(8,128)(2,1)S(1)}, u32[]{:S(2)}, u32[]{:S(2)}) collective-permute-start(bf16[24,2304]{1,0:T(8,128)(2,1)S(1)} %add_convert_fusion.23), channel_id=1, source_target_pairs={{0,8},{1,9},{2,10},{3,11},{4,12},{5,13},{6,14},{7,15},{8,0},{9,1},... | collective-permute-start | bytes 331784 | tf_op jit(solution)/shard_map/ppermute | solution.py:28
  503.6 15.0 %collective-permute-start.67 = (bf16[96,768]{1,0:T(8,128)(2,1)S(1)}, bf16[96,768]{1,0:T(8,128)(2,1)S(1)}, u32[]{:S(2)}, u32[]{:S(2)}) collective-permute-start(bf16[96,768]{1,0:T(8,128)(2,1)S(1)} %constant_dynamic-slice_fusion), channel_id=1, source_target_pairs={{0,8},{1,9},{2,10},{3,11},{4,12},{5,13},{6,14},{7,15},{8,0},{9,1},... | collective-permute-start | bytes 442376 | tf_op jit(solution)/shard_map/ppermute | solution.py:28
  507.5 12.7 %collective-permute-start.57 = (bf16[24,3072]{1,0:T(8,128)(2,1)S(1)}, bf16[24,3072]{1,0:T(8,128)(2,1)S(1)}, u32[]{:S(2)}, u32[]{:S(2)}) collective-permute-start(bf16[24,3072]{1,0:T(8,128)(2,1)S(1)} %constant_dynamic-slice_fusion.4), channel_id=1, source_target_pairs={{0,8},{1,9},{2,10},{3,11},{4,12},{5,13},{6,14},{7,15},{8,0},{9,1},... | collective-permute-start | bytes 442376 | tf_op jit(solution)/shard_map/ppermute | solution.py:28
  518.7 7.7 %collective-permute-start.68 = (bf16[96,768]{1,0:T(8,128)(2,1)S(1)}, bf16[96,768]{1,0:T(8,128)(2,1)S(1)}, u32[]{:S(2)}, u32[]{:S(2)}) collective-permute-start(bf16[96,768]{1,0:T(8,128)(2,1)S(1)} %add_convert_fusion.20), channel_id=1, source_target_pairs={{0,8},{1,9},{2,10},{3,11},{4,12},{5,13},{6,14},{7,15},{8,0},{9,1},... | collective-permute-start | bytes 442376 | tf_op jit(solution)/shard_map/ppermute | solution.py:28
  520.3 8.9 %collective-permute-start.58 = (bf16[24,3072]{1,0:T(8,128)(2,1)S(1)}, bf16[24,3072]{1,0:T(8,128)(2,1)S(1)}, u32[]{:S(2)}, u32[]{:S(2)}) collective-permute-start(bf16[24,3072]{1,0:T(8,128)(2,1)S(1)} %add_convert_fusion.21), channel_id=1, source_target_pairs={{0,8},{1,9},{2,10},{3,11},{4,12},{5,13},{6,14},{7,15},{8,0},{9,1},... | collective-permute-start | bytes 442376 | tf_op jit(solution)/shard_map/ppermute | solution.py:28
  521.8 10.1 %collective-permute-start.34 = (bf16[48,2304]{1,0:T(8,128)(2,1)S(1)}, bf16[48,2304]{1,0:T(8,128)(2,1)S(1)}, u32[]{:S(2)}, u32[]{:S(2)}) collective-permute-start(bf16[48,2304]{1,0:T(8,128)(2,1)S(1)} %maximum_select_fusion.23), channel_id=1, source_target_pairs={{0,4},{1,5},{2,6},{3,7},{4,0},{5,1},{6,2},{7,3},{8,12},{9,13},{10,... | collective-permute-start | bytes 663560 | tf_op jit(solution)/shard_map/ppermute | solution.py:28
  526.4 8.7 %collective-permute-start.69 = (bf16[192,768]{1,0:T(8,128)(2,1)S(1)}, bf16[192,768]{1,0:T(8,128)(2,1)S(1)}, u32[]{:S(2)}, u32[]{:S(2)}) collective-permute-start(bf16[192,768]{1,0:T(8,128)(2,1)S(1)} %maximum_select_fusion.21), channel_id=1, source_target_pairs={{0,4},{1,5},{2,6},{3,7},{4,0},{5,1},{6,2},{7,3},{8,12},{9,13},{10,... | collective-permute-start | bytes 884744 | tf_op jit(solution)/shard_map/ppermute | solution.py:28
  529.2 9.5 %collective-permute-start.59 = (bf16[48,3072]{1,0:T(8,128)(2,1)S(1)}, bf16[48,3072]{1,0:T(8,128)(2,1)S(1)}, u32[]{:S(2)}, u32[]{:S(2)}) collective-permute-start(bf16[48,3072]{1,0:T(8,128)(2,1)S(1)} %maximum_select_fusion.20), channel_id=1, source_target_pairs={{0,4},{1,5},{2,6},{3,7},{4,0},{5,1},{6,2},{7,3},{8,12},{9,13},{10,... | collective-permute-start | bytes 884744 | tf_op jit(solution)/shard_map/ppermute | solution.py:28
  532.1 8.5 %collective-permute-start.35 = (bf16[96,2304]{1,0:T(8,128)(2,1)S(1)}, bf16[96,2304]{1,0:T(8,128)(2,1)S(1)}, u32[]{:S(2)}, u32[]{:S(2)}) collective-permute-start(bf16[96,2304]{1,0:T(8,128)(2,1)S(1)} %maximum_select_fusion.14), channel_id=1, source_target_pairs={{0,2},{1,3},{2,0},{3,1},{4,6},{5,7},{6,4},{7,5},{8,10},{9,11},{10,... | collective-permute-start | bytes 1327112 | tf_op jit(solution)/shard_map/ppermute | solution.py:28
  535.3 14.2 %collective-permute-start.70 = (bf16[384,768]{1,0:T(8,128)(2,1)S(1)}, bf16[384,768]{1,0:T(8,128)(2,1)S(1)}, u32[]{:S(2)}, u32[]{:S(2)}) collective-permute-start(bf16[384,768]{1,0:T(8,128)(2,1)S(1)} %maximum_select_fusion.12), channel_id=1, source_target_pairs={{0,2},{1,3},{2,0},{3,1},{4,6},{5,7},{6,4},{7,5},{8,10},{9,11},{10,... | collective-permute-start | bytes 1769480 | tf_op jit(solution)/shard_map/ppermute | solution.py:28
  538.8 16.4 %collective-permute-start.60 = (bf16[96,3072]{1,0:T(8,128)(2,1)S(1)}, bf16[96,3072]{1,0:T(8,128)(2,1)S(1)}, u32[]{:S(2)}, u32[]{:S(2)}) collective-permute-start(bf16[96,3072]{1,0:T(8,128)(2,1)S(1)} %maximum_select_fusion.11), channel_id=1, source_target_pairs={{0,16},{16,0},{1,17},{17,1},{2,18},{18,2},{3,19},{19,3},{4,20},{20... | collective-permute-start | bytes 1769480 | tf_op jit(solution)/shard_map/ppermute | solution.py:28
  540.7 33.3 %collective-permute-start.36 = (bf16[192,2304]{1,0:T(8,128)(2,1)S(1)}, bf16[192,2304]{1,0:T(8,128)(2,1)S(1)}, u32[]{:S(2)}, u32[]{:S(2)}) collective-permute-start(bf16[192,2304]{1,0:T(8,128)(2,1)S(1)} %maximum_select_fusion.9), channel_id=1, source_target_pairs={{0,16},{16,0},{1,17},{17,1},{2,18},{18,2},{3,19},{19,3},{4,20},{20... | collective-permute-start | bytes 2654216 | tf_op jit(solution)/shard_map/ppermute | solution.py:28
  550.0 43.0 %collective-permute-start.71 = (bf16[768,768]{1,0:T(8,128)(2,1)S(1)}, bf16[768,768]{1,0:T(8,128)(2,1)S(1)}, u32[]{:S(2)}, u32[]{:S(2)}) collective-permute-start(bf16[768,768]{1,0:T(8,128)(2,1)S(1)} %maximum_select_fusion.8), channel_id=1, source_target_pairs={{0,16},{16,0},{1,17},{17,1},{2,18},{18,2},{3,19},{19,3},{4,20},{20... | collective-permute-start | bytes 3538952 | tf_op jit(solution)/shard_map/ppermute | solution.py:28
  551.4 5.1 collective-permute-start.49
  552.4 41.3 %collective-permute-start.25 = (bf16[64,768]{1,0:T(8,128)(2,1)S(1)}, bf16[64,768]{1,0:T(8,128)(2,1)S(1)}, u32[]{:S(2)}, u32[]{:S(2)}) collective-permute-start(bf16[64,768]{1,0:T(8,128)(2,1)S(1)} %add_convert_fusion.25), channel_id=1, source_target_pairs={{0,8},{1,9},{2,10},{3,11},{4,12},{5,13},{6,14},{7,15},{8,0},{9,1},... | collective-permute-start | bytes 294920 | tf_op jit(solution)/shard_map/ppermute | solution.py:28
  555.4 40.6 %collective-permute-start.61 = (bf16[192,3072]{1,0:T(8,128)(2,1)S(1)}, bf16[192,3072]{1,0:T(8,128)(2,1)S(1)}, u32[]{:S(2)}, u32[]{:S(2)}) collective-permute-start(bf16[192,3072]{1,0:T(8,128)(2,1)S(1)} %maximum_select_fusion.7), channel_id=1, source_target_pairs={{0,2},{1,3},{2,0},{3,1},{4,6},{5,7},{6,4},{7,5},{8,10},{9,11},{10,... | collective-permute-start | bytes 3538952 | tf_op jit(solution)/shard_map/ppermute | solution.py:28
  556.6 38.3 %collective-permute-start.50 = (bf16[96,768]{1,0:T(8,128)(2,1)S(1)}, bf16[96,768]{1,0:T(8,128)(2,1)S(1)}, u32[]{:S(2)}, u32[]{:S(2)}) collective-permute-start(bf16[96,768]{1,0:T(8,128)(2,1)S(1)} %maximum_select_fusion.27), channel_id=1, source_target_pairs={{0,16},{16,0},{1,17},{17,1},{2,18},{18,2},{3,19},{19,3},{4,20},{20... | collective-permute-start | bytes 442376 | tf_op jit(solution)/shard_map/ppermute | solution.py:28
  575.8 44.1 %collective-permute-start.37 = (bf16[384,2304]{1,0:T(8,128)(2,1)}, bf16[384,2304]{1,0:T(8,128)(2,1)}, u32[]{:S(2)}, u32[]{:S(2)}) collective-permute-start(bf16[384,2304]{1,0:T(8,128)(2,1)} %maximum_select_fusion.5), channel_id=1, source_target_pairs={{0,1},{1,0},{2,3},{3,2},{4,5},{5,4},{6,7},{7,6},{8,9},{9,8},{10,11... | collective-permute-start | bytes 5308424 | tf_op jit(solution)/shard_map/ppermute | solution.py:28
  593.7 31.8 %collective-permute-start.72 = (bf16[1536,768]{1,0:T(8,128)(2,1)S(1)}, bf16[1536,768]{1,0:T(8,128)(2,1)}, u32[]{:S(2)}, u32[]{:S(2)}) collective-permute-start(bf16[1536,768]{1,0:T(8,128)(2,1)S(1)} %maximum_select_fusion.4), channel_id=1, source_target_pairs={{0,1},{1,0},{2,3},{3,2},{4,5},{5,4},{6,7},{7,6},{8,9},{9,8},{10,11... | collective-permute-start | bytes 7077896 | tf_op jit(solution)/shard_map/ppermute | solution.py:28
  593.8 6.3 collective-permute-start.26
  594.9 10.5 %collective-permute-start.51 = (bf16[192,768]{1,0:T(8,128)(2,1)S(1)}, bf16[192,768]{1,0:T(8,128)(2,1)}, u32[]{:S(2)}, u32[]{:S(2)}) collective-permute-start(bf16[192,768]{1,0:T(8,128)(2,1)S(1)} %maximum_select_fusion.19), channel_id=1, source_target_pairs={{0,2},{1,3},{2,0},{3,1},{4,6},{5,7},{6,4},{7,5},{8,10},{9,11},{10,... | collective-permute-start | bytes 884744 | tf_op jit(solution)/shard_map/ppermute | solution.py:28
  598.0 33.4 %collective-permute-start.62 = (bf16[384,3072]{1,0:T(8,128)(2,1)}, bf16[384,3072]{1,0:T(8,128)(2,1)}, u32[]{:S(2)}, u32[]{:S(2)}) collective-permute-start(bf16[384,3072]{1,0:T(8,128)(2,1)} %maximum_select_fusion.3), channel_id=1, source_target_pairs={{0,1},{1,0},{2,3},{3,2},{4,5},{5,4},{6,7},{7,6},{8,9},{9,8},{10,11... | collective-permute-start | bytes 7077896 | tf_op jit(solution)/shard_map/ppermute | solution.py:28
  600.1 8.1 %collective-permute-start.27 = (bf16[128,768]{1,0:T(8,128)(2,1)S(1)}, bf16[128,768]{1,0:T(8,128)(2,1)S(1)}, u32[]{:S(2)}, u32[]{:S(2)}) collective-permute-start(bf16[128,768]{1,0:T(8,128)(2,1)S(1)} %maximum_select_fusion.26), channel_id=1, source_target_pairs={{0,1},{1,0},{2,3},{3,2},{4,5},{5,4},{6,7},{7,6},{8,9},{9,8},{10,11... | collective-permute-start | bytes 589832 | tf_op jit(solution)/shard_map/ppermute | solution.py:28
  606.7 10.3 %collective-permute-start.52 = (bf16[384,768]{1,0:T(8,128)(2,1)S(1)}, bf16[384,768]{1,0:T(8,128)(2,1)}, u32[]{:S(2)}, u32[]{:S(2)}) collective-permute-start(bf16[384,768]{1,0:T(8,128)(2,1)S(1)} %maximum_select_fusion.10), channel_id=1, source_target_pairs={{0,1},{1,0},{2,3},{3,2},{4,5},{5,4},{6,7},{7,6},{8,9},{9,8},{10,11... | collective-permute-start | bytes 1769480 | tf_op jit(solution)/shard_map/ppermute | solution.py:28
  (153 other events, 1436.8 us)

commit v3 on v2

--- a/solution.py
+++ b/solution.py
@@ -14,9 +14,6 @@
 BF = jnp.bfloat16
 F32 = jnp.float32
 
-T_W = BF
-T_INV = BF
-P_INV = lax.Precision.DEFAULT
 BLOCK = 256
 GROUP = 256
 SUB = 128
@@ -43,61 +40,68 @@
     return mine, other
 
 
-def seq_total(array, join):
+def seq_quarter(array, join):
     bits = [1 << i for i in range(lax.axis_size("seq").bit_length() - 1)]
     for bit in bits[:2]:
         mine, other = halves(array, bit)
         array = join(mine, swap(other, "seq", bit))
     for bit in bits[2:]:
         array = join(array, swap(array, "seq", bit))
-    for bit in reversed(bits[:2]):
-        other = swap(array, "seq", bit)
-        side = (lax.axis_index("seq") // bit) % 2
-        array = jnp.where(
-            side == 0,
-            jnp.concatenate([array, other], 0),
-            jnp.concatenate([other, array], 0),
-        )
     return array
+
+
+def paired(array, axis, bit, dim):
+    other = swap(array, axis, bit)
+    side = (lax.axis_index(axis) // bit) % 2
+    return jnp.where(
+        side == 0,
+        jnp.concatenate([array, other], dim),
+        jnp.concatenate([other, array], dim),
+    )
+
+
+def seq_whole(array):
+    return paired(paired(array, "seq", 2, 0), "seq", 1, 0)
 
 
 def add_join(first, second):
     return (first.astype(F32) + second.astype(F32)).astype(BF)
 
 
-def stages(first):
-    seq_bits = [("seq", 1 << i) for i in range(1, lax.axis_size("seq").bit_length() - 1)]
-    row_bits = [("row", 1 << i) for i in range(lax.axis_size("row").bit_length() - 1)]
-    rest = row_bits + seq_bits if first == "row" else seq_bits[:1] + row_bits + seq_bits[1:]
-    return [("seq", 1)] + rest
-
-
-def all_sum(array, first):
-    plan = stages(first)
-    held = array
-    for axis, bit in plan:
-        half = held.shape[0] // 2
-        side = (lax.axis_index(axis) // bit) % 2
-        mine = lax.dynamic_slice_in_dim(held, side * half, half, 0)
-        other = lax.dynamic_slice_in_dim(held, (1 - side) * half, half, 0)
-        held = mine.astype(F32) + swap(other.astype(T_W), axis, bit).astype(F32)
-        held = held.astype(T_W)
-    for axis, bit in reversed(plan):
-        half = held.shape[0]
-        side = (lax.axis_index(axis) // bit) % 2
-        other = swap(held, axis, bit)
-        held = jnp.where(
-            side == 0,
-            jnp.concatenate([held, other], 0),
-            jnp.concatenate([other, held], 0),
-        )
-    return held.astype(F32)
-
-
-def small_sum(array):
-    for axis, bit in stages("row"):
-        array = array + swap(array, axis, bit)
-    return array
+def stages(order):
+    row = [("row", 1 << i) for i in range(lax.axis_size("row").bit_length() - 1)]
+    seq = [[("seq", 1 << i)] for i in range(lax.axis_size("seq").bit_length() - 1)]
+    named = {"core": seq[0], "row": row, "near": seq[1], "far": seq[2], "rest": sum(seq[3:], [])}
+    return sum([named[name] for name in ("core",) + order + ("rest",)], [])
+
+
+ORDERS = (("row", "far", "near"), ("near", "row", "far"), ("far", "near", "row"))
+
+
+def advance(state, steps):
+    held, plan, done = state
+    for step in range(done, min(done + steps, 2 * len(plan))):
+        if step < len(plan):
+            axis, bit = plan[step]
+            half = held.shape[0] // 2
+            side = (lax.axis_index(axis) // bit) % 2
+            mine = lax.dynamic_slice_in_dim(held, side * half, half, 0)
+            other = lax.dynamic_slice_in_dim(held, (1 - side) * half, half, 0)
+            held = mine.astype(F32) + swap(other.astype(BF), axis, bit).astype(F32)
+            held = held.astype(BF)
+        else:
+            axis, bit = plan[2 * len(plan) - 1 - step]
+            held = paired(held, axis, bit, 0)
+    return held, plan, min(done + steps, 2 * len(plan))
+
+
+def tied(values, states):
+    values, helds = lax.optimization_barrier((values, [state[0] for state in states]))
+    return values, [(held,) + state[1:] for held, state in zip(helds, states)]
+
+
+def small_steps():
+    return stages(("row", "near", "far"))
 
 
 def extended(cells, width, rows):
@@ -260,33 +264,26 @@
     )(first, second)
 
 
-def mix_kernel(docs, inv_ref, stat_ref, mix_ref, level_ref):
-    width = inv_ref.shape[1]
-    for doc in range(docs):
-        rows = slice(doc * LAND, (doc + 1) * LAND)
-        for g in range(width // GROUP):
-            cols = slice(g * GROUP, (g + 1) * GROUP)
-            mix_ref[rows, cols] = dot_nn(
-                inv_ref[rows, cols].astype(BF), spread(stat_ref[rows, cols])
-            ).astype(BF)
-    level_ref[...] = merge_three(stat_ref[:, width:])
-
-
-def mix_back_kernel(docs, inv_ref, stat_ref, grad_ref, out_ref, dots_ref):
-    width = inv_ref.shape[1]
-    pick = (iota((width, 128), 1) == iota((width, 128), 0) // LAND).astype(BF)
-    for doc in range(docs):
-        rows = slice(doc * LAND, (doc + 1) * LAND)
-        dots = jnp.zeros((LAND, 128), F32)
-        for g in range(width // GROUP):
-            cols = slice(g * GROUP, (g + 1) * GROUP)
-            grad = gathered(dot_tn(inv_ref[rows, cols].astype(BF), grad_ref[rows, cols]))
-            out_ref[rows, cols] = grad.astype(BF)
-            product = grad * stat_ref[rows, cols].astype(F32)
-            high = product.astype(BF)
-            low = (product - high.astype(F32)).astype(BF)
-            dots = dots + dot_nn(high, pick[cols]) + dot_nn(low, pick[cols])
-        dots_ref[rows, :] = dots
+def mix_kernel(inv_ref, stat_ref, mix_ref):
+    width = stat_ref.shape[1] - 128
+    for g in range(width // GROUP):
+        cols = slice(g * GROUP, (g + 1) * GROUP)
+        mix_ref[:, cols] = dot_nn(inv_ref[:, cols], spread(stat_ref[:, cols])).astype(BF)
+    mix_ref[:, width:] = stat_ref[:, width:]
+
+
+def mix_back_kernel(inv_ref, stat_ref, grad_ref, out_ref):
+    width = stat_ref.shape[1] - 128
+    columns = []
+    for g in range(width // GROUP):
+        cols = slice(g * GROUP, (g + 1) * GROUP)
+        grad = gathered(dot_tn(inv_ref[:, cols], grad_ref[:, cols]))
+        out_ref[:, cols] = grad.astype(BF)
+        product = grad * stat_ref[:, cols].astype(F32)
+        lane = iota(product.shape, 1) // LAND
+        for h in range(4):
+            columns.append(jnp.sum(jnp.where(lane == h, product, 0.0), axis=1, keepdims=True))
+    out_ref[:, width:] = split_three(by_head(columns, 0, (LAND, 128)))
 
 
 def make_band(taps_ref, band_s):
@@ -428,17 +425,19 @@
             place = iota((1, BLOCK), 1) + first
             valid = (place >= low) & (place < high)
 
-            def column(ref, g):
+            level, dots = merge_three(level_ref[rows, :]), merge_three(dots_ref[rows, :])
+
+            def column(lanes, g):
                 return jnp.concatenate(
-                    [ref[rows, 4 * g + h : 4 * g + h + 1] for h in range(4)], axis=0
+                    [lanes[:, 4 * g + h : 4 * g + h + 1] for h in range(4)], axis=0
                 )
 
             for g in range(groups):
                 cols = slice(g * GROUP, (g + 1) * GROUP)
                 wide_q, wide_g = spread(mq_ref[rows, cols]), spread(grad_ref[rows, cols])
-                scores = dot_nt(wide_q, k_ref[:, cols]) * scale - column(level_ref, g)
+                scores = dot_nt(wide_q, k_ref[:, cols]) * scale - column(level, g)
                 probs = jnp.exp(jnp.where(valid, scores, NEGATIVE))
-                grad = dot_nt(wide_g, v_ref[:, cols]) - column(dots_ref, g)
+                grad = dot_nt(wide_g, v_ref[:, cols]) - column(dots, g)
                 grad = (probs * grad * scale).astype(BF)
                 gv_s[:, cols] += dot_tn(probs.astype(BF), wide_g)
                 gk_s[:, cols] += dot_tn(grad, wide_q)
@@ -517,9 +516,6 @@
     onehot = ((places >= mark_low) & (places < mark_high)).astype(BF)
     rows_in = (((0,), (0,)), ((), ()))
     cols_in = (((1,), (1,)), ((), ()))
-    pair_count = docs * heads
-    own_pairs = -(-pair_count // seq_count)
-    padded = own_pairs * seq_count
     blocks = tok_count // BLOCK
     window_rows = tok_count + GROUP - SUB
     smem = pl.BlockSpec(memory_space=pltpu.SMEM)
@@ -536,7 +532,7 @@
         return jax.ShapeDtypeStruct(shape, dtype)
 
     means = jnp.dot(onehot, tokens, preferred_element_type=F32) / counts
-    mean_in = seq_total(means.astype(BF), add_join)
+    mean_in = seq_whole(seq_quarter(means.astype(BF), add_join))
     marks = jnp.dot(mean_in, w_qkv[:, : 2 * width], preferred_element_type=F32)
     mark_q = (marks[:, :width] + bias_q).astype(BF)
     mark_k = marks[:, width:].astype(BF)
@@ -544,6 +540,7 @@
     bias = jnp.concatenate([bias_q, jnp.zeros_like(bias_q), bias_v])
     qkv = (jnp.dot(tokens, w_qkv, preferred_element_type=F32) + bias).astype(BF)
     value_ext = extended(qkv[:, 2 * width :], radius, window_rows)
+    value_ext, mark_q, mark_k = lax.optimization_barrier((value_ext, mark_q, mark_k))
 
     def one_col(col):
         return pl.BlockSpec((tok_count, width), lambda i: (0, col))
@@ -561,25 +558,43 @@
         compiler_params=params,
         name="landmark",
     )(bounds, mark_q, qkv, qkv)
-    stats = seq_total(stats, join)
-
-    def own(array):
-        array = array.reshape(docs, LAND, heads, size).transpose(0, 2, 1, 3)
-        array = array.reshape(pair_count, LAND, size)
-        array = jnp.pad(array, ((0, padded - pair_count), (0, 0), (0, 0)))
-        return lax.dynamic_slice_in_dim(array, me * own_pairs, own_pairs, 0)
+    far_count = seq_count // 4
+    own_count = -(-heads // far_count)
+    own_doc = (me % 2) * 2 + (me // 2) % 2
+    own_at = (me // 4) * own_count * size
+    spare = far_count * own_count * size - width
+
+    def own_heads(array):
+        array = jnp.pad(array, ((0, 0), (0, spare)))
+        array = lax.dynamic_slice_in_dim(array, own_at, own_count * size, 1)
+        return array.reshape(LAND, own_count, size).transpose(1, 0, 2)
+
+    def of_doc(array):
+        return lax.dynamic_slice_in_dim(array, own_doc * LAND, LAND, 0)
 
     own_inverse, inverse_pullback = jax.vjp(
-        lambda a, b: pinv_kernel(a, b, scale), own(mark_q).astype(F32), own(mark_k).astype(F32)
+        lambda a, b: pinv_kernel(a, b, scale),
+        own_heads(of_doc(mark_q)).astype(F32),
+        own_heads(of_doc(mark_k)).astype(F32),
     )
-    inverse = lax.all_gather(own_inverse.astype(T_INV), "seq", axis=0, tiled=True)[:pair_count]
-    inverse = inverse.reshape(docs, heads, LAND, LAND).transpose(0, 2, 1, 3)
-    inverse = inverse.reshape(mark_count, width)
-    mix, level = pl.pallas_call(
-        lambda *refs: mix_kernel(docs, *refs),
-        out_shape=(shaped((mark_count, width), BF), shaped((mark_count, 128), F32)),
-        name="mix",
+    inverse = own_inverse.transpose(1, 0, 2).reshape(LAND, own_count * size).astype(BF)
+    for bit in (1, 2):
+        mine, other = halves(stats, bit)
+        stats = join(mine, swap(other, "seq", bit))
+    for i in range(2, seq_count.bit_length() - 1):
+        other = swap(jnp.concatenate([stats, inverse], 1), "seq", 1 << i)
+        stats = join(stats, other[:, : width + 128])
+        other = other[:, width + 128 :]
+        inverse = jnp.where(
+            (me >> i) % 2 == 0,
+            jnp.concatenate([inverse, other], 1),
+            jnp.concatenate([other, inverse], 1),
+        )
+    inverse = inverse[:, :width]
+    mix = pl.pallas_call(
+        mix_kernel, out_shape=shaped((LAND, width + 128), BF), name="mix"
     )(inverse, stats)
+    mix = seq_whole(mix)
 
     taps = jnp.pad(conv_taps, ((0, 0), (0, GROUP - tap_count)))
     mark_spec = fixed(mark_count, width)
@@ -613,10 +628,18 @@
     grad_low_two = grad_two.astype(BF)
     grad_bias_down = jnp.sum(grad_low_two.astype(F32), axis=0)
     grad_w_down = lax.dot_general(active, grad_low_two, rows_in, preferred_element_type=F32)
+    down = (grad_w_down.astype(BF), stages(ORDERS[0]), 0)
+    grad_low_two, (down,) = tied(grad_low_two, [down])
+    down = advance(down, 1)
     grad_active = lax.dot_general(grad_low_two, w_down, cols_in, preferred_element_type=F32)
     grad_upper = (grad_active * slope).astype(BF)
+    grad_upper, (down,) = tied(grad_upper, [down])
+    down = advance(down, 1)
     grad_bias_up = jnp.sum(grad_upper.astype(F32), axis=0)
     grad_w_up = lax.dot_general(hidden_low, grad_upper, rows_in, preferred_element_type=F32)
+    up = (grad_w_up.astype(BF), stages(ORDERS[1]), 0)
+    grad_upper, (up,) = tied(grad_upper, [up])
+    up = advance(up, 1)
     grad_hidden = grad_two + lax.dot_general(
         grad_upper, w_up, cols_in, preferred_element_type=F32
     )
@@ -624,11 +647,16 @@
     grad_shift_one = jnp.sum(grad_hidden, axis=0)
     grad_one = norm_back(grad_hidden * norm1_gain, norm_one, inverse_one)
     grad_low_one = grad_one.astype(BF)
+    grad_low_one, (up,) = tied(grad_low_one, [up])
+    up = advance(up, 1)
     grad_bias_out = jnp.sum(grad_low_one.astype(F32), axis=0)
     grad_w_out = lax.dot_general(mixed, grad_low_one, rows_in, preferred_element_type=F32)
+    out = (grad_w_out.astype(BF), stages(ORDERS[2]), 0)
     grad_mixed = lax.dot_general(
         grad_low_one, w_out, cols_in, preferred_element_type=F32
     ).astype(BF)
+    grad_mixed, (down,) = tied(grad_mixed, [down])
+    down = advance(down, 1)
 
     grad_queries, grad_mix, grad_mk = pl.pallas_call(
         lambda *refs: token_back_kernel(docs, scale, *refs),
@@ -646,7 +674,10 @@
         compiler_params=params,
         name="token_back",
     )(bounds, qkv, grad_mixed, probs, mark_k, mix)
-    grad_mix = seq_total(grad_mix.astype(BF), add_join)
+    grad_mix = seq_quarter(grad_mix.astype(BF), add_join)
+    out = advance(out, 1)
+    grad_mix, (down, up, out) = tied(grad_mix, [down, up, out])
+    down, up, out = advance(down, 1), advance(up, 1), advance(out, 1)
 
     grad_ext = extended(grad_mixed, radius, window_rows)
     grad_conv, products = pl.pallas_call(
@@ -666,16 +697,18 @@
     products = jnp.pad(products, ((0, 0), (0, SUB))).reshape(heads, SUB, reach + 1)
     grad_conv_taps = jnp.sum(products, axis=1)[:, :tap_count]
 
-    grad_avg, dots = pl.pallas_call(
-        lambda *refs: mix_back_kernel(docs, *refs),
-        out_shape=(shaped((mark_count, width), BF), shaped((mark_count, 128), F32)),
-        name="mix_back",
+    grad_avg = pl.pallas_call(
+        mix_back_kernel, out_shape=shaped((LAND, width + 128), BF), name="mix_back"
     )(inverse, stats, grad_mix)
+    grad_avg = seq_whole(grad_avg)
+    grad_avg, (down, up, out) = tied(grad_avg, [down, up, out])
+    down, up, out = advance(down, 1), advance(up, 1), advance(out, 1)
     grad_inverse = jnp.einsum(
-        "pie,pje->pij", own(grad_mix), own(stats[:, :width]), preferred_element_type=F32
+        "pie,pje->pij", own_heads(grad_mix), own_heads(stats[:, :width]),
+        preferred_element_type=F32,
     )
     grad_mq_small, grad_mk_small = inverse_pullback(grad_inverse)
-    lane_spec = fixed(mark_count, 128)
+    lane_spec = pl.BlockSpec((mark_count, 128), lambda i: (0, width // 128))
     grad_keys, grad_values, grad_mq = pl.pallas_call(
         lambda *refs: landmark_back_kernel(docs, scale, *refs),
         grid=(blocks,),
@@ -690,13 +723,18 @@
         scratch_shapes=[pltpu.VMEM((BLOCK, width), F32), pltpu.VMEM((BLOCK, width), F32)],
         compiler_params=params,
         name="landmark_back",
-    )(bounds, qkv, qkv, grad_conv, mark_q, grad_avg, level, dots)
+    )(bounds, qkv, qkv, grad_conv, mark_q, grad_avg, mix, grad_avg)
+    grad_keys, (down, up, out) = tied(grad_keys, [down, up, out])
+    down, up, out = advance(down, 1), advance(up, 1), advance(out, 1)
 
     def placed(array):
-        empty = jnp.zeros((padded, LAND, size), F32)
-        array = lax.dynamic_update_slice_in_dim(empty, array, me * own_pairs, 0)[:pair_count]
-        array = array.reshape(docs, heads, LAND, size).transpose(0, 2, 1, 3)
-        return array.reshape(mark_count, width)
+        array = array.transpose(1, 0, 2).reshape(LAND, own_count * size)
+        array = lax.dynamic_update_slice_in_dim(
+            jnp.zeros((LAND, width + spare), F32), array, own_at, 1
+        )[:, :width]
+        return lax.dynamic_update_slice_in_dim(
+            jnp.zeros((mark_count, width), F32), array, own_doc * LAND, 0
+        )
 
     grad_mq = grad_mq + placed(grad_mq_small)
     grad_mk = grad_mk + placed(grad_mk_small)
@@ -704,7 +742,7 @@
     mark_back = lax.dot_general(
         grad_marks, w_qkv[:, : 2 * width], cols_in, preferred_element_type=F32
     ) / counts
-    mark_back = seq_total(mark_back.astype(BF), add_join)
+    mark_back = mark_back.astype(BF)
 
     grad_bias_q = jnp.sum(grad_queries.astype(F32), axis=0) + jnp.sum(grad_mq, axis=0)
     grad_bias_v = jnp.sum(grad_values.astype(F32), axis=0)
@@ -712,12 +750,6 @@
     grad_w_qkv = lax.dot_general(tokens, grad_projected, rows_in, preferred_element_type=F32)
     grad_w_marks = lax.dot_general(mean_in, grad_marks, rows_in, preferred_element_type=F32)
     grad_w_qkv = grad_w_qkv + jnp.pad(grad_w_marks, ((0, 0), (0, width)))
-    grad_input = (
-        grad_one
-        + lax.dot_general(grad_projected, w_qkv, cols_in, preferred_element_type=F32)
-        + lax.dot_general(onehot, mark_back, rows_in, preferred_element_type=F32)
-    )
-
     small = [
         grad_bias_q, grad_bias_v, grad_conv_taps.reshape(-1), grad_bias_out, grad_gain_one,
         grad_shift_one, grad_bias_up, grad_bias_down, grad_gain_two, grad_shift_two,
@@ -726,16 +758,34 @@
     flat = jnp.concatenate(small)
     lanes = -(-flat.shape[0] // 1024) * 8
     flat = jnp.pad(flat, (0, lanes * 128 - flat.shape[0])).reshape(lanes, 128)
-    flat = small_sum(flat).reshape(-1)
+    late = [
+        (grad_w_qkv[:, i * width : (i + 1) * width].astype(BF), stages(ORDERS[i]), 0)
+        for i in range(3)
+    ]
+    late = [advance(state, 1) for state in late]
+    mark_back = seq_quarter(mark_back, add_join)
+    for axis, bit in small_steps():
+        flat = flat + swap(flat, axis, bit)
+    (mark_back, flat), late = tied((mark_back, flat), late)
+    late = [advance(state, 1) for state in late]
+    mark_back = seq_whole(mark_back)
+    mark_back, late = tied(mark_back, late)
+    sum_qkv = [advance(state, 64)[0].astype(F32) for state in late]
+    sum_w_down, sum_w_up, sum_w_out = [
+        advance(state, 64)[0].astype(F32) for state in (down, up, out)
+    ]
+    sum_w_qkv = jnp.concatenate(sum_qkv, axis=1)
+    flat = flat.reshape(-1)
     pieces = []
     at = 0
     for length in sizes:
         pieces.append(flat[at : at + length])
         at += length
-    sum_w_down = all_sum(grad_w_down, "row")
-    sum_w_up = all_sum(grad_w_up, "seq")
-    sum_w_out = all_sum(grad_w_out, "seq")
-    sum_w_qkv = all_sum(grad_w_qkv, "row")
+    grad_input = (
+        grad_one
+        + lax.dot_general(grad_projected, w_qkv, cols_in, preferred_element_type=F32)
+        + lax.dot_general(onehot, mark_back, rows_in, preferred_element_type=F32)
+    )
     return (
         result[None], grad_input[None], sum_w_qkv, pieces[0], pieces[1],
         pieces[2].reshape(heads, tap_count), sum_w_out, pieces[3], pieces[4], pieces[5],

time: 653 us -> 636 us (0.974)
  other arithmetic: 67.6 us -> 97.7 us
  blocking collectives: 25.8 us -> 0 us
  matrix products: 127 us -> 114 us
  local copies, waits for them, and re-layouts: 99.6 us -> 87.4 us
  Pallas kernels: 51.3 us -> 60.6 us
    all_gather x1 -> x0, blocking collectives: 25.8 us -> none  [per_device(): lax.all_gather(own_inverse.astype(T_INV), 'seq', axis=0, tiled=True)]
    reshape x10 -> x6, local copies, waits for them, and re-layouts: 18.8 us -> 2.72 us  [the longest x4 1.67 us: own_heads(): return array.reshape(LAND, own_count, size).transpose(1, 0, 2)]
    select_n x22 -> x36, other arithmetic: 11.1 us -> 23.1 us  [the longest x34 22.3 us: paired(): jnp.where(side == 0, jnp.concatenate([array, other], dim), jnp.concatenat...]
    dynamic_slice x16 -> x38, local copies, waits for them, and re-layouts: 1.3 us -> 12.6 us  [the longest x30 10.9 us: advance(): other = lax.dynamic_slice_in_dim(held, (1 - side) * half, half, 0)]
    convert_element_type x5 -> x2, local copies, waits for them, and re-layouts: 9.94 us -> 0.19 us  [per_device(): own_inverse.transpose(1, 0, 2).reshape(LAND, own_count * size).astype(BF)]
    convert_element_type x25 -> x35, other arithmetic: 33.6 us -> 40.7 us  [the longest x30 21.3 us: advance(): held = held.astype(BF)]
    ppermute x69 -> x89, waiting for transfers between devices: 180 us -> 174 us  [swap(): return lax.ppermute(array, axis, [(i, i ^ bit) for i in range(count)])]
    ppermute x69 -> x89, starting transfers between devices: 78.6 us -> 77.6 us  [swap(): return lax.ppermute(array, axis, [(i, i ^ bit) for i in range(count)])]
  transfers between devices with their start and end apart: 73 -> 93, of which waited for: 34 -> 37; matrix products, arithmetic and copies ran while one was open for 24% -> 24% of each run, Pallas kernels for 4% -> 2%
where the time goes in v3:
time: 636 us; the launch traced here: 625 us
  waiting for transfers between devices  174 us (27%)
  matrix products  114 us (18%)
  other arithmetic  97.7 us (15%)
  local copies, waits for them, and re-layouts  87.4 us (14%)
  starting transfers between devices  86.2 us (14%)
  Pallas kernels  60.6 us (10%)
    ppermute x89, waiting for transfers between devices, swap(): return lax.ppermute(array, axis, [(i, i ^ bit) for i in range(count)])  174 us
    ppermute x89, starting transfers between devices, swap(): return lax.ppermute(array, axis, [(i, i ^ bit) for i in range(count)])  77.6 us
    unnamed x322, local copies, waits for them, and re-layouts  45.6 us
    select_n x34, other arithmetic, paired(): jnp.where(side == 0, jnp.concatenate([array, other], dim), jnp.concatenat...  22.3 us
    convert_element_type x30, other arithmetic, advance(): held = held.astype(BF)  21.3 us
    convert_element_type x3, other arithmetic, per_device(): advance(state, 64)[0].astype(F32)  18.5 us
    pallas_call x1, Pallas kernels, per_device(): pl.pallas_call(lambda *refs: landmark_kernel(docs, scale, *refs), grid=(1...  14.4 us
    dot_general x1, matrix products, per_device(): lax.dot_general(grad_low_two, w_down, cols_in, preferred_element_type=F32)  14.3 us
  transfers between devices with their start and end apart: 93, of which 37 were waited for; matrix products, arithmetic and copies ran while one was open for 24% of the time, Pallas kernels for 2%

profile of v3, /device:TPU:0, one launch (start us, length us, event | category | flops | bytes accessed | tf_op | source)
XLA Modules:
  0.0 624.6 jit_solution(2059496618018853592)
XLA Ops:
  6.7 5.5 add_convert_fusion.refs_2_.refs_3_.refs_1_
  12.2 2.7 collective-permute-start.3
  17.0 3.0 collective-permute-start
  21.9 2.7 copy.84
  26.5 3.7 collective-permute-done.4
  30.3 2.7 collective-permute-start.5
  33.0 5.3 collective-permute-done.5
  39.7 3.3 collective-permute-done.6
  58.6 14.4 %landmark.1 = bf16[256,896]{1,0:T(8,128)(2,1)S(1)} custom-call(s32[8]{0:T(128)S(1)} %add_subtract_fusion.refs_0_, bf16[256,768]{1,0:T(8,128)(2,1)S(1)} %fusion.57.refs_1_.refs_4_, bf16[1024,2304]{1,0:T(8,128)(2,1)S(1)} %copy-done.1, bf16[1024,2304]{1,0:T(8,128)(2,1)S(1)} %copy-done.1), custom_call_target="tpu_custom_call" | custom-call | tf_op jit(solution)/shard_map/landmark/pallas_call | solution.py:548
  76.1 2.6 join.4
  80.7 4.7 collective-permute-done.9.b_ref
  91.7 2.9 collective-permute-done.10
  99.0 8.1 %collective-permute-done.11 = bf16[64,1280]{1,0:T(8,128)(2,1)S(1)} collective-permute-done((bf16[64,1280]{1,0:T(8,128)(2,1)S(1)}, bf16[64,1280]{1,0:T(8,128)(2,1)S(1)}, u32[]{:S(2)}, u32[]{:S(2)}) %collective-permute-start.11) | collective-permute-done | bytes 163872 | tf_op jit(solution)/shard_map/ppermute | solution.py:25
  114.8 2.6 collective-permute-done.12
  125.7 10.1 %token_.1 = (bf16[1024,768]{1,0:T(8,128)(2,1)S(1)}, bf16[768,1024]{1,0:T(8,128)(2,1)S(1)}) custom-call(s32[8]{0:T(128)S(1)} %add_subtract_fusion.refs_0_, bf16[1024,2304]{1,0:T(8,128)(2,1)S(1)} %copy-done.2, bf16[1152,768]{1,0:T(8,128)(2,1)S(1)} %copy-done.4, bf16[256,768]{1,0:T(8,128)(2,1)S(1)} %copy-done.6, ...), custom_call_target="tpu_custom_call" | custom-call | tf_op jit(solution)/shard_map/token/pallas_call | solution.py:601
  140.4 8.3 %fusion.129 = f32[1024,3072]{1,0:T(8,128)} fusion(bf16[768,3072]{1,0:T(8,128)(2,1)S(1)} %bitcast.255, f32[1024,768]{0,1:T(8,128)S(1)} %get-tuple-element.179, f32[768]{0:T(1024)S(1)} %copy-done.108, f32[768]{0:T(1024)S(1)} %copy-done.105, f32[1024]{0:T(1024)S(1)} %add_rsqrt_fusion.1, f32[1024]{0:T(1024)S(1)} %broadcast_multiply_fusion.5), kind=kOutput, calls=%fused_computation.384 | convolution fusion | flops 4835770368 | bytes 20461568 | tf_op jit(solution)/shard_map/dot_general | solution.py:618
  148.8 11.5 %fusion.141 = (f32[1024]{0:T(1024)S(1)}, f32[1024,768]{0,1:T(8,128)S(1)}) fusion(f32[768]{0:T(1024)S(1)} %copy-done.146, bf16[3072,768]{1,0:T(8,128)(2,1)} %param.29, f32[1024,3072]{1,0:T(8,128)} %fusion.129, f32[3072]{0:T(1024)S(1)} %copy-done.143, f32[768]{0:T(1024)S(1)} %copy-done.108, f32[768]{0:T(1024)S(1)} %copy-done.105, ...), kind=kOutput, calls=%fused_computation.394 | convolution fusion | flops 4868799488 | bytes 23626752 | tf_op jit(solution)/shard_map/dot_general | solution.py:621
  164.7 3.7 convert_reduce_fusion.2
  168.4 3.5 copy.116
  171.9 12.1 %convolution_convert_fusion.1 = bf16[3072,768]{1,0:T(8,128)(2,1)S(1)} fusion(bf16[1024,768]{0,1:T(8,128)(2,1)} %get-tuple-element.64, f32[1024,3072]{1,0:T(8,128)} %fusion.129, f32[3072]{0:T(1024)} %param.28), kind=kOutput, calls=%fused_computation.16 | convolution fusion | flops 4865654784 | bytes 18886656 | tf_op jit(solution)/shard_map/dot_general | solution.py:630
  186.6 14.3 %fusion.7 = bf16[1024,3072]{1,0:T(8,128)(2,1)S(1)} fusion(f32[1024,3072]{1,0:T(8,128)} %fusion.129, bf16[1024,768]{0,1:T(8,128)(2,1)S(1)} %copy-done.59, bf16[3072,768]{1,0:T(8,128)(2,1)} %param.29, f32[3072]{0:T(1024)S(1)} %copy-done.144), kind=kOutput, calls=%fused_computation.9 | convolution fusion | flops 4894752768 | bytes 25178112 | tf_op jit(solution)/shard_map/dot_general | solution.py:634
  201.0 3.1 add_convert_fusion.2
  204.3 5.9 convolution_convert_fusion
  215.0 7.2 %multiply_reduce_fusion = (f32[768]{0:T(1024)}, f32[1024]{0:T(1024)S(1)}, f32[1024]{0:T(1024)S(1)}, f32[768]{0:T(1024)}, f32[1024,768]{0,1:T(8,128)S(1)}) fusion(f32[1024,768]{0,1:T(8,128)S(1)} %copy-done.23, f32[1024]{0:T(1024)S(1)} %add_rsqrt_fusion.1, f32[1024]{0:T(1024)S(1)} %broadcast_multiply_fusion.5, f32[768]{0:T(1024)S(1)} %copy-done.105, ...), kind=kOutput, calls=%fused_computation.37 | convolution fusion | flops 4845989888 | bytes 22065152 | tf_op jit(solution)/shard_map/dot_general | solution.py:643
  226.2 24.1 %collective-permute-done.16 = bf16[768,768]{1,0:T(8,128)(2,1)S(1)} collective-permute-done((bf16[768,768]{1,0:T(8,128)(2,1)S(1)}, bf16[768,768]{1,0:T(8,128)(2,1)S(1)}, u32[]{:S(2)}, u32[]{:S(2)}) %collective-permute-start.16) | collective-permute-done | bytes 1179680 | tf_op jit(solution)/shard_map/ppermute | solution.py:25
  250.8 2.9 add_convert_fusion.1
  258.8 8.3 %token_back.1 = (bf16[1024,768]{1,0:T(8,128)(2,1)S(1)}, f32[256,768]{1,0:T(8,128)S(1)}, f32[256,768]{1,0:T(8,128)S(1)}) custom-call(s32[8]{0:T(128)S(1)} %add_subtract_fusion.refs_0_, bf16[1024,2304]{1,0:T(8,128)(2,1)S(1)} %bitcast.250, bf16[1024,768]{1,0:T(8,128)(2,1)S(1)} %convolution_convert_fusion.2.refs_2_, bf16[768,1024]{1,0:T(8,128)(2,1)S(1)} %copy-done.16, ...), custom_call_target="tpu_custom_call" | custom-call | tf_op jit(solution)/shard_map/token_back/pallas_call | solution.py:661
  268.4 3.0 collective-permute-start.17
  277.8 26.4 %collective-permute-done.20 = bf16[64,768]{1,0:T(8,128)(2,1)S(1)} collective-permute-done((bf16[64,768]{1,0:T(8,128)(2,1)S(1)}, bf16[64,768]{1,0:T(8,128)(2,1)S(1)}, u32[]{:S(2)}, u32[]{:S(2)}) %collective-permute-start.20) | collective-permute-done | bytes 98336 | tf_op jit(solution)/shard_map/ppermute | solution.py:25
  310.0 5.4 conv_back.1
  318.2 2.5 reshape.229
  321.8 3.2 reshape.230
  331.3 2.8 add_convert_fusion.3
  379.0 2.7 collective-permute-start.31
  388.5 9.3 %landmark_back.1 = (bf16[1024,768]{1,0:T(8,128)(2,1)S(1)}, bf16[1024,768]{1,0:T(8,128)(2,1)S(1)}, f32[256,768]{1,0:T(8,128)S(1)}) custom-call(s32[8]{0:T(128)S(1)} %add_subtract_fusion.refs_0_, bf16[1024,2304]{1,0:T(8,128)(2,1)S(1)} %copy-done.3, bf16[1024,2304]{1,0:T(8,128)(2,1)S(1)} %copy-done.3, f32[1024,768]{1,0:T(8,128)S(1)} %copy-done.11, ...), custom_call_target="tpu_custom_call" | custom-call | tf_op jit(solution)/shard_map/landmark_back/pallas_call | solution.py:712
  399.9 3.0 add.647
  408.9 2.5 fusion.54
  416.5 3.1 collective-permute-done.40
  423.8 4.8 collective-permute-done.42
  431.7 5.5 fusion.142
  437.4 4.6 fusion.8
  444.7 2.7 collective-permute-done.75
  447.7 2.7 collective-permute-start.76
  450.5 11.7 %collective-permute-done.76 = bf16[24,768]{1,0:T(8,128)(2,1)S(1)} collective-permute-done((bf16[24,768]{1,0:T(8,128)(2,1)S(1)}, bf16[24,768]{1,0:T(8,128)(2,1)S(1)}, u32[]{:S(2)}, u32[]{:S(2)}) %collective-permute-start.76) | collective-permute-done | bytes 36896 | tf_op jit(solution)/shard_map/ppermute | solution.py:25
  462.1 3.0 collective-permute-start.77
  465.2 4.8 collective-permute-done.77
  470.8 3.8 collective-permute-done.78
  474.6 3.3 collective-permute-done.83
  479.5 5.7 collective-permute-done.79
  497.5 4.3 collective-permute-done.46
  507.3 7.2 %collective-permute-done.50 = bf16[192,768]{1,0:T(8,128)(2,1)S(1)} collective-permute-done((bf16[192,768]{1,0:T(8,128)(2,1)}, bf16[192,768]{1,0:T(8,128)(2,1)S(1)}, u32[]{:S(2)}, u32[]{:S(2)}) %collective-permute-start.50) | collective-permute-done | bytes 294944 | tf_op jit(solution)/shard_map/ppermute | solution.py:25
  517.0 3.3 collective-permute-done.67
  522.7 2.9 collective-permute-done.51
  530.2 3.0 collective-permute-start.69
  535.1 2.9 collective-permute-start.53
  540.0 2.9 collective-permute-start.62
  550.6 4.9 collective-permute-done.71
  557.7 11.6 %collective-permute-done.55 = bf16[48,768]{1,0:T(8,128)(2,1)S(1)} collective-permute-done((bf16[48,768]{1,0:T(8,128)(2,1)S(1)}, bf16[48,768]{1,0:T(8,128)(2,1)S(1)}, u32[]{:S(2)}, u32[]{:S(2)}) %collective-permute-start.55) | collective-permute-done | bytes 73760 | tf_op jit(solution)/shard_map/ppermute | solution.py:25
  589.9 3.2 add_bitcast_fusion
  593.2 3.7 copy.117
  596.9 3.3 fusion.35
  605.9 3.2 maximum_convert_fusion
  609.1 5.9 fusion.10
  615.1 9.3 %fusion.9 = f32[768,3072]{1,0:T(8,128)} fusion(bf16[384,3072]{1,0:T(8,128)(2,1)} %collective-permute-done.87, bf16[384,3072]{1,0:T(8,128)(2,1)} %maximum_select_fusion.2, pred[]{:T(512)S(6)} %eq.196), kind=kLoop, calls=%fused_computation.18 | loop fusion | flops 23592960 | bytes 14155777 | tf_op jit(solution)/shard_map/convert_element_type | solution.py:775
  (781 shorter events, 252.4 us)
Async XLA Ops:
  6.1 6.0 collective-permute-start.2
  12.2 12.6 %collective-permute-start.3 = (bf16[64,768]{1,0:T(8,128)(2,1)S(1)}, bf16[64,768]{1,0:T(8,128)(2,1)S(1)}, u32[]{:S(2)}, u32[]{:S(2)}) collective-permute-start(bf16[64,768]{1,0:T(8,128)(2,1)S(1)} %constant_dynamic-slice_fusion.40), channel_id=1, source_target_pairs={{0,2},{1,3},{2,0},{3,1},{4,6},{5,7},{6,4},{7,5},{8,10},{9,11},{10,... | collective-permute-start | bytes 294920 | tf_op jit(solution)/shard_map/ppermute | solution.py:25
  15.7 27.4 %collective-permute-start.1 = (bf16[16,768]{1,0:T(8,128)(2,1)S(1)}, bf16[16,768]{1,0:T(8,128)(2,1)S(1)}, u32[]{:S(2)}, u32[]{:S(2)}) collective-permute-start(bf16[16,768]{1,0:T(8,128)(2,1)S(1)} %get-tuple-element.152), channel_id=1, source_target_pairs={{1,0},{2,1},{3,2},{4,3},{5,4},{6,5},{7,6},{8,7},{9,8},{10,9},{11,1... | collective-permute-start | bytes 73736 | tf_op jit(solution)/shard_map/ppermute | solution.py:115
  17.0 26.1 %collective-permute-start = (bf16[16,768]{1,0:T(8,128)(2,1)S(1)}, bf16[16,768]{1,0:T(8,128)(2,1)S(1)}, u32[]{:S(2)}, u32[]{:S(2)}) collective-permute-start(bf16[16,768]{1,0:T(8,128)(2,1)S(1)} %get-tuple-element.151), channel_id=1, source_target_pairs={{0,1},{1,2},{2,3},{3,4},{4,5},{5,6},{6,7},{7,8},{8,9},{9,10},{10,1... | collective-permute-start | bytes 73736 | tf_op jit(solution)/shard_map/ppermute | solution.py:113
  30.3 7.9 %collective-permute-start.5 = (bf16[64,768]{1,0:T(8,128)(2,1)S(1)}, bf16[64,768]{1,0:T(8,128)(2,1)S(1)}, u32[]{:S(2)}, u32[]{:S(2)}) collective-permute-start(bf16[64,768]{1,0:T(8,128)(2,1)S(1)} %add_convert_fusion.33), channel_id=1, source_target_pairs={{0,8},{1,9},{2,10},{3,11},{4,12},{5,13},{6,14},{7,15},{8,0},{9,1},... | collective-permute-start | bytes 294920 | tf_op jit(solution)/shard_map/ppermute | solution.py:25
  98.4 8.7 %collective-permute-start.11 = (bf16[64,1280]{1,0:T(8,128)(2,1)S(1)}, bf16[64,1280]{1,0:T(8,128)(2,1)S(1)}, u32[]{:S(2)}, u32[]{:S(2)}) collective-permute-start(bf16[64,1280]{1,0:T(8,128)(2,1)S(1)} %pad_maximum_fusion.3), channel_id=1, source_target_pairs={{0,8},{1,9},{2,10},{3,11},{4,12},{5,13},{6,14},{7,15},{8,0},{9,1},... | collective-permute-start | bytes 491528 | tf_op jit(solution)/shard_map/ppermute | solution.py:25
  186.2 14.8 %collective-permute-start.14 = (bf16[1536,768]{1,0:T(8,128)(2,1)S(1)}, bf16[1536,768]{1,0:T(8,128)(2,1)}, u32[]{:S(2)}, u32[]{:S(2)}) collective-permute-start(bf16[1536,768]{1,0:T(8,128)(2,1)S(1)} %constant_dynamic-slice_fusion.35), channel_id=1, source_target_pairs={{0,1},{1,0},{2,3},{3,2},{4,5},{5,4},{6,7},{7,6},{8,9},{9,8},{10,11... | collective-permute-start | bytes 7077896 | tf_op jit(solution)/shard_map/ppermute | solution.py:25
  213.7 37.0 %collective-permute-start.15 = (bf16[384,3072]{1,0:T(8,128)(2,1)}, bf16[384,3072]{1,0:T(8,128)(2,1)}, u32[]{:S(2)}, u32[]{:S(2)}) collective-permute-start(bf16[384,3072]{1,0:T(8,128)(2,1)} %constant_dynamic-slice_fusion.34), channel_id=1, source_target_pairs={{0,1},{1,0},{2,3},{3,2},{4,5},{5,4},{6,7},{7,6},{8,9},{9,8},{10,11... | collective-permute-start | bytes 7077896 | tf_op jit(solution)/shard_map/ppermute | solution.py:25
  222.3 28.1 %collective-permute-start.16 = (bf16[768,768]{1,0:T(8,128)(2,1)S(1)}, bf16[768,768]{1,0:T(8,128)(2,1)S(1)}, u32[]{:S(2)}, u32[]{:S(2)}) collective-permute-start(bf16[768,768]{1,0:T(8,128)(2,1)S(1)} %constant_dynamic-slice_fusion.33), channel_id=1, source_target_pairs={{0,16},{16,0},{1,17},{17,1},{2,18},{18,2},{3,19},{19,3},{4,20},{20... | collective-permute-start | bytes 3538952 | tf_op jit(solution)/shard_map/ppermute | solution.py:25
  267.1 42.5 %collective-permute-start.18 = (bf16[16,768]{1,0:T(8,128)(2,1)S(1)}, bf16[16,768]{1,0:T(8,128)(2,1)S(1)}, u32[]{:S(2)}, u32[]{:S(2)}) collective-permute-start(bf16[16,768]{1,0:T(8,128)(2,1)S(1)} %get-tuple-element.158), channel_id=1, source_target_pairs={{1,0},{2,1},{3,2},{4,3},{5,4},{6,5},{7,6},{8,7},{9,8},{10,9},{11,1... | collective-permute-start | bytes 73736 | tf_op jit(solution)/shard_map/ppermute | solution.py:115
  268.4 41.2 %collective-permute-start.17 = (bf16[16,768]{1,0:T(8,128)(2,1)S(1)}, bf16[16,768]{1,0:T(8,128)(2,1)S(1)}, u32[]{:S(2)}, u32[]{:S(2)}) collective-permute-start(bf16[16,768]{1,0:T(8,128)(2,1)S(1)} %get-tuple-element.157), channel_id=1, source_target_pairs={{0,1},{1,2},{2,3},{3,4},{4,5},{5,6},{6,7},{7,8},{8,9},{9,10},{10,1... | collective-permute-start | bytes 73736 | tf_op jit(solution)/shard_map/ppermute | solution.py:113
  272.4 56.5 %collective-permute-start.23 = (bf16[384,768]{1,0:T(8,128)(2,1)}, bf16[384,768]{1,0:T(8,128)(2,1)}, u32[]{:S(2)}, u32[]{:S(2)}) collective-permute-start(bf16[384,768]{1,0:T(8,128)(2,1)} %constant_dynamic-slice_fusion.30), channel_id=1, source_target_pairs={{0,4},{1,5},{2,6},{3,7},{4,0},{5,1},{6,2},{7,3},{8,12},{9,13},{10,... | collective-permute-start | bytes 1769480 | tf_op jit(solution)/shard_map/ppermute | solution.py:25
  273.5 57.8 %collective-permute-start.24 = (bf16[192,3072]{1,0:T(8,128)(2,1)}, bf16[192,3072]{1,0:T(8,128)(2,1)}, u32[]{:S(2)}, u32[]{:S(2)}) collective-permute-start(bf16[192,3072]{1,0:T(8,128)(2,1)} %constant_dynamic-slice_fusion.29), channel_id=1, source_target_pairs={{0,2},{1,3},{2,0},{3,1},{4,6},{5,7},{6,4},{7,5},{8,10},{9,11},{10,... | collective-permute-start | bytes 3538952 | tf_op jit(solution)/shard_map/ppermute | solution.py:25
  274.5 29.7 %collective-permute-start.20 = (bf16[64,768]{1,0:T(8,128)(2,1)S(1)}, bf16[64,768]{1,0:T(8,128)(2,1)S(1)}, u32[]{:S(2)}, u32[]{:S(2)}) collective-permute-start(bf16[64,768]{1,0:T(8,128)(2,1)S(1)} %constant_dynamic-slice_fusion.31), channel_id=1, source_target_pairs={{0,2},{1,3},{2,0},{3,1},{4,6},{5,7},{6,4},{7,5},{8,10},{9,11},{10,... | collective-permute-start | bytes 294920 | tf_op jit(solution)/shard_map/ppermute | solution.py:25
  308.9 18.6 %collective-permute-start.25 = (bf16[384,768]{1,0:T(8,128)(2,1)}, bf16[384,768]{1,0:T(8,128)(2,1)}, u32[]{:S(2)}, u32[]{:S(2)}) collective-permute-start(bf16[384,768]{1,0:T(8,128)(2,1)} %constant_dynamic-slice_fusion.28), channel_id=1, source_target_pairs={{0,1},{1,0},{2,3},{3,2},{4,5},{5,4},{6,7},{7,6},{8,9},{9,8},{10,11... | collective-permute-start | bytes 1769480 | tf_op jit(solution)/shard_map/ppermute | solution.py:25
  309.6 16.2 %collective-permute-start.22 = (bf16[64,768]{1,0:T(8,128)(2,1)}, bf16[64,768]{1,0:T(8,128)(2,1)}, u32[]{:S(2)}, u32[]{:S(2)}) collective-permute-start(bf16[64,768]{1,0:T(8,128)(2,1)} %add_convert_fusion.30), channel_id=1, source_target_pairs={{0,8},{1,9},{2,10},{3,11},{4,12},{5,13},{6,14},{7,15},{8,0},{9,1},... | collective-permute-start | bytes 294920 | tf_op jit(solution)/shard_map/ppermute | solution.py:25
  357.9 13.1 %collective-permute-start.26 = (bf16[64,896]{1,0:T(8,128)(2,1)}, bf16[64,896]{1,0:T(8,128)(2,1)}, u32[]{:S(2)}, u32[]{:S(2)}) collective-permute-start(bf16[64,896]{1,0:T(8,128)(2,1)} %mix_back.1), channel_id=1, source_target_pairs={{0,2},{1,3},{2,0},{3,1},{4,6},{5,7},{6,4},{7,5},{8,10},{9,11},{10,... | collective-permute-start | bytes 344072 | tf_op jit(solution)/shard_map/ppermute | solution.py:25
  358.9 13.4 %collective-permute-start.28 = (bf16[192,768]{1,0:T(8,128)(2,1)}, bf16[192,768]{1,0:T(8,128)(2,1)}, u32[]{:S(2)}, u32[]{:S(2)}) collective-permute-start(bf16[192,768]{1,0:T(8,128)(2,1)} %constant_dynamic-slice_fusion.27), channel_id=1, source_target_pairs={{0,2},{1,3},{2,0},{3,1},{4,6},{5,7},{6,4},{7,5},{8,10},{9,11},{10,... | collective-permute-start | bytes 884744 | tf_op jit(solution)/shard_map/ppermute | solution.py:25
  361.6 15.5 %collective-permute-start.29 = (bf16[96,3072]{1,0:T(8,128)(2,1)}, bf16[96,3072]{1,0:T(8,128)(2,1)}, u32[]{:S(2)}, u32[]{:S(2)}) collective-permute-start(bf16[96,3072]{1,0:T(8,128)(2,1)} %constant_dynamic-slice_fusion.26), channel_id=1, source_target_pairs={{0,16},{16,0},{1,17},{17,1},{2,18},{18,2},{3,19},{19,3},{4,20},{20... | collective-permute-start | bytes 1769480 | tf_op jit(solution)/shard_map/ppermute | solution.py:25
  363.8 9.7 %collective-permute-start.30 = (bf16[192,768]{1,0:T(8,128)(2,1)}, bf16[192,768]{1,0:T(8,128)(2,1)}, u32[]{:S(2)}, u32[]{:S(2)}) collective-permute-start(bf16[192,768]{1,0:T(8,128)(2,1)} %constant_dynamic-slice_fusion.25), channel_id=1, source_target_pairs={{0,4},{1,5},{2,6},{3,7},{4,0},{5,1},{6,2},{7,3},{8,12},{9,13},{10,... | collective-permute-start | bytes 884744 | tf_op jit(solution)/shard_map/ppermute | solution.py:25
  379.0 40.6 %collective-permute-start.31 = (bf16[96,768]{1,0:T(8,128)(2,1)}, bf16[96,768]{1,0:T(8,128)(2,1)}, u32[]{:S(2)}, u32[]{:S(2)}) collective-permute-start(bf16[96,768]{1,0:T(8,128)(2,1)} %constant_dynamic-slice_fusion.24), channel_id=1, source_target_pairs={{0,8},{1,9},{2,10},{3,11},{4,12},{5,13},{6,14},{7,15},{8,0},{9,1},... | collective-permute-start | bytes 442376 | tf_op jit(solution)/shard_map/ppermute | solution.py:25
  382.5 46.1 %collective-permute-start.32 = (bf16[48,3072]{1,0:T(8,128)(2,1)}, bf16[48,3072]{1,0:T(8,128)(2,1)}, u32[]{:S(2)}, u32[]{:S(2)}) collective-permute-start(bf16[48,3072]{1,0:T(8,128)(2,1)} %constant_dynamic-slice_fusion.23), channel_id=1, source_target_pairs={{0,4},{1,5},{2,6},{3,7},{4,0},{5,1},{6,2},{7,3},{8,12},{9,13},{10,... | collective-permute-start | bytes 884744 | tf_op jit(solution)/shard_map/ppermute | solution.py:25
  384.8 35.8 %collective-permute-start.33 = (bf16[96,768]{1,0:T(8,128)(2,1)}, bf16[96,768]{1,0:T(8,128)(2,1)}, u32[]{:S(2)}, u32[]{:S(2)}) collective-permute-start(bf16[96,768]{1,0:T(8,128)(2,1)} %constant_dynamic-slice_fusion.22), channel_id=1, source_target_pairs={{0,2},{1,3},{2,0},{3,1},{4,6},{5,7},{6,4},{7,5},{8,10},{9,11},{10,... | collective-permute-start | bytes 442376 | tf_op jit(solution)/shard_map/ppermute | solution.py:25
  413.0 10.7 %collective-permute-start.34 = (bf16[128,768]{1,0:T(8,128)(2,1)S(1)}, bf16[128,768]{1,0:T(8,128)(2,1)S(1)}, u32[]{:S(2)}, u32[]{:S(2)}) collective-permute-start(bf16[128,768]{1,0:T(8,128)(2,1)S(1)} %constant_dynamic-slice_fusion.19), channel_id=1, source_target_pairs={{0,1},{1,0},{2,3},{3,2},{4,5},{5,4},{6,7},{7,6},{8,9},{9,8},{10,11... | collective-permute-start | bytes 589832 | tf_op jit(solution)/shard_map/ppermute | solution.py:25
  423.7 13.5 %collective-permute-start.35 = (bf16[64,768]{1,0:T(8,128)(2,1)S(1)}, bf16[64,768]{1,0:T(8,128)(2,1)S(1)}, u32[]{:S(2)}, u32[]{:S(2)}) collective-permute-start(bf16[64,768]{1,0:T(8,128)(2,1)S(1)} %constant_dynamic-slice_fusion.18), channel_id=1, source_target_pairs={{0,2},{1,3},{2,0},{3,1},{4,6},{5,7},{6,4},{7,5},{8,10},{9,11},{10,... | collective-permute-start | bytes 294920 | tf_op jit(solution)/shard_map/ppermute | solution.py:25
  437.3 10.4 %collective-permute-start.36 = (bf16[64,768]{1,0:T(8,128)(2,1)S(1)}, bf16[64,768]{1,0:T(8,128)(2,1)S(1)}, u32[]{:S(2)}, u32[]{:S(2)}) collective-permute-start(bf16[64,768]{1,0:T(8,128)(2,1)S(1)} %add_convert_fusion.28), channel_id=1, source_target_pairs={{0,4},{1,5},{2,6},{3,7},{4,0},{5,1},{6,2},{7,3},{8,12},{9,13},{10,... | collective-permute-start | bytes 294920 | tf_op jit(solution)/shard_map/ppermute | solution.py:25
  442.3 46.0 %collective-permute-start.43 = (bf16[384,768]{1,0:T(8,128)(2,1)S(1)}, bf16[384,768]{1,0:T(8,128)(2,1)S(1)}, u32[]{:S(2)}, u32[]{:S(2)}) collective-permute-start(bf16[384,768]{1,0:T(8,128)(2,1)S(1)} %constant_dynamic-slice_fusion.17), channel_id=1, source_target_pairs={{0,1},{1,0},{2,3},{3,2},{4,5},{5,4},{6,7},{7,6},{8,9},{9,8},{10,11... | collective-permute-start | bytes 1769480 | tf_op jit(solution)/shard_map/ppermute | solution.py:25
  442.5 46.7 %collective-permute-start.44 = (bf16[384,768]{1,0:T(8,128)(2,1)S(1)}, bf16[384,768]{1,0:T(8,128)(2,1)S(1)}, u32[]{:S(2)}, u32[]{:S(2)}) collective-permute-start(bf16[384,768]{1,0:T(8,128)(2,1)S(1)} %constant_dynamic-slice_fusion.16), channel_id=1, source_target_pairs={{0,1},{1,0},{2,3},{3,2},{4,5},{5,4},{6,7},{7,6},{8,9},{9,8},{10,11... | collective-permute-start | bytes 1769480 | tf_op jit(solution)/shard_map/ppermute | solution.py:25
  444.5 17.6 %collective-permute-start.82 = (bf16[24,3072]{1,0:T(8,128)(2,1)S(1)}, bf16[24,3072]{1,0:T(8,128)(2,1)S(1)}, u32[]{:S(2)}, u32[]{:S(2)}) collective-permute-start(bf16[24,3072]{1,0:T(8,128)(2,1)S(1)} %constant_dynamic-slice_fusion), channel_id=1, source_target_pairs={{0,8},{1,9},{2,10},{3,11},{4,12},{5,13},{6,14},{7,15},{8,0},{9,1},... | collective-permute-start | bytes 442376 | tf_op jit(solution)/shard_map/ppermute | solution.py:25
  447.4 22.7 %collective-permute-start.88 = (bf16[96,768]{1,0:T(8,128)(2,1)S(1)}, bf16[96,768]{1,0:T(8,128)(2,1)S(1)}, u32[]{:S(2)}, u32[]{:S(2)}) collective-permute-start(bf16[96,768]{1,0:T(8,128)(2,1)S(1)} %add_convert_fusion.25), channel_id=1, source_target_pairs={{0,8},{1,9},{2,10},{3,11},{4,12},{5,13},{6,14},{7,15},{8,0},{9,1},... | collective-permute-start | bytes 442376 | tf_op jit(solution)/shard_map/ppermute | solution.py:25
  447.7 14.4 %collective-permute-start.76 = (bf16[24,768]{1,0:T(8,128)(2,1)S(1)}, bf16[24,768]{1,0:T(8,128)(2,1)S(1)}, u32[]{:S(2)}, u32[]{:S(2)}) collective-permute-start(bf16[24,768]{1,0:T(8,128)(2,1)S(1)} %constant_dynamic-slice_fusion.1), channel_id=1, source_target_pairs={{0,8},{1,9},{2,10},{3,11},{4,12},{5,13},{6,14},{7,15},{8,0},{9,1},... | collective-permute-start | bytes 110600 | tf_op jit(solution)/shard_map/ppermute | solution.py:25
  462.1 15.8 %collective-permute-start.37 = (bf16[64,768]{1,0:T(8,128)(2,1)S(1)}, bf16[64,768]{1,0:T(8,128)(2,1)S(1)}, u32[]{:S(2)}, u32[]{:S(2)}) collective-permute-start(bf16[64,768]{1,0:T(8,128)(2,1)S(1)} %add_convert_fusion.27), channel_id=1, source_target_pairs={{0,8},{1,9},{2,10},{3,11},{4,12},{5,13},{6,14},{7,15},{8,0},{9,1},... | collective-permute-start | bytes 294920 | tf_op jit(solution)/shard_map/ppermute | solution.py:25
  462.1 7.8 %collective-permute-start.77 = (bf16[24,768]{1,0:T(8,128)(2,1)S(1)}, bf16[24,768]{1,0:T(8,128)(2,1)S(1)}, u32[]{:S(2)}, u32[]{:S(2)}) collective-permute-start(bf16[24,768]{1,0:T(8,128)(2,1)S(1)} %add_convert_fusion.39), channel_id=1, source_target_pairs={{0,8},{1,9},{2,10},{3,11},{4,12},{5,13},{6,14},{7,15},{8,0},{9,1},... | collective-permute-start | bytes 110600 | tf_op jit(solution)/shard_map/ppermute | solution.py:25
  470.0 7.9 %collective-permute-start.83 = (bf16[24,3072]{1,0:T(8,128)(2,1)S(1)}, bf16[24,3072]{1,0:T(8,128)(2,1)S(1)}, u32[]{:S(2)}, u32[]{:S(2)}) collective-permute-start(bf16[24,3072]{1,0:T(8,128)(2,1)S(1)} %add_convert_fusion.20), channel_id=1, source_target_pairs={{0,8},{1,9},{2,10},{3,11},{4,12},{5,13},{6,14},{7,15},{8,0},{9,1},... | collective-permute-start | bytes 442376 | tf_op jit(solution)/shard_map/ppermute | solution.py:25
  474.5 11.4 %collective-permute-start.89 = (bf16[192,768]{1,0:T(8,128)(2,1)S(1)}, bf16[192,768]{1,0:T(8,128)(2,1)S(1)}, u32[]{:S(2)}, u32[]{:S(2)}) collective-permute-start(bf16[192,768]{1,0:T(8,128)(2,1)S(1)} %maximum_select_fusion.25), channel_id=1, source_target_pairs={{0,2},{1,3},{2,0},{3,1},{4,6},{5,7},{6,4},{7,5},{8,10},{9,11},{10,... | collective-permute-start | bytes 884744 | tf_op jit(solution)/shard_map/ppermute | solution.py:25
  477.8 7.3 %collective-permute-start.79 = (bf16[96,768]{1,0:T(8,128)(2,1)S(1)}, bf16[96,768]{1,0:T(8,128)(2,1)S(1)}, u32[]{:S(2)}, u32[]{:S(2)}) collective-permute-start(bf16[96,768]{1,0:T(8,128)(2,1)S(1)} %maximum_select_fusion.33), channel_id=1, source_target_pairs={{0,2},{1,3},{2,0},{3,1},{4,6},{5,7},{6,4},{7,5},{8,10},{9,11},{10,... | collective-permute-start | bytes 442376 | tf_op jit(solution)/shard_map/ppermute | solution.py:25
  477.9 9.5 %collective-permute-start.84 = (bf16[48,3072]{1,0:T(8,128)(2,1)S(1)}, bf16[48,3072]{1,0:T(8,128)(2,1)S(1)}, u32[]{:S(2)}, u32[]{:S(2)}) collective-permute-start(bf16[48,3072]{1,0:T(8,128)(2,1)S(1)} %maximum_select_fusion.24), channel_id=1, source_target_pairs={{0,4},{1,5},{2,6},{3,7},{4,0},{5,1},{6,2},{7,3},{8,12},{9,13},{10,... | collective-permute-start | bytes 884744 | tf_op jit(solution)/shard_map/ppermute | solution.py:25
  485.9 86.5 %collective-permute-start.80 = (bf16[192,768]{1,0:T(8,128)(2,1)}, bf16[192,768]{1,0:T(8,128)(2,1)}, u32[]{:S(2)}, u32[]{:S(2)}) collective-permute-start(bf16[192,768]{1,0:T(8,128)(2,1)} %maximum_select_fusion.23), channel_id=1, source_target_pairs={{0,4},{1,5},{2,6},{3,7},{4,0},{5,1},{6,2},{7,3},{8,12},{9,13},{10,... | collective-permute-start | bytes 884744 | tf_op jit(solution)/shard_map/ppermute | solution.py:25
  487.5 39.4 %collective-permute-start.90 = (bf16[384,768]{1,0:T(8,128)(2,1)S(1)}, bf16[384,768]{1,0:T(8,128)(2,1)}, u32[]{:S(2)}, u32[]{:S(2)}) collective-permute-start(bf16[384,768]{1,0:T(8,128)(2,1)S(1)} %maximum_select_fusion.15), channel_id=1, source_target_pairs={{0,4},{1,5},{2,6},{3,7},{4,0},{5,1},{6,2},{7,3},{8,12},{9,13},{10,... | collective-permute-start | bytes 1769480 | tf_op jit(solution)/shard_map/ppermute | solution.py:25
  488.4 54.6 %collective-permute-start.85 = (bf16[96,3072]{1,0:T(8,128)(2,1)S(1)}, bf16[96,3072]{1,0:T(8,128)(2,1)}, u32[]{:S(2)}, u32[]{:S(2)}) collective-permute-start(bf16[96,3072]{1,0:T(8,128)(2,1)S(1)} %maximum_select_fusion.14), channel_id=1, source_target_pairs={{0,16},{16,0},{1,17},{17,1},{2,18},{18,2},{3,19},{19,3},{4,20},{20... | collective-permute-start | bytes 1769480 | tf_op jit(solution)/shard_map/ppermute | solution.py:25
  490.8 13.4 %collective-permute-start.49 = (bf16[192,768]{1,0:T(8,128)(2,1)}, bf16[192,768]{1,0:T(8,128)(2,1)}, u32[]{:S(2)}, u32[]{:S(2)}) collective-permute-start(bf16[192,768]{1,0:T(8,128)(2,1)} %constant_dynamic-slice_fusion.13), channel_id=1, source_target_pairs={{0,2},{1,3},{2,0},{3,1},{4,6},{5,7},{6,4},{7,5},{8,10},{9,11},{10,... | collective-permute-start | bytes 884744 | tf_op jit(solution)/shard_map/ppermute | solution.py:25
  494.8 7.0 %collective-permute-start.46 = (bf16[64,768]{1,0:T(8,128)(2,1)}, bf16[64,768]{1,0:T(8,128)(2,1)}, u32[]{:S(2)}, u32[]{:S(2)}) collective-permute-start(bf16[64,768]{1,0:T(8,128)(2,1)} %add_convert_fusion.26), channel_id=1, source_target_pairs={{0,2},{1,3},{2,0},{3,1},{4,6},{5,7},{6,4},{7,5},{8,10},{9,11},{10,... | collective-permute-start | bytes 294920 | tf_op jit(solution)/shard_map/ppermute | solution.py:25
  501.8 12.7 %collective-permute-start.50 = (bf16[192,768]{1,0:T(8,128)(2,1)}, bf16[192,768]{1,0:T(8,128)(2,1)S(1)}, u32[]{:S(2)}, u32[]{:S(2)}) collective-permute-start(bf16[192,768]{1,0:T(8,128)(2,1)} %constant_dynamic-slice_fusion.12), channel_id=1, source_target_pairs={{0,4},{1,5},{2,6},{3,7},{4,0},{5,1},{6,2},{7,3},{8,12},{9,13},{10,... | collective-permute-start | bytes 884744 | tf_op jit(solution)/shard_map/ppermute | solution.py:25
  505.8 9.2 %collective-permute-start.48 = (bf16[192,768]{1,0:T(8,128)(2,1)S(1)}, bf16[192,768]{1,0:T(8,128)(2,1)S(1)}, u32[]{:S(2)}, u32[]{:S(2)}) collective-permute-start(bf16[192,768]{1,0:T(8,128)(2,1)S(1)} %constant_dynamic-slice_fusion.14), channel_id=1, source_target_pairs={{0,16},{16,0},{1,17},{17,1},{2,18},{18,2},{3,19},{19,3},{4,20},{20... | collective-permute-start | bytes 884744 | tf_op jit(solution)/shard_map/ppermute | solution.py:25
  515.4 6.3 %collective-permute-start.59 = (bf16[96,768]{1,0:T(8,128)(2,1)S(1)}, bf16[96,768]{1,0:T(8,128)(2,1)S(1)}, u32[]{:S(2)}, u32[]{:S(2)}) collective-permute-start(bf16[96,768]{1,0:T(8,128)(2,1)S(1)} %constant_dynamic-slice_fusion.8), channel_id=1, source_target_pairs={{0,16},{16,0},{1,17},{17,1},{2,18},{18,2},{3,19},{19,3},{4,20},{20... | collective-permute-start | bytes 442376 | tf_op jit(solution)/shard_map/ppermute | solution.py:25
  521.7 7.2 %collective-permute-start.68 = (bf16[48,768]{1,0:T(8,128)(2,1)S(1)}, bf16[48,768]{1,0:T(8,128)(2,1)S(1)}, u32[]{:S(2)}, u32[]{:S(2)}) collective-permute-start(bf16[48,768]{1,0:T(8,128)(2,1)S(1)} %constant_dynamic-slice_fusion.4), channel_id=1, source_target_pairs={{0,16},{16,0},{1,17},{17,1},{2,18},{18,2},{3,19},{19,3},{4,20},{20... | collective-permute-start | bytes 221192 | tf_op jit(solution)/shard_map/ppermute | solution.py:25
  526.8 6.4 %collective-permute-start.52 = (bf16[48,768]{1,0:T(8,128)(2,1)S(1)}, bf16[48,768]{1,0:T(8,128)(2,1)S(1)}, u32[]{:S(2)}, u32[]{:S(2)}) collective-permute-start(bf16[48,768]{1,0:T(8,128)(2,1)S(1)} %constant_dynamic-slice_fusion.10), channel_id=1, source_target_pairs={{0,2},{1,3},{2,0},{3,1},{4,6},{5,7},{6,4},{7,5},{8,10},{9,11},{10,... | collective-permute-start | bytes 221192 | tf_op jit(solution)/shard_map/ppermute | solution.py:25
  528.9 52.8 %collective-permute-start.91 = (bf16[768,768]{1,0:T(8,128)(2,1)S(1)}, bf16[768,768]{1,0:T(8,128)(2,1)S(1)}, u32[]{:S(2)}, u32[]{:S(2)}) collective-permute-start(bf16[768,768]{1,0:T(8,128)(2,1)S(1)} %maximum_select_fusion.9), channel_id=1, source_target_pairs={{0,16},{16,0},{1,17},{17,1},{2,18},{18,2},{3,19},{19,3},{4,20},{20... | collective-permute-start | bytes 3538952 | tf_op jit(solution)/shard_map/ppermute | solution.py:25
  533.2 5.9 collective-permute-start.61
  540.0 7.0 %collective-permute-start.62 = (bf16[24,768]{1,0:T(8,128)(2,1)S(1)}, bf16[24,768]{1,0:T(8,128)(2,1)S(1)}, u32[]{:S(2)}, u32[]{:S(2)}) collective-permute-start(bf16[24,768]{1,0:T(8,128)(2,1)S(1)} %add_convert_fusion.41), channel_id=1, source_target_pairs={{0,8},{1,9},{2,10},{3,11},{4,12},{5,13},{6,14},{7,15},{8,0},{9,1},... | collective-permute-start | bytes 110600 | tf_op jit(solution)/shard_map/ppermute | solution.py:25
  544.6 40.4 %collective-permute-start.86 = (bf16[192,3072]{1,0:T(8,128)(2,1)S(1)}, bf16[192,3072]{1,0:T(8,128)(2,1)S(1)}, u32[]{:S(2)}, u32[]{:S(2)}) collective-permute-start(bf16[192,3072]{1,0:T(8,128)(2,1)S(1)} %maximum_select_fusion.8), channel_id=1, source_target_pairs={{0,2},{1,3},{2,0},{3,1},{4,6},{5,7},{6,4},{7,5},{8,10},{9,11},{10,... | collective-permute-start | bytes 3538952 | tf_op jit(solution)/shard_map/ppermute | solution.py:25
  547.0 8.5 %collective-permute-start.71 = (bf16[48,768]{1,0:T(8,128)(2,1)S(1)}, bf16[48,768]{1,0:T(8,128)(2,1)S(1)}, u32[]{:S(2)}, u32[]{:S(2)}) collective-permute-start(bf16[48,768]{1,0:T(8,128)(2,1)S(1)} %maximum_select_fusion.37), channel_id=1, source_target_pairs={{0,16},{16,0},{1,17},{17,1},{2,18},{18,2},{3,19},{19,3},{4,20},{20... | collective-permute-start | bytes 221192 | tf_op jit(solution)/shard_map/ppermute | solution.py:25
  548.1 9.2 %collective-permute-start.63 = (bf16[48,768]{1,0:T(8,128)(2,1)S(1)}, bf16[48,768]{1,0:T(8,128)(2,1)S(1)}, u32[]{:S(2)}, u32[]{:S(2)}) collective-permute-start(bf16[48,768]{1,0:T(8,128)(2,1)S(1)} %maximum_select_fusion.36), channel_id=1, source_target_pairs={{0,4},{1,5},{2,6},{3,7},{4,0},{5,1},{6,2},{7,3},{8,12},{9,13},{10,... | collective-permute-start | bytes 221192 | tf_op jit(solution)/shard_map/ppermute | solution.py:25
  555.5 13.7 %collective-permute-start.55 = (bf16[48,768]{1,0:T(8,128)(2,1)S(1)}, bf16[48,768]{1,0:T(8,128)(2,1)S(1)}, u32[]{:S(2)}, u32[]{:S(2)}) collective-permute-start(bf16[48,768]{1,0:T(8,128)(2,1)S(1)} %maximum_select_fusion.35), channel_id=1, source_target_pairs={{0,2},{1,3},{2,0},{3,1},{4,6},{5,7},{6,4},{7,5},{8,10},{9,11},{10,... | collective-permute-start | bytes 221192 | tf_op jit(solution)/shard_map/ppermute | solution.py:25
  557.3 13.5 %collective-permute-start.72 = (bf16[96,768]{1,0:T(8,128)(2,1)S(1)}, bf16[96,768]{1,0:T(8,128)(2,1)S(1)}, u32[]{:S(2)}, u32[]{:S(2)}) collective-permute-start(bf16[96,768]{1,0:T(8,128)(2,1)S(1)} %maximum_select_fusion.32), channel_id=1, source_target_pairs={{0,2},{1,3},{2,0},{3,1},{4,6},{5,7},{6,4},{7,5},{8,10},{9,11},{10,... | collective-permute-start | bytes 442376 | tf_op jit(solution)/shard_map/ppermute | solution.py:25
  572.4 6.8 %collective-permute-start.73 = (bf16[192,768]{1,0:T(8,128)(2,1)S(1)}, bf16[192,768]{1,0:T(8,128)(2,1)S(1)}, u32[]{:S(2)}, u32[]{:S(2)}) collective-permute-start(bf16[192,768]{1,0:T(8,128)(2,1)S(1)} %maximum_select_fusion.22), channel_id=1, source_target_pairs={{0,4},{1,5},{2,6},{3,7},{4,0},{5,1},{6,2},{7,3},{8,12},{9,13},{10,... | collective-permute-start | bytes 884744 | tf_op jit(solution)/shard_map/ppermute | solution.py:25
  574.4 14.2 %collective-permute-start.81 = (bf16[384,768]{1,0:T(8,128)(2,1)S(1)}, bf16[384,768]{1,0:T(8,128)(2,1)S(1)}, u32[]{:S(2)}, u32[]{:S(2)}) collective-permute-start(bf16[384,768]{1,0:T(8,128)(2,1)S(1)} %maximum_select_fusion.13), channel_id=1, source_target_pairs={{0,1},{1,0},{2,3},{3,2},{4,5},{5,4},{6,7},{7,6},{8,9},{9,8},{10,11... | collective-permute-start | bytes 1769480 | tf_op jit(solution)/shard_map/ppermute | solution.py:25
  576.0 8.0 %collective-permute-start.65 = (bf16[192,768]{1,0:T(8,128)(2,1)S(1)}, bf16[192,768]{1,0:T(8,128)(2,1)S(1)}, u32[]{:S(2)}, u32[]{:S(2)}) collective-permute-start(bf16[192,768]{1,0:T(8,128)(2,1)S(1)} %maximum_select_fusion.21), channel_id=1, source_target_pairs={{0,2},{1,3},{2,0},{3,1},{4,6},{5,7},{6,4},{7,5},{8,10},{9,11},{10,... | collective-permute-start | bytes 884744 | tf_op jit(solution)/shard_map/ppermute | solution.py:25
  579.2 8.3 %collective-permute-start.57 = (bf16[192,768]{1,0:T(8,128)(2,1)S(1)}, bf16[192,768]{1,0:T(8,128)(2,1)S(1)}, u32[]{:S(2)}, u32[]{:S(2)}) collective-permute-start(bf16[192,768]{1,0:T(8,128)(2,1)S(1)} %maximum_select_fusion.20), channel_id=1, source_target_pairs={{0,16},{16,0},{1,17},{17,1},{2,18},{18,2},{3,19},{19,3},{4,20},{20... | collective-permute-start | bytes 884744 | tf_op jit(solution)/shard_map/ppermute | solution.py:25
  581.7 18.5 %collective-permute-start.74 = (bf16[384,768]{1,0:T(8,128)(2,1)}, bf16[384,768]{1,0:T(8,128)(2,1)}, u32[]{:S(2)}, u32[]{:S(2)}) collective-permute-start(bf16[384,768]{1,0:T(8,128)(2,1)} %maximum_select_fusion.12), channel_id=1, source_target_pairs={{0,1},{1,0},{2,3},{3,2},{4,5},{5,4},{6,7},{7,6},{8,9},{9,8},{10,11... | collective-permute-start | bytes 1769480 | tf_op jit(solution)/shard_map/ppermute | solution.py:25
  584.0 25.1 %collective-permute-start.92 = (bf16[1536,768]{1,0:T(8,128)(2,1)S(1)}, bf16[1536,768]{1,0:T(8,128)(2,1)}, u32[]{:S(2)}, u32[]{:S(2)}) collective-permute-start(bf16[1536,768]{1,0:T(8,128)(2,1)S(1)} %maximum_select_fusion.3), channel_id=1, source_target_pairs={{0,1},{1,0},{2,3},{3,2},{4,5},{5,4},{6,7},{7,6},{8,9},{9,8},{10,11... | collective-permute-start | bytes 7077896 | tf_op jit(solution)/shard_map/ppermute | solution.py:25
  585.0 17.0 %collective-permute-start.66 = (bf16[384,768]{1,0:T(8,128)(2,1)}, bf16[384,768]{1,0:T(8,128)(2,1)}, u32[]{:S(2)}, u32[]{:S(2)}) collective-permute-start(bf16[384,768]{1,0:T(8,128)(2,1)} %maximum_select_fusion.11), channel_id=1, source_target_pairs={{0,1},{1,0},{2,3},{3,2},{4,5},{5,4},{6,7},{7,6},{8,9},{9,8},{10,11... | collective-permute-start | bytes 1769480 | tf_op jit(solution)/shard_map/ppermute | solution.py:25
  587.5 27.6 %collective-permute-start.87 = (bf16[384,3072]{1,0:T(8,128)(2,1)}, bf16[384,3072]{1,0:T(8,128)(2,1)}, u32[]{:S(2)}, u32[]{:S(2)}) collective-permute-start(bf16[384,3072]{1,0:T(8,128)(2,1)} %maximum_select_fusion.2), channel_id=1, source_target_pairs={{0,1},{1,0},{2,3},{3,2},{4,5},{5,4},{6,7},{7,6},{8,9},{9,8},{10,11... | collective-permute-start | bytes 7077896 | tf_op jit(solution)/shard_map/ppermute | solution.py:25
  589.4 14.6 %collective-permute-start.58 = (bf16[384,768]{1,0:T(8,128)(2,1)}, bf16[384,768]{1,0:T(8,128)(2,1)}, u32[]{:S(2)}, u32[]{:S(2)}) collective-permute-start(bf16[384,768]{1,0:T(8,128)(2,1)} %maximum_select_fusion.10), channel_id=1, source_target_pairs={{0,1},{1,0},{2,3},{3,2},{4,5},{5,4},{6,7},{7,6},{8,9},{9,8},{10,11... | collective-permute-start | bytes 1769480 | tf_op jit(solution)/shard_map/ppermute | solution.py:25
  (188 other events, 1703.8 us)

commit v4 on v3

--- a/solution.py
+++ b/solution.py
@@ -98,10 +98,6 @@
 def tied(values, states):
     values, helds = lax.optimization_barrier((values, [state[0] for state in states]))
     return values, [(held,) + state[1:] for held, state in zip(helds, states)]
-
-
-def small_steps():
-    return stages(("row", "near", "far"))
 
 
 def extended(cells, width, rows):
@@ -628,18 +624,13 @@
     grad_low_two = grad_two.astype(BF)
     grad_bias_down = jnp.sum(grad_low_two.astype(F32), axis=0)
     grad_w_down = lax.dot_general(active, grad_low_two, rows_in, preferred_element_type=F32)
-    down = (grad_w_down.astype(BF), stages(ORDERS[0]), 0)
-    grad_low_two, (down,) = tied(grad_low_two, [down])
-    down = advance(down, 1)
     grad_active = lax.dot_general(grad_low_two, w_down, cols_in, preferred_element_type=F32)
     grad_upper = (grad_active * slope).astype(BF)
-    grad_upper, (down,) = tied(grad_upper, [down])
-    down = advance(down, 1)
     grad_bias_up = jnp.sum(grad_upper.astype(F32), axis=0)
     grad_w_up = lax.dot_general(hidden_low, grad_upper, rows_in, preferred_element_type=F32)
-    up = (grad_w_up.astype(BF), stages(ORDERS[1]), 0)
-    grad_upper, (up,) = tied(grad_upper, [up])
-    up = advance(up, 1)
+    sum_w_down, sum_w_up = lax.psum(
+        (grad_w_down.astype(BF), grad_w_up.astype(BF)), ("row", "seq")
+    )
     grad_hidden = grad_two + lax.dot_general(
         grad_upper, w_up, cols_in, preferred_element_type=F32
     )
@@ -647,16 +638,11 @@
     grad_shift_one = jnp.sum(grad_hidden, axis=0)
     grad_one = norm_back(grad_hidden * norm1_gain, norm_one, inverse_one)
     grad_low_one = grad_one.astype(BF)
-    grad_low_one, (up,) = tied(grad_low_one, [up])
-    up = advance(up, 1)
     grad_bias_out = jnp.sum(grad_low_one.astype(F32), axis=0)
     grad_w_out = lax.dot_general(mixed, grad_low_one, rows_in, preferred_element_type=F32)
-    out = (grad_w_out.astype(BF), stages(ORDERS[2]), 0)
     grad_mixed = lax.dot_general(
         grad_low_one, w_out, cols_in, preferred_element_type=F32
     ).astype(BF)
-    grad_mixed, (down,) = tied(grad_mixed, [down])
-    down = advance(down, 1)
 
     grad_queries, grad_mix, grad_mk = pl.pallas_call(
         lambda *refs: token_back_kernel(docs, scale, *refs),
@@ -675,9 +661,6 @@
         name="token_back",
     )(bounds, qkv, grad_mixed, probs, mark_k, mix)
     grad_mix = seq_quarter(grad_mix.astype(BF), add_join)
-    out = advance(out, 1)
-    grad_mix, (down, up, out) = tied(grad_mix, [down, up, out])
-    down, up, out = advance(down, 1), advance(up, 1), advance(out, 1)
 
     grad_ext = extended(grad_mixed, radius, window_rows)
     grad_conv, products = pl.pallas_call(
@@ -701,8 +684,6 @@
         mix_back_kernel, out_shape=shaped((LAND, width + 128), BF), name="mix_back"
     )(inverse, stats, grad_mix)
     grad_avg = seq_whole(grad_avg)
-    grad_avg, (down, up, out) = tied(grad_avg, [down, up, out])
-    down, up, out = advance(down, 1), advance(up, 1), advance(out, 1)
     grad_inverse = jnp.einsum(
         "pie,pje->pij", own_heads(grad_mix), own_heads(stats[:, :width]),
         preferred_element_type=F32,
@@ -724,8 +705,6 @@
         compiler_params=params,
         name="landmark_back",
     )(bounds, qkv, qkv, grad_conv, mark_q, grad_avg, mix, grad_avg)
-    grad_keys, (down, up, out) = tied(grad_keys, [down, up, out])
-    down, up, out = advance(down, 1), advance(up, 1), advance(out, 1)
 
     def placed(array):
         array = array.transpose(1, 0, 2).reshape(LAND, own_count * size)
@@ -749,33 +728,39 @@
     grad_projected = jnp.concatenate([grad_queries, grad_keys, grad_values], axis=1)
     grad_w_qkv = lax.dot_general(tokens, grad_projected, rows_in, preferred_element_type=F32)
     grad_w_marks = lax.dot_general(mean_in, grad_marks, rows_in, preferred_element_type=F32)
-    grad_w_qkv = grad_w_qkv + jnp.pad(grad_w_marks, ((0, 0), (0, width)))
+    grad_w_qkv = (grad_w_qkv + jnp.pad(grad_w_marks, ((0, 0), (0, width)))).astype(BF)
     small = [
         grad_bias_q, grad_bias_v, grad_conv_taps.reshape(-1), grad_bias_out, grad_gain_one,
         grad_shift_one, grad_bias_up, grad_bias_down, grad_gain_two, grad_shift_two,
     ]
     sizes = [piece.shape[0] for piece in small]
     flat = jnp.concatenate(small)
-    lanes = -(-flat.shape[0] // 1024) * 8
-    flat = jnp.pad(flat, (0, lanes * 128 - flat.shape[0])).reshape(lanes, 128)
+    third = width // 3
+    flat = jnp.pad(flat, (0, third * width - flat.shape[0])).reshape(third, width).astype(BF)
+    w_q, w_k, w_v = [grad_w_qkv[:, i * width : (i + 1) * width] for i in range(3)]
     late = [
-        (grad_w_qkv[:, i * width : (i + 1) * width].astype(BF), stages(ORDERS[i]), 0)
-        for i in range(3)
+        jnp.concatenate([grad_w_out.astype(BF), w_q[: 2 * third]], 0),
+        jnp.concatenate([w_q[2 * third :], w_k], 0),
+        jnp.concatenate([w_v, flat], 0),
     ]
-    late = [advance(state, 1) for state in late]
+    late = [advance((array, stages(order), 0), 1) for array, order in zip(late, ORDERS)]
     mark_back = seq_quarter(mark_back, add_join)
-    for axis, bit in small_steps():
-        flat = flat + swap(flat, axis, bit)
-    (mark_back, flat), late = tied((mark_back, flat), late)
+    mark_back, late = tied(mark_back, late)
     late = [advance(state, 1) for state in late]
     mark_back = seq_whole(mark_back)
     mark_back, late = tied(mark_back, late)
-    sum_qkv = [advance(state, 64)[0].astype(F32) for state in late]
-    sum_w_down, sum_w_up, sum_w_out = [
-        advance(state, 64)[0].astype(F32) for state in (down, up, out)
-    ]
-    sum_w_qkv = jnp.concatenate(sum_qkv, axis=1)
-    flat = flat.reshape(-1)
+    first, second, last = [advance(state, 64)[0].astype(F32) for state in late]
+    sum_w_out = first[:width]
+    sum_w_qkv = jnp.concatenate(
+        [
+            jnp.concatenate([first[width:], second[:third]], 0),
+            second[third:],
+            last[:width],
+        ],
+        axis=1,
+    )
+    sum_w_down, sum_w_up = sum_w_down.astype(F32), sum_w_up.astype(F32)
+    flat = last[width:].reshape(-1)
     pieces = []
     at = 0
     for length in sizes:

time: 636 us -> 604 us (0.950)
  other arithmetic: 97.7 us -> 65.2 us
  between operations: 4.7 us -> 17.3 us
  Pallas kernels: 60.6 us -> 48.4 us
  local copies, waits for them, and re-layouts: 87.4 us -> 78 us
  matrix products: 114 us -> 123 us
  starting transfers between devices: 86.2 us -> 94.4 us
    ppermute x89 -> x54, waiting for transfers between devices: 174 us -> 78.7 us  [swap(): return lax.ppermute(array, axis, [(i, i ^ bit) for i in range(count)])]
    psum x0 -> x1, waiting for transfers between devices: none -> 89.1 us  [per_device(): lax.psum((grad_w_down.astype(BF), grad_w_up.astype(BF)), ('row', 'seq'))]
    select_n x34 -> x19, other arithmetic: 22.3 us -> 4.15 us  [paired(): jnp.where(side == 0, jnp.concatenate([array, other], dim), jnp.concatenat...]
    convert_element_type x30 -> x15, other arithmetic: 21.3 us -> 7.22 us  [advance(): held = held.astype(BF)]
    dynamic_slice x30 -> x12, local copies, waits for them, and re-layouts: 10.9 us -> 0.24 us  [advance(): other = lax.dynamic_slice_in_dim(held, (1 - side) * half, half, 0)]
    ppermute x89 -> x54, starting transfers between devices: 77.6 us -> 87.7 us  [swap(): return lax.ppermute(array, axis, [(i, i ^ bit) for i in range(count)])]
    unnamed x322 -> x284, local copies, waits for them, and re-layouts: 45.6 us -> 37.7 us
    convert_element_type x4 -> x5, other arithmetic: 19.4 us -> 17.2 us  [the longest x2 12 us: per_device(): sum_w_down, sum_w_up = (sum_w_down.astype(F32), sum_w_up.astype(F32))]
  transfers between devices with their start and end apart: 93 -> 59, of which waited for: 37 -> 27; matrix products, arithmetic and copies ran while one was open for 24% -> 18% of each run, Pallas kernels for 2% -> 1%
where the time goes in v4:
time: 604 us; the launch traced here: 594 us
  waiting for transfers between devices  168 us (28%)
  matrix products  123 us (20%)
  starting transfers between devices  94.4 us (16%)
  local copies, waits for them, and re-layouts  78 us (13%)
  other arithmetic  65.2 us (11%)
  Pallas kernels  48.4 us (8%)
  between operations  17.3 us (3%)
    psum x1, waiting for transfers between devices, per_device(): lax.psum((grad_w_down.astype(BF), grad_w_up.astype(BF)), ('row', 'seq'))  89.1 us
    ppermute x54, starting transfers between devices, swap(): return lax.ppermute(array, axis, [(i, i ^ bit) for i in range(count)])  87.7 us
    ppermute x54, waiting for transfers between devices, swap(): return lax.ppermute(array, axis, [(i, i ^ bit) for i in range(count)])  78.7 us
    unnamed x284, local copies, waits for them, and re-layouts  37.7 us
    dot_general x1, matrix products, per_device(): lax.dot_general(grad_low_two, w_down, cols_in, preferred_element_type=F32)  16.9 us
    dot_general x1, matrix products, per_device(): lax.dot_general(active, grad_low_two, rows_in, preferred_element_type=F32)  13 us
  transfers between devices with their start and end apart: 59, of which 27 were waited for; matrix products, arithmetic and copies ran while one was open for 18% of the time, Pallas kernels for 1%

profile of v4, /device:TPU:0, one launch (start us, length us, event | category | flops | bytes accessed | tf_op | source)
XLA Modules:
  0.0 594.4 jit_solution(15164271113829335392)
XLA Ops:
  13.7 5.5 add_convert_fusion.refs_2_.refs_3_.refs_1_
  19.3 2.6 collective-permute-start.3
  26.3 4.7 collective-permute-start.4
  31.0 2.6 collective-permute-done.4
  33.6 3.7 collective-permute-start.5
  37.3 3.6 collective-permute-done.5
  42.6 3.0 collective-permute-done.6
  58.4 2.3 copy-done.2
  60.7 9.5 %landmark.1 = bf16[256,896]{1,0:T(8,128)(2,1)S(1)} custom-call(s32[8]{0:T(128)S(1)} %add_subtract_fusion.refs_0_, bf16[256,768]{1,0:T(8,128)(2,1)S(1)} %fusion.61.refs_1_.refs_4_, bf16[1024,2304]{1,0:T(8,128)(2,1)S(1)} %copy-done.2, bf16[1024,2304]{1,0:T(8,128)(2,1)S(1)} %copy-done.2), custom_call_target="tpu_custom_call" | custom-call | tf_op jit(solution)/shard_map/landmark/pallas_call | solution.py:544
  73.3 2.6 join.4
  79.5 3.5 collective-permute-done.9.b_ref
  83.6 2.2 join.5.a_ref
  90.9 2.7 copy.69
  94.2 2.2 join.6.a_ref
  97.4 9.7 %collective-permute-start.11 = (bf16[64,1280]{1,0:T(8,128)(2,1)S(1)}, bf16[64,1280]{1,0:T(8,128)(2,1)S(1)}, u32[]{:S(2)}, u32[]{:S(2)}) collective-permute-start(bf16[64,1280]{1,0:T(8,128)(2,1)S(1)} %pad_maximum_fusion.4), channel_id=1, source_target_pairs={{0,8},{1,9},{2,10},{3,11},{4,12},{5,13},{6,14},{7,15},{8,0},{9,1},... | collective-permute-start | bytes 491528 | tf_op jit(solution)/shard_map/ppermute | solution.py:25
  107.7 6.5 %collective-permute-done.11 = bf16[64,1280]{1,0:T(8,128)(2,1)S(1)} collective-permute-done((bf16[64,1280]{1,0:T(8,128)(2,1)S(1)}, bf16[64,1280]{1,0:T(8,128)(2,1)S(1)}, u32[]{:S(2)}, u32[]{:S(2)}) %collective-permute-start.11) | collective-permute-done | bytes 163872 | tf_op jit(solution)/shard_map/ppermute | solution.py:25
  114.9 2.2 join.7.stat_ref
  122.2 2.5 collective-permute-done.12
  129.7 2.3 copy-done.3
  133.0 7.7 %token_.1 = (bf16[1024,768]{1,0:T(8,128)(2,1)S(1)}, bf16[768,1024]{1,0:T(8,128)(2,1)S(1)}) custom-call(s32[8]{0:T(128)S(1)} %add_subtract_fusion.refs_0_, bf16[1024,2304]{1,0:T(8,128)(2,1)S(1)} %copy-done.3, bf16[1152,768]{1,0:T(8,128)(2,1)S(1)} %copy-done.5, bf16[256,768]{1,0:T(8,128)(2,1)S(1)} %copy-done.7, ...), custom_call_target="tpu_custom_call" | custom-call | tf_op jit(solution)/shard_map/token/pallas_call | solution.py:597
  143.4 8.6 %fusion.133 = f32[1024,3072]{1,0:T(8,128)} fusion(bf16[768,3072]{1,0:T(8,128)(2,1)S(1)} %bitcast.228, f32[1024,768]{0,1:T(8,128)S(1)} %get-tuple-element.138, f32[768]{0:T(1024)S(1)} %copy-done.95, f32[768]{0:T(1024)S(1)} %copy-done.94, f32[1024]{0:T(1024)S(1)} %add_rsqrt_fusion.1, f32[1024]{0:T(1024)S(1)} %broadcast_multiply_fusion.5), kind=kOutput, calls=%fused_computation.350 | convolution fusion | flops 4835770368 | bytes 20461568 | tf_op jit(solution)/shard_map/dot_general | solution.py:614
  152.1 11.6 %fusion.147 = (f32[1024]{0:T(1024)S(1)}, f32[1024,768]{0,1:T(8,128)S(1)}) fusion(f32[768]{0:T(1024)S(1)} %copy-done.131, bf16[3072,768]{1,0:T(8,128)(2,1)} %param.29, f32[1024,3072]{1,0:T(8,128)} %fusion.133, f32[3072]{0:T(1024)S(1)} %copy-done.129, f32[768]{0:T(1024)S(1)} %copy-done.95, f32[768]{0:T(1024)S(1)} %copy-done.94, ...), kind=kOutput, calls=%fused_computation.362 | convolution fusion | flops 4868799488 | bytes 23626752 | tf_op jit(solution)/shard_map/dot_general | solution.py:617
  165.0 3.4 fusion.15
  170.3 13.0 %convolution_convert_fusion = bf16[3072,768]{1,0:T(8,128)(2,1)} fusion(bf16[1024,768]{0,1:T(8,128)(2,1)S(1)} %get-tuple-element.102, f32[1024,3072]{1,0:T(8,128)} %fusion.133, f32[3072]{0:T(1024)S(1)} %copy-done.129), kind=kOutput, calls=%fused_computation.15 | convolution fusion | flops 4865654784 | bytes 18886656 | tf_op jit(solution)/shard_map/dot_general | solution.py:626
  183.4 16.9 %fusion.148 = (bf16[3072]{0:T(1024)(128)(2,1)}, bf16[1024,3072]{1,0:T(8,128)(2,1)}) fusion(f32[1024,3072]{1,0:T(8,128)} %fusion.133, f32[3072]{0:T(1024)S(1)} %copy-done.129, bf16[1024,768]{0,1:T(8,128)(2,1)S(1)} %get-tuple-element.102, bf16[3072,768]{1,0:T(8,128)(2,1)} %param.29), kind=kOutput, calls=%fused_computation.363 | convolution fusion | flops 4897895424 | bytes 25184256 | tf_op jit(solution)/shard_map/dot_general | solution.py:627
  200.3 10.8 %multiply_reduce_fusion = (bf16[768]{0:T(1024)(128)(2,1)}, f32[1024]{0:T(1024)S(1)}, f32[1024]{0:T(1024)S(1)}, bf16[768]{0:T(1024)(128)(2,1)}, f32[1024,768]{0,1:T(8,128)S(1)}) fusion(f32[1024,768]{0,1:T(8,128)S(1)} %get-tuple-element.138, f32[1024]{0:T(1024)S(1)} %add_rsqrt_fusion.1, f32[1024]{0:T(1024)S(1)} %broadcast_multiply_fusion.5, ...), kind=kOutput, calls=%fused_computation.27 | convolution fusion | flops 4845989888 | bytes 22062080 | tf_op jit(solution)/shard_map/dot_general | solution.py:634
  212.9 2.5 convolution_convert_fusion.3
  217.1 6.0 %token_back.1 = (bf16[1024,768]{1,0:T(8,128)(2,1)S(1)}, f32[256,768]{1,0:T(8,128)S(1)}, f32[256,768]{1,0:T(8,128)S(1)}) custom-call(s32[8]{0:T(128)S(1)} %add_subtract_fusion.refs_0_, bf16[1024,2304]{1,0:T(8,128)(2,1)S(1)} %bitcast.223, bf16[1024,768]{1,0:T(8,128)(2,1)S(1)} %convolution_convert_fusion.2.refs_2_, ...), custom_call_target="tpu_custom_call" | custom-call | tf_op jit(solution)/shard_map/token_back/pallas_call | solution.py:647
  227.1 3.9 collective-permute-start.17
  231.8 2.5 collective-permute-done.17
  236.3 2.7 collective-permute-done.18
  239.1 7.3 %collective-permute-start.19 = (bf16[64,768]{1,0:T(8,128)(2,1)S(1)}, bf16[64,768]{1,0:T(8,128)(2,1)S(1)}, u32[]{:S(2)}, u32[]{:S(2)}) collective-permute-start(bf16[64,768]{1,0:T(8,128)(2,1)S(1)} %add_convert_fusion.20), channel_id=1, source_target_pairs={{0,8},{1,9},{2,10},{3,11},{4,12},{5,13},{6,14},{7,15},{8,0},{9,1},... | collective-permute-start | bytes 294920 | tf_op jit(solution)/shard_map/ppermute | solution.py:25
  246.7 5.4 conv_back.1
  254.9 2.5 reshape.229
  258.6 3.2 reshape.230
  284.9 2.8 collective-permute-done.20
  291.2 2.3 copy-done.4
  295.4 6.8 %landmark_back.1 = (bf16[1024,768]{1,0:T(8,128)(2,1)S(1)}, bf16[1024,768]{1,0:T(8,128)(2,1)S(1)}, f32[256,768]{1,0:T(8,128)S(1)}) custom-call(s32[8]{0:T(128)S(1)} %add_subtract_fusion.refs_0_, bf16[1024,2304]{1,0:T(8,128)(2,1)S(1)} %copy-done.4, bf16[1024,2304]{1,0:T(8,128)(2,1)S(1)} %copy-done.4, f32[1024,768]{1,0:T(8,128)S(1)} %copy-done.12, ...), custom_call_target="tpu_custom_call" | custom-call | tf_op jit(solution)/shard_map/landmark_back/pallas_call | solution.py:693
  305.2 2.7 fusion.52
  313.3 4.6 fusion.8
  319.2 7.5 %concatenate.220 = bf16[9612]{0:T(1024)(128)(2,1)} concatenate(bf16[768]{0:T(1024)(128)(2,1)} %add_convert_fusion.28, bf16[768]{0:T(1024)(128)(2,1)} %get-tuple-element.116, bf16[396]{0:T(512)(128)(2,1)} %reshape.231, bf16[768]{0:T(1024)(128)(2,1)} %get-tuple-element.103, bf16[768]{0:T(1024)(128)(2,1)} %get-tuple-element.90, bf16[768]{0:T(1024)(128)(2,1)} %get-tuple-element.97, ...), dimensions={0} | concatenate | bytes 38448 | tf_op jit(solution)/shard_map/concatenate | solution.py:737
  338.1 2.9 collective-permute-start.24
  345.9 9.8 %convolution_convert_fusion.1 = bf16[768,3072]{1,0:T(8,128)(2,1)} fusion(bf16[1024,3072]{1,0:T(8,128)(2,1)} %get-tuple-element.147, f32[1024,768]{0,1:T(8,128)S(1)} %copy-done.19, f32[768]{0:T(1024)S(1)} %copy-done.95, f32[768]{0:T(1024)S(1)} %copy-done.94, f32[1024]{0:T(1024)S(1)} %add_rsqrt_fusion.1, f32[1024]{0:T(1024)S(1)} %broadcast_multiply_fusion.5), kind=kOutput, calls=%fused_computation.16 | convolution fusion | flops 4838129664 | bytes 14170112 | tf_op jit(solution)/shard_map/dot_general | solution.py:630
  360.5 2.8 add_convert_fusion.1
  367.3 3.4 collective-permute-done.29
  374.4 10.7 %collective-permute-done.33 = bf16[256,768]{1,0:T(8,128)(2,1)S(1)} collective-permute-done((bf16[256,768]{1,0:T(8,128)(2,1)S(1)}, bf16[256,768]{1,0:T(8,128)(2,1)S(1)}, u32[]{:S(2)}, u32[]{:S(2)}) %collective-permute-start.33) | collective-permute-done | bytes 393248 | tf_op jit(solution)/shard_map/ppermute | solution.py:25
  390.8 7.8 %collective-permute-done.50 = bf16[128,768]{1,0:T(8,128)(2,1)S(1)} collective-permute-done((bf16[128,768]{1,0:T(8,128)(2,1)S(1)}, bf16[128,768]{1,0:T(8,128)(2,1)S(1)}, u32[]{:S(2)}, u32[]{:S(2)}) %collective-permute-start.50) | collective-permute-done | bytes 196640 | tf_op jit(solution)/shard_map/ppermute | solution.py:25
  401.8 2.2 collective-permute-done.34
  405.1 2.5 collective-permute-start.52
  408.3 2.6 collective-permute-start.44
  411.0 3.4 collective-permute-start.53
  420.3 2.9 collective-permute-done.45
  423.3 2.3 collective-permute-done.36
  428.3 4.3 collective-permute-done.37
  437.6 2.7 collective-permute-start.39
  440.9 3.5 copy.116
  444.5 6.9 %collective-permute-done.39 = bf16[160,768]{1,0:T(8,128)(2,1)S(1)} collective-permute-done((bf16[160,768]{1,0:T(8,128)(2,1)S(1)}, bf16[160,768]{1,0:T(8,128)(2,1)S(1)}, u32[]{:S(2)}, u32[]{:S(2)}) %collective-permute-start.39) | collective-permute-done | bytes 245792 | tf_op jit(solution)/shard_map/ppermute | solution.py:25
  454.5 5.9 fusion.149
  460.9 2.5 add_bitcast_fusion
  463.4 3.8 copy.117
  482.4 3.7 pad_maximum_fusion
  486.1 89.1 %all-reduce.8.cloned.1.call-done = (bf16[768,3072]{1,0:T(8,128)(2,1)}, bf16[3072,768]{1,0:T(8,128)(2,1)}) async-done(((bf16[768,3072]{1,0:T(8,128)(2,1)}, bf16[3072,768]{1,0:T(8,128)(2,1)}), (bf16[768,3072]{1,0:T(8,128)(2,1)}, bf16[3072,768]{1,0:T(8,128)(2,1)})) %all-reduce.8.cloned.1.call-update) | async-done | bytes 9437200 | tf_op jit(solution)/shard_map/psum | solution.py:631
  575.3 7.5 %convert_element_type.482 = f32[768,3072]{1,0:T(8,128)} convert(bf16[768,3072]{1,0:T(8,128)(2,1)} %get-tuple-element.99) | non-fusion elementwise | flops 2359296 | bytes 14155776 | tf_op jit(solution)/shard_map/convert_element_type | solution.py:762
  582.8 4.5 convert_element_type.484
  (634 shorter events, 180.5 us)
Async XLA Ops:
  7.2 133.6 %copy-start = (bf16[768,768]{1,0:T(8,128)(2,1)S(1)}, bf16[768,768]{1,0:T(8,128)(2,1)}, u32[]{:S(2)}) copy-start(bf16[768,768]{1,0:T(8,128)(2,1)} %param.23) | copy-start | bytes 3538948
  7.2 568.0 %all-reduce.8.cloned.1.call-start = ((), (), s32[]{:S(2)}) async-start(), calls=%async_computation | async-start | bytes 18874368 | tf_op jit(solution)/shard_map/psum | solution.py:631
  13.2 6.0 %collective-permute-start.2 = (bf16[128,768]{1,0:T(8,128)(2,1)S(1)}, bf16[128,768]{1,0:T(8,128)(2,1)S(1)}, u32[]{:S(2)}, u32[]{:S(2)}) collective-permute-start(bf16[128,768]{1,0:T(8,128)(2,1)S(1)} %constant_dynamic-slice_fusion.23), channel_id=1, source_target_pairs={{0,1},{1,0},{2,3},{3,2},{4,5},{5,4},{6,7},{7,6},{8,9},{9,8},{10,11... | collective-permute-start | bytes 589832 | tf_op jit(solution)/shard_map/ppermute | solution.py:25
  19.3 6.9 %collective-permute-start.3 = (bf16[64,768]{1,0:T(8,128)(2,1)S(1)}, bf16[64,768]{1,0:T(8,128)(2,1)S(1)}, u32[]{:S(2)}, u32[]{:S(2)}) collective-permute-start(bf16[64,768]{1,0:T(8,128)(2,1)S(1)} %constant_dynamic-slice_fusion.22), channel_id=1, source_target_pairs={{0,2},{1,3},{2,0},{3,1},{4,6},{5,7},{6,4},{7,5},{8,10},{9,11},{10,... | collective-permute-start | bytes 294920 | tf_op jit(solution)/shard_map/ppermute | solution.py:25
  22.7 23.1 %collective-permute-start = (bf16[16,768]{1,0:T(8,128)(2,1)S(1)}, bf16[16,768]{1,0:T(8,128)(2,1)S(1)}, u32[]{:S(2)}, u32[]{:S(2)}) collective-permute-start(bf16[16,768]{1,0:T(8,128)(2,1)S(1)} %get-tuple-element.111), channel_id=1, source_target_pairs={{0,1},{1,2},{2,3},{3,4},{4,5},{5,6},{6,7},{7,8},{8,9},{9,10},{10,1... | collective-permute-start | bytes 73736 | tf_op jit(solution)/shard_map/ppermute | solution.py:109
  24.8 21.0 %collective-permute-start.1 = (bf16[16,768]{1,0:T(8,128)(2,1)S(1)}, bf16[16,768]{1,0:T(8,128)(2,1)S(1)}, u32[]{:S(2)}, u32[]{:S(2)}) collective-permute-start(bf16[16,768]{1,0:T(8,128)(2,1)S(1)} %get-tuple-element.112), channel_id=1, source_target_pairs={{1,0},{2,1},{3,2},{4,3},{5,4},{6,5},{7,6},{8,7},{9,8},{10,9},{11,1... | collective-permute-start | bytes 73736 | tf_op jit(solution)/shard_map/ppermute | solution.py:111
  26.3 7.3 %collective-permute-start.4 = (bf16[64,768]{1,0:T(8,128)(2,1)S(1)}, bf16[64,768]{1,0:T(8,128)(2,1)S(1)}, u32[]{:S(2)}, u32[]{:S(2)}) collective-permute-start(bf16[64,768]{1,0:T(8,128)(2,1)S(1)} %add_convert_fusion.24), channel_id=1, source_target_pairs={{0,4},{1,5},{2,6},{3,7},{4,0},{5,1},{6,2},{7,3},{8,12},{9,13},{10,... | collective-permute-start | bytes 294920 | tf_op jit(solution)/shard_map/ppermute | solution.py:25
  33.6 7.3 %collective-permute-start.5 = (bf16[64,768]{1,0:T(8,128)(2,1)S(1)}, bf16[64,768]{1,0:T(8,128)(2,1)S(1)}, u32[]{:S(2)}, u32[]{:S(2)}) collective-permute-start(bf16[64,768]{1,0:T(8,128)(2,1)S(1)} %add_convert_fusion.23), channel_id=1, source_target_pairs={{0,8},{1,9},{2,10},{3,11},{4,12},{5,13},{6,14},{7,15},{8,0},{9,1},... | collective-permute-start | bytes 294920 | tf_op jit(solution)/shard_map/ppermute | solution.py:25
  41.0 4.7 collective-permute-start.6
  45.7 1.7 collective-permute-start.7
  51.1 56.0 %copy-start.104 = (f32[3,64]{1,0:T(4,128)}, f32[3,64]{1,0:T(4,128)S(1)}, u32[]{:S(2)}) copy-start(f32[3,64]{1,0:T(4,128)S(1)} %get-tuple-element.132) | copy-start | bytes 2308
  51.3 74.6 %copy-start.120 = (f32[3]{0:T(128)}, f32[3]{0:T(128)S(1)}, u32[]{:S(2)}) copy-start(f32[3]{0:T(128)S(1)} %reduce_max.19) | copy-start | bytes 40
  71.0 1.6 collective-permute-start.8
  77.5 5.4 collective-permute-start.9
  87.3 6.2 %collective-permute-start.10 = (bf16[64,1088]{1,0:T(8,128)(2,1)}, bf16[64,1088]{1,0:T(8,128)(2,1)S(1)}, u32[]{:S(2)}, u32[]{:S(2)}) collective-permute-start(bf16[64,1088]{1,0:T(8,128)(2,1)} %pad_maximum_fusion.5), channel_id=1, source_target_pairs={{0,4},{1,5},{2,6},{3,7},{4,0},{5,1},{6,2},{7,3},{8,12},{9,13},{10,... | collective-permute-start | bytes 417800 | tf_op jit(solution)/shard_map/ppermute | solution.py:25
  90.9 38.8 %copy-start.5 = (bf16[1152,768]{1,0:T(8,128)(2,1)S(1)}, bf16[1152,768]{1,0:T(8,128)(2,1)}, u32[]{:S(2)}) copy-start(bf16[1152,768]{1,0:T(8,128)(2,1)} %maximum_maximum_fusion.refs_2_) | copy-start | bytes 5308420
  97.4 16.8 %collective-permute-start.11 = (bf16[64,1280]{1,0:T(8,128)(2,1)S(1)}, bf16[64,1280]{1,0:T(8,128)(2,1)S(1)}, u32[]{:S(2)}, u32[]{:S(2)}) collective-permute-start(bf16[64,1280]{1,0:T(8,128)(2,1)S(1)} %pad_maximum_fusion.4), channel_id=1, source_target_pairs={{0,8},{1,9},{2,10},{3,11},{4,12},{5,13},{6,14},{7,15},{8,0},{9,1},... | collective-permute-start | bytes 491528 | tf_op jit(solution)/shard_map/ppermute | solution.py:25
  119.5 5.3 collective-permute-start.12
  125.8 2.5 collective-permute-start.13
  142.5 68.7 %copy-start.18 = (f32[1024,768]{0,1:T(8,128)}, f32[1024,768]{0,1:T(8,128)S(1)}, u32[]{:S(2)}) copy-start(f32[1024,768]{0,1:T(8,128)S(1)} %get-tuple-element.138) | copy-start | bytes 9437188
  223.2 3.8 collective-permute-start.16
  223.7 22.6 %collective-permute-start.14 = (bf16[16,768]{1,0:T(8,128)(2,1)S(1)}, bf16[16,768]{1,0:T(8,128)(2,1)S(1)}, u32[]{:S(2)}, u32[]{:S(2)}) collective-permute-start(bf16[16,768]{1,0:T(8,128)(2,1)S(1)} %get-tuple-element.118), channel_id=1, source_target_pairs={{0,1},{1,2},{2,3},{3,4},{4,5},{5,6},{6,7},{7,8},{8,9},{9,10},{10,1... | collective-permute-start | bytes 73736 | tf_op jit(solution)/shard_map/ppermute | solution.py:109
  225.7 20.7 %collective-permute-start.15 = (bf16[16,768]{1,0:T(8,128)(2,1)S(1)}, bf16[16,768]{1,0:T(8,128)(2,1)S(1)}, u32[]{:S(2)}, u32[]{:S(2)}) collective-permute-start(bf16[16,768]{1,0:T(8,128)(2,1)S(1)} %get-tuple-element.119), channel_id=1, source_target_pairs={{1,0},{2,1},{3,2},{4,3},{5,4},{6,5},{7,6},{8,7},{9,8},{10,9},{11,1... | collective-permute-start | bytes 73736 | tf_op jit(solution)/shard_map/ppermute | solution.py:111
  227.1 7.3 %collective-permute-start.17 = (bf16[64,768]{1,0:T(8,128)(2,1)S(1)}, bf16[64,768]{1,0:T(8,128)(2,1)S(1)}, u32[]{:S(2)}, u32[]{:S(2)}) collective-permute-start(bf16[64,768]{1,0:T(8,128)(2,1)S(1)} %constant_dynamic-slice_fusion.16), channel_id=1, source_target_pairs={{0,2},{1,3},{2,0},{3,1},{4,6},{5,7},{6,4},{7,5},{8,10},{9,11},{10,... | collective-permute-start | bytes 294920 | tf_op jit(solution)/shard_map/ppermute | solution.py:25
  234.3 4.7 collective-permute-start.18
  239.1 23.7 %collective-permute-start.19 = (bf16[64,768]{1,0:T(8,128)(2,1)S(1)}, bf16[64,768]{1,0:T(8,128)(2,1)S(1)}, u32[]{:S(2)}, u32[]{:S(2)}) collective-permute-start(bf16[64,768]{1,0:T(8,128)(2,1)S(1)} %add_convert_fusion.20), channel_id=1, source_target_pairs={{0,8},{1,9},{2,10},{3,11},{4,12},{5,13},{6,14},{7,15},{8,0},{9,1},... | collective-permute-start | bytes 294920 | tf_op jit(solution)/shard_map/ppermute | solution.py:25
  282.9 4.9 collective-permute-start.20
  287.8 3.3 collective-permute-start.21
  308.7 23.6 %collective-permute-start.22 = (bf16[128,768]{1,0:T(8,128)(2,1)}, bf16[128,768]{1,0:T(8,128)(2,1)}, u32[]{:S(2)}, u32[]{:S(2)}) collective-permute-start(bf16[128,768]{1,0:T(8,128)(2,1)} %constant_dynamic-slice_fusion.13), channel_id=1, source_target_pairs={{0,1},{1,0},{2,3},{3,2},{4,5},{5,4},{6,7},{7,6},{8,9},{9,8},{10,11... | collective-permute-start | bytes 589832 | tf_op jit(solution)/shard_map/ppermute | solution.py:25
  331.7 25.0 %collective-permute-start.27 = (bf16[512,768]{1,0:T(8,128)(2,1)}, bf16[512,768]{1,0:T(8,128)(2,1)}, u32[]{:S(2)}, u32[]{:S(2)}) collective-permute-start(bf16[512,768]{1,0:T(8,128)(2,1)} %fusion.59), channel_id=1, source_target_pairs={{0,1},{1,0},{2,3},{3,2},{4,5},{5,4},{6,7},{7,6},{8,9},{9,8},{10,11... | collective-permute-start | bytes 2359304 | tf_op jit(solution)/shard_map/ppermute | solution.py:25
  333.3 4.8 collective-permute-start.23
  336.2 22.3 %collective-permute-start.28 = (bf16[512,768]{1,0:T(8,128)(2,1)}, bf16[512,768]{1,0:T(8,128)(2,1)}, u32[]{:S(2)}, u32[]{:S(2)}) collective-permute-start(bf16[512,768]{1,0:T(8,128)(2,1)} %fusion.57), channel_id=1, source_target_pairs={{0,1},{1,0},{2,3},{3,2},{4,5},{5,4},{6,7},{7,6},{8,9},{9,8},{10,11... | collective-permute-start | bytes 2359304 | tf_op jit(solution)/shard_map/ppermute | solution.py:25
  338.1 5.5 collective-permute-start.24
  343.1 17.4 %collective-permute-start.26 = (bf16[640,768]{1,0:T(8,128)(2,1)}, bf16[640,768]{1,0:T(8,128)(2,1)}, u32[]{:S(2)}, u32[]{:S(2)}) collective-permute-start(bf16[640,768]{1,0:T(8,128)(2,1)} %fusion.55), channel_id=1, source_target_pairs={{0,1},{1,0},{2,3},{3,2},{4,5},{5,4},{6,7},{7,6},{8,9},{9,8},{10,11... | collective-permute-start | bytes 2949128 | tf_op jit(solution)/shard_map/ppermute | solution.py:25
  344.3 11.4 %collective-permute-start.25 = (bf16[64,768]{1,0:T(8,128)(2,1)}, bf16[64,768]{1,0:T(8,128)(2,1)}, u32[]{:S(2)}, u32[]{:S(2)}) collective-permute-start(bf16[64,768]{1,0:T(8,128)(2,1)} %add_convert_fusion.17), channel_id=1, source_target_pairs={{0,8},{1,9},{2,10},{3,11},{4,12},{5,13},{6,14},{7,15},{8,0},{9,1},... | collective-permute-start | bytes 294920 | tf_op jit(solution)/shard_map/ppermute | solution.py:25
  363.4 7.3 %collective-permute-start.29 = (bf16[64,768]{1,0:T(8,128)(2,1)S(1)}, bf16[64,768]{1,0:T(8,128)(2,1)S(1)}, u32[]{:S(2)}, u32[]{:S(2)}) collective-permute-start(bf16[64,768]{1,0:T(8,128)(2,1)S(1)} %add_convert_fusion.16), channel_id=1, source_target_pairs={{0,2},{1,3},{2,0},{3,1},{4,6},{5,7},{6,4},{7,5},{8,10},{9,11},{10,... | collective-permute-start | bytes 294920 | tf_op jit(solution)/shard_map/ppermute | solution.py:25
  365.1 19.9 %collective-permute-start.33 = (bf16[256,768]{1,0:T(8,128)(2,1)S(1)}, bf16[256,768]{1,0:T(8,128)(2,1)S(1)}, u32[]{:S(2)}, u32[]{:S(2)}) collective-permute-start(bf16[256,768]{1,0:T(8,128)(2,1)S(1)} %constant_dynamic-slice_fusion.9), channel_id=1, source_target_pairs={{0,4},{1,5},{2,6},{3,7},{4,0},{5,1},{6,2},{7,3},{8,12},{9,13},{10,... | collective-permute-start | bytes 1179656 | tf_op jit(solution)/shard_map/ppermute | solution.py:25
  370.7 3.6 collective-permute-start.30
  370.8 15.8 %collective-permute-start.32 = (bf16[256,768]{1,0:T(8,128)(2,1)S(1)}, bf16[256,768]{1,0:T(8,128)(2,1)S(1)}, u32[]{:S(2)}, u32[]{:S(2)}) collective-permute-start(bf16[256,768]{1,0:T(8,128)(2,1)S(1)} %constant_dynamic-slice_fusion.10), channel_id=1, source_target_pairs={{0,2},{1,3},{2,0},{3,1},{4,6},{5,7},{6,4},{7,5},{8,10},{9,11},{10,... | collective-permute-start | bytes 1179656 | tf_op jit(solution)/shard_map/ppermute | solution.py:25
  372.6 14.6 %collective-permute-start.31 = (bf16[320,768]{1,0:T(8,128)(2,1)S(1)}, bf16[320,768]{1,0:T(8,128)(2,1)S(1)}, u32[]{:S(2)}, u32[]{:S(2)}) collective-permute-start(bf16[320,768]{1,0:T(8,128)(2,1)S(1)} %constant_dynamic-slice_fusion.11), channel_id=1, source_target_pairs={{0,16},{16,0},{1,17},{17,1},{2,18},{18,2},{3,19},{19,3},{4,20},{20... | collective-permute-start | bytes 1474568 | tf_op jit(solution)/shard_map/ppermute | solution.py:25
  387.4 11.2 %collective-permute-start.50 = (bf16[128,768]{1,0:T(8,128)(2,1)S(1)}, bf16[128,768]{1,0:T(8,128)(2,1)S(1)}, u32[]{:S(2)}, u32[]{:S(2)}) collective-permute-start(bf16[128,768]{1,0:T(8,128)(2,1)S(1)} %constant_dynamic-slice_fusion.2), channel_id=1, source_target_pairs={{0,2},{1,3},{2,0},{3,1},{4,6},{5,7},{6,4},{7,5},{8,10},{9,11},{10,... | collective-permute-start | bytes 589832 | tf_op jit(solution)/shard_map/ppermute | solution.py:25
  388.8 11.2 %collective-permute-start.42 = (bf16[128,768]{1,0:T(8,128)(2,1)S(1)}, bf16[128,768]{1,0:T(8,128)(2,1)S(1)}, u32[]{:S(2)}, u32[]{:S(2)}) collective-permute-start(bf16[128,768]{1,0:T(8,128)(2,1)S(1)} %constant_dynamic-slice_fusion.5), channel_id=1, source_target_pairs={{0,16},{16,0},{1,17},{17,1},{2,18},{18,2},{3,19},{19,3},{4,20},{20... | collective-permute-start | bytes 589832 | tf_op jit(solution)/shard_map/ppermute | solution.py:25
  389.8 14.2 %collective-permute-start.34 = (bf16[160,768]{1,0:T(8,128)(2,1)S(1)}, bf16[160,768]{1,0:T(8,128)(2,1)S(1)}, u32[]{:S(2)}, u32[]{:S(2)}) collective-permute-start(bf16[160,768]{1,0:T(8,128)(2,1)S(1)} %constant_dynamic-slice_fusion.8), channel_id=1, source_target_pairs={{0,4},{1,5},{2,6},{3,7},{4,0},{5,1},{6,2},{7,3},{8,12},{9,13},{10,... | collective-permute-start | bytes 737288 | tf_op jit(solution)/shard_map/ppermute | solution.py:25
  398.7 6.4 %collective-permute-start.51 = (bf16[64,768]{1,0:T(8,128)(2,1)S(1)}, bf16[64,768]{1,0:T(8,128)(2,1)S(1)}, u32[]{:S(2)}, u32[]{:S(2)}) collective-permute-start(bf16[64,768]{1,0:T(8,128)(2,1)S(1)} %constant_dynamic-slice_fusion.1), channel_id=1, source_target_pairs={{0,16},{16,0},{1,17},{17,1},{2,18},{18,2},{3,19},{19,3},{4,20},{20... | collective-permute-start | bytes 294920 | tf_op jit(solution)/shard_map/ppermute | solution.py:25
  400.1 8.2 %collective-permute-start.43 = (bf16[64,768]{1,0:T(8,128)(2,1)S(1)}, bf16[64,768]{1,0:T(8,128)(2,1)S(1)}, u32[]{:S(2)}, u32[]{:S(2)}) collective-permute-start(bf16[64,768]{1,0:T(8,128)(2,1)S(1)} %constant_dynamic-slice_fusion.4), channel_id=1, source_target_pairs={{0,4},{1,5},{2,6},{3,7},{4,0},{5,1},{6,2},{7,3},{8,12},{9,13},{10,... | collective-permute-start | bytes 294920 | tf_op jit(solution)/shard_map/ppermute | solution.py:25
  404.2 13.2 %collective-permute-start.35 = (bf16[80,768]{1,0:T(8,128)(2,1)S(1)}, bf16[80,768]{1,0:T(8,128)(2,1)S(1)}, u32[]{:S(2)}, u32[]{:S(2)}) collective-permute-start(bf16[80,768]{1,0:T(8,128)(2,1)S(1)} %constant_dynamic-slice_fusion.7), channel_id=1, source_target_pairs={{0,2},{1,3},{2,0},{3,1},{4,6},{5,7},{6,4},{7,5},{8,10},{9,11},{10,... | collective-permute-start | bytes 368648 | tf_op jit(solution)/shard_map/ppermute | solution.py:25
  405.1 5.9 collective-permute-start.52
  408.3 7.6 %collective-permute-start.44 = (bf16[32,768]{1,0:T(8,128)(2,1)S(1)}, bf16[32,768]{1,0:T(8,128)(2,1)S(1)}, u32[]{:S(2)}, u32[]{:S(2)}) collective-permute-start(bf16[32,768]{1,0:T(8,128)(2,1)S(1)} %constant_dynamic-slice_fusion.3), channel_id=1, source_target_pairs={{0,8},{1,9},{2,10},{3,11},{4,12},{5,13},{6,14},{7,15},{8,0},{9,1},... | collective-permute-start | bytes 147464 | tf_op jit(solution)/shard_map/ppermute | solution.py:25
  411.0 8.2 %collective-permute-start.53 = (bf16[32,768]{1,0:T(8,128)(2,1)S(1)}, bf16[32,768]{1,0:T(8,128)(2,1)S(1)}, u32[]{:S(2)}, u32[]{:S(2)}) collective-permute-start(bf16[32,768]{1,0:T(8,128)(2,1)S(1)} %add_convert_fusion.26), channel_id=1, source_target_pairs={{0,8},{1,9},{2,10},{3,11},{4,12},{5,13},{6,14},{7,15},{8,0},{9,1},... | collective-permute-start | bytes 147464 | tf_op jit(solution)/shard_map/ppermute | solution.py:25
  416.0 7.2 %collective-permute-start.45 = (bf16[32,768]{1,0:T(8,128)(2,1)S(1)}, bf16[32,768]{1,0:T(8,128)(2,1)S(1)}, u32[]{:S(2)}, u32[]{:S(2)}) collective-permute-start(bf16[32,768]{1,0:T(8,128)(2,1)S(1)} %add_convert_fusion.27), channel_id=1, source_target_pairs={{0,8},{1,9},{2,10},{3,11},{4,12},{5,13},{6,14},{7,15},{8,0},{9,1},... | collective-permute-start | bytes 147464 | tf_op jit(solution)/shard_map/ppermute | solution.py:25
  417.4 8.2 %collective-permute-start.36 = (bf16[40,768]{1,0:T(8,128)(2,1)S(1)}, bf16[40,768]{1,0:T(8,128)(2,1)S(1)}, u32[]{:S(2)}, u32[]{:S(2)}) collective-permute-start(bf16[40,768]{1,0:T(8,128)(2,1)S(1)} %constant_dynamic-slice_fusion.6), channel_id=1, source_target_pairs={{0,8},{1,9},{2,10},{3,11},{4,12},{5,13},{6,14},{7,15},{8,0},{9,1},... | collective-permute-start | bytes 184328 | tf_op jit(solution)/shard_map/ppermute | solution.py:25
  419.3 7.8 %collective-permute-start.54 = (bf16[64,768]{1,0:T(8,128)(2,1)S(1)}, bf16[64,768]{1,0:T(8,128)(2,1)S(1)}, u32[]{:S(2)}, u32[]{:S(2)}) collective-permute-start(bf16[64,768]{1,0:T(8,128)(2,1)S(1)} %maximum_select_fusion.23), channel_id=1, source_target_pairs={{0,16},{16,0},{1,17},{17,1},{2,18},{18,2},{3,19},{19,3},{4,20},{20... | collective-permute-start | bytes 294920 | tf_op jit(solution)/shard_map/ppermute | solution.py:25
  423.2 11.0 %collective-permute-start.46 = (bf16[64,768]{1,0:T(8,128)(2,1)S(1)}, bf16[64,768]{1,0:T(8,128)(2,1)S(1)}, u32[]{:S(2)}, u32[]{:S(2)}) collective-permute-start(bf16[64,768]{1,0:T(8,128)(2,1)S(1)} %maximum_select_fusion.22), channel_id=1, source_target_pairs={{0,4},{1,5},{2,6},{3,7},{4,0},{5,1},{6,2},{7,3},{8,12},{9,13},{10,... | collective-permute-start | bytes 294920 | tf_op jit(solution)/shard_map/ppermute | solution.py:25
  425.6 6.9 %collective-permute-start.37 = (bf16[40,768]{1,0:T(8,128)(2,1)S(1)}, bf16[40,768]{1,0:T(8,128)(2,1)S(1)}, u32[]{:S(2)}, u32[]{:S(2)}) collective-permute-start(bf16[40,768]{1,0:T(8,128)(2,1)S(1)} %add_convert_fusion.25), channel_id=1, source_target_pairs={{0,8},{1,9},{2,10},{3,11},{4,12},{5,13},{6,14},{7,15},{8,0},{9,1},... | collective-permute-start | bytes 184328 | tf_op jit(solution)/shard_map/ppermute | solution.py:25
  427.1 8.0 %collective-permute-start.55 = (bf16[128,768]{1,0:T(8,128)(2,1)S(1)}, bf16[128,768]{1,0:T(8,128)(2,1)S(1)}, u32[]{:S(2)}, u32[]{:S(2)}) collective-permute-start(bf16[128,768]{1,0:T(8,128)(2,1)S(1)} %maximum_select_fusion.19), channel_id=1, source_target_pairs={{0,2},{1,3},{2,0},{3,1},{4,6},{5,7},{6,4},{7,5},{8,10},{9,11},{10,... | collective-permute-start | bytes 589832 | tf_op jit(solution)/shard_map/ppermute | solution.py:25
  432.6 4.9 collective-permute-start.38
  434.2 6.1 %collective-permute-start.47 = (bf16[128,768]{1,0:T(8,128)(2,1)S(1)}, bf16[128,768]{1,0:T(8,128)(2,1)S(1)}, u32[]{:S(2)}, u32[]{:S(2)}) collective-permute-start(bf16[128,768]{1,0:T(8,128)(2,1)S(1)} %maximum_select_fusion.18), channel_id=1, source_target_pairs={{0,16},{16,0},{1,17},{17,1},{2,18},{18,2},{3,19},{19,3},{4,20},{20... | collective-permute-start | bytes 589832 | tf_op jit(solution)/shard_map/ppermute | solution.py:25
  435.2 17.9 %collective-permute-start.56 = (bf16[256,768]{1,0:T(8,128)(2,1)S(1)}, bf16[256,768]{1,0:T(8,128)(2,1)S(1)}, u32[]{:S(2)}, u32[]{:S(2)}) collective-permute-start(bf16[256,768]{1,0:T(8,128)(2,1)S(1)} %maximum_select_fusion.12), channel_id=1, source_target_pairs={{0,4},{1,5},{2,6},{3,7},{4,0},{5,1},{6,2},{7,3},{8,12},{9,13},{10,... | collective-permute-start | bytes 1179656 | tf_op jit(solution)/shard_map/ppermute | solution.py:25
  437.6 13.8 %collective-permute-start.39 = (bf16[160,768]{1,0:T(8,128)(2,1)S(1)}, bf16[160,768]{1,0:T(8,128)(2,1)S(1)}, u32[]{:S(2)}, u32[]{:S(2)}) collective-permute-start(bf16[160,768]{1,0:T(8,128)(2,1)S(1)} %maximum_select_fusion.13), channel_id=1, source_target_pairs={{0,4},{1,5},{2,6},{3,7},{4,0},{5,1},{6,2},{7,3},{8,12},{9,13},{10,... | collective-permute-start | bytes 737288 | tf_op jit(solution)/shard_map/ppermute | solution.py:25
  440.4 13.2 %collective-permute-start.48 = (bf16[256,768]{1,0:T(8,128)(2,1)S(1)}, bf16[256,768]{1,0:T(8,128)(2,1)S(1)}, u32[]{:S(2)}, u32[]{:S(2)}) collective-permute-start(bf16[256,768]{1,0:T(8,128)(2,1)S(1)} %maximum_select_fusion.11), channel_id=1, source_target_pairs={{0,2},{1,3},{2,0},{3,1},{4,6},{5,7},{6,4},{7,5},{8,10},{9,11},{10,... | collective-permute-start | bytes 1179656 | tf_op jit(solution)/shard_map/ppermute | solution.py:25
  451.5 8.9 %collective-permute-start.40 = (bf16[320,768]{1,0:T(8,128)(2,1)S(1)}, bf16[320,768]{1,0:T(8,128)(2,1)S(1)}, u32[]{:S(2)}, u32[]{:S(2)}) collective-permute-start(bf16[320,768]{1,0:T(8,128)(2,1)S(1)} %maximum_select_fusion.6), channel_id=1, source_target_pairs={{0,16},{16,0},{1,17},{17,1},{2,18},{18,2},{3,19},{19,3},{4,20},{20... | collective-permute-start | bytes 1474568 | tf_op jit(solution)/shard_map/ppermute | solution.py:25
  453.5 13.8 %collective-permute-start.57 = (bf16[512,768]{1,0:T(8,128)(2,1)S(1)}, bf16[512,768]{1,0:T(8,128)(2,1)}, u32[]{:S(2)}, u32[]{:S(2)}) collective-permute-start(bf16[512,768]{1,0:T(8,128)(2,1)S(1)} %maximum_select_fusion.5), channel_id=1, source_target_pairs={{0,1},{1,0},{2,3},{3,2},{4,5},{5,4},{6,7},{7,6},{8,9},{9,8},{10,11... | collective-permute-start | bytes 2359304 | tf_op jit(solution)/shard_map/ppermute | solution.py:25
  453.9 17.5 %collective-permute-start.49 = (bf16[512,768]{1,0:T(8,128)(2,1)S(1)}, bf16[512,768]{1,0:T(8,128)(2,1)}, u32[]{:S(2)}, u32[]{:S(2)}) collective-permute-start(bf16[512,768]{1,0:T(8,128)(2,1)S(1)} %maximum_select_fusion.4), channel_id=1, source_target_pairs={{0,1},{1,0},{2,3},{3,2},{4,5},{5,4},{6,7},{7,6},{8,9},{9,8},{10,11... | collective-permute-start | bytes 2359304 | tf_op jit(solution)/shard_map/ppermute | solution.py:25
  460.8 17.0 %collective-permute-start.41 = (bf16[640,768]{1,0:T(8,128)(2,1)S(1)}, bf16[640,768]{1,0:T(8,128)(2,1)}, u32[]{:S(2)}, u32[]{:S(2)}) collective-permute-start(bf16[640,768]{1,0:T(8,128)(2,1)S(1)} %maximum_select_fusion.3), channel_id=1, source_target_pairs={{0,1},{1,0},{2,3},{3,2},{4,5},{5,4},{6,7},{7,6},{8,9},{9,8},{10,11... | collective-permute-start | bytes 2949128 | tf_op jit(solution)/shard_map/ppermute | solution.py:25
  (136 other events, 769.3 us)
Sparse Core Ops, SparseCore 0:
  355.8 219.4 all-reduce.7

commit v5 on v4

--- a/solution.py
+++ b/solution.py
@@ -18,6 +18,7 @@
 GROUP = 256
 SUB = 128
 TAPS = 33
+FFN_BLOCK = 256
 
 
 def swap(array, axis, bit):
@@ -396,6 +397,65 @@
             own = gm_ref[pl.ds(pl.multiple_of(start + radius, 16), SUB), cols]
             product = dot_nt(spread(own), v_ref[pl.ds(start, GROUP), cols])
             prod_ref[tall, :] += product * same
+
+
+def ffn_kernel(
+    x_ref, mixed_ref, cot_ref, w_out_ref, w_up_ref, w_down_ref, rows_ref, bias_up_ref,
+    result_ref, grad_one_ref, active_ref, grad_up_ref, low_ref, low_two_ref, low_one_ref,
+    grad_mixed_ref, sums_ref, sum_up_ref, slope_s,
+):
+    width = x_ref.shape[1]
+    hidden = w_up_ref.shape[1]
+    chunks = [slice(at, at + width) for at in range(0, hidden, width)]
+
+    def row(i):
+        return rows_ref[i : i + 1, :]
+
+    @pl.when(pl.program_id(0) == 0)
+    def _():
+        sums_ref[...] = jnp.zeros(sums_ref.shape, F32)
+        sum_up_ref[...] = jnp.zeros(sum_up_ref.shape, F32)
+
+    def add_sum(i, cells):
+        sums_ref[i : i + 1, :] += jnp.sum(cells, axis=0, keepdims=True)
+
+    attended = dot_nn(mixed_ref[...], w_out_ref[...]) + row(0)
+    norm_one, inverse_one = normalize(x_ref[...].astype(F32) + attended)
+    hidden_one = norm_one * row(1) + row(2)
+    hidden_low = hidden_one.astype(BF)
+    low_ref[...] = hidden_low
+    lowered = hidden_one + row(3)
+    for cols in chunks:
+        upper = dot_nn(hidden_low, w_up_ref[:, cols]) + bias_up_ref[:1, cols]
+        active, slope = gelu_both(upper)
+        active = active.astype(BF)
+        active_ref[:, cols] = active
+        slope_s[:, cols] = slope.astype(BF)
+        lowered = lowered + dot_nn(active, w_down_ref[cols, :])
+    norm_two, inverse_two = normalize(lowered)
+    result_ref[...] = norm_two * row(4) + row(5)
+    upstream = cot_ref[...].astype(F32)
+    add_sum(0, upstream * norm_two)
+    add_sum(1, upstream)
+    grad_two = norm_back(upstream * row(4), norm_two, inverse_two)
+    low_two = grad_two.astype(BF)
+    low_two_ref[...] = low_two
+    add_sum(2, low_two.astype(F32))
+    grad_hidden = grad_two
+    for cols in chunks:
+        grad_up = dot_nt(low_two, w_down_ref[cols, :]) * slope_s[:, cols].astype(F32)
+        grad_up = grad_up.astype(BF)
+        grad_up_ref[:, cols] = grad_up
+        sum_up_ref[:1, cols] += jnp.sum(grad_up.astype(F32), axis=0, keepdims=True)
+        grad_hidden = grad_hidden + dot_nt(grad_up, w_up_ref[:, cols])
+    add_sum(3, grad_hidden * norm_one)
+    add_sum(4, grad_hidden)
+    grad_one = norm_back(grad_hidden * row(1), norm_one, inverse_one)
+    grad_one_ref[...] = grad_one
+    low_one = grad_one.astype(BF)
+    low_one_ref[...] = low_one
+    add_sum(5, low_one.astype(F32))
+    grad_mixed_ref[...] = dot_nt(low_one, w_out_ref[...]).astype(BF)
 
 
 def landmark_back_kernel(
@@ -607,42 +667,41 @@
         name="token",
     )(bounds, qkv, value_ext, mark_k, mix, taps)
 
-    attended = jnp.dot(mixed, w_out, preferred_element_type=F32) + bias_out
-    norm_one, inverse_one = normalize(tokens.astype(F32) + attended)
-    hidden_one = norm_one * norm1_gain + norm1_bias
-    hidden_low = hidden_one.astype(BF)
-    upper = jnp.dot(hidden_low, w_up, preferred_element_type=F32) + bias_up
-    active, slope = gelu_both(upper)
-    active = active.astype(BF)
-    lowered = jnp.dot(active, w_down, preferred_element_type=F32) + bias_down
-    norm_two, inverse_two = normalize(hidden_one + lowered)
-    result = norm_two * norm2_gain + norm2_bias
-    upstream = cotangent[0].astype(F32)
-    grad_gain_two = jnp.sum(upstream * norm_two, axis=0)
-    grad_shift_two = jnp.sum(upstream, axis=0)
-    grad_two = norm_back(upstream * norm2_gain, norm_two, inverse_two)
-    grad_low_two = grad_two.astype(BF)
-    grad_bias_down = jnp.sum(grad_low_two.astype(F32), axis=0)
-    grad_w_down = lax.dot_general(active, grad_low_two, rows_in, preferred_element_type=F32)
-    grad_active = lax.dot_general(grad_low_two, w_down, cols_in, preferred_element_type=F32)
-    grad_upper = (grad_active * slope).astype(BF)
-    grad_bias_up = jnp.sum(grad_upper.astype(F32), axis=0)
-    grad_w_up = lax.dot_general(hidden_low, grad_upper, rows_in, preferred_element_type=F32)
-    sum_w_down, sum_w_up = lax.psum(
-        (grad_w_down.astype(BF), grad_w_up.astype(BF)), ("row", "seq")
-    )
-    grad_hidden = grad_two + lax.dot_general(
-        grad_upper, w_up, cols_in, preferred_element_type=F32
-    )
-    grad_gain_one = jnp.sum(grad_hidden * norm_one, axis=0)
-    grad_shift_one = jnp.sum(grad_hidden, axis=0)
-    grad_one = norm_back(grad_hidden * norm1_gain, norm_one, inverse_one)
-    grad_low_one = grad_one.astype(BF)
-    grad_bias_out = jnp.sum(grad_low_one.astype(F32), axis=0)
-    grad_w_out = lax.dot_general(mixed, grad_low_one, rows_in, preferred_element_type=F32)
-    grad_mixed = lax.dot_general(
-        grad_low_one, w_out, cols_in, preferred_element_type=F32
-    ).astype(BF)
+    hidden = w_up.shape[1]
+    vectors = jnp.stack([bias_out, norm1_gain, norm1_bias, bias_down, norm2_gain, norm2_bias])
+    vectors = jnp.pad(vectors, ((0, 2), (0, 0)))
+    wide_spec = pl.BlockSpec((FFN_BLOCK, hidden), lambda i: (i, 0))
+    ffn_spec = pl.BlockSpec((FFN_BLOCK, width), lambda i: (i, 0))
+    narrow = shaped((tok_count, width), BF)
+    (
+        result, grad_one, active, grad_upper, hidden_low, grad_low_two, grad_low_one,
+        grad_mixed, sums, sum_up,
+    ) = pl.pallas_call(
+        ffn_kernel,
+        grid=(tok_count // FFN_BLOCK,),
+        in_specs=[
+            ffn_spec, ffn_spec, ffn_spec, fixed(width, width), fixed(width, hidden),
+            fixed(hidden, width), fixed(8, width), fixed(8, hidden),
+        ],
+        out_specs=(
+            ffn_spec, ffn_spec, wide_spec, wide_spec, ffn_spec, ffn_spec, ffn_spec, ffn_spec,
+            fixed(8, width), fixed(8, hidden),
+        ),
+        out_shape=(
+            shaped((tok_count, width), F32), shaped((tok_count, width), F32),
+            shaped((tok_count, hidden), BF), shaped((tok_count, hidden), BF),
+            narrow, narrow, narrow, narrow, shaped((8, width), F32), shaped((8, hidden), F32),
+        ),
+        scratch_shapes=[pltpu.VMEM((FFN_BLOCK, hidden), BF)],
+        compiler_params=pltpu.CompilerParams(vmem_limit_bytes=58 * 1024 * 1024),
+        name="ffn",
+    )(
+        tokens, mixed, cotangent[0], w_out, w_up, w_down, vectors,
+        jnp.broadcast_to(bias_up[None, :], (8, hidden)),
+    )
+    grad_gain_two, grad_shift_two, grad_bias_down = sums[0], sums[1], sums[2]
+    grad_gain_one, grad_shift_one, grad_bias_out = sums[3], sums[4], sums[5]
+    grad_bias_up = sum_up[0]
 
     grad_queries, grad_mix, grad_mk = pl.pallas_call(
         lambda *refs: token_back_kernel(docs, scale, *refs),
@@ -660,7 +719,15 @@
         compiler_params=params,
         name="token_back",
     )(bounds, qkv, grad_mixed, probs, mark_k, mix)
+    grad_w_down = lax.dot_general(active, grad_low_two, rows_in, preferred_element_type=F32)
+    grad_w_up = lax.dot_general(hidden_low, grad_upper, rows_in, preferred_element_type=F32)
+    grad_w_down, grad_w_up = grad_w_down.astype(BF), grad_w_up.astype(BF)
     grad_mix = seq_quarter(grad_mix.astype(BF), add_join)
+    grad_mix, grad_w_down, grad_w_up = lax.optimization_barrier(
+        (grad_mix, grad_w_down, grad_w_up)
+    )
+    sum_w_down, sum_w_up = lax.psum((grad_w_down, grad_w_up), ("row", "seq"))
+    grad_w_out = lax.dot_general(mixed, grad_low_one, rows_in, preferred_element_type=F32)
 
     grad_ext = extended(grad_mixed, radius, window_rows)
     grad_conv, products = pl.pallas_call(

time: 604 us -> 593 us (0.982)
  matrix products: 123 us -> 65.4 us
  Pallas kernels: 48.4 us -> 103 us
  waiting for transfers between devices: 168 us -> 185 us
  starting transfers between devices: 94.4 us -> 80.2 us
  other arithmetic: 65.2 us -> 57.5 us
    dot_general x6 -> x0, matrix products: 51.1 us -> none  [the longest x1 16.9 us: per_device(): lax.dot_general(grad_low_two, w_down, cols_in, preferred_element_type=F32)]
    pallas_call x0 -> x1, Pallas kernels: none -> 40.3 us  [per_device(): pl.pallas_call(ffn_kernel, grid=(tok_count // FFN_BLOCK,), in_specs=[ffn_...]
    ppermute x54, waiting for transfers between devices: 78.7 us -> 111 us  [swap(): return lax.ppermute(array, axis, [(i, i ^ bit) for i in range(count)])]
    psum x1, waiting for transfers between devices: 89.1 us -> 74.6 us  [per_device(): sum_w_down, sum_w_up = lax.psum((grad_w_down, grad_w_up), ('row', 'seq'))]
    ppermute x54, starting transfers between devices: 87.7 us -> 73.6 us  [swap(): return lax.ppermute(array, axis, [(i, i ^ bit) for i in range(count)])]
    pallas_call x1, Pallas kernels: 9.5 us -> 23.3 us  [per_device(): pl.pallas_call(lambda *refs: landmark_kernel(docs, scale, *refs), grid=(1...]
    unnamed x284 -> x292, local copies, waits for them, and re-layouts: 37.7 us -> 24.1 us
    reduce_sum x6 -> x0, other arithmetic: 8.64 us -> none  [the longest x1 3.4 us: per_device(): grad_gain_two = jnp.sum(upstream * norm_two, axis=0)]
  transfers between devices with their start and end apart: 59 -> 59, of which waited for: 27 -> 33; matrix products, arithmetic and copies ran while one was open for 18% -> 19% of each run, Pallas kernels for 1% -> 2%
where the time goes in v5:
time: 593 us; the launch traced here: 582 us
  waiting for transfers between devices  185 us (31%)
  Pallas kernels  103 us (17%)
  starting transfers between devices  80.2 us (14%)
  local copies, waits for them, and re-layouts  73.6 us (12%)
  matrix products  65.4 us (11%)
  other arithmetic  57.5 us (10%)
  between operations  17.4 us (3%)
    ppermute x54, waiting for transfers between devices, swap(): return lax.ppermute(array, axis, [(i, i ^ bit) for i in range(count)])  111 us
    psum x1, waiting for transfers between devices, per_device(): sum_w_down, sum_w_up = lax.psum((grad_w_down, grad_w_up), ('row', 'seq'))  74.6 us
    ppermute x54, starting transfers between devices, swap(): return lax.ppermute(array, axis, [(i, i ^ bit) for i in range(count)])  73.6 us
    pallas_call x1, Pallas kernels, per_device(): pl.pallas_call(ffn_kernel, grid=(tok_count // FFN_BLOCK,), in_specs=[ffn_...  40.3 us
    unnamed x292, local copies, waits for them, and re-layouts  24.1 us
    pallas_call x1, Pallas kernels, per_device(): pl.pallas_call(lambda *refs: landmark_kernel(docs, scale, *refs), grid=(1...  23.3 us
    convert_element_type x2, other arithmetic, per_device(): sum_w_down, sum_w_up = (sum_w_down.astype(F32), sum_w_up.astype(F32))  12 us
  transfers between devices with their start and end apart: 59, of which 33 were waited for; matrix products, arithmetic and copies ran while one was open for 19% of the time, Pallas kernels for 2%

profile of v5, /device:TPU:0, one launch (start us, length us, event | category | flops | bytes accessed | tf_op | source)
XLA Modules:
  0.0 582.2 jit_solution(18186845927341917580)
XLA Ops:
  10.9 2.2 fusion.8
  13.9 5.4 add_convert_fusion.refs_2_.refs_3_.refs_1_
  19.4 3.0 collective-permute-start.3
  26.2 5.3 collective-permute-start.4
  34.1 3.8 collective-permute-start.5
  37.8 3.6 collective-permute-done.5
  43.1 3.1 collective-permute-done.6
  58.8 2.3 copy-done
  61.2 23.3 %landmark.1 = bf16[256,896]{1,0:T(8,128)(2,1)S(1)} custom-call(s32[8]{0:T(128)S(1)} %add_subtract_fusion.refs_0_, bf16[256,768]{1,0:T(8,128)(2,1)S(1)} %fusion.36.refs_1_.refs_4_, bf16[1024,2304]{1,0:T(8,128)(2,1)S(1)} %copy-done, bf16[1024,2304]{1,0:T(8,128)(2,1)S(1)} %copy-done), custom_call_target="tpu_custom_call" | custom-call | tf_op jit(solution)/shard_map/landmark/pallas_call | solution.py:604
  87.6 2.6 join.4
  93.7 3.4 collective-permute-done.9.b_ref
  102.3 3.9 collective-permute-done.10
  106.8 2.2 join.6.a_ref
  110.0 8.8 %collective-permute-start.11 = (bf16[64,1280]{1,0:T(8,128)(2,1)S(1)}, bf16[64,1280]{1,0:T(8,128)(2,1)S(1)}, u32[]{:S(2)}, u32[]{:S(2)}) collective-permute-start(bf16[64,1280]{1,0:T(8,128)(2,1)S(1)} %pad_maximum_fusion.4), channel_id=1, source_target_pairs={{0,8},{1,9},{2,10},{3,11},{4,12},{5,13},{6,14},{7,15},{8,0},{9,1},... | collective-permute-start | bytes 491528 | tf_op jit(solution)/shard_map/ppermute | solution.py:26
  119.4 6.5 %collective-permute-done.11 = bf16[64,1280]{1,0:T(8,128)(2,1)S(1)} collective-permute-done((bf16[64,1280]{1,0:T(8,128)(2,1)S(1)}, bf16[64,1280]{1,0:T(8,128)(2,1)S(1)}, u32[]{:S(2)}, u32[]{:S(2)}) %collective-permute-start.11) | collective-permute-done | bytes 163872 | tf_op jit(solution)/shard_map/ppermute | solution.py:26
  133.7 2.5 collective-permute-done.12
  139.8 2.3 copy-done.1
  142.1 7.7 %token_.1 = (bf16[1024,768]{1,0:T(8,128)(2,1)S(1)}, bf16[768,1024]{1,0:T(8,128)(2,1)S(1)}) custom-call(s32[8]{0:T(128)S(1)} %add_subtract_fusion.refs_0_, bf16[1024,2304]{1,0:T(8,128)(2,1)S(1)} %copy-done.1, bf16[1152,768]{1,0:T(8,128)(2,1)S(1)} %maximum_maximum_fusion.refs_2_, bf16[256,768]{1,0:T(8,128)(2,1)S(1)} %slice.264.refs_3_.refs_4_, ...), custom_call_target="tpu_custom_call" | custom-call | tf_op jit(solution)/shard_map/token/pallas_call | solution.py:657
  152.9 40.3 %ffn.1 = (f32[1024,768]{1,0:T(8,128)}, f32[1024,768]{1,0:T(8,128)}, bf16[1024,3072]{1,0:T(8,128)(2,1)}, bf16[1024,3072]{1,0:T(8,128)(2,1)}, bf16[1024,768]{1,0:T...) custom-call(bf16[1024,768]{1,0:T(8,128)(2,1)} %bitcast.201, ...), custom_call_target="tpu_custom_call" | custom-call | tf_op jit(solution)/shard_map/ffn/pallas_call | solution.py:679
  193.2 4.5 convolution_convert_fusion.2
  198.3 2.4 collective-permute-start.14
  202.1 6.4 %token_back.1 = (bf16[1024,768]{1,0:T(8,128)(2,1)S(1)}, f32[256,768]{1,0:T(8,128)S(1)}, f32[256,768]{1,0:T(8,128)S(1)}) custom-call(s32[8]{0:T(128)S(1)} %add_subtract_fusion.refs_0_, bf16[1024,2304]{1,0:T(8,128)(2,1)S(1)} %bitcast.198, bf16[1024,768]{1,0:T(8,128)(2,1)S(1)} %copy-done.7, bf16[768,1024]{1,0:T(8,128)(2,1)S(1)} %copy-done.20, ...), custom_call_target="tpu_custom_call" | custom-call | tf_op jit(solution)/shard_map/token_back/pallas_call | solution.py:706
  212.1 7.0 %convolution_convert_fusion.1 = bf16[3072,768]{1,0:T(8,128)(2,1)} fusion(bf16[1024,3072]{1,0:T(8,128)(2,1)S(1)} %bitcast.219, bf16[1024,768]{1,0:T(8,128)(2,1)S(1)} %copy-done.133), kind=kOutput, calls=%fused_computation.5 | convolution fusion | flops 4834197504 | bytes 12582912 | tf_op jit(solution)/shard_map/dot_general | solution.py:722
  219.1 6.8 %convolution_convert_fusion = bf16[768,3072]{1,0:T(8,128)(2,1)} fusion(bf16[1024,768]{1,0:T(8,128)(2,1)S(1)} %copy-done.132, bf16[1024,3072]{1,0:T(8,128)(2,1)S(1)} %bitcast.217), kind=kOutput, calls=%fused_computation.4 | convolution fusion | flops 4834197504 | bytes 12582912 | tf_op jit(solution)/shard_map/dot_general | solution.py:723
  231.5 2.4 collective-permute-done.17
  234.0 2.3 collective-permute-start.18
  238.9 7.7 %collective-permute-start.19 = (bf16[64,768]{1,0:T(8,128)(2,1)S(1)}, bf16[64,768]{1,0:T(8,128)(2,1)}, u32[]{:S(2)}, u32[]{:S(2)}) collective-permute-start(bf16[64,768]{1,0:T(8,128)(2,1)S(1)} %add_convert_fusion.20), channel_id=1, source_target_pairs={{0,8},{1,9},{2,10},{3,11},{4,12},{5,13},{6,14},{7,15},{8,0},{9,1},... | collective-permute-start | bytes 294920 | tf_op jit(solution)/shard_map/ppermute | solution.py:26
  247.0 5.3 conv_back.1
  254.0 2.3 reshape.182
  256.3 2.5 pad.28
  258.7 3.2 reshape.183
  287.4 3.0 collective-permute-done.20
  293.9 2.3 copy-done.2
  298.1 6.8 %landmark_back.1 = (bf16[1024,768]{1,0:T(8,128)(2,1)S(1)}, bf16[1024,768]{1,0:T(8,128)(2,1)S(1)}, f32[256,768]{1,0:T(8,128)S(1)}) custom-call(s32[8]{0:T(128)S(1)} %add_subtract_fusion.refs_0_, bf16[1024,2304]{1,0:T(8,128)(2,1)S(1)} %copy-done.2, bf16[1024,2304]{1,0:T(8,128)(2,1)S(1)} %copy-done.2, f32[1024,768]{1,0:T(8,128)S(1)} %copy-done.15, ...), custom_call_target="tpu_custom_call" | custom-call | tf_op jit(solution)/shard_map/landmark_back/pallas_call | solution.py:760
  307.9 2.7 fusion.27
  316.0 4.6 fusion
  321.5 5.4 concatenate.220
  338.2 2.5 collective-permute-start.24
  344.0 2.2 collective-permute-start.25
  346.3 5.4 collective-permute-done.25
  356.5 2.5 add_convert_fusion.1
  361.3 5.4 collective-permute-done.29
  368.5 12.8 %collective-permute-done.33 = bf16[256,768]{1,0:T(8,128)(2,1)S(1)} collective-permute-done((bf16[256,768]{1,0:T(8,128)(2,1)S(1)}, bf16[256,768]{1,0:T(8,128)(2,1)S(1)}, u32[]{:S(2)}, u32[]{:S(2)}) %collective-permute-start.33) | collective-permute-done | bytes 393248 | tf_op jit(solution)/shard_map/ppermute | solution.py:26
  383.1 3.4 collective-permute-done.31
  389.0 3.6 collective-permute-done.50
  392.6 2.7 collective-permute-start.51
  395.5 7.7 %collective-permute-done.34 = bf16[160,768]{1,0:T(8,128)(2,1)S(1)} collective-permute-done((bf16[160,768]{1,0:T(8,128)(2,1)S(1)}, bf16[160,768]{1,0:T(8,128)(2,1)S(1)}, u32[]{:S(2)}, u32[]{:S(2)}) %collective-permute-start.34) | collective-permute-done | bytes 245792 | tf_op jit(solution)/shard_map/ppermute | solution.py:26
  408.3 5.1 collective-permute-done.52
  413.6 2.2 collective-permute-done.44
  416.6 2.3 collective-permute-start.36
  425.9 2.5 collective-permute-done.37
  430.8 4.7 collective-permute-done.55
  435.6 2.9 collective-permute-done.38
  439.4 11.3 %collective-permute-done.39 = bf16[160,768]{1,0:T(8,128)(2,1)S(1)} collective-permute-done((bf16[160,768]{1,0:T(8,128)(2,1)S(1)}, bf16[160,768]{1,0:T(8,128)(2,1)S(1)}, u32[]{:S(2)}, u32[]{:S(2)}) %collective-permute-start.39) | collective-permute-done | bytes 245792 | tf_op jit(solution)/shard_map/ppermute | solution.py:26
  454.8 4.1 fusion.117
  458.9 2.5 collective-permute-done.40
  462.7 2.6 add_bitcast_fusion
  466.8 2.4 reshape.185
  471.2 2.3 fusion.6
  478.8 2.5 fusion.5
  484.8 3.7 pad_maximum_fusion
  488.5 74.6 %all-reduce.9.cloned.1.call-done = (bf16[768,3072]{1,0:T(8,128)(2,1)}, bf16[3072,768]{1,0:T(8,128)(2,1)}) async-done(((bf16[768,3072]{1,0:T(8,128)(2,1)}, bf16[3072,768]{1,0:T(8,128)(2,1)}), (bf16[768,3072]{1,0:T(8,128)(2,1)}, bf16[3072,768]{1,0:T(8,128)(2,1)})) %all-reduce.9.cloned.1.call-update) | async-done | bytes 9437200 | tf_op jit(solution)/shard_map/psum | solution.py:729
  563.1 7.5 %convert_element_type.437 = f32[768,3072]{1,0:T(8,128)} convert(bf16[768,3072]{1,0:T(8,128)(2,1)} %get-tuple-element.92) | non-fusion elementwise | flops 2359296 | bytes 14155776 | tf_op jit(solution)/shard_map/convert_element_type | solution.py:829
  570.7 4.5 convert_element_type.438
  (637 shorter events, 169.0 us)
Async XLA Ops:
  7.2 556.0 %all-reduce.9.cloned.1.call-start = ((), (), s32[]{:S(2)}) async-start(), calls=%async_computation | async-start | bytes 18874368 | tf_op jit(solution)/shard_map/psum | solution.py:729
  13.2 6.1 %collective-permute-start.2 = (bf16[128,768]{1,0:T(8,128)(2,1)S(1)}, bf16[128,768]{1,0:T(8,128)(2,1)S(1)}, u32[]{:S(2)}, u32[]{:S(2)}) collective-permute-start(bf16[128,768]{1,0:T(8,128)(2,1)S(1)} %constant_dynamic-slice_fusion.23), channel_id=1, source_target_pairs={{0,1},{1,0},{2,3},{3,2},{4,5},{5,4},{6,7},{7,6},{8,9},{9,8},{10,11... | collective-permute-start | bytes 589832 | tf_op jit(solution)/shard_map/ppermute | solution.py:26
  19.4 6.8 %collective-permute-start.3 = (bf16[64,768]{1,0:T(8,128)(2,1)S(1)}, bf16[64,768]{1,0:T(8,128)(2,1)S(1)}, u32[]{:S(2)}, u32[]{:S(2)}) collective-permute-start(bf16[64,768]{1,0:T(8,128)(2,1)S(1)} %constant_dynamic-slice_fusion.22), channel_id=1, source_target_pairs={{0,2},{1,3},{2,0},{3,1},{4,6},{5,7},{6,4},{7,5},{8,10},{9,11},{10,... | collective-permute-start | bytes 294920 | tf_op jit(solution)/shard_map/ppermute | solution.py:26
  23.2 23.2 %collective-permute-start = (bf16[16,768]{1,0:T(8,128)(2,1)S(1)}, bf16[16,768]{1,0:T(8,128)(2,1)S(1)}, u32[]{:S(2)}, u32[]{:S(2)}) collective-permute-start(bf16[16,768]{1,0:T(8,128)(2,1)S(1)} %get-tuple-element.100), channel_id=1, source_target_pairs={{0,1},{1,2},{2,3},{3,4},{4,5},{5,6},{6,7},{7,8},{8,9},{9,10},{10,1... | collective-permute-start | bytes 73736 | tf_op jit(solution)/shard_map/ppermute | solution.py:110
  24.7 21.6 %collective-permute-start.1 = (bf16[16,768]{1,0:T(8,128)(2,1)S(1)}, bf16[16,768]{1,0:T(8,128)(2,1)}, u32[]{:S(2)}, u32[]{:S(2)}) collective-permute-start(bf16[16,768]{1,0:T(8,128)(2,1)S(1)} %get-tuple-element.101), channel_id=1, source_target_pairs={{1,0},{2,1},{3,2},{4,3},{5,4},{6,5},{7,6},{8,7},{9,8},{10,9},{11,1... | collective-permute-start | bytes 73736 | tf_op jit(solution)/shard_map/ppermute | solution.py:112
  26.2 7.9 %collective-permute-start.4 = (bf16[64,768]{1,0:T(8,128)(2,1)S(1)}, bf16[64,768]{1,0:T(8,128)(2,1)S(1)}, u32[]{:S(2)}, u32[]{:S(2)}) collective-permute-start(bf16[64,768]{1,0:T(8,128)(2,1)S(1)} %add_convert_fusion.24), channel_id=1, source_target_pairs={{0,4},{1,5},{2,6},{3,7},{4,0},{5,1},{6,2},{7,3},{8,12},{9,13},{10,... | collective-permute-start | bytes 294920 | tf_op jit(solution)/shard_map/ppermute | solution.py:26
  34.1 7.4 %collective-permute-start.5 = (bf16[64,768]{1,0:T(8,128)(2,1)S(1)}, bf16[64,768]{1,0:T(8,128)(2,1)S(1)}, u32[]{:S(2)}, u32[]{:S(2)}) collective-permute-start(bf16[64,768]{1,0:T(8,128)(2,1)S(1)} %add_convert_fusion.23), channel_id=1, source_target_pairs={{0,8},{1,9},{2,10},{3,11},{4,12},{5,13},{6,14},{7,15},{8,0},{9,1},... | collective-permute-start | bytes 294920 | tf_op jit(solution)/shard_map/ppermute | solution.py:26
  41.5 4.7 collective-permute-start.6
  46.3 1.5 collective-permute-start.7
  47.5 92.3 %copy-start.3 = (bf16[1152,768]{1,0:T(8,128)(2,1)}, bf16[1152,768]{1,0:T(8,128)(2,1)S(1)}, u32[]{:S(2)}) copy-start(bf16[1152,768]{1,0:T(8,128)(2,1)S(1)} %maximum_maximum_fusion.refs_2_) | copy-start | bytes 5308420
  48.8 91.0 %copy-start.10 = (bf16[256,768]{1,0:T(8,128)(2,1)}, bf16[256,768]{1,0:T(8,128)(2,1)S(1)}, u32[]{:S(2)}) copy-start(bf16[256,768]{1,0:T(8,128)(2,1)S(1)} %slice.264.refs_3_.refs_4_) | copy-start | bytes 1179652
  85.3 1.6 collective-permute-start.8
  91.8 5.3 collective-permute-start.9
  100.9 5.3 collective-permute-start.10
  110.0 15.9 %collective-permute-start.11 = (bf16[64,1280]{1,0:T(8,128)(2,1)S(1)}, bf16[64,1280]{1,0:T(8,128)(2,1)S(1)}, u32[]{:S(2)}, u32[]{:S(2)}) collective-permute-start(bf16[64,1280]{1,0:T(8,128)(2,1)S(1)} %pad_maximum_fusion.4), channel_id=1, source_target_pairs={{0,8},{1,9},{2,10},{3,11},{4,12},{5,13},{6,14},{7,15},{8,0},{9,1},... | collective-permute-start | bytes 491528 | tf_op jit(solution)/shard_map/ppermute | solution.py:26
  131.2 5.0 collective-permute-start.12
  137.2 2.5 collective-permute-start.13
  152.8 49.1 %slice-start = ((s8[4718592]{0:T(1024)(128)(4,1)}), s8[4194304]{0:T(1024)(128)(4,1)S(1)}, s32[]{:S(2)}) async-start(s8[4718592]{0:T(1024)(128)(4,1)} %bitcast.197), calls=%async_computation.1 | async-start | bytes 8388608
  152.8 49.1 %slice-start.1 = ((s8[4718592]{0:T(1024)(128)(4,1)}), s8[524288]{0:T(1024)(128)(4,1)S(1)}, s32[]{:S(2)}) async-start(s8[4718592]{0:T(1024)(128)(4,1)} %bitcast.197), calls=%async_computation.2 | async-start | bytes 1048576
  198.3 48.3 %collective-permute-start.14 = (bf16[16,768]{1,0:T(8,128)(2,1)}, bf16[16,768]{1,0:T(8,128)(2,1)S(1)}, u32[]{:S(2)}, u32[]{:S(2)}) collective-permute-start(bf16[16,768]{1,0:T(8,128)(2,1)} %get-tuple-element.106), channel_id=1, source_target_pairs={{0,1},{1,2},{2,3},{3,4},{4,5},{5,6},{6,7},{7,8},{8,9},{9,10},{10,1... | collective-permute-start | bytes 73736 | tf_op jit(solution)/shard_map/ppermute | solution.py:110
  200.7 45.9 %collective-permute-start.15 = (bf16[16,768]{1,0:T(8,128)(2,1)}, bf16[16,768]{1,0:T(8,128)(2,1)S(1)}, u32[]{:S(2)}, u32[]{:S(2)}) collective-permute-start(bf16[16,768]{1,0:T(8,128)(2,1)} %get-tuple-element.107), channel_id=1, source_target_pairs={{1,0},{2,1},{3,2},{4,3},{5,4},{6,5},{7,6},{8,7},{9,8},{10,9},{11,1... | collective-permute-start | bytes 73736 | tf_op jit(solution)/shard_map/ppermute | solution.py:112
  209.3 18.4 %collective-permute-start.16 = (bf16[128,768]{1,0:T(8,128)(2,1)}, bf16[128,768]{1,0:T(8,128)(2,1)}, u32[]{:S(2)}, u32[]{:S(2)}) collective-permute-start(bf16[128,768]{1,0:T(8,128)(2,1)} %constant_dynamic-slice_fusion.17), channel_id=1, source_target_pairs={{0,1},{1,0},{2,3},{3,2},{4,5},{5,4},{6,7},{7,6},{8,9},{9,8},{10,11... | collective-permute-start | bytes 589832 | tf_op jit(solution)/shard_map/ppermute | solution.py:26
  228.7 5.2 collective-permute-start.17
  234.0 4.9 collective-permute-start.18
  238.9 23.9 %collective-permute-start.19 = (bf16[64,768]{1,0:T(8,128)(2,1)S(1)}, bf16[64,768]{1,0:T(8,128)(2,1)}, u32[]{:S(2)}, u32[]{:S(2)}) collective-permute-start(bf16[64,768]{1,0:T(8,128)(2,1)S(1)} %add_convert_fusion.20), channel_id=1, source_target_pairs={{0,8},{1,9},{2,10},{3,11},{4,12},{5,13},{6,14},{7,15},{8,0},{9,1},... | collective-permute-start | bytes 294920 | tf_op jit(solution)/shard_map/ppermute | solution.py:26
  285.5 4.9 collective-permute-start.20
  290.4 3.3 collective-permute-start.21
  311.4 21.0 %collective-permute-start.22 = (bf16[128,768]{1,0:T(8,128)(2,1)}, bf16[128,768]{1,0:T(8,128)(2,1)}, u32[]{:S(2)}, u32[]{:S(2)}) collective-permute-start(bf16[128,768]{1,0:T(8,128)(2,1)} %constant_dynamic-slice_fusion.13), channel_id=1, source_target_pairs={{0,1},{1,0},{2,3},{3,2},{4,5},{5,4},{6,7},{7,6},{8,9},{9,8},{10,11... | collective-permute-start | bytes 589832 | tf_op jit(solution)/shard_map/ppermute | solution.py:26
  331.8 20.8 %collective-permute-start.27 = (bf16[512,768]{1,0:T(8,128)(2,1)}, bf16[512,768]{1,0:T(8,128)(2,1)}, u32[]{:S(2)}, u32[]{:S(2)}) collective-permute-start(bf16[512,768]{1,0:T(8,128)(2,1)} %fusion.34), channel_id=1, source_target_pairs={{0,1},{1,0},{2,3},{3,2},{4,5},{5,4},{6,7},{7,6},{8,9},{9,8},{10,11... | collective-permute-start | bytes 2359304 | tf_op jit(solution)/shard_map/ppermute | solution.py:26
  333.3 4.9 collective-permute-start.23
  336.2 18.2 %collective-permute-start.28 = (bf16[512,768]{1,0:T(8,128)(2,1)}, bf16[512,768]{1,0:T(8,128)(2,1)}, u32[]{:S(2)}, u32[]{:S(2)}) collective-permute-start(bf16[512,768]{1,0:T(8,128)(2,1)} %fusion.32), channel_id=1, source_target_pairs={{0,1},{1,0},{2,3},{3,2},{4,5},{5,4},{6,7},{7,6},{8,9},{9,8},{10,11... | collective-permute-start | bytes 2359304 | tf_op jit(solution)/shard_map/ppermute | solution.py:26
  338.2 5.1 collective-permute-start.24
  342.9 13.6 %collective-permute-start.26 = (bf16[640,768]{1,0:T(8,128)(2,1)}, bf16[640,768]{1,0:T(8,128)(2,1)}, u32[]{:S(2)}, u32[]{:S(2)}) collective-permute-start(bf16[640,768]{1,0:T(8,128)(2,1)} %fusion.30), channel_id=1, source_target_pairs={{0,1},{1,0},{2,3},{3,2},{4,5},{5,4},{6,7},{7,6},{8,9},{9,8},{10,11... | collective-permute-start | bytes 2949128 | tf_op jit(solution)/shard_map/ppermute | solution.py:26
  344.0 7.6 %collective-permute-start.25 = (bf16[64,768]{1,0:T(8,128)(2,1)}, bf16[64,768]{1,0:T(8,128)(2,1)}, u32[]{:S(2)}, u32[]{:S(2)}) collective-permute-start(bf16[64,768]{1,0:T(8,128)(2,1)} %add_convert_fusion.17), channel_id=1, source_target_pairs={{0,8},{1,9},{2,10},{3,11},{4,12},{5,13},{6,14},{7,15},{8,0},{9,1},... | collective-permute-start | bytes 294920 | tf_op jit(solution)/shard_map/ppermute | solution.py:26
  359.0 7.7 %collective-permute-start.29 = (bf16[64,768]{1,0:T(8,128)(2,1)S(1)}, bf16[64,768]{1,0:T(8,128)(2,1)S(1)}, u32[]{:S(2)}, u32[]{:S(2)}) collective-permute-start(bf16[64,768]{1,0:T(8,128)(2,1)S(1)} %add_convert_fusion.16), channel_id=1, source_target_pairs={{0,2},{1,3},{2,0},{3,1},{4,6},{5,7},{6,4},{7,5},{8,10},{9,11},{10,... | collective-permute-start | bytes 294920 | tf_op jit(solution)/shard_map/ppermute | solution.py:26
  361.1 20.1 %collective-permute-start.33 = (bf16[256,768]{1,0:T(8,128)(2,1)S(1)}, bf16[256,768]{1,0:T(8,128)(2,1)S(1)}, u32[]{:S(2)}, u32[]{:S(2)}) collective-permute-start(bf16[256,768]{1,0:T(8,128)(2,1)S(1)} %constant_dynamic-slice_fusion.9), channel_id=1, source_target_pairs={{0,4},{1,5},{2,6},{3,7},{4,0},{5,1},{6,2},{7,3},{8,12},{9,13},{10,... | collective-permute-start | bytes 1179656 | tf_op jit(solution)/shard_map/ppermute | solution.py:26
  366.7 1.6 collective-permute-start.30
  366.9 16.1 %collective-permute-start.32 = (bf16[256,768]{1,0:T(8,128)(2,1)S(1)}, bf16[256,768]{1,0:T(8,128)(2,1)S(1)}, u32[]{:S(2)}, u32[]{:S(2)}) collective-permute-start(bf16[256,768]{1,0:T(8,128)(2,1)S(1)} %constant_dynamic-slice_fusion.10), channel_id=1, source_target_pairs={{0,2},{1,3},{2,0},{3,1},{4,6},{5,7},{6,4},{7,5},{8,10},{9,11},{10,... | collective-permute-start | bytes 1179656 | tf_op jit(solution)/shard_map/ppermute | solution.py:26
  368.3 18.2 %collective-permute-start.31 = (bf16[320,768]{1,0:T(8,128)(2,1)S(1)}, bf16[320,768]{1,0:T(8,128)(2,1)S(1)}, u32[]{:S(2)}, u32[]{:S(2)}) collective-permute-start(bf16[320,768]{1,0:T(8,128)(2,1)S(1)} %constant_dynamic-slice_fusion.11), channel_id=1, source_target_pairs={{0,16},{16,0},{1,17},{17,1},{2,18},{18,2},{3,19},{19,3},{4,20},{20... | collective-permute-start | bytes 1474568 | tf_op jit(solution)/shard_map/ppermute | solution.py:26
  382.9 71.8 %slice-start.6 = ((s8[4718592]{0:T(1024)(128)(4,1)}), s8[4194304]{0:T(1024)(128)(4,1)S(1)}, s32[]{:S(2)}) async-start(s8[4718592]{0:T(1024)(128)(4,1)} %bitcast.204), calls=%async_computation.7 | async-start | bytes 8388608
  386.7 5.9 %collective-permute-start.50 = (bf16[128,768]{1,0:T(8,128)(2,1)S(1)}, bf16[128,768]{1,0:T(8,128)(2,1)S(1)}, u32[]{:S(2)}, u32[]{:S(2)}) collective-permute-start(bf16[128,768]{1,0:T(8,128)(2,1)S(1)} %constant_dynamic-slice_fusion.2), channel_id=1, source_target_pairs={{0,2},{1,3},{2,0},{3,1},{4,6},{5,7},{6,4},{7,5},{8,10},{9,11},{10,... | collective-permute-start | bytes 589832 | tf_op jit(solution)/shard_map/ppermute | solution.py:26
  386.8 8.5 %collective-permute-start.42 = (bf16[128,768]{1,0:T(8,128)(2,1)S(1)}, bf16[128,768]{1,0:T(8,128)(2,1)S(1)}, u32[]{:S(2)}, u32[]{:S(2)}) collective-permute-start(bf16[128,768]{1,0:T(8,128)(2,1)S(1)} %constant_dynamic-slice_fusion.5), channel_id=1, source_target_pairs={{0,16},{16,0},{1,17},{17,1},{2,18},{18,2},{3,19},{19,3},{4,20},{20... | collective-permute-start | bytes 589832 | tf_op jit(solution)/shard_map/ppermute | solution.py:26
  388.9 14.3 %collective-permute-start.34 = (bf16[160,768]{1,0:T(8,128)(2,1)S(1)}, bf16[160,768]{1,0:T(8,128)(2,1)S(1)}, u32[]{:S(2)}, u32[]{:S(2)}) collective-permute-start(bf16[160,768]{1,0:T(8,128)(2,1)S(1)} %constant_dynamic-slice_fusion.8), channel_id=1, source_target_pairs={{0,4},{1,5},{2,6},{3,7},{4,0},{5,1},{6,2},{7,3},{8,12},{9,13},{10,... | collective-permute-start | bytes 737288 | tf_op jit(solution)/shard_map/ppermute | solution.py:26
  392.6 12.5 %collective-permute-start.51 = (bf16[64,768]{1,0:T(8,128)(2,1)S(1)}, bf16[64,768]{1,0:T(8,128)(2,1)S(1)}, u32[]{:S(2)}, u32[]{:S(2)}) collective-permute-start(bf16[64,768]{1,0:T(8,128)(2,1)S(1)} %constant_dynamic-slice_fusion.1), channel_id=1, source_target_pairs={{0,16},{16,0},{1,17},{17,1},{2,18},{18,2},{3,19},{19,3},{4,20},{20... | collective-permute-start | bytes 294920 | tf_op jit(solution)/shard_map/ppermute | solution.py:26
  395.4 11.8 %collective-permute-start.43 = (bf16[64,768]{1,0:T(8,128)(2,1)S(1)}, bf16[64,768]{1,0:T(8,128)(2,1)S(1)}, u32[]{:S(2)}, u32[]{:S(2)}) collective-permute-start(bf16[64,768]{1,0:T(8,128)(2,1)S(1)} %constant_dynamic-slice_fusion.4), channel_id=1, source_target_pairs={{0,4},{1,5},{2,6},{3,7},{4,0},{5,1},{6,2},{7,3},{8,12},{9,13},{10,... | collective-permute-start | bytes 294920 | tf_op jit(solution)/shard_map/ppermute | solution.py:26
  403.3 13.2 %collective-permute-start.35 = (bf16[80,768]{1,0:T(8,128)(2,1)S(1)}, bf16[80,768]{1,0:T(8,128)(2,1)S(1)}, u32[]{:S(2)}, u32[]{:S(2)}) collective-permute-start(bf16[80,768]{1,0:T(8,128)(2,1)S(1)} %constant_dynamic-slice_fusion.7), channel_id=1, source_target_pairs={{0,2},{1,3},{2,0},{3,1},{4,6},{5,7},{6,4},{7,5},{8,10},{9,11},{10,... | collective-permute-start | bytes 368648 | tf_op jit(solution)/shard_map/ppermute | solution.py:26
  405.2 8.2 %collective-permute-start.52 = (bf16[32,768]{1,0:T(8,128)(2,1)S(1)}, bf16[32,768]{1,0:T(8,128)(2,1)S(1)}, u32[]{:S(2)}, u32[]{:S(2)}) collective-permute-start(bf16[32,768]{1,0:T(8,128)(2,1)S(1)} %constant_dynamic-slice_fusion), channel_id=1, source_target_pairs={{0,8},{1,9},{2,10},{3,11},{4,12},{5,13},{6,14},{7,15},{8,0},{9,1},... | collective-permute-start | bytes 147464 | tf_op jit(solution)/shard_map/ppermute | solution.py:26
  407.3 8.5 %collective-permute-start.44 = (bf16[32,768]{1,0:T(8,128)(2,1)S(1)}, bf16[32,768]{1,0:T(8,128)(2,1)S(1)}, u32[]{:S(2)}, u32[]{:S(2)}) collective-permute-start(bf16[32,768]{1,0:T(8,128)(2,1)S(1)} %constant_dynamic-slice_fusion.3), channel_id=1, source_target_pairs={{0,8},{1,9},{2,10},{3,11},{4,12},{5,13},{6,14},{7,15},{8,0},{9,1},... | collective-permute-start | bytes 147464 | tf_op jit(solution)/shard_map/ppermute | solution.py:26
  413.5 6.7 %collective-permute-start.53 = (bf16[32,768]{1,0:T(8,128)(2,1)S(1)}, bf16[32,768]{1,0:T(8,128)(2,1)S(1)}, u32[]{:S(2)}, u32[]{:S(2)}) collective-permute-start(bf16[32,768]{1,0:T(8,128)(2,1)S(1)} %add_convert_fusion.26), channel_id=1, source_target_pairs={{0,8},{1,9},{2,10},{3,11},{4,12},{5,13},{6,14},{7,15},{8,0},{9,1},... | collective-permute-start | bytes 147464 | tf_op jit(solution)/shard_map/ppermute | solution.py:26
  415.8 5.4 collective-permute-start.45
  416.6 5.7 collective-permute-start.36
  420.2 4.7 collective-permute-start.54
  421.2 8.0 %collective-permute-start.46 = (bf16[64,768]{1,0:T(8,128)(2,1)S(1)}, bf16[64,768]{1,0:T(8,128)(2,1)S(1)}, u32[]{:S(2)}, u32[]{:S(2)}) collective-permute-start(bf16[64,768]{1,0:T(8,128)(2,1)S(1)} %maximum_select_fusion.22), channel_id=1, source_target_pairs={{0,4},{1,5},{2,6},{3,7},{4,0},{5,1},{6,2},{7,3},{8,12},{9,13},{10,... | collective-permute-start | bytes 294920 | tf_op jit(solution)/shard_map/ppermute | solution.py:26
  422.4 6.0 %collective-permute-start.37 = (bf16[40,768]{1,0:T(8,128)(2,1)S(1)}, bf16[40,768]{1,0:T(8,128)(2,1)S(1)}, u32[]{:S(2)}, u32[]{:S(2)}) collective-permute-start(bf16[40,768]{1,0:T(8,128)(2,1)S(1)} %add_convert_fusion.25), channel_id=1, source_target_pairs={{0,8},{1,9},{2,10},{3,11},{4,12},{5,13},{6,14},{7,15},{8,0},{9,1},... | collective-permute-start | bytes 184328 | tf_op jit(solution)/shard_map/ppermute | solution.py:26
  424.9 10.6 %collective-permute-start.55 = (bf16[128,768]{1,0:T(8,128)(2,1)S(1)}, bf16[128,768]{1,0:T(8,128)(2,1)S(1)}, u32[]{:S(2)}, u32[]{:S(2)}) collective-permute-start(bf16[128,768]{1,0:T(8,128)(2,1)S(1)} %maximum_select_fusion.19), channel_id=1, source_target_pairs={{0,2},{1,3},{2,0},{3,1},{4,6},{5,7},{6,4},{7,5},{8,10},{9,11},{10,... | collective-permute-start | bytes 589832 | tf_op jit(solution)/shard_map/ppermute | solution.py:26
  428.4 10.2 %collective-permute-start.38 = (bf16[80,768]{1,0:T(8,128)(2,1)S(1)}, bf16[80,768]{1,0:T(8,128)(2,1)S(1)}, u32[]{:S(2)}, u32[]{:S(2)}) collective-permute-start(bf16[80,768]{1,0:T(8,128)(2,1)S(1)} %maximum_select_fusion.20), channel_id=1, source_target_pairs={{0,2},{1,3},{2,0},{3,1},{4,6},{5,7},{6,4},{7,5},{8,10},{9,11},{10,... | collective-permute-start | bytes 368648 | tf_op jit(solution)/shard_map/ppermute | solution.py:26
  429.2 9.4 %collective-permute-start.47 = (bf16[128,768]{1,0:T(8,128)(2,1)S(1)}, bf16[128,768]{1,0:T(8,128)(2,1)S(1)}, u32[]{:S(2)}, u32[]{:S(2)}) collective-permute-start(bf16[128,768]{1,0:T(8,128)(2,1)S(1)} %maximum_select_fusion.18), channel_id=1, source_target_pairs={{0,16},{16,0},{1,17},{17,1},{2,18},{18,2},{3,19},{19,3},{4,20},{20... | collective-permute-start | bytes 589832 | tf_op jit(solution)/shard_map/ppermute | solution.py:26
  435.6 17.1 %collective-permute-start.56 = (bf16[256,768]{1,0:T(8,128)(2,1)S(1)}, bf16[256,768]{1,0:T(8,128)(2,1)S(1)}, u32[]{:S(2)}, u32[]{:S(2)}) collective-permute-start(bf16[256,768]{1,0:T(8,128)(2,1)S(1)} %maximum_select_fusion.12), channel_id=1, source_target_pairs={{0,4},{1,5},{2,6},{3,7},{4,0},{5,1},{6,2},{7,3},{8,12},{9,13},{10,... | collective-permute-start | bytes 1179656 | tf_op jit(solution)/shard_map/ppermute | solution.py:26
  438.6 12.1 %collective-permute-start.39 = (bf16[160,768]{1,0:T(8,128)(2,1)S(1)}, bf16[160,768]{1,0:T(8,128)(2,1)S(1)}, u32[]{:S(2)}, u32[]{:S(2)}) collective-permute-start(bf16[160,768]{1,0:T(8,128)(2,1)S(1)} %maximum_select_fusion.13), channel_id=1, source_target_pairs={{0,4},{1,5},{2,6},{3,7},{4,0},{5,1},{6,2},{7,3},{8,12},{9,13},{10,... | collective-permute-start | bytes 737288 | tf_op jit(solution)/shard_map/ppermute | solution.py:26
  438.8 14.3 %collective-permute-start.48 = (bf16[256,768]{1,0:T(8,128)(2,1)S(1)}, bf16[256,768]{1,0:T(8,128)(2,1)S(1)}, u32[]{:S(2)}, u32[]{:S(2)}) collective-permute-start(bf16[256,768]{1,0:T(8,128)(2,1)S(1)} %maximum_select_fusion.11), channel_id=1, source_target_pairs={{0,2},{1,3},{2,0},{3,1},{4,6},{5,7},{6,4},{7,5},{8,10},{9,11},{10,... | collective-permute-start | bytes 1179656 | tf_op jit(solution)/shard_map/ppermute | solution.py:26
  450.9 10.5 %collective-permute-start.40 = (bf16[320,768]{1,0:T(8,128)(2,1)S(1)}, bf16[320,768]{1,0:T(8,128)(2,1)S(1)}, u32[]{:S(2)}, u32[]{:S(2)}) collective-permute-start(bf16[320,768]{1,0:T(8,128)(2,1)S(1)} %maximum_select_fusion.6), channel_id=1, source_target_pairs={{0,16},{16,0},{1,17},{17,1},{2,18},{18,2},{3,19},{19,3},{4,20},{20... | collective-permute-start | bytes 1474568 | tf_op jit(solution)/shard_map/ppermute | solution.py:26
  453.0 12.3 %collective-permute-start.57 = (bf16[512,768]{1,0:T(8,128)(2,1)S(1)}, bf16[512,768]{1,0:T(8,128)(2,1)S(1)}, u32[]{:S(2)}, u32[]{:S(2)}) collective-permute-start(bf16[512,768]{1,0:T(8,128)(2,1)S(1)} %maximum_select_fusion.5), channel_id=1, source_target_pairs={{0,1},{1,0},{2,3},{3,2},{4,5},{5,4},{6,7},{7,6},{8,9},{9,8},{10,11... | collective-permute-start | bytes 2359304 | tf_op jit(solution)/shard_map/ppermute | solution.py:26
  454.3 17.0 %collective-permute-start.49 = (bf16[512,768]{1,0:T(8,128)(2,1)}, bf16[512,768]{1,0:T(8,128)(2,1)}, u32[]{:S(2)}, u32[]{:S(2)}) collective-permute-start(bf16[512,768]{1,0:T(8,128)(2,1)} %maximum_select_fusion.4), channel_id=1, source_target_pairs={{0,1},{1,0},{2,3},{3,2},{4,5},{5,4},{6,7},{7,6},{8,9},{9,8},{10,11... | collective-permute-start | bytes 2359304 | tf_op jit(solution)/shard_map/ppermute | solution.py:26
  462.7 16.1 %collective-permute-start.41 = (bf16[640,768]{1,0:T(8,128)(2,1)}, bf16[640,768]{1,0:T(8,128)(2,1)}, u32[]{:S(2)}, u32[]{:S(2)}) collective-permute-start(bf16[640,768]{1,0:T(8,128)(2,1)} %maximum_select_fusion.3), channel_id=1, source_target_pairs={{0,1},{1,0},{2,3},{3,2},{4,5},{5,4},{6,7},{7,6},{8,9},{9,8},{10,11... | collective-permute-start | bytes 2949128 | tf_op jit(solution)/shard_map/ppermute | solution.py:26
  (142 other events, 981.4 us)
Sparse Core Ops, SparseCore 0:
  346.4 216.7 all-reduce.8

commit v6 on v5

--- a/solution.py
+++ b/solution.py
@@ -76,24 +76,31 @@
     return sum([named[name] for name in ("core",) + order + ("rest",)], [])
 
 
-ORDERS = (("row", "far", "near"), ("near", "row", "far"), ("far", "near", "row"))
+def begin(array, down, back):
+    return array, stages(down), stages(back), 0
 
 
 def advance(state, steps):
-    held, plan, done = state
-    for step in range(done, min(done + steps, 2 * len(plan))):
-        if step < len(plan):
-            axis, bit = plan[step]
+    held, down, back, done = state
+    for step in range(done, min(done + steps, 2 * len(down))):
+        if step < len(down):
+            axis, bit = down[step]
             half = held.shape[0] // 2
             side = (lax.axis_index(axis) // bit) % 2
             mine = lax.dynamic_slice_in_dim(held, side * half, half, 0)
             other = lax.dynamic_slice_in_dim(held, (1 - side) * half, half, 0)
-            held = mine.astype(F32) + swap(other.astype(BF), axis, bit).astype(F32)
+            held = mine.astype(F32) + swap(other, axis, bit).astype(F32)
             held = held.astype(BF)
         else:
-            axis, bit = plan[2 * len(plan) - 1 - step]
+            axis, bit = back[2 * len(down) - 1 - step]
             held = paired(held, axis, bit, 0)
-    return held, plan, min(done + steps, 2 * len(plan))
+    return held, down, back, min(done + steps, 2 * len(down))
+
+
+def last_swap(state):
+    down, back = state[1], state[2]
+    held = advance(state, 2 * len(down) - 1 - state[3])[0]
+    return held, swap(held, *down[0]), down, back
 
 
 def tied(values, states):
@@ -202,6 +209,8 @@
                 spread(mq_ref[rows, g * GROUP : (g + 1) * GROUP]) for g in range(groups)
             ]
 
+            ones = jnp.ones((BLOCK, 128), BF)
+
             def step(block, carry):
                 first = pl.multiple_of(block * BLOCK, BLOCK)
                 at = pl.ds(first, BLOCK)
@@ -211,27 +220,28 @@
                     cols = slice(g * GROUP, (g + 1) * GROUP)
                     scores = dot_nt(wide[g], k_ref[at, cols]) * scale
                     scores = jnp.where(valid, scores, NEGATIVE)
-                    old = max_s[cols, :1]
+                    old = max_s[cols, :]
                     top = jnp.maximum(old, jnp.max(scores, axis=1, keepdims=True))
-                    weights = jnp.exp(scores - top)
+                    weights = jnp.exp(scores - twice(top)).astype(BF)
                     shrink = jnp.exp(old - top)
-                    sums = sum_s[cols, :1] * shrink + jnp.sum(weights, axis=1, keepdims=True)
-                    acc_s[cols, :] = acc_s[cols, :] * shrink + dot_nn(
-                        weights.astype(BF), v_ref[at, cols]
-                    )
-                    max_s[cols, :] = jnp.broadcast_to(top, (GROUP, 128))
-                    sum_s[cols, :] = jnp.broadcast_to(sums, (GROUP, 128))
+                    max_s[cols, :] = top
+                    sum_s[cols, :] = sum_s[cols, :] * shrink + dot_nn(weights, ones)
+                    acc_s[cols, :] = acc_s[cols, :] * twice(shrink) + dot_nn(weights, v_ref[at, cols])
                 return carry
 
             lax.fori_loop(low // BLOCK, (high + BLOCK - 1) // BLOCK, step, 0)
             columns = []
             for g in range(groups):
                 cols = slice(g * GROUP, (g + 1) * GROUP)
-                sums = sum_s[cols, :1]
-                out_ref[rows, cols] = gathered(acc_s[cols, :] / sums).astype(BF)
-                level = max_s[cols, :1] + jnp.log(sums)
+                sums = sum_s[cols, :]
+                out_ref[rows, cols] = gathered(acc_s[cols, :] / twice(sums)).astype(BF)
+                level = max_s[cols, :] + jnp.log(sums)
                 columns += [level[h * LAND : (h + 1) * LAND] for h in range(4)]
             out_ref[rows, width:] = split_three(by_head(columns, 0, (LAND, 128)))
+
+
+def twice(cells):
+    return jnp.concatenate([cells, cells], axis=1)
 
 
 def join_kernel(a_ref, b_ref, out_ref):
@@ -527,21 +537,156 @@
     )
 
 
-def pinv_kernel(queries, key_rows, score_scale):
-    scores = jnp.einsum("pie,pje->pij", queries, key_rows, precision=HIGH) * score_scale
-    row_max = jnp.max(scores, axis=-1, keepdims=True)
-    weights = jnp.exp(scores - row_max)
-    kernel = weights / jnp.sum(weights, axis=-1, keepdims=True)
-    column_max = jnp.max(jnp.sum(kernel, axis=1), axis=-1)
-    inverse = jnp.swapaxes(kernel, -1, -2) / column_max[:, None, None]
-    identity = jnp.eye(LAND, dtype=F32)
+def dot_high(a, b, dims):
+    return lax.dot_general(
+        a, b, (dims, ((), ())), precision=HIGH, preferred_element_type=F32
+    )
+
+
+NN, NT, TN = ((1,), (0,)), ((1,), (1,)), ((0,), (0,))
+
+
+def pinv_kernel(scale, q_ref, k_ref, inverse_ref, kernel_ref, saved_ref):
+    count = q_ref.shape[0]
+    eye = (iota((LAND, LAND), 0) == iota((LAND, LAND), 1)).astype(F32)
+    kernels, inverses = [], []
+    for p in range(count):
+        scores = dot_high(q_ref[p], k_ref[p], NT) * scale
+        weights = jnp.exp(scores - jnp.max(scores, axis=1, keepdims=True))
+        kernel = weights / jnp.sum(weights, axis=1, keepdims=True)
+        kernel_ref[p] = kernel
+        kernels.append(kernel)
+        largest = jnp.max(jnp.sum(kernel, axis=0, keepdims=True), axis=1, keepdims=True)
+        inverses.append(kernel.T / largest)
     for sweep in range(NS_ITERS):
-        product = jnp.matmul(kernel, inverse, precision=HIGH)
-        bracket = 7.0 * identity - product
-        bracket = 15.0 * identity - jnp.matmul(product, bracket, precision=HIGH)
-        bracket = 13.0 * identity - jnp.matmul(product, bracket, precision=HIGH)
-        inverse = 0.25 * jnp.matmul(inverse, bracket, precision=HIGH)
-    return inverse
+        products = [dot_high(kernels[p], inverses[p], NN) for p in range(count)]
+        second = [
+            15.0 * eye - dot_high(products[p], 7.0 * eye - products[p], NN) for p in range(count)
+        ]
+        third = [13.0 * eye - dot_high(products[p], second[p], NN) for p in range(count)]
+        for p in range(count):
+            at = (sweep * count + p) * 4
+            saved_ref[at], saved_ref[at + 1] = inverses[p], products[p]
+            saved_ref[at + 2], saved_ref[at + 3] = second[p], third[p]
+        inverses = [0.25 * dot_high(inverses[p], third[p], NN) for p in range(count)]
+    for p in range(count):
+        inverse_ref[p] = inverses[p]
+
+
+def pinv_back_kernel(scale, q_ref, k_ref, kernel_ref, saved_ref, grad_ref, avg_ref, gq_ref, gk_ref):
+    count = q_ref.shape[0]
+    each = range(count)
+    eye = (iota((LAND, LAND), 0) == iota((LAND, LAND), 1)).astype(F32)
+    grads = [dot_nt(grad_ref[p], avg_ref[p]) for p in each]
+    kernels = [kernel_ref[p] for p in each]
+    totals = [jnp.zeros((LAND, LAND), F32) for p in each]
+    for sweep in reversed(range(NS_ITERS)):
+        first = [(sweep * count + p) * 4 for p in each]
+        inverses, products = [saved_ref[a] for a in first], [saved_ref[a + 1] for a in first]
+        grad_third = [0.25 * dot_high(inverses[p], grads[p], TN) for p in each]
+        nexts = [0.25 * dot_high(grads[p], saved_ref[first[p] + 3], NT) for p in each]
+        grad_second = [-dot_high(products[p], grad_third[p], TN) for p in each]
+        grad_product = [-dot_high(grad_third[p], saved_ref[first[p] + 2], NT) for p in each]
+        grad_first = [-dot_high(products[p], grad_second[p], TN) for p in each]
+        grad_product = [
+            grad_product[p]
+            - dot_high(grad_second[p], 7.0 * eye - products[p], NT)
+            - grad_first[p]
+            for p in each
+        ]
+        totals = [totals[p] + dot_high(grad_product[p], inverses[p], NT) for p in each]
+        grads = [nexts[p] + dot_high(kernels[p], grad_product[p], TN) for p in each]
+    for p in each:
+        kernel = kernels[p]
+        sums = jnp.sum(kernel, axis=0, keepdims=True)
+        largest = jnp.max(sums, axis=1, keepdims=True)
+        flipped = grads[p].T
+        loss = jnp.sum(jnp.sum(flipped * kernel, axis=1, keepdims=True), axis=0, keepdims=True)
+        at_top = (sums == largest).astype(F32)
+        at_top = at_top / jnp.sum(at_top, axis=1, keepdims=True)
+        grad = totals[p] + flipped / largest - at_top * (loss / (largest * largest))
+        grad = kernel * (grad - jnp.sum(grad * kernel, axis=1, keepdims=True)) * scale
+        gq_ref[p] = dot_high(grad, k_ref[p], NN)
+        gk_ref[p] = dot_high(grad, q_ref[p], TN)
+
+
+def settle_kernel(side_ref, mine_ref, other_ref, out_ref):
+    own = pl.program_id(0) == side_ref[0]
+
+    @pl.when(own)
+    def _():
+        out_ref[...] = mine_ref[...].astype(F32)
+
+    @pl.when(jnp.logical_not(own))
+    def _():
+        out_ref[...] = other_ref[...].astype(F32)
+
+
+def settle(state):
+    mine, other, down, back = last_swap(state)
+    moved = len(stages(("row", "near", "far"))) - len(stages(()))
+    down, back = down[1 : 1 + moved], back[1 : 1 + moved]
+    blocks = 1 << moved
+    rows, columns = mine.shape[0] // blocks, mine.shape[1]
+
+    def source(j):
+        bits = {stage: (j >> (moved - 1 - i)) % 2 for i, stage in enumerate(down)}
+        at = 0
+        for stage in back:
+            at = at * 2 + bits[stage]
+        return at
+
+    side = (lax.axis_index("seq") % 2).astype(jnp.int32).reshape(1)
+    return pl.pallas_call(
+        settle_kernel,
+        grid_spec=pltpu.PrefetchScalarGridSpec(
+            num_scalar_prefetch=1,
+            grid=(2, blocks),
+            in_specs=[
+                pl.BlockSpec((rows, columns), lambda h, j, s: (jnp.where(h == s[0], source(j), 0), 0)),
+                pl.BlockSpec((rows, columns), lambda h, j, s: (jnp.where(h == s[0], 0, source(j)), 0)),
+            ],
+            out_specs=pl.BlockSpec((rows, columns), lambda h, j, s: (h * blocks + j, 0)),
+        ),
+        out_shape=jax.ShapeDtypeStruct((2 * blocks * rows, columns), F32),
+        name="settle",
+    )(side, mine, other)
+
+
+def settle_qkv_kernel(side_ref, late_ref, late_other_ref, early_ref, early_other_ref, out_ref):
+    part = pl.program_id(0)
+    own = jnp.where(part == 0, 0, 1) == side_ref[0]
+    choices = [
+        (late_ref, own & (part < 2)),
+        (late_other_ref, jnp.logical_not(own) & (part < 2)),
+        (early_ref, own & (part == 2)),
+        (early_other_ref, jnp.logical_not(own) & (part == 2)),
+    ]
+    for ref, chosen in choices:
+
+        @pl.when(chosen)
+        def _():
+            out_ref[...] = ref[...].astype(F32)
+
+
+def settle_qkv(late, late_other, early, early_other, width):
+    side = (lax.axis_index("seq") % 2).astype(jnp.int32).reshape(1)
+    rows = width // 3
+
+    def spec(used):
+        return pl.BlockSpec((rows, width), lambda j, i, s: (jnp.where(used(j), i, 0), 0))
+
+    return pl.pallas_call(
+        settle_qkv_kernel,
+        grid_spec=pltpu.PrefetchScalarGridSpec(
+            num_scalar_prefetch=1,
+            grid=(3, 3),
+            in_specs=[spec(lambda j: j < 2), spec(lambda j: j < 2)] + [spec(lambda j: j == 2)] * 2,
+            out_specs=pl.BlockSpec((rows, width), lambda j, i, s: (i, j)),
+        ),
+        out_shape=jax.ShapeDtypeStruct((width, 3 * width), F32),
+        name="settle_qkv",
+    )(side, late, late_other, early, early_other)
 
 
 def per_device(
@@ -628,15 +773,23 @@
     def of_doc(array):
         return lax.dynamic_slice_in_dim(array, own_doc * LAND, LAND, 0)
 
-    own_inverse, inverse_pullback = jax.vjp(
-        lambda a, b: pinv_kernel(a, b, scale),
-        own_heads(of_doc(mark_q)).astype(F32),
-        own_heads(of_doc(mark_k)).astype(F32),
-    )
+    mine, other = halves(stats, 1)
+    stats = join(mine, swap(other, "seq", 1))
+    stats, later_q, later_k = lax.optimization_barrier((stats, mark_q, mark_k))
+    own_q = own_heads(of_doc(later_q)).astype(F32)
+    own_k = own_heads(of_doc(later_k)).astype(F32)
+    square = (own_count, LAND, LAND)
+    own_inverse, kernel, saved = pl.pallas_call(
+        lambda *refs: pinv_kernel(scale, *refs),
+        out_shape=(
+            shaped(square, F32), shaped(square, F32),
+            shaped((4 * NS_ITERS * own_count, LAND, LAND), F32),
+        ),
+        name="pinv",
+    )(own_q, own_k)
     inverse = own_inverse.transpose(1, 0, 2).reshape(LAND, own_count * size).astype(BF)
-    for bit in (1, 2):
-        mine, other = halves(stats, bit)
-        stats = join(mine, swap(other, "seq", bit))
+    mine, other = halves(stats, 2)
+    stats = join(mine, swap(other, "seq", 2))
     for i in range(2, seq_count.bit_length() - 1):
         other = swap(jnp.concatenate([stats, inverse], 1), "seq", 1 << i)
         stats = join(stats, other[:, : width + 128])
@@ -699,9 +852,6 @@
         tokens, mixed, cotangent[0], w_out, w_up, w_down, vectors,
         jnp.broadcast_to(bias_up[None, :], (8, hidden)),
     )
-    grad_gain_two, grad_shift_two, grad_bias_down = sums[0], sums[1], sums[2]
-    grad_gain_one, grad_shift_one, grad_bias_out = sums[3], sums[4], sums[5]
-    grad_bias_up = sum_up[0]
 
     grad_queries, grad_mix, grad_mk = pl.pallas_call(
         lambda *refs: token_back_kernel(docs, scale, *refs),
@@ -721,12 +871,12 @@
     )(bounds, qkv, grad_mixed, probs, mark_k, mix)
     grad_w_down = lax.dot_general(active, grad_low_two, rows_in, preferred_element_type=F32)
     grad_w_up = lax.dot_general(hidden_low, grad_upper, rows_in, preferred_element_type=F32)
-    grad_w_down, grad_w_up = grad_w_down.astype(BF), grad_w_up.astype(BF)
+    down = begin(grad_w_down.astype(BF), ("row", "far", "near"), ("far", "near", "row"))
+    up = begin(grad_w_up.astype(BF), ("row", "near", "far"), ("near", "far", "row"))
     grad_mix = seq_quarter(grad_mix.astype(BF), add_join)
-    grad_mix, grad_w_down, grad_w_up = lax.optimization_barrier(
-        (grad_mix, grad_w_down, grad_w_up)
-    )
-    sum_w_down, sum_w_up = lax.psum((grad_w_down, grad_w_up), ("row", "seq"))
+    down, up = advance(down, 1), advance(up, 1)
+    grad_mix, (down, up) = tied(grad_mix, [down, up])
+    down, up = advance(down, 1), advance(up, 1)
     grad_w_out = lax.dot_general(mixed, grad_low_one, rows_in, preferred_element_type=F32)
 
     grad_ext = extended(grad_mixed, radius, window_rows)
@@ -742,20 +892,10 @@
         compiler_params=params,
         name="conv_back",
     )(bounds, grad_ext, value_ext, jnp.pad(conv_taps[:, ::-1], ((0, 0), (0, GROUP - tap_count))))
-    reach = SUB + tap_count - 1
-    products = products.reshape(heads, SUB, GROUP)[:, :, :reach].reshape(heads, SUB * reach)
-    products = jnp.pad(products, ((0, 0), (0, SUB))).reshape(heads, SUB, reach + 1)
-    grad_conv_taps = jnp.sum(products, axis=1)[:, :tap_count]
-
     grad_avg = pl.pallas_call(
         mix_back_kernel, out_shape=shaped((LAND, width + 128), BF), name="mix_back"
     )(inverse, stats, grad_mix)
     grad_avg = seq_whole(grad_avg)
-    grad_inverse = jnp.einsum(
-        "pie,pje->pij", own_heads(grad_mix), own_heads(stats[:, :width]),
-        preferred_element_type=F32,
-    )
-    grad_mq_small, grad_mk_small = inverse_pullback(grad_inverse)
     lane_spec = pl.BlockSpec((mark_count, 128), lambda i: (0, width // 128))
     grad_keys, grad_values, grad_mq = pl.pallas_call(
         lambda *refs: landmark_back_kernel(docs, scale, *refs),
@@ -773,6 +913,15 @@
         name="landmark_back",
     )(bounds, qkv, qkv, grad_conv, mark_q, grad_avg, mix, grad_avg)
 
+    grad_keys, (down, up) = tied(grad_keys, [down, up])
+    down, up = advance(down, 1), advance(up, 1)
+    grad_mix, grad_values = lax.optimization_barrier((grad_mix, grad_values))
+    grad_mq_small, grad_mk_small = pl.pallas_call(
+        lambda *refs: pinv_back_kernel(scale, *refs),
+        out_shape=(shaped(square, F32), shaped(square, F32)),
+        name="pinv_back",
+    )(own_q, own_k, kernel, saved, own_heads(grad_mix), own_heads(stats[:, :width]))
+
     def placed(array):
         array = array.transpose(1, 0, 2).reshape(LAND, own_count * size)
         array = lax.dynamic_update_slice_in_dim(
@@ -793,46 +942,69 @@
     grad_bias_q = jnp.sum(grad_queries.astype(F32), axis=0) + jnp.sum(grad_mq, axis=0)
     grad_bias_v = jnp.sum(grad_values.astype(F32), axis=0)
     grad_projected = jnp.concatenate([grad_queries, grad_keys, grad_values], axis=1)
-    grad_w_qkv = lax.dot_general(tokens, grad_projected, rows_in, preferred_element_type=F32)
-    grad_w_marks = lax.dot_general(mean_in, grad_marks, rows_in, preferred_element_type=F32)
-    grad_w_qkv = (grad_w_qkv + jnp.pad(grad_w_marks, ((0, 0), (0, width)))).astype(BF)
-    small = [
-        grad_bias_q, grad_bias_v, grad_conv_taps.reshape(-1), grad_bias_out, grad_gain_one,
-        grad_shift_one, grad_bias_up, grad_bias_down, grad_gain_two, grad_shift_two,
+
+    def weight_grad(grads):
+        return lax.dot_general(tokens, grads, rows_in, preferred_element_type=F32)
+
+    early = jnp.concatenate([grad_w_out.astype(BF), weight_grad(grad_values).astype(BF)], 0)
+    early = begin(early, ("row", "near", "far"), ("row", "near", "far"))
+    early = advance(early, 1)
+    grad_marks, (early,) = tied(grad_marks, [early])
+    early = advance(early, 1)
+    mark_grad_q = lax.dot_general(
+        mean_in, grad_marks[:, :width], rows_in, preferred_element_type=F32
+    )
+    mark_grad_k = lax.dot_general(
+        mean_in, grad_marks[:, width:], rows_in, preferred_element_type=F32
+    )
+    products, (early,) = tied(products, [early])
+    reach = SUB + tap_count - 1
+    products = products.reshape(heads, SUB, GROUP)[:, :, :reach].reshape(heads, SUB * reach)
+    products = jnp.pad(products, ((0, 0), (0, SUB))).reshape(heads, SUB, reach + 1)
+    grad_conv_taps = jnp.sum(products, axis=1)[:, :tap_count]
+    others = jnp.concatenate(
+        [
+            sum_up[0].reshape(hidden // width, width),
+            grad_bias_q[None],
+            grad_bias_v[None],
+            jnp.pad(grad_conv_taps.reshape(1, -1), ((0, 0), (0, width - heads * tap_count))),
+            jnp.zeros((4 - hidden // width + 1, width), F32),
+        ],
+        0,
+    )
+    spare_rows = width // 6
+    small = jnp.concatenate([sums, others], 0).astype(BF)
+    small = jnp.pad(small, ((0, spare_rows - small.shape[0]), (0, 0)))
+    small = lax.optimization_barrier(small)
+    late = jnp.concatenate(
+        [
+            (weight_grad(grad_queries) + mark_grad_q).astype(BF),
+            small,
+            (weight_grad(grad_keys) + mark_grad_k).astype(BF),
+            jnp.zeros((spare_rows, width), BF),
+        ],
+        0,
+    )
+    late = begin(late, ("row", "far", "near"), ("row", "far", "near"))
+    late = advance(late, 1)
+    mark_back = seq_quarter(mark_back, add_join)
+    mark_back, (early, late, down, up) = tied(mark_back, [early, late, down, up])
+    early, late = advance(early, 1), advance(late, 1)
+    down, up = advance(down, 1), advance(up, 1)
+    mark_back = seq_whole(mark_back)
+    mark_back, (early, late, down, up) = tied(mark_back, [early, late, down, up])
+    early, early_other = last_swap(early)[:2]
+    late, late_other = last_swap(late)[:2]
+    sum_w_down, sum_w_up = settle(down), settle(up)
+    sum_w_qkv = settle_qkv(late, late_other, early, early_other, width)
+    first_core = me % 2 == 0
+    sum_w_out = jnp.where(first_core, early, early_other).astype(F32)
+    flat = jnp.where(first_core, late[width:], late_other[width:])[:16].astype(F32)
+    at = sums.shape[0] + hidden // width
+    pieces = [
+        flat[at], flat[at + 1], flat[at + 2, : heads * tap_count], flat[5], flat[3], flat[4],
+        flat[sums.shape[0] : at].reshape(hidden), flat[2], flat[0], flat[1],
     ]
-    sizes = [piece.shape[0] for piece in small]
-    flat = jnp.concatenate(small)
-    third = width // 3
-    flat = jnp.pad(flat, (0, third * width - flat.shape[0])).reshape(third, width).astype(BF)
-    w_q, w_k, w_v = [grad_w_qkv[:, i * width : (i + 1) * width] for i in range(3)]
-    late = [
-        jnp.concatenate([grad_w_out.astype(BF), w_q[: 2 * third]], 0),
-        jnp.concatenate([w_q[2 * third :], w_k], 0),
-        jnp.concatenate([w_v, flat], 0),
-    ]
-    late = [advance((array, stages(order), 0), 1) for array, order in zip(late, ORDERS)]
-    mark_back = seq_quarter(mark_back, add_join)
-    mark_back, late = tied(mark_back, late)
-    late = [advance(state, 1) for state in late]
-    mark_back = seq_whole(mark_back)
-    mark_back, late = tied(mark_back, late)
-    first, second, last = [advance(state, 64)[0].astype(F32) for state in late]
-    sum_w_out = first[:width]
-    sum_w_qkv = jnp.concatenate(
-        [
-            jnp.concatenate([first[width:], second[:third]], 0),
-            second[third:],
-            last[:width],
-        ],
-        axis=1,
-    )
-    sum_w_down, sum_w_up = sum_w_down.astype(F32), sum_w_up.astype(F32)
-    flat = last[width:].reshape(-1)
-    pieces = []
-    at = 0
-    for length in sizes:
-        pieces.append(flat[at : at + length])
-        at += length
     grad_input = (
         grad_one
         + lax.dot_general(grad_projected, w_qkv, cols_in, preferred_element_type=F32)

time: 593 us -> 537 us (0.906)
  Pallas kernels: 103 us -> 143 us
  waiting for transfers between devices: 185 us -> 163 us
  matrix products: 65.4 us -> 43.9 us
  starting transfers between devices: 80.2 us -> 62.5 us
  between operations: 17.4 us -> 3.17 us
  local copies, waits for them, and re-layouts: 73.6 us -> 64.1 us
    psum x1 -> x0, waiting for transfers between devices: 74.6 us -> none  [per_device(): sum_w_down, sum_w_up = lax.psum((grad_w_down, grad_w_up), ('row', 'seq'))]
    ppermute x54 -> x64, waiting for transfers between devices: 111 us -> 163 us  [swap(): return lax.ppermute(array, axis, [(i, i ^ bit) for i in range(count)])]
    pallas_call x0 -> x5, Pallas kernels: none -> 48.9 us  [the longest x2 22.6 us: settle(): pl.pallas_call(settle_kernel, grid_spec=pltpu.PrefetchScalarGridSpec(num_...]
    ppermute x54 -> x64, starting transfers between devices: 73.6 us -> 53.5 us  [swap(): return lax.ppermute(array, axis, [(i, i ^ bit) for i in range(count)])]
    dot_general x78 -> x5, matrix products: 29.3 us -> 10 us  [the longest x3 6.94 us: weight_grad(): return lax.dot_general(tokens, grads, rows_in, preferred_element_type=F32)]
    pallas_call x1, Pallas kernels: 23.3 us -> 7.32 us  [per_device(): pl.pallas_call(lambda *refs: landmark_kernel(docs, scale, *refs), grid=(1...]
    convert_element_type x15 -> x20, other arithmetic: 6.98 us -> 21.7 us  [advance(): held = held.astype(BF)]
    convert_element_type x5 -> x4, other arithmetic: 17.1 us -> 2.68 us  [the longest x1 1.67 us: per_device(): sum_w_out = jnp.where(first_core, early, early_other).astype(F32)]
  transfers between devices with their start and end apart: 59 -> 68, of which waited for: 33 -> 32; matrix products, arithmetic and copies ran while one was open for 19% -> 21% of each run, Pallas kernels for 2% -> 10%
where the time goes in v6:
time: 537 us; the launch traced here: 532 us
  waiting for transfers between devices  163 us (30%)
  Pallas kernels  143 us (27%)
  local copies, waits for them, and re-layouts  64.1 us (12%)
  starting transfers between devices  62.5 us (12%)
  other arithmetic  52.5 us (10%)
  matrix products  43.9 us (8%)
    ppermute x64, waiting for transfers between devices, swap(): return lax.ppermute(array, axis, [(i, i ^ bit) for i in range(count)])  163 us
    ppermute x64, starting transfers between devices, swap(): return lax.ppermute(array, axis, [(i, i ^ bit) for i in range(count)])  53.5 us
    pallas_call x1, Pallas kernels, per_device(): pl.pallas_call(ffn_kernel, grid=(tok_count // FFN_BLOCK,), in_specs=[ffn_...  40.5 us
    unnamed x150, local copies, waits for them, and re-layouts  23.8 us
    pallas_call x2, Pallas kernels, settle(): pl.pallas_call(settle_kernel, grid_spec=pltpu.PrefetchScalarGridSpec(num_...  22.6 us
    convert_element_type x20, other arithmetic, advance(): held = held.astype(BF)  21.7 us
  transfers between devices with their start and end apart: 68, of which 32 were waited for; matrix products, arithmetic and copies ran while one was open for 21% of the time, Pallas kernels for 10%

profile of v6, /device:TPU:0, one launch (start us, length us, event | category | flops | bytes accessed | tf_op | source)
XLA Modules:
  0.0 532.0 jit_solution(779618757813298356)
XLA Ops:
  3.1 2.2 fusion.15
  7.1 3.0 collective-permute-start.3
  10.0 3.1 collective-permute-done.3
  15.0 6.0 %add_convert_fusion.refs_2_.refs_3_.refs_1_ = bf16[1024,2304]{1,0:T(8,128)(2,1)S(1)} fusion(bf16[768,2304]{1,0:T(8,128)(2,1)} %param.19, f32[2304]{0:T(1024)S(1)} %pad_maximum_fusion.3, bf16[1,1024,768]{2,1,0:T(8,128)(2,1)S(1)} %copy-done.42), kind=kOutput, calls=%fused_computation | convolution fusion | flops 3628597248 | bytes 9839616 | tf_op jit(solution)/shard_map/dot_general | solution.py:742
  21.1 2.7 collective-permute-start.5
  25.0 3.0 collective-permute-start
  29.3 2.2 copy-done
  33.3 3.9 collective-permute-done.6
  41.7 7.3 %landmark.1 = bf16[256,896]{1,0:T(8,128)(2,1)S(1)} custom-call(s32[8]{0:T(128)S(1)} %add_subtract_fusion.refs_0_, bf16[256,768]{1,0:T(8,128)(2,1)S(1)} %fusion.25.refs_1_.refs_4_, bf16[1024,2304]{1,0:T(8,128)(2,1)S(1)} %bitcast.61, bf16[1024,2304]{1,0:T(8,128)(2,1)S(1)} %bitcast.61), custom_call_target="tpu_custom_call" | custom-call | tf_op jit(solution)/shard_map/landmark/pallas_call | solution.py:749
  52.0 2.6 join.4
  58.0 6.9 %pinv.1 = (f32[3,64,64]{2,1,0:T(8,128)}, f32[3,64,64]{2,1,0:T(8,128)}, f32[72,64,64]{2,1,0:T(8,128)}) custom-call(f32[3,64,64]{2,1,0:T(8,128)} %bitcast.67, f32[3,64,64]{2,1,0:T(8,128)} %bitcast.69), custom_call_target="tpu_custom_call" | custom-call | tf_op jit(solution)/shard_map/pinv/pallas_call | solution.py:782
  66.7 2.2 join.5.a_ref
  69.9 5.9 %collective-permute-done.10 = bf16[64,1088]{1,0:T(8,128)(2,1)S(1)} collective-permute-done((bf16[64,1088]{1,0:T(8,128)(2,1)S(1)}, bf16[64,1088]{1,0:T(8,128)(2,1)S(1)}, u32[]{:S(2)}, u32[]{:S(2)}) %collective-permute-start.10) | collective-permute-done | bytes 139296 | tf_op jit(solution)/shard_map/ppermute | solution.py:26
  79.7 9.8 %collective-permute-done.11 = bf16[64,1280]{1,0:T(8,128)(2,1)S(1)} collective-permute-done((bf16[64,1280]{1,0:T(8,128)(2,1)S(1)}, bf16[64,1280]{1,0:T(8,128)(2,1)S(1)}, u32[]{:S(2)}, u32[]{:S(2)}) %collective-permute-start.11) | collective-permute-done | bytes 163872 | tf_op jit(solution)/shard_map/ppermute | solution.py:26
  96.2 3.8 collective-permute-done.12
  105.2 2.3 copy-done.1
  107.6 9.8 %token_.1 = (bf16[1024,768]{1,0:T(8,128)(2,1)S(1)}, bf16[768,1024]{1,0:T(8,128)(2,1)S(1)}) custom-call(s32[8]{0:T(128)S(1)} %add_subtract_fusion.refs_0_, bf16[1024,2304]{1,0:T(8,128)(2,1)S(1)} %copy-done.1, bf16[1152,768]{1,0:T(8,128)(2,1)S(1)} %maximum_maximum_fusion.1.refs_2_, bf16[256,768]{1,0:T(8,128)(2,1)S(1)} %slice.198.refs_3_.refs_4_, ...), custom_call_target="tpu_custom_call" | custom-call | tf_op jit(solution)/shard_map/token/pallas_call | solution.py:810
  120.3 40.5 %ffn.1 = (f32[1024,768]{1,0:T(8,128)}, f32[1024,768]{1,0:T(8,128)}, bf16[1024,3072]{1,0:T(8,128)(2,1)}, bf16[1024,3072]{1,0:T(8,128)(2,1)}, bf16[1024,768]{1,0:T...) custom-call(bf16[1024,768]{1,0:T(8,128)(2,1)} %bitcast.66, ...), custom_call_target="tpu_custom_call" | custom-call | tf_op jit(solution)/shard_map/ffn/pallas_call | solution.py:832
  165.0 8.5 %token_back.1 = (bf16[1024,768]{1,0:T(8,128)(2,1)S(1)}, f32[256,768]{1,0:T(8,128)S(1)}, f32[256,768]{1,0:T(8,128)S(1)}) custom-call(s32[8]{0:T(128)S(1)} %add_subtract_fusion.refs_0_, bf16[1024,2304]{1,0:T(8,128)(2,1)S(1)} %bitcast.63, bf16[1024,768]{1,0:T(8,128)(2,1)S(1)} %copy-done.5, bf16[768,1024]{1,0:T(8,128)(2,1)S(1)} %copy-done.16, ...), custom_call_target="tpu_custom_call" | custom-call | tf_op jit(solution)/shard_map/token_back/pallas_call | solution.py:856
  173.7 7.9 %convolution_convert_fusion.1 = bf16[3072,768]{1,0:T(8,128)(2,1)S(1)} fusion(bf16[1024,3072]{1,0:T(8,128)(2,1)S(1)} %copy-done.63, bf16[1024,768]{1,0:T(8,128)(2,1)} %get-tuple-element.85), kind=kOutput, calls=%fused_computation.2 | convolution fusion | flops 4834197504 | bytes 12582912 | tf_op jit(solution)/shard_map/dot_general | solution.py:872
  184.5 5.4 %convolution_convert_fusion = bf16[768,3072]{1,0:T(8,128)(2,1)S(1)} fusion(bf16[1024,768]{1,0:T(8,128)(2,1)S(1)} %copy-done.68, bf16[1024,3072]{1,0:T(8,128)(2,1)S(1)} %bitcast.86), kind=kOutput, calls=%fused_computation.1 | convolution fusion | flops 4834197504 | bytes 12582912 | tf_op jit(solution)/shard_map/dot_general | solution.py:873
  195.2 3.4 collective-permute-start.14
  198.7 2.5 convolution_convert_fusion.3
  201.1 3.0 fusion.43
  206.4 3.3 collective-permute-done.17
  211.4 3.1 collective-permute-done.18
  216.1 5.5 %conv_back.1 = (f32[1024,768]{1,0:T(8,128)S(1)}, f32[1536,256]{1,0:T(8,128)S(1)}) custom-call(s32[8]{0:T(128)S(1)} %add_subtract_fusion.refs_0_, bf16[1152,768]{1,0:T(8,128)(2,1)S(1)} %maximum_maximum_fusion.2.refs_1_, bf16[1152,768]{1,0:T(8,128)(2,1)S(1)} %copy-done.4, f32[12,256]{1,0:T(8,128)S(1)} %pad.26.refs_3_), custom_call_target="tpu_custom_call" | custom-call | tf_op jit(solution)/shard_map/conv_back/pallas_call | solution.py:883
  222.4 5.3 %add_convert_fusion.2 = bf16[1536,768]{1,0:T(8,128)(2,1)} fusion(bf16[1536,768]{1,0:T(8,128)(2,1)} %collective-permute-done.20, bf16[3072,768]{1,0:T(8,128)(2,1)} %copy-done.32, s32[]{:T(128)S(6)} %select_n.586), kind=kLoop, calls=%fused_computation.10 | loop fusion | flops 4718592 | bytes 7077892 | tf_op jit(solution)/shard_map/convert_element_type | solution.py:93
  227.7 4.7 add_convert_fusion.1
  235.1 2.4 constant_dynamic-slice_fusion.20
  243.3 2.3 copy-done.2
  245.6 9.5 %landmark_back.1 = (bf16[1024,768]{1,0:T(8,128)(2,1)S(1)}, bf16[1024,768]{1,0:T(8,128)(2,1)S(1)}, f32[256,768]{1,0:T(8,128)S(1)}) custom-call(s32[8]{0:T(128)S(1)} %add_subtract_fusion.refs_0_, bf16[1024,2304]{1,0:T(8,128)(2,1)S(1)} %copy-done.2, bf16[1024,2304]{1,0:T(8,128)(2,1)S(1)} %copy-done.2, f32[1024,768]{1,0:T(8,128)S(1)} %copy-done.8, ...), custom_call_target="tpu_custom_call" | custom-call | tf_op jit(solution)/shard_map/landmark_back/pallas_call | solution.py:900
  257.2 2.5 fusion.14
  261.8 9.8 %pinv_back.1 = (f32[3,64,64]{2,1,0:T(8,128)}, f32[3,64,64]{2,1,0:T(8,128)}) custom-call(f32[3,64,64]{2,1,0:T(8,128)} %bitcast.68, f32[3,64,64]{2,1,0:T(8,128)} %bitcast.70, f32[3,64,64]{2,1,0:T(8,128)} %get-tuple-element.96.refs_2_, f32[72,64,64]{2,1,0:T(8,128)} %get-tuple-element.97.refs_3_, bf16[3,64,64]{2,1,0:T(8,128)(2,1)} %bitcast.79, ...), custom_call_target="tpu_custom_call" | custom-call | tf_op jit(solution)/shard_map/pinv_back/pallas_call | solution.py:919
  278.5 2.6 fusion.21
  283.8 4.7 collective-permute-done.27
  305.5 8.4 %collective-permute-done.31 = bf16[384,768]{1,0:T(8,128)(2,1)S(1)} collective-permute-done((bf16[384,768]{1,0:T(8,128)(2,1)S(1)}, bf16[384,768]{1,0:T(8,128)(2,1)S(1)}, u32[]{:S(2)}, u32[]{:S(2)}) %collective-permute-start.31) | collective-permute-done | bytes 589856 | tf_op jit(solution)/shard_map/ppermute | solution.py:26
  314.9 2.2 reshape.144
  317.2 2.5 pad.27
  319.6 3.2 reshape.145
  323.1 3.8 maximum_maximum_fusion
  332.1 6.8 %collective-permute-done.29 = bf16[64,768]{1,0:T(8,128)(2,1)S(1)} collective-permute-done((bf16[64,768]{1,0:T(8,128)(2,1)S(1)}, bf16[64,768]{1,0:T(8,128)(2,1)S(1)}, u32[]{:S(2)}, u32[]{:S(2)}) %collective-permute-start.29) | collective-permute-done | bytes 98336 | tf_op jit(solution)/shard_map/ppermute | solution.py:26
  349.3 6.2 %collective-permute-done.37 = bf16[192,768]{1,0:T(8,128)(2,1)S(1)} collective-permute-done((bf16[192,768]{1,0:T(8,128)(2,1)S(1)}, bf16[192,768]{1,0:T(8,128)(2,1)S(1)}, u32[]{:S(2)}, u32[]{:S(2)}) %collective-permute-start.37) | collective-permute-done | bytes 294944 | tf_op jit(solution)/shard_map/ppermute | solution.py:26
  355.6 5.3 collective-permute-done.39
  365.3 2.5 collective-permute-start.62
  367.8 12.5 %collective-permute-done.49 = bf16[96,768]{1,0:T(8,128)(2,1)S(1)} collective-permute-done((bf16[96,768]{1,0:T(8,128)(2,1)S(1)}, bf16[96,768]{1,0:T(8,128)(2,1)S(1)}, u32[]{:S(2)}, u32[]{:S(2)}) %collective-permute-start.49) | collective-permute-done | bytes 147488 | tf_op jit(solution)/shard_map/ppermute | solution.py:26
  380.5 3.0 collective-permute-start.57
  383.6 9.1 %collective-permute-done.50 = bf16[48,768]{1,0:T(8,128)(2,1)S(1)} collective-permute-done((bf16[48,768]{1,0:T(8,128)(2,1)S(1)}, bf16[48,768]{1,0:T(8,128)(2,1)S(1)}, u32[]{:S(2)}, u32[]{:S(2)}) %collective-permute-start.50) | collective-permute-done | bytes 73760 | tf_op jit(solution)/shard_map/ppermute | solution.py:26
  392.8 3.1 collective-permute-done.57
  401.0 3.5 collective-permute-done.58
  407.9 3.8 collective-permute-start.65
  411.7 7.2 %collective-permute-done.59 = bf16[96,3072]{1,0:T(8,128)(2,1)S(1)} collective-permute-done((bf16[96,3072]{1,0:T(8,128)(2,1)S(1)}, bf16[96,3072]{1,0:T(8,128)(2,1)S(1)}, u32[]{:S(2)}, u32[]{:S(2)}) %collective-permute-start.59) | collective-permute-done | bytes 589856 | tf_op jit(solution)/shard_map/ppermute | solution.py:26
  419.2 4.1 collective-permute-start.60
  423.4 2.5 collective-permute-done.65
  426.5 2.9 collective-permute-done.44
  431.6 23.3 %collective-permute-done.45 = bf16[112,768]{1,0:T(8,128)(2,1)S(1)} collective-permute-done((bf16[112,768]{1,0:T(8,128)(2,1)S(1)}, bf16[112,768]{1,0:T(8,128)(2,1)S(1)}, u32[]{:S(2)}, u32[]{:S(2)}) %collective-permute-start.45) | collective-permute-done | bytes 172064 | tf_op jit(solution)/shard_map/ppermute | solution.py:26
  455.1 4.5 collective-permute-done.53
  459.8 2.5 collective-permute-done.46
  468.3 7.8 %collective-permute-done.54 = bf16[384,768]{1,0:T(8,128)(2,1)S(1)} collective-permute-done((bf16[384,768]{1,0:T(8,128)(2,1)S(1)}, bf16[384,768]{1,0:T(8,128)(2,1)S(1)}, u32[]{:S(2)}, u32[]{:S(2)}) %collective-permute-start.54) | collective-permute-done | bytes 589856 | tf_op jit(solution)/shard_map/ppermute | solution.py:26
  476.6 11.6 %collective-permute-done.47 = bf16[448,768]{1,0:T(8,128)(2,1)S(1)} collective-permute-done((bf16[448,768]{1,0:T(8,128)(2,1)S(1)}, bf16[448,768]{1,0:T(8,128)(2,1)S(1)}, u32[]{:S(2)}, u32[]{:S(2)}) %collective-permute-start.47) | collective-permute-done | bytes 688160 | tf_op jit(solution)/shard_map/ppermute | solution.py:26
  488.9 5.5 %add_bitcast_fusion = f32[1,1024,768]{2,1,0:T(8,128)} fusion(f32[1024,768]{1,0:T(8,128)S(1)} %fusion.24, f32[1024,768]{1,0:T(8,128)S(1)} %copy-done.66, bf16[768,2304]{1,0:T(8,128)(2,1)S(1)} %copy-done.65, bf16[1024,768]{1,0:T(8,128)(2,1)S(1)} %get-tuple-element.94, bf16[1024,768]{1,0:T(8,128)(2,1)S(1)} %copy-done.23, bf16[1024,768]{1,0:T(8,128)(2,1)S(1)} %copy-done.12), kind=kOutput, calls=%fused_computation.11 | convolution fusion | flops 3639607296 | bytes 17694720 | tf_op jit(solution)/shard_map/dot_general | solution.py:1010
  498.7 9.5 %settle_qkv.1 = f32[768,2304]{1,0:T(8,128)} custom-call(s32[1]{0:T(128)} %bitcast.25.side_ref, bf16[896,768]{1,0:T(8,128)(2,1)} %copy-done.30, bf16[896,768]{1,0:T(8,128)(2,1)} %copy-done.41, bf16[768,768]{1,0:T(8,128)(2,1)} %copy-done.26, bf16[768,768]{1,0:T(8,128)(2,1)} %copy-done.31), custom_call_target="tpu_custom_call" | custom-call | tf_op jit(solution)/shard_map/settle_qkv/pallas_call | solution.py:679
  508.9 11.3 %settle.2 = f32[768,3072]{1,0:T(8,128)} custom-call(s32[1]{0:T(128)} %bitcast.25.side_ref, bf16[384,3072]{1,0:T(8,128)(2,1)} %maximum_select_fusion.mine_ref, bf16[384,3072]{1,0:T(8,128)(2,1)} %collective-permute-done.61.other_ref), custom_call_target="tpu_custom_call" | custom-call | tf_op jit(solution)/shard_map/settle/pallas_call | solution.py:640
  520.2 11.3 %settle.3 = f32[3072,768]{1,0:T(8,128)} custom-call(s32[1]{0:T(128)} %bitcast.25.side_ref, bf16[1536,768]{1,0:T(8,128)(2,1)} %maximum_select_fusion.1.mine_ref, bf16[1536,768]{1,0:T(8,128)(2,1)} %collective-permute-done.67.other_ref), custom_call_target="tpu_custom_call" | custom-call | tf_op jit(solution)/shard_map/settle/pallas_call | solution.py:640
  (436 shorter events, 145.3 us)
Async XLA Ops:
  7.1 6.0 %collective-permute-start.3 = (bf16[64,768]{1,0:T(8,128)(2,1)S(1)}, bf16[64,768]{1,0:T(8,128)(2,1)S(1)}, u32[]{:S(2)}, u32[]{:S(2)}) collective-permute-start(bf16[64,768]{1,0:T(8,128)(2,1)S(1)} %constant_dynamic-slice_fusion.29), channel_id=1, source_target_pairs={{0,2},{1,3},{2,0},{3,1},{4,6},{5,7},{6,4},{7,5},{8,10},{9,11},{10,... | collective-permute-start | bytes 294920 | tf_op jit(solution)/shard_map/ppermute | solution.py:26
  13.1 7.9 %collective-permute-start.4 = (bf16[64,768]{1,0:T(8,128)(2,1)S(1)}, bf16[64,768]{1,0:T(8,128)(2,1)S(1)}, u32[]{:S(2)}, u32[]{:S(2)}) collective-permute-start(bf16[64,768]{1,0:T(8,128)(2,1)S(1)} %add_convert_fusion.30), channel_id=1, source_target_pairs={{0,4},{1,5},{2,6},{3,7},{4,0},{5,1},{6,2},{7,3},{8,12},{9,13},{10,... | collective-permute-start | bytes 294920 | tf_op jit(solution)/shard_map/ppermute | solution.py:26
  21.1 10.5 %collective-permute-start.5 = (bf16[64,768]{1,0:T(8,128)(2,1)S(1)}, bf16[64,768]{1,0:T(8,128)(2,1)S(1)}, u32[]{:S(2)}, u32[]{:S(2)}) collective-permute-start(bf16[64,768]{1,0:T(8,128)(2,1)S(1)} %add_convert_fusion.29), channel_id=1, source_target_pairs={{0,8},{1,9},{2,10},{3,11},{4,12},{5,13},{6,14},{7,15},{8,0},{9,1},... | collective-permute-start | bytes 294920 | tf_op jit(solution)/shard_map/ppermute | solution.py:26
  23.7 13.7 %collective-permute-start.1 = (bf16[16,768]{1,0:T(8,128)(2,1)S(1)}, bf16[16,768]{1,0:T(8,128)(2,1)S(1)}, u32[]{:S(2)}, u32[]{:S(2)}) collective-permute-start(bf16[16,768]{1,0:T(8,128)(2,1)S(1)} %get-tuple-element.131), channel_id=1, source_target_pairs={{1,0},{2,1},{3,2},{4,3},{5,4},{6,5},{7,6},{8,7},{9,8},{10,9},{11,1... | collective-permute-start | bytes 73736 | tf_op jit(solution)/shard_map/ppermute | solution.py:119
  25.0 12.4 %collective-permute-start = (bf16[16,768]{1,0:T(8,128)(2,1)S(1)}, bf16[16,768]{1,0:T(8,128)(2,1)S(1)}, u32[]{:S(2)}, u32[]{:S(2)}) collective-permute-start(bf16[16,768]{1,0:T(8,128)(2,1)S(1)} %get-tuple-element.130), channel_id=1, source_target_pairs={{0,1},{1,2},{2,3},{3,4},{4,5},{5,6},{6,7},{7,8},{8,9},{9,10},{10,1... | collective-permute-start | bytes 73736 | tf_op jit(solution)/shard_map/ppermute | solution.py:117
  31.6 5.6 %collective-permute-start.6 = (bf16[64,768]{1,0:T(8,128)(2,1)S(1)}, bf16[64,768]{1,0:T(8,128)(2,1)S(1)}, u32[]{:S(2)}, u32[]{:S(2)}) collective-permute-start(bf16[64,768]{1,0:T(8,128)(2,1)S(1)} %add_convert_fusion.28), channel_id=1, source_target_pairs={{0,2},{1,3},{2,0},{3,1},{4,6},{5,7},{6,4},{7,5},{8,10},{9,11},{10,... | collective-permute-start | bytes 294920 | tf_op jit(solution)/shard_map/ppermute | solution.py:26
  58.0 8.0 %collective-permute-start.9 = (bf16[64,896]{1,0:T(8,128)(2,1)S(1)}, bf16[64,896]{1,0:T(8,128)(2,1)S(1)}, u32[]{:S(2)}, u32[]{:S(2)}) collective-permute-start(bf16[64,896]{1,0:T(8,128)(2,1)S(1)} %get-tuple-element.138), channel_id=1, source_target_pairs={{0,2},{1,3},{2,0},{3,1},{4,6},{5,7},{6,4},{7,5},{8,10},{9,11},{10,... | collective-permute-start | bytes 344072 | tf_op jit(solution)/shard_map/ppermute | solution.py:26
  69.8 6.0 %collective-permute-start.10 = (bf16[64,1088]{1,0:T(8,128)(2,1)S(1)}, bf16[64,1088]{1,0:T(8,128)(2,1)S(1)}, u32[]{:S(2)}, u32[]{:S(2)}) collective-permute-start(bf16[64,1088]{1,0:T(8,128)(2,1)S(1)} %pad_maximum_fusion.2), channel_id=1, source_target_pairs={{0,4},{1,5},{2,6},{3,7},{4,0},{5,1},{6,2},{7,3},{8,12},{9,13},{10,... | collective-permute-start | bytes 417800 | tf_op jit(solution)/shard_map/ppermute | solution.py:26
  79.6 9.9 %collective-permute-start.11 = (bf16[64,1280]{1,0:T(8,128)(2,1)S(1)}, bf16[64,1280]{1,0:T(8,128)(2,1)S(1)}, u32[]{:S(2)}, u32[]{:S(2)}) collective-permute-start(bf16[64,1280]{1,0:T(8,128)(2,1)S(1)} %pad_maximum_fusion.1), channel_id=1, source_target_pairs={{0,8},{1,9},{2,10},{3,11},{4,12},{5,13},{6,14},{7,15},{8,0},{9,1},... | collective-permute-start | bytes 491528 | tf_op jit(solution)/shard_map/ppermute | solution.py:26
  94.8 5.2 collective-permute-start.12
  101.1 2.9 collective-permute-start.13
  173.6 30.5 %collective-permute-start.16 = (bf16[128,768]{1,0:T(8,128)(2,1)S(1)}, bf16[128,768]{1,0:T(8,128)(2,1)S(1)}, u32[]{:S(2)}, u32[]{:S(2)}) collective-permute-start(bf16[128,768]{1,0:T(8,128)(2,1)S(1)} %constant_dynamic-slice_fusion.24), channel_id=1, source_target_pairs={{0,1},{1,0},{2,3},{3,2},{4,5},{5,4},{6,7},{7,6},{8,9},{9,8},{10,11... | collective-permute-start | bytes 589832 | tf_op jit(solution)/shard_map/ppermute | solution.py:26
  184.5 37.9 %collective-permute-start.20 = (bf16[1536,768]{1,0:T(8,128)(2,1)}, bf16[1536,768]{1,0:T(8,128)(2,1)}, u32[]{:S(2)}, u32[]{:S(2)}) collective-permute-start(bf16[1536,768]{1,0:T(8,128)(2,1)} %constant_dynamic-slice_fusion.22), channel_id=1, source_target_pairs={{0,1},{1,0},{2,3},{3,2},{4,5},{5,4},{6,7},{7,6},{8,9},{9,8},{10,11... | collective-permute-start | bytes 7077896 | tf_op jit(solution)/shard_map/ppermute | solution.py:26
  193.4 34.3 %collective-permute-start.21 = (bf16[384,3072]{1,0:T(8,128)(2,1)}, bf16[384,3072]{1,0:T(8,128)(2,1)}, u32[]{:S(2)}, u32[]{:S(2)}) collective-permute-start(bf16[384,3072]{1,0:T(8,128)(2,1)} %constant_dynamic-slice_fusion.21), channel_id=1, source_target_pairs={{0,1},{1,0},{2,3},{3,2},{4,5},{5,4},{6,7},{7,6},{8,9},{9,8},{10,11... | collective-permute-start | bytes 7077896 | tf_op jit(solution)/shard_map/ppermute | solution.py:26
  193.9 20.8 %collective-permute-start.15 = (bf16[16,768]{1,0:T(8,128)(2,1)}, bf16[16,768]{1,0:T(8,128)(2,1)S(1)}, u32[]{:S(2)}, u32[]{:S(2)}) collective-permute-start(bf16[16,768]{1,0:T(8,128)(2,1)} %get-tuple-element.133), channel_id=1, source_target_pairs={{1,0},{2,1},{3,2},{4,3},{5,4},{6,5},{7,6},{8,7},{9,8},{10,9},{11,1... | collective-permute-start | bytes 73736 | tf_op jit(solution)/shard_map/ppermute | solution.py:119
  195.2 19.5 %collective-permute-start.14 = (bf16[16,768]{1,0:T(8,128)(2,1)}, bf16[16,768]{1,0:T(8,128)(2,1)S(1)}, u32[]{:S(2)}, u32[]{:S(2)}) collective-permute-start(bf16[16,768]{1,0:T(8,128)(2,1)} %get-tuple-element.132), channel_id=1, source_target_pairs={{0,1},{1,2},{2,3},{3,4},{4,5},{5,6},{6,7},{7,8},{8,9},{9,10},{10,1... | collective-permute-start | bytes 73736 | tf_op jit(solution)/shard_map/ppermute | solution.py:117
  204.2 5.4 %collective-permute-start.17 = (bf16[64,768]{1,0:T(8,128)(2,1)S(1)}, bf16[64,768]{1,0:T(8,128)(2,1)S(1)}, u32[]{:S(2)}, u32[]{:S(2)}) collective-permute-start(bf16[64,768]{1,0:T(8,128)(2,1)S(1)} %constant_dynamic-slice_fusion.23), channel_id=1, source_target_pairs={{0,2},{1,3},{2,0},{3,1},{4,6},{5,7},{6,4},{7,5},{8,10},{9,11},{10,... | collective-permute-start | bytes 294920 | tf_op jit(solution)/shard_map/ppermute | solution.py:26
  209.7 4.9 collective-permute-start.18
  214.6 7.1 %collective-permute-start.19 = (bf16[64,768]{1,0:T(8,128)(2,1)S(1)}, bf16[64,768]{1,0:T(8,128)(2,1)S(1)}, u32[]{:S(2)}, u32[]{:S(2)}) collective-permute-start(bf16[64,768]{1,0:T(8,128)(2,1)S(1)} %add_convert_fusion.26), channel_id=1, source_target_pairs={{0,8},{1,9},{2,10},{3,11},{4,12},{5,13},{6,14},{7,15},{8,0},{9,1},... | collective-permute-start | bytes 294920 | tf_op jit(solution)/shard_map/ppermute | solution.py:26
  234.5 5.0 collective-permute-start.22
  237.5 53.8 %collective-permute-start.24 = (bf16[768,768]{1,0:T(8,128)(2,1)}, bf16[768,768]{1,0:T(8,128)(2,1)}, u32[]{:S(2)}, u32[]{:S(2)}) collective-permute-start(bf16[768,768]{1,0:T(8,128)(2,1)} %constant_dynamic-slice_fusion.20), channel_id=1, source_target_pairs={{0,16},{16,0},{1,17},{17,1},{2,18},{18,2},{3,19},{19,3},{4,20},{20... | collective-permute-start | bytes 3538952 | tf_op jit(solution)/shard_map/ppermute | solution.py:26
  240.5 2.7 collective-permute-start.23
  241.7 48.0 %collective-permute-start.25 = (bf16[192,3072]{1,0:T(8,128)(2,1)}, bf16[192,3072]{1,0:T(8,128)(2,1)}, u32[]{:S(2)}, u32[]{:S(2)}) collective-permute-start(bf16[192,3072]{1,0:T(8,128)(2,1)} %constant_dynamic-slice_fusion.19), channel_id=1, source_target_pairs={{0,16},{16,0},{1,17},{17,1},{2,18},{18,2},{3,19},{19,3},{4,20},{20... | collective-permute-start | bytes 3538952 | tf_op jit(solution)/shard_map/ppermute | solution.py:26
  283.0 16.1 %collective-permute-start.30 = (bf16[768,768]{1,0:T(8,128)(2,1)S(1)}, bf16[768,768]{1,0:T(8,128)(2,1)S(1)}, u32[]{:S(2)}, u32[]{:S(2)}) collective-permute-start(bf16[768,768]{1,0:T(8,128)(2,1)S(1)} %fusion.16), channel_id=1, source_target_pairs={{0,1},{1,0},{2,3},{3,2},{4,5},{5,4},{6,7},{7,6},{8,9},{9,8},{10,11... | collective-permute-start | bytes 3538952 | tf_op jit(solution)/shard_map/ppermute | solution.py:26
  283.6 4.8 collective-permute-start.27
  288.5 41.2 %collective-permute-start.28 = (bf16[64,768]{1,0:T(8,128)(2,1)S(1)}, bf16[64,768]{1,0:T(8,128)(2,1)}, u32[]{:S(2)}, u32[]{:S(2)}) collective-permute-start(bf16[64,768]{1,0:T(8,128)(2,1)S(1)} %add_convert_fusion.24), channel_id=1, source_target_pairs={{0,4},{1,5},{2,6},{3,7},{4,0},{5,1},{6,2},{7,3},{8,12},{9,13},{10,... | collective-permute-start | bytes 294920 | tf_op jit(solution)/shard_map/ppermute | solution.py:26
  294.3 44.6 %collective-permute-start.33 = (bf16[384,768]{1,0:T(8,128)(2,1)}, bf16[384,768]{1,0:T(8,128)(2,1)}, u32[]{:S(2)}, u32[]{:S(2)}) collective-permute-start(bf16[384,768]{1,0:T(8,128)(2,1)} %constant_dynamic-slice_fusion.12), channel_id=1, source_target_pairs={{0,4},{1,5},{2,6},{3,7},{4,0},{5,1},{6,2},{7,3},{8,12},{9,13},{10,... | collective-permute-start | bytes 1769480 | tf_op jit(solution)/shard_map/ppermute | solution.py:26
  296.2 44.3 %collective-permute-start.34 = (bf16[96,3072]{1,0:T(8,128)(2,1)}, bf16[96,3072]{1,0:T(8,128)(2,1)}, u32[]{:S(2)}, u32[]{:S(2)}) collective-permute-start(bf16[96,3072]{1,0:T(8,128)(2,1)} %constant_dynamic-slice_fusion.11), channel_id=1, source_target_pairs={{0,2},{1,3},{2,0},{3,1},{4,6},{5,7},{6,4},{7,5},{8,10},{9,11},{10,... | collective-permute-start | bytes 1769480 | tf_op jit(solution)/shard_map/ppermute | solution.py:26
  300.8 13.1 %collective-permute-start.31 = (bf16[384,768]{1,0:T(8,128)(2,1)S(1)}, bf16[384,768]{1,0:T(8,128)(2,1)S(1)}, u32[]{:S(2)}, u32[]{:S(2)}) collective-permute-start(bf16[384,768]{1,0:T(8,128)(2,1)S(1)} %constant_dynamic-slice_fusion.14), channel_id=1, source_target_pairs={{0,16},{16,0},{1,17},{17,1},{2,18},{18,2},{3,19},{19,3},{4,20},{20... | collective-permute-start | bytes 1769480 | tf_op jit(solution)/shard_map/ppermute | solution.py:26
  329.7 12.1 %collective-permute-start.32 = (bf16[896,768]{1,0:T(8,128)(2,1)}, bf16[896,768]{1,0:T(8,128)(2,1)}, u32[]{:S(2)}, u32[]{:S(2)}) collective-permute-start(bf16[896,768]{1,0:T(8,128)(2,1)} %constant_dynamic-slice_fusion.13), channel_id=1, source_target_pairs={{0,1},{1,0},{2,3},{3,2},{4,5},{5,4},{6,7},{7,6},{8,9},{9,8},{10,11... | collective-permute-start | bytes 4128776 | tf_op jit(solution)/shard_map/ppermute | solution.py:26
  330.7 8.2 %collective-permute-start.29 = (bf16[64,768]{1,0:T(8,128)(2,1)S(1)}, bf16[64,768]{1,0:T(8,128)(2,1)S(1)}, u32[]{:S(2)}, u32[]{:S(2)}) collective-permute-start(bf16[64,768]{1,0:T(8,128)(2,1)S(1)} %add_convert_fusion.23), channel_id=1, source_target_pairs={{0,8},{1,9},{2,10},{3,11},{4,12},{5,13},{6,14},{7,15},{8,0},{9,1},... | collective-permute-start | bytes 294920 | tf_op jit(solution)/shard_map/ppermute | solution.py:26
  343.6 5.6 %collective-permute-start.35 = (bf16[64,768]{1,0:T(8,128)(2,1)S(1)}, bf16[64,768]{1,0:T(8,128)(2,1)S(1)}, u32[]{:S(2)}, u32[]{:S(2)}) collective-permute-start(bf16[64,768]{1,0:T(8,128)(2,1)S(1)} %add_convert_fusion.22), channel_id=1, source_target_pairs={{0,2},{1,3},{2,0},{3,1},{4,6},{5,7},{6,4},{7,5},{8,10},{9,11},{10,... | collective-permute-start | bytes 294920 | tf_op jit(solution)/shard_map/ppermute | solution.py:26
  344.9 10.7 %collective-permute-start.37 = (bf16[192,768]{1,0:T(8,128)(2,1)S(1)}, bf16[192,768]{1,0:T(8,128)(2,1)S(1)}, u32[]{:S(2)}, u32[]{:S(2)}) collective-permute-start(bf16[192,768]{1,0:T(8,128)(2,1)S(1)} %constant_dynamic-slice_fusion.10), channel_id=1, source_target_pairs={{0,2},{1,3},{2,0},{3,1},{4,6},{5,7},{6,4},{7,5},{8,10},{9,11},{10,... | collective-permute-start | bytes 884744 | tf_op jit(solution)/shard_map/ppermute | solution.py:26
  345.8 16.5 %collective-permute-start.38 = (bf16[448,768]{1,0:T(8,128)(2,1)S(1)}, bf16[448,768]{1,0:T(8,128)(2,1)S(1)}, u32[]{:S(2)}, u32[]{:S(2)}) collective-permute-start(bf16[448,768]{1,0:T(8,128)(2,1)S(1)} %constant_dynamic-slice_fusion.9), channel_id=1, source_target_pairs={{0,16},{16,0},{1,17},{17,1},{2,18},{18,2},{3,19},{19,3},{4,20},{20... | collective-permute-start | bytes 2064392 | tf_op jit(solution)/shard_map/ppermute | solution.py:26
  347.4 13.5 %collective-permute-start.39 = (bf16[192,768]{1,0:T(8,128)(2,1)S(1)}, bf16[192,768]{1,0:T(8,128)(2,1)S(1)}, u32[]{:S(2)}, u32[]{:S(2)}) collective-permute-start(bf16[192,768]{1,0:T(8,128)(2,1)S(1)} %constant_dynamic-slice_fusion.8), channel_id=1, source_target_pairs={{0,2},{1,3},{2,0},{3,1},{4,6},{5,7},{6,4},{7,5},{8,10},{9,11},{10,... | collective-permute-start | bytes 884744 | tf_op jit(solution)/shard_map/ppermute | solution.py:26
  347.8 13.3 %collective-permute-start.40 = (bf16[48,3072]{1,0:T(8,128)(2,1)S(1)}, bf16[48,3072]{1,0:T(8,128)(2,1)S(1)}, u32[]{:S(2)}, u32[]{:S(2)}) collective-permute-start(bf16[48,3072]{1,0:T(8,128)(2,1)S(1)} %constant_dynamic-slice_fusion.7), channel_id=1, source_target_pairs={{0,4},{1,5},{2,6},{3,7},{4,0},{5,1},{6,2},{7,3},{8,12},{9,13},{10,... | collective-permute-start | bytes 884744 | tf_op jit(solution)/shard_map/ppermute | solution.py:26
  349.2 11.7 %collective-permute-start.36 = (bf16[128,768]{1,0:T(8,128)(2,1)S(1)}, bf16[128,768]{1,0:T(8,128)(2,1)S(1)}, u32[]{:S(2)}, u32[]{:S(2)}) collective-permute-start(bf16[128,768]{1,0:T(8,128)(2,1)S(1)} %maximum_select_fusion.21), channel_id=1, source_target_pairs={{0,1},{1,0},{2,3},{3,2},{4,5},{5,4},{6,7},{7,6},{8,9},{9,8},{10,11... | collective-permute-start | bytes 589832 | tf_op jit(solution)/shard_map/ppermute | solution.py:26
  362.6 37.9 %collective-permute-start.41 = (bf16[224,768]{1,0:T(8,128)(2,1)S(1)}, bf16[224,768]{1,0:T(8,128)(2,1)S(1)}, u32[]{:S(2)}, u32[]{:S(2)}) collective-permute-start(bf16[224,768]{1,0:T(8,128)(2,1)S(1)} %constant_dynamic-slice_fusion.6), channel_id=1, source_target_pairs={{0,4},{1,5},{2,6},{3,7},{4,0},{5,1},{6,2},{7,3},{8,12},{9,13},{10,... | collective-permute-start | bytes 1032200 | tf_op jit(solution)/shard_map/ppermute | solution.py:26
  362.7 17.6 %collective-permute-start.49 = (bf16[96,768]{1,0:T(8,128)(2,1)S(1)}, bf16[96,768]{1,0:T(8,128)(2,1)S(1)}, u32[]{:S(2)}, u32[]{:S(2)}) collective-permute-start(bf16[96,768]{1,0:T(8,128)(2,1)S(1)} %constant_dynamic-slice_fusion.3), channel_id=1, source_target_pairs={{0,4},{1,5},{2,6},{3,7},{4,0},{5,1},{6,2},{7,3},{8,12},{9,13},{10,... | collective-permute-start | bytes 442376 | tf_op jit(solution)/shard_map/ppermute | solution.py:26
  364.7 15.7 %collective-permute-start.56 = (bf16[24,3072]{1,0:T(8,128)(2,1)S(1)}, bf16[24,3072]{1,0:T(8,128)(2,1)S(1)}, u32[]{:S(2)}, u32[]{:S(2)}) collective-permute-start(bf16[24,3072]{1,0:T(8,128)(2,1)S(1)} %constant_dynamic-slice_fusion.1), channel_id=1, source_target_pairs={{0,8},{1,9},{2,10},{3,11},{4,12},{5,13},{6,14},{7,15},{8,0},{9,1},... | collective-permute-start | bytes 442376 | tf_op jit(solution)/shard_map/ppermute | solution.py:26
  365.3 18.1 %collective-permute-start.62 = (bf16[96,768]{1,0:T(8,128)(2,1)S(1)}, bf16[96,768]{1,0:T(8,128)(2,1)S(1)}, u32[]{:S(2)}, u32[]{:S(2)}) collective-permute-start(bf16[96,768]{1,0:T(8,128)(2,1)S(1)} %constant_dynamic-slice_fusion), channel_id=1, source_target_pairs={{0,8},{1,9},{2,10},{3,11},{4,12},{5,13},{6,14},{7,15},{8,0},{9,1},... | collective-permute-start | bytes 442376 | tf_op jit(solution)/shard_map/ppermute | solution.py:26
  380.3 12.4 %collective-permute-start.50 = (bf16[48,768]{1,0:T(8,128)(2,1)S(1)}, bf16[48,768]{1,0:T(8,128)(2,1)S(1)}, u32[]{:S(2)}, u32[]{:S(2)}) collective-permute-start(bf16[48,768]{1,0:T(8,128)(2,1)S(1)} %constant_dynamic-slice_fusion.2), channel_id=1, source_target_pairs={{0,8},{1,9},{2,10},{3,11},{4,12},{5,13},{6,14},{7,15},{8,0},{9,1},... | collective-permute-start | bytes 221192 | tf_op jit(solution)/shard_map/ppermute | solution.py:26
  380.5 15.4 %collective-permute-start.57 = (bf16[24,3072]{1,0:T(8,128)(2,1)S(1)}, bf16[24,3072]{1,0:T(8,128)(2,1)S(1)}, u32[]{:S(2)}, u32[]{:S(2)}) collective-permute-start(bf16[24,3072]{1,0:T(8,128)(2,1)S(1)} %add_convert_fusion.20), channel_id=1, source_target_pairs={{0,8},{1,9},{2,10},{3,11},{4,12},{5,13},{6,14},{7,15},{8,0},{9,1},... | collective-permute-start | bytes 442376 | tf_op jit(solution)/shard_map/ppermute | solution.py:26
  383.5 15.3 %collective-permute-start.63 = (bf16[96,768]{1,0:T(8,128)(2,1)S(1)}, bf16[96,768]{1,0:T(8,128)(2,1)S(1)}, u32[]{:S(2)}, u32[]{:S(2)}) collective-permute-start(bf16[96,768]{1,0:T(8,128)(2,1)S(1)} %add_convert_fusion.19), channel_id=1, source_target_pairs={{0,8},{1,9},{2,10},{3,11},{4,12},{5,13},{6,14},{7,15},{8,0},{9,1},... | collective-permute-start | bytes 442376 | tf_op jit(solution)/shard_map/ppermute | solution.py:26
  392.8 12.0 %collective-permute-start.51 = (bf16[48,768]{1,0:T(8,128)(2,1)S(1)}, bf16[48,768]{1,0:T(8,128)(2,1)S(1)}, u32[]{:S(2)}, u32[]{:S(2)}) collective-permute-start(bf16[48,768]{1,0:T(8,128)(2,1)S(1)} %add_convert_fusion.32), channel_id=1, source_target_pairs={{0,8},{1,9},{2,10},{3,11},{4,12},{5,13},{6,14},{7,15},{8,0},{9,1},... | collective-permute-start | bytes 221192 | tf_op jit(solution)/shard_map/ppermute | solution.py:26
  395.9 8.6 %collective-permute-start.58 = (bf16[48,3072]{1,0:T(8,128)(2,1)S(1)}, bf16[48,3072]{1,0:T(8,128)(2,1)S(1)}, u32[]{:S(2)}, u32[]{:S(2)}) collective-permute-start(bf16[48,3072]{1,0:T(8,128)(2,1)S(1)} %maximum_select_fusion.16), channel_id=1, source_target_pairs={{0,16},{16,0},{1,17},{17,1},{2,18},{18,2},{3,19},{19,3},{4,20},{20... | collective-permute-start | bytes 884744 | tf_op jit(solution)/shard_map/ppermute | solution.py:26
  398.8 8.8 %collective-permute-start.64 = (bf16[192,768]{1,0:T(8,128)(2,1)S(1)}, bf16[192,768]{1,0:T(8,128)(2,1)S(1)}, u32[]{:S(2)}, u32[]{:S(2)}) collective-permute-start(bf16[192,768]{1,0:T(8,128)(2,1)S(1)} %maximum_select_fusion.17), channel_id=1, source_target_pairs={{0,16},{16,0},{1,17},{17,1},{2,18},{18,2},{3,19},{19,3},{4,20},{20... | collective-permute-start | bytes 884744 | tf_op jit(solution)/shard_map/ppermute | solution.py:26
  400.6 6.2 %collective-permute-start.42 = (bf16[112,768]{1,0:T(8,128)(2,1)S(1)}, bf16[112,768]{1,0:T(8,128)(2,1)S(1)}, u32[]{:S(2)}, u32[]{:S(2)}) collective-permute-start(bf16[112,768]{1,0:T(8,128)(2,1)S(1)} %constant_dynamic-slice_fusion.5), channel_id=1, source_target_pairs={{0,2},{1,3},{2,0},{3,1},{4,6},{5,7},{6,4},{7,5},{8,10},{9,11},{10,... | collective-permute-start | bytes 516104 | tf_op jit(solution)/shard_map/ppermute | solution.py:26
  404.6 14.3 %collective-permute-start.59 = (bf16[96,3072]{1,0:T(8,128)(2,1)S(1)}, bf16[96,3072]{1,0:T(8,128)(2,1)S(1)}, u32[]{:S(2)}, u32[]{:S(2)}) collective-permute-start(bf16[96,3072]{1,0:T(8,128)(2,1)S(1)} %maximum_select_fusion.8), channel_id=1, source_target_pairs={{0,4},{1,5},{2,6},{3,7},{4,0},{5,1},{6,2},{7,3},{8,12},{9,13},{10,... | collective-permute-start | bytes 1769480 | tf_op jit(solution)/shard_map/ppermute | solution.py:26
  404.8 24.7 %collective-permute-start.52 = (bf16[96,768]{1,0:T(8,128)(2,1)S(1)}, bf16[96,768]{1,0:T(8,128)(2,1)S(1)}, u32[]{:S(2)}, u32[]{:S(2)}) collective-permute-start(bf16[96,768]{1,0:T(8,128)(2,1)S(1)} %maximum_select_fusion.23), channel_id=1, source_target_pairs={{0,4},{1,5},{2,6},{3,7},{4,0},{5,1},{6,2},{7,3},{8,12},{9,13},{10,... | collective-permute-start | bytes 442376 | tf_op jit(solution)/shard_map/ppermute | solution.py:26
  406.9 16.4 %collective-permute-start.43 = (bf16[56,768]{1,0:T(8,128)(2,1)S(1)}, bf16[56,768]{1,0:T(8,128)(2,1)S(1)}, u32[]{:S(2)}, u32[]{:S(2)}) collective-permute-start(bf16[56,768]{1,0:T(8,128)(2,1)S(1)} %constant_dynamic-slice_fusion.4), channel_id=1, source_target_pairs={{0,8},{1,9},{2,10},{3,11},{4,12},{5,13},{6,14},{7,15},{8,0},{9,1},... | collective-permute-start | bytes 258056 | tf_op jit(solution)/shard_map/ppermute | solution.py:26
  407.9 18.1 %collective-permute-start.65 = (bf16[384,768]{1,0:T(8,128)(2,1)S(1)}, bf16[384,768]{1,0:T(8,128)(2,1)S(1)}, u32[]{:S(2)}, u32[]{:S(2)}) collective-permute-start(bf16[384,768]{1,0:T(8,128)(2,1)S(1)} %maximum_select_fusion.9), channel_id=1, source_target_pairs={{0,2},{1,3},{2,0},{3,1},{4,6},{5,7},{6,4},{7,5},{8,10},{9,11},{10,... | collective-permute-start | bytes 1769480 | tf_op jit(solution)/shard_map/ppermute | solution.py:26
  419.2 43.7 %collective-permute-start.60 = (bf16[192,3072]{1,0:T(8,128)(2,1)S(1)}, bf16[192,3072]{1,0:T(8,128)(2,1)S(1)}, u32[]{:S(2)}, u32[]{:S(2)}) collective-permute-start(bf16[192,3072]{1,0:T(8,128)(2,1)S(1)} %maximum_select_fusion.4), channel_id=1, source_target_pairs={{0,2},{1,3},{2,0},{3,1},{4,6},{5,7},{6,4},{7,5},{8,10},{9,11},{10,... | collective-permute-start | bytes 3538952 | tf_op jit(solution)/shard_map/ppermute | solution.py:26
  423.3 6.0 %collective-permute-start.44 = (bf16[56,768]{1,0:T(8,128)(2,1)S(1)}, bf16[56,768]{1,0:T(8,128)(2,1)S(1)}, u32[]{:S(2)}, u32[]{:S(2)}) collective-permute-start(bf16[56,768]{1,0:T(8,128)(2,1)S(1)} %add_convert_fusion.31), channel_id=1, source_target_pairs={{0,8},{1,9},{2,10},{3,11},{4,12},{5,13},{6,14},{7,15},{8,0},{9,1},... | collective-permute-start | bytes 258056 | tf_op jit(solution)/shard_map/ppermute | solution.py:26
  426.4 38.3 %collective-permute-start.66 = (bf16[768,768]{1,0:T(8,128)(2,1)S(1)}, bf16[768,768]{1,0:T(8,128)(2,1)S(1)}, u32[]{:S(2)}, u32[]{:S(2)}) collective-permute-start(bf16[768,768]{1,0:T(8,128)(2,1)S(1)} %maximum_select_fusion.5), channel_id=1, source_target_pairs={{0,4},{1,5},{2,6},{3,7},{4,0},{5,1},{6,2},{7,3},{8,12},{9,13},{10,... | collective-permute-start | bytes 3538952 | tf_op jit(solution)/shard_map/ppermute | solution.py:26
  429.4 25.5 %collective-permute-start.45 = (bf16[112,768]{1,0:T(8,128)(2,1)S(1)}, bf16[112,768]{1,0:T(8,128)(2,1)S(1)}, u32[]{:S(2)}, u32[]{:S(2)}) collective-permute-start(bf16[112,768]{1,0:T(8,128)(2,1)S(1)} %maximum_select_fusion.22), channel_id=1, source_target_pairs={{0,2},{1,3},{2,0},{3,1},{4,6},{5,7},{6,4},{7,5},{8,10},{9,11},{10,... | collective-permute-start | bytes 516104 | tf_op jit(solution)/shard_map/ppermute | solution.py:26
  429.5 30.0 %collective-permute-start.53 = (bf16[192,768]{1,0:T(8,128)(2,1)S(1)}, bf16[192,768]{1,0:T(8,128)(2,1)S(1)}, u32[]{:S(2)}, u32[]{:S(2)}) collective-permute-start(bf16[192,768]{1,0:T(8,128)(2,1)S(1)} %maximum_select_fusion.15), channel_id=1, source_target_pairs={{0,2},{1,3},{2,0},{3,1},{4,6},{5,7},{6,4},{7,5},{8,10},{9,11},{10,... | collective-permute-start | bytes 884744 | tf_op jit(solution)/shard_map/ppermute | solution.py:26
  455.0 7.3 %collective-permute-start.46 = (bf16[224,768]{1,0:T(8,128)(2,1)S(1)}, bf16[224,768]{1,0:T(8,128)(2,1)S(1)}, u32[]{:S(2)}, u32[]{:S(2)}) collective-permute-start(bf16[224,768]{1,0:T(8,128)(2,1)S(1)} %maximum_select_fusion.14), channel_id=1, source_target_pairs={{0,4},{1,5},{2,6},{3,7},{4,0},{5,1},{6,2},{7,3},{8,12},{9,13},{10,... | collective-permute-start | bytes 1032200 | tf_op jit(solution)/shard_map/ppermute | solution.py:26
  459.7 16.3 %collective-permute-start.54 = (bf16[384,768]{1,0:T(8,128)(2,1)S(1)}, bf16[384,768]{1,0:T(8,128)(2,1)S(1)}, u32[]{:S(2)}, u32[]{:S(2)}) collective-permute-start(bf16[384,768]{1,0:T(8,128)(2,1)S(1)} %maximum_select_fusion.7), channel_id=1, source_target_pairs={{0,16},{16,0},{1,17},{17,1},{2,18},{18,2},{3,19},{19,3},{4,20},{20... | collective-permute-start | bytes 1769480 | tf_op jit(solution)/shard_map/ppermute | solution.py:26
  462.5 25.6 %collective-permute-start.47 = (bf16[448,768]{1,0:T(8,128)(2,1)S(1)}, bf16[448,768]{1,0:T(8,128)(2,1)S(1)}, u32[]{:S(2)}, u32[]{:S(2)}) collective-permute-start(bf16[448,768]{1,0:T(8,128)(2,1)S(1)} %maximum_select_fusion.6), channel_id=1, source_target_pairs={{0,16},{16,0},{1,17},{17,1},{2,18},{18,2},{3,19},{19,3},{4,20},{20... | collective-permute-start | bytes 2064392 | tf_op jit(solution)/shard_map/ppermute | solution.py:26
  464.7 44.2 %collective-permute-start.61 = (bf16[384,3072]{1,0:T(8,128)(2,1)}, bf16[384,3072]{1,0:T(8,128)(2,1)}, u32[]{:S(2)}, u32[]{:S(2)}) collective-permute-start(bf16[384,3072]{1,0:T(8,128)(2,1)} %maximum_select_fusion.mine_ref), channel_id=1, source_target_pairs={{0,1},{1,0},{2,3},{3,2},{4,5},{5,4},{6,7},{7,6},{8,9},{9,8},{10,11... | collective-permute-start | bytes 7077896 | tf_op jit(solution)/shard_map/ppermute | solution.py:26
  466.8 53.3 %collective-permute-start.67 = (bf16[1536,768]{1,0:T(8,128)(2,1)}, bf16[1536,768]{1,0:T(8,128)(2,1)}, u32[]{:S(2)}, u32[]{:S(2)}) collective-permute-start(bf16[1536,768]{1,0:T(8,128)(2,1)} %maximum_select_fusion.1.mine_ref), channel_id=1, source_target_pairs={{0,1},{1,0},{2,3},{3,2},{4,5},{5,4},{6,7},{7,6},{8,9},{9,8},{10,11... | collective-permute-start | bytes 7077896 | tf_op jit(solution)/shard_map/ppermute | solution.py:26
  476.5 17.9 %collective-permute-start.55 = (bf16[768,768]{1,0:T(8,128)(2,1)S(1)}, bf16[768,768]{1,0:T(8,128)(2,1)S(1)}, u32[]{:S(2)}, u32[]{:S(2)}) collective-permute-start(bf16[768,768]{1,0:T(8,128)(2,1)S(1)} %maximum_select_fusion.3.early_ref), channel_id=1, source_target_pairs={{0,1},{1,0},{2,3},{3,2},{4,5},{5,4},{6,7},{7,6},{8,9},{9,8},{10,11... | collective-permute-start | bytes 3538952 | tf_op jit(solution)/shard_map/ppermute | solution.py:26
  488.8 7.5 %collective-permute-start.48 = (bf16[896,768]{1,0:T(8,128)(2,1)S(1)}, bf16[896,768]{1,0:T(8,128)(2,1)S(1)}, u32[]{:S(2)}, u32[]{:S(2)}) collective-permute-start(bf16[896,768]{1,0:T(8,128)(2,1)S(1)} %maximum_select_fusion.2.late_ref), channel_id=1, source_target_pairs={{0,1},{1,0},{2,3},{3,2},{4,5},{5,4},{6,7},{7,6},{8,9},{9,8},{10,11... | collective-permute-start | bytes 4128776 | tf_op jit(solution)/shard_map/ppermute | solution.py:26
  (79 other events, 799.2 us)

commit v7 on v6

--- a/solution.py
+++ b/solution.py
@@ -871,145 +871,154 @@
     )(bounds, qkv, grad_mixed, probs, mark_k, mix)
     grad_w_down = lax.dot_general(active, grad_low_two, rows_in, preferred_element_type=F32)
     grad_w_up = lax.dot_general(hidden_low, grad_upper, rows_in, preferred_element_type=F32)
-    down = begin(grad_w_down.astype(BF), ("row", "far", "near"), ("far", "near", "row"))
-    up = begin(grad_w_up.astype(BF), ("row", "near", "far"), ("near", "far", "row"))
-    grad_mix = seq_quarter(grad_mix.astype(BF), add_join)
-    down, up = advance(down, 1), advance(up, 1)
-    grad_mix, (down, up) = tied(grad_mix, [down, up])
-    down, up = advance(down, 1), advance(up, 1)
-    grad_w_out = lax.dot_general(mixed, grad_low_one, rows_in, preferred_element_type=F32)
-
-    grad_ext = extended(grad_mixed, radius, window_rows)
-    grad_conv, products = pl.pallas_call(
-        lambda *refs: conv_back_kernel(docs, *refs),
-        grid=(blocks,),
-        in_specs=[
-            smem, fixed(window_rows, width), fixed(window_rows, width), fixed(heads, GROUP)
-        ],
-        out_specs=(tok_spec, fixed(heads * SUB, GROUP)),
-        out_shape=(shaped((tok_count, width), F32), shaped((heads * SUB, GROUP), F32)),
-        scratch_shapes=[pltpu.VMEM((heads * SUB, GROUP), BF)],
-        compiler_params=params,
-        name="conv_back",
-    )(bounds, grad_ext, value_ext, jnp.pad(conv_taps[:, ::-1], ((0, 0), (0, GROUP - tap_count))))
-    grad_avg = pl.pallas_call(
-        mix_back_kernel, out_shape=shaped((LAND, width + 128), BF), name="mix_back"
-    )(inverse, stats, grad_mix)
-    grad_avg = seq_whole(grad_avg)
-    lane_spec = pl.BlockSpec((mark_count, 128), lambda i: (0, width // 128))
-    grad_keys, grad_values, grad_mq = pl.pallas_call(
-        lambda *refs: landmark_back_kernel(docs, scale, *refs),
-        grid=(blocks,),
-        in_specs=[
-            smem, part(1), part(2), tok_spec, mark_spec, mark_spec, lane_spec, lane_spec
-        ],
-        out_specs=(tok_spec, tok_spec, mark_spec),
-        out_shape=(
-            shaped((tok_count, width), BF), shaped((tok_count, width), BF),
-            shaped((mark_count, width), F32),
-        ),
-        scratch_shapes=[pltpu.VMEM((BLOCK, width), F32), pltpu.VMEM((BLOCK, width), F32)],
-        compiler_params=params,
-        name="landmark_back",
-    )(bounds, qkv, qkv, grad_conv, mark_q, grad_avg, mix, grad_avg)
-
-    grad_keys, (down, up) = tied(grad_keys, [down, up])
-    down, up = advance(down, 1), advance(up, 1)
-    grad_mix, grad_values = lax.optimization_barrier((grad_mix, grad_values))
-    grad_mq_small, grad_mk_small = pl.pallas_call(
-        lambda *refs: pinv_back_kernel(scale, *refs),
-        out_shape=(shaped(square, F32), shaped(square, F32)),
-        name="pinv_back",
-    )(own_q, own_k, kernel, saved, own_heads(grad_mix), own_heads(stats[:, :width]))
-
-    def placed(array):
-        array = array.transpose(1, 0, 2).reshape(LAND, own_count * size)
-        array = lax.dynamic_update_slice_in_dim(
-            jnp.zeros((LAND, width + spare), F32), array, own_at, 1
-        )[:, :width]
-        return lax.dynamic_update_slice_in_dim(
-            jnp.zeros((mark_count, width), F32), array, own_doc * LAND, 0
+    grad_mix, grad_w_down, grad_w_up = lax.optimization_barrier(
+        (grad_mix.astype(BF), grad_w_down.astype(BF), grad_w_up.astype(BF))
+    )
+    sum_w_down, sum_w_up = lax.psum((grad_w_down, grad_w_up), ("row", "seq"))
+
+    def remaining(grad_mix, grad_mk, stats, mix):
+        grad_mix = seq_quarter(grad_mix.astype(BF), add_join)
+        grad_w_out = lax.dot_general(mixed, grad_low_one, rows_in, preferred_element_type=F32)
+
+        grad_ext = extended(grad_mixed, radius, window_rows)
+        grad_conv, products = pl.pallas_call(
+            lambda *refs: conv_back_kernel(docs, *refs),
+            grid=(blocks,),
+            in_specs=[
+                smem, fixed(window_rows, width), fixed(window_rows, width), fixed(heads, GROUP)
+            ],
+            out_specs=(tok_spec, fixed(heads * SUB, GROUP)),
+            out_shape=(shaped((tok_count, width), F32), shaped((heads * SUB, GROUP), F32)),
+            scratch_shapes=[pltpu.VMEM((heads * SUB, GROUP), BF)],
+            compiler_params=params,
+            name="conv_back",
+        )(bounds, grad_ext, value_ext, jnp.pad(conv_taps[:, ::-1], ((0, 0), (0, GROUP - tap_count))))
+        grad_avg = pl.pallas_call(
+            mix_back_kernel, out_shape=shaped((LAND, width + 128), BF), name="mix_back"
+        )(inverse, stats, grad_mix)
+        grad_avg = seq_whole(grad_avg)
+        lane_spec = pl.BlockSpec((mark_count, 128), lambda i: (0, width // 128))
+        grad_keys, grad_values, grad_mq = pl.pallas_call(
+            lambda *refs: landmark_back_kernel(docs, scale, *refs),
+            grid=(blocks,),
+            in_specs=[
+                smem, part(1), part(2), tok_spec, mark_spec, mark_spec, lane_spec, lane_spec
+            ],
+            out_specs=(tok_spec, tok_spec, mark_spec),
+            out_shape=(
+                shaped((tok_count, width), BF), shaped((tok_count, width), BF),
+                shaped((mark_count, width), F32),
+            ),
+            scratch_shapes=[pltpu.VMEM((BLOCK, width), F32), pltpu.VMEM((BLOCK, width), F32)],
+            compiler_params=params,
+            name="landmark_back",
+        )(bounds, qkv, qkv, grad_conv, mark_q, grad_avg, mix, grad_avg)
+
+        grad_mix, grad_values = lax.optimization_barrier((grad_mix, grad_values))
+        grad_mq_small, grad_mk_small = pl.pallas_call(
+            lambda *refs: pinv_back_kernel(scale, *refs),
+            out_shape=(shaped(square, F32), shaped(square, F32)),
+            name="pinv_back",
+        )(own_q, own_k, kernel, saved, own_heads(grad_mix), own_heads(stats[:, :width]))
+
+        def placed(array):
+            array = array.transpose(1, 0, 2).reshape(LAND, own_count * size)
+            array = lax.dynamic_update_slice_in_dim(
+                jnp.zeros((LAND, width + spare), F32), array, own_at, 1
+            )[:, :width]
+            return lax.dynamic_update_slice_in_dim(
+                jnp.zeros((mark_count, width), F32), array, own_doc * LAND, 0
+            )
+
+        grad_mq = grad_mq + placed(grad_mq_small)
+        grad_mk = grad_mk + placed(grad_mk_small)
+        grad_marks = jnp.concatenate([grad_mq, grad_mk], axis=1).astype(BF)
+        mark_back = lax.dot_general(
+            grad_marks, w_qkv[:, : 2 * width], cols_in, preferred_element_type=F32
+        ) / counts
+        mark_back = mark_back.astype(BF)
+
+        grad_bias_q = jnp.sum(grad_queries.astype(F32), axis=0) + jnp.sum(grad_mq, axis=0)
+        grad_bias_v = jnp.sum(grad_values.astype(F32), axis=0)
+        grad_projected = jnp.concatenate([grad_queries, grad_keys, grad_values], axis=1)
+
+        def weight_grad(grads):
+            return lax.dot_general(tokens, grads, rows_in, preferred_element_type=F32)
+
+        early = jnp.concatenate([grad_w_out.astype(BF), weight_grad(grad_values).astype(BF)], 0)
+        early = begin(early, ("row", "near", "far"), ("row", "near", "far"))
+        early = advance(early, 1)
+        grad_marks, (early,) = tied(grad_marks, [early])
+        early = advance(early, 1)
+        mark_grad_q = lax.dot_general(
+            mean_in, grad_marks[:, :width], rows_in, preferred_element_type=F32
         )
-
-    grad_mq = grad_mq + placed(grad_mq_small)
-    grad_mk = grad_mk + placed(grad_mk_small)
-    grad_marks = jnp.concatenate([grad_mq, grad_mk], axis=1).astype(BF)
-    mark_back = lax.dot_general(
-        grad_marks, w_qkv[:, : 2 * width], cols_in, preferred_element_type=F32
-    ) / counts
-    mark_back = mark_back.astype(BF)
-
-    grad_bias_q = jnp.sum(grad_queries.astype(F32), axis=0) + jnp.sum(grad_mq, axis=0)
-    grad_bias_v = jnp.sum(grad_values.astype(F32), axis=0)
-    grad_projected = jnp.concatenate([grad_queries, grad_keys, grad_values], axis=1)
-
-    def weight_grad(grads):
-        return lax.dot_general(tokens, grads, rows_in, preferred_element_type=F32)
-
-    early = jnp.concatenate([grad_w_out.astype(BF), weight_grad(grad_values).astype(BF)], 0)
-    early = begin(early, ("row", "near", "far"), ("row", "near", "far"))
-    early = advance(early, 1)
-    grad_marks, (early,) = tied(grad_marks, [early])
-    early = advance(early, 1)
-    mark_grad_q = lax.dot_general(
-        mean_in, grad_marks[:, :width], rows_in, preferred_element_type=F32
+        mark_grad_k = lax.dot_general(
+            mean_in, grad_marks[:, width:], rows_in, preferred_element_type=F32
+        )
+        products, (early,) = tied(products, [early])
+        reach = SUB + tap_count - 1
+        products = products.reshape(heads, SUB, GROUP)[:, :, :reach].reshape(heads, SUB * reach)
+        products = jnp.pad(products, ((0, 0), (0, SUB))).reshape(heads, SUB, reach + 1)
+        grad_conv_taps = jnp.sum(products, axis=1)[:, :tap_count]
+        others = jnp.concatenate(
+            [
+                sum_up[0].reshape(hidden // width, width),
+                grad_bias_q[None],
+                grad_bias_v[None],
+                jnp.pad(grad_conv_taps.reshape(1, -1), ((0, 0), (0, width - heads * tap_count))),
+                jnp.zeros((4 - hidden // width + 1, width), F32),
+            ],
+            0,
+        )
+        spare_rows = width // 6
+        small = jnp.concatenate([sums, others], 0).astype(BF)
+        small = jnp.pad(small, ((0, spare_rows - small.shape[0]), (0, 0)))
+        small = lax.optimization_barrier(small)
+        late = jnp.concatenate(
+            [
+                (weight_grad(grad_queries) + mark_grad_q).astype(BF),
+                small,
+                (weight_grad(grad_keys) + mark_grad_k).astype(BF),
+                jnp.zeros((spare_rows, width), BF),
+            ],
+            0,
+        )
+        late = begin(late, ("row", "far", "near"), ("row", "far", "near"))
+        late = advance(late, 1)
+        mark_back = seq_quarter(mark_back, add_join)
+        mark_back, (early, late) = tied(mark_back, [early, late])
+        early, late = advance(early, 1), advance(late, 1)
+        mark_back = seq_whole(mark_back)
+        mark_back, (early, late) = tied(mark_back, [early, late])
+        early, early_other = last_swap(early)[:2]
+        late, late_other = last_swap(late)[:2]
+        sum_w_qkv = settle_qkv(late, late_other, early, early_other, width)
+        first_core = me % 2 == 0
+        sum_w_out = jnp.where(first_core, early, early_other).astype(F32)
+        flat = jnp.where(first_core, late[width:], late_other[width:])[:16].astype(F32)
+        grad_input = (
+            grad_one
+            + lax.dot_general(grad_projected, w_qkv, cols_in, preferred_element_type=F32)
+            + lax.dot_general(onehot, mark_back, rows_in, preferred_element_type=F32)
+        )
+        return grad_input, sum_w_qkv, sum_w_out, flat
+
+    def nothing(*unused):
+        return (
+            jnp.zeros((tok_count, width), F32), jnp.zeros((width, 3 * width), F32),
+            jnp.zeros((width, width), F32), jnp.zeros((16, width), F32),
+        )
+
+    grad_input, sum_w_qkv, sum_w_out, flat = lax.cond(
+        lengths[0] > 0, remaining, nothing, grad_mix, grad_mk, stats, mix
     )
-    mark_grad_k = lax.dot_general(
-        mean_in, grad_marks[:, width:], rows_in, preferred_element_type=F32
-    )
-    products, (early,) = tied(products, [early])
-    reach = SUB + tap_count - 1
-    products = products.reshape(heads, SUB, GROUP)[:, :, :reach].reshape(heads, SUB * reach)
-    products = jnp.pad(products, ((0, 0), (0, SUB))).reshape(heads, SUB, reach + 1)
-    grad_conv_taps = jnp.sum(products, axis=1)[:, :tap_count]
-    others = jnp.concatenate(
-        [
-            sum_up[0].reshape(hidden // width, width),
-            grad_bias_q[None],
-            grad_bias_v[None],
-            jnp.pad(grad_conv_taps.reshape(1, -1), ((0, 0), (0, width - heads * tap_count))),
-            jnp.zeros((4 - hidden // width + 1, width), F32),
-        ],
-        0,
-    )
-    spare_rows = width // 6
-    small = jnp.concatenate([sums, others], 0).astype(BF)
-    small = jnp.pad(small, ((0, spare_rows - small.shape[0]), (0, 0)))
-    small = lax.optimization_barrier(small)
-    late = jnp.concatenate(
-        [
-            (weight_grad(grad_queries) + mark_grad_q).astype(BF),
-            small,
-            (weight_grad(grad_keys) + mark_grad_k).astype(BF),
-            jnp.zeros((spare_rows, width), BF),
-        ],
-        0,
-    )
-    late = begin(late, ("row", "far", "near"), ("row", "far", "near"))
-    late = advance(late, 1)
-    mark_back = seq_quarter(mark_back, add_join)
-    mark_back, (early, late, down, up) = tied(mark_back, [early, late, down, up])
-    early, late = advance(early, 1), advance(late, 1)
-    down, up = advance(down, 1), advance(up, 1)
-    mark_back = seq_whole(mark_back)
-    mark_back, (early, late, down, up) = tied(mark_back, [early, late, down, up])
-    early, early_other = last_swap(early)[:2]
-    late, late_other = last_swap(late)[:2]
-    sum_w_down, sum_w_up = settle(down), settle(up)
-    sum_w_qkv = settle_qkv(late, late_other, early, early_other, width)
-    first_core = me % 2 == 0
-    sum_w_out = jnp.where(first_core, early, early_other).astype(F32)
-    flat = jnp.where(first_core, late[width:], late_other[width:])[:16].astype(F32)
+    sum_w_down, sum_w_up = sum_w_down.astype(F32), sum_w_up.astype(F32)
     at = sums.shape[0] + hidden // width
     pieces = [
         flat[at], flat[at + 1], flat[at + 2, : heads * tap_count], flat[5], flat[3], flat[4],
         flat[sums.shape[0] : at].reshape(hidden), flat[2], flat[0], flat[1],
     ]
-    grad_input = (
-        grad_one
-        + lax.dot_general(grad_projected, w_qkv, cols_in, preferred_element_type=F32)
-        + lax.dot_general(onehot, mark_back, rows_in, preferred_element_type=F32)
-    )
     return (
         result[None], grad_input[None], sum_w_qkv, pieces[0], pieces[1],
         pieces[2].reshape(heads, tap_count), sum_w_out, pieces[3], pieces[4], pieces[5],

time: 537 us -> 506 us (0.942)
  starting transfers between devices: 62.5 us -> 31.5 us
  local copies, waits for them, and re-layouts: 64.1 us -> 46.3 us
  Pallas kernels: 143 us -> 126 us
  other arithmetic: 52.5 us -> 67 us
  between operations: 3.17 us -> 15.1 us
  matrix products: 43.9 us -> 50.8 us
    ppermute x64 -> x44, starting transfers between devices: 53.5 us -> 26.1 us  [swap(): return lax.ppermute(array, axis, [(i, i ^ bit) for i in range(count)])]
    unnamed x150 -> x64, local copies, waits for them, and re-layouts: 23.8 us -> 2.65 us
    pallas_call x6 -> x4, Pallas kernels: 49.6 us -> 29 us  [the longest x1 11 us: remaining(): pl.pallas_call(lambda *refs: landmark_back_kernel(docs, scale, *refs), gr...]
    convert_element_type x3 -> x6, other arithmetic: 1.72 us -> 15.4 us  [the longest x2 12 us: per_device(): sum_w_down, sum_w_up = (sum_w_down.astype(F32), sum_w_up.astype(F32))]
    convert_element_type x20 -> x10, other arithmetic: 21.7 us -> 10.4 us  [advance(): held = held.astype(BF)]
    dynamic_slice x19 -> x9, local copies, waits for them, and re-layouts: 9.9 us -> 1.85 us  [advance(): other = lax.dynamic_slice_in_dim(held, (1 - side) * half, half, 0)]
    cond x0 -> x76, local copies, waits for them, and re-layouts: none -> 5.86 us
    ppermute x64 -> x44, waiting for transfers between devices: 163 us -> 161 us  [swap(): return lax.ppermute(array, axis, [(i, i ^ bit) for i in range(count)])]
  transfers between devices with their start and end apart: 68 -> 49, of which waited for: 32 -> 34; matrix products, arithmetic and copies ran while one was open for 21% -> 23% of each run, Pallas kernels for 10% -> 9%
where the time goes in v7:
time: 506 us; the launch traced here: 499 us
  waiting for transfers between devices  161 us (32%)
  Pallas kernels  126 us (25%)
  other arithmetic  67 us (13%)
  matrix products  50.8 us (10%)
  local copies, waits for them, and re-layouts  46.3 us (9%)
  starting transfers between devices  31.5 us (6%)
  between operations  15.1 us (3%)
    ppermute x44, waiting for transfers between devices, swap(): return lax.ppermute(array, axis, [(i, i ^ bit) for i in range(count)])  161 us
    pallas_call x1, Pallas kernels, per_device(): pl.pallas_call(ffn_kernel, grid=(tok_count // FFN_BLOCK,), in_specs=[ffn_...  40.3 us
    ppermute x44, starting transfers between devices, swap(): return lax.ppermute(array, axis, [(i, i ^ bit) for i in range(count)])  26.1 us
    pallas_call x1, Pallas kernels, per_device(): pl.pallas_call(lambda *refs: token_kernel(docs, scale, *refs), grid=(bloc...  12.2 us
    convert_element_type x2, other arithmetic, per_device(): sum_w_down, sum_w_up = (sum_w_down.astype(F32), sum_w_up.astype(F32))  12 us
    pallas_call x1, Pallas kernels, per_device(): pl.pallas_call(lambda *refs: token_back_kernel(docs, scale, *refs), grid=...  11.3 us
    pallas_call x1, Pallas kernels, remaining(): pl.pallas_call(lambda *refs: landmark_back_kernel(docs, scale, *refs), gr...  11 us
    select_n x16, other arithmetic, paired(): jnp.where(side == 0, jnp.concatenate([array, other], dim), jnp.concatenat...  10.5 us
  transfers between devices with their start and end apart: 49, of which 34 were waited for; matrix products, arithmetic and copies ran while one was open for 23% of the time, Pallas kernels for 9%

profile of v7, /device:TPU:0, one launch (start us, length us, event | category | flops | bytes accessed | tf_op | source)
XLA Modules:
  0.0 499.1 jit_solution(12364035720312570959)
XLA Ops:
  10.9 2.2 fusion.27
  14.8 3.0 collective-permute-start.37
  17.7 3.1 collective-permute-done.37
  22.7 6.0 %add_convert_fusion.20.refs_2_.refs_3_.refs_1_ = bf16[1024,2304]{1,0:T(8,128)(2,1)S(1)} fusion(bf16[768,2304]{1,0:T(8,128)(2,1)} %param.21, f32[2304]{0:T(1024)S(1)} %pad_maximum_fusion.4, bf16[1,1024,768]{2,1,0:T(8,128)(2,1)S(1)} %copy-done.29), kind=kOutput, calls=%fused_computation.86 | convolution fusion | flops 3628597248 | bytes 9839616 | tf_op jit(solution)/shard_map/dot_general | solution.py:742
  28.8 2.7 collective-permute-start.39
  35.6 3.2 collective-permute-start.40
  38.8 3.3 collective-permute-done.40
  43.9 2.6 fusion.25
  46.7 8.2 %landmark.1 = bf16[256,896]{1,0:T(8,128)(2,1)S(1)} custom-call(s32[8]{0:T(128)S(1)} %add_subtract_fusion.refs_0_, bf16[256,768]{1,0:T(8,128)(2,1)S(1)} %fusion.29.refs_1_, bf16[1024,2304]{1,0:T(8,128)(2,1)S(1)} %bitcast.67, bf16[1024,2304]{1,0:T(8,128)(2,1)S(1)} %bitcast.67), custom_call_target="tpu_custom_call" | custom-call | tf_op jit(solution)/shard_map/landmark/pallas_call | solution.py:749
  57.7 2.6 join.4
  62.5 6.0 %pinv.1 = (f32[3,64,64]{2,1,0:T(8,128)}, f32[3,64,64]{2,1,0:T(8,128)}, f32[72,64,64]{2,1,0:T(8,128)}) custom-call(f32[3,64,64]{2,1,0:T(8,128)S(1)} %bitcast.75, f32[3,64,64]{2,1,0:T(8,128)S(1)} %bitcast.73), custom_call_target="tpu_custom_call" | custom-call | tf_op jit(solution)/shard_map/pinv/pallas_call | solution.py:782
  70.4 2.2 join.5.a_ref
  73.5 5.9 %collective-permute-done.44 = bf16[64,1088]{1,0:T(8,128)(2,1)S(1)} collective-permute-done((bf16[64,1088]{1,0:T(8,128)(2,1)S(1)}, bf16[64,1088]{1,0:T(8,128)(2,1)S(1)}, u32[]{:S(2)}, u32[]{:S(2)}) %collective-permute-start.44) | collective-permute-done | bytes 139296 | tf_op jit(solution)/shard_map/ppermute | solution.py:26
  80.1 2.3 join.6.a_ref
  83.5 9.8 %collective-permute-done.45 = bf16[64,1280]{1,0:T(8,128)(2,1)S(1)} collective-permute-done((bf16[64,1280]{1,0:T(8,128)(2,1)S(1)}, bf16[64,1280]{1,0:T(8,128)(2,1)S(1)}, u32[]{:S(2)}, u32[]{:S(2)}) %collective-permute-start.45) | collective-permute-done | bytes 163872 | tf_op jit(solution)/shard_map/ppermute | solution.py:26
  97.7 3.8 collective-permute-done.46
  105.5 12.2 %token_.1 = (bf16[1024,768]{1,0:T(8,128)(2,1)}, bf16[768,1024]{1,0:T(8,128)(2,1)S(1)}) custom-call(s32[8]{0:T(128)S(1)} %add_subtract_fusion.refs_0_, bf16[1024,2304]{1,0:T(8,128)(2,1)} %copy-done.4, bf16[1152,768]{1,0:T(8,128)(2,1)S(1)} %copy-done.5, bf16[256,768]{1,0:T(8,128)(2,1)S(1)} %slice.204.refs_3_.refs_4_, ...), custom_call_target="tpu_custom_call" | custom-call | tf_op jit(solution)/shard_map/token/pallas_call | solution.py:810
  118.3 40.3 %ffn.1 = (f32[1024,768]{1,0:T(8,128)}, f32[1024,768]{1,0:T(8,128)}, bf16[1024,3072]{1,0:T(8,128)(2,1)}, bf16[1024,3072]{1,0:T(8,128)(2,1)}, bf16[1024,768]{1,0:T...) custom-call(bf16[1024,768]{1,0:T(8,128)(2,1)} %bitcast.71, ...), custom_call_target="tpu_custom_call" | custom-call | tf_op jit(solution)/shard_map/ffn/pallas_call | solution.py:832
  158.6 11.3 %token_back.1 = (bf16[1024,768]{1,0:T(8,128)(2,1)}, f32[256,768]{1,0:T(8,128)S(1)}, f32[256,768]{1,0:T(8,128)}) custom-call(s32[8]{0:T(128)S(1)} %add_subtract_fusion.refs_0_, bf16[1024,2304]{1,0:T(8,128)(2,1)} %copy-done.4, bf16[1024,768]{1,0:T(8,128)(2,1)} %get-tuple-element.192.refs_2_, bf16[768,1024]{1,0:T(8,128)(2,1)S(1)} %get-tuple-element.193.refs_3_, ...), custom_call_target="tpu_custom_call" | custom-call | tf_op jit(solution)/shard_map/token_back/pallas_call | solution.py:856
  170.0 6.9 %convolution_convert_fusion.3 = bf16[3072,768]{1,0:T(8,128)(2,1)} fusion(bf16[1024,3072]{1,0:T(8,128)(2,1)S(1)} %copy-done.61, bf16[1024,768]{1,0:T(8,128)(2,1)S(1)} %copy-done.63), kind=kOutput, calls=%fused_computation.88 | convolution fusion | flops 4834197504 | bytes 12582912 | tf_op jit(solution)/shard_map/dot_general | solution.py:872
  176.9 6.8 %convolution_convert_fusion.2 = bf16[768,3072]{1,0:T(8,128)(2,1)} fusion(bf16[1024,768]{1,0:T(8,128)(2,1)S(1)} %copy-done.62, bf16[1024,3072]{1,0:T(8,128)(2,1)S(1)} %bitcast.93), kind=kOutput, calls=%fused_computation.87 | convolution fusion | flops 4834197504 | bytes 12582912 | tf_op jit(solution)/shard_map/dot_general | solution.py:873
  185.4 294.5 %conditional.1 = (f32[768,2304]{1,0:T(8,128)}, f32[768,768]{1,0:T(8,128)}, f32[16,768]{1,0:T(8,128)}, f32[1,1024,768]{2,1,0:T(8,128)}, bf16[1,768]{1,0:T(2,128)(...) conditional(s32[]{:T(128)} %bitcast.27, () %tuple.30, ...), branch_computations={%region_1.2_spmd, %region_2.7_spmd} | conditional | flops 10154974208 | bytes 341589792 | solution.py:1013
  190.9 4.5 convolution_convert_fusion.1
  196.5 2.9 fusion.51
  200.7 3.3 collective-permute-done.3
  206.0 5.6 %collective-permute-done.4 = bf16[64,768]{1,0:T(8,128)(2,1)S(1)} collective-permute-done((bf16[64,768]{1,0:T(8,128)(2,1)S(1)}, bf16[64,768]{1,0:T(8,128)(2,1)S(1)}, u32[]{:S(2)}, u32[]{:S(2)}) %collective-permute-start.4) | collective-permute-done | bytes 98336 | tf_op jit(solution)/shard_map/cond/branch_1_fun/ppermute | solution.py:26
  212.4 8.9 %collective-permute-done.5 = bf16[64,768]{1,0:T(8,128)(2,1)S(1)} collective-permute-done((bf16[64,768]{1,0:T(8,128)(2,1)S(1)}, bf16[64,768]{1,0:T(8,128)(2,1)S(1)}, u32[]{:S(2)}, u32[]{:S(2)}) %collective-permute-start.5) | collective-permute-done | bytes 98336 | tf_op jit(solution)/shard_map/cond/branch_1_fun/ppermute | solution.py:26
  224.2 2.4 convert_reduce_fusion
  226.6 2.3 collective-permute-done.6
  231.2 6.2 %conv_back.1 = (f32[1024,768]{1,0:T(8,128)S(1)}, f32[1536,256]{1,0:T(8,128)S(1)}) custom-call(s32[8]{0:T(128)S(1)} %get-tuple-element.79.refs_0_, bf16[1152,768]{1,0:T(8,128)(2,1)S(1)} %maximum_maximum_fusion.1.refs_1_, bf16[1152,768]{1,0:T(8,128)(2,1)} %copy-done.6, f32[12,256]{1,0:T(8,128)S(1)} %pad.18.refs_3_), custom_call_target="tpu_custom_call" | custom-call | tf_op jit(solution)/shard_map/cond/branch_1_fun/conv_back/pallas_call | solution.py:884
  237.6 11.0 %landmark_back.1 = (bf16[1024,768]{1,0:T(8,128)(2,1)S(1)}, bf16[1024,768]{1,0:T(8,128)(2,1)S(1)}, f32[256,768]{1,0:T(8,128)S(1)}) custom-call(s32[8]{0:T(128)S(1)} %get-tuple-element.79.refs_0_, bf16[1024,2304]{1,0:T(8,128)(2,1)S(1)} %bitcast.69, bf16[1024,2304]{1,0:T(8,128)(2,1)S(1)} %bitcast.69, f32[1024,768]{1,0:T(8,128)S(1)} %get-tuple-element.84.refs_3_, ...), custom_call_target="tpu_custom_call" | custom-call | tf_op jit(solution)/shard_map/cond/branch_1_fun/landmark_back/pallas_call | solution.py:901
  252.3 9.9 %pinv_back.1 = (f32[3,64,64]{2,1,0:T(8,128)}, f32[3,64,64]{2,1,0:T(8,128)}) custom-call(f32[3,64,64]{2,1,0:T(8,128)} %get-tuple-element.93.refs_0_, f32[3,64,64]{2,1,0:T(8,128)} %get-tuple-element.94.refs_1_, f32[3,64,64]{2,1,0:T(8,128)} %get-tuple-element.95.refs_2_, f32[72,64,64]{2,1,0:T(8,128)} %get-tuple-element.96.refs_3_, bf16[3,64,64]{2,1,0:T(8,128)(2,1)} %bitcast.85, ...), custom_call_target="tpu_custom_call" | custom-call | tf_op jit(solution)/shard_map/cond/branch_1_fun/pinv_back/pallas_call | solution.py:918
  266.1 3.0 add.283
  270.6 2.9 fusion.10
  273.5 2.7 fusion.12
  278.4 3.2 add.284
  284.0 2.6 fusion.17
  290.0 3.1 add_convert_fusion.2
  296.5 12.5 %collective-permute-done.13 = bf16[384,768]{1,0:T(8,128)(2,1)S(1)} collective-permute-done((bf16[384,768]{1,0:T(8,128)(2,1)S(1)}, bf16[384,768]{1,0:T(8,128)(2,1)S(1)}, u32[]{:S(2)}, u32[]{:S(2)}) %collective-permute-start.13) | collective-permute-done | bytes 589856 | tf_op jit(solution)/shard_map/cond/branch_1_fun/ppermute | solution.py:26
  310.0 2.2 reshape.153
  312.2 2.5 pad.19
  314.7 3.2 reshape.154
  318.3 3.8 maximum_maximum_fusion
  324.4 4.6 collective-permute-done.9
  329.2 5.2 %collective-permute-done.10 = bf16[64,768]{1,0:T(8,128)(2,1)S(1)} collective-permute-done((bf16[64,768]{1,0:T(8,128)(2,1)S(1)}, bf16[64,768]{1,0:T(8,128)(2,1)S(1)}, u32[]{:S(2)}, u32[]{:S(2)}) %collective-permute-start.10) | collective-permute-done | bytes 98336 | tf_op jit(solution)/shard_map/cond/branch_1_fun/ppermute | solution.py:26
  334.5 8.3 %collective-permute-done.11 = bf16[64,768]{1,0:T(8,128)(2,1)S(1)} collective-permute-done((bf16[64,768]{1,0:T(8,128)(2,1)S(1)}, bf16[64,768]{1,0:T(8,128)(2,1)S(1)}, u32[]{:S(2)}, u32[]{:S(2)}) %collective-permute-start.11) | collective-permute-done | bytes 98336 | tf_op jit(solution)/shard_map/cond/branch_1_fun/ppermute | solution.py:26
  346.1 3.5 collective-permute-done.15
  354.2 9.9 %collective-permute-done.17 = bf16[192,768]{1,0:T(8,128)(2,1)} collective-permute-done((bf16[192,768]{1,0:T(8,128)(2,1)}, bf16[192,768]{1,0:T(8,128)(2,1)}, u32[]{:S(2)}, u32[]{:S(2)}) %collective-permute-start.17) | collective-permute-done | bytes 294944 | tf_op jit(solution)/shard_map/cond/branch_1_fun/ppermute | solution.py:26
  371.4 16.2 %collective-permute-done.19 = bf16[224,768]{1,0:T(8,128)(2,1)S(1)} collective-permute-done((bf16[224,768]{1,0:T(8,128)(2,1)S(1)}, bf16[224,768]{1,0:T(8,128)(2,1)S(1)}, u32[]{:S(2)}, u32[]{:S(2)}) %collective-permute-start.19) | collective-permute-done | bytes 344096 | tf_op jit(solution)/shard_map/cond/branch_1_fun/ppermute | solution.py:26
  394.2 2.2 collective-permute-start.21
  396.4 4.1 collective-permute-done.28
  403.6 3.7 collective-permute-done.29
  410.0 2.5 collective-permute-done.30
  412.9 3.7 collective-permute-done.23
  416.8 3.4 collective-permute-done.31
  420.7 3.3 collective-permute-done.24
  424.4 12.4 %collective-permute-done.32 = bf16[384,768]{1,0:T(8,128)(2,1)} collective-permute-done((bf16[384,768]{1,0:T(8,128)(2,1)S(1)}, bf16[384,768]{1,0:T(8,128)(2,1)}, u32[]{:S(2)}, u32[]{:S(2)}) %collective-permute-start.32) | collective-permute-done | bytes 589856 | tf_op jit(solution)/shard_map/cond/branch_1_fun/ppermute | solution.py:26
  438.9 8.9 %collective-permute-done.25 = bf16[448,768]{1,0:T(8,128)(2,1)} collective-permute-done((bf16[448,768]{1,0:T(8,128)(2,1)S(1)}, bf16[448,768]{1,0:T(8,128)(2,1)}, u32[]{:S(2)}, u32[]{:S(2)}) %collective-permute-start.25) | collective-permute-done | bytes 688160 | tf_op jit(solution)/shard_map/cond/branch_1_fun/ppermute | solution.py:26
  449.8 6.4 %fusion = f32[1024,768]{1,0:T(8,128)S(1)} fusion(bf16[768,2304]{1,0:T(8,128)(2,1)} %get-tuple-element.102, bf16[1024,768]{1,0:T(8,128)(2,1)S(1)} %get-tuple-element.107, bf16[1024,768]{1,0:T(8,128)(2,1)S(1)} %copy-done.3, bf16[1024,768]{1,0:T(8,128)(2,1)S(1)} %copy-done.33), kind=kOutput, calls=%fused_computation | convolution fusion | flops 3638034432 | bytes 11403264 | tf_op jit(solution)/shard_map/cond/branch_1_fun/dot_general | solution.py:1002
  456.2 2.3 fusion.6
  463.6 2.2 fusion.39
  470.2 9.5 %settle_qkv.1 = f32[768,2304]{1,0:T(8,128)} custom-call(s32[1]{0:T(128)} %bitcast.side_ref, bf16[896,768]{1,0:T(8,128)(2,1)} %copy-done.12, bf16[896,768]{1,0:T(8,128)(2,1)} %copy-done.27, bf16[768,768]{1,0:T(8,128)(2,1)} %copy-done.8, bf16[768,768]{1,0:T(8,128)(2,1)} %copy-done.13), custom_call_target="tpu_custom_call" | custom-call | tf_op jit(solution)/shard_map/cond/branch_1_fun/settle_qkv/pallas_call | solution.py:679
  480.0 7.5 %convert_element_type.351 = f32[768,3072]{1,0:T(8,128)} convert(bf16[768,3072]{1,0:T(8,128)(2,1)} %get-tuple-element.224) | non-fusion elementwise | flops 2359296 | bytes 14155776 | tf_op jit(solution)/shard_map/convert_element_type | solution.py:1016
  487.5 4.5 convert_element_type.352
  (368 shorter events, 115.7 us)
Async XLA Ops:
  7.2 472.8 %all-reduce.9.cloned.1.call-start = ((), (), s32[]{:S(2)}) async-start(), calls=%async_computation | async-start | bytes 18874368 | tf_op jit(solution)/shard_map/psum | solution.py:877
  13.1 1.6 collective-permute-start.36
  14.8 6.0 %collective-permute-start.37 = (bf16[64,768]{1,0:T(8,128)(2,1)S(1)}, bf16[64,768]{1,0:T(8,128)(2,1)S(1)}, u32[]{:S(2)}, u32[]{:S(2)}) collective-permute-start(bf16[64,768]{1,0:T(8,128)(2,1)S(1)} %constant_dynamic-slice_fusion.19), channel_id=1, source_target_pairs={{0,2},{1,3},{2,0},{3,1},{4,6},{5,7},{6,4},{7,5},{8,10},{9,11},{10,... | collective-permute-start | bytes 294920 | tf_op jit(solution)/shard_map/ppermute | solution.py:26
  20.8 7.9 %collective-permute-start.38 = (bf16[64,768]{1,0:T(8,128)(2,1)S(1)}, bf16[64,768]{1,0:T(8,128)(2,1)S(1)}, u32[]{:S(2)}, u32[]{:S(2)}) collective-permute-start(bf16[64,768]{1,0:T(8,128)(2,1)S(1)} %add_convert_fusion.24), channel_id=1, source_target_pairs={{0,4},{1,5},{2,6},{3,7},{4,0},{5,1},{6,2},{7,3},{8,12},{9,13},{10,... | collective-permute-start | bytes 294920 | tf_op jit(solution)/shard_map/ppermute | solution.py:26
  28.8 6.8 %collective-permute-start.39 = (bf16[64,768]{1,0:T(8,128)(2,1)S(1)}, bf16[64,768]{1,0:T(8,128)(2,1)S(1)}, u32[]{:S(2)}, u32[]{:S(2)}) collective-permute-start(bf16[64,768]{1,0:T(8,128)(2,1)S(1)} %add_convert_fusion.23), channel_id=1, source_target_pairs={{0,8},{1,9},{2,10},{3,11},{4,12},{5,13},{6,14},{7,15},{8,0},{9,1},... | collective-permute-start | bytes 294920 | tf_op jit(solution)/shard_map/ppermute | solution.py:26
  31.5 10.8 %collective-permute-start.34 = (bf16[16,768]{1,0:T(8,128)(2,1)S(1)}, bf16[16,768]{1,0:T(8,128)(2,1)S(1)}, u32[]{:S(2)}, u32[]{:S(2)}) collective-permute-start(bf16[16,768]{1,0:T(8,128)(2,1)S(1)} %get-tuple-element.264), channel_id=1, source_target_pairs={{0,1},{1,2},{2,3},{3,4},{4,5},{5,6},{6,7},{7,8},{8,9},{9,10},{10,1... | collective-permute-start | bytes 73736 | tf_op jit(solution)/shard_map/ppermute | solution.py:117
  32.7 9.5 %collective-permute-start.35 = (bf16[16,768]{1,0:T(8,128)(2,1)S(1)}, bf16[16,768]{1,0:T(8,128)(2,1)S(1)}, u32[]{:S(2)}, u32[]{:S(2)}) collective-permute-start(bf16[16,768]{1,0:T(8,128)(2,1)S(1)} %get-tuple-element.265), channel_id=1, source_target_pairs={{1,0},{2,1},{3,2},{4,3},{5,4},{6,5},{7,6},{8,7},{9,8},{10,9},{11,1... | collective-permute-start | bytes 73736 | tf_op jit(solution)/shard_map/ppermute | solution.py:119
  34.1 12.6 %slice-start = ((s8[4718592]{0:T(1024)(128)(4,1)}), s8[4194304]{0:T(1024)(128)(4,1)S(1)}, s32[]{:S(2)}) async-start(s8[4718592]{0:T(1024)(128)(4,1)} %bitcast.66), calls=%async_computation.1 | async-start | bytes 8388608
  35.6 6.5 %collective-permute-start.40 = (bf16[64,768]{1,0:T(8,128)(2,1)S(1)}, bf16[64,768]{1,0:T(8,128)(2,1)S(1)}, u32[]{:S(2)}, u32[]{:S(2)}) collective-permute-start(bf16[64,768]{1,0:T(8,128)(2,1)S(1)} %add_convert_fusion.22), channel_id=1, source_target_pairs={{0,2},{1,3},{2,0},{3,1},{4,6},{5,7},{6,4},{7,5},{8,10},{9,11},{10,... | collective-permute-start | bytes 294920 | tf_op jit(solution)/shard_map/ppermute | solution.py:26
  42.2 1.7 collective-permute-start.41
  55.6 1.5 collective-permute-start.42
  60.7 18.7 %copy-start.35 = (f32[64,3,64]{2,0,1:T(8,128)}, f32[64,3,64]{2,0,1:T(8,128)S(1)}, u32[]{:S(2)}) copy-start(f32[64,3,64]{2,0,1:T(8,128)S(1)} %copy.48) | copy-start | bytes 147460
  60.9 18.5 %copy-start.36 = (f32[64,3,64]{2,0,1:T(8,128)}, f32[64,3,64]{2,0,1:T(8,128)S(1)}, u32[]{:S(2)}) copy-start(f32[64,3,64]{2,0,1:T(8,128)S(1)} %copy.46) | copy-start | bytes 147460
  62.5 7.2 %collective-permute-start.43 = (bf16[64,896]{1,0:T(8,128)(2,1)S(1)}, bf16[64,896]{1,0:T(8,128)(2,1)S(1)}, u32[]{:S(2)}, u32[]{:S(2)}) collective-permute-start(bf16[64,896]{1,0:T(8,128)(2,1)S(1)} %get-tuple-element.268), channel_id=1, source_target_pairs={{0,2},{1,3},{2,0},{3,1},{4,6},{5,7},{6,4},{7,5},{8,10},{9,11},{10,... | collective-permute-start | bytes 344072 | tf_op jit(solution)/shard_map/ppermute | solution.py:26
  69.5 33.1 %copy-start.53 = (f32[768]{0:T(1024)S(1)}, f32[768]{0:T(1024)}, u32[]{:S(2)}) copy-start(f32[768]{0:T(1024)} %param.26) | copy-start | bytes 9220
  69.5 33.1 %copy-start.54 = (f32[768]{0:T(1024)S(1)}, f32[768]{0:T(1024)}, u32[]{:S(2)}) copy-start(f32[768]{0:T(1024)} %param.27) | copy-start | bytes 9220
  69.6 33.2 %copy-start.55 = (f32[768]{0:T(1024)S(1)}, f32[768]{0:T(1024)}, u32[]{:S(2)}) copy-start(f32[768]{0:T(1024)} %param.28) | copy-start | bytes 9220
  69.6 33.2 %copy-start.56 = (f32[768]{0:T(1024)S(1)}, f32[768]{0:T(1024)}, u32[]{:S(2)}) copy-start(f32[768]{0:T(1024)} %param.32) | copy-start | bytes 9220
  69.6 33.2 %copy-start.57 = (f32[768]{0:T(1024)S(1)}, f32[768]{0:T(1024)}, u32[]{:S(2)}) copy-start(f32[768]{0:T(1024)} %param.33) | copy-start | bytes 9220
  69.6 33.2 %copy-start.58 = (f32[768]{0:T(1024)S(1)}, f32[768]{0:T(1024)}, u32[]{:S(2)}) copy-start(f32[768]{0:T(1024)} %param.34) | copy-start | bytes 9220
  70.4 33.1 %copy-start.41 = (f32[12,33]{1,0:T(8,128)S(1)}, f32[12,33]{1,0:T(8,128)}, u32[]{:S(2)}) copy-start(f32[12,33]{1,0:T(8,128)} %param.24) | copy-start | bytes 4756
  73.5 5.9 %collective-permute-start.44 = (bf16[64,1088]{1,0:T(8,128)(2,1)S(1)}, bf16[64,1088]{1,0:T(8,128)(2,1)S(1)}, u32[]{:S(2)}, u32[]{:S(2)}) collective-permute-start(bf16[64,1088]{1,0:T(8,128)(2,1)S(1)} %pad_maximum_fusion.3), channel_id=1, source_target_pairs={{0,4},{1,5},{2,6},{3,7},{4,0},{5,1},{6,2},{7,3},{8,12},{9,13},{10,... | collective-permute-start | bytes 417800 | tf_op jit(solution)/shard_map/ppermute | solution.py:26
  80.1 25.4 %copy-start.5 = (bf16[1152,768]{1,0:T(8,128)(2,1)S(1)}, bf16[1152,768]{1,0:T(8,128)(2,1)}, u32[]{:S(2)}) copy-start(bf16[1152,768]{1,0:T(8,128)(2,1)} %maximum_maximum_fusion.2.refs_2_) | copy-start | bytes 5308420
  83.4 9.9 %collective-permute-start.45 = (bf16[64,1280]{1,0:T(8,128)(2,1)S(1)}, bf16[64,1280]{1,0:T(8,128)(2,1)S(1)}, u32[]{:S(2)}, u32[]{:S(2)}) collective-permute-start(bf16[64,1280]{1,0:T(8,128)(2,1)S(1)} %pad_maximum_fusion.2), channel_id=1, source_target_pairs={{0,8},{1,9},{2,10},{3,11},{4,12},{5,13},{6,14},{7,15},{8,0},{9,1},... | collective-permute-start | bytes 491528 | tf_op jit(solution)/shard_map/ppermute | solution.py:26
  96.3 5.2 %collective-permute-start.46 = (bf16[64,896]{1,0:T(8,128)(2,1)}, bf16[64,896]{1,0:T(8,128)(2,1)S(1)}, u32[]{:S(2)}, u32[]{:S(2)}) collective-permute-start(bf16[64,896]{1,0:T(8,128)(2,1)} %mix.1), channel_id=1, source_target_pairs={{0,2},{1,3},{2,0},{3,1},{4,6},{5,7},{6,4},{7,5},{8,10},{9,11},{10,... | collective-permute-start | bytes 344072 | tf_op jit(solution)/shard_map/ppermute | solution.py:26
  102.6 1.7 collective-permute-start.47
  186.8 43.2 %collective-permute-start = (bf16[16,768]{1,0:T(8,128)(2,1)}, bf16[16,768]{1,0:T(8,128)(2,1)S(1)}, u32[]{:S(2)}, u32[]{:S(2)}) collective-permute-start(bf16[16,768]{1,0:T(8,128)(2,1)} %get-tuple-element.244), channel_id=1, source_target_pairs={{0,1},{1,2},{2,3},{3,4},{4,5},{5,6},{6,7},{7,8},{8,9},{9,10},{10,1... | collective-permute-start | bytes 73736 | tf_op jit(solution)/shard_map/cond/branch_1_fun/ppermute | solution.py:117
  188.1 41.9 %collective-permute-start.1 = (bf16[16,768]{1,0:T(8,128)(2,1)}, bf16[16,768]{1,0:T(8,128)(2,1)}, u32[]{:S(2)}, u32[]{:S(2)}) collective-permute-start(bf16[16,768]{1,0:T(8,128)(2,1)} %get-tuple-element.245), channel_id=1, source_target_pairs={{1,0},{2,1},{3,2},{4,3},{5,4},{6,5},{7,6},{8,7},{9,8},{10,9},{11,1... | collective-permute-start | bytes 73736 | tf_op jit(solution)/shard_map/cond/branch_1_fun/ppermute | solution.py:119
  189.7 5.7 %collective-permute-start.2 = (bf16[128,768]{1,0:T(8,128)(2,1)S(1)}, bf16[128,768]{1,0:T(8,128)(2,1)}, u32[]{:S(2)}, u32[]{:S(2)}) collective-permute-start(bf16[128,768]{1,0:T(8,128)(2,1)S(1)} %constant_dynamic-slice_fusion.14), channel_id=1, source_target_pairs={{0,1},{1,0},{2,3},{3,2},{4,5},{5,4},{6,7},{7,6},{8,9},{9,8},{10,11... | collective-permute-start | bytes 589832 | tf_op jit(solution)/shard_map/cond/branch_1_fun/ppermute | solution.py:26
  196.4 7.6 %collective-permute-start.3 = (bf16[64,768]{1,0:T(8,128)(2,1)S(1)}, bf16[64,768]{1,0:T(8,128)(2,1)S(1)}, u32[]{:S(2)}, u32[]{:S(2)}) collective-permute-start(bf16[64,768]{1,0:T(8,128)(2,1)S(1)} %constant_dynamic-slice_fusion.13), channel_id=1, source_target_pairs={{0,2},{1,3},{2,0},{3,1},{4,6},{5,7},{6,4},{7,5},{8,10},{9,11},{10,... | collective-permute-start | bytes 294920 | tf_op jit(solution)/shard_map/cond/branch_1_fun/ppermute | solution.py:26
  204.1 7.5 %collective-permute-start.4 = (bf16[64,768]{1,0:T(8,128)(2,1)S(1)}, bf16[64,768]{1,0:T(8,128)(2,1)S(1)}, u32[]{:S(2)}, u32[]{:S(2)}) collective-permute-start(bf16[64,768]{1,0:T(8,128)(2,1)S(1)} %add_convert_fusion.16), channel_id=1, source_target_pairs={{0,4},{1,5},{2,6},{3,7},{4,0},{5,1},{6,2},{7,3},{8,12},{9,13},{10,... | collective-permute-start | bytes 294920 | tf_op jit(solution)/shard_map/cond/branch_1_fun/ppermute | solution.py:26
  205.9 24.2 %copy-start.11 = (bf16[1024,768]{1,0:T(8,128)(2,1)S(1)}, bf16[1024,768]{1,0:T(8,128)(2,1)}, u32[]{:S(2)}) copy-start(bf16[1024,768]{1,0:T(8,128)(2,1)} %get-tuple-element.81) | copy-start | bytes 4718596 | tf_op jit(solution)/shard_map/cond
  211.6 9.7 %collective-permute-start.5 = (bf16[64,768]{1,0:T(8,128)(2,1)S(1)}, bf16[64,768]{1,0:T(8,128)(2,1)S(1)}, u32[]{:S(2)}, u32[]{:S(2)}) collective-permute-start(bf16[64,768]{1,0:T(8,128)(2,1)S(1)} %add_convert_fusion.15), channel_id=1, source_target_pairs={{0,8},{1,9},{2,10},{3,11},{4,12},{5,13},{6,14},{7,15},{8,0},{9,1},... | collective-permute-start | bytes 294920 | tf_op jit(solution)/shard_map/cond/branch_1_fun/ppermute | solution.py:26
  223.9 5.0 %collective-permute-start.6 = (bf16[64,896]{1,0:T(8,128)(2,1)}, bf16[64,896]{1,0:T(8,128)(2,1)S(1)}, u32[]{:S(2)}, u32[]{:S(2)}) collective-permute-start(bf16[64,896]{1,0:T(8,128)(2,1)} %mix_back.1), channel_id=1, source_target_pairs={{0,2},{1,3},{2,0},{3,1},{4,6},{5,7},{6,4},{7,5},{8,10},{9,11},{10,... | collective-permute-start | bytes 344072 | tf_op jit(solution)/shard_map/cond/branch_1_fun/ppermute | solution.py:26
  224.2 13.4 %slice-start.2 = ((s8[4718592]{0:T(1024)(128)(4,1)}), s8[4194304]{0:T(1024)(128)(4,1)S(1)}, s32[]{:S(2)}) async-start(s8[4718592]{0:T(1024)(128)(4,1)} %bitcast.68), calls=%async_computation.3 | async-start | bytes 8388608 | tf_op jit(solution)/shard_map/cond
  230.0 7.5 %collective-permute-start.7 = (bf16[128,896]{1,0:T(8,128)(2,1)S(1)}, bf16[128,896]{1,0:T(8,128)(2,1)S(1)}, u32[]{:S(2)}, u32[]{:S(2)}) collective-permute-start(bf16[128,896]{1,0:T(8,128)(2,1)S(1)} %maximum_select_fusion.8), channel_id=1, source_target_pairs={{0,1},{1,0},{2,3},{3,2},{4,5},{5,4},{6,7},{7,6},{8,9},{9,8},{10,11... | collective-permute-start | bytes 688136 | tf_op jit(solution)/shard_map/cond/branch_1_fun/ppermute | solution.py:26
  276.2 13.6 %collective-permute-start.12 = (bf16[768,768]{1,0:T(8,128)(2,1)}, bf16[768,768]{1,0:T(8,128)(2,1)}, u32[]{:S(2)}, u32[]{:S(2)}) collective-permute-start(bf16[768,768]{1,0:T(8,128)(2,1)} %fusion.12), channel_id=1, source_target_pairs={{0,1},{1,0},{2,3},{3,2},{4,5},{5,4},{6,7},{7,6},{8,9},{9,8},{10,11... | collective-permute-start | bytes 3538952 | tf_op jit(solution)/shard_map/cond/branch_1_fun/ppermute | solution.py:26
  287.3 34.9 %collective-permute-start.8 = (bf16[128,768]{1,0:T(8,128)(2,1)}, bf16[128,768]{1,0:T(8,128)(2,1)}, u32[]{:S(2)}, u32[]{:S(2)}) collective-permute-start(bf16[128,768]{1,0:T(8,128)(2,1)} %constant_dynamic-slice_fusion.10), channel_id=1, source_target_pairs={{0,1},{1,0},{2,3},{3,2},{4,5},{5,4},{6,7},{7,6},{8,9},{9,8},{10,11... | collective-permute-start | bytes 589832 | tf_op jit(solution)/shard_map/cond/branch_1_fun/ppermute | solution.py:26
  293.2 15.8 %collective-permute-start.13 = (bf16[384,768]{1,0:T(8,128)(2,1)S(1)}, bf16[384,768]{1,0:T(8,128)(2,1)S(1)}, u32[]{:S(2)}, u32[]{:S(2)}) collective-permute-start(bf16[384,768]{1,0:T(8,128)(2,1)S(1)} %constant_dynamic-slice_fusion.8), channel_id=1, source_target_pairs={{0,16},{16,0},{1,17},{17,1},{2,18},{18,2},{3,19},{19,3},{4,20},{20... | collective-permute-start | bytes 1769480 | tf_op jit(solution)/shard_map/cond/branch_1_fun/ppermute | solution.py:26
  322.2 20.6 %collective-permute-start.14 = (bf16[896,768]{1,0:T(8,128)(2,1)S(1)}, bf16[896,768]{1,0:T(8,128)(2,1)}, u32[]{:S(2)}, u32[]{:S(2)}) collective-permute-start(bf16[896,768]{1,0:T(8,128)(2,1)S(1)} %constant_dynamic-slice_fusion.7), channel_id=1, source_target_pairs={{0,1},{1,0},{2,3},{3,2},{4,5},{5,4},{6,7},{7,6},{8,9},{9,8},{10,11... | collective-permute-start | bytes 4128776 | tf_op jit(solution)/shard_map/cond/branch_1_fun/ppermute | solution.py:26
  324.4 4.7 collective-permute-start.9
  329.1 5.3 %collective-permute-start.10 = (bf16[64,768]{1,0:T(8,128)(2,1)S(1)}, bf16[64,768]{1,0:T(8,128)(2,1)S(1)}, u32[]{:S(2)}, u32[]{:S(2)}) collective-permute-start(bf16[64,768]{1,0:T(8,128)(2,1)S(1)} %add_convert_fusion.13), channel_id=1, source_target_pairs={{0,4},{1,5},{2,6},{3,7},{4,0},{5,1},{6,2},{7,3},{8,12},{9,13},{10,... | collective-permute-start | bytes 294920 | tf_op jit(solution)/shard_map/cond/branch_1_fun/ppermute | solution.py:26
  334.4 8.4 %collective-permute-start.11 = (bf16[64,768]{1,0:T(8,128)(2,1)S(1)}, bf16[64,768]{1,0:T(8,128)(2,1)S(1)}, u32[]{:S(2)}, u32[]{:S(2)}) collective-permute-start(bf16[64,768]{1,0:T(8,128)(2,1)S(1)} %add_convert_fusion.12), channel_id=1, source_target_pairs={{0,8},{1,9},{2,10},{3,11},{4,12},{5,13},{6,14},{7,15},{8,0},{9,1},... | collective-permute-start | bytes 294920 | tf_op jit(solution)/shard_map/cond/branch_1_fun/ppermute | solution.py:26
  344.9 4.7 collective-permute-start.15
  346.0 21.1 %collective-permute-start.18 = (bf16[448,768]{1,0:T(8,128)(2,1)}, bf16[448,768]{1,0:T(8,128)(2,1)}, u32[]{:S(2)}, u32[]{:S(2)}) collective-permute-start(bf16[448,768]{1,0:T(8,128)(2,1)} %constant_dynamic-slice_fusion.5), channel_id=1, source_target_pairs={{0,16},{16,0},{1,17},{17,1},{2,18},{18,2},{3,19},{19,3},{4,20},{20... | collective-permute-start | bytes 2064392 | tf_op jit(solution)/shard_map/cond/branch_1_fun/ppermute | solution.py:26
  350.3 1.8 collective-permute-start.16
  351.1 13.0 %collective-permute-start.17 = (bf16[192,768]{1,0:T(8,128)(2,1)}, bf16[192,768]{1,0:T(8,128)(2,1)}, u32[]{:S(2)}, u32[]{:S(2)}) collective-permute-start(bf16[192,768]{1,0:T(8,128)(2,1)} %constant_dynamic-slice_fusion.6), channel_id=1, source_target_pairs={{0,2},{1,3},{2,0},{3,1},{4,6},{5,7},{6,4},{7,5},{8,10},{9,11},{10,... | collective-permute-start | bytes 884744 | tf_op jit(solution)/shard_map/cond/branch_1_fun/ppermute | solution.py:26
  369.2 18.3 %collective-permute-start.19 = (bf16[224,768]{1,0:T(8,128)(2,1)S(1)}, bf16[224,768]{1,0:T(8,128)(2,1)S(1)}, u32[]{:S(2)}, u32[]{:S(2)}) collective-permute-start(bf16[224,768]{1,0:T(8,128)(2,1)S(1)} %constant_dynamic-slice_fusion.4), channel_id=1, source_target_pairs={{0,4},{1,5},{2,6},{3,7},{4,0},{5,1},{6,2},{7,3},{8,12},{9,13},{10,... | collective-permute-start | bytes 1032200 | tf_op jit(solution)/shard_map/cond/branch_1_fun/ppermute | solution.py:26
  370.9 20.1 %collective-permute-start.27 = (bf16[96,768]{1,0:T(8,128)(2,1)S(1)}, bf16[96,768]{1,0:T(8,128)(2,1)S(1)}, u32[]{:S(2)}, u32[]{:S(2)}) collective-permute-start(bf16[96,768]{1,0:T(8,128)(2,1)S(1)} %constant_dynamic-slice_fusion.1), channel_id=1, source_target_pairs={{0,4},{1,5},{2,6},{3,7},{4,0},{5,1},{6,2},{7,3},{8,12},{9,13},{10,... | collective-permute-start | bytes 442376 | tf_op jit(solution)/shard_map/cond/branch_1_fun/ppermute | solution.py:26
  388.7 5.5 %collective-permute-start.20 = (bf16[112,768]{1,0:T(8,128)(2,1)S(1)}, bf16[112,768]{1,0:T(8,128)(2,1)S(1)}, u32[]{:S(2)}, u32[]{:S(2)}) collective-permute-start(bf16[112,768]{1,0:T(8,128)(2,1)S(1)} %constant_dynamic-slice_fusion.3), channel_id=1, source_target_pairs={{0,2},{1,3},{2,0},{3,1},{4,6},{5,7},{6,4},{7,5},{8,10},{9,11},{10,... | collective-permute-start | bytes 516104 | tf_op jit(solution)/shard_map/cond/branch_1_fun/ppermute | solution.py:26
  391.0 9.5 %collective-permute-start.28 = (bf16[48,768]{1,0:T(8,128)(2,1)S(1)}, bf16[48,768]{1,0:T(8,128)(2,1)S(1)}, u32[]{:S(2)}, u32[]{:S(2)}) collective-permute-start(bf16[48,768]{1,0:T(8,128)(2,1)S(1)} %constant_dynamic-slice_fusion), channel_id=1, source_target_pairs={{0,8},{1,9},{2,10},{3,11},{4,12},{5,13},{6,14},{7,15},{8,0},{9,1},... | collective-permute-start | bytes 221192 | tf_op jit(solution)/shard_map/cond/branch_1_fun/ppermute | solution.py:26
  394.2 8.1 %collective-permute-start.21 = (bf16[56,768]{1,0:T(8,128)(2,1)S(1)}, bf16[56,768]{1,0:T(8,128)(2,1)S(1)}, u32[]{:S(2)}, u32[]{:S(2)}) collective-permute-start(bf16[56,768]{1,0:T(8,128)(2,1)S(1)} %constant_dynamic-slice_fusion.2), channel_id=1, source_target_pairs={{0,8},{1,9},{2,10},{3,11},{4,12},{5,13},{6,14},{7,15},{8,0},{9,1},... | collective-permute-start | bytes 258056 | tf_op jit(solution)/shard_map/cond/branch_1_fun/ppermute | solution.py:26
  400.5 6.8 %collective-permute-start.29 = (bf16[48,768]{1,0:T(8,128)(2,1)S(1)}, bf16[48,768]{1,0:T(8,128)(2,1)S(1)}, u32[]{:S(2)}, u32[]{:S(2)}) collective-permute-start(bf16[48,768]{1,0:T(8,128)(2,1)S(1)} %add_convert_fusion.18), channel_id=1, source_target_pairs={{0,8},{1,9},{2,10},{3,11},{4,12},{5,13},{6,14},{7,15},{8,0},{9,1},... | collective-permute-start | bytes 221192 | tf_op jit(solution)/shard_map/cond/branch_1_fun/ppermute | solution.py:26
  402.3 6.9 %collective-permute-start.22 = (bf16[56,768]{1,0:T(8,128)(2,1)S(1)}, bf16[56,768]{1,0:T(8,128)(2,1)S(1)}, u32[]{:S(2)}, u32[]{:S(2)}) collective-permute-start(bf16[56,768]{1,0:T(8,128)(2,1)S(1)} %add_convert_fusion.17), channel_id=1, source_target_pairs={{0,8},{1,9},{2,10},{3,11},{4,12},{5,13},{6,14},{7,15},{8,0},{9,1},... | collective-permute-start | bytes 258056 | tf_op jit(solution)/shard_map/cond/branch_1_fun/ppermute | solution.py:26
  407.3 5.2 %collective-permute-start.30 = (bf16[96,768]{1,0:T(8,128)(2,1)S(1)}, bf16[96,768]{1,0:T(8,128)(2,1)S(1)}, u32[]{:S(2)}, u32[]{:S(2)}) collective-permute-start(bf16[96,768]{1,0:T(8,128)(2,1)S(1)} %maximum_select_fusion.11), channel_id=1, source_target_pairs={{0,4},{1,5},{2,6},{3,7},{4,0},{5,1},{6,2},{7,3},{8,12},{9,13},{10,... | collective-permute-start | bytes 442376 | tf_op jit(solution)/shard_map/cond/branch_1_fun/ppermute | solution.py:26
  409.3 7.4 %collective-permute-start.23 = (bf16[112,768]{1,0:T(8,128)(2,1)S(1)}, bf16[112,768]{1,0:T(8,128)(2,1)S(1)}, u32[]{:S(2)}, u32[]{:S(2)}) collective-permute-start(bf16[112,768]{1,0:T(8,128)(2,1)S(1)} %maximum_select_fusion.10), channel_id=1, source_target_pairs={{0,2},{1,3},{2,0},{3,1},{4,6},{5,7},{6,4},{7,5},{8,10},{9,11},{10,... | collective-permute-start | bytes 516104 | tf_op jit(solution)/shard_map/cond/branch_1_fun/ppermute | solution.py:26
  412.5 7.6 %collective-permute-start.31 = (bf16[192,768]{1,0:T(8,128)(2,1)S(1)}, bf16[192,768]{1,0:T(8,128)(2,1)S(1)}, u32[]{:S(2)}, u32[]{:S(2)}) collective-permute-start(bf16[192,768]{1,0:T(8,128)(2,1)S(1)} %maximum_select_fusion.7), channel_id=1, source_target_pairs={{0,2},{1,3},{2,0},{3,1},{4,6},{5,7},{6,4},{7,5},{8,10},{9,11},{10,... | collective-permute-start | bytes 884744 | tf_op jit(solution)/shard_map/cond/branch_1_fun/ppermute | solution.py:26
  416.7 7.3 %collective-permute-start.24 = (bf16[224,768]{1,0:T(8,128)(2,1)S(1)}, bf16[224,768]{1,0:T(8,128)(2,1)S(1)}, u32[]{:S(2)}, u32[]{:S(2)}) collective-permute-start(bf16[224,768]{1,0:T(8,128)(2,1)S(1)} %maximum_select_fusion.6), channel_id=1, source_target_pairs={{0,4},{1,5},{2,6},{3,7},{4,0},{5,1},{6,2},{7,3},{8,12},{9,13},{10,... | collective-permute-start | bytes 1032200 | tf_op jit(solution)/shard_map/cond/branch_1_fun/ppermute | solution.py:26
  420.4 16.4 %collective-permute-start.32 = (bf16[384,768]{1,0:T(8,128)(2,1)S(1)}, bf16[384,768]{1,0:T(8,128)(2,1)}, u32[]{:S(2)}, u32[]{:S(2)}) collective-permute-start(bf16[384,768]{1,0:T(8,128)(2,1)S(1)} %maximum_select_fusion.3), channel_id=1, source_target_pairs={{0,16},{16,0},{1,17},{17,1},{2,18},{18,2},{3,19},{19,3},{4,20},{20... | collective-permute-start | bytes 1769480 | tf_op jit(solution)/shard_map/cond/branch_1_fun/ppermute | solution.py:26
  424.3 23.6 %collective-permute-start.25 = (bf16[448,768]{1,0:T(8,128)(2,1)S(1)}, bf16[448,768]{1,0:T(8,128)(2,1)}, u32[]{:S(2)}, u32[]{:S(2)}) collective-permute-start(bf16[448,768]{1,0:T(8,128)(2,1)S(1)} %maximum_select_fusion.2), channel_id=1, source_target_pairs={{0,16},{16,0},{1,17},{17,1},{2,18},{18,2},{3,19},{19,3},{4,20},{20... | collective-permute-start | bytes 2064392 | tf_op jit(solution)/shard_map/cond/branch_1_fun/ppermute | solution.py:26
  436.8 12.9 %copy-start.33 = (bf16[1024,768]{1,0:T(8,128)(2,1)S(1)}, bf16[1024,768]{1,0:T(8,128)(2,1)}, u32[]{:S(2)}) copy-start(bf16[1024,768]{1,0:T(8,128)(2,1)} %get-tuple-element.111) | copy-start | bytes 4718596 | tf_op jit(solution)/shard_map/cond
  438.8 19.8 %copy-start.8 = (bf16[768,768]{1,0:T(8,128)(2,1)}, bf16[768,768]{1,0:T(8,128)(2,1)S(1)}, u32[]{:S(2)}) copy-start(bf16[768,768]{1,0:T(8,128)(2,1)S(1)} %maximum_select_fusion.1.early_ref) | copy-start | bytes 3538948 | tf_op jit(solution)/shard_map/cond
  438.8 19.7 %collective-permute-start.33 = (bf16[768,768]{1,0:T(8,128)(2,1)S(1)}, bf16[768,768]{1,0:T(8,128)(2,1)S(1)}, u32[]{:S(2)}, u32[]{:S(2)}) collective-permute-start(bf16[768,768]{1,0:T(8,128)(2,1)S(1)} %maximum_select_fusion.1.early_ref), channel_id=1, source_target_pairs={{0,1},{1,0},{2,3},{3,2},{4,5},{5,4},{6,7},{7,6},{8,9},{9,8},{10,11... | collective-permute-start | bytes 3538952 | tf_op jit(solution)/shard_map/cond/branch_1_fun/ppermute | solution.py:26
  449.7 10.8 %collective-permute-start.26 = (bf16[896,768]{1,0:T(8,128)(2,1)S(1)}, bf16[896,768]{1,0:T(8,128)(2,1)S(1)}, u32[]{:S(2)}, u32[]{:S(2)}) collective-permute-start(bf16[896,768]{1,0:T(8,128)(2,1)S(1)} %maximum_select_fusion.late_ref), channel_id=1, source_target_pairs={{0,1},{1,0},{2,3},{3,2},{4,5},{5,4},{6,7},{7,6},{8,9},{9,8},{10,11... | collective-permute-start | bytes 4128776 | tf_op jit(solution)/shard_map/cond/branch_1_fun/ppermute | solution.py:26
  (56 other events, 261.6 us)
Sparse Core Ops, SparseCore 0:
  183.8 206.3 all-reduce.8

commit v8 on v7

--- a/solution.py
+++ b/solution.py
@@ -19,6 +19,7 @@
 SUB = 128
 TAPS = 33
 FFN_BLOCK = 256
+ORDER = ("row", "near", "far")
 
 
 def swap(array, axis, bit):
@@ -63,6 +64,29 @@
 
 def seq_whole(array):
     return paired(paired(array, "seq", 2, 0), "seq", 1, 0)
+
+
+def seq_steps():
+    bits = [1 << i for i in range(lax.axis_size("seq").bit_length() - 1)]
+
+    def halve(bit):
+        def step(array):
+            mine, other = halves(array, bit)
+            return add_join(mine, swap(other, "seq", bit))
+
+        return step
+
+    def whole(bit):
+        return lambda array: add_join(array, swap(array, "seq", bit))
+
+    def double(bit):
+        return lambda array: paired(array, "seq", bit, 0)
+
+    return (
+        [halve(bit) for bit in bits[:2]]
+        + [whole(bit) for bit in bits[2:]]
+        + [double(bit) for bit in reversed(bits[:2])]
+    )
 
 
 def add_join(first, second):
@@ -610,49 +634,6 @@
         gk_ref[p] = dot_high(grad, q_ref[p], TN)
 
 
-def settle_kernel(side_ref, mine_ref, other_ref, out_ref):
-    own = pl.program_id(0) == side_ref[0]
-
-    @pl.when(own)
-    def _():
-        out_ref[...] = mine_ref[...].astype(F32)
-
-    @pl.when(jnp.logical_not(own))
-    def _():
-        out_ref[...] = other_ref[...].astype(F32)
-
-
-def settle(state):
-    mine, other, down, back = last_swap(state)
-    moved = len(stages(("row", "near", "far"))) - len(stages(()))
-    down, back = down[1 : 1 + moved], back[1 : 1 + moved]
-    blocks = 1 << moved
-    rows, columns = mine.shape[0] // blocks, mine.shape[1]
-
-    def source(j):
-        bits = {stage: (j >> (moved - 1 - i)) % 2 for i, stage in enumerate(down)}
-        at = 0
-        for stage in back:
-            at = at * 2 + bits[stage]
-        return at
-
-    side = (lax.axis_index("seq") % 2).astype(jnp.int32).reshape(1)
-    return pl.pallas_call(
-        settle_kernel,
-        grid_spec=pltpu.PrefetchScalarGridSpec(
-            num_scalar_prefetch=1,
-            grid=(2, blocks),
-            in_specs=[
-                pl.BlockSpec((rows, columns), lambda h, j, s: (jnp.where(h == s[0], source(j), 0), 0)),
-                pl.BlockSpec((rows, columns), lambda h, j, s: (jnp.where(h == s[0], 0, source(j)), 0)),
-            ],
-            out_specs=pl.BlockSpec((rows, columns), lambda h, j, s: (h * blocks + j, 0)),
-        ),
-        out_shape=jax.ShapeDtypeStruct((2 * blocks * rows, columns), F32),
-        name="settle",
-    )(side, mine, other)
-
-
 def settle_qkv_kernel(side_ref, late_ref, late_other_ref, early_ref, early_other_ref, out_ref):
     part = pl.program_id(0)
     own = jnp.where(part == 0, 0, 1) == side_ref[0]
@@ -671,7 +652,7 @@
 
 def settle_qkv(late, late_other, early, early_other, width):
     side = (lax.axis_index("seq") % 2).astype(jnp.int32).reshape(1)
-    rows = width // 3
+    rows = width // 2
 
     def spec(used):
         return pl.BlockSpec((rows, width), lambda j, i, s: (jnp.where(used(j), i, 0), 0))
@@ -680,7 +661,7 @@
         settle_qkv_kernel,
         grid_spec=pltpu.PrefetchScalarGridSpec(
             num_scalar_prefetch=1,
-            grid=(3, 3),
+            grid=(3, 2),
             in_specs=[spec(lambda j: j < 2), spec(lambda j: j < 2)] + [spec(lambda j: j == 2)] * 2,
             out_specs=pl.BlockSpec((rows, width), lambda j, i, s: (i, j)),
         ),
@@ -893,6 +874,14 @@
             compiler_params=params,
             name="conv_back",
         )(bounds, grad_ext, value_ext, jnp.pad(conv_taps[:, ::-1], ((0, 0), (0, GROUP - tap_count))))
+        reach = SUB + tap_count - 1
+        products = products.reshape(heads, SUB, GROUP)[:, :, :reach].reshape(heads, SUB * reach)
+        products = jnp.pad(products, ((0, 0), (0, SUB))).reshape(heads, SUB, reach + 1)
+        grad_conv_taps = jnp.sum(products, axis=1)[:, :tap_count]
+        grad_mix, grad_conv, grad_conv_taps = lax.optimization_barrier(
+            (grad_mix, grad_conv, grad_conv_taps)
+        )
+
         grad_avg = pl.pallas_call(
             mix_back_kernel, out_shape=shaped((LAND, width + 128), BF), name="mix_back"
         )(inverse, stats, grad_mix)
@@ -914,24 +903,32 @@
             name="landmark_back",
         )(bounds, qkv, qkv, grad_conv, mark_q, grad_avg, mix, grad_avg)
 
-        grad_mix, grad_values = lax.optimization_barrier((grad_mix, grad_values))
+
+        def weight_grad(grads):
+            return lax.dot_general(tokens, grads, rows_in, preferred_element_type=F32)
+
+        early = jnp.concatenate(
+            [grad_w_out.astype(BF), weight_grad(grad_values).astype(BF)], 0
+        )
+        grad_mix, early = lax.optimization_barrier((grad_mix, early))
+        early = advance(begin(early, ORDER, ORDER), 1)
         grad_mq_small, grad_mk_small = pl.pallas_call(
             lambda *refs: pinv_back_kernel(scale, *refs),
             out_shape=(shaped(square, F32), shaped(square, F32)),
             name="pinv_back",
         )(own_q, own_k, kernel, saved, own_heads(grad_mix), own_heads(stats[:, :width]))
 
-        def placed(array):
-            array = array.transpose(1, 0, 2).reshape(LAND, own_count * size)
-            array = lax.dynamic_update_slice_in_dim(
-                jnp.zeros((LAND, width + spare), F32), array, own_at, 1
+        def with_small(array, small):
+            small = small.transpose(1, 0, 2).reshape(LAND, own_count * size)
+            small = lax.dynamic_update_slice_in_dim(
+                jnp.zeros((LAND, width + spare), F32), small, own_at, 1
             )[:, :width]
-            return lax.dynamic_update_slice_in_dim(
-                jnp.zeros((mark_count, width), F32), array, own_doc * LAND, 0
-            )
-
-        grad_mq = grad_mq + placed(grad_mq_small)
-        grad_mk = grad_mk + placed(grad_mk_small)
+            first = own_doc * LAND
+            rows = lax.dynamic_slice_in_dim(array, first, LAND, 0) + small
+            return lax.dynamic_update_slice_in_dim(array, rows, first, 0)
+
+        grad_mq = with_small(grad_mq, grad_mq_small)
+        grad_mk = with_small(grad_mk, grad_mk_small)
         grad_marks = jnp.concatenate([grad_mq, grad_mk], axis=1).astype(BF)
         mark_back = lax.dot_general(
             grad_marks, w_qkv[:, : 2 * width], cols_in, preferred_element_type=F32
@@ -940,27 +937,12 @@
 
         grad_bias_q = jnp.sum(grad_queries.astype(F32), axis=0) + jnp.sum(grad_mq, axis=0)
         grad_bias_v = jnp.sum(grad_values.astype(F32), axis=0)
-        grad_projected = jnp.concatenate([grad_queries, grad_keys, grad_values], axis=1)
-
-        def weight_grad(grads):
-            return lax.dot_general(tokens, grads, rows_in, preferred_element_type=F32)
-
-        early = jnp.concatenate([grad_w_out.astype(BF), weight_grad(grad_values).astype(BF)], 0)
-        early = begin(early, ("row", "near", "far"), ("row", "near", "far"))
-        early = advance(early, 1)
-        grad_marks, (early,) = tied(grad_marks, [early])
-        early = advance(early, 1)
         mark_grad_q = lax.dot_general(
             mean_in, grad_marks[:, :width], rows_in, preferred_element_type=F32
         )
         mark_grad_k = lax.dot_general(
             mean_in, grad_marks[:, width:], rows_in, preferred_element_type=F32
         )
-        products, (early,) = tied(products, [early])
-        reach = SUB + tap_count - 1
-        products = products.reshape(heads, SUB, GROUP)[:, :, :reach].reshape(heads, SUB * reach)
-        products = jnp.pad(products, ((0, 0), (0, SUB))).reshape(heads, SUB, reach + 1)
-        grad_conv_taps = jnp.sum(products, axis=1)[:, :tap_count]
         others = jnp.concatenate(
             [
                 sum_up[0].reshape(hidden // width, width),
@@ -984,36 +966,50 @@
             ],
             0,
         )
-        late = begin(late, ("row", "far", "near"), ("row", "far", "near"))
-        late = advance(late, 1)
-        mark_back = seq_quarter(mark_back, add_join)
-        mark_back, (early, late) = tied(mark_back, [early, late])
-        early, late = advance(early, 1), advance(late, 1)
-        mark_back = seq_whole(mark_back)
-        mark_back, (early, late) = tied(mark_back, [early, late])
-        early, early_other = last_swap(early)[:2]
-        late, late_other = last_swap(late)[:2]
-        sum_w_qkv = settle_qkv(late, late_other, early, early_other, width)
-        first_core = me % 2 == 0
-        sum_w_out = jnp.where(first_core, early, early_other).astype(F32)
-        flat = jnp.where(first_core, late[width:], late_other[width:])[:16].astype(F32)
-        grad_input = (
-            grad_one
-            + lax.dot_general(grad_projected, w_qkv, cols_in, preferred_element_type=F32)
-            + lax.dot_general(onehot, mark_back, rows_in, preferred_element_type=F32)
+        late = begin(late, ORDER, ORDER)
+        for step in seq_steps():
+            mark_back = step(mark_back)
+            early, late = advance(early, 1), advance(late, 1)
+            mark_back, (early, late) = tied(mark_back, [early, late])
+        return early[0], late[0], mark_back, grad_keys, grad_values
+
+    plan = stages(ORDER)
+    sent = len(seq_steps())
+
+    def rows_left(rows, done):
+        return rows >> min(done, 2 * len(plan) - done)
+
+    early_rows = rows_left(2 * width, sent + 1)
+    late_rows = rows_left(2 * width + width // 3, sent)
+
+    def nothing(*unused):
+        return tuple(
+            jnp.zeros((rows, width), BF)
+            for rows in (early_rows, late_rows, mark_count, tok_count, tok_count)
         )
-        return grad_input, sum_w_qkv, sum_w_out, flat
-
-    def nothing(*unused):
-        return (
-            jnp.zeros((tok_count, width), F32), jnp.zeros((width, 3 * width), F32),
-            jnp.zeros((width, width), F32), jnp.zeros((16, width), F32),
-        )
-
-    grad_input, sum_w_qkv, sum_w_out, flat = lax.cond(
+
+    early, late, mark_back, grad_keys, grad_values = lax.cond(
         lengths[0] > 0, remaining, nothing, grad_mix, grad_mk, stats, mix
     )
+    early, late = (early, plan, plan, sent + 1), (late, plan, plan, sent)
+    last = 2 * len(plan) - 1
+    early, late = advance(early, last - sent - 1), advance(late, last - sent)
     sum_w_down, sum_w_up = sum_w_down.astype(F32), sum_w_up.astype(F32)
+    grad_projected = jnp.concatenate([grad_queries, grad_keys, grad_values], axis=1)
+    grad_input = (
+        grad_one
+        + lax.dot_general(grad_projected, w_qkv, cols_in, preferred_element_type=F32)
+        + lax.dot_general(onehot, mark_back, rows_in, preferred_element_type=F32)
+    )
+    (sum_w_down, sum_w_up, grad_input), (early, late) = tied(
+        (sum_w_down, sum_w_up, grad_input), [early, late]
+    )
+    early, early_other = last_swap(early)[:2]
+    late, late_other = last_swap(late)[:2]
+    sum_w_qkv = settle_qkv(late, late_other, early, early_other, width)
+    first_core = me % 2 == 0
+    sum_w_out = jnp.where(first_core, early, early_other).astype(F32)
+    flat = jnp.where(first_core, late[width:], late_other[width:])[:16].astype(F32)
     at = sums.shape[0] + hidden // width
     pieces = [
         flat[at], flat[at + 1], flat[at + 2, : heads * tap_count], flat[5], flat[3], flat[4],

time: 506 us -> 491 us (0.970)
  waiting for transfers between devices: 161 us -> 123 us
  starting transfers between devices: 31.5 us -> 68.2 us
  Pallas kernels: 126 us -> 111 us
  other arithmetic: 67 us -> 60.3 us
    ppermute x44, waiting for transfers between devices: 161 us -> 123 us  [swap(): return lax.ppermute(array, axis, [(i, i ^ bit) for i in range(count)])]
    ppermute x44, starting transfers between devices: 26.1 us -> 61.3 us  [swap(): return lax.ppermute(array, axis, [(i, i ^ bit) for i in range(count)])]
    add x2 -> x0, local copies, waits for them, and re-layouts: 6.16 us -> none  [the longest x1 3.17 us: remaining(): grad_mk = grad_mk + placed(grad_mk_small)]
    dynamic_update_slice x0 -> x2, local copies, waits for them, and re-layouts: none -> 5.9 us  [with_small(): return lax.dynamic_update_slice_in_dim(array, rows, first, 0)]
  transfers between devices with their start and end apart: 49 -> 49, of which waited for: 34 -> 30; matrix products, arithmetic and copies ran while one was open for 23% -> 23% of each run, Pallas kernels for 9% -> 7%
where the time goes in v8:
time: 491 us; the launch traced here: 482 us
  waiting for transfers between devices  123 us (25%)
  Pallas kernels  111 us (23%)
  starting transfers between devices  68.2 us (14%)
  other arithmetic  60.3 us (12%)
  matrix products  54.3 us (11%)
  local copies, waits for them, and re-layouts  49.1 us (10%)
  between operations  15.1 us (3%)
    ppermute x44, waiting for transfers between devices, swap(): return lax.ppermute(array, axis, [(i, i ^ bit) for i in range(count)])  123 us
    ppermute x44, starting transfers between devices, swap(): return lax.ppermute(array, axis, [(i, i ^ bit) for i in range(count)])  61.3 us
    pallas_call x1, Pallas kernels, per_device(): pl.pallas_call(ffn_kernel, grid=(tok_count // FFN_BLOCK,), in_specs=[ffn_...  40.3 us
    convert_element_type x2, other arithmetic, per_device(): sum_w_down, sum_w_up = (sum_w_down.astype(F32), sum_w_up.astype(F32))  12.4 us
    select_n x16, other arithmetic, paired(): jnp.where(side == 0, jnp.concatenate([array, other], dim), jnp.concatenat...  11.5 us
    dot_general x3, matrix products, weight_grad(): return lax.dot_general(tokens, grads, rows_in, preferred_element_type=F32)  11.3 us
    pallas_call x1, Pallas kernels, remaining(): pl.pallas_call(lambda *refs: pinv_back_kernel(scale, *refs), out_shape=(s...  10 us
  transfers between devices with their start and end apart: 49, of which 30 were waited for; matrix products, arithmetic and copies ran while one was open for 23% of the time, Pallas kernels for 7%

profile of v8, /device:TPU:0, one launch (start us, length us, event | category | flops | bytes accessed | tf_op | source)
XLA Modules:
  0.0 481.8 jit_solution(3618854203875115612)
XLA Ops:
  10.9 2.2 fusion.24
  14.8 3.0 collective-permute-start.30
  17.7 3.1 collective-permute-done.30
  22.7 6.0 %add_convert_fusion.20.refs_2_.refs_3_.refs_1_ = bf16[1024,2304]{1,0:T(8,128)(2,1)S(1)} fusion(bf16[768,2304]{1,0:T(8,128)(2,1)} %param.21, f32[2304]{0:T(1024)S(1)} %pad_maximum_fusion.3, bf16[1,1024,768]{2,1,0:T(8,128)(2,1)S(1)} %copy-done.24), kind=kOutput, calls=%fused_computation.65 | convolution fusion | flops 3628597248 | bytes 9839616 | tf_op jit(solution)/shard_map/dot_general | solution.py:723
  28.8 2.7 collective-permute-start.32
  35.6 3.2 collective-permute-start.33
  38.8 3.3 collective-permute-done.33
  43.9 2.6 fusion.22
  46.7 4.7 landmark.1
  54.4 2.6 join.4
  60.4 6.0 %pinv.1 = (f32[3,64,64]{2,1,0:T(8,128)}, f32[3,64,64]{2,1,0:T(8,128)}, f32[72,64,64]{2,1,0:T(8,128)}) custom-call(f32[3,64,64]{2,1,0:T(8,128)S(1)} %bitcast.70, f32[3,64,64]{2,1,0:T(8,128)S(1)} %bitcast.68), custom_call_target="tpu_custom_call" | custom-call | tf_op jit(solution)/shard_map/pinv/pallas_call | solution.py:763
  68.3 2.2 join.5.a_ref
  72.7 4.5 collective-permute-done.37
  77.9 2.3 join.6.a_ref
  81.2 4.3 collective-permute-start.38
  85.5 7.4 %collective-permute-done.38 = bf16[64,1280]{1,0:T(8,128)(2,1)S(1)} collective-permute-done((bf16[64,1280]{1,0:T(8,128)(2,1)S(1)}, bf16[64,1280]{1,0:T(8,128)(2,1)S(1)}, u32[]{:S(2)}, u32[]{:S(2)}) %collective-permute-start.38) | collective-permute-done | bytes 163872 | tf_op jit(solution)/shard_map/ppermute | solution.py:27
  96.5 4.5 collective-permute-done.39
  104.9 9.0 %token_.1 = (bf16[1024,768]{1,0:T(8,128)(2,1)}, bf16[768,1024]{1,0:T(8,128)(2,1)S(1)}) custom-call(s32[8]{0:T(128)S(1)} %add_subtract_fusion.refs_0_, bf16[1024,2304]{1,0:T(8,128)(2,1)} %copy-done.3, bf16[1152,768]{1,0:T(8,128)(2,1)S(1)} %copy-done.4, bf16[256,768]{1,0:T(8,128)(2,1)S(1)} %slice.192.refs_3_.refs_4_, ...), custom_call_target="tpu_custom_call" | custom-call | tf_op jit(solution)/shard_map/token/pallas_call | solution.py:791
  114.6 40.3 %ffn.1 = (f32[1024,768]{1,0:T(8,128)}, f32[1024,768]{1,0:T(8,128)}, bf16[1024,3072]{1,0:T(8,128)(2,1)}, bf16[1024,3072]{1,0:T(8,128)(2,1)}, bf16[1024,768]{1,0:T...) custom-call(bf16[1024,768]{1,0:T(8,128)(2,1)} %bitcast.66, ...), custom_call_target="tpu_custom_call" | custom-call | tf_op jit(solution)/shard_map/ffn/pallas_call | solution.py:813
  154.9 8.1 %token_back.1 = (bf16[1024,768]{1,0:T(8,128)(2,1)}, f32[256,768]{1,0:T(8,128)S(1)}, f32[256,768]{1,0:T(8,128)}) custom-call(s32[8]{0:T(128)S(1)} %add_subtract_fusion.refs_0_, bf16[1024,2304]{1,0:T(8,128)(2,1)} %copy-done.3, bf16[1024,768]{1,0:T(8,128)(2,1)} %get-tuple-element.170.refs_2_, bf16[768,1024]{1,0:T(8,128)(2,1)S(1)} %get-tuple-element.171.refs_3_, ...), custom_call_target="tpu_custom_call" | custom-call | tf_op jit(solution)/shard_map/token_back/pallas_call | solution.py:837
  163.1 6.9 %convolution_convert_fusion.3 = bf16[3072,768]{1,0:T(8,128)(2,1)} fusion(bf16[1024,3072]{1,0:T(8,128)(2,1)S(1)} %copy-done.61, bf16[1024,768]{1,0:T(8,128)(2,1)S(1)} %copy-done.63), kind=kOutput, calls=%fused_computation.67 | convolution fusion | flops 4834197504 | bytes 12582912 | tf_op jit(solution)/shard_map/dot_general | solution.py:853
  170.0 6.8 %convolution_convert_fusion.2 = bf16[768,3072]{1,0:T(8,128)(2,1)} fusion(bf16[1024,768]{1,0:T(8,128)(2,1)S(1)} %copy-done.62, bf16[1024,3072]{1,0:T(8,128)(2,1)S(1)} %bitcast.88), kind=kOutput, calls=%fused_computation.66 | convolution fusion | flops 4834197504 | bytes 12582912 | tf_op jit(solution)/shard_map/dot_general | solution.py:854
  177.5 233.8 %conditional.1 = (bf16[192,768]{1,0:T(8,128)(2,1)}, bf16[112,768]{1,0:T(8,128)(2,1)}, bf16[256,768]{1,0:T(8,128)(2,1)}, bf16[1024,768]{1,0:T(8,128)(2,1)}, bf16[1024,768]{1,0:T(8,128)(2,1)}) conditional(s32[]{:T(128)} %bitcast.24, () %tuple.31, (bf16[256,768]{1,0:T(8,128)(2,1)S(1)}, bf16[1024,768]{1,0:T(8,128)(2,1)}, f32[12,33]{1,0:T(8,128)S(1)}, ...), branch_computations={%region_3.4_spmd, %region_4.9_spmd} | conditional | flops 6091719680 | bytes 216654144 | solution.py:991
  179.3 2.9 collective-permute-start.4
  185.8 4.8 fusion.43
  192.0 4.5 convolution_convert_fusion.1
  198.7 10.3 %collective-permute-start.3 = (bf16[64,768]{1,0:T(8,128)(2,1)}, bf16[64,768]{1,0:T(8,128)(2,1)}, u32[]{:S(2)}, u32[]{:S(2)}) collective-permute-start(bf16[64,768]{1,0:T(8,128)(2,1)} %add_convert_fusion.15), channel_id=1, source_target_pairs={{0,8},{1,9},{2,10},{3,11},{4,12},{5,13},{6,14},{7,15},{8,0},{9,1},... | collective-permute-start | bytes 294920 | tf_op jit(solution)/shard_map/cond/branch_1_fun/ppermute | solution.py:27
  210.1 5.2 %conv_back.1 = (f32[1024,768]{1,0:T(8,128)S(1)}, f32[1536,256]{1,0:T(8,128)S(1)}) custom-call(s32[8]{0:T(128)S(1)} %get-tuple-element.52.refs_0_, bf16[1152,768]{1,0:T(8,128)(2,1)S(1)} %maximum_maximum_fusion.1.refs_1_, bf16[1152,768]{1,0:T(8,128)(2,1)S(1)} %copy-done.6, f32[12,256]{1,0:T(8,128)S(1)} %pad.18.refs_3_), custom_call_target="tpu_custom_call" | custom-call | tf_op jit(solution)/shard_map/cond/branch_1_fun/conv_back/pallas_call | solution.py:865
  216.5 3.6 reshape.144
  220.0 2.5 pad.19
  222.6 4.3 reshape.145
  230.1 2.1 mix_back.1
  234.1 3.0 collective-permute-done.6
  243.8 2.3 convert_reduce_fusion
  249.4 8.4 %landmark_back.1 = (bf16[1024,768]{1,0:T(8,128)(2,1)}, bf16[1024,768]{1,0:T(8,128)(2,1)}, f32[256,768]{1,0:T(8,128)S(1)}) custom-call(s32[8]{0:T(128)} %copy-done.41, bf16[1024,2304]{1,0:T(8,128)(2,1)} %get-tuple-element.53.refs_1_.refs_2_, bf16[1024,2304]{1,0:T(8,128)(2,1)} %get-tuple-element.53.refs_1_.refs_2_, f32[1024,768]{1,0:T(8,128)S(1)} %get-tuple-element.60.refs_3_, ...), custom_call_target="tpu_custom_call" | custom-call | tf_op jit(solution)/shard_map/cond/branch_1_fun/landmark_back/pallas_call | solution.py:890
  260.4 3.4 fusion.3
  266.4 10.0 %pinv_back.1 = (f32[3,64,64]{2,1,0:T(8,128)}, f32[3,64,64]{2,1,0:T(8,128)}) custom-call(f32[3,64,64]{2,1,0:T(8,128)S(1)} %copy-done.33, f32[3,64,64]{2,1,0:T(8,128)S(1)} %copy-done.31, f32[3,64,64]{2,1,0:T(8,128)S(1)} %copy-done.38, f32[72,64,64]{2,1,0:T(8,128)} %get-tuple-element.72.refs_3_, bf16[3,64,64]{2,1,0:T(8,128)(2,1)} %bitcast.80, ...), custom_call_target="tpu_custom_call" | custom-call | tf_op jit(solution)/shard_map/cond/branch_1_fun/pinv_back/pallas_call | solution.py:915
  280.2 3.0 dynamic_update_slice.11
  284.4 2.9 dynamic_update_slice.9
  290.8 3.0 fusion.44
  295.1 6.2 %maximum_maximum_fusion = bf16[1792,768]{1,0:T(8,128)(2,1)S(1)} fusion(bf16[768,768]{1,0:T(8,128)(2,1)S(1)} %fusion.4, bf16[128,768]{1,0:T(8,128)(2,1)S(1)} %pad.21, bf16[768,768]{1,0:T(8,128)(2,1)S(1)} %fusion, bf16[1792]{0:T(1024)(128)(2,1)S(1)} %copy-done.44), kind=kLoop, calls=%fused_computation.1 | loop fusion | flops 11010048 | bytes 5312000 | tf_op jit(solution)/shard_map/cond/branch_1_fun/concatenate | solution.py:960
  303.0 2.6 fusion.8
  308.6 3.5 collective-permute-start.10
  315.0 13.3 %collective-permute-done.10 = bf16[384,768]{1,0:T(8,128)(2,1)} collective-permute-done((bf16[384,768]{1,0:T(8,128)(2,1)S(1)}, bf16[384,768]{1,0:T(8,128)(2,1)}, u32[]{:S(2)}, u32[]{:S(2)}) %collective-permute-start.10) | collective-permute-done | bytes 589856 | tf_op jit(solution)/shard_map/cond/branch_1_fun/ppermute | solution.py:27
  332.2 4.2 collective-permute-done.12
  336.4 11.2 %collective-permute-done.13 = bf16[192,768]{1,0:T(8,128)(2,1)S(1)} collective-permute-done((bf16[192,768]{1,0:T(8,128)(2,1)S(1)}, bf16[192,768]{1,0:T(8,128)(2,1)S(1)}, u32[]{:S(2)}, u32[]{:S(2)}) %collective-permute-start.13) | collective-permute-done | bytes 294944 | tf_op jit(solution)/shard_map/cond/branch_1_fun/ppermute | solution.py:27
  347.7 11.5 %collective-permute-done.14 = bf16[448,768]{1,0:T(8,128)(2,1)S(1)} collective-permute-done((bf16[448,768]{1,0:T(8,128)(2,1)S(1)}, bf16[448,768]{1,0:T(8,128)(2,1)S(1)}, u32[]{:S(2)}, u32[]{:S(2)}) %collective-permute-start.14) | collective-permute-done | bytes 688160 | tf_op jit(solution)/shard_map/cond/branch_1_fun/ppermute | solution.py:27
  364.1 4.2 collective-permute-done.15
  368.3 5.0 %collective-permute-done.16 = bf16[96,768]{1,0:T(8,128)(2,1)S(1)} collective-permute-done((bf16[96,768]{1,0:T(8,128)(2,1)S(1)}, bf16[96,768]{1,0:T(8,128)(2,1)S(1)}, u32[]{:S(2)}, u32[]{:S(2)}) %collective-permute-start.16) | collective-permute-done | bytes 147488 | tf_op jit(solution)/shard_map/cond/branch_1_fun/ppermute | solution.py:27
  373.4 3.0 collective-permute-start.19
  378.1 4.8 collective-permute-done.19
  382.8 4.0 collective-permute-done.18
  386.9 4.4 collective-permute-done.20
  395.0 4.2 collective-permute-done.22
  399.2 3.1 collective-permute-done.23
  403.9 4.9 %collective-permute-done.26 = bf16[56,768]{1,0:T(8,128)(2,1)S(1)} collective-permute-done((bf16[56,768]{1,0:T(8,128)(2,1)S(1)}, bf16[56,768]{1,0:T(8,128)(2,1)S(1)}, u32[]{:S(2)}, u32[]{:S(2)}) %collective-permute-start.26) | collective-permute-done | bytes 86048 | tf_op jit(solution)/shard_map/cond/branch_1_fun/ppermute | solution.py:27
  413.5 3.5 collective-permute-done.43
  427.3 6.7 %fusion.16 = f32[1024,768]{1,0:T(8,128)S(1)} fusion(bf16[768,2304]{1,0:T(8,128)(2,1)} %param.21, bf16[1024,768]{1,0:T(8,128)(2,1)} %get-tuple-element.189, bf16[1024,768]{1,0:T(8,128)(2,1)} %get-tuple-element.188, bf16[1024,768]{1,0:T(8,128)(2,1)S(1)} %copy-done.26), kind=kOutput, calls=%fused_computation.68 | convolution fusion | flops 3638034432 | bytes 11403264 | tf_op jit(solution)/shard_map/dot_general | solution.py:1001
  434.1 3.6 add_add_fusion
  439.4 6.9 %collective-permute-done.45 = bf16[448,768]{1,0:T(8,128)(2,1)S(1)} collective-permute-done((bf16[448,768]{1,0:T(8,128)(2,1)S(1)}, bf16[448,768]{1,0:T(8,128)(2,1)S(1)}, u32[]{:S(2)}, u32[]{:S(2)}) %collective-permute-start.45) | collective-permute-done | bytes 688160 | tf_op jit(solution)/shard_map/ppermute | solution.py:27
  446.9 7.3 %convert_element_type.344 = f32[3072,768]{1,0:T(8,128)} convert(bf16[3072,768]{1,0:T(8,128)(2,1)} %get-tuple-element.207) | non-fusion elementwise | flops 2359296 | bytes 14155776 | tf_op jit(solution)/shard_map/convert_element_type | solution.py:997
  454.3 5.0 %convert_element_type.345 = f32[768,3072]{1,0:T(8,128)} convert(bf16[768,3072]{1,0:T(8,128)(2,1)S(1)} %copy-done.15) | non-fusion elementwise | flops 2359296 | bytes 14155776 | tf_op jit(solution)/shard_map/convert_element_type | solution.py:997
  459.8 2.3 collective-permute-done.47.early_other_ref
  467.2 7.6 %settle_qkv.1 = f32[768,2304]{1,0:T(8,128)} custom-call(s32[1]{0:T(128)} %bitcast.26.side_ref, bf16[896,768]{1,0:T(8,128)(2,1)} %copy-done.12, bf16[896,768]{1,0:T(8,128)(2,1)} %copy-done.23, bf16[768,768]{1,0:T(8,128)(2,1)} %copy-done.7, bf16[768,768]{1,0:T(8,128)(2,1)} %copy-done.14), custom_call_target="tpu_custom_call" | custom-call | tf_op jit(solution)/shard_map/settle_qkv/pallas_call | solution.py:660
  (362 shorter events, 121.3 us)
Async XLA Ops:
  7.2 439.7 %all-reduce.9.cloned.1.call-start = ((), (), s32[]{:S(2)}) async-start(), calls=%async_computation | async-start | bytes 18874368 | tf_op jit(solution)/shard_map/psum | solution.py:858
  13.1 1.6 collective-permute-start.29
  14.8 6.0 %collective-permute-start.30 = (bf16[64,768]{1,0:T(8,128)(2,1)S(1)}, bf16[64,768]{1,0:T(8,128)(2,1)S(1)}, u32[]{:S(2)}, u32[]{:S(2)}) collective-permute-start(bf16[64,768]{1,0:T(8,128)(2,1)S(1)} %constant_dynamic-slice_fusion.20), channel_id=1, source_target_pairs={{0,2},{1,3},{2,0},{3,1},{4,6},{5,7},{6,4},{7,5},{8,10},{9,11},{10,... | collective-permute-start | bytes 294920 | tf_op jit(solution)/shard_map/ppermute | solution.py:27
  20.8 7.9 %collective-permute-start.31 = (bf16[64,768]{1,0:T(8,128)(2,1)S(1)}, bf16[64,768]{1,0:T(8,128)(2,1)S(1)}, u32[]{:S(2)}, u32[]{:S(2)}) collective-permute-start(bf16[64,768]{1,0:T(8,128)(2,1)S(1)} %add_convert_fusion.24), channel_id=1, source_target_pairs={{0,4},{1,5},{2,6},{3,7},{4,0},{5,1},{6,2},{7,3},{8,12},{9,13},{10,... | collective-permute-start | bytes 294920 | tf_op jit(solution)/shard_map/ppermute | solution.py:27
  28.8 6.8 %collective-permute-start.32 = (bf16[64,768]{1,0:T(8,128)(2,1)S(1)}, bf16[64,768]{1,0:T(8,128)(2,1)S(1)}, u32[]{:S(2)}, u32[]{:S(2)}) collective-permute-start(bf16[64,768]{1,0:T(8,128)(2,1)S(1)} %add_convert_fusion.23), channel_id=1, source_target_pairs={{0,8},{1,9},{2,10},{3,11},{4,12},{5,13},{6,14},{7,15},{8,0},{9,1},... | collective-permute-start | bytes 294920 | tf_op jit(solution)/shard_map/ppermute | solution.py:27
  31.5 10.8 %collective-permute-start.27 = (bf16[16,768]{1,0:T(8,128)(2,1)S(1)}, bf16[16,768]{1,0:T(8,128)(2,1)S(1)}, u32[]{:S(2)}, u32[]{:S(2)}) collective-permute-start(bf16[16,768]{1,0:T(8,128)(2,1)S(1)} %get-tuple-element.215), channel_id=1, source_target_pairs={{0,1},{1,2},{2,3},{3,4},{4,5},{5,6},{6,7},{7,8},{8,9},{9,10},{10,1... | collective-permute-start | bytes 73736 | tf_op jit(solution)/shard_map/ppermute | solution.py:141
  32.7 9.5 %collective-permute-start.28 = (bf16[16,768]{1,0:T(8,128)(2,1)S(1)}, bf16[16,768]{1,0:T(8,128)(2,1)S(1)}, u32[]{:S(2)}, u32[]{:S(2)}) collective-permute-start(bf16[16,768]{1,0:T(8,128)(2,1)S(1)} %get-tuple-element.216), channel_id=1, source_target_pairs={{1,0},{2,1},{3,2},{4,3},{5,4},{6,5},{7,6},{8,7},{9,8},{10,9},{11,1... | collective-permute-start | bytes 73736 | tf_op jit(solution)/shard_map/ppermute | solution.py:143
  35.6 6.5 %collective-permute-start.33 = (bf16[64,768]{1,0:T(8,128)(2,1)S(1)}, bf16[64,768]{1,0:T(8,128)(2,1)S(1)}, u32[]{:S(2)}, u32[]{:S(2)}) collective-permute-start(bf16[64,768]{1,0:T(8,128)(2,1)S(1)} %add_convert_fusion.22), channel_id=1, source_target_pairs={{0,2},{1,3},{2,0},{3,1},{4,6},{5,7},{6,4},{7,5},{8,10},{9,11},{10,... | collective-permute-start | bytes 294920 | tf_op jit(solution)/shard_map/ppermute | solution.py:27
  42.2 1.7 collective-permute-start.34
  52.1 1.6 collective-permute-start.35
  57.3 20.0 %copy-start.30 = (f32[64,3,64]{2,0,1:T(8,128)}, f32[64,3,64]{2,0,1:T(8,128)S(1)}, u32[]{:S(2)}) copy-start(f32[64,3,64]{2,0,1:T(8,128)S(1)} %copy.46) | copy-start | bytes 147460
  57.5 19.8 %copy-start.32 = (f32[64,3,64]{2,0,1:T(8,128)}, f32[64,3,64]{2,0,1:T(8,128)S(1)}, u32[]{:S(2)}) copy-start(f32[64,3,64]{2,0,1:T(8,128)S(1)} %copy.44) | copy-start | bytes 147460
  59.1 8.5 %collective-permute-start.36 = (bf16[64,896]{1,0:T(8,128)(2,1)S(1)}, bf16[64,896]{1,0:T(8,128)(2,1)S(1)}, u32[]{:S(2)}, u32[]{:S(2)}) collective-permute-start(bf16[64,896]{1,0:T(8,128)(2,1)S(1)} %get-tuple-element.219), channel_id=1, source_target_pairs={{0,2},{1,3},{2,0},{3,1},{4,6},{5,7},{6,4},{7,5},{8,10},{9,11},{10,... | collective-permute-start | bytes 344072 | tf_op jit(solution)/shard_map/ppermute | solution.py:27
  67.4 34.7 %copy-start.53 = (f32[768]{0:T(1024)S(1)}, f32[768]{0:T(1024)}, u32[]{:S(2)}) copy-start(f32[768]{0:T(1024)} %param.26) | copy-start | bytes 9220
  67.4 34.7 %copy-start.54 = (f32[768]{0:T(1024)S(1)}, f32[768]{0:T(1024)}, u32[]{:S(2)}) copy-start(f32[768]{0:T(1024)} %param.27) | copy-start | bytes 9220
  67.4 34.7 %copy-start.55 = (f32[768]{0:T(1024)S(1)}, f32[768]{0:T(1024)}, u32[]{:S(2)}) copy-start(f32[768]{0:T(1024)} %param.28) | copy-start | bytes 9220
  67.5 34.7 %copy-start.56 = (f32[768]{0:T(1024)S(1)}, f32[768]{0:T(1024)}, u32[]{:S(2)}) copy-start(f32[768]{0:T(1024)} %param.32) | copy-start | bytes 9220
  67.5 34.7 %copy-start.57 = (f32[768]{0:T(1024)S(1)}, f32[768]{0:T(1024)}, u32[]{:S(2)}) copy-start(f32[768]{0:T(1024)} %param.33) | copy-start | bytes 9220
  67.5 34.8 %copy-start.58 = (f32[768]{0:T(1024)S(1)}, f32[768]{0:T(1024)}, u32[]{:S(2)}) copy-start(f32[768]{0:T(1024)} %param.34) | copy-start | bytes 9220
  68.2 34.7 %copy-start.39 = (f32[12,33]{1,0:T(8,128)S(1)}, f32[12,33]{1,0:T(8,128)}, u32[]{:S(2)}) copy-start(f32[12,33]{1,0:T(8,128)} %param.24) | copy-start | bytes 4756
  71.3 5.9 %collective-permute-start.37 = (bf16[64,1088]{1,0:T(8,128)(2,1)S(1)}, bf16[64,1088]{1,0:T(8,128)(2,1)S(1)}, u32[]{:S(2)}, u32[]{:S(2)}) collective-permute-start(bf16[64,1088]{1,0:T(8,128)(2,1)S(1)} %pad_maximum_fusion.2), channel_id=1, source_target_pairs={{0,4},{1,5},{2,6},{3,7},{4,0},{5,1},{6,2},{7,3},{8,12},{9,13},{10,... | collective-permute-start | bytes 417800 | tf_op jit(solution)/shard_map/ppermute | solution.py:27
  77.9 27.0 %copy-start.4 = (bf16[1152,768]{1,0:T(8,128)(2,1)S(1)}, bf16[1152,768]{1,0:T(8,128)(2,1)}, u32[]{:S(2)}) copy-start(bf16[1152,768]{1,0:T(8,128)(2,1)} %maximum_maximum_fusion.2.refs_2_) | copy-start | bytes 5308420
  81.2 11.7 %collective-permute-start.38 = (bf16[64,1280]{1,0:T(8,128)(2,1)S(1)}, bf16[64,1280]{1,0:T(8,128)(2,1)S(1)}, u32[]{:S(2)}, u32[]{:S(2)}) collective-permute-start(bf16[64,1280]{1,0:T(8,128)(2,1)S(1)} %pad_maximum_fusion.1), channel_id=1, source_target_pairs={{0,8},{1,9},{2,10},{3,11},{4,12},{5,13},{6,14},{7,15},{8,0},{9,1},... | collective-permute-start | bytes 491528 | tf_op jit(solution)/shard_map/ppermute | solution.py:27
  96.0 5.0 %collective-permute-start.39 = (bf16[64,896]{1,0:T(8,128)(2,1)}, bf16[64,896]{1,0:T(8,128)(2,1)S(1)}, u32[]{:S(2)}, u32[]{:S(2)}) collective-permute-start(bf16[64,896]{1,0:T(8,128)(2,1)} %mix.1), channel_id=1, source_target_pairs={{0,2},{1,3},{2,0},{3,1},{4,6},{5,7},{6,4},{7,5},{8,10},{9,11},{10,... | collective-permute-start | bytes 344072 | tf_op jit(solution)/shard_map/ppermute | solution.py:27
  102.0 1.7 collective-permute-start.40
  177.6 19.1 %copy-start.22 = (bf16[64,896]{1,0:T(8,128)(2,1)}, bf16[64,896]{1,0:T(8,128)(2,1)S(1)}, u32[]{:S(2)}) copy-start(bf16[64,896]{1,0:T(8,128)(2,1)S(1)} %get-tuple-element.63.stat_ref) | copy-start | bytes 344068 | tf_op jit(solution)/shard_map/cond
  177.6 32.6 %copy-start.41 = (s32[8]{0:T(128)}, s32[8]{0:T(128)S(1)}, u32[]{:S(2)}) copy-start(s32[8]{0:T(128)S(1)} %get-tuple-element.52.refs_0_) | copy-start | bytes 100 | tf_op jit(solution)/shard_map/cond
  177.6 6.1 %collective-permute-start = (bf16[128,768]{1,0:T(8,128)(2,1)S(1)}, bf16[128,768]{1,0:T(8,128)(2,1)S(1)}, u32[]{:S(2)}, u32[]{:S(2)}) collective-permute-start(bf16[128,768]{1,0:T(8,128)(2,1)S(1)} %constant_dynamic-slice_fusion.15), channel_id=1, source_target_pairs={{0,1},{1,0},{2,3},{3,2},{4,5},{5,4},{6,7},{7,6},{8,9},{9,8},{10,11... | collective-permute-start | bytes 589832 | tf_op jit(solution)/shard_map/cond/branch_1_fun/ppermute | solution.py:27
  179.3 29.7 %collective-permute-start.4 = (bf16[16,768]{1,0:T(8,128)(2,1)}, bf16[16,768]{1,0:T(8,128)(2,1)}, u32[]{:S(2)}, u32[]{:S(2)}) collective-permute-start(bf16[16,768]{1,0:T(8,128)(2,1)} %get-tuple-element.209), channel_id=1, source_target_pairs={{0,1},{1,2},{2,3},{3,4},{4,5},{5,6},{6,7},{7,8},{8,9},{9,10},{10,1... | collective-permute-start | bytes 73736 | tf_op jit(solution)/shard_map/cond/branch_1_fun/ppermute | solution.py:141
  182.2 26.8 %collective-permute-start.5 = (bf16[16,768]{1,0:T(8,128)(2,1)}, bf16[16,768]{1,0:T(8,128)(2,1)}, u32[]{:S(2)}, u32[]{:S(2)}) collective-permute-start(bf16[16,768]{1,0:T(8,128)(2,1)} %get-tuple-element.210), channel_id=1, source_target_pairs={{1,0},{2,1},{3,2},{4,3},{5,4},{6,5},{7,6},{8,7},{9,8},{10,9},{11,1... | collective-permute-start | bytes 73736 | tf_op jit(solution)/shard_map/cond/branch_1_fun/ppermute | solution.py:143
  183.8 6.8 %collective-permute-start.1 = (bf16[64,768]{1,0:T(8,128)(2,1)S(1)}, bf16[64,768]{1,0:T(8,128)(2,1)S(1)}, u32[]{:S(2)}, u32[]{:S(2)}) collective-permute-start(bf16[64,768]{1,0:T(8,128)(2,1)S(1)} %constant_dynamic-slice_fusion.14), channel_id=1, source_target_pairs={{0,2},{1,3},{2,0},{3,1},{4,6},{5,7},{6,4},{7,5},{8,10},{9,11},{10,... | collective-permute-start | bytes 294920 | tf_op jit(solution)/shard_map/cond/branch_1_fun/ppermute | solution.py:27
  190.6 7.5 %collective-permute-start.2 = (bf16[64,768]{1,0:T(8,128)(2,1)S(1)}, bf16[64,768]{1,0:T(8,128)(2,1)S(1)}, u32[]{:S(2)}, u32[]{:S(2)}) collective-permute-start(bf16[64,768]{1,0:T(8,128)(2,1)S(1)} %add_convert_fusion.16), channel_id=1, source_target_pairs={{0,4},{1,5},{2,6},{3,7},{4,0},{5,1},{6,2},{7,3},{8,12},{9,13},{10,... | collective-permute-start | bytes 294920 | tf_op jit(solution)/shard_map/cond/branch_1_fun/ppermute | solution.py:27
  192.0 17.0 %copy-start.11 = (bf16[1024,768]{1,0:T(8,128)(2,1)S(1)}, bf16[1024,768]{1,0:T(8,128)(2,1)}, u32[]{:S(2)}) copy-start(bf16[1024,768]{1,0:T(8,128)(2,1)} %get-tuple-element.55) | copy-start | bytes 4718596 | tf_op jit(solution)/shard_map/cond
  198.7 29.7 %collective-permute-start.3 = (bf16[64,768]{1,0:T(8,128)(2,1)}, bf16[64,768]{1,0:T(8,128)(2,1)}, u32[]{:S(2)}, u32[]{:S(2)}) collective-permute-start(bf16[64,768]{1,0:T(8,128)(2,1)} %add_convert_fusion.15), channel_id=1, source_target_pairs={{0,8},{1,9},{2,10},{3,11},{4,12},{5,13},{6,14},{7,15},{8,0},{9,1},... | collective-permute-start | bytes 294920 | tf_op jit(solution)/shard_map/cond/branch_1_fun/ppermute | solution.py:27
  232.2 5.0 %collective-permute-start.6 = (bf16[64,896]{1,0:T(8,128)(2,1)}, bf16[64,896]{1,0:T(8,128)(2,1)S(1)}, u32[]{:S(2)}, u32[]{:S(2)}) collective-permute-start(bf16[64,896]{1,0:T(8,128)(2,1)} %mix_back.1), channel_id=1, source_target_pairs={{0,2},{1,3},{2,0},{3,1},{4,6},{5,7},{6,4},{7,5},{8,10},{9,11},{10,... | collective-permute-start | bytes 344072 | tf_op jit(solution)/shard_map/cond/branch_1_fun/ppermute | solution.py:27
  238.9 9.1 %collective-permute-start.7 = (bf16[128,896]{1,0:T(8,128)(2,1)}, bf16[128,896]{1,0:T(8,128)(2,1)}, u32[]{:S(2)}, u32[]{:S(2)}) collective-permute-start(bf16[128,896]{1,0:T(8,128)(2,1)} %maximum_select_fusion.3), channel_id=1, source_target_pairs={{0,1},{1,0},{2,3},{3,2},{4,5},{5,4},{6,7},{7,6},{8,9},{9,8},{10,11... | collective-permute-start | bytes 688136 | tf_op jit(solution)/shard_map/cond/branch_1_fun/ppermute | solution.py:27
  264.6 24.4 %copy-start.8 = (bf16[1536,768]{1,0:T(8,128)(2,1)}, bf16[1536,768]{1,0:T(8,128)(2,1)S(1)}, u32[]{:S(2)}) copy-start(bf16[1536,768]{1,0:T(8,128)(2,1)S(1)} %pad_maximum_fusion) | copy-start | bytes 7077892 | tf_op jit(solution)/shard_map/cond
  290.1 15.7 %collective-permute-start.9 = (bf16[768,768]{1,0:T(8,128)(2,1)}, bf16[768,768]{1,0:T(8,128)(2,1)}, u32[]{:S(2)}, u32[]{:S(2)}) collective-permute-start(bf16[768,768]{1,0:T(8,128)(2,1)} %constant_dynamic-slice_fusion.10), channel_id=1, source_target_pairs={{0,1},{1,0},{2,3},{3,2},{4,5},{5,4},{6,7},{7,6},{8,9},{9,8},{10,11... | collective-permute-start | bytes 3538952 | tf_op jit(solution)/shard_map/cond/branch_1_fun/ppermute | solution.py:27
  302.4 10.8 %collective-permute-start.11 = (bf16[896,768]{1,0:T(8,128)(2,1)}, bf16[896,768]{1,0:T(8,128)(2,1)}, u32[]{:S(2)}, u32[]{:S(2)}) collective-permute-start(bf16[896,768]{1,0:T(8,128)(2,1)} %constant_dynamic-slice_fusion.8), channel_id=1, source_target_pairs={{0,1},{1,0},{2,3},{3,2},{4,5},{5,4},{6,7},{7,6},{8,9},{9,8},{10,11... | collective-permute-start | bytes 4128776 | tf_op jit(solution)/shard_map/cond/branch_1_fun/ppermute | solution.py:27
  305.7 6.4 %collective-permute-start.8 = (bf16[128,768]{1,0:T(8,128)(2,1)S(1)}, bf16[128,768]{1,0:T(8,128)(2,1)}, u32[]{:S(2)}, u32[]{:S(2)}) collective-permute-start(bf16[128,768]{1,0:T(8,128)(2,1)S(1)} %constant_dynamic-slice_fusion.11), channel_id=1, source_target_pairs={{0,1},{1,0},{2,3},{3,2},{4,5},{5,4},{6,7},{7,6},{8,9},{9,8},{10,11... | collective-permute-start | bytes 589832 | tf_op jit(solution)/shard_map/cond/branch_1_fun/ppermute | solution.py:27
  308.6 19.7 %collective-permute-start.10 = (bf16[384,768]{1,0:T(8,128)(2,1)S(1)}, bf16[384,768]{1,0:T(8,128)(2,1)}, u32[]{:S(2)}, u32[]{:S(2)}) collective-permute-start(bf16[384,768]{1,0:T(8,128)(2,1)S(1)} %constant_dynamic-slice_fusion.9), channel_id=1, source_target_pairs={{0,16},{16,0},{1,17},{17,1},{2,18},{18,2},{3,19},{19,3},{4,20},{20... | collective-permute-start | bytes 1769480 | tf_op jit(solution)/shard_map/cond/branch_1_fun/ppermute | solution.py:27
  329.6 29.6 %collective-permute-start.14 = (bf16[448,768]{1,0:T(8,128)(2,1)S(1)}, bf16[448,768]{1,0:T(8,128)(2,1)S(1)}, u32[]{:S(2)}, u32[]{:S(2)}) collective-permute-start(bf16[448,768]{1,0:T(8,128)(2,1)S(1)} %constant_dynamic-slice_fusion.5), channel_id=1, source_target_pairs={{0,16},{16,0},{1,17},{17,1},{2,18},{18,2},{3,19},{19,3},{4,20},{20... | collective-permute-start | bytes 2064392 | tf_op jit(solution)/shard_map/cond/branch_1_fun/ppermute | solution.py:27
  330.0 6.4 %collective-permute-start.12 = (bf16[64,768]{1,0:T(8,128)(2,1)S(1)}, bf16[64,768]{1,0:T(8,128)(2,1)S(1)}, u32[]{:S(2)}, u32[]{:S(2)}) collective-permute-start(bf16[64,768]{1,0:T(8,128)(2,1)S(1)} %constant_dynamic-slice_fusion.7), channel_id=1, source_target_pairs={{0,2},{1,3},{2,0},{3,1},{4,6},{5,7},{6,4},{7,5},{8,10},{9,11},{10,... | collective-permute-start | bytes 294920 | tf_op jit(solution)/shard_map/cond/branch_1_fun/ppermute | solution.py:27
  331.8 15.8 %collective-permute-start.13 = (bf16[192,768]{1,0:T(8,128)(2,1)S(1)}, bf16[192,768]{1,0:T(8,128)(2,1)S(1)}, u32[]{:S(2)}, u32[]{:S(2)}) collective-permute-start(bf16[192,768]{1,0:T(8,128)(2,1)S(1)} %constant_dynamic-slice_fusion.6), channel_id=1, source_target_pairs={{0,2},{1,3},{2,0},{3,1},{4,6},{5,7},{6,4},{7,5},{8,10},{9,11},{10,... | collective-permute-start | bytes 884744 | tf_op jit(solution)/shard_map/cond/branch_1_fun/ppermute | solution.py:27
  360.5 7.8 %collective-permute-start.15 = (bf16[64,768]{1,0:T(8,128)(2,1)S(1)}, bf16[64,768]{1,0:T(8,128)(2,1)S(1)}, u32[]{:S(2)}, u32[]{:S(2)}) collective-permute-start(bf16[64,768]{1,0:T(8,128)(2,1)S(1)} %add_convert_fusion.13), channel_id=1, source_target_pairs={{0,4},{1,5},{2,6},{3,7},{4,0},{5,1},{6,2},{7,3},{8,12},{9,13},{10,... | collective-permute-start | bytes 294920 | tf_op jit(solution)/shard_map/cond/branch_1_fun/ppermute | solution.py:27
  362.1 11.2 %collective-permute-start.16 = (bf16[96,768]{1,0:T(8,128)(2,1)S(1)}, bf16[96,768]{1,0:T(8,128)(2,1)S(1)}, u32[]{:S(2)}, u32[]{:S(2)}) collective-permute-start(bf16[96,768]{1,0:T(8,128)(2,1)S(1)} %constant_dynamic-slice_fusion.4), channel_id=1, source_target_pairs={{0,4},{1,5},{2,6},{3,7},{4,0},{5,1},{6,2},{7,3},{8,12},{9,13},{10,... | collective-permute-start | bytes 442376 | tf_op jit(solution)/shard_map/cond/branch_1_fun/ppermute | solution.py:27
  362.7 10.7 %collective-permute-start.17 = (bf16[224,768]{1,0:T(8,128)(2,1)S(1)}, bf16[224,768]{1,0:T(8,128)(2,1)S(1)}, u32[]{:S(2)}, u32[]{:S(2)}) collective-permute-start(bf16[224,768]{1,0:T(8,128)(2,1)S(1)} %constant_dynamic-slice_fusion.3), channel_id=1, source_target_pairs={{0,2},{1,3},{2,0},{3,1},{4,6},{5,7},{6,4},{7,5},{8,10},{9,11},{10,... | collective-permute-start | bytes 1032200 | tf_op jit(solution)/shard_map/cond/branch_1_fun/ppermute | solution.py:27
  373.4 9.4 %collective-permute-start.19 = (bf16[48,768]{1,0:T(8,128)(2,1)S(1)}, bf16[48,768]{1,0:T(8,128)(2,1)S(1)}, u32[]{:S(2)}, u32[]{:S(2)}) collective-permute-start(bf16[48,768]{1,0:T(8,128)(2,1)S(1)} %constant_dynamic-slice_fusion.2), channel_id=1, source_target_pairs={{0,8},{1,9},{2,10},{3,11},{4,12},{5,13},{6,14},{7,15},{8,0},{9,1},... | collective-permute-start | bytes 221192 | tf_op jit(solution)/shard_map/cond/branch_1_fun/ppermute | solution.py:27
  376.4 10.4 %collective-permute-start.18 = (bf16[64,768]{1,0:T(8,128)(2,1)S(1)}, bf16[64,768]{1,0:T(8,128)(2,1)S(1)}, u32[]{:S(2)}, u32[]{:S(2)}) collective-permute-start(bf16[64,768]{1,0:T(8,128)(2,1)S(1)} %add_convert_fusion.12), channel_id=1, source_target_pairs={{0,8},{1,9},{2,10},{3,11},{4,12},{5,13},{6,14},{7,15},{8,0},{9,1},... | collective-permute-start | bytes 294920 | tf_op jit(solution)/shard_map/cond/branch_1_fun/ppermute | solution.py:27
  376.5 14.7 %collective-permute-start.20 = (bf16[112,768]{1,0:T(8,128)(2,1)S(1)}, bf16[112,768]{1,0:T(8,128)(2,1)S(1)}, u32[]{:S(2)}, u32[]{:S(2)}) collective-permute-start(bf16[112,768]{1,0:T(8,128)(2,1)S(1)} %constant_dynamic-slice_fusion.1), channel_id=1, source_target_pairs={{0,4},{1,5},{2,6},{3,7},{4,0},{5,1},{6,2},{7,3},{8,12},{9,13},{10,... | collective-permute-start | bytes 516104 | tf_op jit(solution)/shard_map/cond/branch_1_fun/ppermute | solution.py:27
  391.3 7.9 %collective-permute-start.22 = (bf16[48,768]{1,0:T(8,128)(2,1)S(1)}, bf16[48,768]{1,0:T(8,128)(2,1)S(1)}, u32[]{:S(2)}, u32[]{:S(2)}) collective-permute-start(bf16[48,768]{1,0:T(8,128)(2,1)S(1)} %add_convert_fusion.18), channel_id=1, source_target_pairs={{0,8},{1,9},{2,10},{3,11},{4,12},{5,13},{6,14},{7,15},{8,0},{9,1},... | collective-permute-start | bytes 221192 | tf_op jit(solution)/shard_map/cond/branch_1_fun/ppermute | solution.py:27
  393.1 9.2 %collective-permute-start.23 = (bf16[56,768]{1,0:T(8,128)(2,1)S(1)}, bf16[56,768]{1,0:T(8,128)(2,1)S(1)}, u32[]{:S(2)}, u32[]{:S(2)}) collective-permute-start(bf16[56,768]{1,0:T(8,128)(2,1)S(1)} %constant_dynamic-slice_fusion), channel_id=1, source_target_pairs={{0,8},{1,9},{2,10},{3,11},{4,12},{5,13},{6,14},{7,15},{8,0},{9,1},... | collective-permute-start | bytes 258056 | tf_op jit(solution)/shard_map/cond/branch_1_fun/ppermute | solution.py:27
  394.3 8.0 %collective-permute-start.21 = (bf16[64,768]{1,0:T(8,128)(2,1)S(1)}, bf16[64,768]{1,0:T(8,128)(2,1)S(1)}, u32[]{:S(2)}, u32[]{:S(2)}) collective-permute-start(bf16[64,768]{1,0:T(8,128)(2,1)S(1)} %add_convert_fusion.11), channel_id=1, source_target_pairs={{0,2},{1,3},{2,0},{3,1},{4,6},{5,7},{6,4},{7,5},{8,10},{9,11},{10,... | collective-permute-start | bytes 294920 | tf_op jit(solution)/shard_map/cond/branch_1_fun/ppermute | solution.py:27
  402.4 6.4 %collective-permute-start.26 = (bf16[56,768]{1,0:T(8,128)(2,1)S(1)}, bf16[56,768]{1,0:T(8,128)(2,1)S(1)}, u32[]{:S(2)}, u32[]{:S(2)}) collective-permute-start(bf16[56,768]{1,0:T(8,128)(2,1)S(1)} %add_convert_fusion.17), channel_id=1, source_target_pairs={{0,8},{1,9},{2,10},{3,11},{4,12},{5,13},{6,14},{7,15},{8,0},{9,1},... | collective-permute-start | bytes 258056 | tf_op jit(solution)/shard_map/cond/branch_1_fun/ppermute | solution.py:27
  402.5 7.0 %collective-permute-start.25 = (bf16[96,768]{1,0:T(8,128)(2,1)S(1)}, bf16[96,768]{1,0:T(8,128)(2,1)S(1)}, u32[]{:S(2)}, u32[]{:S(2)}) collective-permute-start(bf16[96,768]{1,0:T(8,128)(2,1)S(1)} %maximum_select_fusion.6), channel_id=1, source_target_pairs={{0,4},{1,5},{2,6},{3,7},{4,0},{5,1},{6,2},{7,3},{8,12},{9,13},{10,... | collective-permute-start | bytes 442376 | tf_op jit(solution)/shard_map/cond/branch_1_fun/ppermute | solution.py:27
  403.9 6.4 %collective-permute-start.24 = (bf16[128,768]{1,0:T(8,128)(2,1)S(1)}, bf16[128,768]{1,0:T(8,128)(2,1)S(1)}, u32[]{:S(2)}, u32[]{:S(2)}) collective-permute-start(bf16[128,768]{1,0:T(8,128)(2,1)S(1)} %maximum_select_fusion.4), channel_id=1, source_target_pairs={{0,1},{1,0},{2,3},{3,2},{4,5},{5,4},{6,7},{7,6},{8,9},{9,8},{10,11... | collective-permute-start | bytes 589832 | tf_op jit(solution)/shard_map/cond/branch_1_fun/ppermute | solution.py:27
  411.3 5.7 %collective-permute-start.43 = (bf16[112,768]{1,0:T(8,128)(2,1)}, bf16[112,768]{1,0:T(8,128)(2,1)S(1)}, u32[]{:S(2)}, u32[]{:S(2)}) collective-permute-start(bf16[112,768]{1,0:T(8,128)(2,1)} %get-tuple-element.192), channel_id=1, source_target_pairs={{0,4},{1,5},{2,6},{3,7},{4,0},{5,1},{6,2},{7,3},{8,12},{9,13},{10,... | collective-permute-start | bytes 516104 | tf_op jit(solution)/shard_map/ppermute | solution.py:27
  411.9 10.0 %collective-permute-start.41 = (bf16[192,768]{1,0:T(8,128)(2,1)}, bf16[192,768]{1,0:T(8,128)(2,1)S(1)}, u32[]{:S(2)}, u32[]{:S(2)}) collective-permute-start(bf16[192,768]{1,0:T(8,128)(2,1)} %get-tuple-element.191), channel_id=1, source_target_pairs={{0,2},{1,3},{2,0},{3,1},{4,6},{5,7},{6,4},{7,5},{8,10},{9,11},{10,... | collective-permute-start | bytes 884744 | tf_op jit(solution)/shard_map/ppermute | solution.py:27
  418.1 7.7 %collective-permute-start.44 = (bf16[224,768]{1,0:T(8,128)(2,1)S(1)}, bf16[224,768]{1,0:T(8,128)(2,1)S(1)}, u32[]{:S(2)}, u32[]{:S(2)}) collective-permute-start(bf16[224,768]{1,0:T(8,128)(2,1)S(1)} %maximum_select_fusion.13), channel_id=1, source_target_pairs={{0,2},{1,3},{2,0},{3,1},{4,6},{5,7},{6,4},{7,5},{8,10},{9,11},{10,... | collective-permute-start | bytes 1032200 | tf_op jit(solution)/shard_map/ppermute | solution.py:27
  423.2 15.7 %collective-permute-start.42 = (bf16[384,768]{1,0:T(8,128)(2,1)S(1)}, bf16[384,768]{1,0:T(8,128)(2,1)S(1)}, u32[]{:S(2)}, u32[]{:S(2)}) collective-permute-start(bf16[384,768]{1,0:T(8,128)(2,1)S(1)} %maximum_select_fusion.10), channel_id=1, source_target_pairs={{0,16},{16,0},{1,17},{17,1},{2,18},{18,2},{3,19},{19,3},{4,20},{20... | collective-permute-start | bytes 1769480 | tf_op jit(solution)/shard_map/ppermute | solution.py:27
  426.0 20.3 %collective-permute-start.45 = (bf16[448,768]{1,0:T(8,128)(2,1)S(1)}, bf16[448,768]{1,0:T(8,128)(2,1)S(1)}, u32[]{:S(2)}, u32[]{:S(2)}) collective-permute-start(bf16[448,768]{1,0:T(8,128)(2,1)S(1)} %maximum_select_fusion.9), channel_id=1, source_target_pairs={{0,16},{16,0},{1,17},{17,1},{2,18},{18,2},{3,19},{19,3},{4,20},{20... | collective-permute-start | bytes 2064392 | tf_op jit(solution)/shard_map/ppermute | solution.py:27
  439.4 22.8 %copy-start.7 = (bf16[768,768]{1,0:T(8,128)(2,1)}, bf16[768,768]{1,0:T(8,128)(2,1)S(1)}, u32[]{:S(2)}) copy-start(bf16[768,768]{1,0:T(8,128)(2,1)S(1)} %maximum_select_fusion.8.early_ref) | copy-start | bytes 3538948
  459.3 2.8 collective-permute-start.47
  459.3 4.8 collective-permute-start.46
  (55 other events, 317.6 us)
Sparse Core Ops, SparseCore 0:
  177.0 224.4 all-reduce.8

commit v9 on v8

--- a/solution.py
+++ b/solution.py
@@ -407,7 +407,7 @@
     gq_ref[...] = gq_s[...].astype(BF)
 
 
-def conv_back_kernel(docs, bounds, gm_ref, v_ref, taps_ref, out_ref, prod_ref, band_s):
+def conv_back_kernel(docs, bounds, gm_ref, v_ref, taps_ref, out_ref, sum_ref, band_s, prod_s):
     width = gm_ref.shape[1]
     groups = width // GROUP
     radius = (TAPS - 1) // 2
@@ -416,7 +416,7 @@
     @pl.when(pl.program_id(0) == 0)
     def _():
         make_band(taps_ref, band_s)
-        prod_ref[...] = jnp.zeros(prod_ref.shape, F32)
+        prod_s[...] = jnp.zeros(prod_s.shape, F32)
 
     for sub in range(BLOCK // SUB):
         start = pl.multiple_of(first + sub * SUB, SUB)
@@ -430,7 +430,18 @@
             out_ref[sub * SUB : (sub + 1) * SUB, cols] = gathered(res)
             own = gm_ref[pl.ds(pl.multiple_of(start + radius, 16), SUB), cols]
             product = dot_nt(spread(own), v_ref[pl.ds(start, GROUP), cols])
-            prod_ref[tall, :] += product * same
+            prod_s[tall, :] += product * same
+
+    @pl.when(pl.program_id(0) == pl.num_programs(0) - 1)
+    def _():
+        flip = (iota((SUB, SUB), 0) + iota((SUB, SUB), 1) == SUB - 1).astype(F32).astype(BF)
+        sum_ref[...] = jnp.zeros(sum_ref.shape, F32)
+        for head in range(taps_ref.shape[0]):
+            product = prod_s[head * SUB : (head + 1) * SUB, :]
+            high = product.astype(BF)
+            low = (product - high.astype(F32)).astype(BF)
+            turned = pltpu.roll(dot_nn(flip, high) + dot_nn(flip, low), 0, 1, stride=1, stride_axis=0)
+            sum_ref[head : head + 1, :] = jnp.sum(turned, axis=0, keepdims=True)
 
 
 def ffn_kernel(
@@ -868,16 +879,15 @@
             in_specs=[
                 smem, fixed(window_rows, width), fixed(window_rows, width), fixed(heads, GROUP)
             ],
-            out_specs=(tok_spec, fixed(heads * SUB, GROUP)),
-            out_shape=(shaped((tok_count, width), F32), shaped((heads * SUB, GROUP), F32)),
-            scratch_shapes=[pltpu.VMEM((heads * SUB, GROUP), BF)],
+            out_specs=(tok_spec, fixed(16, GROUP)),
+            out_shape=(shaped((tok_count, width), F32), shaped((16, GROUP), F32)),
+            scratch_shapes=[
+                pltpu.VMEM((heads * SUB, GROUP), BF), pltpu.VMEM((heads * SUB, GROUP), F32)
+            ],
             compiler_params=params,
             name="conv_back",
         )(bounds, grad_ext, value_ext, jnp.pad(conv_taps[:, ::-1], ((0, 0), (0, GROUP - tap_count))))
-        reach = SUB + tap_count - 1
-        products = products.reshape(heads, SUB, GROUP)[:, :, :reach].reshape(heads, SUB * reach)
-        products = jnp.pad(products, ((0, 0), (0, SUB))).reshape(heads, SUB, reach + 1)
-        grad_conv_taps = jnp.sum(products, axis=1)[:, :tap_count]
+        grad_conv_taps = products[:heads, SUB - 1 : SUB - 1 + tap_count]
         grad_mix, grad_conv, grad_conv_taps = lax.optimization_barrier(
             (grad_mix, grad_conv, grad_conv_taps)
         )
@@ -907,8 +917,9 @@
         def weight_grad(grads):
             return lax.dot_general(tokens, grads, rows_in, preferred_element_type=F32)
 
-        early = jnp.concatenate(
-            [grad_w_out.astype(BF), weight_grad(grad_values).astype(BF)], 0
+        early = jnp.pad(grad_w_out.astype(BF), ((0, width), (0, 0)))
+        early = lax.dynamic_update_slice_in_dim(
+            early, weight_grad(grad_values).astype(BF), width, 0
         )
         grad_mix, early = lax.optimization_barrier((grad_mix, early))
         early = advance(begin(early, ORDER, ORDER), 1)
@@ -917,6 +928,9 @@
             out_shape=(shaped(square, F32), shaped(square, F32)),
             name="pinv_back",
         )(own_q, own_k, kernel, saved, own_heads(grad_mix), own_heads(stats[:, :width]))
+
+        grad_mq_small, (early,) = tied(grad_mq_small, [early])
+        early = advance(early, 1)
 
         def with_small(array, small):
             small = small.transpose(1, 0, 2).reshape(LAND, own_count * size)
@@ -955,17 +969,15 @@
         )
         spare_rows = width // 6
         small = jnp.concatenate([sums, others], 0).astype(BF)
-        small = jnp.pad(small, ((0, spare_rows - small.shape[0]), (0, 0)))
-        small = lax.optimization_barrier(small)
-        late = jnp.concatenate(
-            [
-                (weight_grad(grad_queries) + mark_grad_q).astype(BF),
-                small,
-                (weight_grad(grad_keys) + mark_grad_k).astype(BF),
-                jnp.zeros((spare_rows, width), BF),
-            ],
-            0,
+        below = width + 2 * spare_rows - small.shape[0]
+        late = jnp.pad(small, ((width, below), (0, 0)))
+        late = lax.dynamic_update_slice_in_dim(
+            late, (weight_grad(grad_queries) + mark_grad_q).astype(BF), 0, 0
         )
+        late = lax.dynamic_update_slice_in_dim(
+            late, (weight_grad(grad_keys) + mark_grad_k).astype(BF), width + spare_rows, 0
+        )
+        late, (early,) = tied(late, [early])
         late = begin(late, ORDER, ORDER)
         for step in seq_steps():
             mark_back = step(mark_back)
@@ -979,7 +991,7 @@
     def rows_left(rows, done):
         return rows >> min(done, 2 * len(plan) - done)
 
-    early_rows = rows_left(2 * width, sent + 1)
+    early_rows = rows_left(2 * width, sent + 2)
     late_rows = rows_left(2 * width + width // 3, sent)
 
     def nothing(*unused):
@@ -991,19 +1003,20 @@
     early, late, mark_back, grad_keys, grad_values = lax.cond(
         lengths[0] > 0, remaining, nothing, grad_mix, grad_mk, stats, mix
     )
-    early, late = (early, plan, plan, sent + 1), (late, plan, plan, sent)
+    early, late = (early, plan, plan, sent + 2), (late, plan, plan, sent)
     last = 2 * len(plan) - 1
-    early, late = advance(early, last - sent - 1), advance(late, last - sent)
-    sum_w_down, sum_w_up = sum_w_down.astype(F32), sum_w_up.astype(F32)
+    late = advance(late, 2)
+    (sum_w_down, sum_w_up), (late,) = tied(
+        (sum_w_down.astype(F32), sum_w_up.astype(F32)), [late]
+    )
+    early, late = advance(early, last - early[3]), advance(late, last - late[3])
     grad_projected = jnp.concatenate([grad_queries, grad_keys, grad_values], axis=1)
     grad_input = (
         grad_one
         + lax.dot_general(grad_projected, w_qkv, cols_in, preferred_element_type=F32)
         + lax.dot_general(onehot, mark_back, rows_in, preferred_element_type=F32)
     )
-    (sum_w_down, sum_w_up, grad_input), (early, late) = tied(
-        (sum_w_down, sum_w_up, grad_input), [early, late]
-    )
+    grad_input, (early, late) = tied(grad_input, [early, late])
     early, early_other = last_swap(early)[:2]
     late, late_other = last_swap(late)[:2]
     sum_w_qkv = settle_qkv(late, late_other, early, early_other, width)

time: 491 us -> 472 us (0.961)
  starting transfers between devices: 68.2 us -> 41.6 us
  waiting for transfers between devices: 123 us -> 147 us
  other arithmetic: 60.3 us -> 43.4 us
  Pallas kernels: 111 us -> 124 us
  local copies, waits for them, and re-layouts: 49.1 us -> 37.5 us
    ppermute x44, starting transfers between devices: 61.3 us -> 32.2 us  [swap(): return lax.ppermute(array, axis, [(i, i ^ bit) for i in range(count)])]
    ppermute x44, waiting for transfers between devices: 123 us -> 147 us  [swap(): return lax.ppermute(array, axis, [(i, i ^ bit) for i in range(count)])]
    reshape x2 -> x0, local copies, waits for them, and re-layouts: 7.9 us -> none  [the longest x1 4.32 us: remaining(): jnp.pad(products, ((0, 0), (0, SUB))).reshape(heads, SUB, reach + 1)]
    concatenate x2 -> x0, other arithmetic: 6.32 us -> none  [the longest x1 6.17 us: remaining(): jnp.concatenate([(weight_grad(grad_queries) + mark_grad_q).astype(BF), sm...]
  transfers between devices with their start and end apart: 49 -> 49, of which waited for: 30 -> 33; matrix products, arithmetic and copies ran while one was open for 23% -> 21% of each run, Pallas kernels for 7% -> 8%
where the time goes in v9:
time: 472 us; the launch traced here: 464 us
  waiting for transfers between devices  147 us (31%)
  Pallas kernels  124 us (26%)
  matrix products  53.7 us (11%)
  other arithmetic  43.4 us (9%)
  starting transfers between devices  41.6 us (9%)
  local copies, waits for them, and re-layouts  37.5 us (8%)
  between operations  15.4 us (3%)
    ppermute x44, waiting for transfers between devices, swap(): return lax.ppermute(array, axis, [(i, i ^ bit) for i in range(count)])  147 us
    pallas_call x1, Pallas kernels, per_device(): pl.pallas_call(ffn_kernel, grid=(tok_count // FFN_BLOCK,), in_specs=[ffn_...  40.3 us
    ppermute x44, starting transfers between devices, swap(): return lax.ppermute(array, axis, [(i, i ^ bit) for i in range(count)])  32.2 us
    pallas_call x1, Pallas kernels, per_device(): pl.pallas_call(lambda *refs: token_kernel(docs, scale, *refs), grid=(bloc...  12 us
    dot_general x3, matrix products, weight_grad(): return lax.dot_general(tokens, grads, rows_in, preferred_element_type=F32)  11.8 us
    pallas_call x1, Pallas kernels, remaining(): pl.pallas_call(lambda *refs: landmark_back_kernel(docs, scale, *refs), gr...  11.7 us
    pallas_call x1, Pallas kernels, per_device(): pl.pallas_call(lambda *refs: token_back_kernel(docs, scale, *refs), grid=...  11.5 us
    pallas_call x1, Pallas kernels, remaining(): pl.pallas_call(lambda *refs: pinv_back_kernel(scale, *refs), out_shape=(s...  9.82 us
  transfers between devices with their start and end apart: 49, of which 33 were waited for; matrix products, arithmetic and copies ran while one was open for 21% of the time, Pallas kernels for 8%

profile of v9, /device:TPU:0, one launch (start us, length us, event | category | flops | bytes accessed | tf_op | source)
XLA Modules:
  0.0 464.0 jit_solution(12153888361704426745)
XLA Ops:
  10.9 2.2 fusion.25
  14.7 3.0 collective-permute-start.31
  17.7 3.1 collective-permute-done.31
  20.8 1.9 collective-permute-start.32
  22.7 6.0 %add_convert_fusion.20.refs_2_.refs_3_.refs_1_ = bf16[1024,2304]{1,0:T(8,128)(2,1)S(1)} fusion(bf16[768,2304]{1,0:T(8,128)(2,1)} %param.21, f32[2304]{0:T(1024)S(1)} %pad_maximum_fusion.3, bf16[1,1024,768]{2,1,0:T(8,128)(2,1)S(1)} %copy-done.22), kind=kOutput, calls=%fused_computation.67 | convolution fusion | flops 3628597248 | bytes 9839616 | tf_op jit(solution)/shard_map/dot_general | solution.py:734
  28.8 2.7 collective-permute-start.33
  32.7 3.0 collective-permute-start.28
  37.7 3.9 collective-permute-done.34
  46.1 8.1 %landmark.1 = bf16[256,896]{1,0:T(8,128)(2,1)S(1)} custom-call(s32[8]{0:T(128)S(1)} %add_subtract_fusion.refs_0_, bf16[256,768]{1,0:T(8,128)(2,1)S(1)} %fusion.26.refs_1_, bf16[1024,2304]{1,0:T(8,128)(2,1)S(1)} %copy-done.3, bf16[1024,2304]{1,0:T(8,128)(2,1)S(1)} %copy-done.3), custom_call_target="tpu_custom_call" | custom-call | tf_op jit(solution)/shard_map/landmark/pallas_call | solution.py:741
  57.2 2.6 join.4
  61.9 6.0 %pinv.1 = (f32[3,64,64]{2,1,0:T(8,128)}, f32[3,64,64]{2,1,0:T(8,128)}, f32[72,64,64]{2,1,0:T(8,128)}) custom-call(f32[3,64,64]{2,1,0:T(8,128)S(1)} %bitcast.67, f32[3,64,64]{2,1,0:T(8,128)S(1)} %bitcast.69), custom_call_target="tpu_custom_call" | custom-call | tf_op jit(solution)/shard_map/pinv/pallas_call | solution.py:774
  69.8 2.2 join.5.a_ref
  72.9 5.9 %collective-permute-done.38 = bf16[64,1088]{1,0:T(8,128)(2,1)S(1)} collective-permute-done((bf16[64,1088]{1,0:T(8,128)(2,1)S(1)}, bf16[64,1088]{1,0:T(8,128)(2,1)S(1)}, u32[]{:S(2)}, u32[]{:S(2)}) %collective-permute-start.38) | collective-permute-done | bytes 139296 | tf_op jit(solution)/shard_map/ppermute | solution.py:27
  79.5 2.2 join.6.a_ref
  82.7 9.8 %collective-permute-done.39 = bf16[64,1280]{1,0:T(8,128)(2,1)S(1)} collective-permute-done((bf16[64,1280]{1,0:T(8,128)(2,1)S(1)}, bf16[64,1280]{1,0:T(8,128)(2,1)S(1)}, u32[]{:S(2)}, u32[]{:S(2)}) %collective-permute-start.39) | collective-permute-done | bytes 163872 | tf_op jit(solution)/shard_map/ppermute | solution.py:27
  97.1 3.8 collective-permute-done.40
  104.8 12.0 %token_.1 = (bf16[1024,768]{1,0:T(8,128)(2,1)}, bf16[768,1024]{1,0:T(8,128)(2,1)S(1)}) custom-call(s32[8]{0:T(128)S(1)} %add_subtract_fusion.refs_0_, bf16[1024,2304]{1,0:T(8,128)(2,1)} %copy-done.2, bf16[1152,768]{1,0:T(8,128)(2,1)S(1)} %maximum_maximum_fusion.1.refs_2_, bf16[256,768]{1,0:T(8,128)(2,1)S(1)} %slice.187.refs_3_.refs_4_, ...), custom_call_target="tpu_custom_call" | custom-call | tf_op jit(solution)/shard_map/token/pallas_call | solution.py:802
  117.4 40.3 %ffn.1 = (f32[1024,768]{1,0:T(8,128)}, f32[1024,768]{1,0:T(8,128)}, bf16[1024,3072]{1,0:T(8,128)(2,1)}, bf16[1024,3072]{1,0:T(8,128)(2,1)}, bf16[1024,768]{1,0:T...) custom-call(bf16[1024,768]{1,0:T(8,128)(2,1)} %bitcast.65, ...), custom_call_target="tpu_custom_call" | custom-call | tf_op jit(solution)/shard_map/ffn/pallas_call | solution.py:824
  157.7 11.5 %token_back.1 = (bf16[1024,768]{1,0:T(8,128)(2,1)}, f32[256,768]{1,0:T(8,128)S(1)}, f32[256,768]{1,0:T(8,128)}) custom-call(s32[8]{0:T(128)S(1)} %add_subtract_fusion.refs_0_, bf16[1024,2304]{1,0:T(8,128)(2,1)} %copy-done.2, bf16[1024,768]{1,0:T(8,128)(2,1)} %get-tuple-element.176.refs_2_, bf16[768,1024]{1,0:T(8,128)(2,1)S(1)} %get-tuple-element.177.refs_3_, ...), custom_call_target="tpu_custom_call" | custom-call | tf_op jit(solution)/shard_map/token_back/pallas_call | solution.py:848
  169.3 6.9 %convolution_convert_fusion.3 = bf16[3072,768]{1,0:T(8,128)(2,1)} fusion(bf16[1024,3072]{1,0:T(8,128)(2,1)S(1)} %copy-done.63, bf16[1024,768]{1,0:T(8,128)(2,1)S(1)} %copy-done.67), kind=kOutput, calls=%fused_computation.69 | convolution fusion | flops 4834197504 | bytes 12582912 | tf_op jit(solution)/shard_map/dot_general | solution.py:864
  176.2 6.8 %convolution_convert_fusion.2 = bf16[768,3072]{1,0:T(8,128)(2,1)} fusion(bf16[1024,768]{1,0:T(8,128)(2,1)S(1)} %copy-done.66, bf16[1024,3072]{1,0:T(8,128)(2,1)S(1)} %bitcast.87), kind=kOutput, calls=%fused_computation.68 | convolution fusion | flops 4834197504 | bytes 12582912 | tf_op jit(solution)/shard_map/dot_general | solution.py:865
  183.7 209.6 %conditional.1 = (bf16[384,768]{1,0:T(8,128)(2,1)}, bf16[112,768]{1,0:T(8,128)(2,1)}, bf16[256,768]{1,0:T(8,128)(2,1)}, bf16[1024,768]{1,0:T(8,128)(2,1)}, bf16[1024,768]{1,0:T(8,128)(2,1)}) conditional(s32[]{:T(128)} %bitcast.23, () %tuple.33, (bf16[256,768]{1,0:T(8,128)(2,1)S(1)}, bf16[1024,768]{1,0:T(8,128)(2,1)}, f32[12,33]{1,0:T(8,128)S(1)}, ...), branch_computations={%region_1.2_spmd, %region_2.6_spmd} | conditional | flops 6083118080 | bytes 205958944 | solution.py:1003
  186.6 3.8 collective-permute-start.4
  191.6 4.5 convolution_convert_fusion.1
  196.4 2.0 collective-permute-done.1
  200.3 6.7 %collective-permute-done.2 = bf16[64,768]{1,0:T(8,128)(2,1)S(1)} collective-permute-done((bf16[64,768]{1,0:T(8,128)(2,1)S(1)}, bf16[64,768]{1,0:T(8,128)(2,1)S(1)}, u32[]{:S(2)}, u32[]{:S(2)}) %collective-permute-start.2) | collective-permute-done | bytes 98336 | tf_op jit(solution)/shard_map/cond/branch_1_fun/ppermute | solution.py:27
  208.6 5.8 %conv_back.1 = (f32[1024,768]{1,0:T(8,128)S(1)}, f32[16,256]{1,0:T(8,128)S(1)}) custom-call(s32[8]{0:T(128)S(1)} %get-tuple-element.52.refs_0_, bf16[1152,768]{1,0:T(8,128)(2,1)S(1)} %maximum_maximum_fusion.refs_1_, bf16[1152,768]{1,0:T(8,128)(2,1)S(1)} %copy-done.5, f32[12,256]{1,0:T(8,128)S(1)} %pad.17.refs_3_), custom_call_target="tpu_custom_call" | custom-call | tf_op jit(solution)/shard_map/cond/branch_1_fun/conv_back/pallas_call | solution.py:876
  215.2 1.7 collective-permute-done.3
  217.6 2.1 mix_back.1
  226.0 5.0 %fusion.44 = f32[768,768]{1,0:T(8,128)} fusion(bf16[1024,768]{1,0:T(8,128)(2,1)} %get-tuple-element.76, bf16[1024,768]{1,0:T(8,128)(2,1)} %get-tuple-element.87), kind=kOutput, calls=%fused_computation.151 | convolution fusion | flops 1207959552 | bytes 5505024 | tf_op jit(solution)/shard_map/cond/branch_1_fun/dot_general | solution.py:918
  231.2 11.7 %landmark_back.1 = (bf16[1024,768]{1,0:T(8,128)(2,1)}, bf16[1024,768]{1,0:T(8,128)(2,1)}, f32[256,768]{1,0:T(8,128)S(1)}) custom-call(s32[8]{0:T(128)S(1)} %get-tuple-element.52.refs_0_, bf16[1024,2304]{1,0:T(8,128)(2,1)S(1)} %bitcast.62, bf16[1024,2304]{1,0:T(8,128)(2,1)S(1)} %bitcast.62, f32[1024,768]{1,0:T(8,128)S(1)} %get-tuple-element.60.refs_3_, ...), custom_call_target="tpu_custom_call" | custom-call | tf_op jit(solution)/shard_map/cond/branch_1_fun/landmark_back/pallas_call | solution.py:900
  242.9 3.2 fusion.4
  249.1 1.7 reduce
  252.6 9.8 %pinv_back.1 = (f32[3,64,64]{2,1,0:T(8,128)}, f32[3,64,64]{2,1,0:T(8,128)}) custom-call(f32[3,64,64]{2,1,0:T(8,128)S(1)} %copy-done.31, f32[3,64,64]{2,1,0:T(8,128)S(1)} %copy-done.33, f32[3,64,64]{2,1,0:T(8,128)S(1)} %copy-done.38, f32[72,64,64]{2,1,0:T(8,128)} %get-tuple-element.72.refs_3_, bf16[3,64,64]{2,1,0:T(8,128)(2,1)} %bitcast.79, ...), custom_call_target="tpu_custom_call" | custom-call | tf_op jit(solution)/shard_map/cond/branch_1_fun/pinv_back/pallas_call | solution.py:926
  265.9 3.6 fusion.45
  270.1 1.7 copy.46
  271.8 2.7 add_convert_fusion.2
  279.7 2.3 fusion.3
  282.1 12.3 %collective-permute-done.10 = bf16[384,768]{1,0:T(8,128)(2,1)} collective-permute-done((bf16[384,768]{1,0:T(8,128)(2,1)}, bf16[384,768]{1,0:T(8,128)(2,1)}, u32[]{:S(2)}, u32[]{:S(2)}) %collective-permute-start.10) | collective-permute-done | bytes 589856 | tf_op jit(solution)/shard_map/cond/branch_1_fun/ppermute | solution.py:27
  296.9 2.7 fusion.9
  303.3 11.3 %collective-permute-done.11 = bf16[192,768]{1,0:T(8,128)(2,1)} collective-permute-done((bf16[192,768]{1,0:T(8,128)(2,1)}, bf16[192,768]{1,0:T(8,128)(2,1)}, u32[]{:S(2)}, u32[]{:S(2)}) %collective-permute-start.11) | collective-permute-done | bytes 294944 | tf_op jit(solution)/shard_map/cond/branch_1_fun/ppermute | solution.py:27
  317.7 4.5 collective-permute-done.13
  322.3 2.6 collective-permute-done.14
  324.9 7.2 %collective-permute-done.15 = bf16[448,768]{1,0:T(8,128)(2,1)S(1)} collective-permute-done((bf16[448,768]{1,0:T(8,128)(2,1)S(1)}, bf16[448,768]{1,0:T(8,128)(2,1)S(1)}, u32[]{:S(2)}, u32[]{:S(2)}) %collective-permute-start.15) | collective-permute-done | bytes 688160 | tf_op jit(solution)/shard_map/cond/branch_1_fun/ppermute | solution.py:27
  335.0 4.5 collective-permute-done.17
  339.7 11.4 %collective-permute-done.18 = bf16[224,768]{1,0:T(8,128)(2,1)S(1)} collective-permute-done((bf16[224,768]{1,0:T(8,128)(2,1)S(1)}, bf16[224,768]{1,0:T(8,128)(2,1)S(1)}, u32[]{:S(2)}, u32[]{:S(2)}) %collective-permute-start.18) | collective-permute-done | bytes 344096 | tf_op jit(solution)/shard_map/cond/branch_1_fun/ppermute | solution.py:27
  351.3 2.9 collective-permute-start.20
  354.3 10.5 %collective-permute-done.20 = bf16[48,768]{1,0:T(8,128)(2,1)S(1)} collective-permute-done((bf16[48,768]{1,0:T(8,128)(2,1)S(1)}, bf16[48,768]{1,0:T(8,128)(2,1)S(1)}, u32[]{:S(2)}, u32[]{:S(2)}) %collective-permute-start.20) | collective-permute-done | bytes 73760 | tf_op jit(solution)/shard_map/cond/branch_1_fun/ppermute | solution.py:27
  364.9 2.1 collective-permute-done.21
  367.0 2.4 collective-permute-start.24
  369.5 2.2 collective-permute-start.22
  371.7 3.6 collective-permute-done.24
  375.4 5.2 %collective-permute-done.23 = bf16[96,768]{1,0:T(8,128)(2,1)S(1)} collective-permute-done((bf16[96,768]{1,0:T(8,128)(2,1)S(1)}, bf16[96,768]{1,0:T(8,128)(2,1)S(1)}, u32[]{:S(2)}, u32[]{:S(2)}) %collective-permute-start.23) | collective-permute-done | bytes 147488 | tf_op jit(solution)/shard_map/cond/branch_1_fun/ppermute | solution.py:27
  380.6 2.0 collective-permute-start.27
  383.8 5.0 %collective-permute-done.27 = bf16[56,768]{1,0:T(8,128)(2,1)S(1)} collective-permute-done((bf16[56,768]{1,0:T(8,128)(2,1)S(1)}, bf16[56,768]{1,0:T(8,128)(2,1)S(1)}, u32[]{:S(2)}, u32[]{:S(2)}) %collective-permute-start.27) | collective-permute-done | bytes 86048 | tf_op jit(solution)/shard_map/cond/branch_1_fun/ppermute | solution.py:27
  393.6 7.5 %collective-permute-done.43 = bf16[112,768]{1,0:T(8,128)(2,1)S(1)} collective-permute-done((bf16[112,768]{1,0:T(8,128)(2,1)}, bf16[112,768]{1,0:T(8,128)(2,1)S(1)}, u32[]{:S(2)}, u32[]{:S(2)}) %collective-permute-start.43) | collective-permute-done | bytes 172064 | tf_op jit(solution)/shard_map/ppermute | solution.py:27
  404.6 7.4 %collective-permute-done.44 = bf16[224,768]{1,0:T(8,128)(2,1)S(1)} collective-permute-done((bf16[224,768]{1,0:T(8,128)(2,1)S(1)}, bf16[224,768]{1,0:T(8,128)(2,1)S(1)}, u32[]{:S(2)}, u32[]{:S(2)}) %collective-permute-start.44) | collective-permute-done | bytes 344096 | tf_op jit(solution)/shard_map/ppermute | solution.py:27
  412.3 7.0 %convert_element_type.348 = f32[3072,768]{1,0:T(8,128)} convert(bf16[3072,768]{1,0:T(8,128)(2,1)} %get-tuple-element.213) | non-fusion elementwise | flops 2359296 | bytes 14155776 | tf_op jit(solution)/shard_map/convert_element_type | solution.py:1010
  419.2 5.0 %convert_element_type.349 = f32[768,3072]{1,0:T(8,128)} convert(bf16[768,3072]{1,0:T(8,128)(2,1)S(1)} %copy-done.12) | non-fusion elementwise | flops 2359296 | bytes 14155776 | tf_op jit(solution)/shard_map/convert_element_type | solution.py:1010
  425.3 5.6 %fusion.17 = f32[1024,768]{1,0:T(8,128)S(1)} fusion(bf16[768,2304]{1,0:T(8,128)(2,1)S(1)} %copy-done.65, bf16[1024,768]{1,0:T(8,128)(2,1)} %get-tuple-element.192, bf16[1024,768]{1,0:T(8,128)(2,1)} %get-tuple-element.191, bf16[1024,768]{1,0:T(8,128)(2,1)S(1)} %copy-done.24), kind=kOutput, calls=%fused_computation.70 | convolution fusion | flops 3638034432 | bytes 11403264 | tf_op jit(solution)/shard_map/dot_general | solution.py:1016
  431.0 3.6 add_add_fusion
  436.2 4.3 collective-permute-done.45
  441.7 2.3 collective-permute-done.47.early_other_ref
  449.1 7.6 %settle_qkv.1 = f32[768,2304]{1,0:T(8,128)} custom-call(s32[1]{0:T(128)} %bitcast.25.side_ref, bf16[896,768]{1,0:T(8,128)(2,1)} %copy-done.10, bf16[896,768]{1,0:T(8,128)(2,1)} %copy-done.21, bf16[768,768]{1,0:T(8,128)(2,1)} %copy-done.6, bf16[768,768]{1,0:T(8,128)(2,1)} %copy-done.11), custom_call_target="tpu_custom_call" | custom-call | tf_op jit(solution)/shard_map/settle_qkv/pallas_call | solution.py:671
  (364 shorter events, 92.3 us)
Async XLA Ops:
  7.2 405.1 %all-reduce.8.cloned.1.call-start = ((), (), s32[]{:S(2)}) async-start(), calls=%async_computation | async-start | bytes 18874368 | tf_op jit(solution)/shard_map/psum | solution.py:869
  13.1 1.6 collective-permute-start.30
  14.7 6.1 %collective-permute-start.31 = (bf16[64,768]{1,0:T(8,128)(2,1)S(1)}, bf16[64,768]{1,0:T(8,128)(2,1)S(1)}, u32[]{:S(2)}, u32[]{:S(2)}) collective-permute-start(bf16[64,768]{1,0:T(8,128)(2,1)S(1)} %constant_dynamic-slice_fusion.20), channel_id=1, source_target_pairs={{0,2},{1,3},{2,0},{3,1},{4,6},{5,7},{6,4},{7,5},{8,10},{9,11},{10,... | collective-permute-start | bytes 294920 | tf_op jit(solution)/shard_map/ppermute | solution.py:27
  20.8 7.9 %collective-permute-start.32 = (bf16[64,768]{1,0:T(8,128)(2,1)S(1)}, bf16[64,768]{1,0:T(8,128)(2,1)S(1)}, u32[]{:S(2)}, u32[]{:S(2)}) collective-permute-start(bf16[64,768]{1,0:T(8,128)(2,1)S(1)} %add_convert_fusion.24), channel_id=1, source_target_pairs={{0,4},{1,5},{2,6},{3,7},{4,0},{5,1},{6,2},{7,3},{8,12},{9,13},{10,... | collective-permute-start | bytes 294920 | tf_op jit(solution)/shard_map/ppermute | solution.py:27
  28.8 7.2 %collective-permute-start.33 = (bf16[64,768]{1,0:T(8,128)(2,1)S(1)}, bf16[64,768]{1,0:T(8,128)(2,1)S(1)}, u32[]{:S(2)}, u32[]{:S(2)}) collective-permute-start(bf16[64,768]{1,0:T(8,128)(2,1)S(1)} %add_convert_fusion.23), channel_id=1, source_target_pairs={{0,8},{1,9},{2,10},{3,11},{4,12},{5,13},{6,14},{7,15},{8,0},{9,1},... | collective-permute-start | bytes 294920 | tf_op jit(solution)/shard_map/ppermute | solution.py:27
  31.4 10.4 %collective-permute-start.29 = (bf16[16,768]{1,0:T(8,128)(2,1)S(1)}, bf16[16,768]{1,0:T(8,128)(2,1)S(1)}, u32[]{:S(2)}, u32[]{:S(2)}) collective-permute-start(bf16[16,768]{1,0:T(8,128)(2,1)S(1)} %get-tuple-element.220), channel_id=1, source_target_pairs={{1,0},{2,1},{3,2},{4,3},{5,4},{6,5},{7,6},{8,7},{9,8},{10,9},{11,1... | collective-permute-start | bytes 73736 | tf_op jit(solution)/shard_map/ppermute | solution.py:143
  32.7 9.1 %collective-permute-start.28 = (bf16[16,768]{1,0:T(8,128)(2,1)S(1)}, bf16[16,768]{1,0:T(8,128)(2,1)S(1)}, u32[]{:S(2)}, u32[]{:S(2)}) collective-permute-start(bf16[16,768]{1,0:T(8,128)(2,1)S(1)} %get-tuple-element.219), channel_id=1, source_target_pairs={{0,1},{1,2},{2,3},{3,4},{4,5},{5,6},{6,7},{7,8},{8,9},{9,10},{10,1... | collective-permute-start | bytes 73736 | tf_op jit(solution)/shard_map/ppermute | solution.py:141
  36.0 5.6 %collective-permute-start.34 = (bf16[64,768]{1,0:T(8,128)(2,1)S(1)}, bf16[64,768]{1,0:T(8,128)(2,1)S(1)}, u32[]{:S(2)}, u32[]{:S(2)}) collective-permute-start(bf16[64,768]{1,0:T(8,128)(2,1)S(1)} %add_convert_fusion.22), channel_id=1, source_target_pairs={{0,2},{1,3},{2,0},{3,1},{4,6},{5,7},{6,4},{7,5},{8,10},{9,11},{10,... | collective-permute-start | bytes 294920 | tf_op jit(solution)/shard_map/ppermute | solution.py:27
  41.6 1.5 collective-permute-start.35
  55.0 1.5 collective-permute-start.36
  60.1 34.7 %copy-start.30 = (f32[64,3,64]{2,0,1:T(8,128)}, f32[64,3,64]{2,0,1:T(8,128)S(1)}, u32[]{:S(2)}) copy-start(f32[64,3,64]{2,0,1:T(8,128)S(1)} %copy.48) | copy-start | bytes 147460
  60.3 34.5 %copy-start.32 = (f32[64,3,64]{2,0,1:T(8,128)}, f32[64,3,64]{2,0,1:T(8,128)S(1)}, u32[]{:S(2)}) copy-start(f32[64,3,64]{2,0,1:T(8,128)S(1)} %copy.50) | copy-start | bytes 147460
  61.9 7.2 %collective-permute-start.37 = (bf16[64,896]{1,0:T(8,128)(2,1)S(1)}, bf16[64,896]{1,0:T(8,128)(2,1)S(1)}, u32[]{:S(2)}, u32[]{:S(2)}) collective-permute-start(bf16[64,896]{1,0:T(8,128)(2,1)S(1)} %get-tuple-element.223), channel_id=1, source_target_pairs={{0,2},{1,3},{2,0},{3,1},{4,6},{5,7},{6,4},{7,5},{8,10},{9,11},{10,... | collective-permute-start | bytes 344072 | tf_op jit(solution)/shard_map/ppermute | solution.py:27
  68.9 33.1 %copy-start.40 = (f32[12,33]{1,0:T(8,128)S(1)}, f32[12,33]{1,0:T(8,128)}, u32[]{:S(2)}) copy-start(f32[12,33]{1,0:T(8,128)} %param.24) | copy-start | bytes 4756
  68.9 33.1 %copy-start.55 = (f32[768]{0:T(1024)S(1)}, f32[768]{0:T(1024)}, u32[]{:S(2)}) copy-start(f32[768]{0:T(1024)} %param.26) | copy-start | bytes 9220
  69.0 33.1 %copy-start.56 = (f32[768]{0:T(1024)S(1)}, f32[768]{0:T(1024)}, u32[]{:S(2)}) copy-start(f32[768]{0:T(1024)} %param.27) | copy-start | bytes 9220
  69.0 33.1 %copy-start.57 = (f32[768]{0:T(1024)S(1)}, f32[768]{0:T(1024)}, u32[]{:S(2)}) copy-start(f32[768]{0:T(1024)} %param.28) | copy-start | bytes 9220
  69.0 33.1 %copy-start.58 = (f32[768]{0:T(1024)S(1)}, f32[768]{0:T(1024)}, u32[]{:S(2)}) copy-start(f32[768]{0:T(1024)} %param.32) | copy-start | bytes 9220
  69.0 33.1 %copy-start.59 = (f32[768]{0:T(1024)S(1)}, f32[768]{0:T(1024)}, u32[]{:S(2)}) copy-start(f32[768]{0:T(1024)} %param.33) | copy-start | bytes 9220
  69.0 33.1 %copy-start.60 = (f32[768]{0:T(1024)S(1)}, f32[768]{0:T(1024)}, u32[]{:S(2)}) copy-start(f32[768]{0:T(1024)} %param.34) | copy-start | bytes 9220
  72.8 6.0 %collective-permute-start.38 = (bf16[64,1088]{1,0:T(8,128)(2,1)S(1)}, bf16[64,1088]{1,0:T(8,128)(2,1)S(1)}, u32[]{:S(2)}, u32[]{:S(2)}) collective-permute-start(bf16[64,1088]{1,0:T(8,128)(2,1)S(1)} %pad_maximum_fusion.2), channel_id=1, source_target_pairs={{0,4},{1,5},{2,6},{3,7},{4,0},{5,1},{6,2},{7,3},{8,12},{9,13},{10,... | collective-permute-start | bytes 417800 | tf_op jit(solution)/shard_map/ppermute | solution.py:27
  82.6 9.9 %collective-permute-start.39 = (bf16[64,1280]{1,0:T(8,128)(2,1)S(1)}, bf16[64,1280]{1,0:T(8,128)(2,1)S(1)}, u32[]{:S(2)}, u32[]{:S(2)}) collective-permute-start(bf16[64,1280]{1,0:T(8,128)(2,1)S(1)} %pad_maximum_fusion.1), channel_id=1, source_target_pairs={{0,8},{1,9},{2,10},{3,11},{4,12},{5,13},{6,14},{7,15},{8,0},{9,1},... | collective-permute-start | bytes 491528 | tf_op jit(solution)/shard_map/ppermute | solution.py:27
  95.6 5.2 %collective-permute-start.40 = (bf16[64,896]{1,0:T(8,128)(2,1)}, bf16[64,896]{1,0:T(8,128)(2,1)S(1)}, u32[]{:S(2)}, u32[]{:S(2)}) collective-permute-start(bf16[64,896]{1,0:T(8,128)(2,1)} %mix.1), channel_id=1, source_target_pairs={{0,2},{1,3},{2,0},{3,1},{4,6},{5,7},{6,4},{7,5},{8,10},{9,11},{10,... | collective-permute-start | bytes 344072 | tf_op jit(solution)/shard_map/ppermute | solution.py:27
  101.9 1.7 collective-permute-start.41
  104.8 12.0 %copy-start.47 = (f32[3072]{0:T(1024)S(1)}, f32[3072]{0:T(1024)}, u32[]{:S(2)}) copy-start(f32[3072]{0:T(1024)} %param.30) | copy-start | bytes 36868
  183.7 12.3 %copy-start.4 = (bf16[1152,768]{1,0:T(8,128)(2,1)}, bf16[1152,768]{1,0:T(8,128)(2,1)S(1)}, u32[]{:S(2)}) copy-start(bf16[1152,768]{1,0:T(8,128)(2,1)S(1)} %get-tuple-element.56.refs_2_) | copy-start | bytes 5308420 | tf_op jit(solution)/shard_map/cond
  183.7 12.3 %copy-start.7 = (bf16[256,896]{1,0:T(8,128)(2,1)}, bf16[256,896]{1,0:T(8,128)(2,1)S(1)}, u32[]{:S(2)}) copy-start(bf16[256,896]{1,0:T(8,128)(2,1)S(1)} %get-tuple-element.65.refs_6_) | copy-start | bytes 1376260 | tf_op jit(solution)/shard_map/cond
  183.8 12.5 %copy-start.20 = (bf16[64,896]{1,0:T(8,128)(2,1)}, bf16[64,896]{1,0:T(8,128)(2,1)S(1)}, u32[]{:S(2)}) copy-start(bf16[64,896]{1,0:T(8,128)(2,1)S(1)} %get-tuple-element.63.stat_ref) | copy-start | bytes 344068 | tf_op jit(solution)/shard_map/cond
  183.8 6.7 %collective-permute-start = (bf16[128,768]{1,0:T(8,128)(2,1)S(1)}, bf16[128,768]{1,0:T(8,128)(2,1)S(1)}, u32[]{:S(2)}, u32[]{:S(2)}) collective-permute-start(bf16[128,768]{1,0:T(8,128)(2,1)S(1)} %constant_dynamic-slice_fusion.15), channel_id=1, source_target_pairs={{0,1},{1,0},{2,3},{3,2},{4,5},{5,4},{6,7},{7,6},{8,9},{9,8},{10,11... | collective-permute-start | bytes 589832 | tf_op jit(solution)/shard_map/cond/branch_1_fun/ppermute | solution.py:27
  185.3 21.8 %collective-permute-start.5 = (bf16[16,768]{1,0:T(8,128)(2,1)}, bf16[16,768]{1,0:T(8,128)(2,1)}, u32[]{:S(2)}, u32[]{:S(2)}) collective-permute-start(bf16[16,768]{1,0:T(8,128)(2,1)} %get-tuple-element.216), channel_id=1, source_target_pairs={{1,0},{2,1},{3,2},{4,3},{5,4},{6,5},{7,6},{8,7},{9,8},{10,9},{11,1... | collective-permute-start | bytes 73736 | tf_op jit(solution)/shard_map/cond/branch_1_fun/ppermute | solution.py:143
  186.6 20.5 %collective-permute-start.4 = (bf16[16,768]{1,0:T(8,128)(2,1)}, bf16[16,768]{1,0:T(8,128)(2,1)}, u32[]{:S(2)}, u32[]{:S(2)}) collective-permute-start(bf16[16,768]{1,0:T(8,128)(2,1)} %get-tuple-element.215), channel_id=1, source_target_pairs={{0,1},{1,2},{2,3},{3,4},{4,5},{5,6},{6,7},{7,8},{8,9},{9,10},{10,1... | collective-permute-start | bytes 73736 | tf_op jit(solution)/shard_map/cond/branch_1_fun/ppermute | solution.py:141
  190.6 7.9 %collective-permute-start.1 = (bf16[64,768]{1,0:T(8,128)(2,1)S(1)}, bf16[64,768]{1,0:T(8,128)(2,1)}, u32[]{:S(2)}, u32[]{:S(2)}) collective-permute-start(bf16[64,768]{1,0:T(8,128)(2,1)S(1)} %constant_dynamic-slice_fusion.14), channel_id=1, source_target_pairs={{0,2},{1,3},{2,0},{3,1},{4,6},{5,7},{6,4},{7,5},{8,10},{9,11},{10,... | collective-permute-start | bytes 294920 | tf_op jit(solution)/shard_map/cond/branch_1_fun/ppermute | solution.py:27
  199.4 7.6 %collective-permute-start.2 = (bf16[64,768]{1,0:T(8,128)(2,1)S(1)}, bf16[64,768]{1,0:T(8,128)(2,1)S(1)}, u32[]{:S(2)}, u32[]{:S(2)}) collective-permute-start(bf16[64,768]{1,0:T(8,128)(2,1)S(1)} %add_convert_fusion.16), channel_id=1, source_target_pairs={{0,4},{1,5},{2,6},{3,7},{4,0},{5,1},{6,2},{7,3},{8,12},{9,13},{10,... | collective-permute-start | bytes 294920 | tf_op jit(solution)/shard_map/cond/branch_1_fun/ppermute | solution.py:27
  207.1 9.8 %collective-permute-start.3 = (bf16[64,768]{1,0:T(8,128)(2,1)S(1)}, bf16[64,768]{1,0:T(8,128)(2,1)S(1)}, u32[]{:S(2)}, u32[]{:S(2)}) collective-permute-start(bf16[64,768]{1,0:T(8,128)(2,1)S(1)} %add_convert_fusion.15), channel_id=1, source_target_pairs={{0,8},{1,9},{2,10},{3,11},{4,12},{5,13},{6,14},{7,15},{8,0},{9,1},... | collective-permute-start | bytes 294920 | tf_op jit(solution)/shard_map/cond/branch_1_fun/ppermute | solution.py:27
  219.6 5.1 %collective-permute-start.6 = (bf16[64,896]{1,0:T(8,128)(2,1)}, bf16[64,896]{1,0:T(8,128)(2,1)}, u32[]{:S(2)}, u32[]{:S(2)}) collective-permute-start(bf16[64,896]{1,0:T(8,128)(2,1)} %mix_back.1), channel_id=1, source_target_pairs={{0,2},{1,3},{2,0},{3,1},{4,6},{5,7},{6,4},{7,5},{8,10},{9,11},{10,... | collective-permute-start | bytes 344072 | tf_op jit(solution)/shard_map/cond/branch_1_fun/ppermute | solution.py:27
  225.9 5.2 %collective-permute-start.7 = (bf16[128,896]{1,0:T(8,128)(2,1)S(1)}, bf16[128,896]{1,0:T(8,128)(2,1)S(1)}, u32[]{:S(2)}, u32[]{:S(2)}) collective-permute-start(bf16[128,896]{1,0:T(8,128)(2,1)S(1)} %maximum_select_fusion.4), channel_id=1, source_target_pairs={{0,1},{1,0},{2,3},{3,2},{4,5},{5,4},{6,7},{7,6},{8,9},{9,8},{10,11... | collective-permute-start | bytes 688136 | tf_op jit(solution)/shard_map/cond/branch_1_fun/ppermute | solution.py:27
  247.4 24.4 %collective-permute-start.8 = (bf16[768,768]{1,0:T(8,128)(2,1)}, bf16[768,768]{1,0:T(8,128)(2,1)}, u32[]{:S(2)}, u32[]{:S(2)}) collective-permute-start(bf16[768,768]{1,0:T(8,128)(2,1)} %constant_dynamic-slice_fusion.11), channel_id=1, source_target_pairs={{0,1},{1,0},{2,3},{3,2},{4,5},{5,4},{6,7},{7,6},{8,9},{9,8},{10,11... | collective-permute-start | bytes 3538952 | tf_op jit(solution)/shard_map/cond/branch_1_fun/ppermute | solution.py:27
  250.8 12.7 %copy-start.29 = (f32[256,768]{1,0:T(8,128)S(1)}, f32[256,768]{1,0:T(8,128)}, u32[]{:S(2)}) copy-start(f32[256,768]{1,0:T(8,128)} %get-tuple-element.81) | copy-start | bytes 2359300 | tf_op jit(solution)/shard_map/cond
  277.5 17.0 %collective-permute-start.10 = (bf16[384,768]{1,0:T(8,128)(2,1)}, bf16[384,768]{1,0:T(8,128)(2,1)}, u32[]{:S(2)}, u32[]{:S(2)}) collective-permute-start(bf16[384,768]{1,0:T(8,128)(2,1)} %constant_dynamic-slice_fusion.9), channel_id=1, source_target_pairs={{0,16},{16,0},{1,17},{17,1},{2,18},{18,2},{3,19},{19,3},{4,20},{20... | collective-permute-start | bytes 1769480 | tf_op jit(solution)/shard_map/cond/branch_1_fun/ppermute | solution.py:27
  282.0 12.4 %copy-start.15 = (bf16[768,768]{1,0:T(8,128)(2,1)S(1)}, bf16[768,768]{1,0:T(8,128)(2,1)}, u32[]{:S(2)}) copy-start(bf16[768,768]{1,0:T(8,128)(2,1)} %add_convert_fusion.2) | copy-start | bytes 3538948 | tf_op jit(solution)/shard_map/cond
  296.8 18.9 %collective-permute-start.12 = (bf16[896,768]{1,0:T(8,128)(2,1)}, bf16[896,768]{1,0:T(8,128)(2,1)}, u32[]{:S(2)}, u32[]{:S(2)}) collective-permute-start(bf16[896,768]{1,0:T(8,128)(2,1)} %constant_dynamic-slice_fusion.7), channel_id=1, source_target_pairs={{0,1},{1,0},{2,3},{3,2},{4,5},{5,4},{6,7},{7,6},{8,9},{9,8},{10,11... | collective-permute-start | bytes 4128776 | tf_op jit(solution)/shard_map/cond/branch_1_fun/ppermute | solution.py:27
  300.5 1.8 collective-permute-start.9
  301.8 12.9 %collective-permute-start.11 = (bf16[192,768]{1,0:T(8,128)(2,1)}, bf16[192,768]{1,0:T(8,128)(2,1)}, u32[]{:S(2)}, u32[]{:S(2)}) collective-permute-start(bf16[192,768]{1,0:T(8,128)(2,1)} %constant_dynamic-slice_fusion.8), channel_id=1, source_target_pairs={{0,2},{1,3},{2,0},{3,1},{4,6},{5,7},{6,4},{7,5},{8,10},{9,11},{10,... | collective-permute-start | bytes 884744 | tf_op jit(solution)/shard_map/cond/branch_1_fun/ppermute | solution.py:27
  317.4 14.7 %collective-permute-start.15 = (bf16[448,768]{1,0:T(8,128)(2,1)S(1)}, bf16[448,768]{1,0:T(8,128)(2,1)S(1)}, u32[]{:S(2)}, u32[]{:S(2)}) collective-permute-start(bf16[448,768]{1,0:T(8,128)(2,1)S(1)} %constant_dynamic-slice_fusion.4), channel_id=1, source_target_pairs={{0,16},{16,0},{1,17},{17,1},{2,18},{18,2},{3,19},{19,3},{4,20},{20... | collective-permute-start | bytes 2064392 | tf_op jit(solution)/shard_map/cond/branch_1_fun/ppermute | solution.py:27
  317.5 4.7 %collective-permute-start.13 = (bf16[64,768]{1,0:T(8,128)(2,1)S(1)}, bf16[64,768]{1,0:T(8,128)(2,1)S(1)}, u32[]{:S(2)}, u32[]{:S(2)}) collective-permute-start(bf16[64,768]{1,0:T(8,128)(2,1)S(1)} %constant_dynamic-slice_fusion.6), channel_id=1, source_target_pairs={{0,2},{1,3},{2,0},{3,1},{4,6},{5,7},{6,4},{7,5},{8,10},{9,11},{10,... | collective-permute-start | bytes 294920 | tf_op jit(solution)/shard_map/cond/branch_1_fun/ppermute | solution.py:27
  317.7 7.2 %collective-permute-start.14 = (bf16[96,768]{1,0:T(8,128)(2,1)S(1)}, bf16[96,768]{1,0:T(8,128)(2,1)S(1)}, u32[]{:S(2)}, u32[]{:S(2)}) collective-permute-start(bf16[96,768]{1,0:T(8,128)(2,1)S(1)} %constant_dynamic-slice_fusion.5), channel_id=1, source_target_pairs={{0,4},{1,5},{2,6},{3,7},{4,0},{5,1},{6,2},{7,3},{8,12},{9,13},{10,... | collective-permute-start | bytes 442376 | tf_op jit(solution)/shard_map/cond/branch_1_fun/ppermute | solution.py:27
  332.4 7.3 %collective-permute-start.16 = (bf16[64,768]{1,0:T(8,128)(2,1)S(1)}, bf16[64,768]{1,0:T(8,128)(2,1)S(1)}, u32[]{:S(2)}, u32[]{:S(2)}) collective-permute-start(bf16[64,768]{1,0:T(8,128)(2,1)S(1)} %add_convert_fusion.13), channel_id=1, source_target_pairs={{0,4},{1,5},{2,6},{3,7},{4,0},{5,1},{6,2},{7,3},{8,12},{9,13},{10,... | collective-permute-start | bytes 294920 | tf_op jit(solution)/shard_map/cond/branch_1_fun/ppermute | solution.py:27
  332.5 7.0 %collective-permute-start.17 = (bf16[48,768]{1,0:T(8,128)(2,1)S(1)}, bf16[48,768]{1,0:T(8,128)(2,1)S(1)}, u32[]{:S(2)}, u32[]{:S(2)}) collective-permute-start(bf16[48,768]{1,0:T(8,128)(2,1)S(1)} %constant_dynamic-slice_fusion.3), channel_id=1, source_target_pairs={{0,8},{1,9},{2,10},{3,11},{4,12},{5,13},{6,14},{7,15},{8,0},{9,1},... | collective-permute-start | bytes 221192 | tf_op jit(solution)/shard_map/cond/branch_1_fun/ppermute | solution.py:27
  333.5 17.6 %collective-permute-start.18 = (bf16[224,768]{1,0:T(8,128)(2,1)S(1)}, bf16[224,768]{1,0:T(8,128)(2,1)S(1)}, u32[]{:S(2)}, u32[]{:S(2)}) collective-permute-start(bf16[224,768]{1,0:T(8,128)(2,1)S(1)} %constant_dynamic-slice_fusion.2), channel_id=1, source_target_pairs={{0,2},{1,3},{2,0},{3,1},{4,6},{5,7},{6,4},{7,5},{8,10},{9,11},{10,... | collective-permute-start | bytes 1032200 | tf_op jit(solution)/shard_map/cond/branch_1_fun/ppermute | solution.py:27
  351.2 13.7 %collective-permute-start.19 = (bf16[64,768]{1,0:T(8,128)(2,1)S(1)}, bf16[64,768]{1,0:T(8,128)(2,1)S(1)}, u32[]{:S(2)}, u32[]{:S(2)}) collective-permute-start(bf16[64,768]{1,0:T(8,128)(2,1)S(1)} %add_convert_fusion.12), channel_id=1, source_target_pairs={{0,8},{1,9},{2,10},{3,11},{4,12},{5,13},{6,14},{7,15},{8,0},{9,1},... | collective-permute-start | bytes 294920 | tf_op jit(solution)/shard_map/cond/branch_1_fun/ppermute | solution.py:27
  351.3 13.6 %collective-permute-start.20 = (bf16[48,768]{1,0:T(8,128)(2,1)S(1)}, bf16[48,768]{1,0:T(8,128)(2,1)S(1)}, u32[]{:S(2)}, u32[]{:S(2)}) collective-permute-start(bf16[48,768]{1,0:T(8,128)(2,1)S(1)} %add_convert_fusion.18), channel_id=1, source_target_pairs={{0,8},{1,9},{2,10},{3,11},{4,12},{5,13},{6,14},{7,15},{8,0},{9,1},... | collective-permute-start | bytes 221192 | tf_op jit(solution)/shard_map/cond/branch_1_fun/ppermute | solution.py:27
  354.2 12.8 %collective-permute-start.21 = (bf16[112,768]{1,0:T(8,128)(2,1)S(1)}, bf16[112,768]{1,0:T(8,128)(2,1)S(1)}, u32[]{:S(2)}, u32[]{:S(2)}) collective-permute-start(bf16[112,768]{1,0:T(8,128)(2,1)S(1)} %constant_dynamic-slice_fusion.1), channel_id=1, source_target_pairs={{0,4},{1,5},{2,6},{3,7},{4,0},{5,1},{6,2},{7,3},{8,12},{9,13},{10,... | collective-permute-start | bytes 516104 | tf_op jit(solution)/shard_map/cond/branch_1_fun/ppermute | solution.py:27
  367.0 8.2 %collective-permute-start.24 = (bf16[56,768]{1,0:T(8,128)(2,1)S(1)}, bf16[56,768]{1,0:T(8,128)(2,1)S(1)}, u32[]{:S(2)}, u32[]{:S(2)}) collective-permute-start(bf16[56,768]{1,0:T(8,128)(2,1)S(1)} %constant_dynamic-slice_fusion), channel_id=1, source_target_pairs={{0,8},{1,9},{2,10},{3,11},{4,12},{5,13},{6,14},{7,15},{8,0},{9,1},... | collective-permute-start | bytes 258056 | tf_op jit(solution)/shard_map/cond/branch_1_fun/ppermute | solution.py:27
  369.5 5.9 %collective-permute-start.22 = (bf16[64,768]{1,0:T(8,128)(2,1)S(1)}, bf16[64,768]{1,0:T(8,128)(2,1)S(1)}, u32[]{:S(2)}, u32[]{:S(2)}) collective-permute-start(bf16[64,768]{1,0:T(8,128)(2,1)S(1)} %add_convert_fusion.11), channel_id=1, source_target_pairs={{0,2},{1,3},{2,0},{3,1},{4,6},{5,7},{6,4},{7,5},{8,10},{9,11},{10,... | collective-permute-start | bytes 294920 | tf_op jit(solution)/shard_map/cond/branch_1_fun/ppermute | solution.py:27
  371.7 8.9 %collective-permute-start.23 = (bf16[96,768]{1,0:T(8,128)(2,1)S(1)}, bf16[96,768]{1,0:T(8,128)(2,1)S(1)}, u32[]{:S(2)}, u32[]{:S(2)}) collective-permute-start(bf16[96,768]{1,0:T(8,128)(2,1)S(1)} %maximum_select_fusion.7), channel_id=1, source_target_pairs={{0,4},{1,5},{2,6},{3,7},{4,0},{5,1},{6,2},{7,3},{8,12},{9,13},{10,... | collective-permute-start | bytes 442376 | tf_op jit(solution)/shard_map/cond/branch_1_fun/ppermute | solution.py:27
  380.6 8.2 %collective-permute-start.27 = (bf16[56,768]{1,0:T(8,128)(2,1)S(1)}, bf16[56,768]{1,0:T(8,128)(2,1)S(1)}, u32[]{:S(2)}, u32[]{:S(2)}) collective-permute-start(bf16[56,768]{1,0:T(8,128)(2,1)S(1)} %add_convert_fusion.17), channel_id=1, source_target_pairs={{0,8},{1,9},{2,10},{3,11},{4,12},{5,13},{6,14},{7,15},{8,0},{9,1},... | collective-permute-start | bytes 258056 | tf_op jit(solution)/shard_map/cond/branch_1_fun/ppermute | solution.py:27
  382.6 6.9 %collective-permute-start.25 = (bf16[128,768]{1,0:T(8,128)(2,1)S(1)}, bf16[128,768]{1,0:T(8,128)(2,1)S(1)}, u32[]{:S(2)}, u32[]{:S(2)}) collective-permute-start(bf16[128,768]{1,0:T(8,128)(2,1)S(1)} %maximum_select_fusion.5), channel_id=1, source_target_pairs={{0,1},{1,0},{2,3},{3,2},{4,5},{5,4},{6,7},{7,6},{8,9},{9,8},{10,11... | collective-permute-start | bytes 589832 | tf_op jit(solution)/shard_map/cond/branch_1_fun/ppermute | solution.py:27
  382.6 9.4 %collective-permute-start.26 = (bf16[192,768]{1,0:T(8,128)(2,1)S(1)}, bf16[192,768]{1,0:T(8,128)(2,1)S(1)}, u32[]{:S(2)}, u32[]{:S(2)}) collective-permute-start(bf16[192,768]{1,0:T(8,128)(2,1)S(1)} %maximum_select_fusion.3), channel_id=1, source_target_pairs={{0,2},{1,3},{2,0},{3,1},{4,6},{5,7},{6,4},{7,5},{8,10},{9,11},{10,... | collective-permute-start | bytes 884744 | tf_op jit(solution)/shard_map/cond/branch_1_fun/ppermute | solution.py:27
  393.3 7.8 %collective-permute-start.43 = (bf16[112,768]{1,0:T(8,128)(2,1)}, bf16[112,768]{1,0:T(8,128)(2,1)S(1)}, u32[]{:S(2)}, u32[]{:S(2)}) collective-permute-start(bf16[112,768]{1,0:T(8,128)(2,1)} %get-tuple-element.197), channel_id=1, source_target_pairs={{0,4},{1,5},{2,6},{3,7},{4,0},{5,1},{6,2},{7,3},{8,12},{9,13},{10,... | collective-permute-start | bytes 516104 | tf_op jit(solution)/shard_map/ppermute | solution.py:27
  402.2 9.8 %collective-permute-start.44 = (bf16[224,768]{1,0:T(8,128)(2,1)S(1)}, bf16[224,768]{1,0:T(8,128)(2,1)S(1)}, u32[]{:S(2)}, u32[]{:S(2)}) collective-permute-start(bf16[224,768]{1,0:T(8,128)(2,1)S(1)} %maximum_select_fusion.13), channel_id=1, source_target_pairs={{0,2},{1,3},{2,0},{3,1},{4,6},{5,7},{6,4},{7,5},{8,10},{9,11},{10,... | collective-permute-start | bytes 1032200 | tf_op jit(solution)/shard_map/ppermute | solution.py:27
  403.3 31.2 %collective-permute-start.42 = (bf16[384,768]{1,0:T(8,128)(2,1)}, bf16[384,768]{1,0:T(8,128)(2,1)S(1)}, u32[]{:S(2)}, u32[]{:S(2)}) collective-permute-start(bf16[384,768]{1,0:T(8,128)(2,1)} %get-tuple-element.194), channel_id=1, source_target_pairs={{0,16},{16,0},{1,17},{17,1},{2,18},{18,2},{3,19},{19,3},{4,20},{20... | collective-permute-start | bytes 1769480 | tf_op jit(solution)/shard_map/ppermute | solution.py:27
  424.3 16.2 %collective-permute-start.45 = (bf16[448,768]{1,0:T(8,128)(2,1)S(1)}, bf16[448,768]{1,0:T(8,128)(2,1)S(1)}, u32[]{:S(2)}, u32[]{:S(2)}) collective-permute-start(bf16[448,768]{1,0:T(8,128)(2,1)S(1)} %maximum_select_fusion.10), channel_id=1, source_target_pairs={{0,16},{16,0},{1,17},{17,1},{2,18},{18,2},{3,19},{19,3},{4,20},{20... | collective-permute-start | bytes 2064392 | tf_op jit(solution)/shard_map/ppermute | solution.py:27
  441.1 2.9 collective-permute-start.47
  441.2 4.8 %collective-permute-start.46 = (bf16[896,768]{1,0:T(8,128)(2,1)S(1)}, bf16[896,768]{1,0:T(8,128)(2,1)S(1)}, u32[]{:S(2)}, u32[]{:S(2)}) collective-permute-start(bf16[896,768]{1,0:T(8,128)(2,1)S(1)} %maximum_select_fusion.8.late_ref), channel_id=1, source_target_pairs={{0,1},{1,0},{2,3},{3,2},{4,5},{5,4},{6,7},{7,6},{8,9},{9,8},{10,11... | collective-permute-start | bytes 4128776 | tf_op jit(solution)/shard_map/ppermute | solution.py:27
  (57 other events, 272.4 us)
Sparse Core Ops, SparseCore 0:
  183.2 216.9 all-reduce.7

commit v10 on v9

--- a/solution.py
+++ b/solution.py
@@ -279,11 +279,13 @@
     exp_a, exp_b = jnp.exp(first - top), jnp.exp(second - top)
     both = exp_a + exp_b
     level = top + jnp.log(both)
-    pick = head_lanes(heads, width)
-    share_a = jnp.dot(exp_a / both, pick, precision=HIGH, preferred_element_type=F32)
-    share_b = jnp.dot(exp_b / both, pick, precision=HIGH, preferred_element_type=F32)
-    joined = a_ref[:, :width].astype(F32) * share_a + b_ref[:, :width].astype(F32) * share_b
-    out_ref[:, :width] = joined.astype(BF)
+    pick = head_lanes(heads, width).astype(BF)
+    share = exp_b / both
+    high = share.astype(BF)
+    low = (share - high.astype(F32)).astype(BF)
+    share = dot_nn(jnp.concatenate([high, low], 1), jnp.concatenate([pick, pick], 0))
+    from_a, from_b = a_ref[:, :width].astype(F32), b_ref[:, :width].astype(F32)
+    out_ref[:, :width] = (from_a + share * (from_b - from_a)).astype(BF)
     level = jnp.where(lane < heads, level, 0.0)
     level = level + pltpu.roll(level, 16, 1) + pltpu.roll(level, 32, 1)
     out_ref[:, width:] = split_three(level)
@@ -863,8 +865,9 @@
     )(bounds, qkv, grad_mixed, probs, mark_k, mix)
     grad_w_down = lax.dot_general(active, grad_low_two, rows_in, preferred_element_type=F32)
     grad_w_up = lax.dot_general(hidden_low, grad_upper, rows_in, preferred_element_type=F32)
-    grad_mix, grad_w_down, grad_w_up = lax.optimization_barrier(
-        (grad_mix.astype(BF), grad_w_down.astype(BF), grad_w_up.astype(BF))
+    grad_ext = extended(grad_mixed, radius, window_rows)
+    grad_mix, grad_w_down, grad_w_up, grad_ext = lax.optimization_barrier(
+        (grad_mix.astype(BF), grad_w_down.astype(BF), grad_w_up.astype(BF), grad_ext)
     )
     sum_w_down, sum_w_up = lax.psum((grad_w_down, grad_w_up), ("row", "seq"))
 
@@ -872,7 +875,6 @@
         grad_mix = seq_quarter(grad_mix.astype(BF), add_join)
         grad_w_out = lax.dot_general(mixed, grad_low_one, rows_in, preferred_element_type=F32)
 
-        grad_ext = extended(grad_mixed, radius, window_rows)
         grad_conv, products = pl.pallas_call(
             lambda *refs: conv_back_kernel(docs, *refs),
             grid=(blocks,),
@@ -977,13 +979,16 @@
         late = lax.dynamic_update_slice_in_dim(
             late, (weight_grad(grad_keys) + mark_grad_k).astype(BF), width + spare_rows, 0
         )
-        late, (early,) = tied(late, [early])
         late = begin(late, ORDER, ORDER)
+        grad_projected = jnp.concatenate([grad_queries, grad_keys, grad_values], axis=1)
+        grad_input = grad_one + lax.dot_general(
+            grad_projected, w_qkv, cols_in, preferred_element_type=F32
+        )
         for step in seq_steps():
             mark_back = step(mark_back)
             early, late = advance(early, 1), advance(late, 1)
-            mark_back, (early, late) = tied(mark_back, [early, late])
-        return early[0], late[0], mark_back, grad_keys, grad_values
+            (mark_back, grad_input), (early, late) = tied((mark_back, grad_input), [early, late])
+        return early[0], late[0], mark_back, grad_input
 
     plan = stages(ORDER)
     sent = len(seq_steps())
@@ -996,11 +1001,10 @@
 
     def nothing(*unused):
         return tuple(
-            jnp.zeros((rows, width), BF)
-            for rows in (early_rows, late_rows, mark_count, tok_count, tok_count)
-        )
-
-    early, late, mark_back, grad_keys, grad_values = lax.cond(
+            jnp.zeros((rows, width), BF) for rows in (early_rows, late_rows, mark_count)
+        ) + (jnp.zeros((tok_count, width), F32),)
+
+    early, late, mark_back, grad_input = lax.cond(
         lengths[0] > 0, remaining, nothing, grad_mix, grad_mk, stats, mix
     )
     early, late = (early, plan, plan, sent + 2), (late, plan, plan, sent)
@@ -1010,11 +1014,8 @@
         (sum_w_down.astype(F32), sum_w_up.astype(F32)), [late]
     )
     early, late = advance(early, last - early[3]), advance(late, last - late[3])
-    grad_projected = jnp.concatenate([grad_queries, grad_keys, grad_values], axis=1)
-    grad_input = (
-        grad_one
-        + lax.dot_general(grad_projected, w_qkv, cols_in, preferred_element_type=F32)
-        + lax.dot_general(onehot, mark_back, rows_in, preferred_element_type=F32)
+    grad_input = grad_input + lax.dot_general(
+        onehot, mark_back, rows_in, preferred_element_type=F32
     )
     grad_input, (early, late) = tied(grad_input, [early, late])
     early, early_other = last_swap(early)[:2]

time: 472 us -> 483 us (1.023)
  local copies, waits for them, and re-layouts: 37.5 us -> 47.2 us
  other arithmetic: 43.4 us -> 51.6 us
  transfers between devices with their start and end apart: 49 -> 49, of which waited for: 33 -> 32; matrix products, arithmetic and copies ran while one was open for 21% -> 25% of each run, Pallas kernels for 8% -> 10%
where the time goes in v10:
time: 483 us; the launch traced here: 474 us
  waiting for transfers between devices  146 us (30%)
  Pallas kernels  123 us (25%)
  matrix products  51.9 us (11%)
  other arithmetic  51.6 us (11%)
  local copies, waits for them, and re-layouts  47.2 us (10%)
  starting transfers between devices  38 us (8%)
  between operations  15.5 us (3%)
    ppermute x44, waiting for transfers between devices, swap(): return lax.ppermute(array, axis, [(i, i ^ bit) for i in range(count)])  146 us
    pallas_call x1, Pallas kernels, per_device(): pl.pallas_call(ffn_kernel, grid=(tok_count // FFN_BLOCK,), in_specs=[ffn_...  39.9 us
    ppermute x44, starting transfers between devices, swap(): return lax.ppermute(array, axis, [(i, i ^ bit) for i in range(count)])  32.2 us
    pallas_call x1, Pallas kernels, per_device(): pl.pallas_call(lambda *refs: token_kernel(docs, scale, *refs), grid=(bloc...  12.2 us
    pallas_call x1, Pallas kernels, per_device(): pl.pallas_call(lambda *refs: token_back_kernel(docs, scale, *refs), grid=...  10.9 us
    pallas_call x1, Pallas kernels, remaining(): pl.pallas_call(lambda *refs: landmark_back_kernel(docs, scale, *refs), gr...  10.8 us
    pallas_call x1, Pallas kernels, remaining(): pl.pallas_call(lambda *refs: pinv_back_kernel(scale, *refs), out_shape=(s...  9.96 us
    select_n x16, other arithmetic, paired(): jnp.where(side == 0, jnp.concatenate([array, other], dim), jnp.concatenat...  9.87 us
  transfers between devices with their start and end apart: 49, of which 32 were waited for; matrix products, arithmetic and copies ran while one was open for 25% of the time, Pallas kernels for 10%

profile of v10, /device:TPU:0, one launch (start us, length us, event | category | flops | bytes accessed | tf_op | source)
XLA Modules:
  0.0 474.0 jit_solution(17899261039855552085)
XLA Ops:
  10.9 2.2 fusion.29
  14.8 3.0 collective-permute-start.29
  17.8 3.1 collective-permute-done.29
  20.9 1.9 collective-permute-start.30
  22.7 6.0 %add_convert_fusion.20.refs_2_.refs_3_.refs_1_ = bf16[1024,2304]{1,0:T(8,128)(2,1)S(1)} fusion(bf16[768,2304]{1,0:T(8,128)(2,1)} %param.21, f32[2304]{0:T(1024)S(1)} %pad_maximum_fusion.3, bf16[1,1024,768]{2,1,0:T(8,128)(2,1)S(1)} %copy-done.25), kind=kOutput, calls=%fused_computation.74 | convolution fusion | flops 3628597248 | bytes 9839616 | tf_op jit(solution)/shard_map/dot_general | solution.py:736
  28.9 2.7 collective-permute-start.31
  35.7 3.2 collective-permute-start.32
  38.9 3.3 collective-permute-done.32
  44.0 2.6 fusion.27
  46.8 8.1 %landmark.1 = bf16[256,896]{1,0:T(8,128)(2,1)S(1)} custom-call(s32[8]{0:T(128)S(1)} %add_subtract_fusion.refs_0_, bf16[256,768]{1,0:T(8,128)(2,1)S(1)} %fusion.31.refs_1_, bf16[1024,2304]{1,0:T(8,128)(2,1)S(1)} %bitcast.62, bf16[1024,2304]{1,0:T(8,128)(2,1)S(1)} %bitcast.62), custom_call_target="tpu_custom_call" | custom-call | tf_op jit(solution)/shard_map/landmark/pallas_call | solution.py:743
  57.8 2.0 join.4
  62.0 6.0 %pinv.1 = (f32[3,64,64]{2,1,0:T(8,128)}, f32[3,64,64]{2,1,0:T(8,128)}, f32[72,64,64]{2,1,0:T(8,128)}) custom-call(f32[3,64,64]{2,1,0:T(8,128)S(1)} %bitcast.69, f32[3,64,64]{2,1,0:T(8,128)S(1)} %bitcast.71), custom_call_target="tpu_custom_call" | custom-call | tf_op jit(solution)/shard_map/pinv/pallas_call | solution.py:776
  69.8 1.9 join.5.a_ref
  72.7 5.9 %collective-permute-done.36 = bf16[64,1088]{1,0:T(8,128)(2,1)S(1)} collective-permute-done((bf16[64,1088]{1,0:T(8,128)(2,1)S(1)}, bf16[64,1088]{1,0:T(8,128)(2,1)S(1)}, u32[]{:S(2)}, u32[]{:S(2)}) %collective-permute-start.36) | collective-permute-done | bytes 139296 | tf_op jit(solution)/shard_map/ppermute | solution.py:27
  79.2 1.9 join.6.a_ref
  82.2 9.8 %collective-permute-done.37 = bf16[64,1280]{1,0:T(8,128)(2,1)S(1)} collective-permute-done((bf16[64,1280]{1,0:T(8,128)(2,1)S(1)}, bf16[64,1280]{1,0:T(8,128)(2,1)S(1)}, u32[]{:S(2)}, u32[]{:S(2)}) %collective-permute-start.37) | collective-permute-done | bytes 163872 | tf_op jit(solution)/shard_map/ppermute | solution.py:27
  96.2 3.8 collective-permute-done.38
  102.8 12.2 %token_.1 = (bf16[1024,768]{1,0:T(8,128)(2,1)S(1)}, bf16[768,1024]{1,0:T(8,128)(2,1)S(1)}) custom-call(s32[8]{0:T(128)} %copy-done.48, bf16[1024,2304]{1,0:T(8,128)(2,1)} %copy-done.8, bf16[1152,768]{1,0:T(8,128)(2,1)} %maximum_maximum_fusion.refs_2_, bf16[256,768]{1,0:T(8,128)(2,1)S(1)} %slice.189.refs_3_.refs_4_, ...), custom_call_target="tpu_custom_call" | custom-call | tf_op jit(solution)/shard_map/token/pallas_call | solution.py:804
  115.7 39.9 %ffn.1 = (f32[1024,768]{1,0:T(8,128)}, f32[1024,768]{1,0:T(8,128)}, bf16[1024,3072]{1,0:T(8,128)(2,1)}, bf16[1024,3072]{1,0:T(8,128)(2,1)}, bf16[1024,768]{1,0:T...) custom-call(bf16[1024,768]{1,0:T(8,128)(2,1)S(1)} %bitcast.68, ...), custom_call_target="tpu_custom_call" | custom-call | tf_op jit(solution)/shard_map/ffn/pallas_call | solution.py:826
  156.9 1.9 collective-permute-start.40
  160.1 9.7 %convolution_convert_fusion.3 = bf16[3072,768]{1,0:T(8,128)(2,1)} fusion(bf16[1024,3072]{1,0:T(8,128)(2,1)} %get-tuple-element.185, bf16[1024,768]{1,0:T(8,128)(2,1)} %get-tuple-element.186), kind=kOutput, calls=%fused_computation.76 | convolution fusion | flops 4834197504 | bytes 12582912 | tf_op jit(solution)/shard_map/dot_general | solution.py:866
  169.9 6.8 %convolution_convert_fusion.2 = bf16[768,3072]{1,0:T(8,128)(2,1)} fusion(bf16[1024,768]{1,0:T(8,128)(2,1)S(1)} %copy-done.76, bf16[1024,3072]{1,0:T(8,128)(2,1)S(1)} %copy-done.73), kind=kOutput, calls=%fused_computation.75 | convolution fusion | flops 4834197504 | bytes 12582912 | tf_op jit(solution)/shard_map/dot_general | solution.py:867
  176.7 10.9 %token_back.1 = (bf16[1024,768]{1,0:T(8,128)(2,1)}, f32[256,768]{1,0:T(8,128)S(1)}, f32[256,768]{1,0:T(8,128)}) custom-call(s32[8]{0:T(128)S(1)} %copy-done.49, bf16[1024,2304]{1,0:T(8,128)(2,1)} %copy-done.8, bf16[1024,768]{1,0:T(8,128)(2,1)S(1)} %copy-done, bf16[768,1024]{1,0:T(8,128)(2,1)S(1)} %get-tuple-element.183.refs_3_, ...), custom_call_target="tpu_custom_call" | custom-call | tf_op jit(solution)/shard_map/token_back/pallas_call | solution.py:850
  187.7 2.3 maximum_maximum_fusion.1
  191.6 212.7 %conditional.1 = (bf16[384,768]{1,0:T(8,128)(2,1)}, bf16[112,768]{1,0:T(8,128)(2,1)}, bf16[256,768]{1,0:T(8,128)(2,1)}, f32[1024,768]{1,0:T(8,128)}) conditional(s32[]{:T(128)} %bitcast.23, () %tuple.32, (bf16[256,768]{1,0:T(8,128)(2,1)S(1)}, f32[12,33]{1,0:T(8,128)S(1)}, s32[8]{0:T(128)S(1)}, bf16[1152,768]{1,0:T(8,128)(2,1)}, ...), branch_computations={%region_1.2_spmd, %region_2.6_spmd} | conditional | flops 9714861056 | bytes 264522528 | solution.py:1007
  193.2 7.3 %collective-permute-done.1 = bf16[64,768]{1,0:T(8,128)(2,1)S(1)} collective-permute-done((bf16[64,768]{1,0:T(8,128)(2,1)S(1)}, bf16[64,768]{1,0:T(8,128)(2,1)S(1)}, u32[]{:S(2)}, u32[]{:S(2)}) %collective-permute-start.1) | collective-permute-done | bytes 98336 | tf_op jit(solution)/shard_map/cond/branch_1_fun/ppermute | solution.py:27
  201.2 3.9 convolution_convert_fusion.1
  205.2 7.6 %conv_back.1 = (f32[1024,768]{1,0:T(8,128)S(1)}, f32[16,256]{1,0:T(8,128)S(1)}) custom-call(s32[8]{0:T(128)S(1)} %get-tuple-element.54.refs_0_, bf16[1152,768]{1,0:T(8,128)(2,1)} %get-tuple-element.57.refs_1_, bf16[1152,768]{1,0:T(8,128)(2,1)} %get-tuple-element.58.refs_2_, f32[12,256]{1,0:T(8,128)S(1)} %pad.17.refs_3_), custom_call_target="tpu_custom_call" | custom-call | tf_op jit(solution)/shard_map/cond/branch_1_fun/conv_back/pallas_call | solution.py:878
  222.1 6.8 %collective-permute-done.3 = bf16[64,768]{1,0:T(8,128)(2,1)} collective-permute-done((bf16[64,768]{1,0:T(8,128)(2,1)}, bf16[64,768]{1,0:T(8,128)(2,1)}, u32[]{:S(2)}, u32[]{:S(2)}) %collective-permute-start.3) | collective-permute-done | bytes 98336 | tf_op jit(solution)/shard_map/cond/branch_1_fun/ppermute | solution.py:27
  230.5 2.1 mix_back.1
  239.0 4.9 %fusion.48 = f32[768,768]{1,0:T(8,128)} fusion(bf16[1024,768]{1,0:T(8,128)(2,1)} %get-tuple-element.78, bf16[1024,768]{1,0:T(8,128)(2,1)} %get-tuple-element.88), kind=kOutput, calls=%fused_computation.152 | convolution fusion | flops 1207959552 | bytes 5505024 | tf_op jit(solution)/shard_map/cond/branch_1_fun/dot_general | solution.py:920
  244.0 10.8 %landmark_back.1 = (bf16[1024,768]{1,0:T(8,128)(2,1)S(1)}, bf16[1024,768]{1,0:T(8,128)(2,1)S(1)}, f32[256,768]{1,0:T(8,128)S(1)}) custom-call(s32[8]{0:T(128)S(1)} %get-tuple-element.54.refs_0_, bf16[1024,2304]{1,0:T(8,128)(2,1)S(1)} %bitcast.64, bf16[1024,2304]{1,0:T(8,128)(2,1)S(1)} %bitcast.64, f32[1024,768]{1,0:T(8,128)S(1)} %get-tuple-element.62.refs_3_, ...), custom_call_target="tpu_custom_call" | custom-call | tf_op jit(solution)/shard_map/cond/branch_1_fun/landmark_back/pallas_call | solution.py:902
  263.3 10.0 %pinv_back.1 = (f32[3,64,64]{2,1,0:T(8,128)}, f32[3,64,64]{2,1,0:T(8,128)}) custom-call(f32[3,64,64]{2,1,0:T(8,128)S(1)} %copy-done.37, f32[3,64,64]{2,1,0:T(8,128)S(1)} %copy-done.39, f32[3,64,64]{2,1,0:T(8,128)S(1)} %copy-done.43, f32[72,64,64]{2,1,0:T(8,128)} %get-tuple-element.74.refs_3_, bf16[3,64,64]{2,1,0:T(8,128)(2,1)} %bitcast.81, ...), custom_call_target="tpu_custom_call" | custom-call | tf_op jit(solution)/shard_map/cond/branch_1_fun/pinv_back/pallas_call | solution.py:928
  275.3 3.0 dynamic_update_slice.18
  279.5 3.0 fusion.49
  284.2 1.8 copy.46
  286.0 3.0 add_convert_fusion.2
  293.8 2.4 dynamic_update_slice.16
  305.6 11.1 %collective-permute-done.8 = bf16[384,768]{1,0:T(8,128)(2,1)S(1)} collective-permute-done((bf16[384,768]{1,0:T(8,128)(2,1)S(1)}, bf16[384,768]{1,0:T(8,128)(2,1)S(1)}, u32[]{:S(2)}, u32[]{:S(2)}) %collective-permute-start.8) | collective-permute-done | bytes 589856 | tf_op jit(solution)/shard_map/cond/branch_1_fun/ppermute | solution.py:27
  317.0 5.5 %fusion.9 = f32[1024,768]{1,0:T(8,128)} fusion(f32[1024,768]{1,0:T(8,128)S(1)} %copy-done.75, bf16[768,2304]{1,0:T(8,128)(2,1)S(1)} %copy-done.74, bf16[1024,768]{1,0:T(8,128)(2,1)S(1)} %copy-done.2, bf16[1024,768]{1,0:T(8,128)(2,1)S(1)} %copy-done.7, bf16[1024,768]{1,0:T(8,128)(2,1)S(1)} %copy-done.31), kind=kOutput, calls=%fused_computation.15 | convolution fusion | flops 3638820864 | bytes 14548992 | tf_op jit(solution)/shard_map/cond/branch_1_fun/dot_general | solution.py:984
  322.5 3.6 collective-permute-done.9
  329.1 3.8 collective-permute-done.11
  332.9 2.2 collective-permute-done.12
  335.1 12.4 %collective-permute-done.13 = bf16[448,768]{1,0:T(8,128)(2,1)S(1)} collective-permute-done((bf16[448,768]{1,0:T(8,128)(2,1)S(1)}, bf16[448,768]{1,0:T(8,128)(2,1)S(1)}, u32[]{:S(2)}, u32[]{:S(2)}) %collective-permute-start.13) | collective-permute-done | bytes 688160 | tf_op jit(solution)/shard_map/cond/branch_1_fun/ppermute | solution.py:27
  348.0 6.6 %collective-permute-done.15 = bf16[48,768]{1,0:T(8,128)(2,1)S(1)} collective-permute-done((bf16[48,768]{1,0:T(8,128)(2,1)S(1)}, bf16[48,768]{1,0:T(8,128)(2,1)S(1)}, u32[]{:S(2)}, u32[]{:S(2)}) %collective-permute-start.15) | collective-permute-done | bytes 73760 | tf_op jit(solution)/shard_map/cond/branch_1_fun/ppermute | solution.py:27
  355.5 6.9 %collective-permute-done.16 = bf16[224,768]{1,0:T(8,128)(2,1)S(1)} collective-permute-done((bf16[224,768]{1,0:T(8,128)(2,1)S(1)}, bf16[224,768]{1,0:T(8,128)(2,1)S(1)}, u32[]{:S(2)}, u32[]{:S(2)}) %collective-permute-start.16) | collective-permute-done | bytes 344096 | tf_op jit(solution)/shard_map/cond/branch_1_fun/ppermute | solution.py:27
  362.5 2.5 collective-permute-start.18
  365.6 4.3 collective-permute-done.18
  370.0 9.6 %collective-permute-done.17 = bf16[64,768]{1,0:T(8,128)(2,1)S(1)} collective-permute-done((bf16[64,768]{1,0:T(8,128)(2,1)S(1)}, bf16[64,768]{1,0:T(8,128)(2,1)S(1)}, u32[]{:S(2)}, u32[]{:S(2)}) %collective-permute-start.17) | collective-permute-done | bytes 98336 | tf_op jit(solution)/shard_map/cond/branch_1_fun/ppermute | solution.py:27
  379.7 3.5 collective-permute-start.22
  383.9 4.1 collective-permute-done.22
  388.1 5.1 %collective-permute-done.21 = bf16[96,768]{1,0:T(8,128)(2,1)S(1)} collective-permute-done((bf16[96,768]{1,0:T(8,128)(2,1)S(1)}, bf16[96,768]{1,0:T(8,128)(2,1)S(1)}, u32[]{:S(2)}, u32[]{:S(2)}) %collective-permute-start.21) | collective-permute-done | bytes 147488 | tf_op jit(solution)/shard_map/cond/branch_1_fun/ppermute | solution.py:27
  394.2 6.8 %collective-permute-done.25 = bf16[56,768]{1,0:T(8,128)(2,1)S(1)} collective-permute-done((bf16[56,768]{1,0:T(8,128)(2,1)S(1)}, bf16[56,768]{1,0:T(8,128)(2,1)S(1)}, u32[]{:S(2)}, u32[]{:S(2)}) %collective-permute-start.25) | collective-permute-done | bytes 86048 | tf_op jit(solution)/shard_map/cond/branch_1_fun/ppermute | solution.py:27
  404.2 2.5 collective-permute-start.43
  406.8 4.4 collective-permute-done.43
  414.0 7.3 %collective-permute-done.44 = bf16[224,768]{1,0:T(8,128)(2,1)S(1)} collective-permute-done((bf16[224,768]{1,0:T(8,128)(2,1)S(1)}, bf16[224,768]{1,0:T(8,128)(2,1)S(1)}, u32[]{:S(2)}, u32[]{:S(2)}) %collective-permute-start.44) | collective-permute-done | bytes 344096 | tf_op jit(solution)/shard_map/ppermute | solution.py:27
  421.7 7.0 %convert_element_type.348 = f32[3072,768]{1,0:T(8,128)} convert(bf16[3072,768]{1,0:T(8,128)(2,1)} %get-tuple-element.220) | non-fusion elementwise | flops 2359296 | bytes 14155776 | tf_op jit(solution)/shard_map/convert_element_type | solution.py:1014
  428.6 5.0 %convert_element_type.349 = f32[768,3072]{1,0:T(8,128)} convert(bf16[768,3072]{1,0:T(8,128)(2,1)S(1)} %copy-done.15) | non-fusion elementwise | flops 2359296 | bytes 14155776 | tf_op jit(solution)/shard_map/convert_element_type | solution.py:1014
  434.7 1.9 fusion.30
  436.6 4.0 add.373
  442.2 7.1 %collective-permute-done.45 = bf16[448,768]{1,0:T(8,128)(2,1)} collective-permute-done((bf16[448,768]{1,0:T(8,128)(2,1)S(1)}, bf16[448,768]{1,0:T(8,128)(2,1)}, u32[]{:S(2)}, u32[]{:S(2)}) %collective-permute-start.45) | collective-permute-done | bytes 688160 | tf_op jit(solution)/shard_map/ppermute | solution.py:27
  449.3 1.8 maximum_select_fusion.8.late_ref
  451.7 2.3 collective-permute-done.47.early_other_ref
  459.1 7.6 %settle_qkv.1 = f32[768,2304]{1,0:T(8,128)} custom-call(s32[1]{0:T(128)} %bitcast.25.side_ref, bf16[896,768]{1,0:T(8,128)(2,1)} %copy-done.13, bf16[896,768]{1,0:T(8,128)(2,1)} %copy-done.24, bf16[768,768]{1,0:T(8,128)(2,1)} %copy-done.9, bf16[768,768]{1,0:T(8,128)(2,1)} %copy-done.14), custom_call_target="tpu_custom_call" | custom-call | tf_op jit(solution)/shard_map/settle_qkv/pallas_call | solution.py:673
  (382 shorter events, 101.2 us)
Async XLA Ops:
  7.2 414.5 %all-reduce.8.cloned.1.call-start = ((), (), s32[]{:S(2)}) async-start(), calls=%async_computation | async-start | bytes 18874368 | tf_op jit(solution)/shard_map/psum | solution.py:872
  13.1 1.6 collective-permute-start.28
  14.8 6.0 %collective-permute-start.29 = (bf16[64,768]{1,0:T(8,128)(2,1)S(1)}, bf16[64,768]{1,0:T(8,128)(2,1)S(1)}, u32[]{:S(2)}, u32[]{:S(2)}) collective-permute-start(bf16[64,768]{1,0:T(8,128)(2,1)S(1)} %constant_dynamic-slice_fusion.20), channel_id=1, source_target_pairs={{0,2},{1,3},{2,0},{3,1},{4,6},{5,7},{6,4},{7,5},{8,10},{9,11},{10,... | collective-permute-start | bytes 294920 | tf_op jit(solution)/shard_map/ppermute | solution.py:27
  20.9 7.9 %collective-permute-start.30 = (bf16[64,768]{1,0:T(8,128)(2,1)S(1)}, bf16[64,768]{1,0:T(8,128)(2,1)S(1)}, u32[]{:S(2)}, u32[]{:S(2)}) collective-permute-start(bf16[64,768]{1,0:T(8,128)(2,1)S(1)} %add_convert_fusion.24), channel_id=1, source_target_pairs={{0,4},{1,5},{2,6},{3,7},{4,0},{5,1},{6,2},{7,3},{8,12},{9,13},{10,... | collective-permute-start | bytes 294920 | tf_op jit(solution)/shard_map/ppermute | solution.py:27
  28.9 6.8 %collective-permute-start.31 = (bf16[64,768]{1,0:T(8,128)(2,1)S(1)}, bf16[64,768]{1,0:T(8,128)(2,1)S(1)}, u32[]{:S(2)}, u32[]{:S(2)}) collective-permute-start(bf16[64,768]{1,0:T(8,128)(2,1)S(1)} %add_convert_fusion.23), channel_id=1, source_target_pairs={{0,8},{1,9},{2,10},{3,11},{4,12},{5,13},{6,14},{7,15},{8,0},{9,1},... | collective-permute-start | bytes 294920 | tf_op jit(solution)/shard_map/ppermute | solution.py:27
  31.5 10.8 %collective-permute-start.26 = (bf16[16,768]{1,0:T(8,128)(2,1)S(1)}, bf16[16,768]{1,0:T(8,128)(2,1)S(1)}, u32[]{:S(2)}, u32[]{:S(2)}) collective-permute-start(bf16[16,768]{1,0:T(8,128)(2,1)S(1)} %get-tuple-element.224), channel_id=1, source_target_pairs={{0,1},{1,2},{2,3},{3,4},{4,5},{5,6},{6,7},{7,8},{8,9},{9,10},{10,1... | collective-permute-start | bytes 73736 | tf_op jit(solution)/shard_map/ppermute | solution.py:141
  32.8 9.5 %collective-permute-start.27 = (bf16[16,768]{1,0:T(8,128)(2,1)S(1)}, bf16[16,768]{1,0:T(8,128)(2,1)S(1)}, u32[]{:S(2)}, u32[]{:S(2)}) collective-permute-start(bf16[16,768]{1,0:T(8,128)(2,1)S(1)} %get-tuple-element.225), channel_id=1, source_target_pairs={{1,0},{2,1},{3,2},{4,3},{5,4},{6,5},{7,6},{8,7},{9,8},{10,9},{11,1... | collective-permute-start | bytes 73736 | tf_op jit(solution)/shard_map/ppermute | solution.py:143
  34.1 12.6 %slice-start = ((s8[4718592]{0:T(1024)(128)(4,1)}), s8[4194304]{0:T(1024)(128)(4,1)S(1)}, s32[]{:S(2)}) async-start(s8[4718592]{0:T(1024)(128)(4,1)} %bitcast.61), calls=%async_computation.1 | async-start | bytes 8388608
  35.7 6.5 %collective-permute-start.32 = (bf16[64,768]{1,0:T(8,128)(2,1)S(1)}, bf16[64,768]{1,0:T(8,128)(2,1)S(1)}, u32[]{:S(2)}, u32[]{:S(2)}) collective-permute-start(bf16[64,768]{1,0:T(8,128)(2,1)S(1)} %add_convert_fusion.22), channel_id=1, source_target_pairs={{0,2},{1,3},{2,0},{3,1},{4,6},{5,7},{6,4},{7,5},{8,10},{9,11},{10,... | collective-permute-start | bytes 294920 | tf_op jit(solution)/shard_map/ppermute | solution.py:27
  42.2 1.7 collective-permute-start.33
  46.7 14.8 %copy-start.17 = (bf16[256,768]{1,0:T(8,128)(2,1)}, bf16[256,768]{1,0:T(8,128)(2,1)S(1)}, u32[]{:S(2)}) copy-start(bf16[256,768]{1,0:T(8,128)(2,1)S(1)} %fusion.31.refs_1_) | copy-start | bytes 1179652
  55.6 1.5 collective-permute-start.34
  61.5 7.7 %collective-permute-start.35 = (bf16[64,896]{1,0:T(8,128)(2,1)S(1)}, bf16[64,896]{1,0:T(8,128)(2,1)S(1)}, u32[]{:S(2)}, u32[]{:S(2)}) collective-permute-start(bf16[64,896]{1,0:T(8,128)(2,1)S(1)} %get-tuple-element.230), channel_id=1, source_target_pairs={{0,2},{1,3},{2,0},{3,1},{4,6},{5,7},{6,4},{7,5},{8,10},{9,11},{10,... | collective-permute-start | bytes 344072 | tf_op jit(solution)/shard_map/ppermute | solution.py:27
  61.8 30.2 %copy-start.36 = (f32[64,3,64]{2,0,1:T(8,128)}, f32[64,3,64]{2,0,1:T(8,128)S(1)}, u32[]{:S(2)}) copy-start(f32[64,3,64]{2,0,1:T(8,128)S(1)} %copy.48) | copy-start | bytes 147460
  62.0 30.0 %copy-start.38 = (f32[64,3,64]{2,0,1:T(8,128)}, f32[64,3,64]{2,0,1:T(8,128)S(1)}, u32[]{:S(2)}) copy-start(f32[64,3,64]{2,0,1:T(8,128)S(1)} %copy.50) | copy-start | bytes 147460
  69.0 32.2 %copy-start.46 = (f32[12,33]{1,0:T(8,128)S(1)}, f32[12,33]{1,0:T(8,128)}, u32[]{:S(2)}) copy-start(f32[12,33]{1,0:T(8,128)} %param.24) | copy-start | bytes 4756
  69.0 32.2 %copy-start.60 = (f32[768]{0:T(1024)S(1)}, f32[768]{0:T(1024)}, u32[]{:S(2)}) copy-start(f32[768]{0:T(1024)} %param.26) | copy-start | bytes 9220
  69.0 32.2 %copy-start.61 = (f32[768]{0:T(1024)S(1)}, f32[768]{0:T(1024)}, u32[]{:S(2)}) copy-start(f32[768]{0:T(1024)} %param.27) | copy-start | bytes 9220
  69.0 32.2 %copy-start.62 = (f32[768]{0:T(1024)S(1)}, f32[768]{0:T(1024)}, u32[]{:S(2)}) copy-start(f32[768]{0:T(1024)} %param.28) | copy-start | bytes 9220
  69.0 32.2 %copy-start.63 = (f32[768]{0:T(1024)S(1)}, f32[768]{0:T(1024)}, u32[]{:S(2)}) copy-start(f32[768]{0:T(1024)} %param.32) | copy-start | bytes 9220
  69.0 32.2 %copy-start.64 = (f32[768]{0:T(1024)S(1)}, f32[768]{0:T(1024)}, u32[]{:S(2)}) copy-start(f32[768]{0:T(1024)} %param.33) | copy-start | bytes 9220
  69.1 32.2 %copy-start.65 = (f32[768]{0:T(1024)S(1)}, f32[768]{0:T(1024)}, u32[]{:S(2)}) copy-start(f32[768]{0:T(1024)} %param.34) | copy-start | bytes 9220
  72.6 6.0 %collective-permute-start.36 = (bf16[64,1088]{1,0:T(8,128)(2,1)S(1)}, bf16[64,1088]{1,0:T(8,128)(2,1)S(1)}, u32[]{:S(2)}, u32[]{:S(2)}) collective-permute-start(bf16[64,1088]{1,0:T(8,128)(2,1)S(1)} %pad_maximum_fusion.2), channel_id=1, source_target_pairs={{0,4},{1,5},{2,6},{3,7},{4,0},{5,1},{6,2},{7,3},{8,12},{9,13},{10,... | collective-permute-start | bytes 417800 | tf_op jit(solution)/shard_map/ppermute | solution.py:27
  82.1 9.9 %collective-permute-start.37 = (bf16[64,1280]{1,0:T(8,128)(2,1)S(1)}, bf16[64,1280]{1,0:T(8,128)(2,1)S(1)}, u32[]{:S(2)}, u32[]{:S(2)}) collective-permute-start(bf16[64,1280]{1,0:T(8,128)(2,1)S(1)} %pad_maximum_fusion.1), channel_id=1, source_target_pairs={{0,8},{1,9},{2,10},{3,11},{4,12},{5,13},{6,14},{7,15},{8,0},{9,1},... | collective-permute-start | bytes 491528 | tf_op jit(solution)/shard_map/ppermute | solution.py:27
  94.8 5.2 %collective-permute-start.38 = (bf16[64,896]{1,0:T(8,128)(2,1)}, bf16[64,896]{1,0:T(8,128)(2,1)S(1)}, u32[]{:S(2)}, u32[]{:S(2)}) collective-permute-start(bf16[64,896]{1,0:T(8,128)(2,1)} %mix.1), channel_id=1, source_target_pairs={{0,2},{1,3},{2,0},{3,1},{4,6},{5,7},{6,4},{7,5},{8,10},{9,11},{10,... | collective-permute-start | bytes 344072 | tf_op jit(solution)/shard_map/ppermute | solution.py:27
  101.1 1.6 collective-permute-start.39
  102.7 12.9 %copy-start.26 = (bf16[1,1024,768]{2,1,0:T(8,128)(2,1)S(1)}, bf16[1,1024,768]{2,1,0:T(8,128)(2,1)}, u32[]{:S(2)}) copy-start(bf16[1,1024,768]{2,1,0:T(8,128)(2,1)} %param.19) | copy-start | bytes 4718596
  115.0 40.6 %copy-start.28 = (bf16[1024,768]{1,0:T(8,128)(2,1)}, bf16[1024,768]{1,0:T(8,128)(2,1)S(1)}, u32[]{:S(2)}) copy-start(bf16[1024,768]{1,0:T(8,128)(2,1)S(1)} %get-tuple-element.180.mixed_ref) | copy-start | bytes 4718596
  156.9 30.7 %collective-permute-start.40 = (bf16[16,768]{1,0:T(8,128)(2,1)}, bf16[16,768]{1,0:T(8,128)(2,1)}, u32[]{:S(2)}, u32[]{:S(2)}) collective-permute-start(bf16[16,768]{1,0:T(8,128)(2,1)} %get-tuple-element.226), channel_id=1, source_target_pairs={{0,1},{1,2},{2,3},{3,4},{4,5},{5,6},{6,7},{7,8},{8,9},{9,10},{10,1... | collective-permute-start | bytes 73736 | tf_op jit(solution)/shard_map/ppermute | solution.py:141
  158.8 28.8 %collective-permute-start.41 = (bf16[16,768]{1,0:T(8,128)(2,1)}, bf16[16,768]{1,0:T(8,128)(2,1)}, u32[]{:S(2)}, u32[]{:S(2)}) collective-permute-start(bf16[16,768]{1,0:T(8,128)(2,1)} %get-tuple-element.227), channel_id=1, source_target_pairs={{1,0},{2,1},{3,2},{4,3},{5,4},{6,5},{7,6},{8,7},{9,8},{10,9},{11,1... | collective-permute-start | bytes 73736 | tf_op jit(solution)/shard_map/ppermute | solution.py:143
  191.6 1.5 collective-permute-start
  193.2 7.4 %collective-permute-start.1 = (bf16[64,768]{1,0:T(8,128)(2,1)S(1)}, bf16[64,768]{1,0:T(8,128)(2,1)S(1)}, u32[]{:S(2)}, u32[]{:S(2)}) collective-permute-start(bf16[64,768]{1,0:T(8,128)(2,1)S(1)} %constant_dynamic-slice_fusion.14), channel_id=1, source_target_pairs={{0,2},{1,3},{2,0},{3,1},{4,6},{5,7},{6,4},{7,5},{8,10},{9,11},{10,... | collective-permute-start | bytes 294920 | tf_op jit(solution)/shard_map/cond/branch_1_fun/ppermute | solution.py:27
  201.2 15.6 %collective-permute-start.2 = (bf16[64,768]{1,0:T(8,128)(2,1)}, bf16[64,768]{1,0:T(8,128)(2,1)}, u32[]{:S(2)}, u32[]{:S(2)}) collective-permute-start(bf16[64,768]{1,0:T(8,128)(2,1)} %add_convert_fusion.16), channel_id=1, source_target_pairs={{0,4},{1,5},{2,6},{3,7},{4,0},{5,1},{6,2},{7,3},{8,12},{9,13},{10,... | collective-permute-start | bytes 294920 | tf_op jit(solution)/shard_map/cond/branch_1_fun/ppermute | solution.py:27
  218.4 10.5 %collective-permute-start.3 = (bf16[64,768]{1,0:T(8,128)(2,1)}, bf16[64,768]{1,0:T(8,128)(2,1)}, u32[]{:S(2)}, u32[]{:S(2)}) collective-permute-start(bf16[64,768]{1,0:T(8,128)(2,1)} %add_convert_fusion.15), channel_id=1, source_target_pairs={{0,8},{1,9},{2,10},{3,11},{4,12},{5,13},{6,14},{7,15},{8,0},{9,1},... | collective-permute-start | bytes 294920 | tf_op jit(solution)/shard_map/cond/branch_1_fun/ppermute | solution.py:27
  232.6 5.1 %collective-permute-start.4 = (bf16[64,896]{1,0:T(8,128)(2,1)}, bf16[64,896]{1,0:T(8,128)(2,1)}, u32[]{:S(2)}, u32[]{:S(2)}) collective-permute-start(bf16[64,896]{1,0:T(8,128)(2,1)} %mix_back.1), channel_id=1, source_target_pairs={{0,2},{1,3},{2,0},{3,1},{4,6},{5,7},{6,4},{7,5},{8,10},{9,11},{10,... | collective-permute-start | bytes 344072 | tf_op jit(solution)/shard_map/cond/branch_1_fun/ppermute | solution.py:27
  238.8 5.0 %collective-permute-start.5 = (bf16[128,896]{1,0:T(8,128)(2,1)S(1)}, bf16[128,896]{1,0:T(8,128)(2,1)S(1)}, u32[]{:S(2)}, u32[]{:S(2)}) collective-permute-start(bf16[128,896]{1,0:T(8,128)(2,1)S(1)} %maximum_select_fusion.4), channel_id=1, source_target_pairs={{0,1},{1,0},{2,3},{3,2},{4,5},{5,4},{6,7},{7,6},{8,9},{9,8},{10,11... | collective-permute-start | bytes 688136 | tf_op jit(solution)/shard_map/cond/branch_1_fun/ppermute | solution.py:27
  259.7 26.3 %collective-permute-start.6 = (bf16[768,768]{1,0:T(8,128)(2,1)}, bf16[768,768]{1,0:T(8,128)(2,1)}, u32[]{:S(2)}, u32[]{:S(2)}) collective-permute-start(bf16[768,768]{1,0:T(8,128)(2,1)} %constant_dynamic-slice_fusion.11), channel_id=1, source_target_pairs={{0,1},{1,0},{2,3},{3,2},{4,5},{5,4},{6,7},{7,6},{8,9},{9,8},{10,11... | collective-permute-start | bytes 3538952 | tf_op jit(solution)/shard_map/cond/branch_1_fun/ppermute | solution.py:27
  263.3 16.2 %copy-start.6 = (bf16[1024,768]{1,0:T(8,128)(2,1)S(1)}, bf16[1024,768]{1,0:T(8,128)(2,1)}, u32[]{:S(2)}) copy-start(bf16[1024,768]{1,0:T(8,128)(2,1)} %copy-done.5) | copy-start | bytes 4718596 | tf_op jit(solution)/shard_map/cond
  299.1 17.5 %collective-permute-start.8 = (bf16[384,768]{1,0:T(8,128)(2,1)S(1)}, bf16[384,768]{1,0:T(8,128)(2,1)S(1)}, u32[]{:S(2)}, u32[]{:S(2)}) collective-permute-start(bf16[384,768]{1,0:T(8,128)(2,1)S(1)} %constant_dynamic-slice_fusion.9), channel_id=1, source_target_pairs={{0,16},{16,0},{1,17},{17,1},{2,18},{18,2},{3,19},{19,3},{4,20},{20... | collective-permute-start | bytes 1769480 | tf_op jit(solution)/shard_map/cond/branch_1_fun/ppermute | solution.py:27
  302.4 23.8 %collective-permute-start.10 = (bf16[896,768]{1,0:T(8,128)(2,1)S(1)}, bf16[896,768]{1,0:T(8,128)(2,1)S(1)}, u32[]{:S(2)}, u32[]{:S(2)}) collective-permute-start(bf16[896,768]{1,0:T(8,128)(2,1)S(1)} %constant_dynamic-slice_fusion.7), channel_id=1, source_target_pairs={{0,1},{1,0},{2,3},{3,2},{4,5},{5,4},{6,7},{7,6},{8,9},{9,8},{10,11... | collective-permute-start | bytes 4128776 | tf_op jit(solution)/shard_map/cond/branch_1_fun/ppermute | solution.py:27
  305.3 17.2 %collective-permute-start.7 = (bf16[128,768]{1,0:T(8,128)(2,1)S(1)}, bf16[128,768]{1,0:T(8,128)(2,1)S(1)}, u32[]{:S(2)}, u32[]{:S(2)}) collective-permute-start(bf16[128,768]{1,0:T(8,128)(2,1)S(1)} %constant_dynamic-slice_fusion.10), channel_id=1, source_target_pairs={{0,1},{1,0},{2,3},{3,2},{4,5},{5,4},{6,7},{7,6},{8,9},{9,8},{10,11... | collective-permute-start | bytes 589832 | tf_op jit(solution)/shard_map/cond/branch_1_fun/ppermute | solution.py:27
  316.9 9.3 %collective-permute-start.9 = (bf16[192,768]{1,0:T(8,128)(2,1)S(1)}, bf16[192,768]{1,0:T(8,128)(2,1)S(1)}, u32[]{:S(2)}, u32[]{:S(2)}) collective-permute-start(bf16[192,768]{1,0:T(8,128)(2,1)S(1)} %constant_dynamic-slice_fusion.8), channel_id=1, source_target_pairs={{0,2},{1,3},{2,0},{3,1},{4,6},{5,7},{6,4},{7,5},{8,10},{9,11},{10,... | collective-permute-start | bytes 884744 | tf_op jit(solution)/shard_map/cond/branch_1_fun/ppermute | solution.py:27
  326.7 20.8 %collective-permute-start.13 = (bf16[448,768]{1,0:T(8,128)(2,1)S(1)}, bf16[448,768]{1,0:T(8,128)(2,1)S(1)}, u32[]{:S(2)}, u32[]{:S(2)}) collective-permute-start(bf16[448,768]{1,0:T(8,128)(2,1)S(1)} %constant_dynamic-slice_fusion.4), channel_id=1, source_target_pairs={{0,16},{16,0},{1,17},{17,1},{2,18},{18,2},{3,19},{19,3},{4,20},{20... | collective-permute-start | bytes 2064392 | tf_op jit(solution)/shard_map/cond/branch_1_fun/ppermute | solution.py:27
  328.2 4.7 collective-permute-start.11
  328.8 6.3 %collective-permute-start.12 = (bf16[96,768]{1,0:T(8,128)(2,1)S(1)}, bf16[96,768]{1,0:T(8,128)(2,1)S(1)}, u32[]{:S(2)}, u32[]{:S(2)}) collective-permute-start(bf16[96,768]{1,0:T(8,128)(2,1)S(1)} %constant_dynamic-slice_fusion.5), channel_id=1, source_target_pairs={{0,4},{1,5},{2,6},{3,7},{4,0},{5,1},{6,2},{7,3},{8,12},{9,13},{10,... | collective-permute-start | bytes 442376 | tf_op jit(solution)/shard_map/cond/branch_1_fun/ppermute | solution.py:27
  347.7 6.9 %collective-permute-start.15 = (bf16[48,768]{1,0:T(8,128)(2,1)S(1)}, bf16[48,768]{1,0:T(8,128)(2,1)S(1)}, u32[]{:S(2)}, u32[]{:S(2)}) collective-permute-start(bf16[48,768]{1,0:T(8,128)(2,1)S(1)} %constant_dynamic-slice_fusion.3), channel_id=1, source_target_pairs={{0,8},{1,9},{2,10},{3,11},{4,12},{5,13},{6,14},{7,15},{8,0},{9,1},... | collective-permute-start | bytes 221192 | tf_op jit(solution)/shard_map/cond/branch_1_fun/ppermute | solution.py:27
  347.8 14.6 %collective-permute-start.16 = (bf16[224,768]{1,0:T(8,128)(2,1)S(1)}, bf16[224,768]{1,0:T(8,128)(2,1)S(1)}, u32[]{:S(2)}, u32[]{:S(2)}) collective-permute-start(bf16[224,768]{1,0:T(8,128)(2,1)S(1)} %constant_dynamic-slice_fusion.2), channel_id=1, source_target_pairs={{0,2},{1,3},{2,0},{3,1},{4,6},{5,7},{6,4},{7,5},{8,10},{9,11},{10,... | collective-permute-start | bytes 1032200 | tf_op jit(solution)/shard_map/cond/branch_1_fun/ppermute | solution.py:27
  347.9 7.5 %collective-permute-start.14 = (bf16[64,768]{1,0:T(8,128)(2,1)S(1)}, bf16[64,768]{1,0:T(8,128)(2,1)S(1)}, u32[]{:S(2)}, u32[]{:S(2)}) collective-permute-start(bf16[64,768]{1,0:T(8,128)(2,1)S(1)} %add_convert_fusion.13), channel_id=1, source_target_pairs={{0,4},{1,5},{2,6},{3,7},{4,0},{5,1},{6,2},{7,3},{8,12},{9,13},{10,... | collective-permute-start | bytes 294920 | tf_op jit(solution)/shard_map/cond/branch_1_fun/ppermute | solution.py:27
  362.5 7.4 %collective-permute-start.18 = (bf16[48,768]{1,0:T(8,128)(2,1)S(1)}, bf16[48,768]{1,0:T(8,128)(2,1)S(1)}, u32[]{:S(2)}, u32[]{:S(2)}) collective-permute-start(bf16[48,768]{1,0:T(8,128)(2,1)S(1)} %add_convert_fusion.18), channel_id=1, source_target_pairs={{0,8},{1,9},{2,10},{3,11},{4,12},{5,13},{6,14},{7,15},{8,0},{9,1},... | collective-permute-start | bytes 221192 | tf_op jit(solution)/shard_map/cond/branch_1_fun/ppermute | solution.py:27
  365.0 14.6 %collective-permute-start.19 = (bf16[112,768]{1,0:T(8,128)(2,1)S(1)}, bf16[112,768]{1,0:T(8,128)(2,1)S(1)}, u32[]{:S(2)}, u32[]{:S(2)}) collective-permute-start(bf16[112,768]{1,0:T(8,128)(2,1)S(1)} %constant_dynamic-slice_fusion.1), channel_id=1, source_target_pairs={{0,4},{1,5},{2,6},{3,7},{4,0},{5,1},{6,2},{7,3},{8,12},{9,13},{10,... | collective-permute-start | bytes 516104 | tf_op jit(solution)/shard_map/cond/branch_1_fun/ppermute | solution.py:27
  365.1 14.5 %collective-permute-start.17 = (bf16[64,768]{1,0:T(8,128)(2,1)S(1)}, bf16[64,768]{1,0:T(8,128)(2,1)S(1)}, u32[]{:S(2)}, u32[]{:S(2)}) collective-permute-start(bf16[64,768]{1,0:T(8,128)(2,1)S(1)} %add_convert_fusion.12), channel_id=1, source_target_pairs={{0,8},{1,9},{2,10},{3,11},{4,12},{5,13},{6,14},{7,15},{8,0},{9,1},... | collective-permute-start | bytes 294920 | tf_op jit(solution)/shard_map/cond/branch_1_fun/ppermute | solution.py:27
  379.7 8.4 %collective-permute-start.22 = (bf16[56,768]{1,0:T(8,128)(2,1)S(1)}, bf16[56,768]{1,0:T(8,128)(2,1)S(1)}, u32[]{:S(2)}, u32[]{:S(2)}) collective-permute-start(bf16[56,768]{1,0:T(8,128)(2,1)S(1)} %constant_dynamic-slice_fusion), channel_id=1, source_target_pairs={{0,8},{1,9},{2,10},{3,11},{4,12},{5,13},{6,14},{7,15},{8,0},{9,1},... | collective-permute-start | bytes 258056 | tf_op jit(solution)/shard_map/cond/branch_1_fun/ppermute | solution.py:27
  383.1 10.1 %collective-permute-start.21 = (bf16[96,768]{1,0:T(8,128)(2,1)S(1)}, bf16[96,768]{1,0:T(8,128)(2,1)S(1)}, u32[]{:S(2)}, u32[]{:S(2)}) collective-permute-start(bf16[96,768]{1,0:T(8,128)(2,1)S(1)} %maximum_select_fusion.7), channel_id=1, source_target_pairs={{0,4},{1,5},{2,6},{3,7},{4,0},{5,1},{6,2},{7,3},{8,12},{9,13},{10,... | collective-permute-start | bytes 442376 | tf_op jit(solution)/shard_map/cond/branch_1_fun/ppermute | solution.py:27
  383.2 4.9 %collective-permute-start.20 = (bf16[64,768]{1,0:T(8,128)(2,1)S(1)}, bf16[64,768]{1,0:T(8,128)(2,1)S(1)}, u32[]{:S(2)}, u32[]{:S(2)}) collective-permute-start(bf16[64,768]{1,0:T(8,128)(2,1)S(1)} %add_convert_fusion.11), channel_id=1, source_target_pairs={{0,2},{1,3},{2,0},{3,1},{4,6},{5,7},{6,4},{7,5},{8,10},{9,11},{10,... | collective-permute-start | bytes 294920 | tf_op jit(solution)/shard_map/cond/branch_1_fun/ppermute | solution.py:27
  393.3 7.7 %collective-permute-start.25 = (bf16[56,768]{1,0:T(8,128)(2,1)S(1)}, bf16[56,768]{1,0:T(8,128)(2,1)S(1)}, u32[]{:S(2)}, u32[]{:S(2)}) collective-permute-start(bf16[56,768]{1,0:T(8,128)(2,1)S(1)} %add_convert_fusion.17), channel_id=1, source_target_pairs={{0,8},{1,9},{2,10},{3,11},{4,12},{5,13},{6,14},{7,15},{8,0},{9,1},... | collective-permute-start | bytes 258056 | tf_op jit(solution)/shard_map/cond/branch_1_fun/ppermute | solution.py:27
  393.4 8.3 %collective-permute-start.23 = (bf16[128,768]{1,0:T(8,128)(2,1)S(1)}, bf16[128,768]{1,0:T(8,128)(2,1)S(1)}, u32[]{:S(2)}, u32[]{:S(2)}) collective-permute-start(bf16[128,768]{1,0:T(8,128)(2,1)S(1)} %maximum_select_fusion.5), channel_id=1, source_target_pairs={{0,1},{1,0},{2,3},{3,2},{4,5},{5,4},{6,7},{7,6},{8,9},{9,8},{10,11... | collective-permute-start | bytes 589832 | tf_op jit(solution)/shard_map/cond/branch_1_fun/ppermute | solution.py:27
  393.5 9.4 %collective-permute-start.24 = (bf16[192,768]{1,0:T(8,128)(2,1)S(1)}, bf16[192,768]{1,0:T(8,128)(2,1)S(1)}, u32[]{:S(2)}, u32[]{:S(2)}) collective-permute-start(bf16[192,768]{1,0:T(8,128)(2,1)S(1)} %maximum_select_fusion.3), channel_id=1, source_target_pairs={{0,2},{1,3},{2,0},{3,1},{4,6},{5,7},{6,4},{7,5},{8,10},{9,11},{10,... | collective-permute-start | bytes 884744 | tf_op jit(solution)/shard_map/cond/branch_1_fun/ppermute | solution.py:27
  404.2 7.0 %collective-permute-start.43 = (bf16[112,768]{1,0:T(8,128)(2,1)}, bf16[112,768]{1,0:T(8,128)(2,1)S(1)}, u32[]{:S(2)}, u32[]{:S(2)}) collective-permute-start(bf16[112,768]{1,0:T(8,128)(2,1)} %get-tuple-element.204), channel_id=1, source_target_pairs={{0,4},{1,5},{2,6},{3,7},{4,0},{5,1},{6,2},{7,3},{8,12},{9,13},{10,... | collective-permute-start | bytes 516104 | tf_op jit(solution)/shard_map/ppermute | solution.py:27
  412.3 9.1 %collective-permute-start.44 = (bf16[224,768]{1,0:T(8,128)(2,1)S(1)}, bf16[224,768]{1,0:T(8,128)(2,1)S(1)}, u32[]{:S(2)}, u32[]{:S(2)}) collective-permute-start(bf16[224,768]{1,0:T(8,128)(2,1)S(1)} %maximum_select_fusion.13), channel_id=1, source_target_pairs={{0,2},{1,3},{2,0},{3,1},{4,6},{5,7},{6,4},{7,5},{8,10},{9,11},{10,... | collective-permute-start | bytes 1032200 | tf_op jit(solution)/shard_map/ppermute | solution.py:27
  413.1 27.5 %collective-permute-start.42 = (bf16[384,768]{1,0:T(8,128)(2,1)}, bf16[384,768]{1,0:T(8,128)(2,1)S(1)}, u32[]{:S(2)}, u32[]{:S(2)}) collective-permute-start(bf16[384,768]{1,0:T(8,128)(2,1)} %get-tuple-element.201), channel_id=1, source_target_pairs={{0,16},{16,0},{1,17},{17,1},{2,18},{18,2},{3,19},{19,3},{4,20},{20... | collective-permute-start | bytes 1769480 | tf_op jit(solution)/shard_map/ppermute | solution.py:27
  433.7 15.6 %collective-permute-start.45 = (bf16[448,768]{1,0:T(8,128)(2,1)S(1)}, bf16[448,768]{1,0:T(8,128)(2,1)}, u32[]{:S(2)}, u32[]{:S(2)}) collective-permute-start(bf16[448,768]{1,0:T(8,128)(2,1)S(1)} %maximum_select_fusion.10), channel_id=1, source_target_pairs={{0,16},{16,0},{1,17},{17,1},{2,18},{18,2},{3,19},{19,3},{4,20},{20... | collective-permute-start | bytes 2064392 | tf_op jit(solution)/shard_map/ppermute | solution.py:27
  442.2 13.5 %copy-start.9 = (bf16[768,768]{1,0:T(8,128)(2,1)}, bf16[768,768]{1,0:T(8,128)(2,1)S(1)}, u32[]{:S(2)}) copy-start(bf16[768,768]{1,0:T(8,128)(2,1)S(1)} %maximum_select_fusion.9.early_ref) | copy-start | bytes 3538948
  451.1 2.9 collective-permute-start.47
  451.2 4.8 %collective-permute-start.46 = (bf16[896,768]{1,0:T(8,128)(2,1)S(1)}, bf16[896,768]{1,0:T(8,128)(2,1)S(1)}, u32[]{:S(2)}, u32[]{:S(2)}) collective-permute-start(bf16[896,768]{1,0:T(8,128)(2,1)S(1)} %maximum_select_fusion.8.late_ref), channel_id=1, source_target_pairs={{0,1},{1,0},{2,3},{3,2},{4,5},{5,4},{6,7},{7,6},{8,9},{9,8},{10,11... | collective-permute-start | bytes 4128776 | tf_op jit(solution)/shard_map/ppermute | solution.py:27
  (67 other events, 321.7 us)
Sparse Core Ops, SparseCore 0:
  190.2 214.5 all-reduce.7

commit v11 on v10

--- a/solution.py
+++ b/solution.py
@@ -649,7 +649,7 @@
 
 def settle_qkv_kernel(side_ref, late_ref, late_other_ref, early_ref, early_other_ref, out_ref):
     part = pl.program_id(0)
-    own = jnp.where(part == 0, 0, 1) == side_ref[0]
+    own = jnp.where(part == 2, pl.program_id(1), part) == side_ref[0]
     choices = [
         (late_ref, own & (part < 2)),
         (late_other_ref, jnp.logical_not(own) & (part < 2)),
@@ -675,7 +675,7 @@
         grid_spec=pltpu.PrefetchScalarGridSpec(
             num_scalar_prefetch=1,
             grid=(3, 2),
-            in_specs=[spec(lambda j: j < 2), spec(lambda j: j < 2)] + [spec(lambda j: j == 2)] * 2,
+            in_specs=[spec(lambda j: j < 2)] * 2 + [spec(lambda j: j < 0)] * 2,
             out_specs=pl.BlockSpec((rows, width), lambda j, i, s: (i, j)),
         ),
         out_shape=jax.ShapeDtypeStruct((width, 3 * width), F32),
@@ -865,16 +865,18 @@
     )(bounds, qkv, grad_mixed, probs, mark_k, mix)
     grad_w_down = lax.dot_general(active, grad_low_two, rows_in, preferred_element_type=F32)
     grad_w_up = lax.dot_general(hidden_low, grad_upper, rows_in, preferred_element_type=F32)
-    grad_ext = extended(grad_mixed, radius, window_rows)
-    grad_mix, grad_w_down, grad_w_up, grad_ext = lax.optimization_barrier(
-        (grad_mix.astype(BF), grad_w_down.astype(BF), grad_w_up.astype(BF), grad_ext)
-    )
-    sum_w_down, sum_w_up = lax.psum((grad_w_down, grad_w_up), ("row", "seq"))
+    grad_w_out = lax.dot_general(mixed, grad_low_one, rows_in, preferred_element_type=F32)
+    grad_mix, grad_w_down, grad_w_up, grad_w_out = lax.optimization_barrier(
+        (grad_mix.astype(BF), grad_w_down.astype(BF), grad_w_up.astype(BF), grad_w_out.astype(BF))
+    )
+    sum_w_down, sum_w_up, sum_w_out = lax.psum(
+        (grad_w_down, grad_w_up, grad_w_out), ("row", "seq")
+    )
 
     def remaining(grad_mix, grad_mk, stats, mix):
         grad_mix = seq_quarter(grad_mix.astype(BF), add_join)
-        grad_w_out = lax.dot_general(mixed, grad_low_one, rows_in, preferred_element_type=F32)
-
+
+        grad_ext = extended(grad_mixed, radius, window_rows)
         grad_conv, products = pl.pallas_call(
             lambda *refs: conv_back_kernel(docs, *refs),
             grid=(blocks,),
@@ -919,10 +921,7 @@
         def weight_grad(grads):
             return lax.dot_general(tokens, grads, rows_in, preferred_element_type=F32)
 
-        early = jnp.pad(grad_w_out.astype(BF), ((0, width), (0, 0)))
-        early = lax.dynamic_update_slice_in_dim(
-            early, weight_grad(grad_values).astype(BF), width, 0
-        )
+        early = weight_grad(grad_values).astype(BF)
         grad_mix, early = lax.optimization_barrier((grad_mix, early))
         early = advance(begin(early, ORDER, ORDER), 1)
         grad_mq_small, grad_mk_small = pl.pallas_call(
@@ -996,7 +995,7 @@
     def rows_left(rows, done):
         return rows >> min(done, 2 * len(plan) - done)
 
-    early_rows = rows_left(2 * width, sent + 2)
+    early_rows = rows_left(width, sent + 2)
     late_rows = rows_left(2 * width + width // 3, sent)
 
     def nothing(*unused):
@@ -1010,8 +1009,8 @@
     early, late = (early, plan, plan, sent + 2), (late, plan, plan, sent)
     last = 2 * len(plan) - 1
     late = advance(late, 2)
-    (sum_w_down, sum_w_up), (late,) = tied(
-        (sum_w_down.astype(F32), sum_w_up.astype(F32)), [late]
+    (sum_w_down, sum_w_up, sum_w_out), (late,) = tied(
+        (sum_w_down.astype(F32), sum_w_up.astype(F32), sum_w_out.astype(F32)), [late]
     )
     early, late = advance(early, last - early[3]), advance(late, last - late[3])
     grad_input = grad_input + lax.dot_general(
@@ -1022,7 +1021,6 @@
     late, late_other = last_swap(late)[:2]
     sum_w_qkv = settle_qkv(late, late_other, early, early_other, width)
     first_core = me % 2 == 0
-    sum_w_out = jnp.where(first_core, early, early_other).astype(F32)
     flat = jnp.where(first_core, late[width:], late_other[width:])[:16].astype(F32)
     at = sums.shape[0] + hidden // width
     pieces = [

time: 483 us -> 497 us (1.029)
  starting transfers between devices: 38 us -> 62.1 us
  waiting for transfers between devices: 146 us -> 162 us
  Pallas kernels: 123 us -> 108 us
  local copies, waits for them, and re-layouts: 47.2 us -> 40.2 us
    ppermute x44, starting transfers between devices: 32.2 us -> 56.3 us  [swap(): return lax.ppermute(array, axis, [(i, i ^ bit) for i in range(count)])]
    psum x1, waiting for transfers between devices: 0.02 us -> 10.4 us  [per_device(): lax.psum((grad_w_down, grad_w_up, grad_w_out), ('row', 'seq'))]
    ppermute x44, waiting for transfers between devices: 146 us -> 152 us  [swap(): return lax.ppermute(array, axis, [(i, i ^ bit) for i in range(count)])]
  transfers between devices with their start and end apart: 49 -> 49, of which waited for: 32 -> 27; matrix products, arithmetic and copies ran while one was open for 25% -> 16% of each run, Pallas kernels for 10% -> 6%
where the time goes in v11:
time: 497 us; the launch traced here: 488 us
  waiting for transfers between devices  162 us (33%)
  Pallas kernels  108 us (22%)
  starting transfers between devices  62.1 us (12%)
  matrix products  50.3 us (10%)
  other arithmetic  48.4 us (10%)
  local copies, waits for them, and re-layouts  40.2 us (8%)
  between operations  15.5 us (3%)
    ppermute x44, waiting for transfers between devices, swap(): return lax.ppermute(array, axis, [(i, i ^ bit) for i in range(count)])  152 us
    ppermute x44, starting transfers between devices, swap(): return lax.ppermute(array, axis, [(i, i ^ bit) for i in range(count)])  56.3 us
    pallas_call x1, Pallas kernels, per_device(): pl.pallas_call(ffn_kernel, grid=(tok_count // FFN_BLOCK,), in_specs=[ffn_...  40.6 us
    select_n x16, other arithmetic, paired(): jnp.where(side == 0, jnp.concatenate([array, other], dim), jnp.concatenat...  11.1 us
    psum x1, waiting for transfers between devices, per_device(): lax.psum((grad_w_down, grad_w_up, grad_w_out), ('row', 'seq'))  10.4 us
    pallas_call x1, Pallas kernels, remaining(): pl.pallas_call(lambda *refs: pinv_back_kernel(scale, *refs), out_shape=(s...  10 us
  transfers between devices with their start and end apart: 49, of which 27 were waited for; matrix products, arithmetic and copies ran while one was open for 16% of the time, Pallas kernels for 6%

profile of v11, /device:TPU:0, one launch (start us, length us, event | category | flops | bytes accessed | tf_op | source)
XLA Modules:
  0.0 487.9 jit_solution(12684453654757237729)
XLA Ops:
  10.9 2.2 fusion.29
  14.8 3.0 collective-permute-start.31
  17.8 3.1 collective-permute-done.31
  20.9 1.9 collective-permute-start.32
  22.7 6.0 %add_convert_fusion.20.refs_2_.refs_3_.refs_1_ = bf16[1024,2304]{1,0:T(8,128)(2,1)S(1)} fusion(bf16[768,2304]{1,0:T(8,128)(2,1)} %param.21, f32[2304]{0:T(1024)S(1)} %pad_maximum_fusion.2, bf16[1,1024,768]{2,1,0:T(8,128)(2,1)S(1)} %copy-done.23), kind=kOutput, calls=%fused_computation.73 | convolution fusion | flops 3628597248 | bytes 9839616 | tf_op jit(solution)/shard_map/dot_general | solution.py:736
  28.8 2.7 collective-permute-start.33
  35.6 3.2 collective-permute-start.34
  38.9 3.3 collective-permute-done.34
  44.0 2.6 fusion.27
  46.8 4.7 landmark.1
  54.4 2.0 join.4
  59.9 6.0 %pinv.1 = (f32[3,64,64]{2,1,0:T(8,128)}, f32[3,64,64]{2,1,0:T(8,128)}, f32[72,64,64]{2,1,0:T(8,128)}) custom-call(f32[3,64,64]{2,1,0:T(8,128)S(1)} %bitcast.67, f32[3,64,64]{2,1,0:T(8,128)S(1)} %bitcast.69), custom_call_target="tpu_custom_call" | custom-call | tf_op jit(solution)/shard_map/pinv/pallas_call | solution.py:776
  67.7 1.9 join.5.a_ref
  71.9 4.5 collective-permute-done.38
  77.1 2.0 join.6.a_ref
  80.1 4.3 collective-permute-start.39
  84.4 7.4 %collective-permute-done.39 = bf16[64,1280]{1,0:T(8,128)(2,1)S(1)} collective-permute-done((bf16[64,1280]{1,0:T(8,128)(2,1)S(1)}, bf16[64,1280]{1,0:T(8,128)(2,1)S(1)}, u32[]{:S(2)}, u32[]{:S(2)}) %collective-permute-start.39) | collective-permute-done | bytes 163872 | tf_op jit(solution)/shard_map/ppermute | solution.py:27
  95.1 4.5 collective-permute-done.40
  103.5 8.3 %token_.1 = (bf16[1024,768]{1,0:T(8,128)(2,1)S(1)}, bf16[768,1024]{1,0:T(8,128)(2,1)S(1)}) custom-call(s32[8]{0:T(128)S(1)} %copy-done.45, bf16[1024,2304]{1,0:T(8,128)(2,1)} %copy-done.8, bf16[1152,768]{1,0:T(8,128)(2,1)S(1)} %copy-done.9, bf16[256,768]{1,0:T(8,128)(2,1)S(1)} %slice.187.refs_3_.refs_4_, ...), custom_call_target="tpu_custom_call" | custom-call | tf_op jit(solution)/shard_map/token/pallas_call | solution.py:804
  113.7 40.6 %ffn.1 = (f32[1024,768]{1,0:T(8,128)}, f32[1024,768]{1,0:T(8,128)}, bf16[1024,3072]{1,0:T(8,128)(2,1)}, bf16[1024,3072]{1,0:T(8,128)(2,1)}, bf16[1024,768]{1,0:T...) custom-call(bf16[1024,768]{1,0:T(8,128)(2,1)} %bitcast.65, ...), custom_call_target="tpu_custom_call" | custom-call | tf_op jit(solution)/shard_map/ffn/pallas_call | solution.py:826
  154.3 4.0 convolution_convert_fusion.3
  158.3 7.6 %token_back.1 = (bf16[1024,768]{1,0:T(8,128)(2,1)}, f32[256,768]{1,0:T(8,128)S(1)}, f32[256,768]{1,0:T(8,128)}) custom-call(s32[8]{0:T(128)S(1)} %copy-done.45, bf16[1024,2304]{1,0:T(8,128)(2,1)} %copy-done.8, bf16[1024,768]{1,0:T(8,128)(2,1)S(1)} %copy-done.12, bf16[768,1024]{1,0:T(8,128)(2,1)S(1)} %get-tuple-element.178.refs_3_, ...), custom_call_target="tpu_custom_call" | custom-call | tf_op jit(solution)/shard_map/token_back/pallas_call | solution.py:850
  166.0 6.8 %convolution_convert_fusion.1 = bf16[768,3072]{1,0:T(8,128)(2,1)} fusion(bf16[1024,768]{1,0:T(8,128)(2,1)S(1)} %copy-done.71, bf16[1024,3072]{1,0:T(8,128)(2,1)S(1)} %bitcast.89), kind=kOutput, calls=%fused_computation.74 | convolution fusion | flops 4834197504 | bytes 12582912 | tf_op jit(solution)/shard_map/dot_general | solution.py:867
  172.8 6.9 %convolution_convert_fusion.2 = bf16[3072,768]{1,0:T(8,128)(2,1)} fusion(bf16[1024,3072]{1,0:T(8,128)(2,1)S(1)} %bitcast.87, bf16[1024,768]{1,0:T(8,128)(2,1)S(1)} %copy-done.70), kind=kOutput, calls=%fused_computation.75 | convolution fusion | flops 4834197504 | bytes 12582912 | tf_op jit(solution)/shard_map/dot_general | solution.py:866
  181.1 209.0 %conditional.1 = (bf16[192,768]{1,0:T(8,128)(2,1)}, bf16[112,768]{1,0:T(8,128)(2,1)}, bf16[256,768]{1,0:T(8,128)(2,1)}, f32[1024,768]{1,0:T(8,128)}) conditional(s32[]{:T(128)} %bitcast.23, () %tuple.32, (bf16[256,768]{1,0:T(8,128)(2,1)S(1)}, bf16[1024,768]{1,0:T(8,128)(2,1)S(1)}, f32[12,33]{1,0:T(8,128)S(1)}, s32[8]{0:T(128)S(1)}, ...), branch_computations={%region_1.2_spmd, %region_2.6_spmd} | conditional | flops 8504062976 | bytes 207604768 | solution.py:1006
  183.3 1.8 collective-permute-start.4
  187.7 3.4 collective-permute-start.2
  191.1 4.9 fusion.48
  197.1 9.5 %collective-permute-start.3 = (bf16[64,768]{1,0:T(8,128)(2,1)S(1)}, bf16[64,768]{1,0:T(8,128)(2,1)S(1)}, u32[]{:S(2)}, u32[]{:S(2)}) collective-permute-start(bf16[64,768]{1,0:T(8,128)(2,1)S(1)} %add_convert_fusion.16), channel_id=1, source_target_pairs={{0,8},{1,9},{2,10},{3,11},{4,12},{5,13},{6,14},{7,15},{8,0},{9,1},... | collective-permute-start | bytes 294920 | tf_op jit(solution)/shard_map/cond/branch_1_fun/ppermute | solution.py:27
  206.9 5.9 %conv_back.1 = (f32[1024,768]{1,0:T(8,128)S(1)}, f32[16,256]{1,0:T(8,128)S(1)}) custom-call(s32[8]{0:T(128)S(1)} %copy-done.47, bf16[1152,768]{1,0:T(8,128)(2,1)S(1)} %maximum_maximum_fusion.refs_1_, bf16[1152,768]{1,0:T(8,128)(2,1)S(1)} %copy-done.10, f32[12,256]{1,0:T(8,128)S(1)} %pad.15.refs_3_), custom_call_target="tpu_custom_call" | custom-call | tf_op jit(solution)/shard_map/cond/branch_1_fun/conv_back/pallas_call | solution.py:880
  213.5 2.1 mix_back.1
  217.7 2.9 collective-permute-done.6
  220.6 1.7 maximum_select_fusion.3
  228.5 2.3 convert_reduce_fusion
  232.9 7.6 %landmark_back.1 = (bf16[1024,768]{1,0:T(8,128)(2,1)S(1)}, bf16[1024,768]{1,0:T(8,128)(2,1)S(1)}, f32[256,768]{1,0:T(8,128)S(1)}) custom-call(s32[8]{0:T(128)S(1)} %copy-done.48, bf16[1024,2304]{1,0:T(8,128)(2,1)} %get-tuple-element.51.refs_1_.refs_2_, bf16[1024,2304]{1,0:T(8,128)(2,1)} %get-tuple-element.51.refs_1_.refs_2_, ...), custom_call_target="tpu_custom_call" | custom-call | tf_op jit(solution)/shard_map/cond/branch_1_fun/landmark_back/pallas_call | solution.py:904
  245.3 2.2 reduce
  250.8 10.0 %pinv_back.1 = (f32[3,64,64]{2,1,0:T(8,128)}, f32[3,64,64]{2,1,0:T(8,128)}) custom-call(f32[3,64,64]{2,1,0:T(8,128)S(1)} %copy-done.32, f32[3,64,64]{2,1,0:T(8,128)S(1)} %copy-done.34, f32[3,64,64]{2,1,0:T(8,128)S(1)} %copy-done.39, f32[72,64,64]{2,1,0:T(8,128)} %get-tuple-element.70.refs_3_, bf16[3,64,64]{2,1,0:T(8,128)(2,1)} %bitcast.79, ...), custom_call_target="tpu_custom_call" | custom-call | tf_op jit(solution)/shard_map/cond/branch_1_fun/pinv_back/pallas_call | solution.py:927
  262.9 3.1 dynamic_update_slice.15
  270.2 2.7 copy.70
  273.0 9.2 %fusion.9 = f32[1024,768]{1,0:T(8,128)} fusion(f32[1024,768]{1,0:T(8,128)} %get-tuple-element.81, bf16[768,2304]{1,0:T(8,128)(2,1)} %get-tuple-element.79, bf16[1024,768]{1,0:T(8,128)(2,1)S(1)} %copy-done.3, bf16[1024,768]{1,0:T(8,128)(2,1)S(1)} %copy-done.7, bf16[1024,768]{1,0:T(8,128)(2,1)} %get-tuple-element.82), kind=kOutput, calls=%fused_computation.14 | convolution fusion | flops 3638820864 | bytes 14548992 | tf_op jit(solution)/shard_map/cond/branch_1_fun/dot_general | solution.py:983
  289.2 5.6 %collective-permute-start.10 = (bf16[192,768]{0,1:T(8,128)(2,1)S(1)}, bf16[192,768]{0,1:T(8,128)(2,1)S(1)}, u32[]{:S(2)}, u32[]{:S(2)}) collective-permute-start(bf16[192,768]{0,1:T(8,128)(2,1)S(1)} %constant_dynamic-slice_fusion.9), channel_id=1, source_target_pairs={{0,16},{16,0},{1,17},{17,1},{2,18},{18,2},{3,19},{19,3},{4,20},{20... | collective-permute-start | bytes 884744 | tf_op jit(solution)/shard_map/cond/branch_1_fun/ppermute | solution.py:27
  295.7 8.4 %collective-permute-done.10 = bf16[192,768]{0,1:T(8,128)(2,1)S(1)} collective-permute-done((bf16[192,768]{0,1:T(8,128)(2,1)S(1)}, bf16[192,768]{0,1:T(8,128)(2,1)S(1)}, u32[]{:S(2)}, u32[]{:S(2)}) %collective-permute-start.10) | collective-permute-done | bytes 294944 | tf_op jit(solution)/shard_map/cond/branch_1_fun/ppermute | solution.py:27
  304.6 8.3 %collective-permute-done.11 = bf16[96,768]{0,1:T(8,128)(2,1)S(1)} collective-permute-done((bf16[96,768]{0,1:T(8,128)(2,1)S(1)}, bf16[96,768]{0,1:T(8,128)(2,1)S(1)}, u32[]{:S(2)}, u32[]{:S(2)}) %collective-permute-start.11) | collective-permute-done | bytes 147488 | tf_op jit(solution)/shard_map/cond/branch_1_fun/ppermute | solution.py:27
  316.0 5.3 %collective-permute-done.14 = bf16[48,768]{0,1:T(8,128)(2,1)S(1)} collective-permute-done((bf16[48,768]{0,1:T(8,128)(2,1)S(1)}, bf16[48,768]{0,1:T(8,128)(2,1)S(1)}, u32[]{:S(2)}, u32[]{:S(2)}) %collective-permute-start.14) | collective-permute-done | bytes 73760 | tf_op jit(solution)/shard_map/cond/branch_1_fun/ppermute | solution.py:27
  321.4 13.6 %collective-permute-done.15 = bf16[448,768]{1,0:T(8,128)(2,1)S(1)} collective-permute-done((bf16[448,768]{1,0:T(8,128)(2,1)S(1)}, bf16[448,768]{1,0:T(8,128)(2,1)S(1)}, u32[]{:S(2)}, u32[]{:S(2)}) %collective-permute-start.15) | collective-permute-done | bytes 688160 | tf_op jit(solution)/shard_map/cond/branch_1_fun/ppermute | solution.py:27
  335.5 4.0 collective-permute-start.16
  339.5 9.9 %collective-permute-done.17 = bf16[24,768]{0,1:T(8,128)(2,1)S(1)} collective-permute-done((bf16[24,768]{0,1:T(8,128)(2,1)S(1)}, bf16[24,768]{0,1:T(8,128)(2,1)S(1)}, u32[]{:S(2)}, u32[]{:S(2)}) %collective-permute-start.17) | collective-permute-done | bytes 36896 | tf_op jit(solution)/shard_map/cond/branch_1_fun/ppermute | solution.py:27
  349.9 2.0 collective-permute-start.21
  352.9 11.5 %collective-permute-done.20 = bf16[24,768]{0,1:T(8,128)(2,1)S(1)} collective-permute-done((bf16[24,768]{0,1:T(8,128)(2,1)S(1)}, bf16[24,768]{0,1:T(8,128)(2,1)S(1)}, u32[]{:S(2)}, u32[]{:S(2)}) %collective-permute-start.20) | collective-permute-done | bytes 36896 | tf_op jit(solution)/shard_map/cond/branch_1_fun/ppermute | solution.py:27
  364.6 4.7 collective-permute-done.19
  369.5 2.7 collective-permute-start.24
  372.2 4.7 collective-permute-done.23
  376.9 2.1 collective-permute-done.24
  379.8 7.7 %collective-permute-done.27 = bf16[56,768]{1,0:T(8,128)(2,1)S(1)} collective-permute-done((bf16[56,768]{1,0:T(8,128)(2,1)S(1)}, bf16[56,768]{1,0:T(8,128)(2,1)S(1)}, u32[]{:S(2)}, u32[]{:S(2)}) %collective-permute-start.27) | collective-permute-done | bytes 86048 | tf_op jit(solution)/shard_map/cond/branch_1_fun/ppermute | solution.py:27
  390.2 9.9 %collective-permute-done.43 = bf16[112,768]{1,0:T(8,128)(2,1)S(1)} collective-permute-done((bf16[112,768]{1,0:T(8,128)(2,1)}, bf16[112,768]{1,0:T(8,128)(2,1)S(1)}, u32[]{:S(2)}, u32[]{:S(2)}) %collective-permute-start.43) | collective-permute-done | bytes 172064 | tf_op jit(solution)/shard_map/ppermute | solution.py:27
  401.4 15.7 %collective-permute-done.44 = bf16[224,768]{1,0:T(8,128)(2,1)S(1)} collective-permute-done((bf16[224,768]{1,0:T(8,128)(2,1)S(1)}, bf16[224,768]{1,0:T(8,128)(2,1)S(1)}, u32[]{:S(2)}, u32[]{:S(2)}) %collective-permute-start.44) | collective-permute-done | bytes 344096 | tf_op jit(solution)/shard_map/ppermute | solution.py:27
  417.3 10.4 %all-reduce.8.cloned.1.call-done = (bf16[3072,768]{1,0:T(8,128)(2,1)}, bf16[768,3072]{1,0:T(8,128)(2,1)}, bf16[768,768]{1,0:T(8,128)(2,1)}) async-done(((bf16[3072,768]{1,0:T(8,128)(2,1)}, bf16[768,3072]{1,0:T(8,128)(2,1)}, bf16[768,768]{1,0:T(8,128)(2,1)}), (bf16[3072,768]{1,0:T(8,128)(2,1)}, bf16[768,3072]{1,0:T(8,128)(2,1)}, bf16[768,768]{1,0:T(8,128)(2,1)})) %all-reduce.8.cloned.1.call-update) | async-done | bytes 10616848 | tf_op jit(solution)/shard_map/psum | solution.py:872
  427.7 7.0 %convert_element_type.347 = f32[3072,768]{1,0:T(8,128)} convert(bf16[3072,768]{1,0:T(8,128)(2,1)} %get-tuple-element.216) | non-fusion elementwise | flops 2359296 | bytes 14155776 | tf_op jit(solution)/shard_map/convert_element_type | solution.py:1013
  434.7 5.0 %convert_element_type.348 = f32[768,3072]{1,0:T(8,128)} convert(bf16[768,3072]{1,0:T(8,128)(2,1)S(1)} %copy-done.15) | non-fusion elementwise | flops 2359296 | bytes 14155776 | tf_op jit(solution)/shard_map/convert_element_type | solution.py:1013
  443.3 1.9 fusion.30
  445.2 4.0 add.375
  449.2 14.8 %collective-permute-done.42 = bf16[192,768]{1,0:T(8,128)(2,1)S(1)} collective-permute-done((bf16[192,768]{1,0:T(8,128)(2,1)}, bf16[192,768]{1,0:T(8,128)(2,1)S(1)}, u32[]{:S(2)}, u32[]{:S(2)}) %collective-permute-start.42) | collective-permute-done | bytes 294944 | tf_op jit(solution)/shard_map/ppermute | solution.py:27
  466.5 2.6 collective-permute-done.46.late_other_ref
  473.0 7.6 %settle_qkv.1 = f32[768,2304]{1,0:T(8,128)} custom-call(s32[1]{0:T(128)} %bitcast.25.side_ref, bf16[896,768]{1,0:T(8,128)(2,1)} %copy-done.14, bf16[896,768]{1,0:T(8,128)(2,1)} %copy-done.22, bf16[384,768]{1,0:T(8,128)(2,1)} %copy-done.19, bf16[384,768]{1,0:T(8,128)(2,1)} %copy-done.36), custom_call_target="tpu_custom_call" | custom-call | tf_op jit(solution)/shard_map/settle_qkv/pallas_call | solution.py:673
  (380 shorter events, 93.8 us)
Async XLA Ops:
  7.2 420.5 %all-reduce.8.cloned.1.call-start = ((), (), s32[]{:S(2)}) async-start(), calls=%async_computation | async-start | bytes 21233664 | tf_op jit(solution)/shard_map/psum | solution.py:872
  13.1 1.6 collective-permute-start.30
  14.8 6.0 %collective-permute-start.31 = (bf16[64,768]{1,0:T(8,128)(2,1)S(1)}, bf16[64,768]{1,0:T(8,128)(2,1)S(1)}, u32[]{:S(2)}, u32[]{:S(2)}) collective-permute-start(bf16[64,768]{1,0:T(8,128)(2,1)S(1)} %constant_dynamic-slice_fusion.20), channel_id=1, source_target_pairs={{0,2},{1,3},{2,0},{3,1},{4,6},{5,7},{6,4},{7,5},{8,10},{9,11},{10,... | collective-permute-start | bytes 294920 | tf_op jit(solution)/shard_map/ppermute | solution.py:27
  20.9 7.9 %collective-permute-start.32 = (bf16[64,768]{1,0:T(8,128)(2,1)S(1)}, bf16[64,768]{1,0:T(8,128)(2,1)S(1)}, u32[]{:S(2)}, u32[]{:S(2)}) collective-permute-start(bf16[64,768]{1,0:T(8,128)(2,1)S(1)} %add_convert_fusion.24), channel_id=1, source_target_pairs={{0,4},{1,5},{2,6},{3,7},{4,0},{5,1},{6,2},{7,3},{8,12},{9,13},{10,... | collective-permute-start | bytes 294920 | tf_op jit(solution)/shard_map/ppermute | solution.py:27
  28.8 6.8 %collective-permute-start.33 = (bf16[64,768]{1,0:T(8,128)(2,1)S(1)}, bf16[64,768]{1,0:T(8,128)(2,1)S(1)}, u32[]{:S(2)}, u32[]{:S(2)}) collective-permute-start(bf16[64,768]{1,0:T(8,128)(2,1)S(1)} %add_convert_fusion.23), channel_id=1, source_target_pairs={{0,8},{1,9},{2,10},{3,11},{4,12},{5,13},{6,14},{7,15},{8,0},{9,1},... | collective-permute-start | bytes 294920 | tf_op jit(solution)/shard_map/ppermute | solution.py:27
  31.5 10.8 %collective-permute-start.28 = (bf16[16,768]{1,0:T(8,128)(2,1)S(1)}, bf16[16,768]{1,0:T(8,128)(2,1)S(1)}, u32[]{:S(2)}, u32[]{:S(2)}) collective-permute-start(bf16[16,768]{1,0:T(8,128)(2,1)S(1)} %get-tuple-element.223), channel_id=1, source_target_pairs={{0,1},{1,2},{2,3},{3,4},{4,5},{5,6},{6,7},{7,8},{8,9},{9,10},{10,1... | collective-permute-start | bytes 73736 | tf_op jit(solution)/shard_map/ppermute | solution.py:141
  32.8 9.5 %collective-permute-start.29 = (bf16[16,768]{1,0:T(8,128)(2,1)S(1)}, bf16[16,768]{1,0:T(8,128)(2,1)S(1)}, u32[]{:S(2)}, u32[]{:S(2)}) collective-permute-start(bf16[16,768]{1,0:T(8,128)(2,1)S(1)} %get-tuple-element.224), channel_id=1, source_target_pairs={{1,0},{2,1},{3,2},{4,3},{5,4},{6,5},{7,6},{8,7},{9,8},{10,9},{11,1... | collective-permute-start | bytes 73736 | tf_op jit(solution)/shard_map/ppermute | solution.py:143
  35.6 6.5 %collective-permute-start.34 = (bf16[64,768]{1,0:T(8,128)(2,1)S(1)}, bf16[64,768]{1,0:T(8,128)(2,1)S(1)}, u32[]{:S(2)}, u32[]{:S(2)}) collective-permute-start(bf16[64,768]{1,0:T(8,128)(2,1)S(1)} %add_convert_fusion.22), channel_id=1, source_target_pairs={{0,2},{1,3},{2,0},{3,1},{4,6},{5,7},{6,4},{7,5},{8,10},{9,11},{10,... | collective-permute-start | bytes 294920 | tf_op jit(solution)/shard_map/ppermute | solution.py:27
  42.2 1.7 collective-permute-start.35
  52.2 1.6 collective-permute-start.36
  58.1 9.0 %collective-permute-start.37 = (bf16[64,896]{1,0:T(8,128)(2,1)S(1)}, bf16[64,896]{1,0:T(8,128)(2,1)S(1)}, u32[]{:S(2)}, u32[]{:S(2)}) collective-permute-start(bf16[64,896]{1,0:T(8,128)(2,1)S(1)} %get-tuple-element.227), channel_id=1, source_target_pairs={{0,2},{1,3},{2,0},{3,1},{4,6},{5,7},{6,4},{7,5},{8,10},{9,11},{10,... | collective-permute-start | bytes 344072 | tf_op jit(solution)/shard_map/ppermute | solution.py:27
  59.7 16.7 %copy-start.31 = (f32[64,3,64]{2,0,1:T(8,128)}, f32[64,3,64]{2,0,1:T(8,128)S(1)}, u32[]{:S(2)}) copy-start(f32[64,3,64]{2,0,1:T(8,128)S(1)} %copy.76) | copy-start | bytes 147460
  59.9 16.5 %copy-start.33 = (f32[64,3,64]{2,0,1:T(8,128)}, f32[64,3,64]{2,0,1:T(8,128)S(1)}, u32[]{:S(2)}) copy-start(f32[64,3,64]{2,0,1:T(8,128)S(1)} %copy.78) | copy-start | bytes 147460
  66.9 33.8 %copy-start.42 = (f32[12,33]{1,0:T(8,128)S(1)}, f32[12,33]{1,0:T(8,128)}, u32[]{:S(2)}) copy-start(f32[12,33]{1,0:T(8,128)} %param.24) | copy-start | bytes 4756
  66.9 33.8 %copy-start.60 = (f32[768]{0:T(1024)S(1)}, f32[768]{0:T(1024)}, u32[]{:S(2)}) copy-start(f32[768]{0:T(1024)} %param.26) | copy-start | bytes 9220
  66.9 33.8 %copy-start.61 = (f32[768]{0:T(1024)S(1)}, f32[768]{0:T(1024)}, u32[]{:S(2)}) copy-start(f32[768]{0:T(1024)} %param.27) | copy-start | bytes 9220
  66.9 33.9 %copy-start.62 = (f32[768]{0:T(1024)S(1)}, f32[768]{0:T(1024)}, u32[]{:S(2)}) copy-start(f32[768]{0:T(1024)} %param.28) | copy-start | bytes 9220
  66.9 33.9 %copy-start.63 = (f32[768]{0:T(1024)S(1)}, f32[768]{0:T(1024)}, u32[]{:S(2)}) copy-start(f32[768]{0:T(1024)} %param.32) | copy-start | bytes 9220
  67.0 33.9 %copy-start.64 = (f32[768]{0:T(1024)S(1)}, f32[768]{0:T(1024)}, u32[]{:S(2)}) copy-start(f32[768]{0:T(1024)} %param.33) | copy-start | bytes 9220
  67.0 33.9 %copy-start.65 = (f32[768]{0:T(1024)S(1)}, f32[768]{0:T(1024)}, u32[]{:S(2)}) copy-start(f32[768]{0:T(1024)} %param.34) | copy-start | bytes 9220
  70.5 5.9 %collective-permute-start.38 = (bf16[64,1088]{1,0:T(8,128)(2,1)S(1)}, bf16[64,1088]{1,0:T(8,128)(2,1)S(1)}, u32[]{:S(2)}, u32[]{:S(2)}) collective-permute-start(bf16[64,1088]{1,0:T(8,128)(2,1)S(1)} %pad_maximum_fusion.1), channel_id=1, source_target_pairs={{0,4},{1,5},{2,6},{3,7},{4,0},{5,1},{6,2},{7,3},{8,12},{9,13},{10,... | collective-permute-start | bytes 417800 | tf_op jit(solution)/shard_map/ppermute | solution.py:27
  77.1 26.4 %copy-start.9 = (bf16[1152,768]{1,0:T(8,128)(2,1)S(1)}, bf16[1152,768]{1,0:T(8,128)(2,1)}, u32[]{:S(2)}) copy-start(bf16[1152,768]{1,0:T(8,128)(2,1)} %maximum_maximum_fusion.1.refs_2_) | copy-start | bytes 5308420
  77.1 26.4 %copy-start.45 = (s32[8]{0:T(128)S(1)}, s32[8]{0:T(128)}, u32[]{:S(2)}) copy-start(s32[8]{0:T(128)} %copy-done.44) | copy-start | bytes 100
  80.1 11.7 %collective-permute-start.39 = (bf16[64,1280]{1,0:T(8,128)(2,1)S(1)}, bf16[64,1280]{1,0:T(8,128)(2,1)S(1)}, u32[]{:S(2)}, u32[]{:S(2)}) collective-permute-start(bf16[64,1280]{1,0:T(8,128)(2,1)S(1)} %pad_maximum_fusion), channel_id=1, source_target_pairs={{0,8},{1,9},{2,10},{3,11},{4,12},{5,13},{6,14},{7,15},{8,0},{9,1},... | collective-permute-start | bytes 491528 | tf_op jit(solution)/shard_map/ppermute | solution.py:27
  94.6 5.0 %collective-permute-start.40 = (bf16[64,896]{1,0:T(8,128)(2,1)}, bf16[64,896]{1,0:T(8,128)(2,1)S(1)}, u32[]{:S(2)}, u32[]{:S(2)}) collective-permute-start(bf16[64,896]{1,0:T(8,128)(2,1)} %mix.1), channel_id=1, source_target_pairs={{0,2},{1,3},{2,0},{3,1},{4,6},{5,7},{6,4},{7,5},{8,10},{9,11},{10,... | collective-permute-start | bytes 344072 | tf_op jit(solution)/shard_map/ppermute | solution.py:27
  100.6 1.7 collective-permute-start.41
  113.7 40.6 %copy-start.1 = (bf16[1024,768]{1,0:T(8,128)(2,1)S(1)}, bf16[1024,768]{1,0:T(8,128)(2,1)}, u32[]{:S(2)}) copy-start(bf16[1024,768]{1,0:T(8,128)(2,1)} %copy-done) | copy-start | bytes 4718596
  181.2 1.5 collective-permute-start
  182.7 4.9 %collective-permute-start.1 = (bf16[64,768]{1,0:T(8,128)(2,1)S(1)}, bf16[64,768]{1,0:T(8,128)(2,1)S(1)}, u32[]{:S(2)}, u32[]{:S(2)}) collective-permute-start(bf16[64,768]{1,0:T(8,128)(2,1)S(1)} %constant_dynamic-slice_fusion.14), channel_id=1, source_target_pairs={{0,2},{1,3},{2,0},{3,1},{4,6},{5,7},{6,4},{7,5},{8,10},{9,11},{10,... | collective-permute-start | bytes 294920 | tf_op jit(solution)/shard_map/cond/branch_1_fun/ppermute | solution.py:27
  183.3 23.2 %collective-permute-start.4 = (bf16[16,768]{1,0:T(8,128)(2,1)S(1)}, bf16[16,768]{1,0:T(8,128)(2,1)S(1)}, u32[]{:S(2)}, u32[]{:S(2)}) collective-permute-start(bf16[16,768]{1,0:T(8,128)(2,1)S(1)} %get-tuple-element.219), channel_id=1, source_target_pairs={{0,1},{1,2},{2,3},{3,4},{4,5},{5,6},{6,7},{7,8},{8,9},{9,10},{10,1... | collective-permute-start | bytes 73736 | tf_op jit(solution)/shard_map/cond/branch_1_fun/ppermute | solution.py:141
  185.1 21.4 %collective-permute-start.5 = (bf16[16,768]{1,0:T(8,128)(2,1)S(1)}, bf16[16,768]{1,0:T(8,128)(2,1)S(1)}, u32[]{:S(2)}, u32[]{:S(2)}) collective-permute-start(bf16[16,768]{1,0:T(8,128)(2,1)S(1)} %get-tuple-element.220), channel_id=1, source_target_pairs={{1,0},{2,1},{3,2},{4,3},{5,4},{6,5},{7,6},{8,7},{9,8},{10,9},{11,1... | collective-permute-start | bytes 73736 | tf_op jit(solution)/shard_map/cond/branch_1_fun/ppermute | solution.py:143
  187.7 9.3 %collective-permute-start.2 = (bf16[64,768]{1,0:T(8,128)(2,1)S(1)}, bf16[64,768]{1,0:T(8,128)(2,1)S(1)}, u32[]{:S(2)}, u32[]{:S(2)}) collective-permute-start(bf16[64,768]{1,0:T(8,128)(2,1)S(1)} %add_convert_fusion.17), channel_id=1, source_target_pairs={{0,4},{1,5},{2,6},{3,7},{4,0},{5,1},{6,2},{7,3},{8,12},{9,13},{10,... | collective-permute-start | bytes 294920 | tf_op jit(solution)/shard_map/cond/branch_1_fun/ppermute | solution.py:27
  197.1 15.8 %collective-permute-start.3 = (bf16[64,768]{1,0:T(8,128)(2,1)S(1)}, bf16[64,768]{1,0:T(8,128)(2,1)S(1)}, u32[]{:S(2)}, u32[]{:S(2)}) collective-permute-start(bf16[64,768]{1,0:T(8,128)(2,1)S(1)} %add_convert_fusion.16), channel_id=1, source_target_pairs={{0,8},{1,9},{2,10},{3,11},{4,12},{5,13},{6,14},{7,15},{8,0},{9,1},... | collective-permute-start | bytes 294920 | tf_op jit(solution)/shard_map/cond/branch_1_fun/ppermute | solution.py:27
  215.6 5.0 %collective-permute-start.6 = (bf16[64,896]{1,0:T(8,128)(2,1)}, bf16[64,896]{1,0:T(8,128)(2,1)S(1)}, u32[]{:S(2)}, u32[]{:S(2)}) collective-permute-start(bf16[64,896]{1,0:T(8,128)(2,1)} %mix_back.1), channel_id=1, source_target_pairs={{0,2},{1,3},{2,0},{3,1},{4,6},{5,7},{6,4},{7,5},{8,10},{9,11},{10,... | collective-permute-start | bytes 344072 | tf_op jit(solution)/shard_map/cond/branch_1_fun/ppermute | solution.py:27
  216.7 16.2 %copy-start.48 = (s32[8]{0:T(128)S(1)}, s32[8]{0:T(128)}, u32[]{:S(2)}) copy-start(s32[8]{0:T(128)} %copy-done.46) | copy-start | bytes 100 | tf_op jit(solution)/shard_map/cond
  222.3 9.2 %collective-permute-start.7 = (bf16[128,896]{1,0:T(8,128)(2,1)}, bf16[128,896]{1,0:T(8,128)(2,1)}, u32[]{:S(2)}, u32[]{:S(2)}) collective-permute-start(bf16[128,896]{1,0:T(8,128)(2,1)} %maximum_select_fusion.3), channel_id=1, source_target_pairs={{0,1},{1,0},{2,3},{3,2},{4,5},{5,4},{6,7},{7,6},{8,9},{9,8},{10,11... | collective-permute-start | bytes 688136 | tf_op jit(solution)/shard_map/cond/branch_1_fun/ppermute | solution.py:27
  248.4 33.8 %collective-permute-start.8 = (bf16[384,768]{0,1:T(8,128)(2,1)}, bf16[384,768]{0,1:T(8,128)(2,1)}, u32[]{:S(2)}, u32[]{:S(2)}) collective-permute-start(bf16[384,768]{0,1:T(8,128)(2,1)} %constant_dynamic-slice_fusion.11), channel_id=1, source_target_pairs={{0,1},{1,0},{2,3},{3,2},{4,5},{5,4},{6,7},{7,6},{8,9},{9,8},{10,11... | collective-permute-start | bytes 1769480 | tf_op jit(solution)/shard_map/cond/branch_1_fun/ppermute | solution.py:27
  250.7 16.4 %copy-start.7 = (bf16[1024,768]{1,0:T(8,128)(2,1)S(1)}, bf16[1024,768]{1,0:T(8,128)(2,1)}, u32[]{:S(2)}) copy-start(bf16[1024,768]{1,0:T(8,128)(2,1)} %copy-done.6) | copy-start | bytes 4718596 | tf_op jit(solution)/shard_map/cond
  250.7 16.4 %copy-start.25 = (bf16[1024,768]{1,0:T(8,128)(2,1)S(1)}, bf16[1024,768]{1,0:T(8,128)(2,1)}, u32[]{:S(2)}) copy-start(bf16[1024,768]{1,0:T(8,128)(2,1)} %get-tuple-element.72) | copy-start | bytes 4718596 | tf_op jit(solution)/shard_map/cond
  288.9 24.1 %collective-permute-start.12 = (bf16[896,768]{1,0:T(8,128)(2,1)S(1)}, bf16[896,768]{1,0:T(8,128)(2,1)S(1)}, u32[]{:S(2)}, u32[]{:S(2)}) collective-permute-start(bf16[896,768]{1,0:T(8,128)(2,1)S(1)} %constant_dynamic-slice_fusion.7), channel_id=1, source_target_pairs={{0,1},{1,0},{2,3},{3,2},{4,5},{5,4},{6,7},{7,6},{8,9},{9,8},{10,11... | collective-permute-start | bytes 4128776 | tf_op jit(solution)/shard_map/cond/branch_1_fun/ppermute | solution.py:27
  289.2 14.9 %collective-permute-start.10 = (bf16[192,768]{0,1:T(8,128)(2,1)S(1)}, bf16[192,768]{0,1:T(8,128)(2,1)S(1)}, u32[]{:S(2)}, u32[]{:S(2)}) collective-permute-start(bf16[192,768]{0,1:T(8,128)(2,1)S(1)} %constant_dynamic-slice_fusion.9), channel_id=1, source_target_pairs={{0,16},{16,0},{1,17},{17,1},{2,18},{18,2},{3,19},{19,3},{4,20},{20... | collective-permute-start | bytes 884744 | tf_op jit(solution)/shard_map/cond/branch_1_fun/ppermute | solution.py:27
  295.6 8.9 %collective-permute-start.9 = (bf16[128,768]{1,0:T(8,128)(2,1)S(1)}, bf16[128,768]{1,0:T(8,128)(2,1)S(1)}, u32[]{:S(2)}, u32[]{:S(2)}) collective-permute-start(bf16[128,768]{1,0:T(8,128)(2,1)S(1)} %constant_dynamic-slice_fusion.10), channel_id=1, source_target_pairs={{0,1},{1,0},{2,3},{3,2},{4,5},{5,4},{6,7},{7,6},{8,9},{9,8},{10,11... | collective-permute-start | bytes 589832 | tf_op jit(solution)/shard_map/cond/branch_1_fun/ppermute | solution.py:27
  304.4 8.4 %collective-permute-start.11 = (bf16[96,768]{0,1:T(8,128)(2,1)S(1)}, bf16[96,768]{0,1:T(8,128)(2,1)S(1)}, u32[]{:S(2)}, u32[]{:S(2)}) collective-permute-start(bf16[96,768]{0,1:T(8,128)(2,1)S(1)} %constant_dynamic-slice_fusion.8), channel_id=1, source_target_pairs={{0,2},{1,3},{2,0},{3,1},{4,6},{5,7},{6,4},{7,5},{8,10},{9,11},{10,... | collective-permute-start | bytes 442376 | tf_op jit(solution)/shard_map/cond/branch_1_fun/ppermute | solution.py:27
  313.4 21.6 %collective-permute-start.15 = (bf16[448,768]{1,0:T(8,128)(2,1)S(1)}, bf16[448,768]{1,0:T(8,128)(2,1)S(1)}, u32[]{:S(2)}, u32[]{:S(2)}) collective-permute-start(bf16[448,768]{1,0:T(8,128)(2,1)S(1)} %constant_dynamic-slice_fusion.4), channel_id=1, source_target_pairs={{0,16},{16,0},{1,17},{17,1},{2,18},{18,2},{3,19},{19,3},{4,20},{20... | collective-permute-start | bytes 2064392 | tf_op jit(solution)/shard_map/cond/branch_1_fun/ppermute | solution.py:27
  315.1 6.2 %collective-permute-start.14 = (bf16[48,768]{0,1:T(8,128)(2,1)S(1)}, bf16[48,768]{0,1:T(8,128)(2,1)S(1)}, u32[]{:S(2)}, u32[]{:S(2)}) collective-permute-start(bf16[48,768]{0,1:T(8,128)(2,1)S(1)} %constant_dynamic-slice_fusion.5), channel_id=1, source_target_pairs={{0,4},{1,5},{2,6},{3,7},{4,0},{5,1},{6,2},{7,3},{8,12},{9,13},{10,... | collective-permute-start | bytes 221192 | tf_op jit(solution)/shard_map/cond/branch_1_fun/ppermute | solution.py:27
  315.2 6.2 %collective-permute-start.13 = (bf16[64,768]{1,0:T(8,128)(2,1)S(1)}, bf16[64,768]{1,0:T(8,128)(2,1)S(1)}, u32[]{:S(2)}, u32[]{:S(2)}) collective-permute-start(bf16[64,768]{1,0:T(8,128)(2,1)S(1)} %constant_dynamic-slice_fusion.6), channel_id=1, source_target_pairs={{0,2},{1,3},{2,0},{3,1},{4,6},{5,7},{6,4},{7,5},{8,10},{9,11},{10,... | collective-permute-start | bytes 294920 | tf_op jit(solution)/shard_map/cond/branch_1_fun/ppermute | solution.py:27
  335.3 14.0 %collective-permute-start.17 = (bf16[24,768]{0,1:T(8,128)(2,1)S(1)}, bf16[24,768]{0,1:T(8,128)(2,1)S(1)}, u32[]{:S(2)}, u32[]{:S(2)}) collective-permute-start(bf16[24,768]{0,1:T(8,128)(2,1)S(1)} %constant_dynamic-slice_fusion.3), channel_id=1, source_target_pairs={{0,8},{1,9},{2,10},{3,11},{4,12},{5,13},{6,14},{7,15},{8,0},{9,1},... | collective-permute-start | bytes 110600 | tf_op jit(solution)/shard_map/cond/branch_1_fun/ppermute | solution.py:27
  335.4 14.1 %collective-permute-start.18 = (bf16[224,768]{1,0:T(8,128)(2,1)S(1)}, bf16[224,768]{1,0:T(8,128)(2,1)S(1)}, u32[]{:S(2)}, u32[]{:S(2)}) collective-permute-start(bf16[224,768]{1,0:T(8,128)(2,1)S(1)} %constant_dynamic-slice_fusion.2), channel_id=1, source_target_pairs={{0,2},{1,3},{2,0},{3,1},{4,6},{5,7},{6,4},{7,5},{8,10},{9,11},{10,... | collective-permute-start | bytes 1032200 | tf_op jit(solution)/shard_map/cond/branch_1_fun/ppermute | solution.py:27
  335.5 14.0 %collective-permute-start.16 = (bf16[64,768]{1,0:T(8,128)(2,1)S(1)}, bf16[64,768]{1,0:T(8,128)(2,1)S(1)}, u32[]{:S(2)}, u32[]{:S(2)}) collective-permute-start(bf16[64,768]{1,0:T(8,128)(2,1)S(1)} %add_convert_fusion.14), channel_id=1, source_target_pairs={{0,4},{1,5},{2,6},{3,7},{4,0},{5,1},{6,2},{7,3},{8,12},{9,13},{10,... | collective-permute-start | bytes 294920 | tf_op jit(solution)/shard_map/cond/branch_1_fun/ppermute | solution.py:27
  349.6 14.8 %collective-permute-start.20 = (bf16[24,768]{0,1:T(8,128)(2,1)S(1)}, bf16[24,768]{0,1:T(8,128)(2,1)S(1)}, u32[]{:S(2)}, u32[]{:S(2)}) collective-permute-start(bf16[24,768]{0,1:T(8,128)(2,1)S(1)} %add_convert_fusion.6), channel_id=1, source_target_pairs={{0,8},{1,9},{2,10},{3,11},{4,12},{5,13},{6,14},{7,15},{8,0},{9,1},... | collective-permute-start | bytes 110600 | tf_op jit(solution)/shard_map/cond/branch_1_fun/ppermute | solution.py:27
  349.9 19.4 %collective-permute-start.21 = (bf16[112,768]{1,0:T(8,128)(2,1)S(1)}, bf16[112,768]{1,0:T(8,128)(2,1)S(1)}, u32[]{:S(2)}, u32[]{:S(2)}) collective-permute-start(bf16[112,768]{1,0:T(8,128)(2,1)S(1)} %constant_dynamic-slice_fusion.1), channel_id=1, source_target_pairs={{0,4},{1,5},{2,6},{3,7},{4,0},{5,1},{6,2},{7,3},{8,12},{9,13},{10,... | collective-permute-start | bytes 516104 | tf_op jit(solution)/shard_map/cond/branch_1_fun/ppermute | solution.py:27
  351.8 17.4 %collective-permute-start.19 = (bf16[64,768]{1,0:T(8,128)(2,1)S(1)}, bf16[64,768]{1,0:T(8,128)(2,1)S(1)}, u32[]{:S(2)}, u32[]{:S(2)}) collective-permute-start(bf16[64,768]{1,0:T(8,128)(2,1)S(1)} %add_convert_fusion.13), channel_id=1, source_target_pairs={{0,8},{1,9},{2,10},{3,11},{4,12},{5,13},{6,14},{7,15},{8,0},{9,1},... | collective-permute-start | bytes 294920 | tf_op jit(solution)/shard_map/cond/branch_1_fun/ppermute | solution.py:27
  369.4 7.5 %collective-permute-start.23 = (bf16[48,768]{1,0:T(8,128)(2,1)S(1)}, bf16[48,768]{1,0:T(8,128)(2,1)S(1)}, u32[]{:S(2)}, u32[]{:S(2)}) collective-permute-start(bf16[48,768]{1,0:T(8,128)(2,1)S(1)} %maximum_select_fusion.7), channel_id=1, source_target_pairs={{0,4},{1,5},{2,6},{3,7},{4,0},{5,1},{6,2},{7,3},{8,12},{9,13},{10,... | collective-permute-start | bytes 221192 | tf_op jit(solution)/shard_map/cond/branch_1_fun/ppermute | solution.py:27
  369.5 9.5 %collective-permute-start.24 = (bf16[56,768]{1,0:T(8,128)(2,1)S(1)}, bf16[56,768]{1,0:T(8,128)(2,1)S(1)}, u32[]{:S(2)}, u32[]{:S(2)}) collective-permute-start(bf16[56,768]{1,0:T(8,128)(2,1)S(1)} %constant_dynamic-slice_fusion), channel_id=1, source_target_pairs={{0,8},{1,9},{2,10},{3,11},{4,12},{5,13},{6,14},{7,15},{8,0},{9,1},... | collective-permute-start | bytes 258056 | tf_op jit(solution)/shard_map/cond/branch_1_fun/ppermute | solution.py:27
  372.2 6.8 %collective-permute-start.22 = (bf16[64,768]{1,0:T(8,128)(2,1)S(1)}, bf16[64,768]{1,0:T(8,128)(2,1)S(1)}, u32[]{:S(2)}, u32[]{:S(2)}) collective-permute-start(bf16[64,768]{1,0:T(8,128)(2,1)S(1)} %add_convert_fusion.12), channel_id=1, source_target_pairs={{0,2},{1,3},{2,0},{3,1},{4,6},{5,7},{6,4},{7,5},{8,10},{9,11},{10,... | collective-permute-start | bytes 294920 | tf_op jit(solution)/shard_map/cond/branch_1_fun/ppermute | solution.py:27
  379.1 8.4 %collective-permute-start.27 = (bf16[56,768]{1,0:T(8,128)(2,1)S(1)}, bf16[56,768]{1,0:T(8,128)(2,1)S(1)}, u32[]{:S(2)}, u32[]{:S(2)}) collective-permute-start(bf16[56,768]{1,0:T(8,128)(2,1)S(1)} %add_convert_fusion.18), channel_id=1, source_target_pairs={{0,8},{1,9},{2,10},{3,11},{4,12},{5,13},{6,14},{7,15},{8,0},{9,1},... | collective-permute-start | bytes 258056 | tf_op jit(solution)/shard_map/cond/branch_1_fun/ppermute | solution.py:27
  379.8 8.4 %collective-permute-start.26 = (bf16[96,768]{1,0:T(8,128)(2,1)S(1)}, bf16[96,768]{1,0:T(8,128)(2,1)S(1)}, u32[]{:S(2)}, u32[]{:S(2)}) collective-permute-start(bf16[96,768]{1,0:T(8,128)(2,1)S(1)} %maximum_select_fusion.6), channel_id=1, source_target_pairs={{0,2},{1,3},{2,0},{3,1},{4,6},{5,7},{6,4},{7,5},{8,10},{9,11},{10,... | collective-permute-start | bytes 442376 | tf_op jit(solution)/shard_map/cond/branch_1_fun/ppermute | solution.py:27
  379.8 9.2 %collective-permute-start.25 = (bf16[128,768]{1,0:T(8,128)(2,1)S(1)}, bf16[128,768]{1,0:T(8,128)(2,1)S(1)}, u32[]{:S(2)}, u32[]{:S(2)}) collective-permute-start(bf16[128,768]{1,0:T(8,128)(2,1)S(1)} %maximum_select_fusion.4), channel_id=1, source_target_pairs={{0,1},{1,0},{2,3},{3,2},{4,5},{5,4},{6,7},{7,6},{8,9},{9,8},{10,11... | collective-permute-start | bytes 589832 | tf_op jit(solution)/shard_map/cond/branch_1_fun/ppermute | solution.py:27
  390.1 10.0 %collective-permute-start.43 = (bf16[112,768]{1,0:T(8,128)(2,1)}, bf16[112,768]{1,0:T(8,128)(2,1)S(1)}, u32[]{:S(2)}, u32[]{:S(2)}) collective-permute-start(bf16[112,768]{1,0:T(8,128)(2,1)} %get-tuple-element.199), channel_id=1, source_target_pairs={{0,4},{1,5},{2,6},{3,7},{4,0},{5,1},{6,2},{7,3},{8,12},{9,13},{10,... | collective-permute-start | bytes 516104 | tf_op jit(solution)/shard_map/ppermute | solution.py:27
  401.3 15.7 %collective-permute-start.44 = (bf16[224,768]{1,0:T(8,128)(2,1)S(1)}, bf16[224,768]{1,0:T(8,128)(2,1)S(1)}, u32[]{:S(2)}, u32[]{:S(2)}) collective-permute-start(bf16[224,768]{1,0:T(8,128)(2,1)S(1)} %maximum_select_fusion.13), channel_id=1, source_target_pairs={{0,2},{1,3},{2,0},{3,1},{4,6},{5,7},{6,4},{7,5},{8,10},{9,11},{10,... | collective-permute-start | bytes 1032200 | tf_op jit(solution)/shard_map/ppermute | solution.py:27
  441.3 24.0 %collective-permute-start.45 = (bf16[448,768]{1,0:T(8,128)(2,1)S(1)}, bf16[448,768]{1,0:T(8,128)(2,1)S(1)}, u32[]{:S(2)}, u32[]{:S(2)}) collective-permute-start(bf16[448,768]{1,0:T(8,128)(2,1)S(1)} %maximum_select_fusion.9), channel_id=1, source_target_pairs={{0,16},{16,0},{1,17},{17,1},{2,18},{18,2},{3,19},{19,3},{4,20},{20... | collective-permute-start | bytes 2064392 | tf_op jit(solution)/shard_map/ppermute | solution.py:27
  442.1 21.9 %collective-permute-start.42 = (bf16[192,768]{1,0:T(8,128)(2,1)}, bf16[192,768]{1,0:T(8,128)(2,1)S(1)}, u32[]{:S(2)}, u32[]{:S(2)}) collective-permute-start(bf16[192,768]{1,0:T(8,128)(2,1)} %get-tuple-element.195), channel_id=1, source_target_pairs={{0,16},{16,0},{1,17},{17,1},{2,18},{18,2},{3,19},{19,3},{4,20},{20... | collective-permute-start | bytes 884744 | tf_op jit(solution)/shard_map/ppermute | solution.py:27
  465.9 3.2 collective-permute-start.46
  466.0 6.2 %collective-permute-start.47 = (bf16[384,768]{1,0:T(8,128)(2,1)S(1)}, bf16[384,768]{1,0:T(8,128)(2,1)S(1)}, u32[]{:S(2)}, u32[]{:S(2)}) collective-permute-start(bf16[384,768]{1,0:T(8,128)(2,1)S(1)} %maximum_select_fusion.10.early_ref), channel_id=1, source_target_pairs={{0,1},{1,0},{2,3},{3,2},{4,5},{5,4},{6,7},{7,6},{8,9},{9,8},{10,11... | collective-permute-start | bytes 1769480 | tf_op jit(solution)/shard_map/ppermute | solution.py:27
  (64 other events, 323.2 us)
Sparse Core Ops, SparseCore 0:
  179.9 247.7 all-reduce.7

commit v12 on v10

--- a/solution.py
+++ b/solution.py
@@ -119,6 +119,19 @@
             axis, bit = back[2 * len(down) - 1 - step]
             held = paired(held, axis, bit, 0)
     return held, down, back, min(done + steps, 2 * len(down))
+
+
+def double_beside(state, values):
+    held, down, back, done = state
+    axis, bit = back[2 * len(down) - 1 - done]
+    other, values = lax.optimization_barrier((swap(held, axis, bit), values))
+    side = (lax.axis_index(axis) // bit) % 2
+    held = jnp.where(
+        side == 0,
+        jnp.concatenate([held, other], 0),
+        jnp.concatenate([other, held], 0),
+    )
+    return (held, down, back, done + 1), values
 
 
 def last_swap(state):
@@ -865,9 +878,8 @@
     )(bounds, qkv, grad_mixed, probs, mark_k, mix)
     grad_w_down = lax.dot_general(active, grad_low_two, rows_in, preferred_element_type=F32)
     grad_w_up = lax.dot_general(hidden_low, grad_upper, rows_in, preferred_element_type=F32)
-    grad_ext = extended(grad_mixed, radius, window_rows)
-    grad_mix, grad_w_down, grad_w_up, grad_ext = lax.optimization_barrier(
-        (grad_mix.astype(BF), grad_w_down.astype(BF), grad_w_up.astype(BF), grad_ext)
+    grad_mix, grad_w_down, grad_w_up = lax.optimization_barrier(
+        (grad_mix.astype(BF), grad_w_down.astype(BF), grad_w_up.astype(BF))
     )
     sum_w_down, sum_w_up = lax.psum((grad_w_down, grad_w_up), ("row", "seq"))
 
@@ -875,6 +887,7 @@
         grad_mix = seq_quarter(grad_mix.astype(BF), add_join)
         grad_w_out = lax.dot_general(mixed, grad_low_one, rows_in, preferred_element_type=F32)
 
+        grad_ext = extended(grad_mixed, radius, window_rows)
         grad_conv, products = pl.pallas_call(
             lambda *refs: conv_back_kernel(docs, *refs),
             grid=(blocks,),
@@ -979,6 +992,7 @@
         late = lax.dynamic_update_slice_in_dim(
             late, (weight_grad(grad_keys) + mark_grad_k).astype(BF), width + spare_rows, 0
         )
+        late, (early,) = tied(late, [early])
         late = begin(late, ORDER, ORDER)
         grad_projected = jnp.concatenate([grad_queries, grad_keys, grad_values], axis=1)
         grad_input = grad_one + lax.dot_general(
@@ -1009,11 +1023,10 @@
     )
     early, late = (early, plan, plan, sent + 2), (late, plan, plan, sent)
     last = 2 * len(plan) - 1
-    late = advance(late, 2)
-    (sum_w_down, sum_w_up), (late,) = tied(
-        (sum_w_down.astype(F32), sum_w_up.astype(F32)), [late]
-    )
-    early, late = advance(early, last - early[3]), advance(late, last - late[3])
+    early, late = advance(early, last - early[3]), advance(late, last - 1 - late[3])
+    late, (sum_w_down, sum_w_up) = double_beside(
+        late, (sum_w_down.astype(F32), sum_w_up.astype(F32))
+    )
     grad_input = grad_input + lax.dot_general(
         onehot, mark_back, rows_in, preferred_element_type=F32
     )

time: 483 us -> 466 us (0.965)
  waiting for transfers between devices: 146 us -> 116 us
  starting transfers between devices: 38 us -> 67.2 us
  Pallas kernels: 123 us -> 109 us
    ppermute x44, waiting for transfers between devices: 146 us -> 116 us  [swap(): return lax.ppermute(array, axis, [(i, i ^ bit) for i in range(count)])]
    ppermute x44, starting transfers between devices: 32.2 us -> 60.1 us  [swap(): return lax.ppermute(array, axis, [(i, i ^ bit) for i in range(count)])]
    select_n x16 -> x15, other arithmetic: 9.87 us -> 9.08 us  [paired(): jnp.where(side == 0, jnp.concatenate([array, other], dim), jnp.concatenat...]
  transfers between devices with their start and end apart: 49 -> 49, of which waited for: 32 -> 29; matrix products, arithmetic and copies ran while one was open for 25% -> 23% of each run, Pallas kernels for 10% -> 7%
where the time goes in v12:
time: 466 us; the launch traced here: 457 us
  waiting for transfers between devices  116 us (25%)
  Pallas kernels  109 us (23%)
  starting transfers between devices  67.2 us (14%)
  other arithmetic  50.5 us (11%)
  local copies, waits for them, and re-layouts  49.4 us (11%)
  matrix products  49.4 us (11%)
  between operations  15.1 us (3%)
    ppermute x44, waiting for transfers between devices, swap(): return lax.ppermute(array, axis, [(i, i ^ bit) for i in range(count)])  116 us
    ppermute x44, starting transfers between devices, swap(): return lax.ppermute(array, axis, [(i, i ^ bit) for i in range(count)])  60.1 us
    pallas_call x1, Pallas kernels, per_device(): pl.pallas_call(ffn_kernel, grid=(tok_count // FFN_BLOCK,), in_specs=[ffn_...  40.2 us
    pallas_call x1, Pallas kernels, remaining(): pl.pallas_call(lambda *refs: pinv_back_kernel(scale, *refs), out_shape=(s...  9.93 us
  transfers between devices with their start and end apart: 49, of which 29 were waited for; matrix products, arithmetic and copies ran while one was open for 23% of the time, Pallas kernels for 7%

profile of v12, /device:TPU:0, one launch (start us, length us, event | category | flops | bytes accessed | tf_op | source)
XLA Modules:
  0.0 457.0 jit_solution(6463702639294957378)
XLA Ops:
  10.9 2.2 fusion.29
  14.8 3.0 collective-permute-start.31
  17.7 3.1 collective-permute-done.31
  22.7 6.0 %add_convert_fusion.20.refs_2_.refs_3_.refs_1_ = bf16[1024,2304]{1,0:T(8,128)(2,1)S(1)} fusion(bf16[768,2304]{1,0:T(8,128)(2,1)} %param.21, f32[2304]{0:T(1024)S(1)} %pad_maximum_fusion.3, bf16[1,1024,768]{2,1,0:T(8,128)(2,1)S(1)} %copy-done.25), kind=kOutput, calls=%fused_computation.75 | convolution fusion | flops 3628597248 | bytes 9839616 | tf_op jit(solution)/shard_map/dot_general | solution.py:749
  28.8 2.7 collective-permute-start.33
  35.6 3.2 collective-permute-start.34
  38.8 3.3 collective-permute-done.34
  43.9 2.6 fusion.27
  46.7 5.0 %landmark.1 = bf16[256,896]{1,0:T(8,128)(2,1)S(1)} custom-call(s32[8]{0:T(128)S(1)} %add_subtract_fusion.refs_0_, bf16[256,768]{1,0:T(8,128)(2,1)S(1)} %fusion.31.refs_1_, bf16[1024,2304]{1,0:T(8,128)(2,1)S(1)} %bitcast.62, bf16[1024,2304]{1,0:T(8,128)(2,1)S(1)} %bitcast.62), custom_call_target="tpu_custom_call" | custom-call | tf_op jit(solution)/shard_map/landmark/pallas_call | solution.py:756
  54.7 2.0 join.4
  60.2 6.0 %pinv.1 = (f32[3,64,64]{2,1,0:T(8,128)}, f32[3,64,64]{2,1,0:T(8,128)}, f32[72,64,64]{2,1,0:T(8,128)}) custom-call(f32[3,64,64]{2,1,0:T(8,128)S(1)} %bitcast.71, f32[3,64,64]{2,1,0:T(8,128)S(1)} %bitcast.69), custom_call_target="tpu_custom_call" | custom-call | tf_op jit(solution)/shard_map/pinv/pallas_call | solution.py:789
  68.0 1.9 join.5.a_ref
  72.2 4.5 collective-permute-done.38
  77.4 2.0 join.6.a_ref
  80.4 4.3 collective-permute-start.39
  84.7 7.4 %collective-permute-done.39 = bf16[64,1280]{1,0:T(8,128)(2,1)S(1)} collective-permute-done((bf16[64,1280]{1,0:T(8,128)(2,1)S(1)}, bf16[64,1280]{1,0:T(8,128)(2,1)S(1)}, u32[]{:S(2)}, u32[]{:S(2)}) %collective-permute-start.39) | collective-permute-done | bytes 163872 | tf_op jit(solution)/shard_map/ppermute | solution.py:27
  95.4 4.5 collective-permute-done.40
  103.8 9.0 %token_.1 = (bf16[1024,768]{1,0:T(8,128)(2,1)}, bf16[768,1024]{1,0:T(8,128)(2,1)S(1)}) custom-call(s32[8]{0:T(128)S(1)} %add_subtract_fusion.refs_0_, bf16[1024,2304]{1,0:T(8,128)(2,1)} %copy-done.7, bf16[1152,768]{1,0:T(8,128)(2,1)S(1)} %copy-done.8, bf16[256,768]{1,0:T(8,128)(2,1)S(1)} %slice.187.refs_3_.refs_4_, ...), custom_call_target="tpu_custom_call" | custom-call | tf_op jit(solution)/shard_map/token/pallas_call | solution.py:817
  113.5 40.2 %ffn.1 = (f32[1024,768]{1,0:T(8,128)}, f32[1024,768]{1,0:T(8,128)}, bf16[1024,3072]{1,0:T(8,128)(2,1)}, bf16[1024,3072]{1,0:T(8,128)(2,1)}, bf16[1024,768]{1,0:T...) custom-call(bf16[1024,768]{1,0:T(8,128)(2,1)} %bitcast.67, ...), custom_call_target="tpu_custom_call" | custom-call | tf_op jit(solution)/shard_map/ffn/pallas_call | solution.py:839
  153.7 7.9 %token_back.1 = (bf16[1024,768]{1,0:T(8,128)(2,1)}, f32[256,768]{1,0:T(8,128)S(1)}, f32[256,768]{1,0:T(8,128)}) custom-call(s32[8]{0:T(128)S(1)} %add_subtract_fusion.refs_0_, bf16[1024,2304]{1,0:T(8,128)(2,1)} %copy-done.7, bf16[1024,768]{1,0:T(8,128)(2,1)} %get-tuple-element.183.refs_2_, bf16[768,1024]{1,0:T(8,128)(2,1)S(1)} %get-tuple-element.184.refs_3_, ...), custom_call_target="tpu_custom_call" | custom-call | tf_op jit(solution)/shard_map/token_back/pallas_call | solution.py:863
  161.7 6.9 %convolution_convert_fusion.3 = bf16[3072,768]{1,0:T(8,128)(2,1)} fusion(bf16[1024,3072]{1,0:T(8,128)(2,1)S(1)} %copy-done.64, bf16[1024,768]{1,0:T(8,128)(2,1)S(1)} %copy-done.68), kind=kOutput, calls=%fused_computation.77 | convolution fusion | flops 4834197504 | bytes 12582912 | tf_op jit(solution)/shard_map/dot_general | solution.py:879
  168.7 6.8 %convolution_convert_fusion.2 = bf16[768,3072]{1,0:T(8,128)(2,1)} fusion(bf16[1024,768]{1,0:T(8,128)(2,1)S(1)} %copy-done.67, bf16[1024,3072]{1,0:T(8,128)(2,1)S(1)} %bitcast.89), kind=kOutput, calls=%fused_computation.76 | convolution fusion | flops 4834197504 | bytes 12582912 | tf_op jit(solution)/shard_map/dot_general | solution.py:880
  176.2 217.0 %conditional.1 = (bf16[384,768]{1,0:T(8,128)(2,1)}, bf16[112,768]{1,0:T(8,128)(2,1)}, bf16[256,768]{1,0:T(8,128)(2,1)}, f32[1024,768]{1,0:T(8,128)}) conditional(s32[]{:T(128)} %bitcast.23, () %tuple.33, (bf16[256,768]{1,0:T(8,128)(2,1)S(1)}, bf16[1024,768]{1,0:T(8,128)(2,1)}, f32[12,33]{1,0:T(8,128)S(1)}, s32[8]{0:T(128)S(1)}, ...), branch_computations={%region_1.2_spmd, %region_2.6_spmd} | conditional | flops 9721938944 | bytes 284669888 | solution.py:1021
  177.9 2.9 collective-permute-start.4
  182.6 2.0 collective-permute-start.1
  184.6 4.8 %fusion.48 = f32[768,768]{1,0:T(8,128)} fusion(bf16[1024,768]{1,0:T(8,128)(2,1)} %get-tuple-element.78, bf16[1024,768]{1,0:T(8,128)(2,1)} %get-tuple-element.88), kind=kOutput, calls=%fused_computation.152 | convolution fusion | flops 1207959552 | bytes 5505024 | tf_op jit(solution)/shard_map/cond/branch_1_fun/dot_general | solution.py:933
  193.5 5.2 %collective-permute-done.2 = bf16[64,768]{1,0:T(8,128)(2,1)S(1)} collective-permute-done((bf16[64,768]{1,0:T(8,128)(2,1)S(1)}, bf16[64,768]{1,0:T(8,128)(2,1)S(1)}, u32[]{:S(2)}, u32[]{:S(2)}) %collective-permute-start.2) | collective-permute-done | bytes 98336 | tf_op jit(solution)/shard_map/cond/branch_1_fun/ppermute | solution.py:27
  198.7 8.2 %collective-permute-start.3 = (bf16[64,768]{1,0:T(8,128)(2,1)S(1)}, bf16[64,768]{1,0:T(8,128)(2,1)S(1)}, u32[]{:S(2)}, u32[]{:S(2)}) collective-permute-start(bf16[64,768]{1,0:T(8,128)(2,1)S(1)} %add_convert_fusion.15), channel_id=1, source_target_pairs={{0,8},{1,9},{2,10},{3,11},{4,12},{5,13},{6,14},{7,15},{8,0},{9,1},... | collective-permute-start | bytes 294920 | tf_op jit(solution)/shard_map/cond/branch_1_fun/ppermute | solution.py:27
  208.7 5.9 %conv_back.1 = (f32[1024,768]{1,0:T(8,128)S(1)}, f32[16,256]{1,0:T(8,128)S(1)}) custom-call(s32[8]{0:T(128)S(1)} %get-tuple-element.54.refs_0_, bf16[1152,768]{1,0:T(8,128)(2,1)S(1)} %maximum_maximum_fusion.refs_1_, bf16[1152,768]{1,0:T(8,128)(2,1)S(1)} %copy-done.10, f32[12,256]{1,0:T(8,128)S(1)} %pad.17.refs_3_), custom_call_target="tpu_custom_call" | custom-call | tf_op jit(solution)/shard_map/cond/branch_1_fun/conv_back/pallas_call | solution.py:891
  215.9 2.1 mix_back.1
  226.4 3.6 convolution_convert_fusion.1
  230.2 7.0 %landmark_back.1 = (bf16[1024,768]{1,0:T(8,128)(2,1)S(1)}, bf16[1024,768]{1,0:T(8,128)(2,1)S(1)}, f32[256,768]{1,0:T(8,128)S(1)}) custom-call(s32[8]{0:T(128)S(1)} %get-tuple-element.54.refs_0_, bf16[1024,2304]{1,0:T(8,128)(2,1)S(1)} %bitcast.64, bf16[1024,2304]{1,0:T(8,128)(2,1)S(1)} %bitcast.64, f32[1024,768]{1,0:T(8,128)S(1)} %get-tuple-element.62.refs_3_, ...), custom_call_target="tpu_custom_call" | custom-call | tf_op jit(solution)/shard_map/cond/branch_1_fun/landmark_back/pallas_call | solution.py:915
  245.8 9.9 %pinv_back.1 = (f32[3,64,64]{2,1,0:T(8,128)}, f32[3,64,64]{2,1,0:T(8,128)}) custom-call(f32[3,64,64]{2,1,0:T(8,128)S(1)} %copy-done.36, f32[3,64,64]{2,1,0:T(8,128)S(1)} %copy-done.34, f32[3,64,64]{2,1,0:T(8,128)S(1)} %copy-done.42, f32[72,64,64]{2,1,0:T(8,128)} %get-tuple-element.74.refs_3_, bf16[3,64,64]{2,1,0:T(8,128)(2,1)} %bitcast.81, ...), custom_call_target="tpu_custom_call" | custom-call | tf_op jit(solution)/shard_map/cond/branch_1_fun/pinv_back/pallas_call | solution.py:941
  257.8 3.0 dynamic_update_slice.18
  262.0 3.0 fusion.49
  268.4 3.0 add_convert_fusion.2
  276.2 2.4 dynamic_update_slice.16
  279.3 1.9 constant_dynamic-slice_fusion.9
  281.5 2.5 fusion.18
  286.2 2.0 concatenate.100
  290.5 8.1 %collective-permute-done.10 = bf16[384,768]{1,0:T(8,128)(2,1)} collective-permute-done((bf16[384,768]{1,0:T(8,128)(2,1)}, bf16[384,768]{1,0:T(8,128)(2,1)}, u32[]{:S(2)}, u32[]{:S(2)}) %collective-permute-start.10) | collective-permute-done | bytes 589856 | tf_op jit(solution)/shard_map/cond/branch_1_fun/ppermute | solution.py:27
  301.6 5.6 %fusion.9 = f32[1024,768]{1,0:T(8,128)} fusion(f32[1024,768]{1,0:T(8,128)S(1)} %copy-done.66, bf16[768,2304]{1,0:T(8,128)(2,1)S(1)} %copy-done.65, bf16[1024,768]{1,0:T(8,128)(2,1)S(1)} %copy-done.1, bf16[1024,768]{1,0:T(8,128)(2,1)S(1)} %copy-done.6, bf16[1024,768]{1,0:T(8,128)(2,1)S(1)} %copy-done.28), kind=kOutput, calls=%fused_computation.16 | convolution fusion | flops 3638820864 | bytes 14548992 | tf_op jit(solution)/shard_map/cond/branch_1_fun/dot_general | solution.py:998
  309.9 3.2 collective-permute-start.14
  313.1 3.4 collective-permute-done.13
  317.9 11.2 %collective-permute-done.15 = bf16[448,768]{1,0:T(8,128)(2,1)S(1)} collective-permute-done((bf16[448,768]{1,0:T(8,128)(2,1)S(1)}, bf16[448,768]{1,0:T(8,128)(2,1)S(1)}, u32[]{:S(2)}, u32[]{:S(2)}) %collective-permute-start.15) | collective-permute-done | bytes 688160 | tf_op jit(solution)/shard_map/cond/branch_1_fun/ppermute | solution.py:27
  329.3 2.5 collective-permute-start.17
  336.7 2.6 collective-permute-done.16
  339.3 11.7 %collective-permute-done.18 = bf16[224,768]{1,0:T(8,128)(2,1)S(1)} collective-permute-done((bf16[224,768]{1,0:T(8,128)(2,1)S(1)}, bf16[224,768]{1,0:T(8,128)(2,1)S(1)}, u32[]{:S(2)}, u32[]{:S(2)}) %collective-permute-start.18) | collective-permute-done | bytes 344096 | tf_op jit(solution)/shard_map/cond/branch_1_fun/ppermute | solution.py:27
  351.3 2.8 collective-permute-start.19
  354.6 6.3 %collective-permute-done.20 = bf16[48,768]{1,0:T(8,128)(2,1)S(1)} collective-permute-done((bf16[48,768]{1,0:T(8,128)(2,1)S(1)}, bf16[48,768]{1,0:T(8,128)(2,1)S(1)}, u32[]{:S(2)}, u32[]{:S(2)}) %collective-permute-start.20) | collective-permute-done | bytes 73760 | tf_op jit(solution)/shard_map/cond/branch_1_fun/ppermute | solution.py:27
  361.0 4.1 collective-permute-done.19
  367.0 2.9 collective-permute-start.24
  371.8 3.5 collective-permute-done.24
  375.4 5.3 %collective-permute-done.23 = bf16[96,768]{1,0:T(8,128)(2,1)S(1)} collective-permute-done((bf16[96,768]{1,0:T(8,128)(2,1)S(1)}, bf16[96,768]{1,0:T(8,128)(2,1)S(1)}, u32[]{:S(2)}, u32[]{:S(2)}) %collective-permute-start.23) | collective-permute-done | bytes 147488 | tf_op jit(solution)/shard_map/cond/branch_1_fun/ppermute | solution.py:27
  383.8 5.1 %collective-permute-done.27 = bf16[56,768]{1,0:T(8,128)(2,1)S(1)} collective-permute-done((bf16[56,768]{1,0:T(8,128)(2,1)S(1)}, bf16[56,768]{1,0:T(8,128)(2,1)S(1)}, u32[]{:S(2)}, u32[]{:S(2)}) %collective-permute-start.27) | collective-permute-done | bytes 86048 | tf_op jit(solution)/shard_map/cond/branch_1_fun/ppermute | solution.py:27
  393.8 5.7 %collective-permute-done.43 = bf16[112,768]{1,0:T(8,128)(2,1)S(1)} collective-permute-done((bf16[112,768]{1,0:T(8,128)(2,1)}, bf16[112,768]{1,0:T(8,128)(2,1)S(1)}, u32[]{:S(2)}, u32[]{:S(2)}) %collective-permute-start.43) | collective-permute-done | bytes 172064 | tf_op jit(solution)/shard_map/ppermute | solution.py:27
  402.6 7.1 %collective-permute-done.44 = bf16[224,768]{1,0:T(8,128)(2,1)S(1)} collective-permute-done((bf16[224,768]{1,0:T(8,128)(2,1)S(1)}, bf16[224,768]{1,0:T(8,128)(2,1)S(1)}, u32[]{:S(2)}, u32[]{:S(2)}) %collective-permute-start.44) | collective-permute-done | bytes 344096 | tf_op jit(solution)/shard_map/ppermute | solution.py:27
  409.9 2.6 collective-permute-start.45
  412.5 1.9 fusion.30
  414.4 3.9 add.373
  420.2 7.3 %convert_element_type.348 = f32[3072,768]{1,0:T(8,128)} convert(bf16[3072,768]{1,0:T(8,128)(2,1)} %get-tuple-element.220) | non-fusion elementwise | flops 2359296 | bytes 14155776 | tf_op jit(solution)/shard_map/convert_element_type | solution.py:1028
  427.5 5.0 %convert_element_type.349 = f32[768,3072]{1,0:T(8,128)} convert(bf16[768,3072]{1,0:T(8,128)(2,1)S(1)} %copy-done.17) | non-fusion elementwise | flops 2359296 | bytes 14155776 | tf_op jit(solution)/shard_map/convert_element_type | solution.py:1028
  434.9 2.3 collective-permute-done.47.early_other_ref
  442.3 7.6 %settle_qkv.1 = f32[768,2304]{1,0:T(8,128)} custom-call(s32[1]{0:T(128)} %bitcast.25.side_ref, bf16[896,768]{1,0:T(8,128)(2,1)} %copy-done.15, bf16[896,768]{1,0:T(8,128)(2,1)} %copy-done.24, bf16[768,768]{1,0:T(8,128)(2,1)} %copy-done.11, bf16[768,768]{1,0:T(8,128)(2,1)} %copy-done.16), custom_call_target="tpu_custom_call" | custom-call | tf_op jit(solution)/shard_map/settle_qkv/pallas_call | solution.py:686
  (373 shorter events, 115.3 us)
Async XLA Ops:
  7.2 413.0 %all-reduce.8.cloned.1.call-start = ((), (), s32[]{:S(2)}) async-start(), calls=%async_computation | async-start | bytes 18874368 | tf_op jit(solution)/shard_map/psum | solution.py:884
  13.1 1.6 collective-permute-start.30
  14.8 6.0 %collective-permute-start.31 = (bf16[64,768]{1,0:T(8,128)(2,1)S(1)}, bf16[64,768]{1,0:T(8,128)(2,1)S(1)}, u32[]{:S(2)}, u32[]{:S(2)}) collective-permute-start(bf16[64,768]{1,0:T(8,128)(2,1)S(1)} %constant_dynamic-slice_fusion.20), channel_id=1, source_target_pairs={{0,2},{1,3},{2,0},{3,1},{4,6},{5,7},{6,4},{7,5},{8,10},{9,11},{10,... | collective-permute-start | bytes 294920 | tf_op jit(solution)/shard_map/ppermute | solution.py:27
  20.8 7.9 %collective-permute-start.32 = (bf16[64,768]{1,0:T(8,128)(2,1)S(1)}, bf16[64,768]{1,0:T(8,128)(2,1)S(1)}, u32[]{:S(2)}, u32[]{:S(2)}) collective-permute-start(bf16[64,768]{1,0:T(8,128)(2,1)S(1)} %add_convert_fusion.24), channel_id=1, source_target_pairs={{0,4},{1,5},{2,6},{3,7},{4,0},{5,1},{6,2},{7,3},{8,12},{9,13},{10,... | collective-permute-start | bytes 294920 | tf_op jit(solution)/shard_map/ppermute | solution.py:27
  28.8 6.8 %collective-permute-start.33 = (bf16[64,768]{1,0:T(8,128)(2,1)S(1)}, bf16[64,768]{1,0:T(8,128)(2,1)S(1)}, u32[]{:S(2)}, u32[]{:S(2)}) collective-permute-start(bf16[64,768]{1,0:T(8,128)(2,1)S(1)} %add_convert_fusion.23), channel_id=1, source_target_pairs={{0,8},{1,9},{2,10},{3,11},{4,12},{5,13},{6,14},{7,15},{8,0},{9,1},... | collective-permute-start | bytes 294920 | tf_op jit(solution)/shard_map/ppermute | solution.py:27
  31.5 10.8 %collective-permute-start.28 = (bf16[16,768]{1,0:T(8,128)(2,1)S(1)}, bf16[16,768]{1,0:T(8,128)(2,1)S(1)}, u32[]{:S(2)}, u32[]{:S(2)}) collective-permute-start(bf16[16,768]{1,0:T(8,128)(2,1)S(1)} %get-tuple-element.226), channel_id=1, source_target_pairs={{0,1},{1,2},{2,3},{3,4},{4,5},{5,6},{6,7},{7,8},{8,9},{9,10},{10,1... | collective-permute-start | bytes 73736 | tf_op jit(solution)/shard_map/ppermute | solution.py:154
  32.7 9.5 %collective-permute-start.29 = (bf16[16,768]{1,0:T(8,128)(2,1)S(1)}, bf16[16,768]{1,0:T(8,128)(2,1)S(1)}, u32[]{:S(2)}, u32[]{:S(2)}) collective-permute-start(bf16[16,768]{1,0:T(8,128)(2,1)S(1)} %get-tuple-element.227), channel_id=1, source_target_pairs={{1,0},{2,1},{3,2},{4,3},{5,4},{6,5},{7,6},{8,7},{9,8},{10,9},{11,1... | collective-permute-start | bytes 73736 | tf_op jit(solution)/shard_map/ppermute | solution.py:156
  35.6 6.5 %collective-permute-start.34 = (bf16[64,768]{1,0:T(8,128)(2,1)S(1)}, bf16[64,768]{1,0:T(8,128)(2,1)S(1)}, u32[]{:S(2)}, u32[]{:S(2)}) collective-permute-start(bf16[64,768]{1,0:T(8,128)(2,1)S(1)} %add_convert_fusion.22), channel_id=1, source_target_pairs={{0,2},{1,3},{2,0},{3,1},{4,6},{5,7},{6,4},{7,5},{8,10},{9,11},{10,... | collective-permute-start | bytes 294920 | tf_op jit(solution)/shard_map/ppermute | solution.py:27
  42.2 1.7 collective-permute-start.35
  52.4 1.6 collective-permute-start.36
  57.1 19.7 %copy-start.33 = (f32[64,3,64]{2,0,1:T(8,128)}, f32[64,3,64]{2,0,1:T(8,128)S(1)}, u32[]{:S(2)}) copy-start(f32[64,3,64]{2,0,1:T(8,128)S(1)} %copy.50) | copy-start | bytes 147460
  57.3 19.5 %copy-start.35 = (f32[64,3,64]{2,0,1:T(8,128)}, f32[64,3,64]{2,0,1:T(8,128)S(1)}, u32[]{:S(2)}) copy-start(f32[64,3,64]{2,0,1:T(8,128)S(1)} %copy.48) | copy-start | bytes 147460
  58.9 8.4 %collective-permute-start.37 = (bf16[64,896]{1,0:T(8,128)(2,1)S(1)}, bf16[64,896]{1,0:T(8,128)(2,1)S(1)}, u32[]{:S(2)}, u32[]{:S(2)}) collective-permute-start(bf16[64,896]{1,0:T(8,128)(2,1)S(1)} %get-tuple-element.230), channel_id=1, source_target_pairs={{0,2},{1,3},{2,0},{3,1},{4,6},{5,7},{6,4},{7,5},{8,10},{9,11},{10,... | collective-permute-start | bytes 344072 | tf_op jit(solution)/shard_map/ppermute | solution.py:27
  67.2 33.8 %copy-start.55 = (f32[768]{0:T(1024)S(1)}, f32[768]{0:T(1024)}, u32[]{:S(2)}) copy-start(f32[768]{0:T(1024)} %param.26) | copy-start | bytes 9220
  67.2 33.8 %copy-start.56 = (f32[768]{0:T(1024)S(1)}, f32[768]{0:T(1024)}, u32[]{:S(2)}) copy-start(f32[768]{0:T(1024)} %param.27) | copy-start | bytes 9220
  67.2 33.8 %copy-start.57 = (f32[768]{0:T(1024)S(1)}, f32[768]{0:T(1024)}, u32[]{:S(2)}) copy-start(f32[768]{0:T(1024)} %param.28) | copy-start | bytes 9220
  67.2 33.9 %copy-start.58 = (f32[768]{0:T(1024)S(1)}, f32[768]{0:T(1024)}, u32[]{:S(2)}) copy-start(f32[768]{0:T(1024)} %param.32) | copy-start | bytes 9220
  67.3 33.9 %copy-start.59 = (f32[768]{0:T(1024)S(1)}, f32[768]{0:T(1024)}, u32[]{:S(2)}) copy-start(f32[768]{0:T(1024)} %param.33) | copy-start | bytes 9220
  67.3 33.9 %copy-start.60 = (f32[768]{0:T(1024)S(1)}, f32[768]{0:T(1024)}, u32[]{:S(2)}) copy-start(f32[768]{0:T(1024)} %param.34) | copy-start | bytes 9220
  68.0 33.8 %copy-start.43 = (f32[12,33]{1,0:T(8,128)S(1)}, f32[12,33]{1,0:T(8,128)}, u32[]{:S(2)}) copy-start(f32[12,33]{1,0:T(8,128)} %param.24) | copy-start | bytes 4756
  70.8 5.9 %collective-permute-start.38 = (bf16[64,1088]{1,0:T(8,128)(2,1)S(1)}, bf16[64,1088]{1,0:T(8,128)(2,1)S(1)}, u32[]{:S(2)}, u32[]{:S(2)}) collective-permute-start(bf16[64,1088]{1,0:T(8,128)(2,1)S(1)} %pad_maximum_fusion.2), channel_id=1, source_target_pairs={{0,4},{1,5},{2,6},{3,7},{4,0},{5,1},{6,2},{7,3},{8,12},{9,13},{10,... | collective-permute-start | bytes 417800 | tf_op jit(solution)/shard_map/ppermute | solution.py:27
  77.4 26.4 %copy-start.8 = (bf16[1152,768]{1,0:T(8,128)(2,1)S(1)}, bf16[1152,768]{1,0:T(8,128)(2,1)}, u32[]{:S(2)}) copy-start(bf16[1152,768]{1,0:T(8,128)(2,1)} %maximum_maximum_fusion.1.refs_2_) | copy-start | bytes 5308420
  80.4 11.7 %collective-permute-start.39 = (bf16[64,1280]{1,0:T(8,128)(2,1)S(1)}, bf16[64,1280]{1,0:T(8,128)(2,1)S(1)}, u32[]{:S(2)}, u32[]{:S(2)}) collective-permute-start(bf16[64,1280]{1,0:T(8,128)(2,1)S(1)} %pad_maximum_fusion.1), channel_id=1, source_target_pairs={{0,8},{1,9},{2,10},{3,11},{4,12},{5,13},{6,14},{7,15},{8,0},{9,1},... | collective-permute-start | bytes 491528 | tf_op jit(solution)/shard_map/ppermute | solution.py:27
  94.9 5.0 %collective-permute-start.40 = (bf16[64,896]{1,0:T(8,128)(2,1)}, bf16[64,896]{1,0:T(8,128)(2,1)S(1)}, u32[]{:S(2)}, u32[]{:S(2)}) collective-permute-start(bf16[64,896]{1,0:T(8,128)(2,1)} %mix.1), channel_id=1, source_target_pairs={{0,2},{1,3},{2,0},{3,1},{4,6},{5,7},{6,4},{7,5},{8,10},{9,11},{10,... | collective-permute-start | bytes 344072 | tf_op jit(solution)/shard_map/ppermute | solution.py:27
  101.0 1.7 collective-permute-start.41
  176.3 6.3 %collective-permute-start = (bf16[128,768]{1,0:T(8,128)(2,1)S(1)}, bf16[128,768]{1,0:T(8,128)(2,1)S(1)}, u32[]{:S(2)}, u32[]{:S(2)}) collective-permute-start(bf16[128,768]{1,0:T(8,128)(2,1)S(1)} %constant_dynamic-slice_fusion.15), channel_id=1, source_target_pairs={{0,1},{1,0},{2,3},{3,2},{4,5},{5,4},{6,7},{7,6},{8,9},{9,8},{10,11... | collective-permute-start | bytes 589832 | tf_op jit(solution)/shard_map/cond/branch_1_fun/ppermute | solution.py:27
  177.9 29.0 %collective-permute-start.4 = (bf16[16,768]{1,0:T(8,128)(2,1)}, bf16[16,768]{1,0:T(8,128)(2,1)}, u32[]{:S(2)}, u32[]{:S(2)}) collective-permute-start(bf16[16,768]{1,0:T(8,128)(2,1)} %get-tuple-element.222), channel_id=1, source_target_pairs={{0,1},{1,2},{2,3},{3,4},{4,5},{5,6},{6,7},{7,8},{8,9},{9,10},{10,1... | collective-permute-start | bytes 73736 | tf_op jit(solution)/shard_map/cond/branch_1_fun/ppermute | solution.py:154
  180.8 26.1 %collective-permute-start.5 = (bf16[16,768]{1,0:T(8,128)(2,1)}, bf16[16,768]{1,0:T(8,128)(2,1)}, u32[]{:S(2)}, u32[]{:S(2)}) collective-permute-start(bf16[16,768]{1,0:T(8,128)(2,1)} %get-tuple-element.223), channel_id=1, source_target_pairs={{1,0},{2,1},{3,2},{4,3},{5,4},{6,5},{7,6},{8,7},{9,8},{10,9},{11,1... | collective-permute-start | bytes 73736 | tf_op jit(solution)/shard_map/cond/branch_1_fun/ppermute | solution.py:156
  182.6 8.5 %collective-permute-start.1 = (bf16[64,768]{1,0:T(8,128)(2,1)S(1)}, bf16[64,768]{1,0:T(8,128)(2,1)S(1)}, u32[]{:S(2)}, u32[]{:S(2)}) collective-permute-start(bf16[64,768]{1,0:T(8,128)(2,1)S(1)} %constant_dynamic-slice_fusion.14), channel_id=1, source_target_pairs={{0,2},{1,3},{2,0},{3,1},{4,6},{5,7},{6,4},{7,5},{8,10},{9,11},{10,... | collective-permute-start | bytes 294920 | tf_op jit(solution)/shard_map/cond/branch_1_fun/ppermute | solution.py:27
  191.2 7.5 %collective-permute-start.2 = (bf16[64,768]{1,0:T(8,128)(2,1)S(1)}, bf16[64,768]{1,0:T(8,128)(2,1)S(1)}, u32[]{:S(2)}, u32[]{:S(2)}) collective-permute-start(bf16[64,768]{1,0:T(8,128)(2,1)S(1)} %add_convert_fusion.16), channel_id=1, source_target_pairs={{0,4},{1,5},{2,6},{3,7},{4,0},{5,1},{6,2},{7,3},{8,12},{9,13},{10,... | collective-permute-start | bytes 294920 | tf_op jit(solution)/shard_map/cond/branch_1_fun/ppermute | solution.py:27
  198.7 16.6 %collective-permute-start.3 = (bf16[64,768]{1,0:T(8,128)(2,1)S(1)}, bf16[64,768]{1,0:T(8,128)(2,1)S(1)}, u32[]{:S(2)}, u32[]{:S(2)}) collective-permute-start(bf16[64,768]{1,0:T(8,128)(2,1)S(1)} %add_convert_fusion.15), channel_id=1, source_target_pairs={{0,8},{1,9},{2,10},{3,11},{4,12},{5,13},{6,14},{7,15},{8,0},{9,1},... | collective-permute-start | bytes 294920 | tf_op jit(solution)/shard_map/cond/branch_1_fun/ppermute | solution.py:27
  218.0 7.1 %collective-permute-start.6 = (bf16[64,896]{1,0:T(8,128)(2,1)}, bf16[64,896]{1,0:T(8,128)(2,1)}, u32[]{:S(2)}, u32[]{:S(2)}) collective-permute-start(bf16[64,896]{1,0:T(8,128)(2,1)} %mix_back.1), channel_id=1, source_target_pairs={{0,2},{1,3},{2,0},{3,1},{4,6},{5,7},{6,4},{7,5},{8,10},{9,11},{10,... | collective-permute-start | bytes 344072 | tf_op jit(solution)/shard_map/cond/branch_1_fun/ppermute | solution.py:27
  226.3 3.8 collective-permute-start.7
  241.9 26.6 %collective-permute-start.8 = (bf16[768,768]{1,0:T(8,128)(2,1)}, bf16[768,768]{1,0:T(8,128)(2,1)}, u32[]{:S(2)}, u32[]{:S(2)}) collective-permute-start(bf16[768,768]{1,0:T(8,128)(2,1)} %constant_dynamic-slice_fusion.11), channel_id=1, source_target_pairs={{0,1},{1,0},{2,3},{3,2},{4,5},{5,4},{6,7},{7,6},{8,9},{9,8},{10,11... | collective-permute-start | bytes 3538952 | tf_op jit(solution)/shard_map/cond/branch_1_fun/ppermute | solution.py:27
  245.8 16.2 %copy-start.5 = (bf16[1024,768]{1,0:T(8,128)(2,1)S(1)}, bf16[1024,768]{1,0:T(8,128)(2,1)}, u32[]{:S(2)}) copy-start(bf16[1024,768]{1,0:T(8,128)(2,1)} %copy-done.4) | copy-start | bytes 4718596 | tf_op jit(solution)/shard_map/cond
  281.3 17.3 %collective-permute-start.10 = (bf16[384,768]{1,0:T(8,128)(2,1)}, bf16[384,768]{1,0:T(8,128)(2,1)}, u32[]{:S(2)}, u32[]{:S(2)}) collective-permute-start(bf16[384,768]{1,0:T(8,128)(2,1)} %constant_dynamic-slice_fusion.9), channel_id=1, source_target_pairs={{0,16},{16,0},{1,17},{17,1},{2,18},{18,2},{3,19},{19,3},{4,20},{20... | collective-permute-start | bytes 1769480 | tf_op jit(solution)/shard_map/cond/branch_1_fun/ppermute | solution.py:27
  285.4 21.8 %collective-permute-start.9 = (bf16[128,768]{1,0:T(8,128)(2,1)}, bf16[128,768]{1,0:T(8,128)(2,1)}, u32[]{:S(2)}, u32[]{:S(2)}) collective-permute-start(bf16[128,768]{1,0:T(8,128)(2,1)} %constant_dynamic-slice_fusion.10), channel_id=1, source_target_pairs={{0,1},{1,0},{2,3},{3,2},{4,5},{5,4},{6,7},{7,6},{8,9},{9,8},{10,11... | collective-permute-start | bytes 589832 | tf_op jit(solution)/shard_map/cond/branch_1_fun/ppermute | solution.py:27
  299.8 8.5 %collective-permute-start.11 = (bf16[192,768]{1,0:T(8,128)(2,1)S(1)}, bf16[192,768]{1,0:T(8,128)(2,1)S(1)}, u32[]{:S(2)}, u32[]{:S(2)}) collective-permute-start(bf16[192,768]{1,0:T(8,128)(2,1)S(1)} %constant_dynamic-slice_fusion.8), channel_id=1, source_target_pairs={{0,2},{1,3},{2,0},{3,1},{4,6},{5,7},{6,4},{7,5},{8,10},{9,11},{10,... | collective-permute-start | bytes 884744 | tf_op jit(solution)/shard_map/cond/branch_1_fun/ppermute | solution.py:27
  300.0 8.4 %collective-permute-start.12 = (bf16[896,768]{1,0:T(8,128)(2,1)S(1)}, bf16[896,768]{1,0:T(8,128)(2,1)S(1)}, u32[]{:S(2)}, u32[]{:S(2)}) collective-permute-start(bf16[896,768]{1,0:T(8,128)(2,1)S(1)} %constant_dynamic-slice_fusion.7), channel_id=1, source_target_pairs={{0,1},{1,0},{2,3},{3,2},{4,5},{5,4},{6,7},{7,6},{8,9},{9,8},{10,11... | collective-permute-start | bytes 4128776 | tf_op jit(solution)/shard_map/cond/branch_1_fun/ppermute | solution.py:27
  308.8 20.3 %collective-permute-start.15 = (bf16[448,768]{1,0:T(8,128)(2,1)S(1)}, bf16[448,768]{1,0:T(8,128)(2,1)S(1)}, u32[]{:S(2)}, u32[]{:S(2)}) collective-permute-start(bf16[448,768]{1,0:T(8,128)(2,1)S(1)} %constant_dynamic-slice_fusion.4), channel_id=1, source_target_pairs={{0,16},{16,0},{1,17},{17,1},{2,18},{18,2},{3,19},{19,3},{4,20},{20... | collective-permute-start | bytes 2064392 | tf_op jit(solution)/shard_map/cond/branch_1_fun/ppermute | solution.py:27
  309.5 7.0 %collective-permute-start.13 = (bf16[64,768]{1,0:T(8,128)(2,1)S(1)}, bf16[64,768]{1,0:T(8,128)(2,1)S(1)}, u32[]{:S(2)}, u32[]{:S(2)}) collective-permute-start(bf16[64,768]{1,0:T(8,128)(2,1)S(1)} %constant_dynamic-slice_fusion.6), channel_id=1, source_target_pairs={{0,2},{1,3},{2,0},{3,1},{4,6},{5,7},{6,4},{7,5},{8,10},{9,11},{10,... | collective-permute-start | bytes 294920 | tf_op jit(solution)/shard_map/cond/branch_1_fun/ppermute | solution.py:27
  309.9 7.9 %collective-permute-start.14 = (bf16[96,768]{1,0:T(8,128)(2,1)S(1)}, bf16[96,768]{1,0:T(8,128)(2,1)S(1)}, u32[]{:S(2)}, u32[]{:S(2)}) collective-permute-start(bf16[96,768]{1,0:T(8,128)(2,1)S(1)} %constant_dynamic-slice_fusion.5), channel_id=1, source_target_pairs={{0,4},{1,5},{2,6},{3,7},{4,0},{5,1},{6,2},{7,3},{8,12},{9,13},{10,... | collective-permute-start | bytes 442376 | tf_op jit(solution)/shard_map/cond/branch_1_fun/ppermute | solution.py:27
  329.3 7.4 %collective-permute-start.17 = (bf16[48,768]{1,0:T(8,128)(2,1)S(1)}, bf16[48,768]{1,0:T(8,128)(2,1)S(1)}, u32[]{:S(2)}, u32[]{:S(2)}) collective-permute-start(bf16[48,768]{1,0:T(8,128)(2,1)S(1)} %constant_dynamic-slice_fusion.3), channel_id=1, source_target_pairs={{0,8},{1,9},{2,10},{3,11},{4,12},{5,13},{6,14},{7,15},{8,0},{9,1},... | collective-permute-start | bytes 221192 | tf_op jit(solution)/shard_map/cond/branch_1_fun/ppermute | solution.py:27
  331.7 7.6 %collective-permute-start.16 = (bf16[64,768]{1,0:T(8,128)(2,1)S(1)}, bf16[64,768]{1,0:T(8,128)(2,1)S(1)}, u32[]{:S(2)}, u32[]{:S(2)}) collective-permute-start(bf16[64,768]{1,0:T(8,128)(2,1)S(1)} %add_convert_fusion.13), channel_id=1, source_target_pairs={{0,4},{1,5},{2,6},{3,7},{4,0},{5,1},{6,2},{7,3},{8,12},{9,13},{10,... | collective-permute-start | bytes 294920 | tf_op jit(solution)/shard_map/cond/branch_1_fun/ppermute | solution.py:27
  333.2 17.8 %collective-permute-start.18 = (bf16[224,768]{1,0:T(8,128)(2,1)S(1)}, bf16[224,768]{1,0:T(8,128)(2,1)S(1)}, u32[]{:S(2)}, u32[]{:S(2)}) collective-permute-start(bf16[224,768]{1,0:T(8,128)(2,1)S(1)} %constant_dynamic-slice_fusion.2), channel_id=1, source_target_pairs={{0,2},{1,3},{2,0},{3,1},{4,6},{5,7},{6,4},{7,5},{8,10},{9,11},{10,... | collective-permute-start | bytes 1032200 | tf_op jit(solution)/shard_map/cond/branch_1_fun/ppermute | solution.py:27
  351.1 9.8 %collective-permute-start.20 = (bf16[48,768]{1,0:T(8,128)(2,1)S(1)}, bf16[48,768]{1,0:T(8,128)(2,1)S(1)}, u32[]{:S(2)}, u32[]{:S(2)}) collective-permute-start(bf16[48,768]{1,0:T(8,128)(2,1)S(1)} %add_convert_fusion.18), channel_id=1, source_target_pairs={{0,8},{1,9},{2,10},{3,11},{4,12},{5,13},{6,14},{7,15},{8,0},{9,1},... | collective-permute-start | bytes 221192 | tf_op jit(solution)/shard_map/cond/branch_1_fun/ppermute | solution.py:27
  351.3 13.8 %collective-permute-start.19 = (bf16[64,768]{1,0:T(8,128)(2,1)S(1)}, bf16[64,768]{1,0:T(8,128)(2,1)S(1)}, u32[]{:S(2)}, u32[]{:S(2)}) collective-permute-start(bf16[64,768]{1,0:T(8,128)(2,1)S(1)} %add_convert_fusion.12), channel_id=1, source_target_pairs={{0,8},{1,9},{2,10},{3,11},{4,12},{5,13},{6,14},{7,15},{8,0},{9,1},... | collective-permute-start | bytes 294920 | tf_op jit(solution)/shard_map/cond/branch_1_fun/ppermute | solution.py:27
  354.1 12.8 %collective-permute-start.21 = (bf16[112,768]{1,0:T(8,128)(2,1)S(1)}, bf16[112,768]{1,0:T(8,128)(2,1)S(1)}, u32[]{:S(2)}, u32[]{:S(2)}) collective-permute-start(bf16[112,768]{1,0:T(8,128)(2,1)S(1)} %constant_dynamic-slice_fusion.1), channel_id=1, source_target_pairs={{0,4},{1,5},{2,6},{3,7},{4,0},{5,1},{6,2},{7,3},{8,12},{9,13},{10,... | collective-permute-start | bytes 516104 | tf_op jit(solution)/shard_map/cond/branch_1_fun/ppermute | solution.py:27
  367.0 8.3 %collective-permute-start.24 = (bf16[56,768]{1,0:T(8,128)(2,1)S(1)}, bf16[56,768]{1,0:T(8,128)(2,1)S(1)}, u32[]{:S(2)}, u32[]{:S(2)}) collective-permute-start(bf16[56,768]{1,0:T(8,128)(2,1)S(1)} %constant_dynamic-slice_fusion), channel_id=1, source_target_pairs={{0,8},{1,9},{2,10},{3,11},{4,12},{5,13},{6,14},{7,15},{8,0},{9,1},... | collective-permute-start | bytes 258056 | tf_op jit(solution)/shard_map/cond/branch_1_fun/ppermute | solution.py:27
  369.9 5.4 %collective-permute-start.22 = (bf16[64,768]{1,0:T(8,128)(2,1)S(1)}, bf16[64,768]{1,0:T(8,128)(2,1)S(1)}, u32[]{:S(2)}, u32[]{:S(2)}) collective-permute-start(bf16[64,768]{1,0:T(8,128)(2,1)S(1)} %add_convert_fusion.11), channel_id=1, source_target_pairs={{0,2},{1,3},{2,0},{3,1},{4,6},{5,7},{6,4},{7,5},{8,10},{9,11},{10,... | collective-permute-start | bytes 294920 | tf_op jit(solution)/shard_map/cond/branch_1_fun/ppermute | solution.py:27
  371.8 8.9 %collective-permute-start.23 = (bf16[96,768]{1,0:T(8,128)(2,1)S(1)}, bf16[96,768]{1,0:T(8,128)(2,1)S(1)}, u32[]{:S(2)}, u32[]{:S(2)}) collective-permute-start(bf16[96,768]{1,0:T(8,128)(2,1)S(1)} %maximum_select_fusion.7), channel_id=1, source_target_pairs={{0,4},{1,5},{2,6},{3,7},{4,0},{5,1},{6,2},{7,3},{8,12},{9,13},{10,... | collective-permute-start | bytes 442376 | tf_op jit(solution)/shard_map/cond/branch_1_fun/ppermute | solution.py:27
  380.7 8.2 %collective-permute-start.27 = (bf16[56,768]{1,0:T(8,128)(2,1)S(1)}, bf16[56,768]{1,0:T(8,128)(2,1)S(1)}, u32[]{:S(2)}, u32[]{:S(2)}) collective-permute-start(bf16[56,768]{1,0:T(8,128)(2,1)S(1)} %add_convert_fusion.17), channel_id=1, source_target_pairs={{0,8},{1,9},{2,10},{3,11},{4,12},{5,13},{6,14},{7,15},{8,0},{9,1},... | collective-permute-start | bytes 258056 | tf_op jit(solution)/shard_map/cond/branch_1_fun/ppermute | solution.py:27
  382.5 7.1 %collective-permute-start.25 = (bf16[128,768]{1,0:T(8,128)(2,1)S(1)}, bf16[128,768]{1,0:T(8,128)(2,1)S(1)}, u32[]{:S(2)}, u32[]{:S(2)}) collective-permute-start(bf16[128,768]{1,0:T(8,128)(2,1)S(1)} %maximum_select_fusion.5), channel_id=1, source_target_pairs={{0,1},{1,0},{2,3},{3,2},{4,5},{5,4},{6,7},{7,6},{8,9},{9,8},{10,11... | collective-permute-start | bytes 589832 | tf_op jit(solution)/shard_map/cond/branch_1_fun/ppermute | solution.py:27
  382.5 9.4 %collective-permute-start.26 = (bf16[192,768]{1,0:T(8,128)(2,1)S(1)}, bf16[192,768]{1,0:T(8,128)(2,1)S(1)}, u32[]{:S(2)}, u32[]{:S(2)}) collective-permute-start(bf16[192,768]{1,0:T(8,128)(2,1)S(1)} %maximum_select_fusion.3), channel_id=1, source_target_pairs={{0,2},{1,3},{2,0},{3,1},{4,6},{5,7},{6,4},{7,5},{8,10},{9,11},{10,... | collective-permute-start | bytes 884744 | tf_op jit(solution)/shard_map/cond/branch_1_fun/ppermute | solution.py:27
  393.2 19.3 %copy-start.47 = (s32[1024]{0:T(1024)S(1)}, s32[1024]{0:T(1024)}, u32[]{:S(2)}) copy-start(s32[1024]{0:T(1024)} %copy-done.46) | copy-start | bytes 12292
  393.2 19.3 %copy-start.51 = (s32[256]{0:T(256)S(1)}, s32[256]{0:T(256)}, u32[]{:S(2)}) copy-start(s32[256]{0:T(256)} %copy-done.50) | copy-start | bytes 3076
  393.2 19.3 %copy-start.53 = (s32[256]{0:T(256)S(1)}, s32[256]{0:T(256)}, u32[]{:S(2)}) copy-start(s32[256]{0:T(256)} %copy-done.52) | copy-start | bytes 3076
  393.2 6.4 %collective-permute-start.43 = (bf16[112,768]{1,0:T(8,128)(2,1)}, bf16[112,768]{1,0:T(8,128)(2,1)S(1)}, u32[]{:S(2)}, u32[]{:S(2)}) collective-permute-start(bf16[112,768]{1,0:T(8,128)(2,1)} %get-tuple-element.202), channel_id=1, source_target_pairs={{0,4},{1,5},{2,6},{3,7},{4,0},{5,1},{6,2},{7,3},{8,12},{9,13},{10,... | collective-permute-start | bytes 516104 | tf_op jit(solution)/shard_map/ppermute | solution.py:27
  400.7 9.0 %collective-permute-start.44 = (bf16[224,768]{1,0:T(8,128)(2,1)S(1)}, bf16[224,768]{1,0:T(8,128)(2,1)S(1)}, u32[]{:S(2)}, u32[]{:S(2)}) collective-permute-start(bf16[224,768]{1,0:T(8,128)(2,1)S(1)} %maximum_select_fusion.13), channel_id=1, source_target_pairs={{0,2},{1,3},{2,0},{3,1},{4,6},{5,7},{6,4},{7,5},{8,10},{9,11},{10,... | collective-permute-start | bytes 1032200 | tf_op jit(solution)/shard_map/ppermute | solution.py:27
  402.1 16.5 %collective-permute-start.42 = (bf16[384,768]{1,0:T(8,128)(2,1)}, bf16[384,768]{1,0:T(8,128)(2,1)S(1)}, u32[]{:S(2)}, u32[]{:S(2)}) collective-permute-start(bf16[384,768]{1,0:T(8,128)(2,1)} %get-tuple-element.201), channel_id=1, source_target_pairs={{0,16},{16,0},{1,17},{17,1},{2,18},{18,2},{3,19},{19,3},{4,20},{20... | collective-permute-start | bytes 1769480 | tf_op jit(solution)/shard_map/ppermute | solution.py:27
  409.9 22.6 %collective-permute-start.45 = (bf16[448,768]{1,0:T(8,128)(2,1)S(1)}, bf16[448,768]{1,0:T(8,128)(2,1)}, u32[]{:S(2)}, u32[]{:S(2)}) collective-permute-start(bf16[448,768]{1,0:T(8,128)(2,1)S(1)} %maximum_select_fusion.10), channel_id=1, source_target_pairs={{0,16},{16,0},{1,17},{17,1},{2,18},{18,2},{3,19},{19,3},{4,20},{20... | collective-permute-start | bytes 2064392 | tf_op jit(solution)/shard_map/ppermute | solution.py:27
  420.1 17.1 %copy-start.11 = (bf16[768,768]{1,0:T(8,128)(2,1)}, bf16[768,768]{1,0:T(8,128)(2,1)S(1)}, u32[]{:S(2)}) copy-start(bf16[768,768]{1,0:T(8,128)(2,1)S(1)} %maximum_select_fusion.9.early_ref) | copy-start | bytes 3538948
  434.3 2.9 collective-permute-start.47
  434.4 4.8 %collective-permute-start.46 = (bf16[896,768]{1,0:T(8,128)(2,1)S(1)}, bf16[896,768]{1,0:T(8,128)(2,1)S(1)}, u32[]{:S(2)}, u32[]{:S(2)}) collective-permute-start(bf16[896,768]{1,0:T(8,128)(2,1)S(1)} %maximum_select_fusion.8.late_ref), channel_id=1, source_target_pairs={{0,1},{1,0},{2,3},{3,2},{4,5},{5,4},{6,7},{7,6},{8,9},{9,8},{10,11... | collective-permute-start | bytes 4128776 | tf_op jit(solution)/shard_map/ppermute | solution.py:27
  (61 other events, 293.7 us)
Sparse Core Ops, SparseCore 0:
  175.6 220.7 all-reduce.7

commit v13 on v12

--- a/solution.py
+++ b/solution.py
@@ -936,8 +936,9 @@
         early = lax.dynamic_update_slice_in_dim(
             early, weight_grad(grad_values).astype(BF), width, 0
         )
-        grad_mix, early = lax.optimization_barrier((grad_mix, early))
         early = advance(begin(early, ORDER, ORDER), 1)
+        grad_mix, (early,) = tied(grad_mix, [early])
+        early = advance(early, 1)
         grad_mq_small, grad_mk_small = pl.pallas_call(
             lambda *refs: pinv_back_kernel(scale, *refs),
             out_shape=(shaped(square, F32), shaped(square, F32)),
@@ -945,7 +946,6 @@
         )(own_q, own_k, kernel, saved, own_heads(grad_mix), own_heads(stats[:, :width]))
 
         grad_mq_small, (early,) = tied(grad_mq_small, [early])
-        early = advance(early, 1)
 
         def with_small(array, small):
             small = small.transpose(1, 0, 2).reshape(LAND, own_count * size)
@@ -992,7 +992,6 @@
         late = lax.dynamic_update_slice_in_dim(
             late, (weight_grad(grad_keys) + mark_grad_k).astype(BF), width + spare_rows, 0
         )
-        late, (early,) = tied(late, [early])
         late = begin(late, ORDER, ORDER)
         grad_projected = jnp.concatenate([grad_queries, grad_keys, grad_values], axis=1)
         grad_input = grad_one + lax.dot_general(

time: 466 us -> 460 us (0.987)
  local copies, waits for them, and re-layouts: 49.4 us -> 40 us
  starting transfers between devices: 67.2 us -> 58 us
  Pallas kernels: 109 us -> 114 us
    ppermute x44, starting transfers between devices: 60.1 us -> 52.8 us  [swap(): return lax.ppermute(array, axis, [(i, i ^ bit) for i in range(count)])]
  transfers between devices with their start and end apart: 49 -> 49, of which waited for: 29 -> 30; matrix products, arithmetic and copies ran while one was open for 23% -> 22% of each run, Pallas kernels for 7% -> 7%
where the time goes in v13:
time: 460 us; the launch traced here: 452 us
  waiting for transfers between devices  120 us (26%)
  Pallas kernels  114 us (25%)
  starting transfers between devices  58 us (13%)
  matrix products  53.6 us (12%)
  other arithmetic  50.6 us (11%)
  local copies, waits for them, and re-layouts  40 us (9%)
  between operations  15.1 us (3%)
    ppermute x44, waiting for transfers between devices, swap(): return lax.ppermute(array, axis, [(i, i ^ bit) for i in range(count)])  120 us
    ppermute x44, starting transfers between devices, swap(): return lax.ppermute(array, axis, [(i, i ^ bit) for i in range(count)])  52.8 us
    pallas_call x1, Pallas kernels, per_device(): pl.pallas_call(ffn_kernel, grid=(tok_count // FFN_BLOCK,), in_specs=[ffn_...  40.1 us
    dot_general x3, matrix products, weight_grad(): return lax.dot_general(tokens, grads, rows_in, preferred_element_type=F32)  10.8 us
    pallas_call x1, Pallas kernels, per_device(): pl.pallas_call(lambda *refs: token_kernel(docs, scale, *refs), grid=(bloc...  10.2 us
    pallas_call x1, Pallas kernels, remaining(): pl.pallas_call(lambda *refs: pinv_back_kernel(scale, *refs), out_shape=(s...  10.1 us
  transfers between devices with their start and end apart: 49, of which 30 were waited for; matrix products, arithmetic and copies ran while one was open for 22% of the time, Pallas kernels for 7%

profile of v13, /device:TPU:0, one launch (start us, length us, event | category | flops | bytes accessed | tf_op | source)
XLA Modules:
  0.0 452.3 jit_solution(14453269089453316405)
XLA Ops:
  10.9 2.2 fusion.31
  14.8 3.0 collective-permute-start.31
  17.7 3.1 collective-permute-done.31
  22.7 6.0 %add_convert_fusion.20.refs_2_.refs_3_.refs_1_ = bf16[1024,2304]{1,0:T(8,128)(2,1)S(1)} fusion(bf16[768,2304]{1,0:T(8,128)(2,1)} %param.21, f32[2304]{0:T(1024)S(1)} %pad_maximum_fusion.2, bf16[1,1024,768]{2,1,0:T(8,128)(2,1)S(1)} %copy-done.28), kind=kOutput, calls=%fused_computation.79 | convolution fusion | flops 3628597248 | bytes 9839616 | tf_op jit(solution)/shard_map/dot_general | solution.py:749
  28.8 2.7 collective-permute-start.33
  35.6 3.2 collective-permute-start.34
  38.8 3.3 collective-permute-done.34
  43.9 2.6 fusion.29
  46.7 5.9 %landmark.1 = bf16[256,896]{1,0:T(8,128)(2,1)S(1)} custom-call(s32[8]{0:T(128)S(1)} %add_subtract_fusion.refs_0_, bf16[256,768]{1,0:T(8,128)(2,1)S(1)} %fusion.33.refs_1_, bf16[1024,2304]{1,0:T(8,128)(2,1)S(1)} %bitcast.62, bf16[1024,2304]{1,0:T(8,128)(2,1)S(1)} %bitcast.62), custom_call_target="tpu_custom_call" | custom-call | tf_op jit(solution)/shard_map/landmark/pallas_call | solution.py:756
  55.4 2.0 join.4
  59.9 6.0 %pinv.1 = (f32[3,64,64]{2,1,0:T(8,128)}, f32[3,64,64]{2,1,0:T(8,128)}, f32[72,64,64]{2,1,0:T(8,128)}) custom-call(f32[3,64,64]{2,1,0:T(8,128)S(1)} %bitcast.71, f32[3,64,64]{2,1,0:T(8,128)S(1)} %bitcast.69), custom_call_target="tpu_custom_call" | custom-call | tf_op jit(solution)/shard_map/pinv/pallas_call | solution.py:789
  71.9 4.5 %collective-permute-done.38 = bf16[64,1088]{1,0:T(8,128)(2,1)S(1)} collective-permute-done((bf16[64,1088]{1,0:T(8,128)(2,1)S(1)}, bf16[64,1088]{1,0:T(8,128)(2,1)S(1)}, u32[]{:S(2)}, u32[]{:S(2)}) %collective-permute-start.38) | collective-permute-done | bytes 139296 | tf_op jit(solution)/shard_map/ppermute | solution.py:27
  80.1 3.1 collective-permute-start.39
  83.2 7.4 %collective-permute-done.39 = bf16[64,1280]{1,0:T(8,128)(2,1)S(1)} collective-permute-done((bf16[64,1280]{1,0:T(8,128)(2,1)S(1)}, bf16[64,1280]{1,0:T(8,128)(2,1)S(1)}, u32[]{:S(2)}, u32[]{:S(2)}) %collective-permute-start.39) | collective-permute-done | bytes 163872 | tf_op jit(solution)/shard_map/ppermute | solution.py:27
  94.0 4.4 collective-permute-done.40
  101.2 10.2 %token_.1 = (bf16[1024,768]{1,0:T(8,128)(2,1)}, bf16[768,1024]{1,0:T(8,128)(2,1)S(1)}) custom-call(s32[8]{0:T(128)S(1)} %add_subtract_fusion.refs_0_, bf16[1024,2304]{1,0:T(8,128)(2,1)} %copy-done.7, bf16[1152,768]{1,0:T(8,128)(2,1)S(1)} %copy-done.8, bf16[256,768]{1,0:T(8,128)(2,1)S(1)} %slice.187.refs_3_.refs_4_, ...), custom_call_target="tpu_custom_call" | custom-call | tf_op jit(solution)/shard_map/token/pallas_call | solution.py:817
  112.0 40.1 %ffn.1 = (f32[1024,768]{1,0:T(8,128)}, f32[1024,768]{1,0:T(8,128)}, bf16[1024,3072]{1,0:T(8,128)(2,1)}, bf16[1024,3072]{1,0:T(8,128)(2,1)}, bf16[1024,768]{1,0:T...) custom-call(bf16[1024,768]{1,0:T(8,128)(2,1)} %bitcast.67, ...), custom_call_target="tpu_custom_call" | custom-call | tf_op jit(solution)/shard_map/ffn/pallas_call | solution.py:839
  152.2 8.9 %token_back.1 = (bf16[1024,768]{1,0:T(8,128)(2,1)}, f32[256,768]{1,0:T(8,128)S(1)}, f32[256,768]{1,0:T(8,128)}) custom-call(s32[8]{0:T(128)S(1)} %add_subtract_fusion.refs_0_, bf16[1024,2304]{1,0:T(8,128)(2,1)} %copy-done.7, bf16[1024,768]{1,0:T(8,128)(2,1)} %get-tuple-element.181.refs_2_, bf16[768,1024]{1,0:T(8,128)(2,1)S(1)} %get-tuple-element.182.refs_3_, ...), custom_call_target="tpu_custom_call" | custom-call | tf_op jit(solution)/shard_map/token_back/pallas_call | solution.py:863
  161.2 6.9 %convolution_convert_fusion.3 = bf16[3072,768]{1,0:T(8,128)(2,1)} fusion(bf16[1024,3072]{1,0:T(8,128)(2,1)S(1)} %copy-done.66, bf16[1024,768]{1,0:T(8,128)(2,1)S(1)} %copy-done.69), kind=kOutput, calls=%fused_computation.81 | convolution fusion | flops 4834197504 | bytes 12582912 | tf_op jit(solution)/shard_map/dot_general | solution.py:879
  168.1 6.8 %convolution_convert_fusion.2 = bf16[768,3072]{1,0:T(8,128)(2,1)} fusion(bf16[1024,768]{1,0:T(8,128)(2,1)S(1)} %copy-done.68, bf16[1024,3072]{1,0:T(8,128)(2,1)S(1)} %bitcast.89), kind=kOutput, calls=%fused_computation.80 | convolution fusion | flops 4834197504 | bytes 12582912 | tf_op jit(solution)/shard_map/dot_general | solution.py:880
  175.6 211.5 %conditional.1 = (bf16[384,768]{1,0:T(8,128)(2,1)}, bf16[112,768]{1,0:T(8,128)(2,1)}, bf16[256,768]{1,0:T(8,128)(2,1)}, f32[1024,768]{1,0:T(8,128)}) conditional(s32[]{:T(128)} %bitcast.23, () %tuple.32, (bf16[256,768]{1,0:T(8,128)(2,1)S(1)}, bf16[1024,768]{1,0:T(8,128)(2,1)}, f32[12,33]{1,0:T(8,128)S(1)}, s32[8]{0:T(128)S(1)}, ...), branch_computations={%region_1.2_spmd, %region_2.6_spmd} | conditional | flops 9721349120 | bytes 271235040 | solution.py:1020
  177.4 4.8 %collective-permute-done.1 = bf16[64,768]{1,0:T(8,128)(2,1)S(1)} collective-permute-done((bf16[64,768]{1,0:T(8,128)(2,1)S(1)}, bf16[64,768]{1,0:T(8,128)(2,1)S(1)}, u32[]{:S(2)}, u32[]{:S(2)}) %collective-permute-start.1) | collective-permute-done | bytes 98336 | tf_op jit(solution)/shard_map/cond/branch_1_fun/ppermute | solution.py:27
  185.8 3.6 collective-permute-done.2
  189.4 6.0 %collective-permute-start.3 = (bf16[64,768]{1,0:T(8,128)(2,1)S(1)}, bf16[64,768]{1,0:T(8,128)(2,1)S(1)}, u32[]{:S(2)}, u32[]{:S(2)}) collective-permute-start(bf16[64,768]{1,0:T(8,128)(2,1)S(1)} %add_convert_fusion.15), channel_id=1, source_target_pairs={{0,8},{1,9},{2,10},{3,11},{4,12},{5,13},{6,14},{7,15},{8,0},{9,1},... | collective-permute-start | bytes 294920 | tf_op jit(solution)/shard_map/cond/branch_1_fun/ppermute | solution.py:27
  197.2 7.0 %conv_back.1 = (f32[1024,768]{1,0:T(8,128)S(1)}, f32[16,256]{1,0:T(8,128)S(1)}) custom-call(s32[8]{0:T(128)S(1)} %get-tuple-element.54.refs_0_, bf16[1152,768]{1,0:T(8,128)(2,1)S(1)} %maximum_maximum_fusion.refs_1_, bf16[1152,768]{1,0:T(8,128)(2,1)} %copy-done.9, f32[12,256]{1,0:T(8,128)S(1)} %pad.17.refs_3_), custom_call_target="tpu_custom_call" | custom-call | tf_op jit(solution)/shard_map/cond/branch_1_fun/conv_back/pallas_call | solution.py:891
  205.6 2.1 mix_back.1
  211.6 2.4 collective-permute-done.6
  215.2 3.5 convolution_convert_fusion.1
  218.9 8.5 %landmark_back.1 = (bf16[1024,768]{1,0:T(8,128)(2,1)S(1)}, bf16[1024,768]{1,0:T(8,128)(2,1)S(1)}, f32[256,768]{1,0:T(8,128)S(1)}) custom-call(s32[8]{0:T(128)S(1)} %get-tuple-element.54.refs_0_, bf16[1024,2304]{1,0:T(8,128)(2,1)S(1)} %bitcast.64, bf16[1024,2304]{1,0:T(8,128)(2,1)S(1)} %bitcast.64, f32[1024,768]{1,0:T(8,128)S(1)} %get-tuple-element.62.refs_3_, ...), custom_call_target="tpu_custom_call" | custom-call | tf_op jit(solution)/shard_map/cond/branch_1_fun/landmark_back/pallas_call | solution.py:915
  229.4 2.7 fusion.15
  234.7 5.0 %fusion.50 = f32[768,768]{1,0:T(8,128)} fusion(bf16[1024,768]{1,0:T(8,128)(2,1)} %get-tuple-element.78, bf16[1024,768]{1,0:T(8,128)(2,1)} %get-tuple-element.88), kind=kOutput, calls=%fused_computation.156 | convolution fusion | flops 1207959552 | bytes 5505024 | tf_op jit(solution)/shard_map/cond/branch_1_fun/dot_general | solution.py:933
  241.2 4.4 fusion.51
  245.7 3.0 add_convert_fusion.2
  249.7 3.6 collective-permute-start.9
  255.0 10.1 %pinv_back.1 = (f32[3,64,64]{2,1,0:T(8,128)}, f32[3,64,64]{2,1,0:T(8,128)}) custom-call(f32[3,64,64]{2,1,0:T(8,128)S(1)} %copy-done.37, f32[3,64,64]{2,1,0:T(8,128)S(1)} %copy-done.35, f32[3,64,64]{2,1,0:T(8,128)S(1)} %copy-done.43, f32[72,64,64]{2,1,0:T(8,128)} %get-tuple-element.74.refs_3_, bf16[3,64,64]{2,1,0:T(8,128)(2,1)} %bitcast.81, ...), custom_call_target="tpu_custom_call" | custom-call | tf_op jit(solution)/shard_map/cond/branch_1_fun/pinv_back/pallas_call | solution.py:942
  267.1 3.0 dynamic_update_slice.18
  272.1 3.2 fusion.14
  275.3 2.4 copy.46
  277.7 2.0 add_convert_fusion.4
  283.3 2.5 fusion.20
  293.8 6.7 %fusion.9 = f32[1024,768]{1,0:T(8,128)} fusion(f32[1024,768]{1,0:T(8,128)} %get-tuple-element.87, bf16[768,2304]{1,0:T(8,128)(2,1)S(1)} %copy-done.67, bf16[1024,768]{1,0:T(8,128)(2,1)S(1)} %copy-done.1, bf16[1024,768]{1,0:T(8,128)(2,1)S(1)} %copy-done.6, bf16[1024,768]{1,0:T(8,128)(2,1)S(1)} %copy-done.31), kind=kOutput, calls=%fused_computation.19 | convolution fusion | flops 3638820864 | bytes 14548992 | tf_op jit(solution)/shard_map/cond/branch_1_fun/dot_general | solution.py:997
  302.4 2.1 collective-permute-start.13
  304.5 5.3 %collective-permute-done.13 = bf16[64,768]{1,0:T(8,128)(2,1)S(1)} collective-permute-done((bf16[64,768]{1,0:T(8,128)(2,1)S(1)}, bf16[64,768]{1,0:T(8,128)(2,1)S(1)}, u32[]{:S(2)}, u32[]{:S(2)}) %collective-permute-start.13) | collective-permute-done | bytes 98336 | tf_op jit(solution)/shard_map/cond/branch_1_fun/ppermute | solution.py:27
  310.9 13.0 %collective-permute-done.15 = bf16[448,768]{1,0:T(8,128)(2,1)S(1)} collective-permute-done((bf16[448,768]{1,0:T(8,128)(2,1)S(1)}, bf16[448,768]{1,0:T(8,128)(2,1)S(1)}, u32[]{:S(2)}, u32[]{:S(2)}) %collective-permute-start.15) | collective-permute-done | bytes 688160 | tf_op jit(solution)/shard_map/cond/branch_1_fun/ppermute | solution.py:27
  325.1 2.5 collective-permute-start.16
  328.0 2.4 collective-permute-done.17
  332.5 12.1 %collective-permute-done.18 = bf16[224,768]{1,0:T(8,128)(2,1)S(1)} collective-permute-done((bf16[224,768]{1,0:T(8,128)(2,1)S(1)}, bf16[224,768]{1,0:T(8,128)(2,1)S(1)}, u32[]{:S(2)}, u32[]{:S(2)}) %collective-permute-start.18) | collective-permute-done | bytes 344096 | tf_op jit(solution)/shard_map/cond/branch_1_fun/ppermute | solution.py:27
  345.0 2.7 collective-permute-start.19
  347.8 5.6 %collective-permute-done.20 = bf16[48,768]{1,0:T(8,128)(2,1)S(1)} collective-permute-done((bf16[48,768]{1,0:T(8,128)(2,1)S(1)}, bf16[48,768]{1,0:T(8,128)(2,1)S(1)}, u32[]{:S(2)}, u32[]{:S(2)}) %collective-permute-start.20) | collective-permute-done | bytes 73760 | tf_op jit(solution)/shard_map/cond/branch_1_fun/ppermute | solution.py:27
  353.4 3.9 collective-permute-done.19
  357.3 2.9 collective-permute-done.21
  362.2 2.5 collective-permute-start.23
  364.7 3.1 collective-permute-done.24
  367.9 3.5 collective-permute-done.23
  371.5 5.0 %collective-permute-start.27 = (bf16[56,768]{1,0:T(8,128)(2,1)S(1)}, bf16[56,768]{1,0:T(8,128)(2,1)S(1)}, u32[]{:S(2)}, u32[]{:S(2)}) collective-permute-start(bf16[56,768]{1,0:T(8,128)(2,1)S(1)} %add_convert_fusion.17), channel_id=1, source_target_pairs={{0,8},{1,9},{2,10},{3,11},{4,12},{5,13},{6,14},{7,15},{8,0},{9,1},... | collective-permute-start | bytes 258056 | tf_op jit(solution)/shard_map/cond/branch_1_fun/ppermute | solution.py:27
  377.7 3.9 collective-permute-done.27
  383.2 2.8 collective-permute-done.26
  387.5 8.5 %collective-permute-done.43 = bf16[112,768]{1,0:T(8,128)(2,1)S(1)} collective-permute-done((bf16[112,768]{1,0:T(8,128)(2,1)}, bf16[112,768]{1,0:T(8,128)(2,1)S(1)}, u32[]{:S(2)}, u32[]{:S(2)}) %collective-permute-start.43) | collective-permute-done | bytes 172064 | tf_op jit(solution)/shard_map/ppermute | solution.py:27
  399.2 7.7 %collective-permute-done.44 = bf16[224,768]{1,0:T(8,128)(2,1)S(1)} collective-permute-done((bf16[224,768]{1,0:T(8,128)(2,1)S(1)}, bf16[224,768]{1,0:T(8,128)(2,1)S(1)}, u32[]{:S(2)}, u32[]{:S(2)}) %collective-permute-start.44) | collective-permute-done | bytes 344096 | tf_op jit(solution)/shard_map/ppermute | solution.py:27
  410.0 3.9 add.373
  415.6 7.3 %convert_element_type.348 = f32[3072,768]{1,0:T(8,128)} convert(bf16[3072,768]{1,0:T(8,128)(2,1)} %get-tuple-element.218) | non-fusion elementwise | flops 2359296 | bytes 14155776 | tf_op jit(solution)/shard_map/convert_element_type | solution.py:1027
  422.9 5.0 %convert_element_type.349 = f32[768,3072]{1,0:T(8,128)} convert(bf16[768,3072]{1,0:T(8,128)(2,1)S(1)} %copy-done.15) | non-fusion elementwise | flops 2359296 | bytes 14155776 | tf_op jit(solution)/shard_map/convert_element_type | solution.py:1027
  430.3 2.3 collective-permute-done.47.early_other_ref
  437.7 7.6 %settle_qkv.1 = f32[768,2304]{1,0:T(8,128)} custom-call(s32[1]{0:T(128)} %bitcast.25.side_ref, bf16[896,768]{1,0:T(8,128)(2,1)} %copy-done.13, bf16[896,768]{1,0:T(8,128)(2,1)} %copy-done.27, bf16[768,768]{1,0:T(8,128)(2,1)} %copy-done.10, bf16[768,768]{1,0:T(8,128)(2,1)} %copy-done.14), custom_call_target="tpu_custom_call" | custom-call | tf_op jit(solution)/shard_map/settle_qkv/pallas_call | solution.py:686
  (375 shorter events, 101.9 us)
Async XLA Ops:
  7.2 408.4 %all-reduce.8.cloned.1.call-start = ((), (), s32[]{:S(2)}) async-start(), calls=%async_computation | async-start | bytes 18874368 | tf_op jit(solution)/shard_map/psum | solution.py:884
  13.1 1.6 collective-permute-start.30
  14.8 6.0 %collective-permute-start.31 = (bf16[64,768]{1,0:T(8,128)(2,1)S(1)}, bf16[64,768]{1,0:T(8,128)(2,1)S(1)}, u32[]{:S(2)}, u32[]{:S(2)}) collective-permute-start(bf16[64,768]{1,0:T(8,128)(2,1)S(1)} %constant_dynamic-slice_fusion.19), channel_id=1, source_target_pairs={{0,2},{1,3},{2,0},{3,1},{4,6},{5,7},{6,4},{7,5},{8,10},{9,11},{10,... | collective-permute-start | bytes 294920 | tf_op jit(solution)/shard_map/ppermute | solution.py:27
  20.8 7.9 %collective-permute-start.32 = (bf16[64,768]{1,0:T(8,128)(2,1)S(1)}, bf16[64,768]{1,0:T(8,128)(2,1)S(1)}, u32[]{:S(2)}, u32[]{:S(2)}) collective-permute-start(bf16[64,768]{1,0:T(8,128)(2,1)S(1)} %add_convert_fusion.24), channel_id=1, source_target_pairs={{0,4},{1,5},{2,6},{3,7},{4,0},{5,1},{6,2},{7,3},{8,12},{9,13},{10,... | collective-permute-start | bytes 294920 | tf_op jit(solution)/shard_map/ppermute | solution.py:27
  28.8 6.8 %collective-permute-start.33 = (bf16[64,768]{1,0:T(8,128)(2,1)S(1)}, bf16[64,768]{1,0:T(8,128)(2,1)S(1)}, u32[]{:S(2)}, u32[]{:S(2)}) collective-permute-start(bf16[64,768]{1,0:T(8,128)(2,1)S(1)} %add_convert_fusion.23), channel_id=1, source_target_pairs={{0,8},{1,9},{2,10},{3,11},{4,12},{5,13},{6,14},{7,15},{8,0},{9,1},... | collective-permute-start | bytes 294920 | tf_op jit(solution)/shard_map/ppermute | solution.py:27
  31.5 10.8 %collective-permute-start.28 = (bf16[16,768]{1,0:T(8,128)(2,1)S(1)}, bf16[16,768]{1,0:T(8,128)(2,1)S(1)}, u32[]{:S(2)}, u32[]{:S(2)}) collective-permute-start(bf16[16,768]{1,0:T(8,128)(2,1)S(1)} %get-tuple-element.224), channel_id=1, source_target_pairs={{0,1},{1,2},{2,3},{3,4},{4,5},{5,6},{6,7},{7,8},{8,9},{9,10},{10,1... | collective-permute-start | bytes 73736 | tf_op jit(solution)/shard_map/ppermute | solution.py:154
  32.7 9.5 %collective-permute-start.29 = (bf16[16,768]{1,0:T(8,128)(2,1)S(1)}, bf16[16,768]{1,0:T(8,128)(2,1)S(1)}, u32[]{:S(2)}, u32[]{:S(2)}) collective-permute-start(bf16[16,768]{1,0:T(8,128)(2,1)S(1)} %get-tuple-element.225), channel_id=1, source_target_pairs={{1,0},{2,1},{3,2},{4,3},{5,4},{6,5},{7,6},{8,7},{9,8},{10,9},{11,1... | collective-permute-start | bytes 73736 | tf_op jit(solution)/shard_map/ppermute | solution.py:156
  35.6 6.5 %collective-permute-start.34 = (bf16[64,768]{1,0:T(8,128)(2,1)S(1)}, bf16[64,768]{1,0:T(8,128)(2,1)S(1)}, u32[]{:S(2)}, u32[]{:S(2)}) collective-permute-start(bf16[64,768]{1,0:T(8,128)(2,1)S(1)} %add_convert_fusion.22), channel_id=1, source_target_pairs={{0,2},{1,3},{2,0},{3,1},{4,6},{5,7},{6,4},{7,5},{8,10},{9,11},{10,... | collective-permute-start | bytes 294920 | tf_op jit(solution)/shard_map/ppermute | solution.py:27
  42.2 1.7 collective-permute-start.35
  53.3 1.5 collective-permute-start.36
  57.8 18.6 %copy-start.34 = (f32[64,3,64]{2,0,1:T(8,128)}, f32[64,3,64]{2,0,1:T(8,128)S(1)}, u32[]{:S(2)}) copy-start(f32[64,3,64]{2,0,1:T(8,128)S(1)} %copy.50) | copy-start | bytes 147460
  58.0 18.4 %copy-start.36 = (f32[64,3,64]{2,0,1:T(8,128)}, f32[64,3,64]{2,0,1:T(8,128)S(1)}, u32[]{:S(2)}) copy-start(f32[64,3,64]{2,0,1:T(8,128)S(1)} %copy.48) | copy-start | bytes 147460
  59.7 7.4 %collective-permute-start.37 = (bf16[64,896]{1,0:T(8,128)(2,1)S(1)}, bf16[64,896]{1,0:T(8,128)(2,1)S(1)}, u32[]{:S(2)}, u32[]{:S(2)}) collective-permute-start(bf16[64,896]{1,0:T(8,128)(2,1)S(1)} %get-tuple-element.228), channel_id=1, source_target_pairs={{0,2},{1,3},{2,0},{3,1},{4,6},{5,7},{6,4},{7,5},{8,10},{9,11},{10,... | collective-permute-start | bytes 344072 | tf_op jit(solution)/shard_map/ppermute | solution.py:27
  66.9 32.7 %copy-start.57 = (f32[768]{0:T(1024)S(1)}, f32[768]{0:T(1024)}, u32[]{:S(2)}) copy-start(f32[768]{0:T(1024)} %param.26) | copy-start | bytes 9220
  66.9 32.7 %copy-start.58 = (f32[768]{0:T(1024)S(1)}, f32[768]{0:T(1024)}, u32[]{:S(2)}) copy-start(f32[768]{0:T(1024)} %param.27) | copy-start | bytes 9220
  66.9 32.7 %copy-start.59 = (f32[768]{0:T(1024)S(1)}, f32[768]{0:T(1024)}, u32[]{:S(2)}) copy-start(f32[768]{0:T(1024)} %param.28) | copy-start | bytes 9220
  66.9 32.7 %copy-start.60 = (f32[768]{0:T(1024)S(1)}, f32[768]{0:T(1024)}, u32[]{:S(2)}) copy-start(f32[768]{0:T(1024)} %param.32) | copy-start | bytes 9220
  66.9 32.7 %copy-start.61 = (f32[768]{0:T(1024)S(1)}, f32[768]{0:T(1024)}, u32[]{:S(2)}) copy-start(f32[768]{0:T(1024)} %param.33) | copy-start | bytes 9220
  67.0 32.7 %copy-start.62 = (f32[768]{0:T(1024)S(1)}, f32[768]{0:T(1024)}, u32[]{:S(2)}) copy-start(f32[768]{0:T(1024)} %param.34) | copy-start | bytes 9220
  67.7 32.6 %copy-start.44 = (f32[12,33]{1,0:T(8,128)S(1)}, f32[12,33]{1,0:T(8,128)}, u32[]{:S(2)}) copy-start(f32[12,33]{1,0:T(8,128)} %param.24) | copy-start | bytes 4756
  70.5 5.9 %collective-permute-start.38 = (bf16[64,1088]{1,0:T(8,128)(2,1)S(1)}, bf16[64,1088]{1,0:T(8,128)(2,1)S(1)}, u32[]{:S(2)}, u32[]{:S(2)}) collective-permute-start(bf16[64,1088]{1,0:T(8,128)(2,1)S(1)} %pad_maximum_fusion.1), channel_id=1, source_target_pairs={{0,4},{1,5},{2,6},{3,7},{4,0},{5,1},{6,2},{7,3},{8,12},{9,13},{10,... | collective-permute-start | bytes 417800 | tf_op jit(solution)/shard_map/ppermute | solution.py:27
  77.1 24.1 %copy-start.8 = (bf16[1152,768]{1,0:T(8,128)(2,1)S(1)}, bf16[1152,768]{1,0:T(8,128)(2,1)}, u32[]{:S(2)}) copy-start(bf16[1152,768]{1,0:T(8,128)(2,1)} %maximum_maximum_fusion.1.refs_2_) | copy-start | bytes 5308420
  80.1 10.6 %collective-permute-start.39 = (bf16[64,1280]{1,0:T(8,128)(2,1)S(1)}, bf16[64,1280]{1,0:T(8,128)(2,1)S(1)}, u32[]{:S(2)}, u32[]{:S(2)}) collective-permute-start(bf16[64,1280]{1,0:T(8,128)(2,1)S(1)} %pad_maximum_fusion), channel_id=1, source_target_pairs={{0,8},{1,9},{2,10},{3,11},{4,12},{5,13},{6,14},{7,15},{8,0},{9,1},... | collective-permute-start | bytes 491528 | tf_op jit(solution)/shard_map/ppermute | solution.py:27
  93.5 5.0 %collective-permute-start.40 = (bf16[64,896]{1,0:T(8,128)(2,1)}, bf16[64,896]{1,0:T(8,128)(2,1)S(1)}, u32[]{:S(2)}, u32[]{:S(2)}) collective-permute-start(bf16[64,896]{1,0:T(8,128)(2,1)} %mix.1), channel_id=1, source_target_pairs={{0,2},{1,3},{2,0},{3,1},{4,6},{5,7},{6,4},{7,5},{8,10},{9,11},{10,... | collective-permute-start | bytes 344072 | tf_op jit(solution)/shard_map/ppermute | solution.py:27
  99.5 1.6 collective-permute-start.41
  175.6 21.6 %copy-start.9 = (bf16[1152,768]{1,0:T(8,128)(2,1)}, bf16[1152,768]{1,0:T(8,128)(2,1)S(1)}, u32[]{:S(2)}) copy-start(bf16[1152,768]{1,0:T(8,128)(2,1)S(1)} %get-tuple-element.58.refs_2_) | copy-start | bytes 5308420 | tf_op jit(solution)/shard_map/cond
  175.7 21.6 %copy-start.11 = (bf16[256,896]{1,0:T(8,128)(2,1)}, bf16[256,896]{1,0:T(8,128)(2,1)S(1)}, u32[]{:S(2)}) copy-start(bf16[256,896]{1,0:T(8,128)(2,1)S(1)} %get-tuple-element.67.refs_6_) | copy-start | bytes 1376260 | tf_op jit(solution)/shard_map/cond
  175.7 1.5 collective-permute-start
  177.3 4.9 %collective-permute-start.1 = (bf16[64,768]{1,0:T(8,128)(2,1)S(1)}, bf16[64,768]{1,0:T(8,128)(2,1)S(1)}, u32[]{:S(2)}, u32[]{:S(2)}) collective-permute-start(bf16[64,768]{1,0:T(8,128)(2,1)S(1)} %constant_dynamic-slice_fusion.13), channel_id=1, source_target_pairs={{0,2},{1,3},{2,0},{3,1},{4,6},{5,7},{6,4},{7,5},{8,10},{9,11},{10,... | collective-permute-start | bytes 294920 | tf_op jit(solution)/shard_map/cond/branch_1_fun/ppermute | solution.py:27
  182.2 7.2 %collective-permute-start.2 = (bf16[64,768]{1,0:T(8,128)(2,1)S(1)}, bf16[64,768]{1,0:T(8,128)(2,1)S(1)}, u32[]{:S(2)}, u32[]{:S(2)}) collective-permute-start(bf16[64,768]{1,0:T(8,128)(2,1)S(1)} %add_convert_fusion.16), channel_id=1, source_target_pairs={{0,4},{1,5},{2,6},{3,7},{4,0},{5,1},{6,2},{7,3},{8,12},{9,13},{10,... | collective-permute-start | bytes 294920 | tf_op jit(solution)/shard_map/cond/branch_1_fun/ppermute | solution.py:27
  183.1 12.3 %collective-permute-start.4 = (bf16[16,768]{1,0:T(8,128)(2,1)S(1)}, bf16[16,768]{1,0:T(8,128)(2,1)S(1)}, u32[]{:S(2)}, u32[]{:S(2)}) collective-permute-start(bf16[16,768]{1,0:T(8,128)(2,1)S(1)} %get-tuple-element.220), channel_id=1, source_target_pairs={{0,1},{1,2},{2,3},{3,4},{4,5},{5,6},{6,7},{7,8},{8,9},{9,10},{10,1... | collective-permute-start | bytes 73736 | tf_op jit(solution)/shard_map/cond/branch_1_fun/ppermute | solution.py:154
  184.4 11.0 %collective-permute-start.5 = (bf16[16,768]{1,0:T(8,128)(2,1)S(1)}, bf16[16,768]{1,0:T(8,128)(2,1)S(1)}, u32[]{:S(2)}, u32[]{:S(2)}) collective-permute-start(bf16[16,768]{1,0:T(8,128)(2,1)S(1)} %get-tuple-element.221), channel_id=1, source_target_pairs={{1,0},{2,1},{3,2},{4,3},{5,4},{6,5},{7,6},{8,7},{9,8},{10,9},{11,1... | collective-permute-start | bytes 73736 | tf_op jit(solution)/shard_map/cond/branch_1_fun/ppermute | solution.py:156
  189.4 15.5 %collective-permute-start.3 = (bf16[64,768]{1,0:T(8,128)(2,1)S(1)}, bf16[64,768]{1,0:T(8,128)(2,1)S(1)}, u32[]{:S(2)}, u32[]{:S(2)}) collective-permute-start(bf16[64,768]{1,0:T(8,128)(2,1)S(1)} %add_convert_fusion.15), channel_id=1, source_target_pairs={{0,8},{1,9},{2,10},{3,11},{4,12},{5,13},{6,14},{7,15},{8,0},{9,1},... | collective-permute-start | bytes 294920 | tf_op jit(solution)/shard_map/cond/branch_1_fun/ppermute | solution.py:27
  207.7 6.3 %collective-permute-start.6 = (bf16[64,896]{1,0:T(8,128)(2,1)}, bf16[64,896]{1,0:T(8,128)(2,1)}, u32[]{:S(2)}, u32[]{:S(2)}) collective-permute-start(bf16[64,896]{1,0:T(8,128)(2,1)} %mix_back.1), channel_id=1, source_target_pairs={{0,2},{1,3},{2,0},{3,1},{4,6},{5,7},{6,4},{7,5},{8,10},{9,11},{10,... | collective-permute-start | bytes 344072 | tf_op jit(solution)/shard_map/cond/branch_1_fun/ppermute | solution.py:27
  215.1 3.6 collective-permute-start.7
  232.1 13.6 %collective-permute-start.8 = (bf16[768,768]{1,0:T(8,128)(2,1)}, bf16[768,768]{1,0:T(8,128)(2,1)}, u32[]{:S(2)}, u32[]{:S(2)}) collective-permute-start(bf16[768,768]{1,0:T(8,128)(2,1)} %fusion.15), channel_id=1, source_target_pairs={{0,1},{1,0},{2,3},{3,2},{4,5},{5,4},{6,7},{7,6},{8,9},{9,8},{10,11... | collective-permute-start | bytes 3538952 | tf_op jit(solution)/shard_map/cond/branch_1_fun/ppermute | solution.py:27
  249.7 28.1 %collective-permute-start.9 = (bf16[384,768]{1,0:T(8,128)(2,1)}, bf16[384,768]{1,0:T(8,128)(2,1)}, u32[]{:S(2)}, u32[]{:S(2)}) collective-permute-start(bf16[384,768]{1,0:T(8,128)(2,1)} %constant_dynamic-slice_fusion.10), channel_id=1, source_target_pairs={{0,16},{16,0},{1,17},{17,1},{2,18},{18,2},{3,19},{19,3},{4,20},{20... | collective-permute-start | bytes 1769480 | tf_op jit(solution)/shard_map/cond/branch_1_fun/ppermute | solution.py:27
  286.6 13.8 %collective-permute-start.10 = (bf16[128,768]{1,0:T(8,128)(2,1)S(1)}, bf16[128,768]{1,0:T(8,128)(2,1)}, u32[]{:S(2)}, u32[]{:S(2)}) collective-permute-start(bf16[128,768]{1,0:T(8,128)(2,1)S(1)} %constant_dynamic-slice_fusion.9), channel_id=1, source_target_pairs={{0,1},{1,0},{2,3},{3,2},{4,5},{5,4},{6,7},{7,6},{8,9},{9,8},{10,11... | collective-permute-start | bytes 589832 | tf_op jit(solution)/shard_map/cond/branch_1_fun/ppermute | solution.py:27
  287.8 13.7 %collective-permute-start.11 = (bf16[192,768]{1,0:T(8,128)(2,1)}, bf16[192,768]{1,0:T(8,128)(2,1)S(1)}, u32[]{:S(2)}, u32[]{:S(2)}) collective-permute-start(bf16[192,768]{1,0:T(8,128)(2,1)} %constant_dynamic-slice_fusion.8), channel_id=1, source_target_pairs={{0,2},{1,3},{2,0},{3,1},{4,6},{5,7},{6,4},{7,5},{8,10},{9,11},{10,... | collective-permute-start | bytes 884744 | tf_op jit(solution)/shard_map/cond/branch_1_fun/ppermute | solution.py:27
  291.7 9.9 %collective-permute-start.12 = (bf16[896,768]{1,0:T(8,128)(2,1)S(1)}, bf16[896,768]{1,0:T(8,128)(2,1)S(1)}, u32[]{:S(2)}, u32[]{:S(2)}) collective-permute-start(bf16[896,768]{1,0:T(8,128)(2,1)S(1)} %constant_dynamic-slice_fusion.7), channel_id=1, source_target_pairs={{0,1},{1,0},{2,3},{3,2},{4,5},{5,4},{6,7},{7,6},{8,9},{9,8},{10,11... | collective-permute-start | bytes 4128776 | tf_op jit(solution)/shard_map/cond/branch_1_fun/ppermute | solution.py:27
  302.0 21.9 %collective-permute-start.15 = (bf16[448,768]{1,0:T(8,128)(2,1)S(1)}, bf16[448,768]{1,0:T(8,128)(2,1)S(1)}, u32[]{:S(2)}, u32[]{:S(2)}) collective-permute-start(bf16[448,768]{1,0:T(8,128)(2,1)S(1)} %constant_dynamic-slice_fusion.4), channel_id=1, source_target_pairs={{0,16},{16,0},{1,17},{17,1},{2,18},{18,2},{3,19},{19,3},{4,20},{20... | collective-permute-start | bytes 2064392 | tf_op jit(solution)/shard_map/cond/branch_1_fun/ppermute | solution.py:27
  302.4 7.4 %collective-permute-start.13 = (bf16[64,768]{1,0:T(8,128)(2,1)S(1)}, bf16[64,768]{1,0:T(8,128)(2,1)S(1)}, u32[]{:S(2)}, u32[]{:S(2)}) collective-permute-start(bf16[64,768]{1,0:T(8,128)(2,1)S(1)} %constant_dynamic-slice_fusion.6), channel_id=1, source_target_pairs={{0,2},{1,3},{2,0},{3,1},{4,6},{5,7},{6,4},{7,5},{8,10},{9,11},{10,... | collective-permute-start | bytes 294920 | tf_op jit(solution)/shard_map/cond/branch_1_fun/ppermute | solution.py:27
  304.5 6.4 %collective-permute-start.14 = (bf16[96,768]{1,0:T(8,128)(2,1)S(1)}, bf16[96,768]{1,0:T(8,128)(2,1)S(1)}, u32[]{:S(2)}, u32[]{:S(2)}) collective-permute-start(bf16[96,768]{1,0:T(8,128)(2,1)S(1)} %constant_dynamic-slice_fusion.5), channel_id=1, source_target_pairs={{0,4},{1,5},{2,6},{3,7},{4,0},{5,1},{6,2},{7,3},{8,12},{9,13},{10,... | collective-permute-start | bytes 442376 | tf_op jit(solution)/shard_map/cond/branch_1_fun/ppermute | solution.py:27
  324.1 6.4 %collective-permute-start.17 = (bf16[48,768]{1,0:T(8,128)(2,1)S(1)}, bf16[48,768]{1,0:T(8,128)(2,1)S(1)}, u32[]{:S(2)}, u32[]{:S(2)}) collective-permute-start(bf16[48,768]{1,0:T(8,128)(2,1)S(1)} %constant_dynamic-slice_fusion.3), channel_id=1, source_target_pairs={{0,8},{1,9},{2,10},{3,11},{4,12},{5,13},{6,14},{7,15},{8,0},{9,1},... | collective-permute-start | bytes 221192 | tf_op jit(solution)/shard_map/cond/branch_1_fun/ppermute | solution.py:27
  325.1 7.4 %collective-permute-start.16 = (bf16[64,768]{1,0:T(8,128)(2,1)S(1)}, bf16[64,768]{1,0:T(8,128)(2,1)S(1)}, u32[]{:S(2)}, u32[]{:S(2)}) collective-permute-start(bf16[64,768]{1,0:T(8,128)(2,1)S(1)} %add_convert_fusion.13), channel_id=1, source_target_pairs={{0,4},{1,5},{2,6},{3,7},{4,0},{5,1},{6,2},{7,3},{8,12},{9,13},{10,... | collective-permute-start | bytes 294920 | tf_op jit(solution)/shard_map/cond/branch_1_fun/ppermute | solution.py:27
  327.7 17.0 %collective-permute-start.18 = (bf16[224,768]{1,0:T(8,128)(2,1)S(1)}, bf16[224,768]{1,0:T(8,128)(2,1)S(1)}, u32[]{:S(2)}, u32[]{:S(2)}) collective-permute-start(bf16[224,768]{1,0:T(8,128)(2,1)S(1)} %constant_dynamic-slice_fusion.2), channel_id=1, source_target_pairs={{0,2},{1,3},{2,0},{3,1},{4,6},{5,7},{6,4},{7,5},{8,10},{9,11},{10,... | collective-permute-start | bytes 1032200 | tf_op jit(solution)/shard_map/cond/branch_1_fun/ppermute | solution.py:27
  344.7 8.7 %collective-permute-start.20 = (bf16[48,768]{1,0:T(8,128)(2,1)S(1)}, bf16[48,768]{1,0:T(8,128)(2,1)S(1)}, u32[]{:S(2)}, u32[]{:S(2)}) collective-permute-start(bf16[48,768]{1,0:T(8,128)(2,1)S(1)} %add_convert_fusion.18), channel_id=1, source_target_pairs={{0,8},{1,9},{2,10},{3,11},{4,12},{5,13},{6,14},{7,15},{8,0},{9,1},... | collective-permute-start | bytes 221192 | tf_op jit(solution)/shard_map/cond/branch_1_fun/ppermute | solution.py:27
  345.0 12.3 %collective-permute-start.19 = (bf16[64,768]{1,0:T(8,128)(2,1)S(1)}, bf16[64,768]{1,0:T(8,128)(2,1)S(1)}, u32[]{:S(2)}, u32[]{:S(2)}) collective-permute-start(bf16[64,768]{1,0:T(8,128)(2,1)S(1)} %add_convert_fusion.12), channel_id=1, source_target_pairs={{0,8},{1,9},{2,10},{3,11},{4,12},{5,13},{6,14},{7,15},{8,0},{9,1},... | collective-permute-start | bytes 294920 | tf_op jit(solution)/shard_map/cond/branch_1_fun/ppermute | solution.py:27
  347.7 12.5 %collective-permute-start.21 = (bf16[112,768]{1,0:T(8,128)(2,1)S(1)}, bf16[112,768]{1,0:T(8,128)(2,1)S(1)}, u32[]{:S(2)}, u32[]{:S(2)}) collective-permute-start(bf16[112,768]{1,0:T(8,128)(2,1)S(1)} %constant_dynamic-slice_fusion.1), channel_id=1, source_target_pairs={{0,4},{1,5},{2,6},{3,7},{4,0},{5,1},{6,2},{7,3},{8,12},{9,13},{10,... | collective-permute-start | bytes 516104 | tf_op jit(solution)/shard_map/cond/branch_1_fun/ppermute | solution.py:27
  360.3 7.5 %collective-permute-start.24 = (bf16[56,768]{1,0:T(8,128)(2,1)S(1)}, bf16[56,768]{1,0:T(8,128)(2,1)S(1)}, u32[]{:S(2)}, u32[]{:S(2)}) collective-permute-start(bf16[56,768]{1,0:T(8,128)(2,1)S(1)} %constant_dynamic-slice_fusion), channel_id=1, source_target_pairs={{0,8},{1,9},{2,10},{3,11},{4,12},{5,13},{6,14},{7,15},{8,0},{9,1},... | collective-permute-start | bytes 258056 | tf_op jit(solution)/shard_map/cond/branch_1_fun/ppermute | solution.py:27
  361.5 6.3 %collective-permute-start.22 = (bf16[64,768]{1,0:T(8,128)(2,1)S(1)}, bf16[64,768]{1,0:T(8,128)(2,1)S(1)}, u32[]{:S(2)}, u32[]{:S(2)}) collective-permute-start(bf16[64,768]{1,0:T(8,128)(2,1)S(1)} %add_convert_fusion.11), channel_id=1, source_target_pairs={{0,2},{1,3},{2,0},{3,1},{4,6},{5,7},{6,4},{7,5},{8,10},{9,11},{10,... | collective-permute-start | bytes 294920 | tf_op jit(solution)/shard_map/cond/branch_1_fun/ppermute | solution.py:27
  362.2 9.2 %collective-permute-start.23 = (bf16[96,768]{1,0:T(8,128)(2,1)S(1)}, bf16[96,768]{1,0:T(8,128)(2,1)S(1)}, u32[]{:S(2)}, u32[]{:S(2)}) collective-permute-start(bf16[96,768]{1,0:T(8,128)(2,1)S(1)} %maximum_select_fusion.7), channel_id=1, source_target_pairs={{0,4},{1,5},{2,6},{3,7},{4,0},{5,1},{6,2},{7,3},{8,12},{9,13},{10,... | collective-permute-start | bytes 442376 | tf_op jit(solution)/shard_map/cond/branch_1_fun/ppermute | solution.py:27
  371.5 10.1 %collective-permute-start.27 = (bf16[56,768]{1,0:T(8,128)(2,1)S(1)}, bf16[56,768]{1,0:T(8,128)(2,1)S(1)}, u32[]{:S(2)}, u32[]{:S(2)}) collective-permute-start(bf16[56,768]{1,0:T(8,128)(2,1)S(1)} %add_convert_fusion.17), channel_id=1, source_target_pairs={{0,8},{1,9},{2,10},{3,11},{4,12},{5,13},{6,14},{7,15},{8,0},{9,1},... | collective-permute-start | bytes 258056 | tf_op jit(solution)/shard_map/cond/branch_1_fun/ppermute | solution.py:27
  376.5 5.8 %collective-permute-start.25 = (bf16[128,768]{1,0:T(8,128)(2,1)S(1)}, bf16[128,768]{1,0:T(8,128)(2,1)S(1)}, u32[]{:S(2)}, u32[]{:S(2)}) collective-permute-start(bf16[128,768]{1,0:T(8,128)(2,1)S(1)} %maximum_select_fusion.5), channel_id=1, source_target_pairs={{0,1},{1,0},{2,3},{3,2},{4,5},{5,4},{6,7},{7,6},{8,9},{9,8},{10,11... | collective-permute-start | bytes 589832 | tf_op jit(solution)/shard_map/cond/branch_1_fun/ppermute | solution.py:27
  376.5 9.4 %collective-permute-start.26 = (bf16[192,768]{1,0:T(8,128)(2,1)S(1)}, bf16[192,768]{1,0:T(8,128)(2,1)S(1)}, u32[]{:S(2)}, u32[]{:S(2)}) collective-permute-start(bf16[192,768]{1,0:T(8,128)(2,1)S(1)} %maximum_select_fusion.3), channel_id=1, source_target_pairs={{0,2},{1,3},{2,0},{3,1},{4,6},{5,7},{6,4},{7,5},{8,10},{9,11},{10,... | collective-permute-start | bytes 884744 | tf_op jit(solution)/shard_map/cond/branch_1_fun/ppermute | solution.py:27
  387.1 21.0 %copy-start.49 = (s32[1024]{0:T(1024)S(1)}, s32[1024]{0:T(1024)}, u32[]{:S(2)}) copy-start(s32[1024]{0:T(1024)} %copy-done.48) | copy-start | bytes 12292
  387.1 20.9 %copy-start.53 = (s32[256]{0:T(256)S(1)}, s32[256]{0:T(256)}, u32[]{:S(2)}) copy-start(s32[256]{0:T(256)} %copy-done.52) | copy-start | bytes 3076
  387.1 20.9 %copy-start.55 = (s32[256]{0:T(256)S(1)}, s32[256]{0:T(256)}, u32[]{:S(2)}) copy-start(s32[256]{0:T(256)} %copy-done.54) | copy-start | bytes 3076
  387.2 8.8 %collective-permute-start.43 = (bf16[112,768]{1,0:T(8,128)(2,1)}, bf16[112,768]{1,0:T(8,128)(2,1)S(1)}, u32[]{:S(2)}, u32[]{:S(2)}) collective-permute-start(bf16[112,768]{1,0:T(8,128)(2,1)} %get-tuple-element.200), channel_id=1, source_target_pairs={{0,4},{1,5},{2,6},{3,7},{4,0},{5,1},{6,2},{7,3},{8,12},{9,13},{10,... | collective-permute-start | bytes 516104 | tf_op jit(solution)/shard_map/ppermute | solution.py:27
  397.1 9.8 %collective-permute-start.44 = (bf16[224,768]{1,0:T(8,128)(2,1)S(1)}, bf16[224,768]{1,0:T(8,128)(2,1)S(1)}, u32[]{:S(2)}, u32[]{:S(2)}) collective-permute-start(bf16[224,768]{1,0:T(8,128)(2,1)S(1)} %maximum_select_fusion.13), channel_id=1, source_target_pairs={{0,2},{1,3},{2,0},{3,1},{4,6},{5,7},{6,4},{7,5},{8,10},{9,11},{10,... | collective-permute-start | bytes 1032200 | tf_op jit(solution)/shard_map/ppermute | solution.py:27
  397.3 16.6 %collective-permute-start.42 = (bf16[384,768]{1,0:T(8,128)(2,1)}, bf16[384,768]{1,0:T(8,128)(2,1)S(1)}, u32[]{:S(2)}, u32[]{:S(2)}) collective-permute-start(bf16[384,768]{1,0:T(8,128)(2,1)} %get-tuple-element.199), channel_id=1, source_target_pairs={{0,16},{16,0},{1,17},{17,1},{2,18},{18,2},{3,19},{19,3},{4,20},{20... | collective-permute-start | bytes 1769480 | tf_op jit(solution)/shard_map/ppermute | solution.py:27
  407.1 20.8 %collective-permute-start.45 = (bf16[448,768]{1,0:T(8,128)(2,1)S(1)}, bf16[448,768]{1,0:T(8,128)(2,1)}, u32[]{:S(2)}, u32[]{:S(2)}) collective-permute-start(bf16[448,768]{1,0:T(8,128)(2,1)S(1)} %maximum_select_fusion.10), channel_id=1, source_target_pairs={{0,16},{16,0},{1,17},{17,1},{2,18},{18,2},{3,19},{19,3},{4,20},{20... | collective-permute-start | bytes 2064392 | tf_op jit(solution)/shard_map/ppermute | solution.py:27
  429.7 2.9 collective-permute-start.47
  429.8 4.8 %collective-permute-start.46 = (bf16[896,768]{1,0:T(8,128)(2,1)S(1)}, bf16[896,768]{1,0:T(8,128)(2,1)S(1)}, u32[]{:S(2)}, u32[]{:S(2)}) collective-permute-start(bf16[896,768]{1,0:T(8,128)(2,1)S(1)} %maximum_select_fusion.8.late_ref), channel_id=1, source_target_pairs={{0,1},{1,0},{2,3},{3,2},{4,5},{5,4},{6,7},{7,6},{8,9},{9,8},{10,11... | collective-permute-start | bytes 4128776 | tf_op jit(solution)/shard_map/ppermute | solution.py:27
  (63 other events, 320.5 us)
Sparse Core Ops, SparseCore 0:
  175.1 220.7 all-reduce.7

commit v14 on v13

--- a/solution.py
+++ b/solution.py
@@ -564,10 +564,11 @@
 
 
 def gelu_both(upper):
-    tangent = jnp.tanh(0.7978845608028654 * (upper + 0.044715 * upper * upper * upper))
-    inner_slope = 0.7978845608028654 * (1.0 + 3.0 * 0.044715 * upper * upper)
-    active = 0.5 * upper * (1.0 + tangent)
-    slope = 0.5 * (1.0 + tangent) + 0.5 * upper * (1.0 - tangent * tangent) * inner_slope
+    cubic = (0.7978845608028654 * 0.044715) * upper * upper
+    tangent = jnp.tanh(upper * (0.7978845608028654 + cubic))
+    gate = 0.5 + 0.5 * tangent
+    active = upper * gate
+    slope = gate + active * (1.0 - tangent) * (0.7978845608028654 + 3.0 * cubic)
     return active, slope
 
 

time: 460 us -> 461 us (level)
  transfers between devices with their start and end apart: 49 -> 49, of which waited for: 30 -> 31; matrix products, arithmetic and copies ran while one was open for 22% -> 22% of each run, Pallas kernels for 7% -> 7%
where the time goes in v14:
time: 461 us; the launch traced here: 453 us
  waiting for transfers between devices  118 us (26%)
  Pallas kernels  113 us (25%)
  starting transfers between devices  62.4 us (14%)
  matrix products  53.7 us (12%)
  other arithmetic  50.6 us (11%)
  local copies, waits for them, and re-layouts  40 us (9%)
  between operations  15.1 us (3%)
    ppermute x44, waiting for transfers between devices, swap(): return lax.ppermute(array, axis, [(i, i ^ bit) for i in range(count)])  118 us
    ppermute x44, starting transfers between devices, swap(): return lax.ppermute(array, axis, [(i, i ^ bit) for i in range(count)])  57.2 us
    pallas_call x1, Pallas kernels, per_device(): pl.pallas_call(ffn_kernel, grid=(tok_count // FFN_BLOCK,), in_specs=[ffn_...  38.5 us
    dot_general x3, matrix products, weight_grad(): return lax.dot_general(tokens, grads, rows_in, preferred_element_type=F32)  10.8 us
    pallas_call x1, Pallas kernels, per_device(): pl.pallas_call(lambda *refs: token_kernel(docs, scale, *refs), grid=(bloc...  10.2 us
    pallas_call x1, Pallas kernels, remaining(): pl.pallas_call(lambda *refs: pinv_back_kernel(scale, *refs), out_shape=(s...  10 us
  transfers between devices with their start and end apart: 49, of which 31 were waited for; matrix products, arithmetic and copies ran while one was open for 22% of the time, Pallas kernels for 7%

profile of v14, /device:TPU:0, one launch (start us, length us, event | category | flops | bytes accessed | tf_op | source)
XLA Modules:
  0.0 453.2 jit_solution(10223773047499020285)
XLA Ops:
  10.9 2.2 fusion.31
  14.8 3.0 collective-permute-start.31
  17.7 3.1 collective-permute-done.31
  22.7 6.0 %add_convert_fusion.20.refs_2_.refs_3_.refs_1_ = bf16[1024,2304]{1,0:T(8,128)(2,1)S(1)} fusion(bf16[768,2304]{1,0:T(8,128)(2,1)} %param.21, f32[2304]{0:T(1024)S(1)} %pad_maximum_fusion.2, bf16[1,1024,768]{2,1,0:T(8,128)(2,1)S(1)} %copy-done.28), kind=kOutput, calls=%fused_computation.79 | convolution fusion | flops 3628597248 | bytes 9839616 | tf_op jit(solution)/shard_map/dot_general | solution.py:750
  28.8 2.7 collective-permute-start.33
  35.6 3.2 collective-permute-start.34
  38.8 3.3 collective-permute-done.34
  43.9 2.6 fusion.29
  46.7 5.9 %landmark.1 = bf16[256,896]{1,0:T(8,128)(2,1)S(1)} custom-call(s32[8]{0:T(128)S(1)} %add_subtract_fusion.refs_0_, bf16[256,768]{1,0:T(8,128)(2,1)S(1)} %fusion.33.refs_1_, bf16[1024,2304]{1,0:T(8,128)(2,1)S(1)} %bitcast.62, bf16[1024,2304]{1,0:T(8,128)(2,1)S(1)} %bitcast.62), custom_call_target="tpu_custom_call" | custom-call | tf_op jit(solution)/shard_map/landmark/pallas_call | solution.py:757
  55.4 2.0 join.4
  59.9 6.0 %pinv.1 = (f32[3,64,64]{2,1,0:T(8,128)}, f32[3,64,64]{2,1,0:T(8,128)}, f32[72,64,64]{2,1,0:T(8,128)}) custom-call(f32[3,64,64]{2,1,0:T(8,128)S(1)} %bitcast.71, f32[3,64,64]{2,1,0:T(8,128)S(1)} %bitcast.69), custom_call_target="tpu_custom_call" | custom-call | tf_op jit(solution)/shard_map/pinv/pallas_call | solution.py:790
  71.9 4.5 %collective-permute-done.38 = bf16[64,1088]{1,0:T(8,128)(2,1)S(1)} collective-permute-done((bf16[64,1088]{1,0:T(8,128)(2,1)S(1)}, bf16[64,1088]{1,0:T(8,128)(2,1)S(1)}, u32[]{:S(2)}, u32[]{:S(2)}) %collective-permute-start.38) | collective-permute-done | bytes 139296 | tf_op jit(solution)/shard_map/ppermute | solution.py:27
  80.1 3.1 collective-permute-start.39
  83.2 7.4 %collective-permute-done.39 = bf16[64,1280]{1,0:T(8,128)(2,1)S(1)} collective-permute-done((bf16[64,1280]{1,0:T(8,128)(2,1)S(1)}, bf16[64,1280]{1,0:T(8,128)(2,1)S(1)}, u32[]{:S(2)}, u32[]{:S(2)}) %collective-permute-start.39) | collective-permute-done | bytes 163872 | tf_op jit(solution)/shard_map/ppermute | solution.py:27
  94.0 4.4 collective-permute-done.40
  101.2 10.2 %token_.1 = (bf16[1024,768]{1,0:T(8,128)(2,1)}, bf16[768,1024]{1,0:T(8,128)(2,1)S(1)}) custom-call(s32[8]{0:T(128)S(1)} %add_subtract_fusion.refs_0_, bf16[1024,2304]{1,0:T(8,128)(2,1)} %copy-done.7, bf16[1152,768]{1,0:T(8,128)(2,1)S(1)} %copy-done.8, bf16[256,768]{1,0:T(8,128)(2,1)S(1)} %slice.187.refs_3_.refs_4_, ...), custom_call_target="tpu_custom_call" | custom-call | tf_op jit(solution)/shard_map/token/pallas_call | solution.py:818
  112.0 38.5 %ffn.1 = (f32[1024,768]{1,0:T(8,128)}, f32[1024,768]{1,0:T(8,128)}, bf16[1024,3072]{1,0:T(8,128)(2,1)}, bf16[1024,3072]{1,0:T(8,128)(2,1)}, bf16[1024,768]{1,0:T...) custom-call(bf16[1024,768]{1,0:T(8,128)(2,1)} %bitcast.67, ...), custom_call_target="tpu_custom_call" | custom-call | tf_op jit(solution)/shard_map/ffn/pallas_call | solution.py:840
  150.5 8.9 %token_back.1 = (bf16[1024,768]{1,0:T(8,128)(2,1)}, f32[256,768]{1,0:T(8,128)S(1)}, f32[256,768]{1,0:T(8,128)}) custom-call(s32[8]{0:T(128)S(1)} %add_subtract_fusion.refs_0_, bf16[1024,2304]{1,0:T(8,128)(2,1)} %copy-done.7, bf16[1024,768]{1,0:T(8,128)(2,1)} %get-tuple-element.181.refs_2_, bf16[768,1024]{1,0:T(8,128)(2,1)S(1)} %get-tuple-element.182.refs_3_, ...), custom_call_target="tpu_custom_call" | custom-call | tf_op jit(solution)/shard_map/token_back/pallas_call | solution.py:864
  159.6 6.9 %convolution_convert_fusion.3 = bf16[3072,768]{1,0:T(8,128)(2,1)} fusion(bf16[1024,3072]{1,0:T(8,128)(2,1)S(1)} %copy-done.66, bf16[1024,768]{1,0:T(8,128)(2,1)S(1)} %copy-done.69), kind=kOutput, calls=%fused_computation.81 | convolution fusion | flops 4834197504 | bytes 12582912 | tf_op jit(solution)/shard_map/dot_general | solution.py:880
  166.5 6.8 %convolution_convert_fusion.2 = bf16[768,3072]{1,0:T(8,128)(2,1)} fusion(bf16[1024,768]{1,0:T(8,128)(2,1)S(1)} %copy-done.68, bf16[1024,3072]{1,0:T(8,128)(2,1)S(1)} %bitcast.89), kind=kOutput, calls=%fused_computation.80 | convolution fusion | flops 4834197504 | bytes 12582912 | tf_op jit(solution)/shard_map/dot_general | solution.py:881
  174.0 213.7 %conditional.1 = (bf16[384,768]{1,0:T(8,128)(2,1)}, bf16[112,768]{1,0:T(8,128)(2,1)}, bf16[256,768]{1,0:T(8,128)(2,1)}, f32[1024,768]{1,0:T(8,128)}) conditional(s32[]{:T(128)} %bitcast.23, () %tuple.32, (bf16[256,768]{1,0:T(8,128)(2,1)S(1)}, bf16[1024,768]{1,0:T(8,128)(2,1)}, f32[12,33]{1,0:T(8,128)S(1)}, s32[8]{0:T(128)S(1)}, ...), branch_computations={%region_1.2_spmd, %region_2.6_spmd} | conditional | flops 9721349120 | bytes 271235040 | solution.py:1021
  175.8 4.8 %collective-permute-done.1 = bf16[64,768]{1,0:T(8,128)(2,1)S(1)} collective-permute-done((bf16[64,768]{1,0:T(8,128)(2,1)S(1)}, bf16[64,768]{1,0:T(8,128)(2,1)S(1)}, u32[]{:S(2)}, u32[]{:S(2)}) %collective-permute-start.1) | collective-permute-done | bytes 98336 | tf_op jit(solution)/shard_map/cond/branch_1_fun/ppermute | solution.py:27
  184.2 3.1 collective-permute-done.2
  187.3 5.8 %collective-permute-start.3 = (bf16[64,768]{1,0:T(8,128)(2,1)S(1)}, bf16[64,768]{1,0:T(8,128)(2,1)S(1)}, u32[]{:S(2)}, u32[]{:S(2)}) collective-permute-start(bf16[64,768]{1,0:T(8,128)(2,1)S(1)} %add_convert_fusion.15), channel_id=1, source_target_pairs={{0,8},{1,9},{2,10},{3,11},{4,12},{5,13},{6,14},{7,15},{8,0},{9,1},... | collective-permute-start | bytes 294920 | tf_op jit(solution)/shard_map/cond/branch_1_fun/ppermute | solution.py:27
  194.9 7.0 %conv_back.1 = (f32[1024,768]{1,0:T(8,128)S(1)}, f32[16,256]{1,0:T(8,128)S(1)}) custom-call(s32[8]{0:T(128)S(1)} %get-tuple-element.54.refs_0_, bf16[1152,768]{1,0:T(8,128)(2,1)S(1)} %maximum_maximum_fusion.refs_1_, bf16[1152,768]{1,0:T(8,128)(2,1)} %copy-done.9, f32[12,256]{1,0:T(8,128)S(1)} %pad.17.refs_3_), custom_call_target="tpu_custom_call" | custom-call | tf_op jit(solution)/shard_map/cond/branch_1_fun/conv_back/pallas_call | solution.py:892
  203.3 2.1 mix_back.1
  208.6 4.0 collective-permute-done.6
  213.9 3.5 convolution_convert_fusion.1
  217.6 8.5 %landmark_back.1 = (bf16[1024,768]{1,0:T(8,128)(2,1)S(1)}, bf16[1024,768]{1,0:T(8,128)(2,1)S(1)}, f32[256,768]{1,0:T(8,128)S(1)}) custom-call(s32[8]{0:T(128)S(1)} %get-tuple-element.54.refs_0_, bf16[1024,2304]{1,0:T(8,128)(2,1)S(1)} %bitcast.64, bf16[1024,2304]{1,0:T(8,128)(2,1)S(1)} %bitcast.64, f32[1024,768]{1,0:T(8,128)S(1)} %get-tuple-element.62.refs_3_, ...), custom_call_target="tpu_custom_call" | custom-call | tf_op jit(solution)/shard_map/cond/branch_1_fun/landmark_back/pallas_call | solution.py:916
  228.1 2.7 fusion.15
  233.3 5.0 %fusion.50 = f32[768,768]{1,0:T(8,128)} fusion(bf16[1024,768]{1,0:T(8,128)(2,1)} %get-tuple-element.78, bf16[1024,768]{1,0:T(8,128)(2,1)} %get-tuple-element.88), kind=kOutput, calls=%fused_computation.156 | convolution fusion | flops 1207959552 | bytes 5505024 | tf_op jit(solution)/shard_map/cond/branch_1_fun/dot_general | solution.py:934
  239.9 4.4 fusion.51
  244.3 3.0 add_convert_fusion.2
  248.3 8.7 %collective-permute-start.9 = (bf16[384,768]{1,0:T(8,128)(2,1)}, bf16[384,768]{1,0:T(8,128)(2,1)}, u32[]{:S(2)}, u32[]{:S(2)}) collective-permute-start(bf16[384,768]{1,0:T(8,128)(2,1)} %constant_dynamic-slice_fusion.10), channel_id=1, source_target_pairs={{0,16},{16,0},{1,17},{17,1},{2,18},{18,2},{3,19},{19,3},{4,20},{20... | collective-permute-start | bytes 1769480 | tf_op jit(solution)/shard_map/cond/branch_1_fun/ppermute | solution.py:27
  258.7 10.0 %pinv_back.1 = (f32[3,64,64]{2,1,0:T(8,128)}, f32[3,64,64]{2,1,0:T(8,128)}) custom-call(f32[3,64,64]{2,1,0:T(8,128)S(1)} %copy-done.37, f32[3,64,64]{2,1,0:T(8,128)S(1)} %copy-done.35, f32[3,64,64]{2,1,0:T(8,128)S(1)} %copy-done.43, f32[72,64,64]{2,1,0:T(8,128)} %get-tuple-element.74.refs_3_, bf16[3,64,64]{2,1,0:T(8,128)(2,1)} %bitcast.81, ...), custom_call_target="tpu_custom_call" | custom-call | tf_op jit(solution)/shard_map/cond/branch_1_fun/pinv_back/pallas_call | solution.py:943
  270.9 3.0 dynamic_update_slice.18
  275.8 3.2 fusion.14
  279.0 2.4 copy.46
  287.0 2.5 fusion.20
  297.5 6.7 %fusion.9 = f32[1024,768]{1,0:T(8,128)} fusion(f32[1024,768]{1,0:T(8,128)} %get-tuple-element.87, bf16[768,2304]{1,0:T(8,128)(2,1)S(1)} %copy-done.67, bf16[1024,768]{1,0:T(8,128)(2,1)S(1)} %copy-done.1, bf16[1024,768]{1,0:T(8,128)(2,1)S(1)} %copy-done.6, bf16[1024,768]{1,0:T(8,128)(2,1)S(1)} %copy-done.31), kind=kOutput, calls=%fused_computation.19 | convolution fusion | flops 3638820864 | bytes 14548992 | tf_op jit(solution)/shard_map/cond/branch_1_fun/dot_general | solution.py:998
  306.0 2.1 collective-permute-start.13
  308.2 2.8 collective-permute-done.13
  311.0 4.1 collective-permute-done.14
  315.2 8.6 %collective-permute-done.15 = bf16[448,768]{1,0:T(8,128)(2,1)S(1)} collective-permute-done((bf16[448,768]{1,0:T(8,128)(2,1)S(1)}, bf16[448,768]{1,0:T(8,128)(2,1)S(1)}, u32[]{:S(2)}, u32[]{:S(2)}) %collective-permute-start.15) | collective-permute-done | bytes 688160 | tf_op jit(solution)/shard_map/cond/branch_1_fun/ppermute | solution.py:27
  324.0 2.5 collective-permute-start.17
  330.4 3.3 collective-permute-done.16
  333.7 10.9 %collective-permute-done.18 = bf16[224,768]{1,0:T(8,128)(2,1)S(1)} collective-permute-done((bf16[224,768]{1,0:T(8,128)(2,1)S(1)}, bf16[224,768]{1,0:T(8,128)(2,1)S(1)}, u32[]{:S(2)}, u32[]{:S(2)}) %collective-permute-start.18) | collective-permute-done | bytes 344096 | tf_op jit(solution)/shard_map/cond/branch_1_fun/ppermute | solution.py:27
  345.0 2.7 collective-permute-start.19
  348.6 5.3 %collective-permute-done.20 = bf16[48,768]{1,0:T(8,128)(2,1)S(1)} collective-permute-done((bf16[48,768]{1,0:T(8,128)(2,1)S(1)}, bf16[48,768]{1,0:T(8,128)(2,1)S(1)}, u32[]{:S(2)}, u32[]{:S(2)}) %collective-permute-start.20) | collective-permute-done | bytes 73760 | tf_op jit(solution)/shard_map/cond/branch_1_fun/ppermute | solution.py:27
  353.9 4.2 collective-permute-done.19
  360.1 3.3 collective-permute-start.24
  365.0 3.4 collective-permute-done.24
  368.4 5.0 %collective-permute-done.23 = bf16[96,768]{1,0:T(8,128)(2,1)S(1)} collective-permute-done((bf16[96,768]{1,0:T(8,128)(2,1)S(1)}, bf16[96,768]{1,0:T(8,128)(2,1)S(1)}, u32[]{:S(2)}, u32[]{:S(2)}) %collective-permute-start.23) | collective-permute-done | bytes 147488 | tf_op jit(solution)/shard_map/cond/branch_1_fun/ppermute | solution.py:27
  373.5 2.7 collective-permute-start.27
  376.1 2.8 collective-permute-start.26
  378.9 2.4 collective-permute-done.27
  382.9 3.7 collective-permute-done.26
  387.9 8.5 %collective-permute-done.43 = bf16[112,768]{1,0:T(8,128)(2,1)S(1)} collective-permute-done((bf16[112,768]{1,0:T(8,128)(2,1)}, bf16[112,768]{1,0:T(8,128)(2,1)S(1)}, u32[]{:S(2)}, u32[]{:S(2)}) %collective-permute-start.43) | collective-permute-done | bytes 172064 | tf_op jit(solution)/shard_map/ppermute | solution.py:27
  398.8 8.5 %collective-permute-done.44 = bf16[224,768]{1,0:T(8,128)(2,1)S(1)} collective-permute-done((bf16[224,768]{1,0:T(8,128)(2,1)S(1)}, bf16[224,768]{1,0:T(8,128)(2,1)S(1)}, u32[]{:S(2)}, u32[]{:S(2)}) %collective-permute-start.44) | collective-permute-done | bytes 344096 | tf_op jit(solution)/shard_map/ppermute | solution.py:27
  409.9 3.9 add.373
  416.5 7.3 %convert_element_type.348 = f32[3072,768]{1,0:T(8,128)} convert(bf16[3072,768]{1,0:T(8,128)(2,1)} %get-tuple-element.218) | non-fusion elementwise | flops 2359296 | bytes 14155776 | tf_op jit(solution)/shard_map/convert_element_type | solution.py:1028
  423.8 5.0 %convert_element_type.349 = f32[768,3072]{1,0:T(8,128)} convert(bf16[768,3072]{1,0:T(8,128)(2,1)S(1)} %copy-done.15) | non-fusion elementwise | flops 2359296 | bytes 14155776 | tf_op jit(solution)/shard_map/convert_element_type | solution.py:1028
  431.2 2.3 collective-permute-done.47.early_other_ref
  438.6 7.6 %settle_qkv.1 = f32[768,2304]{1,0:T(8,128)} custom-call(s32[1]{0:T(128)} %bitcast.25.side_ref, bf16[896,768]{1,0:T(8,128)(2,1)} %copy-done.13, bf16[896,768]{1,0:T(8,128)(2,1)} %copy-done.27, bf16[768,768]{1,0:T(8,128)(2,1)} %copy-done.10, bf16[768,768]{1,0:T(8,128)(2,1)} %copy-done.14), custom_call_target="tpu_custom_call" | custom-call | tf_op jit(solution)/shard_map/settle_qkv/pallas_call | solution.py:687
  (375 shorter events, 103.3 us)
Async XLA Ops:
  7.2 409.3 %all-reduce.8.cloned.1.call-start = ((), (), s32[]{:S(2)}) async-start(), calls=%async_computation | async-start | bytes 18874368 | tf_op jit(solution)/shard_map/psum | solution.py:885
  13.1 1.6 collective-permute-start.30
  14.8 6.0 %collective-permute-start.31 = (bf16[64,768]{1,0:T(8,128)(2,1)S(1)}, bf16[64,768]{1,0:T(8,128)(2,1)S(1)}, u32[]{:S(2)}, u32[]{:S(2)}) collective-permute-start(bf16[64,768]{1,0:T(8,128)(2,1)S(1)} %constant_dynamic-slice_fusion.19), channel_id=1, source_target_pairs={{0,2},{1,3},{2,0},{3,1},{4,6},{5,7},{6,4},{7,5},{8,10},{9,11},{10,... | collective-permute-start | bytes 294920 | tf_op jit(solution)/shard_map/ppermute | solution.py:27
  20.8 7.9 %collective-permute-start.32 = (bf16[64,768]{1,0:T(8,128)(2,1)S(1)}, bf16[64,768]{1,0:T(8,128)(2,1)S(1)}, u32[]{:S(2)}, u32[]{:S(2)}) collective-permute-start(bf16[64,768]{1,0:T(8,128)(2,1)S(1)} %add_convert_fusion.24), channel_id=1, source_target_pairs={{0,4},{1,5},{2,6},{3,7},{4,0},{5,1},{6,2},{7,3},{8,12},{9,13},{10,... | collective-permute-start | bytes 294920 | tf_op jit(solution)/shard_map/ppermute | solution.py:27
  28.8 6.8 %collective-permute-start.33 = (bf16[64,768]{1,0:T(8,128)(2,1)S(1)}, bf16[64,768]{1,0:T(8,128)(2,1)S(1)}, u32[]{:S(2)}, u32[]{:S(2)}) collective-permute-start(bf16[64,768]{1,0:T(8,128)(2,1)S(1)} %add_convert_fusion.23), channel_id=1, source_target_pairs={{0,8},{1,9},{2,10},{3,11},{4,12},{5,13},{6,14},{7,15},{8,0},{9,1},... | collective-permute-start | bytes 294920 | tf_op jit(solution)/shard_map/ppermute | solution.py:27
  31.5 10.8 %collective-permute-start.28 = (bf16[16,768]{1,0:T(8,128)(2,1)S(1)}, bf16[16,768]{1,0:T(8,128)(2,1)S(1)}, u32[]{:S(2)}, u32[]{:S(2)}) collective-permute-start(bf16[16,768]{1,0:T(8,128)(2,1)S(1)} %get-tuple-element.224), channel_id=1, source_target_pairs={{0,1},{1,2},{2,3},{3,4},{4,5},{5,6},{6,7},{7,8},{8,9},{9,10},{10,1... | collective-permute-start | bytes 73736 | tf_op jit(solution)/shard_map/ppermute | solution.py:154
  32.7 9.5 %collective-permute-start.29 = (bf16[16,768]{1,0:T(8,128)(2,1)S(1)}, bf16[16,768]{1,0:T(8,128)(2,1)S(1)}, u32[]{:S(2)}, u32[]{:S(2)}) collective-permute-start(bf16[16,768]{1,0:T(8,128)(2,1)S(1)} %get-tuple-element.225), channel_id=1, source_target_pairs={{1,0},{2,1},{3,2},{4,3},{5,4},{6,5},{7,6},{8,7},{9,8},{10,9},{11,1... | collective-permute-start | bytes 73736 | tf_op jit(solution)/shard_map/ppermute | solution.py:156
  35.6 6.5 %collective-permute-start.34 = (bf16[64,768]{1,0:T(8,128)(2,1)S(1)}, bf16[64,768]{1,0:T(8,128)(2,1)S(1)}, u32[]{:S(2)}, u32[]{:S(2)}) collective-permute-start(bf16[64,768]{1,0:T(8,128)(2,1)S(1)} %add_convert_fusion.22), channel_id=1, source_target_pairs={{0,2},{1,3},{2,0},{3,1},{4,6},{5,7},{6,4},{7,5},{8,10},{9,11},{10,... | collective-permute-start | bytes 294920 | tf_op jit(solution)/shard_map/ppermute | solution.py:27
  42.2 1.7 collective-permute-start.35
  53.3 1.5 collective-permute-start.36
  57.8 18.6 %copy-start.34 = (f32[64,3,64]{2,0,1:T(8,128)}, f32[64,3,64]{2,0,1:T(8,128)S(1)}, u32[]{:S(2)}) copy-start(f32[64,3,64]{2,0,1:T(8,128)S(1)} %copy.50) | copy-start | bytes 147460
  58.0 18.4 %copy-start.36 = (f32[64,3,64]{2,0,1:T(8,128)}, f32[64,3,64]{2,0,1:T(8,128)S(1)}, u32[]{:S(2)}) copy-start(f32[64,3,64]{2,0,1:T(8,128)S(1)} %copy.48) | copy-start | bytes 147460
  59.7 7.4 %collective-permute-start.37 = (bf16[64,896]{1,0:T(8,128)(2,1)S(1)}, bf16[64,896]{1,0:T(8,128)(2,1)S(1)}, u32[]{:S(2)}, u32[]{:S(2)}) collective-permute-start(bf16[64,896]{1,0:T(8,128)(2,1)S(1)} %get-tuple-element.228), channel_id=1, source_target_pairs={{0,2},{1,3},{2,0},{3,1},{4,6},{5,7},{6,4},{7,5},{8,10},{9,11},{10,... | collective-permute-start | bytes 344072 | tf_op jit(solution)/shard_map/ppermute | solution.py:27
  66.9 32.7 %copy-start.57 = (f32[768]{0:T(1024)S(1)}, f32[768]{0:T(1024)}, u32[]{:S(2)}) copy-start(f32[768]{0:T(1024)} %param.26) | copy-start | bytes 9220
  66.9 32.7 %copy-start.58 = (f32[768]{0:T(1024)S(1)}, f32[768]{0:T(1024)}, u32[]{:S(2)}) copy-start(f32[768]{0:T(1024)} %param.27) | copy-start | bytes 9220
  66.9 32.7 %copy-start.59 = (f32[768]{0:T(1024)S(1)}, f32[768]{0:T(1024)}, u32[]{:S(2)}) copy-start(f32[768]{0:T(1024)} %param.28) | copy-start | bytes 9220
  66.9 32.7 %copy-start.60 = (f32[768]{0:T(1024)S(1)}, f32[768]{0:T(1024)}, u32[]{:S(2)}) copy-start(f32[768]{0:T(1024)} %param.32) | copy-start | bytes 9220
  66.9 32.7 %copy-start.61 = (f32[768]{0:T(1024)S(1)}, f32[768]{0:T(1024)}, u32[]{:S(2)}) copy-start(f32[768]{0:T(1024)} %param.33) | copy-start | bytes 9220
  67.0 32.7 %copy-start.62 = (f32[768]{0:T(1024)S(1)}, f32[768]{0:T(1024)}, u32[]{:S(2)}) copy-start(f32[768]{0:T(1024)} %param.34) | copy-start | bytes 9220
  67.7 32.6 %copy-start.44 = (f32[12,33]{1,0:T(8,128)S(1)}, f32[12,33]{1,0:T(8,128)}, u32[]{:S(2)}) copy-start(f32[12,33]{1,0:T(8,128)} %param.24) | copy-start | bytes 4756
  70.5 5.9 %collective-permute-start.38 = (bf16[64,1088]{1,0:T(8,128)(2,1)S(1)}, bf16[64,1088]{1,0:T(8,128)(2,1)S(1)}, u32[]{:S(2)}, u32[]{:S(2)}) collective-permute-start(bf16[64,1088]{1,0:T(8,128)(2,1)S(1)} %pad_maximum_fusion.1), channel_id=1, source_target_pairs={{0,4},{1,5},{2,6},{3,7},{4,0},{5,1},{6,2},{7,3},{8,12},{9,13},{10,... | collective-permute-start | bytes 417800 | tf_op jit(solution)/shard_map/ppermute | solution.py:27
  77.1 24.1 %copy-start.8 = (bf16[1152,768]{1,0:T(8,128)(2,1)S(1)}, bf16[1152,768]{1,0:T(8,128)(2,1)}, u32[]{:S(2)}) copy-start(bf16[1152,768]{1,0:T(8,128)(2,1)} %maximum_maximum_fusion.1.refs_2_) | copy-start | bytes 5308420
  80.1 10.6 %collective-permute-start.39 = (bf16[64,1280]{1,0:T(8,128)(2,1)S(1)}, bf16[64,1280]{1,0:T(8,128)(2,1)S(1)}, u32[]{:S(2)}, u32[]{:S(2)}) collective-permute-start(bf16[64,1280]{1,0:T(8,128)(2,1)S(1)} %pad_maximum_fusion), channel_id=1, source_target_pairs={{0,8},{1,9},{2,10},{3,11},{4,12},{5,13},{6,14},{7,15},{8,0},{9,1},... | collective-permute-start | bytes 491528 | tf_op jit(solution)/shard_map/ppermute | solution.py:27
  93.5 5.0 %collective-permute-start.40 = (bf16[64,896]{1,0:T(8,128)(2,1)}, bf16[64,896]{1,0:T(8,128)(2,1)S(1)}, u32[]{:S(2)}, u32[]{:S(2)}) collective-permute-start(bf16[64,896]{1,0:T(8,128)(2,1)} %mix.1), channel_id=1, source_target_pairs={{0,2},{1,3},{2,0},{3,1},{4,6},{5,7},{6,4},{7,5},{8,10},{9,11},{10,... | collective-permute-start | bytes 344072 | tf_op jit(solution)/shard_map/ppermute | solution.py:27
  99.5 1.6 collective-permute-start.41
  174.0 20.9 %copy-start.9 = (bf16[1152,768]{1,0:T(8,128)(2,1)}, bf16[1152,768]{1,0:T(8,128)(2,1)S(1)}, u32[]{:S(2)}) copy-start(bf16[1152,768]{1,0:T(8,128)(2,1)S(1)} %get-tuple-element.58.refs_2_) | copy-start | bytes 5308420 | tf_op jit(solution)/shard_map/cond
  174.0 20.9 %copy-start.11 = (bf16[256,896]{1,0:T(8,128)(2,1)}, bf16[256,896]{1,0:T(8,128)(2,1)S(1)}, u32[]{:S(2)}) copy-start(bf16[256,896]{1,0:T(8,128)(2,1)S(1)} %get-tuple-element.67.refs_6_) | copy-start | bytes 1376260 | tf_op jit(solution)/shard_map/cond
  174.1 1.5 collective-permute-start
  175.7 4.9 %collective-permute-start.1 = (bf16[64,768]{1,0:T(8,128)(2,1)S(1)}, bf16[64,768]{1,0:T(8,128)(2,1)S(1)}, u32[]{:S(2)}, u32[]{:S(2)}) collective-permute-start(bf16[64,768]{1,0:T(8,128)(2,1)S(1)} %constant_dynamic-slice_fusion.13), channel_id=1, source_target_pairs={{0,2},{1,3},{2,0},{3,1},{4,6},{5,7},{6,4},{7,5},{8,10},{9,11},{10,... | collective-permute-start | bytes 294920 | tf_op jit(solution)/shard_map/cond/branch_1_fun/ppermute | solution.py:27
  180.6 6.7 %collective-permute-start.2 = (bf16[64,768]{1,0:T(8,128)(2,1)S(1)}, bf16[64,768]{1,0:T(8,128)(2,1)S(1)}, u32[]{:S(2)}, u32[]{:S(2)}) collective-permute-start(bf16[64,768]{1,0:T(8,128)(2,1)S(1)} %add_convert_fusion.16), channel_id=1, source_target_pairs={{0,4},{1,5},{2,6},{3,7},{4,0},{5,1},{6,2},{7,3},{8,12},{9,13},{10,... | collective-permute-start | bytes 294920 | tf_op jit(solution)/shard_map/cond/branch_1_fun/ppermute | solution.py:27
  181.4 11.7 %collective-permute-start.4 = (bf16[16,768]{1,0:T(8,128)(2,1)S(1)}, bf16[16,768]{1,0:T(8,128)(2,1)S(1)}, u32[]{:S(2)}, u32[]{:S(2)}) collective-permute-start(bf16[16,768]{1,0:T(8,128)(2,1)S(1)} %get-tuple-element.220), channel_id=1, source_target_pairs={{0,1},{1,2},{2,3},{3,4},{4,5},{5,6},{6,7},{7,8},{8,9},{9,10},{10,1... | collective-permute-start | bytes 73736 | tf_op jit(solution)/shard_map/cond/branch_1_fun/ppermute | solution.py:154
  182.7 10.4 %collective-permute-start.5 = (bf16[16,768]{1,0:T(8,128)(2,1)S(1)}, bf16[16,768]{1,0:T(8,128)(2,1)S(1)}, u32[]{:S(2)}, u32[]{:S(2)}) collective-permute-start(bf16[16,768]{1,0:T(8,128)(2,1)S(1)} %get-tuple-element.221), channel_id=1, source_target_pairs={{1,0},{2,1},{3,2},{4,3},{5,4},{6,5},{7,6},{8,7},{9,8},{10,9},{11,1... | collective-permute-start | bytes 73736 | tf_op jit(solution)/shard_map/cond/branch_1_fun/ppermute | solution.py:156
  187.3 15.3 %collective-permute-start.3 = (bf16[64,768]{1,0:T(8,128)(2,1)S(1)}, bf16[64,768]{1,0:T(8,128)(2,1)S(1)}, u32[]{:S(2)}, u32[]{:S(2)}) collective-permute-start(bf16[64,768]{1,0:T(8,128)(2,1)S(1)} %add_convert_fusion.15), channel_id=1, source_target_pairs={{0,8},{1,9},{2,10},{3,11},{4,12},{5,13},{6,14},{7,15},{8,0},{9,1},... | collective-permute-start | bytes 294920 | tf_op jit(solution)/shard_map/cond/branch_1_fun/ppermute | solution.py:27
  205.4 7.2 %collective-permute-start.6 = (bf16[64,896]{1,0:T(8,128)(2,1)}, bf16[64,896]{1,0:T(8,128)(2,1)}, u32[]{:S(2)}, u32[]{:S(2)}) collective-permute-start(bf16[64,896]{1,0:T(8,128)(2,1)} %mix_back.1), channel_id=1, source_target_pairs={{0,2},{1,3},{2,0},{3,1},{4,6},{5,7},{6,4},{7,5},{8,10},{9,11},{10,... | collective-permute-start | bytes 344072 | tf_op jit(solution)/shard_map/cond/branch_1_fun/ppermute | solution.py:27
  213.7 3.6 collective-permute-start.7
  230.7 13.6 %collective-permute-start.8 = (bf16[768,768]{1,0:T(8,128)(2,1)}, bf16[768,768]{1,0:T(8,128)(2,1)}, u32[]{:S(2)}, u32[]{:S(2)}) collective-permute-start(bf16[768,768]{1,0:T(8,128)(2,1)} %fusion.15), channel_id=1, source_target_pairs={{0,1},{1,0},{2,3},{3,2},{4,5},{5,4},{6,7},{7,6},{8,9},{9,8},{10,11... | collective-permute-start | bytes 3538952 | tf_op jit(solution)/shard_map/cond/branch_1_fun/ppermute | solution.py:27
  248.3 33.1 %collective-permute-start.9 = (bf16[384,768]{1,0:T(8,128)(2,1)}, bf16[384,768]{1,0:T(8,128)(2,1)}, u32[]{:S(2)}, u32[]{:S(2)}) collective-permute-start(bf16[384,768]{1,0:T(8,128)(2,1)} %constant_dynamic-slice_fusion.10), channel_id=1, source_target_pairs={{0,16},{16,0},{1,17},{17,1},{2,18},{18,2},{3,19},{19,3},{4,20},{20... | collective-permute-start | bytes 1769480 | tf_op jit(solution)/shard_map/cond/branch_1_fun/ppermute | solution.py:27
  290.4 13.8 %collective-permute-start.10 = (bf16[128,768]{1,0:T(8,128)(2,1)S(1)}, bf16[128,768]{1,0:T(8,128)(2,1)}, u32[]{:S(2)}, u32[]{:S(2)}) collective-permute-start(bf16[128,768]{1,0:T(8,128)(2,1)S(1)} %constant_dynamic-slice_fusion.9), channel_id=1, source_target_pairs={{0,1},{1,0},{2,3},{3,2},{4,5},{5,4},{6,7},{7,6},{8,9},{9,8},{10,11... | collective-permute-start | bytes 589832 | tf_op jit(solution)/shard_map/cond/branch_1_fun/ppermute | solution.py:27
  291.5 13.7 %collective-permute-start.11 = (bf16[192,768]{1,0:T(8,128)(2,1)}, bf16[192,768]{1,0:T(8,128)(2,1)S(1)}, u32[]{:S(2)}, u32[]{:S(2)}) collective-permute-start(bf16[192,768]{1,0:T(8,128)(2,1)} %constant_dynamic-slice_fusion.8), channel_id=1, source_target_pairs={{0,2},{1,3},{2,0},{3,1},{4,6},{5,7},{6,4},{7,5},{8,10},{9,11},{10,... | collective-permute-start | bytes 884744 | tf_op jit(solution)/shard_map/cond/branch_1_fun/ppermute | solution.py:27
  295.4 9.9 %collective-permute-start.12 = (bf16[896,768]{1,0:T(8,128)(2,1)S(1)}, bf16[896,768]{1,0:T(8,128)(2,1)S(1)}, u32[]{:S(2)}, u32[]{:S(2)}) collective-permute-start(bf16[896,768]{1,0:T(8,128)(2,1)S(1)} %constant_dynamic-slice_fusion.7), channel_id=1, source_target_pairs={{0,1},{1,0},{2,3},{3,2},{4,5},{5,4},{6,7},{7,6},{8,9},{9,8},{10,11... | collective-permute-start | bytes 4128776 | tf_op jit(solution)/shard_map/cond/branch_1_fun/ppermute | solution.py:27
  305.7 18.1 %collective-permute-start.15 = (bf16[448,768]{1,0:T(8,128)(2,1)S(1)}, bf16[448,768]{1,0:T(8,128)(2,1)S(1)}, u32[]{:S(2)}, u32[]{:S(2)}) collective-permute-start(bf16[448,768]{1,0:T(8,128)(2,1)S(1)} %constant_dynamic-slice_fusion.4), channel_id=1, source_target_pairs={{0,16},{16,0},{1,17},{17,1},{2,18},{18,2},{3,19},{19,3},{4,20},{20... | collective-permute-start | bytes 2064392 | tf_op jit(solution)/shard_map/cond/branch_1_fun/ppermute | solution.py:27
  306.0 5.0 %collective-permute-start.13 = (bf16[64,768]{1,0:T(8,128)(2,1)S(1)}, bf16[64,768]{1,0:T(8,128)(2,1)S(1)}, u32[]{:S(2)}, u32[]{:S(2)}) collective-permute-start(bf16[64,768]{1,0:T(8,128)(2,1)S(1)} %constant_dynamic-slice_fusion.6), channel_id=1, source_target_pairs={{0,2},{1,3},{2,0},{3,1},{4,6},{5,7},{6,4},{7,5},{8,10},{9,11},{10,... | collective-permute-start | bytes 294920 | tf_op jit(solution)/shard_map/cond/branch_1_fun/ppermute | solution.py:27
  308.1 7.0 %collective-permute-start.14 = (bf16[96,768]{1,0:T(8,128)(2,1)S(1)}, bf16[96,768]{1,0:T(8,128)(2,1)S(1)}, u32[]{:S(2)}, u32[]{:S(2)}) collective-permute-start(bf16[96,768]{1,0:T(8,128)(2,1)S(1)} %constant_dynamic-slice_fusion.5), channel_id=1, source_target_pairs={{0,4},{1,5},{2,6},{3,7},{4,0},{5,1},{6,2},{7,3},{8,12},{9,13},{10,... | collective-permute-start | bytes 442376 | tf_op jit(solution)/shard_map/cond/branch_1_fun/ppermute | solution.py:27
  324.0 6.4 %collective-permute-start.17 = (bf16[48,768]{1,0:T(8,128)(2,1)S(1)}, bf16[48,768]{1,0:T(8,128)(2,1)S(1)}, u32[]{:S(2)}, u32[]{:S(2)}) collective-permute-start(bf16[48,768]{1,0:T(8,128)(2,1)S(1)} %constant_dynamic-slice_fusion.3), channel_id=1, source_target_pairs={{0,8},{1,9},{2,10},{3,11},{4,12},{5,13},{6,14},{7,15},{8,0},{9,1},... | collective-permute-start | bytes 221192 | tf_op jit(solution)/shard_map/cond/branch_1_fun/ppermute | solution.py:27
  326.5 7.2 %collective-permute-start.16 = (bf16[64,768]{1,0:T(8,128)(2,1)S(1)}, bf16[64,768]{1,0:T(8,128)(2,1)S(1)}, u32[]{:S(2)}, u32[]{:S(2)}) collective-permute-start(bf16[64,768]{1,0:T(8,128)(2,1)S(1)} %add_convert_fusion.13), channel_id=1, source_target_pairs={{0,4},{1,5},{2,6},{3,7},{4,0},{5,1},{6,2},{7,3},{8,12},{9,13},{10,... | collective-permute-start | bytes 294920 | tf_op jit(solution)/shard_map/cond/branch_1_fun/ppermute | solution.py:27
  327.5 17.0 %collective-permute-start.18 = (bf16[224,768]{1,0:T(8,128)(2,1)S(1)}, bf16[224,768]{1,0:T(8,128)(2,1)S(1)}, u32[]{:S(2)}, u32[]{:S(2)}) collective-permute-start(bf16[224,768]{1,0:T(8,128)(2,1)S(1)} %constant_dynamic-slice_fusion.2), channel_id=1, source_target_pairs={{0,2},{1,3},{2,0},{3,1},{4,6},{5,7},{6,4},{7,5},{8,10},{9,11},{10,... | collective-permute-start | bytes 1032200 | tf_op jit(solution)/shard_map/cond/branch_1_fun/ppermute | solution.py:27
  344.6 9.2 %collective-permute-start.20 = (bf16[48,768]{1,0:T(8,128)(2,1)S(1)}, bf16[48,768]{1,0:T(8,128)(2,1)S(1)}, u32[]{:S(2)}, u32[]{:S(2)}) collective-permute-start(bf16[48,768]{1,0:T(8,128)(2,1)S(1)} %add_convert_fusion.18), channel_id=1, source_target_pairs={{0,8},{1,9},{2,10},{3,11},{4,12},{5,13},{6,14},{7,15},{8,0},{9,1},... | collective-permute-start | bytes 221192 | tf_op jit(solution)/shard_map/cond/branch_1_fun/ppermute | solution.py:27
  345.0 13.1 %collective-permute-start.19 = (bf16[64,768]{1,0:T(8,128)(2,1)S(1)}, bf16[64,768]{1,0:T(8,128)(2,1)S(1)}, u32[]{:S(2)}, u32[]{:S(2)}) collective-permute-start(bf16[64,768]{1,0:T(8,128)(2,1)S(1)} %add_convert_fusion.12), channel_id=1, source_target_pairs={{0,8},{1,9},{2,10},{3,11},{4,12},{5,13},{6,14},{7,15},{8,0},{9,1},... | collective-permute-start | bytes 294920 | tf_op jit(solution)/shard_map/cond/branch_1_fun/ppermute | solution.py:27
  347.6 12.4 %collective-permute-start.21 = (bf16[112,768]{1,0:T(8,128)(2,1)S(1)}, bf16[112,768]{1,0:T(8,128)(2,1)S(1)}, u32[]{:S(2)}, u32[]{:S(2)}) collective-permute-start(bf16[112,768]{1,0:T(8,128)(2,1)S(1)} %constant_dynamic-slice_fusion.1), channel_id=1, source_target_pairs={{0,4},{1,5},{2,6},{3,7},{4,0},{5,1},{6,2},{7,3},{8,12},{9,13},{10,... | collective-permute-start | bytes 516104 | tf_op jit(solution)/shard_map/cond/branch_1_fun/ppermute | solution.py:27
  360.1 8.2 %collective-permute-start.24 = (bf16[56,768]{1,0:T(8,128)(2,1)S(1)}, bf16[56,768]{1,0:T(8,128)(2,1)S(1)}, u32[]{:S(2)}, u32[]{:S(2)}) collective-permute-start(bf16[56,768]{1,0:T(8,128)(2,1)S(1)} %constant_dynamic-slice_fusion), channel_id=1, source_target_pairs={{0,8},{1,9},{2,10},{3,11},{4,12},{5,13},{6,14},{7,15},{8,0},{9,1},... | collective-permute-start | bytes 258056 | tf_op jit(solution)/shard_map/cond/branch_1_fun/ppermute | solution.py:27
  363.5 4.9 %collective-permute-start.22 = (bf16[64,768]{1,0:T(8,128)(2,1)S(1)}, bf16[64,768]{1,0:T(8,128)(2,1)S(1)}, u32[]{:S(2)}, u32[]{:S(2)}) collective-permute-start(bf16[64,768]{1,0:T(8,128)(2,1)S(1)} %add_convert_fusion.11), channel_id=1, source_target_pairs={{0,2},{1,3},{2,0},{3,1},{4,6},{5,7},{6,4},{7,5},{8,10},{9,11},{10,... | collective-permute-start | bytes 294920 | tf_op jit(solution)/shard_map/cond/branch_1_fun/ppermute | solution.py:27
  364.8 8.6 %collective-permute-start.23 = (bf16[96,768]{1,0:T(8,128)(2,1)S(1)}, bf16[96,768]{1,0:T(8,128)(2,1)S(1)}, u32[]{:S(2)}, u32[]{:S(2)}) collective-permute-start(bf16[96,768]{1,0:T(8,128)(2,1)S(1)} %maximum_select_fusion.7), channel_id=1, source_target_pairs={{0,4},{1,5},{2,6},{3,7},{4,0},{5,1},{6,2},{7,3},{8,12},{9,13},{10,... | collective-permute-start | bytes 442376 | tf_op jit(solution)/shard_map/cond/branch_1_fun/ppermute | solution.py:27
  373.5 7.9 %collective-permute-start.27 = (bf16[56,768]{1,0:T(8,128)(2,1)S(1)}, bf16[56,768]{1,0:T(8,128)(2,1)S(1)}, u32[]{:S(2)}, u32[]{:S(2)}) collective-permute-start(bf16[56,768]{1,0:T(8,128)(2,1)S(1)} %add_convert_fusion.17), channel_id=1, source_target_pairs={{0,8},{1,9},{2,10},{3,11},{4,12},{5,13},{6,14},{7,15},{8,0},{9,1},... | collective-permute-start | bytes 258056 | tf_op jit(solution)/shard_map/cond/branch_1_fun/ppermute | solution.py:27
  376.1 5.9 %collective-permute-start.25 = (bf16[128,768]{1,0:T(8,128)(2,1)S(1)}, bf16[128,768]{1,0:T(8,128)(2,1)S(1)}, u32[]{:S(2)}, u32[]{:S(2)}) collective-permute-start(bf16[128,768]{1,0:T(8,128)(2,1)S(1)} %maximum_select_fusion.5), channel_id=1, source_target_pairs={{0,1},{1,0},{2,3},{3,2},{4,5},{5,4},{6,7},{7,6},{8,9},{9,8},{10,11... | collective-permute-start | bytes 589832 | tf_op jit(solution)/shard_map/cond/branch_1_fun/ppermute | solution.py:27
  376.1 10.4 %collective-permute-start.26 = (bf16[192,768]{1,0:T(8,128)(2,1)S(1)}, bf16[192,768]{1,0:T(8,128)(2,1)S(1)}, u32[]{:S(2)}, u32[]{:S(2)}) collective-permute-start(bf16[192,768]{1,0:T(8,128)(2,1)S(1)} %maximum_select_fusion.3), channel_id=1, source_target_pairs={{0,2},{1,3},{2,0},{3,1},{4,6},{5,7},{6,4},{7,5},{8,10},{9,11},{10,... | collective-permute-start | bytes 884744 | tf_op jit(solution)/shard_map/cond/branch_1_fun/ppermute | solution.py:27
  387.8 20.3 %copy-start.49 = (s32[1024]{0:T(1024)S(1)}, s32[1024]{0:T(1024)}, u32[]{:S(2)}) copy-start(s32[1024]{0:T(1024)} %copy-done.48) | copy-start | bytes 12292
  387.8 20.3 %copy-start.53 = (s32[256]{0:T(256)S(1)}, s32[256]{0:T(256)}, u32[]{:S(2)}) copy-start(s32[256]{0:T(256)} %copy-done.52) | copy-start | bytes 3076
  387.8 20.2 %copy-start.55 = (s32[256]{0:T(256)S(1)}, s32[256]{0:T(256)}, u32[]{:S(2)}) copy-start(s32[256]{0:T(256)} %copy-done.54) | copy-start | bytes 3076
  387.8 8.6 %collective-permute-start.43 = (bf16[112,768]{1,0:T(8,128)(2,1)}, bf16[112,768]{1,0:T(8,128)(2,1)S(1)}, u32[]{:S(2)}, u32[]{:S(2)}) collective-permute-start(bf16[112,768]{1,0:T(8,128)(2,1)} %get-tuple-element.200), channel_id=1, source_target_pairs={{0,4},{1,5},{2,6},{3,7},{4,0},{5,1},{6,2},{7,3},{8,12},{9,13},{10,... | collective-permute-start | bytes 516104 | tf_op jit(solution)/shard_map/ppermute | solution.py:27
  397.5 9.8 %collective-permute-start.44 = (bf16[224,768]{1,0:T(8,128)(2,1)S(1)}, bf16[224,768]{1,0:T(8,128)(2,1)S(1)}, u32[]{:S(2)}, u32[]{:S(2)}) collective-permute-start(bf16[224,768]{1,0:T(8,128)(2,1)S(1)} %maximum_select_fusion.13), channel_id=1, source_target_pairs={{0,2},{1,3},{2,0},{3,1},{4,6},{5,7},{6,4},{7,5},{8,10},{9,11},{10,... | collective-permute-start | bytes 1032200 | tf_op jit(solution)/shard_map/ppermute | solution.py:27
  398.4 16.5 %collective-permute-start.42 = (bf16[384,768]{1,0:T(8,128)(2,1)}, bf16[384,768]{1,0:T(8,128)(2,1)S(1)}, u32[]{:S(2)}, u32[]{:S(2)}) collective-permute-start(bf16[384,768]{1,0:T(8,128)(2,1)} %get-tuple-element.199), channel_id=1, source_target_pairs={{0,16},{16,0},{1,17},{17,1},{2,18},{18,2},{3,19},{19,3},{4,20},{20... | collective-permute-start | bytes 1769480 | tf_op jit(solution)/shard_map/ppermute | solution.py:27
  407.5 21.3 %collective-permute-start.45 = (bf16[448,768]{1,0:T(8,128)(2,1)S(1)}, bf16[448,768]{1,0:T(8,128)(2,1)}, u32[]{:S(2)}, u32[]{:S(2)}) collective-permute-start(bf16[448,768]{1,0:T(8,128)(2,1)S(1)} %maximum_select_fusion.10), channel_id=1, source_target_pairs={{0,16},{16,0},{1,17},{17,1},{2,18},{18,2},{3,19},{19,3},{4,20},{20... | collective-permute-start | bytes 2064392 | tf_op jit(solution)/shard_map/ppermute | solution.py:27
  430.6 2.9 collective-permute-start.47
  430.7 4.8 %collective-permute-start.46 = (bf16[896,768]{1,0:T(8,128)(2,1)S(1)}, bf16[896,768]{1,0:T(8,128)(2,1)S(1)}, u32[]{:S(2)}, u32[]{:S(2)}) collective-permute-start(bf16[896,768]{1,0:T(8,128)(2,1)S(1)} %maximum_select_fusion.8.late_ref), channel_id=1, source_target_pairs={{0,1},{1,0},{2,3},{3,2},{4,5},{5,4},{6,7},{7,6},{8,9},{9,8},{10,11... | collective-permute-start | bytes 4128776 | tf_op jit(solution)/shard_map/ppermute | solution.py:27
  (63 other events, 335.8 us)
Sparse Core Ops, SparseCore 0:
  173.4 222.6 all-reduce.7
